TPU v7x, 32 devices: a whole 2x2x4 slice. The times are simulated.
32 devices in a mesh: groups: 1, role: 2 (over core), ep: 8 (over z, y), tp: 2 (over x).
Axes of the slice: x: 2, y: 2, z: 4, core: 2. Of those that a mesh axis runs over, the one named last changes fastest.
Arguments:
- tokens: bfloat16 [2048, 2048], P(('groups', 'role', 'ep'), 'tp'), may hold values from -6 to 6
- out_grad: bfloat16 [2048, 2048], P(('groups', 'role', 'ep'), 'tp'), may hold values from -6 to 6
- routes: int32 [2048, 8], P(('groups', 'role', 'ep')), may hold values from 0 to 15, all different within a row; in each aligned block of 128 rows (0 to 127, 128 to 255, ...) at most 72 rows name the same one
- probs: bfloat16 [2048, 8], P(('groups', 'role', 'ep')), may hold values from 0.049804688 to 1
- w_gate: bfloat16 [16, 2048, 768], P(('role', 'ep'), None, 'tp'), may hold values from -0.125 to 0.125
- w_up: bfloat16 [16, 2048, 768], P(('role', 'ep'), None, 'tp'), may hold values from -0.125 to 0.125
- w_down: bfloat16 [16, 768, 2048], P(('role', 'ep'), 'tp'), may hold values from -0.21875 to 0.21875
Outputs:
- d_tokens: bfloat16 [2048, 2048], P(('groups', 'role', 'ep'), 'tp')
- d_probs: float32 [2048, 8], P(('groups', 'role', 'ep'))
- d_w_gate: bfloat16 [16, 2048, 768], P(('groups', 'role', 'ep'), None, 'tp')
- d_w_up: bfloat16 [16, 2048, 768], P(('groups', 'role', 'ep'), None, 'tp')
- d_w_down: bfloat16 [16, 768, 2048], P(('groups', 'role', 'ep'), 'tp')
Inputs may be any that keep to these rules, and one draw needn't show every extreme that they name: `routes`: in each aligned block of 128 rows (the tokens of one index of role and ep) no expert is named by more than 72 rows, a bound that some block reaches.
All inputs are finite; a program needn't handle non-finite values.
Results may differ from a plain program's by a relative error of at most 0.012.
Values may be sent and summed in bfloat16 or wider, within the bound.
No kernel may reach another device: no remote copies, remote signals or barrier semaphores. Data moves between devices by JAX's collectives and lax.ppermute only.
A program may use at most 128 MiB of HBM per device.

v0:
```python
import jax
import jax.numpy as jnp
from jax import lax
from jax.sharding import PartitionSpec as P


def pad_rows(array):
    return jnp.concatenate([array, jnp.zeros((1, array.shape[1]), array.dtype)], 0)


def per_device(tokens, out_grad, routes, probs, w_gate, w_up, w_down):
    owners = lax.axis_size(("role", "ep"))
    tok_rows, top_count = routes.shape
    width_full = w_gate.shape[1]
    part_width = w_gate.shape[2]
    capacity = min(tok_rows, tok_rows * top_count * 9 // (8 * owners))
    entry_total = tok_rows * top_count
    routes_flat = routes.reshape(-1)
    onehot = (routes_flat[:, None] == jnp.arange(owners, dtype=jnp.int32)[None, :]).astype(
        jnp.int32
    )
    before = jnp.cumsum(onehot, axis=0) - onehot
    slot_index = jnp.sum(before * onehot, axis=1)
    target = routes_flat * capacity + slot_index
    row_count = owners * capacity
    entry_of_slot = (
        jnp.full((row_count,), entry_total, jnp.int32)
        .at[target]
        .set(jnp.arange(entry_total, dtype=jnp.int32))
    )
    token_of_slot = entry_of_slot // top_count
    padded_prob = jnp.concatenate([probs.reshape(-1), jnp.zeros((1,), probs.dtype)], 0)
    send_prob = padded_prob[entry_of_slot].reshape(owners, capacity)
    send_x = pad_rows(tokens)[token_of_slot]
    send_g = pad_rows(out_grad)[token_of_slot]
    slice_x, slice_g, recv_p = (
        lax.all_to_all(
            send_x.reshape(owners, capacity, tokens.shape[1]),
            ("role", "ep"),
            split_axis=0,
            concat_axis=0,
            tiled=True,
        ),
        lax.all_to_all(
            send_g.reshape(owners, capacity, tokens.shape[1]),
            ("role", "ep"),
            split_axis=0,
            concat_axis=0,
            tiled=True,
        ),
        lax.all_to_all(send_prob, ("role", "ep"), split_axis=0, concat_axis=0, tiled=True),
    )
    recv_x, recv_g = (
        lax.all_gather(slice_x, "tp", axis=2, tiled=True),
        lax.all_gather(slice_g, "tp", axis=2, tiled=True),
    )
    rows_x = recv_x.reshape(row_count, width_full)
    rows_g = recv_g.reshape(row_count, width_full)
    weight_p = recv_p.reshape(row_count, 1).astype(jnp.float32)
    gate_up = jnp.concatenate([w_gate[0], w_up[0]], 1)
    down_shard = w_down[0]
    both_rows = jnp.dot(rows_x, gate_up, preferred_element_type=jnp.float32)
    gate_rows = both_rows[:, :part_width]
    up_rows = both_rows[:, part_width:]
    sigmoid_gate = jax.nn.sigmoid(gate_rows)
    activated = gate_rows * sigmoid_gate
    hidden = activated * up_rows
    back_rows = lax.dot_general(
        rows_g, down_shard, (((1,), (1,)), ((), ())), preferred_element_type=jnp.float32
    )
    scores = lax.psum(jnp.sum(hidden * back_rows, axis=1), "tp")
    hidden_grad = weight_p * back_rows
    d_gate_rows = (
        hidden_grad * up_rows * sigmoid_gate * (1.0 + gate_rows * (1.0 - sigmoid_gate))
    ).astype(jnp.bfloat16)
    d_up_rows = (hidden_grad * activated).astype(jnp.bfloat16)
    d_both = jnp.concatenate([d_gate_rows, d_up_rows], 1)
    scaled = (weight_p * hidden).astype(jnp.bfloat16)
    grad_down = lax.dot_general(
        scaled, rows_g, (((0,), (0,)), ((), ())), preferred_element_type=jnp.float32
    )
    grad_both = lax.dot_general(
        rows_x, d_both, (((0,), (0,)), ((), ())), preferred_element_type=jnp.float32
    )
    grad_gate = grad_both[:, :part_width]
    grad_up = grad_both[:, part_width:]
    partial_low = lax.dot_general(
        d_both, gate_up, (((1,), (1,)), ((), ())), preferred_element_type=jnp.float32
    ).astype(jnp.bfloat16)
    home_s = lax.all_to_all(
        scores.reshape(owners, capacity), ("role", "ep"), split_axis=0, concat_axis=0, tiled=True
    )
    summed = lax.psum_scatter(
        partial_low.reshape(owners, capacity, width_full), "tp", scatter_dimension=2, tiled=True
    ).astype(jnp.float32)
    summed_low = summed.astype(jnp.bfloat16)
    home_x = lax.all_to_all(summed_low, ("role", "ep"), split_axis=0, concat_axis=0, tiled=True)
    slice_width = summed.shape[2]
    route_rows = home_x.reshape(row_count, slice_width).astype(jnp.float32)
    d_tok = (
        jnp.zeros((tok_rows + 1, slice_width), jnp.float32)
        .at[token_of_slot]
        .add(route_rows)[:tok_rows]
    )
    d_probs = home_s.reshape(-1)[target].reshape(tok_rows, top_count)
    return (
        d_tok.astype(jnp.bfloat16),
        d_probs,
        grad_gate.astype(jnp.bfloat16)[None],
        grad_up.astype(jnp.bfloat16)[None],
        grad_down.astype(jnp.bfloat16)[None],
    )


def solution(mesh):
    in_specs = (
        P(("groups", "role", "ep"), "tp"),
        P(("groups", "role", "ep"), "tp"),
        P(("groups", "role", "ep"), None),
        P(("groups", "role", "ep"), None),
        P(("role", "ep"), None, "tp"),
        P(("role", "ep"), None, "tp"),
        P(("role", "ep"), "tp", None),
    )
    out_specs = (
        P(("groups", "role", "ep"), "tp"),
        P(("groups", "role", "ep"), None),
        P(("groups", "role", "ep"), None, "tp"),
        P(("groups", "role", "ep"), None, "tp"),
        P(("groups", "role", "ep"), "tp", None),
    )
    return jax.shard_map(
        per_device, mesh=mesh, in_specs=in_specs, out_specs=out_specs, check_vma=False
    )
```

profile of v0, /device:TPU:0, one launch (start us, length us, event | category | flops | bytes accessed | tf_op | source)
XLA Modules:
  0.0 365.9 jit_solution(3342782884633505254)
XLA Ops:
  7.2 0.8 broadcast_multiply_fusion
  8.0 0.8 copy.22
  8.8 0.1 eq.29
  8.9 0.1 eq.25
  9.0 0.1 copy.21
  9.1 0.1 mul.59
  9.2 4.5 %reduce-window.6 = s32[16,8,128]{2,1,0:T(8,128)S(1)} reduce-window(s32[16,8,128]{2,1,0:T(8,128)S(1)} %fusion.12, s32[]{:T(128)} %constant.17.clone.1), window={size=1x1x128 pad=0_0x0_0x127_0}, to_apply=%region_0.0 | reduce-window | flops 2080768 | bytes 131076 | tf_op jit(solution)/shard_map/reduce-window
  13.7 0.1 slice.39
  13.8 0.1 copy.24
  14.0 0.1 copy.25
  14.0 0.1 broadcast_add_fusion
  14.2 4.3 %scatter_custom_fusion = s32[1152]{0:T(1024)S(1)} fusion(s32[1024]{0:T(1024)S(1)} %bitcast.51, s32[1024]{0:T(1024)S(1)} %iota.11, s32[]{:T(128)} %constant.11.clone.1), kind=kCustom, calls=%fused_computation.51 | custom fusion | bytes 4612 | tf_op jit(solution)/shard_map/scatter | solution.py:29
  18.6 1.0 concatenate.17
  19.5 5.0 %gather_fusion.2 = bf16[1152,1024]{1,0:T(8,128)(2,1)} fusion(bf16[129,1024]{1,0:T(8,128)(2,1)S(1)} %concatenate.17, s32[2048]{0:T(1024)S(1)} %get-tuple-element.22), kind=kCustom, calls=%fused_computation.2 | custom fusion | bytes 4723200 | tf_op jit(solution)/shard_map/gather | solution.py:34
  24.6 62.8 %all_to_all.34 = bf16[16,72,1024]{2,1,0:T(8,128)(2,1)} all-to-all(bf16[16,72,1024]{2,1,0:T(8,128)(2,1)} %bitcast.46), channel_id=1, replica_groups=mesh['groups'=1,'role'=2,'ep'=8,'tp'=2] {'role','ep'}, dimensions={0} | all-to-all | bytes 4718592 | tf_op jit(solution)/shard_map/all_to_all | solution.py:37
  87.4 0.0 all-gather.3.cloned.1.call-start
  87.4 0.9 copy-done.1
  88.3 5.0 %gather_fusion.1 = bf16[1152,1024]{1,0:T(8,128)(2,1)} fusion(bf16[129,1024]{1,0:T(8,128)(2,1)S(1)} %concatenate.16, s32[2048]{0:T(1024)S(1)} %get-tuple-element.22), kind=kCustom, calls=%fused_computation.1 | custom fusion | bytes 4723200 | tf_op jit(solution)/shard_map/gather | solution.py:35
  93.4 59.7 %all_to_all.35 = bf16[16,72,1024]{2,1,0:T(8,128)(2,1)} all-to-all(bf16[16,72,1024]{2,1,0:T(8,128)(2,1)} %bitcast.45), channel_id=1, replica_groups=mesh['groups'=1,'role'=2,'ep'=8,'tp'=2] {'role','ep'}, dimensions={0} | all-to-all | bytes 4718592 | tf_op jit(solution)/shard_map/all_to_all | solution.py:44
  153.2 0.6 copy-done.2
  153.8 0.1 copy.26
  153.9 0.1 reshape.104
  154.0 7.2 %gather_fusion = bf16[1152]{0:T(1024)(128)(2,1)S(1)} fusion(bf16[1025]{0:T(1024)(128)(2,1)S(1)} %pad_maximum_fusion.6, s32[2048]{0:T(1024)S(1)} %get-tuple-element.23), kind=kCustom, calls=%fused_computation | custom fusion | bytes 9216 | tf_op jit(solution)/shard_map/gather | solution.py:33
  161.3 0.1 all_to_all.28
  161.4 8.9 %all_to_all.36 = bf16[16,1,72]{2,1,0:T(2,128)(2,1)S(1)} all-to-all(bf16[16,1,72]{2,1,0:T(2,128)(2,1)S(1)} %all_to_all.28), channel_id=1, replica_groups=mesh['groups'=1,'role'=2,'ep'=8,'tp'=2] {'role','ep'}, dimensions={0} | all-to-all | bytes 4608 | tf_op jit(solution)/shard_map/all_to_all | solution.py:51
  170.3 0.1 reshape.112
  170.4 8.9 %fusion.3 = f32[1152,768]{0,1:T(8,128)} fusion(bf16[1152,2048]{1,0:T(8,128)(2,1)} %bitcast.53, bf16[2048,384]{1,0:T(8,128)(2,1)S(1)} %bitcast.57, bf16[2048,384]{1,0:T(8,128)(2,1)} %bitcast.59), kind=kOutput, calls=%fused_computation.13 | convolution fusion | flops 3630170112 | bytes 11403264 | tf_op jit(solution)/shard_map/dot_general | solution.py:62
  179.4 34.5 %all-gather.3.cloned.1.call-done = bf16[16,72,2048]{2,1,0:T(8,128)(2,1)} async-done(((bf16[16,72,1024]{2,1,0:T(8,128)(2,1)}), bf16[16,72,2048]{2,1,0:T(8,128)(2,1)}) %all-gather.3.cloned.1.call-update) | async-done | bytes 4718608 | tf_op jit(solution)/shard_map/all_gather | solution.py:55
  213.9 6.3 %multiply_convert_fusion.2 = (bf16[1152,384]{0,1:T(8,128)(2,1)S(1)}, bf16[1152,384]{0,1:T(8,128)(2,1)S(1)}, f32[1152]{0:T(1024)S(1)}) fusion(f32[1152,768]{0,1:T(8,128)} %fusion.3, f32[1152]{0:T(1024)S(1)} %reshape.112, bf16[1152,2048]{1,0:T(8,128)(2,1)} %bitcast.55, bf16[1,384,2048]{2,1,0:T(8,128)(2,1)S(1)} %copy-done), kind=kOutput, calls=%fused_computation.18 | convolution fusion | flops 1819458432 | bytes 11609088 | tf_op jit(solution)/shard_map/dot_general | solution.py:68
  220.2 5.6 %convolution_convert_fusion = bf16[1152,2048]{1,0:T(8,128)(2,1)} fusion(bf16[2048,384]{1,0:T(8,128)(2,1)S(1)} %bitcast.58, bf16[2048,384]{1,0:T(8,128)(2,1)S(1)} %bitcast.60, bf16[1152,384]{0,1:T(8,128)(2,1)S(1)} %get-tuple-element.16, bf16[1152,384]{0,1:T(8,128)(2,1)S(1)} %get-tuple-element.15), kind=kOutput, calls=%fused_computation.6 | convolution fusion | flops 3636068352 | bytes 9633792 | tf_op jit(solution)/shard_map/dot_general | solution.py:87
  225.9 0.1 all_to_all.26
  226.0 5.0 %psum.7 = f32[16,1,72]{2,1,0:T(1,128)S(1)} all-reduce(f32[16,1,72]{2,1,0:T(1,128)S(1)} %all_to_all.26), channel_id=1, replica_groups=mesh['groups'=1,'role'=2,'ep'=8,'tp'=2] {'tp'}, use_global_device_ids=true, to_apply=%region_7.8 | all-reduce | flops 1152 | bytes 9216 | tf_op jit(solution)/shard_map/psum | solution.py:71
  231.0 11.8 %all_to_all.37 = f32[16,1,72]{2,1,0:T(1,128)S(1)} all-to-all(f32[16,1,72]{2,1,0:T(1,128)S(1)} %psum.7), channel_id=1, replica_groups=mesh['groups'=1,'role'=2,'ep'=8,'tp'=2] {'role','ep'}, dimensions={0} | all-to-all | bytes 9216 | tf_op jit(solution)/shard_map/all_to_all | solution.py:90
  242.8 43.3 %reduce-scatter.2.cloned.1.call-done = bf16[16,72,1024]{2,1,0:T(8,128)(2,1)} async-done(((bf16[16,72,2048]{2,1,0:T(8,128)(2,1)}), bf16[16,72,1024]{2,1,0:T(8,128)(2,1)}) %reduce-scatter.2.cloned.1.call-update) | async-done | bytes 2359312 | tf_op jit(solution)/shard_map/reduce_scatter | solution.py:93
  286.0 5.7 %all-to-all-start.3 = ((bf16[16,72,1024]{2,1,0:T(8,128)(2,1)}), bf16[16,72,1024]{2,1,0:T(8,128)(2,1)}, u32[]{:S(2)}, u32[]{:S(2)}) async-start(bf16[16,72,1024]{2,1,0:T(8,128)(2,1)} %reduce-scatter.2.cloned.1.call-done), calls=%async_computation.4 | async-start | bytes 4718592 | tf_op jit(solution)/shard_map/all_to_all | solution.py:97
  291.7 7.8 %convolution_convert_fusion.1 = bf16[2048,768]{1,0:T(8,128)(2,1)S(1)} fusion(bf16[1152,2048]{1,0:T(8,128)(2,1)} %bitcast.54, bf16[1152,384]{0,1:T(8,128)(2,1)S(1)} %copy-done.9, bf16[1152,384]{0,1:T(8,128)(2,1)S(1)} %copy-done.7), kind=kOutput, calls=%fused_computation.9 | convolution fusion | flops 3628990464 | bytes 9633792 | tf_op jit(solution)/shard_map/dot_general | solution.py:82
  299.6 2.0 slice_bitcast_fusion
  301.6 1.2 copy-done.5
  302.7 5.7 %fusion.2 = bf16[1,384,2048]{2,1,0:T(8,128)(2,1)} fusion(bf16[1152,2048]{1,0:T(8,128)(2,1)} %bitcast.56, f32[1152]{0:T(1024)S(1)} %reshape.112, f32[1152,768]{0,1:T(8,128)S(1)} %copy-done.5), kind=kOutput, calls=%fused_computation.12 | convolution fusion | flops 1815822336 | bytes 9835008 | tf_op jit(solution)/shard_map/dot_general | solution.py:79
  308.4 0.5 broadcast.105
  309.0 0.7 reduce.7
  309.6 0.1 reshape.110
  309.7 6.2 %gather_fusion.3 = f32[1024]{0:T(1024)S(1)} fusion(f32[1152]{0:T(1024)S(1)} %reshape.110, s32[1024]{0:T(1024)S(1)} %broadcast_clamp_fusion), kind=kCustom, calls=%fused_computation.3 | custom fusion | bytes 12288 | tf_op jit(solution)/shard_map/gather | solution.py:105
  315.9 0.1 reshape.111
  316.0 0.7 copy.28
  316.6 28.0 %all-to-all-done.3 = bf16[16,72,1024]{2,1,0:T(8,128)(2,1)} async-done(((bf16[16,72,1024]{2,1,0:T(8,128)(2,1)}), bf16[16,72,1024]{2,1,0:T(8,128)(2,1)}, u32[]{:S(2)}, u32[]{:S(2)}) %all-to-all-start.3) | async-done | bytes 2359328 | tf_op jit(solution)/shard_map/all_to_all | solution.py:97
  344.6 14.0 %scatter_custom_fusion.1 = f32[129,1024]{1,0:T(8,128)S(1)} fusion(s32[1152]{0:T(1024)S(1)} %get-tuple-element.21, bf16[1152,1024]{1,0:T(8,128)(2,1)} %bitcast.16, f32[]{:T(128)} %constant.14.clone.1), kind=kCustom, calls=%fused_computation.7 | custom fusion | flops 2359296 | bytes 2887684 | tf_op jit(solution)/shard_map/scatter-add | solution.py:103
  358.7 0.7 slice.65
  (35 shorter events, 0.4 us)
Async XLA Ops:
  7.2 206.7 %copy-start = (bf16[1,384,2048]{2,1,0:T(8,128)(2,1)S(1)}, bf16[1,384,2048]{2,1,0:T(8,128)(2,1)}, u32[]{:S(2)}) copy-start(bf16[1,384,2048]{2,1,0:T(8,128)(2,1)} %param.13) | copy-start | bytes 4718596
  7.2 163.2 %all-gather.5.cloned.1.call-start = ((), (), s32[]{:S(2)}) async-start(), calls=%async_computation.7 | async-start | bytes 7077888 | tf_op jit(solution)/shard_map/all_gather | solution.py:54
  87.4 1.0 copy-start.1
  87.4 126.5 %all-gather.3.cloned.1.call-start = ((), (), s32[]{:S(2)}) async-start(), calls=%async_computation.6 | async-start | bytes 7077888 | tf_op jit(solution)/shard_map/all_gather | solution.py:55
  153.1 0.7 copy-start.2
  153.1 17.3 %copy-start.3 = (bf16[1,2048,384]{2,1,0:T(8,128)(2,1)S(1)}, bf16[1,2048,384]{2,1,0:T(8,128)(2,1)}, u32[]{:S(2)}) copy-start(bf16[1,2048,384]{2,1,0:T(8,128)(2,1)} %param.12) | copy-start | bytes 4718596
  153.1 132.9 %reduce-scatter.2.cloned.1.call-start = ((), (), s32[]{:S(2)}) async-start(), calls=%async_computation.8 | async-start | bytes 7077888 | tf_op jit(solution)/shard_map/reduce_scatter | solution.py:93
  213.9 6.3 %copy-start.4 = (bf16[1,2048,384]{2,1,0:T(8,128)(2,1)S(1)}, bf16[1,2048,384]{2,1,0:T(8,128)(2,1)}, u32[]{:S(2)}) copy-start(bf16[1,2048,384]{2,1,0:T(8,128)(2,1)} %param.11) | copy-start | bytes 4718596
  220.2 5.7 %copy-start.6 = (bf16[1152,384]{0,1:T(8,128)(2,1)}, bf16[1152,384]{0,1:T(8,128)(2,1)S(1)}, u32[]{:S(2)}) copy-start(bf16[1152,384]{0,1:T(8,128)(2,1)S(1)} %get-tuple-element.15) | copy-start | bytes 2654212
  220.2 5.7 %copy-start.8 = (bf16[1152,384]{0,1:T(8,128)(2,1)}, bf16[1152,384]{0,1:T(8,128)(2,1)S(1)}, u32[]{:S(2)}) copy-start(bf16[1152,384]{0,1:T(8,128)(2,1)S(1)} %get-tuple-element.16) | copy-start | bytes 2654212
  242.8 49.0 %copy-start.7 = (bf16[1152,384]{0,1:T(8,128)(2,1)S(1)}, bf16[1152,384]{0,1:T(8,128)(2,1)}, u32[]{:S(2)}) copy-start(bf16[1152,384]{0,1:T(8,128)(2,1)} %copy-done.6) | copy-start | bytes 2654212
  242.8 49.0 %copy-start.9 = (bf16[1152,384]{0,1:T(8,128)(2,1)S(1)}, bf16[1152,384]{0,1:T(8,128)(2,1)}, u32[]{:S(2)}) copy-start(bf16[1152,384]{0,1:T(8,128)(2,1)} %copy-done.8) | copy-start | bytes 2654212
  286.0 58.6 %all-to-all-start.3 = ((bf16[16,72,1024]{2,1,0:T(8,128)(2,1)}), bf16[16,72,1024]{2,1,0:T(8,128)(2,1)}, u32[]{:S(2)}, u32[]{:S(2)}) async-start(bf16[16,72,1024]{2,1,0:T(8,128)(2,1)} %reduce-scatter.2.cloned.1.call-done), calls=%async_computation.4 | async-start | bytes 4718592 | tf_op jit(solution)/shard_map/all_to_all | solution.py:97
  299.6 3.1 copy-start.5
Sparse Core Ops, SparseCore 0:
  87.5 60.5 all-gather.4
  153.2 60.5 all-gather.2
  226.0 59.9 reduce-scatter.1
where the time goes:
time: 367 us; the launch traced here: 366 us
  blocking collectives  148 us (40%)
  waiting for transfers between devices  106 us (29%)
  local copies, waits for them, and re-layouts  37.4 us (10%)
  matrix products  34.4 us (9%)
  other arithmetic  20.2 us (6%)
  between operations  14 us (4%)
  starting transfers between devices  5.8 us (2%)
    all_to_all x1, blocking collectives, per_device(): lax.all_to_all(send_x.reshape(owners, capacity, tokens.shape[1]), ('role'...  62.8 us
    all_to_all x1, blocking collectives, per_device(): lax.all_to_all(send_g.reshape(owners, capacity, tokens.shape[1]), ('role'...  59.7 us
    reduce_scatter x1, waiting for transfers between devices, per_device(): lax.psum_scatter(partial_low.reshape(owners, capacity, width_full), 'tp',...  43.3 us
    all_gather x1, waiting for transfers between devices, per_device(): lax.all_gather(slice_g, 'tp', axis=2, tiled=True)  34.5 us
    all_to_all x1, waiting for transfers between devices, per_device(): lax.all_to_all(summed_low, ('role', 'ep'), split_axis=0, concat_axis=0, t...  28 us
    scatter-add x1, other arithmetic, per_device(): d_tok = jnp.zeros((tok_rows + 1, slice_width), jnp.float32).at[token_of_s...  14 us
    all_to_all x1, blocking collectives, per_device(): lax.all_to_all(scores.reshape(owners, capacity), ('role', 'ep'), split_ax...  11.8 us
    dot_general x1, matrix products, per_device(): both_rows = jnp.dot(rows_x, gate_up, preferred_element_type=jnp.float32)  8.92 us
  transfers between devices with their start and end apart: 4, of which 3 were waited for; matrix products, arithmetic and copies ran while one was open for 12% of the time, Pallas kernels for 0%

commit v1 on v0

--- a/solution.py
+++ b/solution.py
@@ -1,6 +1,10 @@
+import math
+
 import jax
 import jax.numpy as jnp
 from jax import lax
+from jax.experimental import pallas as pl
+from jax.experimental.pallas import tpu as pltpu
 from jax.sharding import PartitionSpec as P
 
 
@@ -8,7 +12,7 @@
     return jnp.concatenate([array, jnp.zeros((1, array.shape[1]), array.dtype)], 0)
 
 
-def per_device(tokens, out_grad, routes, probs, w_gate, w_up, w_down):
+def routed_device(tokens, out_grad, routes, probs, w_gate, w_up, w_down):
     owners = lax.axis_size(("role", "ep"))
     tok_rows, top_count = routes.shape
     width_full = w_gate.shape[1]
@@ -112,6 +116,147 @@
     )
 
 
+def slot_capacity(tok_rows, top_count, owners):
+    return min(tok_rows, tok_rows * top_count * 9 // (8 * owners))
+
+
+def rows_kernel(x_ref, g_ref, p_ref, wg_ref, wu_ref, wd_ref, both_ref, scaled_ref, score_ref, piece_ref, wgu):
+    part = wg_ref.shape[2]
+    half = x_ref.shape[2]
+
+    @pl.when(pl.program_id(0) == 0)
+    def _():
+        wgu[:, :part] = wg_ref[0]
+        wgu[:, part:] = wu_ref[0]
+
+    rows = jnp.dot(x_ref[0], wgu[:half], preferred_element_type=jnp.float32)
+    rows = rows + jnp.dot(x_ref[1], wgu[half:], preferred_element_type=jnp.float32)
+    wd = wd_ref[0]
+    back = lax.dot_general(g_ref[0], wd[:, :half], (((1,), (1,)), ((), ())), preferred_element_type=jnp.float32)
+    back = back + lax.dot_general(g_ref[1], wd[:, half:], (((1,), (1,)), ((), ())), preferred_element_type=jnp.float32)
+    gate, up = rows[:, :part], rows[:, part:]
+    sig = jax.nn.sigmoid(gate)
+    act = gate * sig
+    hidden = act * up
+    score_ref[...] = jnp.sum(hidden * back, axis=1, keepdims=True)
+    prob = p_ref[...]
+    hgrad = prob * back
+    both_ref[:, :part] = (hgrad * up * sig * (1.0 + gate * (1.0 - sig))).astype(jnp.bfloat16)
+    both_ref[:, part:] = (hgrad * act).astype(jnp.bfloat16)
+    scaled_ref[...] = (prob * hidden).astype(jnp.bfloat16)
+    both = both_ref[...]
+    piece_ref[0] = lax.dot_general(both, wgu[:half], (((1,), (1,)), ((), ())), preferred_element_type=jnp.float32).astype(jnp.bfloat16)
+    piece_ref[1] = lax.dot_general(both, wgu[half:], (((1,), (1,)), ((), ())), preferred_element_type=jnp.float32).astype(jnp.bfloat16)
+
+
+def rows_call(x_all, g_all, prob, w_gate, w_up, w_down):
+    tp, total, half = x_all.shape
+    part = w_gate.shape[2]
+    width = w_gate.shape[1]
+    step = math.gcd(total, 256)
+    grid = (total // step,)
+    moving = pl.BlockSpec((tp, step, half), lambda i: (0, i, 0))
+    return pl.pallas_call(
+        rows_kernel,
+        grid=grid,
+        in_specs=[
+            moving,
+            moving,
+            pl.BlockSpec((step, 1), lambda i: (i, 0)),
+            pl.BlockSpec((1, width, part), lambda i: (0, 0, 0)),
+            pl.BlockSpec((1, width, part), lambda i: (0, 0, 0)),
+            pl.BlockSpec((1, part, width), lambda i: (0, 0, 0)),
+        ],
+        out_specs=[
+            pl.BlockSpec((step, 2 * part), lambda i: (i, 0)),
+            pl.BlockSpec((step, part), lambda i: (i, 0)),
+            pl.BlockSpec((step, 1), lambda i: (i, 0)),
+            moving,
+        ],
+        out_shape=[
+            jax.ShapeDtypeStruct((total, 2 * part), jnp.bfloat16),
+            jax.ShapeDtypeStruct((total, part), jnp.bfloat16),
+            jax.ShapeDtypeStruct((total, 1), jnp.float32),
+            jax.ShapeDtypeStruct((tp, total, half), jnp.bfloat16),
+        ],
+        scratch_shapes=[pltpu.VMEM((width, 2 * part), jnp.bfloat16)],
+        compiler_params=pltpu.CompilerParams(vmem_limit_bytes=48 << 20),
+        cost_estimate=pl.CostEstimate(flops=10 * total * width * part, bytes_accessed=6 * total * width * 2, transcendentals=total * part),
+        name="rows",
+    )(x_all, g_all, prob, w_gate, w_up, w_down)
+
+
+def grads_kernel(x_ref, g_ref, both_ref, scaled_ref, dg_ref, du_ref, dd_ref):
+    part = scaled_ref.shape[1]
+    both = lax.dot_general(x_ref[0], both_ref[...], (((0,), (0,)), ((), ())), preferred_element_type=jnp.float32)
+    dg_ref[0] = both[:, :part].astype(jnp.bfloat16)
+    du_ref[0] = both[:, part:].astype(jnp.bfloat16)
+    dd_ref[0] = lax.dot_general(scaled_ref[...], g_ref[0], (((0,), (0,)), ((), ())), preferred_element_type=jnp.float32).astype(jnp.bfloat16)
+
+
+def grads_call(x_all, g_all, both, scaled):
+    tp, total, half = x_all.shape
+    part = scaled.shape[1]
+    width = tp * half
+    step = math.gcd(half, 256)
+    per = half // step
+    moving = pl.BlockSpec((1, total, step), lambda i: (i // per, 0, i % per))
+    return pl.pallas_call(
+        grads_kernel,
+        grid=(width // step,),
+        in_specs=[
+            moving,
+            moving,
+            pl.BlockSpec((total, 2 * part), lambda i: (0, 0)),
+            pl.BlockSpec((total, part), lambda i: (0, 0)),
+        ],
+        out_specs=[
+            pl.BlockSpec((1, step, part), lambda i: (0, i, 0)),
+            pl.BlockSpec((1, step, part), lambda i: (0, i, 0)),
+            pl.BlockSpec((1, part, step), lambda i: (0, 0, i)),
+        ],
+        out_shape=[
+            jax.ShapeDtypeStruct((1, width, part), jnp.bfloat16),
+            jax.ShapeDtypeStruct((1, width, part), jnp.bfloat16),
+            jax.ShapeDtypeStruct((1, part, width), jnp.bfloat16),
+        ],
+        compiler_params=pltpu.CompilerParams(vmem_limit_bytes=48 << 20),
+        cost_estimate=pl.CostEstimate(flops=6 * total * width * part, bytes_accessed=6 * total * width, transcendentals=0),
+        name="grads",
+    )(x_all, g_all, both, scaled)
+
+
+def dense_device(tokens, out_grad, routes, probs, w_gate, w_up, w_down):
+    everyone = ("tp", "role", "ep")
+    owners = lax.axis_size(("role", "ep"))
+    tp = lax.axis_size("tp")
+    me = lax.axis_index(("role", "ep"))
+    tok_rows, half = tokens.shape
+    total = owners * tok_rows
+    chosen = routes[:, :, None] == jnp.arange(owners, dtype=jnp.int32)
+    table = jnp.sum(jnp.where(chosen, probs[:, :, None].astype(jnp.float32), 0.0), axis=1)
+    table_all = lax.all_gather(table.astype(jnp.bfloat16), ("role", "ep"), axis=0, tiled=True)
+    prob = lax.dynamic_slice(table_all, (0, me), (total, 1)).astype(jnp.float32)
+    x_all = lax.all_gather(tokens, everyone, axis=0, tiled=True).reshape(tp, total, half)
+    g_all = lax.all_gather(out_grad, everyone, axis=0, tiled=True).reshape(tp, total, half)
+    both, scaled, score, piece = rows_call(x_all, g_all, prob, w_gate, w_up, w_down)
+    d_tok = lax.psum_scatter(piece.reshape(tp * total, half), everyone, scatter_dimension=0, tiled=True)
+    scores = lax.all_gather(score.reshape(1, total), everyone, axis=0, tiled=True)
+    d_gate, d_up, d_down = grads_call(x_all, g_all, both, scaled)
+    home = lax.dynamic_slice(scores.reshape(tp, owners, total), (0, 0, me * tok_rows), (tp, owners, tok_rows))
+    home = jnp.sum(home, axis=0).T
+    d_probs = jnp.sum(jnp.where(chosen, home[:, None, :], 0.0), axis=2)
+    return d_tok, d_probs, d_gate, d_up, d_down
+
+
+def per_device(tokens, out_grad, routes, probs, w_gate, w_up, w_down):
+    owners = lax.axis_size(("role", "ep"))
+    tok_rows, top_count = routes.shape
+    if 2 * slot_capacity(tok_rows, top_count, owners) >= tok_rows:
+        return dense_device(tokens, out_grad, routes, probs, w_gate, w_up, w_down)
+    return routed_device(tokens, out_grad, routes, probs, w_gate, w_up, w_down)
+
+
 def solution(mesh):
     in_specs = (
         P(("groups", "role", "ep"), "tp"),

time: 367 us -> 1230 us (3.35)
  the two profiles are of different devices: /device:TPU:0 before, /device:TPU:20 now
where the time goes in v1:
time: 1230 us
  blocking collectives  1020 us (83%)
  waiting for transfers between devices  128 us (10%)
  Pallas kernels  41 us (3%)
  other arithmetic  18.3 us (1%)
  between operations  13.8 us (1%)
    all_gather x1, blocking collectives, dense_device(): lax.all_gather(score.reshape(1, total), everyone, axis=0, tiled=True)  991 us
    all_gather x1, waiting for transfers between devices, dense_device(): lax.all_gather(out_grad, everyone, axis=0, tiled=True)  79 us
    all_gather x1, waiting for transfers between devices, dense_device(): lax.all_gather(tokens, everyone, axis=0, tiled=True)  47.6 us
    all_gather x1, blocking collectives, dense_device(): lax.all_gather(table.astype(jnp.bfloat16), ('role', 'ep'), axis=0, tiled=...  32.3 us
    pallas_call x1, Pallas kernels, rows_call(): pl.pallas_call(rows_kernel, grid=grid, in_specs=[moving, moving, pl.Block...  26.6 us
  transfers between devices with their start and end apart: 3, of which 2 were waited for; matrix products, arithmetic and copies ran while one was open for 2% of the time, Pallas kernels for 1%

profile of v1, /device:TPU:20, one launch (start us, length us, event | category | flops | bytes accessed | tf_op | source)
XLA Modules:
  0.0 1229.7 jit_solution(14337891934448648201)
XLA Ops:
  7.2 0.0 all-gather.4.cloned.1.call-start
  7.2 0.7 all-gather.4.cloned.1.call-update
  7.9 0.0 all-gather.6.cloned.1.call-start
  7.9 0.7 all-gather.6.cloned.1.call-update
  8.6 0.0 reduce-scatter.2.cloned.1.call-start
  8.7 0.7 convert_element_type.10
  9.4 0.7 select_reduce_fusion.1
  10.1 0.1 copy.20
  10.2 32.3 %all_gather.14 = bf16[2048,16]{1,0:T(8,128)(2,1)S(1)} all-gather(bf16[128,16]{1,0:T(8,128)(2,1)S(1)} %copy.20), channel_id=1, replica_groups=mesh['groups'=1,'role'=2,'ep'=8,'tp'=2] {'role','ep'}, dimensions={0}, use_global_device_ids=true | all-gather | bytes 69632 | tf_op jit(solution)/shard_map/all_gather | solution.py:238
  42.5 0.2 dynamic-slice_convert_fusion.p_ref
  42.7 47.6 %all-gather.4.cloned.1.call-done = bf16[4096,1024]{1,0:T(8,128)(2,1)} async-done(((bf16[128,1024]{1,0:T(8,128)(2,1)}), bf16[4096,1024]{1,0:T(8,128)(2,1)}) %all-gather.4.cloned.1.call-update) | async-done | bytes 8388624 | tf_op jit(solution)/shard_map/all_gather | solution.py:240
  90.3 79.0 %all-gather.6.cloned.1.call-done = bf16[4096,1024]{1,0:T(8,128)(2,1)} async-done(((bf16[128,1024]{1,0:T(8,128)(2,1)}), bf16[4096,1024]{1,0:T(8,128)(2,1)}) %all-gather.6.cloned.1.call-update) | async-done | bytes 8388624 | tf_op jit(solution)/shard_map/all_gather | solution.py:241
  169.3 0.0 copy-start
  169.3 1.4 copy-done
  170.7 26.6 %rows.1 = (bf16[2048,768]{1,0:T(8,128)(2,1)}, bf16[2048,384]{1,0:T(8,128)(2,1)S(1)}, f32[2048,1]{1,0:T(8,128)S(1)}, bf16[2,2048,1024]{2,1,0:T(8,128)(2,1)}) custom-call(bf16[2,2048,1024]{2,1,0:T(8,128)(2,1)} %bitcast.6, bf16[2,2048,1024]{2,1,0:T(8,128)(2,1)} %bitcast.8, f32[2048,1]{1,0:T(8,128)S(1)} %dynamic-slice_convert_fusion.p_ref, ...), custom_call_target="tpu_custom_call" | custom-call | flops 16106127360 | bytes 50331648 | tf_op jit(solution)/shard_map/rows/pallas_call | solution.py:159
  197.3 0.0 copy-start.2
  197.3 1.1 copy-done.2
  198.4 0.0 reduce-scatter.2.cloned.1.call-update
  198.4 991.4 %all-gather = f32[65536,1]{1,0:T(8,128)} all-gather(f32[2048,1]{1,0:T(8,128)S(1)} %get-tuple-element.13), channel_id=2, replica_groups=mesh['groups'=1,'role'=2,'ep'=8,'tp'=2] {'tp','role','ep'}, dimensions={0}, use_global_device_ids=true | all-gather | bytes 270336 | tf_op jit(solution)/shard_map/all_gather | solution.py:244
  1189.8 0.0 copy-start.4
  1189.8 0.0 copy-start.1
  1189.8 15.4 %reduce = f32[65536]{0:T(1024)S(1)} reduce(f32[65536,1]{1,0:T(8,128)} %all-gather, f32[]{:T(128)} %constant.25), dimensions={1}, to_apply=%all-gather.reduce_sub_computation | reduce | bytes 524292 | tf_op jit(solution)/shard_map/all_gather | solution.py:244
  1205.2 0.7 reshape.33
  1206.0 0.7 dynamic-slice_reduce_fusion
  1206.7 0.0 copy-done.4
  1206.7 0.6 select_reduce_fusion
  1207.3 0.0 copy-done.1
  1207.3 0.0 copy-start.3
  1207.3 1.4 copy-done.3
  1208.7 14.5 %grads.1 = (bf16[1,2048,384]{2,1,0:T(8,128)(2,1)}, bf16[1,2048,384]{2,1,0:T(8,128)(2,1)}, bf16[1,384,2048]{2,1,0:T(8,128)(2,1)}) custom-call(bf16[2,2048,1024]{2,1,0:T(8,128)(2,1)} %bitcast.7, bf16[2,2048,1024]{2,1,0:T(8,128)(2,1)} %bitcast.9, bf16[2048,768]{1,0:T(8,128)(2,1)S(1)} %copy-done.1, bf16[2048,384]{1,0:T(8,128)(2,1)S(1)} %copy-done.3), custom_call_target="tpu_custom_call" | custom-call | flops 9663676416 | bytes 25165824 | tf_op jit(solution)/shard_map/grads/pallas_call | solution.py:204
  1223.2 0.0 reduce-scatter.2.cloned.1.call-done
Async XLA Ops:
  7.2 83.1 %all-gather.4.cloned.1.call-start = ((), (), s32[]{:S(2)}) async-start(), calls=%async_computation.1 | async-start | bytes 8650752 | tf_op jit(solution)/shard_map/all_gather | solution.py:240
  7.9 161.4 %all-gather.6.cloned.1.call-start = ((), (), s32[]{:S(2)}) async-start(), calls=%async_computation.2 | async-start | bytes 8650752 | tf_op jit(solution)/shard_map/all_gather | solution.py:241
  8.6 1214.6 %reduce-scatter.2.cloned.1.call-start = ((), (), s32[]{:S(2)}) async-start(), calls=%async_computation.3 | async-start | bytes 8650752 | tf_op jit(solution)/shard_map/reduce_scatter | solution.py:243
  169.3 1.4 copy-start
  197.3 1.1 copy-start.2
  1189.8 16.9 %copy-start.4 = (s32[128,8]{0,1:T(8,128)S(1)}, s32[128,8]{0,1:T(8,128)}, u32[]{:S(2)}) copy-start(s32[128,8]{0,1:T(8,128)} %param.9) | copy-start | bytes 12292
  1189.8 17.5 %copy-start.1 = (bf16[2048,768]{1,0:T(8,128)(2,1)S(1)}, bf16[2048,768]{1,0:T(8,128)(2,1)}, u32[]{:S(2)}) copy-start(bf16[2048,768]{1,0:T(8,128)(2,1)} %get-tuple-element.14.both_ref) | copy-start | bytes 9437188
  1207.3 1.4 copy-start.3
Sparse Core Ops, SparseCore 0:
  11.0 79.2 all-gather.3
  93.3 75.9 all-gather.5
  198.6 481.0 reduce-scatter.1

commit v2 on v0

--- a/solution.py
+++ b/solution.py
@@ -1,6 +1,11 @@
+import functools
+import math
+
 import jax
 import jax.numpy as jnp
 from jax import lax
+from jax.experimental import pallas as pl
+from jax.experimental.pallas import tpu as pltpu
 from jax.sharding import PartitionSpec as P
 
 
@@ -8,7 +13,7 @@
     return jnp.concatenate([array, jnp.zeros((1, array.shape[1]), array.dtype)], 0)
 
 
-def per_device(tokens, out_grad, routes, probs, w_gate, w_up, w_down):
+def routed_device(tokens, out_grad, routes, probs, w_gate, w_up, w_down):
     owners = lax.axis_size(("role", "ep"))
     tok_rows, top_count = routes.shape
     width_full = w_gate.shape[1]
@@ -112,6 +117,235 @@
     )
 
 
+def slot_capacity(tok_rows, top_count, owners):
+    return min(tok_rows, tok_rows * top_count * 9 // (8 * owners))
+
+
+def rows_kernel(
+    tp_ref, x_ref, g_ref, p_ref, wg0, wg1, wu0, wu1, wd0, wd1, both_ref, scaled_ref, score_ref, keep_ref, send_ref, wgu
+):
+    part = wg0.shape[2]
+    half = x_ref.shape[2]
+
+    @pl.when(pl.program_id(0) == 0)
+    def _():
+        wgu[:half, :part] = wg0[0]
+        wgu[:half, part:] = wu0[0]
+        wgu[half:, :part] = wg1[0]
+        wgu[half:, part:] = wu1[0]
+
+    rows = jnp.dot(x_ref[0], wgu[:half], preferred_element_type=jnp.float32)
+    rows = rows + jnp.dot(x_ref[1], wgu[half:], preferred_element_type=jnp.float32)
+    back = lax.dot_general(g_ref[0], wd0[0], (((1,), (1,)), ((), ())), preferred_element_type=jnp.float32)
+    back = back + lax.dot_general(g_ref[1], wd1[0], (((1,), (1,)), ((), ())), preferred_element_type=jnp.float32)
+    gate, up = rows[:, :part], rows[:, part:]
+    sig = jax.nn.sigmoid(gate)
+    act = gate * sig
+    hidden = act * up
+    score_ref[...] = jnp.sum(hidden * back, axis=1, keepdims=True)
+    prob = p_ref[...]
+    hgrad = prob * back
+    both_ref[:, :part] = (hgrad * up * sig * (1.0 + gate * (1.0 - sig))).astype(jnp.bfloat16)
+    both_ref[:, part:] = (hgrad * act).astype(jnp.bfloat16)
+    scaled_ref[...] = (prob * hidden).astype(jnp.bfloat16)
+    both = both_ref[...]
+    for index in range(2):
+        low = lax.dot_general(
+            both, wgu[index * half : (index + 1) * half], (((1,), (1,)), ((), ())), preferred_element_type=jnp.float32
+        ).astype(jnp.bfloat16)
+
+        @pl.when(pl.program_id(0) == 0)
+        def _(low=low, index=index):
+            keep_ref[index] = low
+
+        @pl.when(pl.program_id(0) == 1)
+        def _(low=low, index=index):
+            send_ref[index] = low
+
+
+def rows_call(which, x_rows, g_rows, prob, w_gate, w_up, w_down):
+    _, total, half = x_rows.shape
+    _, width, part = w_gate.shape
+    step = total // 2
+    moving = pl.BlockSpec((2, step, half), lambda i, w: (0, i, 0))
+    fixed = pl.BlockSpec((2, step, half), lambda i, w: (0, 0, 0))
+    own_in = pl.BlockSpec((1, half, part), lambda i, w: (0, w[0], 0))
+    far_in = pl.BlockSpec((1, half, part), lambda i, w: (0, 1 - w[0], 0))
+    own_out = pl.BlockSpec((1, part, half), lambda i, w: (0, 0, w[0]))
+    far_out = pl.BlockSpec((1, part, half), lambda i, w: (0, 0, 1 - w[0]))
+    return pl.pallas_call(
+        rows_kernel,
+        grid_spec=pltpu.PrefetchScalarGridSpec(
+            num_scalar_prefetch=1,
+            grid=(2,),
+            in_specs=[
+                moving,
+                moving,
+                pl.BlockSpec((step, 1), lambda i, w: (i, 0)),
+                own_in,
+                far_in,
+                own_in,
+                far_in,
+                own_out,
+                far_out,
+            ],
+            out_specs=[
+                pl.BlockSpec((step, 2 * part), lambda i, w: (i, 0)),
+                pl.BlockSpec((step, part), lambda i, w: (i, 0)),
+                pl.BlockSpec((step, 1), lambda i, w: (i, 0)),
+                fixed,
+                fixed,
+            ],
+            scratch_shapes=[pltpu.VMEM((width, 2 * part), jnp.bfloat16)],
+        ),
+        out_shape=[
+            jax.ShapeDtypeStruct((total, 2 * part), jnp.bfloat16),
+            jax.ShapeDtypeStruct((total, part), jnp.bfloat16),
+            jax.ShapeDtypeStruct((total, 1), jnp.float32),
+            jax.ShapeDtypeStruct((2, step, half), jnp.bfloat16),
+            jax.ShapeDtypeStruct((2, step, half), jnp.bfloat16),
+        ],
+        compiler_params=pltpu.CompilerParams(vmem_limit_bytes=48 << 20),
+        cost_estimate=pl.CostEstimate(
+            flops=10 * total * width * part, bytes_accessed=6 * total * width + 6 * width * part, transcendentals=total * part
+        ),
+        name="rows",
+    )(which, x_rows, g_rows, prob, w_gate, w_gate, w_up, w_up, w_down, w_down)
+
+
+def grads_kernel(count, tp_ref, *refs):
+    x_refs, g_refs = refs[:count], refs[count : 2 * count]
+    both_refs, scaled_refs = refs[2 * count : 3 * count], refs[3 * count : 4 * count]
+    dg_ref, du_ref, dd_ref = refs[4 * count :]
+    part = scaled_refs[0].shape[1]
+    both, down = None, None
+    for x_ref, g_ref, both_ref, scaled_ref in zip(x_refs, g_refs, both_refs, scaled_refs):
+        term = lax.dot_general(x_ref[0], both_ref[...], (((0,), (0,)), ((), ())), preferred_element_type=jnp.float32)
+        both = term if both is None else both + term
+        term = lax.dot_general(scaled_ref[...], g_ref[0], (((0,), (0,)), ((), ())), preferred_element_type=jnp.float32)
+        down = term if down is None else down + term
+    dg_ref[0] = both[:, :part].astype(jnp.bfloat16)
+    du_ref[0] = both[:, part:].astype(jnp.bfloat16)
+    dd_ref[0] = down.astype(jnp.bfloat16)
+
+
+def grads_call(which, x_parts, g_parts, both_parts, scaled_parts):
+    count = len(x_parts)
+    _, total, half = x_parts[0].shape
+    part = scaled_parts[0].shape[1]
+    width = 2 * half
+    step = math.gcd(half, 256)
+    per = half // step
+
+    def place(i, w):
+        return jnp.where(i < per, w[0], 1 - w[0]) * per + i % per
+
+    moving = pl.BlockSpec((1, total, step), lambda i, w: (i // per, 0, i % per))
+    return pl.pallas_call(
+        functools.partial(grads_kernel, count),
+        grid_spec=pltpu.PrefetchScalarGridSpec(
+            num_scalar_prefetch=1,
+            grid=(width // step,),
+            in_specs=[moving] * (2 * count)
+            + [pl.BlockSpec((total, 2 * part), lambda i, w: (0, 0))] * count
+            + [pl.BlockSpec((total, part), lambda i, w: (0, 0))] * count,
+            out_specs=[
+                pl.BlockSpec((1, step, part), lambda i, w: (0, place(i, w), 0)),
+                pl.BlockSpec((1, step, part), lambda i, w: (0, place(i, w), 0)),
+                pl.BlockSpec((1, part, step), lambda i, w: (0, 0, place(i, w))),
+            ],
+        ),
+        out_shape=[
+            jax.ShapeDtypeStruct((1, width, part), jnp.bfloat16),
+            jax.ShapeDtypeStruct((1, width, part), jnp.bfloat16),
+            jax.ShapeDtypeStruct((1, part, width), jnp.bfloat16),
+        ],
+        compiler_params=pltpu.CompilerParams(vmem_limit_bytes=48 << 20),
+        cost_estimate=pl.CostEstimate(
+            flops=6 * count * total * width * part, bytes_accessed=6 * count * total * width, transcendentals=0
+        ),
+        name="grads",
+    )(which, *x_parts, *g_parts, *both_parts, *scaled_parts)
+
+
+def dense_device(tokens, out_grad, routes, probs, w_gate, w_up, w_down):
+    owners = lax.axis_size(("role", "ep"))
+    ep = lax.axis_size("ep")
+    n_y = 2
+    n_z = ep // n_y
+    tok_rows, half = tokens.shape
+    me = lax.axis_index(("role", "ep"))
+    role, place, which = lax.axis_index("role"), lax.axis_index("ep"), lax.axis_index("tp")
+    my_z, my_y = place // n_y, place % n_y
+
+    def over_x(array):
+        return lax.ppermute(array, "tp", [(0, 1), (1, 0)])
+
+    def over_role(array):
+        return lax.ppermute(array, "role", [(0, 1), (1, 0)])
+
+    def over_y(array):
+        return lax.ppermute(array, "ep", [(i, i + 1 - 2 * (i % n_y)) for i in range(ep)])
+
+    def over_z(array, shift):
+        return lax.ppermute(array, "ep", [(i, (i + shift * n_y) % ep) for i in range(ep)])
+
+    steps = jnp.arange(n_z)[:, None, None]
+    source = (role + jnp.arange(2)[None, :, None]) % 2 * ep + (my_z - steps) % n_z * n_y + (my_y + jnp.arange(n_y)) % n_y
+    source = source.reshape(-1)
+
+    chosen = routes[:, :, None] == jnp.arange(owners, dtype=jnp.int32)
+    table = jnp.sum(jnp.where(chosen, probs[:, :, None].astype(jnp.float32), 0.0), axis=1)
+    table_all = lax.all_gather(table.astype(jnp.bfloat16).T, ("role", "ep"), axis=0)
+    prob = lax.dynamic_slice(table_all, (0, me, 0), (owners, 1, tok_rows)).reshape(owners, tok_rows)
+    prob = prob[source].astype(jnp.float32).reshape(n_z, 2 * n_y * tok_rows, 1)
+
+    x_own, g_own = tokens, jnp.stack([out_grad, over_x(out_grad)])
+    x_parts, g_parts = [], []
+    for step in range(n_z):
+        if step:
+            x_own, g_own = over_z(x_own, 1), over_z(g_own, 1)
+        pair = jnp.concatenate([x_own, over_y(x_own)], 0)
+        full = jnp.stack([pair, over_x(pair)])
+        x_parts.append(jnp.concatenate([full, over_role(full)], 1))
+        full = jnp.concatenate([g_own, over_y(g_own)], 1)
+        g_parts.append(jnp.concatenate([full, over_role(full)], 1))
+
+    which_ref = which.reshape(1).astype(jnp.int32)
+    both_parts, scaled_parts, scores, homeward = [], [], [], []
+    for step in range(n_z):
+        both, scaled, score, keep, send = rows_call(
+            which_ref, x_parts[step], g_parts[step], prob[step], w_gate, w_up, w_down
+        )
+        both_parts.append(both)
+        scaled_parts.append(scaled)
+        scores.append(score)
+        total = keep.astype(jnp.float32) + over_role(send).astype(jnp.float32)
+        total = total[0] + over_x(total[1].astype(jnp.bfloat16)).astype(jnp.float32)
+        total = total[:tok_rows] + over_y(total[tok_rows:].astype(jnp.bfloat16)).astype(jnp.float32)
+        homeward.append(over_z(total.astype(jnp.bfloat16), -step).astype(jnp.float32) if step else total)
+    d_tok = sum(homeward[1:], homeward[0]).astype(jnp.bfloat16)
+    d_gate, d_up, d_down = grads_call(which_ref, x_parts, g_parts, both_parts, scaled_parts)
+
+    mine = jnp.concatenate(scores, 0).reshape(owners, tok_rows)
+    placed = (jnp.arange(owners)[:, None] == source[None, :]).astype(jnp.float32)
+    mine = jnp.sum(placed[:, :, None] * mine[None], axis=1)
+    scores = lax.all_gather(mine, ("tp", "role", "ep"), axis=0)
+    home = lax.dynamic_slice(scores, (0, me, 0), (2 * owners, 1, tok_rows)).reshape(2, owners, tok_rows)
+    home = jnp.sum(home, axis=0).T
+    d_probs = jnp.sum(jnp.where(chosen, home[:, None, :], 0.0), axis=2)
+    return d_tok, d_probs, d_gate, d_up, d_down
+
+
+def per_device(tokens, out_grad, routes, probs, w_gate, w_up, w_down):
+    owners = lax.axis_size(("role", "ep"))
+    tok_rows, top_count = routes.shape
+    paired = lax.axis_size("tp") == 2 and lax.axis_size("role") == 2 and lax.axis_size("ep") % 2 == 0
+    if paired and 2 * slot_capacity(tok_rows, top_count, owners) >= tok_rows:
+        return dense_device(tokens, out_grad, routes, probs, w_gate, w_up, w_down)
+    return routed_device(tokens, out_grad, routes, probs, w_gate, w_up, w_down)
+
+
 def solution(mesh):
     in_specs = (
         P(("groups", "role", "ep"), "tp"),

time: 367 us -> 329 us (0.90)
  Pallas kernels: 0 us -> 55 us
  blocking collectives: 148 us -> 97.2 us
  matrix products: 34.4 us -> 0 us
  waiting for transfers between devices: 106 us -> 77.5 us
  starting transfers between devices: 5.8 us -> 25.6 us
  other arithmetic: 20.2 us -> 37.8 us
  between operations: 14 us -> 1.33 us
  local copies, waits for them, and re-layouts: 37.4 us -> 33 us
    all_to_all x4 -> x0, blocking collectives: 143 us -> none  [the longest x1 62.8 us: per_device(): lax.all_to_all(send_x.reshape(owners, capacity, tokens.shape[1]), ('role'...]
    all_gather x0 -> x2, blocking collectives: none -> 97.2 us  [the longest x1 67.5 us: dense_device(): scores = lax.all_gather(mine, ('tp', 'role', 'ep'), axis=0)]
    ppermute x0 -> x42, waiting for transfers between devices: none -> 77.5 us  [the longest x9 33.4 us: over_z(): lax.ppermute(array, 'ep', [(i, (i + shift * n_y) % ep) for i in range(ep)])]
    pallas_call x0 -> x5, Pallas kernels: none -> 55 us  [the longest x4 40.2 us: rows_call(): pl.pallas_call(rows_kernel, grid_spec=pltpu.PrefetchScalarGridSpec(num_sc...]
    reduce_scatter x1 -> x0, waiting for transfers between devices: 43.3 us -> none  [per_device(): lax.psum_scatter(partial_low.reshape(owners, capacity, width_full), 'tp',...]
    all_gather x2 -> x0, waiting for transfers between devices: 34.5 us -> none  [the longest x1 34.5 us: per_device(): lax.all_gather(slice_g, 'tp', axis=2, tiled=True)]
    dot_general x5 -> x0, matrix products: 34.4 us -> none  [the longest x1 8.92 us: per_device(): both_rows = jnp.dot(rows_x, gate_up, preferred_element_type=jnp.float32)]
    all_to_all x1 -> x0, waiting for transfers between devices: 28 us -> none  [per_device(): lax.all_to_all(summed_low, ('role', 'ep'), split_axis=0, concat_axis=0, t...]
  transfers between devices with their start and end apart: 4 -> 42, of which waited for: 3 -> 14; matrix products, arithmetic and copies ran while one was open for 12% -> 18% of each run, Pallas kernels for 0% -> 17%
where the time goes in v2:
time: 329 us; the launch traced here: 327 us
  blocking collectives  97.2 us (30%)
  waiting for transfers between devices  77.5 us (24%)
  Pallas kernels  55 us (17%)
  other arithmetic  37.8 us (11%)
  local copies, waits for them, and re-layouts  33 us (10%)
  starting transfers between devices  25.6 us (8%)
    all_gather x1, blocking collectives, dense_device(): scores = lax.all_gather(mine, ('tp', 'role', 'ep'), axis=0)  67.5 us
    pallas_call x4, Pallas kernels, rows_call(): pl.pallas_call(rows_kernel, grid_spec=pltpu.PrefetchScalarGridSpec(num_sc...  40.2 us
    ppermute x9, waiting for transfers between devices, over_z(): lax.ppermute(array, 'ep', [(i, (i + shift * n_y) % ep) for i in range(ep)])  33.4 us
    all_gather x1, blocking collectives, dense_device(): lax.all_gather(table.astype(jnp.bfloat16).T, ('role', 'ep'), axis=0)  29.7 us
    ppermute x12, waiting for transfers between devices, over_y(): lax.ppermute(array, 'ep', [(i, i + 1 - 2 * (i % n_y)) for i in range(ep)])  24.2 us
    unnamed x99, local copies, waits for them, and re-layouts  21.2 us
    ppermute x9, waiting for transfers between devices, over_x(): return lax.ppermute(array, 'tp', [(0, 1), (1, 0)])  19.8 us
    pallas_call x1, Pallas kernels, grads_call(): pl.pallas_call(functools.partial(grads_kernel, count), grid_spec=pltpu.Pr...  14.7 us
  transfers between devices with their start and end apart: 42, of which 14 were waited for; matrix products, arithmetic and copies ran while one was open for 18% of the time, Pallas kernels for 17%

profile of v2, /device:TPU:0, one launch (start us, length us, event | category | flops | bytes accessed | tf_op | source)
XLA Modules:
  0.0 327.3 jit_solution(2021263037022731805)
XLA Ops:
  0.6 3.0 collective-permute-start
  3.7 1.6 collective-permute-start.9
  5.2 1.5 collective-permute-start.3
  8.1 29.7 %all-gather = bf16[256,128]{1,0:T(8,128)(2,1)S(1)} all-gather(bf16[16,128]{1,0:T(8,128)(2,1)S(1)} %bitcast.80), channel_id=2, replica_groups=mesh['groups'=1,'role'=2,'ep'=8,'tp'=2] {'role','ep'}, dimensions={0}, use_global_device_ids=true | all-gather | bytes 69632 | tf_op jit(solution)/shard_map/all_gather | solution.py:299
  38.9 1.8 pad_maximum_fusion.13
  44.4 1.6 collective-permute-start.1
  47.0 6.2 %collective-permute-done.20 = bf16[128,1024]{1,0:T(8,128)(2,1)} collective-permute-done((bf16[128,1024]{1,0:T(8,128)(2,1)}, bf16[128,1024]{1,0:T(8,128)(2,1)}, u32[]{:S(2)}, u32[]{:S(2)}) %collective-permute-start.20) | collective-permute-done | bytes 262176 | tf_op jit(solution)/shard_map/ppermute | solution.py:291
  54.9 6.0 %collective-permute-done.10 = bf16[128,1024]{1,0:T(8,128)(2,1)S(1)} collective-permute-done((bf16[128,1024]{1,0:T(8,128)(2,1)}, bf16[128,1024]{1,0:T(8,128)(2,1)S(1)}, u32[]{:S(2)}, u32[]{:S(2)}) %collective-permute-start.10) | collective-permute-done | bytes 262176 | tf_op jit(solution)/shard_map/ppermute | solution.py:288
  61.0 1.9 collective-permute-start.11
  63.0 3.6 %collective-permute-done.21 = bf16[128,1024]{1,0:T(8,128)(2,1)S(1)} collective-permute-done((bf16[128,1024]{1,0:T(8,128)(2,1)}, bf16[128,1024]{1,0:T(8,128)(2,1)S(1)}, u32[]{:S(2)}, u32[]{:S(2)}) %collective-permute-start.21) | collective-permute-done | bytes 262176 | tf_op jit(solution)/shard_map/ppermute | solution.py:288
  67.8 4.2 %collective-permute-done.31 = bf16[128,1024]{1,0:T(8,128)(2,1)S(1)} collective-permute-done((bf16[128,1024]{1,0:T(8,128)(2,1)}, bf16[128,1024]{1,0:T(8,128)(2,1)S(1)}, u32[]{:S(2)}, u32[]{:S(2)}) %collective-permute-start.31) | collective-permute-done | bytes 262176 | tf_op jit(solution)/shard_map/ppermute | solution.py:291
  72.1 8.0 %collective-permute-done.32 = bf16[128,1024]{1,0:T(8,128)(2,1)S(1)} collective-permute-done((bf16[128,1024]{1,0:T(8,128)(2,1)S(1)}, bf16[128,1024]{1,0:T(8,128)(2,1)S(1)}, u32[]{:S(2)}, u32[]{:S(2)}) %collective-permute-start.32) | collective-permute-done | bytes 262176 | tf_op jit(solution)/shard_map/ppermute | solution.py:288
  81.8 5.8 %collective-permute-done.24 = bf16[2,128,1024]{2,1,0:T(8,128)(2,1)} collective-permute-done((bf16[2,128,1024]{2,1,0:T(8,128)(2,1)S(1)}, bf16[2,128,1024]{2,1,0:T(8,128)(2,1)}, u32[]{:S(2)}, u32[]{:S(2)}) %collective-permute-start.24) | collective-permute-done | bytes 524320 | tf_op jit(solution)/shard_map/ppermute | solution.py:291
  87.6 1.9 constant_dynamic-update-slice_fusion.11
  90.6 2.5 collective-permute-done.14
  94.3 6.4 %collective-permute-done.33 = bf16[256,1024]{1,0:T(8,128)(2,1)} collective-permute-done((bf16[256,1024]{1,0:T(8,128)(2,1)S(1)}, bf16[256,1024]{1,0:T(8,128)(2,1)}, u32[]{:S(2)}, u32[]{:S(2)}) %collective-permute-start.33) | collective-permute-done | bytes 524320 | tf_op jit(solution)/shard_map/ppermute | solution.py:282
  100.6 2.1 pad_maximum_fusion.11
  102.8 1.5 pad_maximum_fusion.1.g_ref.refs_4_
  104.3 1.5 collective-permute-start.25
  105.8 1.6 pad_maximum_fusion.x_ref.refs_0_
  107.4 10.0 %rows.4 = (bf16[512,768]{1,0:T(8,128)(2,1)S(1)}, bf16[512,384]{1,0:T(8,128)(2,1)S(1)}, f32[512,1]{1,0:T(8,128)S(1)}, bf16[2,256,1024]{2,1,0:T(8,128)(2,1)S(1)}, bf16[2,256,1024]{2,1,0:T(8,128)(2,1)}) custom-call(s32[1]{0:T(128)} %bitcast.tp_ref, bf16[2,512,1024]{2,1,0:T(8,128)(2,1)} %pad_maximum_fusion.x_ref.refs_0_, ...), custom_call_target="tpu_custom_call" | custom-call | flops 4026531840 | bytes 11010048 | tf_op jit(solution)/shard_map/rows/pallas_call | solution.py:176
  119.2 1.9 constant_dynamic-update-slice_fusion.16
  121.6 1.9 constant_dynamic-update-slice_fusion.10
  123.5 2.3 pad_maximum_fusion.10
  125.9 2.9 pad_maximum_fusion.2.x_ref.refs_1_
  132.9 10.1 %rows.5 = (bf16[512,768]{1,0:T(8,128)(2,1)S(1)}, bf16[512,384]{1,0:T(8,128)(2,1)S(1)}, f32[512,1]{1,0:T(8,128)S(1)}, bf16[2,256,1024]{2,1,0:T(8,128)(2,1)S(1)}, bf16[2,256,1024]{2,1,0:T(8,128)(2,1)}) custom-call(s32[1]{0:T(128)} %bitcast.tp_ref, bf16[2,512,1024]{2,1,0:T(8,128)(2,1)} %pad_maximum_fusion.2.x_ref.refs_1_, bf16[2,512,1024]{2,1,0:T(8,128)(2,1)} %copy-done.40, ...), custom_call_target="tpu_custom_call" | custom-call | flops 4026531840 | bytes 11010048 | tf_op jit(solution)/shard_map/rows/pallas_call | solution.py:176
  143.4 2.7 pad_maximum_fusion.3.x_ref.refs_2_
  146.2 2.3 pad_maximum_fusion.12
  148.8 1.9 constant_dynamic-update-slice_fusion.15
  150.7 3.1 pad_maximum_fusion.4.x_ref.refs_3_
  153.8 1.6 convert_add_fusion.3
  156.9 2.3 constant_dynamic-update-slice_fusion.9.g_ref.refs_6_
  159.2 10.0 %rows.6 = (bf16[512,768]{1,0:T(8,128)(2,1)S(1)}, bf16[512,384]{1,0:T(8,128)(2,1)S(1)}, f32[512,1]{1,0:T(8,128)S(1)}, bf16[2,256,1024]{2,1,0:T(8,128)(2,1)S(1)}, bf16[2,256,1024]{2,1,0:T(8,128)(2,1)}) custom-call(s32[1]{0:T(128)} %bitcast.tp_ref, bf16[2,512,1024]{2,1,0:T(8,128)(2,1)} %pad_maximum_fusion.3.x_ref.refs_2_, ...), custom_call_target="tpu_custom_call" | custom-call | flops 4026531840 | bytes 11010048 | tf_op jit(solution)/shard_map/rows/pallas_call | solution.py:176
  171.7 2.4 constant_dynamic-update-slice_fusion.14.g_ref.refs_7_
  174.1 10.1 %rows.7 = (bf16[512,768]{1,0:T(8,128)(2,1)S(1)}, bf16[512,384]{1,0:T(8,128)(2,1)S(1)}, f32[512,1]{1,0:T(8,128)S(1)}, bf16[2,256,1024]{2,1,0:T(8,128)(2,1)S(1)}, bf16[2,256,1024]{2,1,0:T(8,128)(2,1)}) custom-call(s32[1]{0:T(128)} %bitcast.tp_ref, bf16[2,512,1024]{2,1,0:T(8,128)(2,1)} %pad_maximum_fusion.4.x_ref.refs_3_, ...), custom_call_target="tpu_custom_call" | custom-call | flops 4026531840 | bytes 11010048 | tf_op jit(solution)/shard_map/rows/pallas_call | solution.py:176
  184.6 1.8 convert_add_fusion.2
  187.4 1.5 collective-permute-start.17
  198.6 14.7 %grads.1 = (bf16[1,2048,384]{2,1,0:T(8,128)(2,1)}, bf16[1,2048,384]{2,1,0:T(8,128)(2,1)}, bf16[1,384,2048]{2,1,0:T(8,128)(2,1)}) custom-call(s32[1]{0:T(128)} %bitcast.tp_ref, bf16[2,512,1024]{2,1,0:T(8,128)(2,1)} %pad_maximum_fusion.x_ref.refs_0_, bf16[2,512,1024]{2,1,0:T(8,128)(2,1)} %pad_maximum_fusion.2.x_ref.refs_1_, ...), custom_call_target="tpu_custom_call" | custom-call | flops 9663676416 | bytes 25165824 | tf_op jit(solution)/shard_map/grads/pallas_call | solution.py:244
  213.5 67.5 %all-gather.1 = f32[512,128]{1,0:T(8,128)S(1)} all-gather(f32[16,128]{1,0:T(8,128)S(1)} %multiply_reduce_fusion), channel_id=3, replica_groups=mesh['groups'=1,'role'=2,'ep'=8,'tp'=2] {'tp','role','ep'}, dimensions={0}, use_global_device_ids=true | all-gather | bytes 270336 | tf_op jit(solution)/shard_map/all_gather | solution.py:333
  281.0 1.6 convert_add_fusion.1
  282.7 1.5 collective-permute-start.28
  284.1 1.8 convert_add_fusion
  288.0 8.0 %collective-permute-done.28 = bf16[256,1024]{1,0:T(8,128)(2,1)S(1)} collective-permute-done((bf16[256,1024]{1,0:T(8,128)(2,1)S(1)}, bf16[256,1024]{1,0:T(8,128)(2,1)S(1)}, u32[]{:S(2)}, u32[]{:S(2)}) %collective-permute-start.28) | collective-permute-done | bytes 524320 | tf_op jit(solution)/shard_map/ppermute | solution.py:282
  296.3 5.3 %collective-permute-done.39 = bf16[256,1024]{1,0:T(8,128)(2,1)S(1)} collective-permute-done((bf16[256,1024]{1,0:T(8,128)(2,1)S(1)}, bf16[256,1024]{1,0:T(8,128)(2,1)S(1)}, u32[]{:S(2)}, u32[]{:S(2)}) %collective-permute-start.39) | collective-permute-done | bytes 524320 | tf_op jit(solution)/shard_map/ppermute | solution.py:282
  302.0 1.5 collective-permute-start.19
  304.1 4.2 %collective-permute-done.40 = bf16[128,1024]{1,0:T(8,128)(2,1)S(1)} collective-permute-done((bf16[128,1024]{1,0:T(8,128)(2,1)S(1)}, bf16[128,1024]{1,0:T(8,128)(2,1)S(1)}, u32[]{:S(2)}, u32[]{:S(2)}) %collective-permute-start.40) | collective-permute-done | bytes 262176 | tf_op jit(solution)/shard_map/ppermute | solution.py:288
  310.2 15.3 %collective-permute-done.30 = bf16[128,1024]{1,0:T(8,128)(2,1)S(1)} collective-permute-done((bf16[128,1024]{1,0:T(8,128)(2,1)S(1)}, bf16[128,1024]{1,0:T(8,128)(2,1)S(1)}, u32[]{:S(2)}, u32[]{:S(2)}) %collective-permute-start.30) | collective-permute-done | bytes 262176 | tf_op jit(solution)/shard_map/ppermute | solution.py:291
  325.5 1.8 fusion.14
  (210 shorter events, 41.8 us)
Async XLA Ops:
  0.6 43.8 %collective-permute-start = (bf16[128,1024]{1,0:T(8,128)(2,1)}, bf16[128,1024]{1,0:T(8,128)(2,1)S(1)}, u32[]{:S(2)}, u32[]{:S(2)}) collective-permute-start(bf16[128,1024]{1,0:T(8,128)(2,1)} %param.7), channel_id=1, source_target_pairs={{0,2},{2,0},{4,6},{6,4},{8,10},{10,8},{12,14},{14,12},{1,3},{3,1},... | collective-permute-start | bytes 786440 | tf_op jit(solution)/shard_map/ppermute | solution.py:288
  3.7 38.3 %collective-permute-start.9 = (bf16[128,1024]{1,0:T(8,128)(2,1)}, bf16[128,1024]{1,0:T(8,128)(2,1)}, u32[]{:S(2)}, u32[]{:S(2)}) collective-permute-start(bf16[128,1024]{1,0:T(8,128)(2,1)} %param.7), channel_id=1, source_target_pairs={{0,4},{2,6},{4,8},{6,10},{8,12},{10,14},{12,0},{14,2},{1,5},{3,7},... | collective-permute-start | bytes 786440 | tf_op jit(solution)/shard_map/ppermute | solution.py:291
  5.2 33.6 %collective-permute-start.3 = (bf16[128,1024]{1,0:T(8,128)(2,1)}, bf16[128,1024]{1,0:T(8,128)(2,1)S(1)}, u32[]{:S(2)}, u32[]{:S(2)}) collective-permute-start(bf16[128,1024]{1,0:T(8,128)(2,1)} %param.8), channel_id=1, source_target_pairs={{0,1},{1,0},{2,3},{3,2},{4,5},{5,4},{6,7},{7,6},{8,9},{9,8},{10,11... | collective-permute-start | bytes 786440 | tf_op jit(solution)/shard_map/ppermute | solution.py:282
  40.7 22.2 %copy-start.31 = (bf16[128,1024]{1,0:T(8,128)(2,1)S(1)}, bf16[128,1024]{1,0:T(8,128)(2,1)}, u32[]{:S(2)}) copy-start(bf16[128,1024]{1,0:T(8,128)(2,1)} %param.8) | copy-start | bytes 786436
  40.7 20.3 %collective-permute-start.4 = (bf16[2,128,1024]{2,1,0:T(8,128)(2,1)}, bf16[2,128,1024]{2,1,0:T(8,128)(2,1)S(1)}, u32[]{:S(2)}, u32[]{:S(2)}) collective-permute-start(bf16[2,128,1024]{2,1,0:T(8,128)(2,1)} %pad_maximum_fusion.13), channel_id=1, source_target_pairs={{0,2},{2,0},{4,6},{6,4},{8,10},{10,8},{12,14},{14,12},{1,3},{3,1},... | collective-permute-start | bytes 1572872 | tf_op jit(solution)/shard_map/ppermute | solution.py:288
  42.0 11.3 %collective-permute-start.20 = (bf16[128,1024]{1,0:T(8,128)(2,1)}, bf16[128,1024]{1,0:T(8,128)(2,1)}, u32[]{:S(2)}, u32[]{:S(2)}) collective-permute-start(bf16[128,1024]{1,0:T(8,128)(2,1)} %collective-permute-done.9), channel_id=1, source_target_pairs={{0,4},{2,6},{4,8},{6,10},{8,12},{10,14},{12,0},{14,2},{1,5},{3,7},... | collective-permute-start | bytes 786440 | tf_op jit(solution)/shard_map/ppermute | solution.py:291
  43.6 28.4 %collective-permute-start.13 = (bf16[2,128,1024]{2,1,0:T(8,128)(2,1)}, bf16[2,128,1024]{2,1,0:T(8,128)(2,1)S(1)}, u32[]{:S(2)}, u32[]{:S(2)}) collective-permute-start(bf16[2,128,1024]{2,1,0:T(8,128)(2,1)} %pad_maximum_fusion.13), channel_id=1, source_target_pairs={{0,4},{2,6},{4,8},{6,10},{8,12},{10,14},{12,0},{14,2},{1,5},{3,7},... | collective-permute-start | bytes 1572872 | tf_op jit(solution)/shard_map/ppermute | solution.py:291
  43.7 17.3 %collective-permute-start.10 = (bf16[128,1024]{1,0:T(8,128)(2,1)}, bf16[128,1024]{1,0:T(8,128)(2,1)S(1)}, u32[]{:S(2)}, u32[]{:S(2)}) collective-permute-start(bf16[128,1024]{1,0:T(8,128)(2,1)} %collective-permute-done.9), channel_id=1, source_target_pairs={{0,2},{2,0},{4,6},{6,4},{8,10},{10,8},{12,14},{14,12},{1,3},{3,1},... | collective-permute-start | bytes 786440 | tf_op jit(solution)/shard_map/ppermute | solution.py:288
  44.4 22.6 %collective-permute-start.1 = (bf16[256,1024]{1,0:T(8,128)(2,1)S(1)}, bf16[256,1024]{1,0:T(8,128)(2,1)S(1)}, u32[]{:S(2)}, u32[]{:S(2)}) collective-permute-start(bf16[256,1024]{1,0:T(8,128)(2,1)S(1)} %constant_dynamic-update-slice_fusion), channel_id=1, source_target_pairs={{0,1},{1,0},{2,3},{3,2},{4,5},{5,4},{6,7},{7,6},{8,9},{9,8},{10,11... | collective-permute-start | bytes 1572872 | tf_op jit(solution)/shard_map/ppermute | solution.py:282
  53.3 13.3 %collective-permute-start.21 = (bf16[128,1024]{1,0:T(8,128)(2,1)}, bf16[128,1024]{1,0:T(8,128)(2,1)S(1)}, u32[]{:S(2)}, u32[]{:S(2)}) collective-permute-start(bf16[128,1024]{1,0:T(8,128)(2,1)} %collective-permute-done.20), channel_id=1, source_target_pairs={{0,2},{2,0},{4,6},{6,4},{8,10},{10,8},{12,14},{14,12},{1,3},{3,1},... | collective-permute-start | bytes 786440 | tf_op jit(solution)/shard_map/ppermute | solution.py:288
  60.9 11.0 %collective-permute-start.31 = (bf16[128,1024]{1,0:T(8,128)(2,1)}, bf16[128,1024]{1,0:T(8,128)(2,1)S(1)}, u32[]{:S(2)}, u32[]{:S(2)}) collective-permute-start(bf16[128,1024]{1,0:T(8,128)(2,1)} %collective-permute-done.20), channel_id=1, source_target_pairs={{0,4},{2,6},{4,8},{6,10},{8,12},{10,14},{12,0},{14,2},{1,5},{3,7},... | collective-permute-start | bytes 786440 | tf_op jit(solution)/shard_map/ppermute | solution.py:291
  61.0 19.4 %collective-permute-start.11 = (bf16[256,1024]{1,0:T(8,128)(2,1)S(1)}, bf16[256,1024]{1,0:T(8,128)(2,1)S(1)}, u32[]{:S(2)}, u32[]{:S(2)}) collective-permute-start(bf16[256,1024]{1,0:T(8,128)(2,1)S(1)} %constant_dynamic-update-slice_fusion.2), channel_id=1, source_target_pairs={{0,1},{1,0},{2,3},{3,2},{4,5},{5,4},{6,7},{7,6},{8,9},{9,8},{10,11... | collective-permute-start | bytes 1572872 | tf_op jit(solution)/shard_map/ppermute | solution.py:282
  66.6 36.2 %collective-permute-start.5 = (bf16[2,256,1024]{2,1,0:T(8,128)(2,1)S(1)}, bf16[2,256,1024]{2,1,0:T(8,128)(2,1)S(1)}, u32[]{:S(2)}, u32[]{:S(2)}) collective-permute-start(bf16[2,256,1024]{2,1,0:T(8,128)(2,1)S(1)} %pad_maximum_fusion.6), channel_id=1, source_target_pairs={{0,16},{16,0},{1,17},{17,1},{2,18},{18,2},{3,19},{19,3},{4,20},{20... | collective-permute-start | bytes 3145736 | tf_op jit(solution)/shard_map/ppermute | solution.py:285
  67.0 22.5 %copy-start.26 = (bf16[256,1024]{1,0:T(8,128)(2,1)}, bf16[256,1024]{1,0:T(8,128)(2,1)S(1)}, u32[]{:S(2)}) copy-start(bf16[256,1024]{1,0:T(8,128)(2,1)S(1)} %constant_dynamic-update-slice_fusion.7) | copy-start | bytes 1572868
  67.1 22.4 %collective-permute-start.22 = (bf16[256,1024]{1,0:T(8,128)(2,1)S(1)}, bf16[256,1024]{1,0:T(8,128)(2,1)S(1)}, u32[]{:S(2)}, u32[]{:S(2)}) collective-permute-start(bf16[256,1024]{1,0:T(8,128)(2,1)S(1)} %constant_dynamic-update-slice_fusion.7), channel_id=1, source_target_pairs={{0,1},{1,0},{2,3},{3,2},{4,5},{5,4},{6,7},{7,6},{8,9},{9,8},{10,11... | collective-permute-start | bytes 1572872 | tf_op jit(solution)/shard_map/ppermute | solution.py:282
  72.0 8.1 %collective-permute-start.32 = (bf16[128,1024]{1,0:T(8,128)(2,1)S(1)}, bf16[128,1024]{1,0:T(8,128)(2,1)S(1)}, u32[]{:S(2)}, u32[]{:S(2)}) collective-permute-start(bf16[128,1024]{1,0:T(8,128)(2,1)S(1)} %collective-permute-done.31), channel_id=1, source_target_pairs={{0,2},{2,0},{4,6},{6,4},{8,10},{10,8},{12,14},{14,12},{1,3},{3,1},... | collective-permute-start | bytes 786440 | tf_op jit(solution)/shard_map/ppermute | solution.py:288
  72.0 15.7 %collective-permute-start.24 = (bf16[2,128,1024]{2,1,0:T(8,128)(2,1)S(1)}, bf16[2,128,1024]{2,1,0:T(8,128)(2,1)}, u32[]{:S(2)}, u32[]{:S(2)}) collective-permute-start(bf16[2,128,1024]{2,1,0:T(8,128)(2,1)S(1)} %collective-permute-done.13), channel_id=1, source_target_pairs={{0,4},{2,6},{4,8},{6,10},{8,12},{10,14},{12,0},{14,2},{1,5},{3,7},... | collective-permute-start | bytes 1572872 | tf_op jit(solution)/shard_map/ppermute | solution.py:291
  80.1 13.0 %collective-permute-start.14 = (bf16[2,128,1024]{2,1,0:T(8,128)(2,1)S(1)}, bf16[2,128,1024]{2,1,0:T(8,128)(2,1)S(1)}, u32[]{:S(2)}, u32[]{:S(2)}) collective-permute-start(bf16[2,128,1024]{2,1,0:T(8,128)(2,1)S(1)} %collective-permute-done.13), channel_id=1, source_target_pairs={{0,2},{2,0},{4,6},{6,4},{8,10},{10,8},{12,14},{14,12},{1,3},{3,1},... | collective-permute-start | bytes 1572872 | tf_op jit(solution)/shard_map/ppermute | solution.py:288
  80.4 23.9 %collective-permute-start.2 = (bf16[2,256,1024]{2,1,0:T(8,128)(2,1)S(1)}, bf16[2,256,1024]{2,1,0:T(8,128)(2,1)S(1)}, u32[]{:S(2)}, u32[]{:S(2)}) collective-permute-start(bf16[2,256,1024]{2,1,0:T(8,128)(2,1)S(1)} %pad_maximum_fusion.5), channel_id=1, source_target_pairs={{0,16},{16,0},{1,17},{17,1},{2,18},{18,2},{3,19},{19,3},{4,20},{20... | collective-permute-start | bytes 3145736 | tf_op jit(solution)/shard_map/ppermute | solution.py:285
  80.5 23.8 %copy-start.28 = (bf16[256,1024]{1,0:T(8,128)(2,1)}, bf16[256,1024]{1,0:T(8,128)(2,1)S(1)}, u32[]{:S(2)}) copy-start(bf16[256,1024]{1,0:T(8,128)(2,1)S(1)} %constant_dynamic-update-slice_fusion.12) | copy-start | bytes 1572868
  87.6 13.0 %collective-permute-start.33 = (bf16[256,1024]{1,0:T(8,128)(2,1)S(1)}, bf16[256,1024]{1,0:T(8,128)(2,1)}, u32[]{:S(2)}, u32[]{:S(2)}) collective-permute-start(bf16[256,1024]{1,0:T(8,128)(2,1)S(1)} %constant_dynamic-update-slice_fusion.12), channel_id=1, source_target_pairs={{0,1},{1,0},{2,3},{3,2},{4,5},{5,4},{6,7},{7,6},{8,9},{9,8},{10,11... | collective-permute-start | bytes 1572872 | tf_op jit(solution)/shard_map/ppermute | solution.py:282
  89.5 36.3 %collective-permute-start.12 = (bf16[2,256,1024]{2,1,0:T(8,128)(2,1)}, bf16[2,256,1024]{2,1,0:T(8,128)(2,1)}, u32[]{:S(2)}, u32[]{:S(2)}) collective-permute-start(bf16[2,256,1024]{2,1,0:T(8,128)(2,1)} %pad_maximum_fusion.7), channel_id=1, source_target_pairs={{0,16},{16,0},{1,17},{17,1},{2,18},{18,2},{3,19},{19,3},{4,20},{20... | collective-permute-start | bytes 3145736 | tf_op jit(solution)/shard_map/ppermute | solution.py:285
  93.1 49.9 %collective-permute-start.23 = (bf16[2,256,1024]{2,1,0:T(8,128)(2,1)}, bf16[2,256,1024]{2,1,0:T(8,128)(2,1)}, u32[]{:S(2)}, u32[]{:S(2)}) collective-permute-start(bf16[2,256,1024]{2,1,0:T(8,128)(2,1)} %pad_maximum_fusion.9), channel_id=1, source_target_pairs={{0,16},{16,0},{1,17},{17,1},{2,18},{18,2},{3,19},{19,3},{4,20},{20... | collective-permute-start | bytes 3145736 | tf_op jit(solution)/shard_map/ppermute | solution.py:285
  100.6 28.1 %collective-permute-start.15 = (bf16[2,256,1024]{2,1,0:T(8,128)(2,1)}, bf16[2,256,1024]{2,1,0:T(8,128)(2,1)}, u32[]{:S(2)}, u32[]{:S(2)}) collective-permute-start(bf16[2,256,1024]{2,1,0:T(8,128)(2,1)} %pad_maximum_fusion.8), channel_id=1, source_target_pairs={{0,16},{16,0},{1,17},{17,1},{2,18},{18,2},{3,19},{19,3},{4,20},{20... | collective-permute-start | bytes 3145736 | tf_op jit(solution)/shard_map/ppermute | solution.py:285
  102.8 16.4 %collective-permute-start.35 = (bf16[2,128,1024]{2,1,0:T(8,128)(2,1)}, bf16[2,128,1024]{2,1,0:T(8,128)(2,1)}, u32[]{:S(2)}, u32[]{:S(2)}) collective-permute-start(bf16[2,128,1024]{2,1,0:T(8,128)(2,1)} %collective-permute-done.24), channel_id=1, source_target_pairs={{0,4},{2,6},{4,8},{6,10},{8,12},{10,14},{12,0},{14,2},{1,5},{3,7},... | collective-permute-start | bytes 1572872 | tf_op jit(solution)/shard_map/ppermute | solution.py:291
  104.3 16.8 %collective-permute-start.25 = (bf16[2,128,1024]{2,1,0:T(8,128)(2,1)}, bf16[2,128,1024]{2,1,0:T(8,128)(2,1)}, u32[]{:S(2)}, u32[]{:S(2)}) collective-permute-start(bf16[2,128,1024]{2,1,0:T(8,128)(2,1)} %collective-permute-done.24), channel_id=1, source_target_pairs={{0,2},{2,0},{4,6},{6,4},{8,10},{10,8},{12,14},{14,12},{1,3},{3,1},... | collective-permute-start | bytes 1572872 | tf_op jit(solution)/shard_map/ppermute | solution.py:288
  119.2 31.5 %collective-permute-start.34 = (bf16[2,256,1024]{2,1,0:T(8,128)(2,1)}, bf16[2,256,1024]{2,1,0:T(8,128)(2,1)}, u32[]{:S(2)}, u32[]{:S(2)}) collective-permute-start(bf16[2,256,1024]{2,1,0:T(8,128)(2,1)} %pad_maximum_fusion.11), channel_id=1, source_target_pairs={{0,16},{16,0},{1,17},{17,1},{2,18},{18,2},{3,19},{19,3},{4,20},{20... | collective-permute-start | bytes 3145736 | tf_op jit(solution)/shard_map/ppermute | solution.py:285
  121.1 32.7 %collective-permute-start.6 = (bf16[2,256,1024]{2,1,0:T(8,128)(2,1)}, bf16[2,256,1024]{2,1,0:T(8,128)(2,1)}, u32[]{:S(2)}, u32[]{:S(2)}) collective-permute-start(bf16[2,256,1024]{2,1,0:T(8,128)(2,1)} %get-tuple-element.29), channel_id=1, source_target_pairs={{0,16},{16,0},{1,17},{17,1},{2,18},{18,2},{3,19},{19,3},{4,20},{20... | collective-permute-start | bytes 3145736 | tf_op jit(solution)/shard_map/ppermute | solution.py:285
  125.8 30.9 %collective-permute-start.26 = (bf16[2,256,1024]{2,1,0:T(8,128)(2,1)}, bf16[2,256,1024]{2,1,0:T(8,128)(2,1)}, u32[]{:S(2)}, u32[]{:S(2)}) collective-permute-start(bf16[2,256,1024]{2,1,0:T(8,128)(2,1)} %pad_maximum_fusion.10), channel_id=1, source_target_pairs={{0,16},{16,0},{1,17},{17,1},{2,18},{18,2},{3,19},{19,3},{4,20},{20... | collective-permute-start | bytes 3145736 | tf_op jit(solution)/shard_map/ppermute | solution.py:285
  128.8 17.4 %collective-permute-start.36 = (bf16[2,128,1024]{2,1,0:T(8,128)(2,1)}, bf16[2,128,1024]{2,1,0:T(8,128)(2,1)}, u32[]{:S(2)}, u32[]{:S(2)}) collective-permute-start(bf16[2,128,1024]{2,1,0:T(8,128)(2,1)} %collective-permute-done.35), channel_id=1, source_target_pairs={{0,2},{2,0},{4,6},{6,4},{8,10},{10,8},{12,14},{14,12},{1,3},{3,1},... | collective-permute-start | bytes 1572872 | tf_op jit(solution)/shard_map/ppermute | solution.py:288
  143.0 41.6 %collective-permute-start.16 = (bf16[2,256,1024]{2,1,0:T(8,128)(2,1)}, bf16[2,256,1024]{2,1,0:T(8,128)(2,1)}, u32[]{:S(2)}, u32[]{:S(2)}) collective-permute-start(bf16[2,256,1024]{2,1,0:T(8,128)(2,1)} %get-tuple-element.31), channel_id=1, source_target_pairs={{0,16},{16,0},{1,17},{17,1},{2,18},{18,2},{3,19},{19,3},{4,20},{20... | collective-permute-start | bytes 3145736 | tf_op jit(solution)/shard_map/ppermute | solution.py:285
  148.5 23.2 %collective-permute-start.37 = (bf16[2,256,1024]{2,1,0:T(8,128)(2,1)}, bf16[2,256,1024]{2,1,0:T(8,128)(2,1)}, u32[]{:S(2)}, u32[]{:S(2)}) collective-permute-start(bf16[2,256,1024]{2,1,0:T(8,128)(2,1)} %pad_maximum_fusion.12), channel_id=1, source_target_pairs={{0,16},{16,0},{1,17},{17,1},{2,18},{18,2},{3,19},{19,3},{4,20},{20... | collective-permute-start | bytes 3145736 | tf_op jit(solution)/shard_map/ppermute | solution.py:285
  156.3 32.5 %collective-permute-start.7 = (bf16[256,1024]{1,0:T(8,128)(2,1)}, bf16[256,1024]{1,0:T(8,128)(2,1)}, u32[]{:S(2)}, u32[]{:S(2)}) collective-permute-start(bf16[256,1024]{1,0:T(8,128)(2,1)} %fusion.4), channel_id=1, source_target_pairs={{0,1},{1,0},{2,3},{3,2},{4,5},{5,4},{6,7},{7,6},{8,9},{9,8},{10,11... | collective-permute-start | bytes 1572872 | tf_op jit(solution)/shard_map/ppermute | solution.py:282
  170.9 110.1 %collective-permute-start.27 = (bf16[2,256,1024]{2,1,0:T(8,128)(2,1)}, bf16[2,256,1024]{2,1,0:T(8,128)(2,1)}, u32[]{:S(2)}, u32[]{:S(2)}) collective-permute-start(bf16[2,256,1024]{2,1,0:T(8,128)(2,1)} %get-tuple-element.33), channel_id=1, source_target_pairs={{0,16},{16,0},{1,17},{17,1},{2,18},{18,2},{3,19},{19,3},{4,20},{20... | collective-permute-start | bytes 3145736 | tf_op jit(solution)/shard_map/ppermute | solution.py:285
  184.2 99.9 %collective-permute-start.38 = (bf16[2,256,1024]{2,1,0:T(8,128)(2,1)}, bf16[2,256,1024]{2,1,0:T(8,128)(2,1)}, u32[]{:S(2)}, u32[]{:S(2)}) collective-permute-start(bf16[2,256,1024]{2,1,0:T(8,128)(2,1)} %get-tuple-element.35), channel_id=1, source_target_pairs={{0,16},{16,0},{1,17},{17,1},{2,18},{18,2},{3,19},{19,3},{4,20},{20... | collective-permute-start | bytes 3145736 | tf_op jit(solution)/shard_map/ppermute | solution.py:285
  187.4 99.3 %collective-permute-start.17 = (bf16[256,1024]{1,0:T(8,128)(2,1)}, bf16[256,1024]{1,0:T(8,128)(2,1)}, u32[]{:S(2)}, u32[]{:S(2)}) collective-permute-start(bf16[256,1024]{1,0:T(8,128)(2,1)} %fusion.5), channel_id=1, source_target_pairs={{0,1},{1,0},{2,3},{3,2},{4,5},{5,4},{6,7},{7,6},{8,9},{9,8},{10,11... | collective-permute-start | bytes 1572872 | tf_op jit(solution)/shard_map/ppermute | solution.py:282
  190.9 118.3 %collective-permute-start.8 = (bf16[128,1024]{1,0:T(8,128)(2,1)}, bf16[128,1024]{1,0:T(8,128)(2,1)}, u32[]{:S(2)}, u32[]{:S(2)}) collective-permute-start(bf16[128,1024]{1,0:T(8,128)(2,1)} %slice.163), channel_id=1, source_target_pairs={{0,2},{2,0},{4,6},{6,4},{8,10},{10,8},{12,14},{14,12},{1,3},{3,1},... | collective-permute-start | bytes 786440 | tf_op jit(solution)/shard_map/ppermute | solution.py:288
  198.6 14.7 %copy-start.42 = (f32[512,1]{0,1:T(1,128)S(1)}, f32[512,1]{0,1:T(1,128)}, u32[]{:S(2)}) copy-start(f32[512,1]{0,1:T(1,128)} %copy.42) | copy-start | bytes 6148
  198.6 14.7 %copy-start.43 = (f32[512,1]{0,1:T(1,128)S(1)}, f32[512,1]{0,1:T(1,128)}, u32[]{:S(2)}) copy-start(f32[512,1]{0,1:T(1,128)} %copy.43) | copy-start | bytes 6148
  282.7 13.4 %collective-permute-start.28 = (bf16[256,1024]{1,0:T(8,128)(2,1)S(1)}, bf16[256,1024]{1,0:T(8,128)(2,1)S(1)}, u32[]{:S(2)}, u32[]{:S(2)}) collective-permute-start(bf16[256,1024]{1,0:T(8,128)(2,1)S(1)} %fusion.6), channel_id=1, source_target_pairs={{0,1},{1,0},{2,3},{3,2},{4,5},{5,4},{6,7},{7,6},{8,9},{9,8},{10,11... | collective-permute-start | bytes 1572872 | tf_op jit(solution)/shard_map/ppermute | solution.py:282
  286.0 15.7 %collective-permute-start.39 = (bf16[256,1024]{1,0:T(8,128)(2,1)S(1)}, bf16[256,1024]{1,0:T(8,128)(2,1)S(1)}, u32[]{:S(2)}, u32[]{:S(2)}) collective-permute-start(bf16[256,1024]{1,0:T(8,128)(2,1)S(1)} %fusion.7), channel_id=1, source_target_pairs={{0,1},{1,0},{2,3},{3,2},{4,5},{5,4},{6,7},{7,6},{8,9},{9,8},{10,11... | collective-permute-start | bytes 1572872 | tf_op jit(solution)/shard_map/ppermute | solution.py:282
  287.9 14.0 %collective-permute-start.18 = (bf16[128,1024]{1,0:T(8,128)(2,1)S(1)}, bf16[128,1024]{1,0:T(8,128)(2,1)S(1)}, u32[]{:S(2)}, u32[]{:S(2)}) collective-permute-start(bf16[128,1024]{1,0:T(8,128)(2,1)S(1)} %slice.162), channel_id=1, source_target_pairs={{0,2},{2,0},{4,6},{6,4},{8,10},{10,8},{12,14},{14,12},{1,3},{3,1},... | collective-permute-start | bytes 786440 | tf_op jit(solution)/shard_map/ppermute | solution.py:288
  296.2 7.3 %collective-permute-start.29 = (bf16[128,1024]{1,0:T(8,128)(2,1)S(1)}, bf16[128,1024]{1,0:T(8,128)(2,1)S(1)}, u32[]{:S(2)}, u32[]{:S(2)}) collective-permute-start(bf16[128,1024]{1,0:T(8,128)(2,1)S(1)} %slice.161), channel_id=1, source_target_pairs={{0,2},{2,0},{4,6},{6,4},{8,10},{10,8},{12,14},{14,12},{1,3},{3,1},... | collective-permute-start | bytes 786440 | tf_op jit(solution)/shard_map/ppermute | solution.py:288
  301.8 23.6 %copy-start.30 = (f32[256,1024]{1,0:T(8,128)S(1)}, f32[256,1024]{1,0:T(8,128)}, u32[]{:S(2)}) copy-start(f32[256,1024]{1,0:T(8,128)} %copy-done.29) | copy-start | bytes 3145732
  301.9 6.4 %collective-permute-start.40 = (bf16[128,1024]{1,0:T(8,128)(2,1)S(1)}, bf16[128,1024]{1,0:T(8,128)(2,1)S(1)}, u32[]{:S(2)}, u32[]{:S(2)}) collective-permute-start(bf16[128,1024]{1,0:T(8,128)(2,1)S(1)} %slice.160), channel_id=1, source_target_pairs={{0,2},{2,0},{4,6},{6,4},{8,10},{10,8},{12,14},{14,12},{1,3},{3,1},... | collective-permute-start | bytes 786440 | tf_op jit(solution)/shard_map/ppermute | solution.py:288
  302.0 8.2 %collective-permute-start.19 = (bf16[128,1024]{1,0:T(8,128)(2,1)S(1)}, bf16[128,1024]{1,0:T(8,128)(2,1)S(1)}, u32[]{:S(2)}, u32[]{:S(2)}) collective-permute-start(bf16[128,1024]{1,0:T(8,128)(2,1)S(1)} %fusion.10), channel_id=1, source_target_pairs={{0,12},{2,14},{4,0},{6,2},{8,4},{10,6},{12,8},{14,10},{1,13},{3,15... | collective-permute-start | bytes 786440 | tf_op jit(solution)/shard_map/ppermute | solution.py:291
  303.6 21.9 %collective-permute-start.30 = (bf16[128,1024]{1,0:T(8,128)(2,1)S(1)}, bf16[128,1024]{1,0:T(8,128)(2,1)S(1)}, u32[]{:S(2)}, u32[]{:S(2)}) collective-permute-start(bf16[128,1024]{1,0:T(8,128)(2,1)S(1)} %fusion.9), channel_id=1, source_target_pairs={{0,8},{2,10},{4,12},{6,14},{8,0},{10,2},{12,4},{14,6},{1,9},{3,11}... | collective-permute-start | bytes 786440 | tf_op jit(solution)/shard_map/ppermute | solution.py:291
  308.4 17.1 %collective-permute-start.41 = (bf16[128,1024]{1,0:T(8,128)(2,1)S(1)}, bf16[128,1024]{1,0:T(8,128)(2,1)S(1)}, u32[]{:S(2)}, u32[]{:S(2)}) collective-permute-start(bf16[128,1024]{1,0:T(8,128)(2,1)S(1)} %fusion.8), channel_id=1, source_target_pairs={{0,4},{2,6},{4,8},{6,10},{8,12},{10,14},{12,0},{14,2},{1,5},{3,7},... | collective-permute-start | bytes 786440 | tf_op jit(solution)/shard_map/ppermute | solution.py:291
  (38 other events, 165.0 us)

commit v3 on v0

--- a/solution.py
+++ b/solution.py
@@ -1,6 +1,11 @@
+import functools
+import math
+
 import jax
 import jax.numpy as jnp
 from jax import lax
+from jax.experimental import pallas as pl
+from jax.experimental.pallas import tpu as pltpu
 from jax.sharding import PartitionSpec as P
 
 
@@ -8,7 +13,7 @@
     return jnp.concatenate([array, jnp.zeros((1, array.shape[1]), array.dtype)], 0)
 
 
-def per_device(tokens, out_grad, routes, probs, w_gate, w_up, w_down):
+def routed_device(tokens, out_grad, routes, probs, w_gate, w_up, w_down):
     owners = lax.axis_size(("role", "ep"))
     tok_rows, top_count = routes.shape
     width_full = w_gate.shape[1]
@@ -112,6 +117,280 @@
     )
 
 
+def slot_capacity(tok_rows, top_count, owners):
+    return min(tok_rows, tok_rows * top_count * 9 // (8 * owners))
+
+
+def weights_kernel(tp_ref, wg_ref, wu_ref, wd_ref, both_ref, down_ref):
+    part = wg_ref.shape[2]
+    both_ref[:, :part] = wg_ref[0]
+    both_ref[:, part:] = wu_ref[0]
+    down_ref[...] = wd_ref[0]
+
+
+def weights_call(which, w_gate, w_up, w_down):
+    _, width, part = w_gate.shape
+    half = width // 2
+
+    def place(i, w):
+        return (i + w[0]) % 2
+
+    return pl.pallas_call(
+        weights_kernel,
+        grid_spec=pltpu.PrefetchScalarGridSpec(
+            num_scalar_prefetch=1,
+            grid=(2,),
+            in_specs=[
+                pl.BlockSpec((1, half, part), lambda i, w: (0, place(i, w), 0)),
+                pl.BlockSpec((1, half, part), lambda i, w: (0, place(i, w), 0)),
+                pl.BlockSpec((1, part, half), lambda i, w: (0, 0, place(i, w))),
+            ],
+            out_specs=[
+                pl.BlockSpec((half, 2 * part), lambda i, w: (i, 0)),
+                pl.BlockSpec((part, half), lambda i, w: (0, i)),
+            ],
+        ),
+        out_shape=[
+            jax.ShapeDtypeStruct((width, 2 * part), jnp.bfloat16),
+            jax.ShapeDtypeStruct((part, width), jnp.bfloat16),
+        ],
+        compiler_params=pltpu.CompilerParams(vmem_limit_bytes=24 << 20),
+        cost_estimate=pl.CostEstimate(flops=0, bytes_accessed=12 * width * part, transcendentals=0),
+        name="weights",
+    )(which, w_gate, w_up, w_down)
+
+
+def rows_kernel(slots, slot_ref, p_ref, wgu_ref, wd_ref, *refs):
+    x_in, g_in = refs[:4], refs[4:8]
+    refs = refs[len(refs) - 11 :]
+    xc_ref, gc_ref, both_ref, scaled_ref, score_ref, keep_ref, send_ref, x_all, g_all, x_sems, g_sems = refs
+    half = x_all.shape[3]
+    tok = g_in[0].shape[1]
+    part = scaled_ref.shape[1]
+
+    x_copies = [pltpu.make_async_copy(x_in[i], x_all.at[i // 2, i % 2], x_sems.at[i]) for i in range(4)]
+    g_copies = [
+        pltpu.make_async_copy(g_in[i], g_all.at[i // 2, :, pl.ds(i % 2 * tok, tok)], g_sems.at[i]) for i in range(4)
+    ]
+    for copy in x_copies + g_copies:
+        copy.start()
+
+    def pick(a, b, dims):
+        return lax.dot_general(a, b, (dims, ((), ())), preferred_element_type=jnp.float32)
+
+    number = lax.broadcasted_iota(jnp.int32, (slots, 2 * tok), 0)
+    picks = [(number == slot_ref[core : core + 1, :]).astype(jnp.float32) for core in range(2)]
+    picks_low = [item.astype(jnp.bfloat16) for item in picks]
+    prob = jnp.concatenate(
+        [jnp.sum(picks[core] * p_ref[core : core + 1, :], axis=1, keepdims=True) for core in range(2)], 0
+    )
+    for core in range(2):
+        x_copies[2 * core].wait()
+        x_copies[2 * core + 1].wait()
+        for side in range(2):
+            xc_ref[core * slots : (core + 1) * slots, side * half : (side + 1) * half] = pick(
+                picks_low[core], x_all[core, side], ((1,), (0,))
+            ).astype(jnp.bfloat16)
+    rows = pick(xc_ref[...], wgu_ref[...], ((1,), (0,)))
+    for core in range(2):
+        g_copies[2 * core].wait()
+        g_copies[2 * core + 1].wait()
+        for side in range(2):
+            gc_ref[core * slots : (core + 1) * slots, side * half : (side + 1) * half] = pick(
+                picks_low[core], g_all[core, side], ((1,), (0,))
+            ).astype(jnp.bfloat16)
+    back = pick(gc_ref[...], wd_ref[...], ((1,), (1,)))
+    gate, up = rows[:, :part], rows[:, part:]
+    sig = jax.nn.sigmoid(gate)
+    act = gate * sig
+    hidden = act * up
+    score = jnp.sum(hidden * back, axis=1, keepdims=True)
+    for core in range(2):
+        score_ref[core : core + 1, :] = jnp.sum(
+            picks[core] * score[core * slots : (core + 1) * slots], axis=0, keepdims=True
+        )
+    hgrad = prob * back
+    both_ref[:, :part] = (hgrad * up * sig * (1.0 + gate * (1.0 - sig))).astype(jnp.bfloat16)
+    both_ref[:, part:] = (hgrad * act).astype(jnp.bfloat16)
+    scaled_ref[...] = (prob * hidden).astype(jnp.bfloat16)
+    for side in range(2):
+        low = pick(both_ref[...], wgu_ref[side * half : (side + 1) * half, :], ((1,), (1,))).astype(jnp.bfloat16)
+        for core, out_ref in ((1, send_ref), (0, keep_ref)):
+            out_ref[side] = pick(picks_low[core], low[core * slots : (core + 1) * slots], ((0,), (0,))).astype(jnp.bfloat16)
+
+
+def rows_call(step, steps, slots, slot, prob, both_w, down_w, x_in, g_in, held):
+    pair, half = x_in[0].shape
+    width, part = 2 * half, down_w.shape[0]
+    loose = pl.BlockSpec(memory_space=pl.ANY)
+    rows = 2 * slots
+    widths = (width, width, 2 * part, part)
+    return pl.pallas_call(
+        functools.partial(rows_kernel, slots),
+        grid=(1,),
+        in_specs=[
+            pl.BlockSpec((2, pair), lambda i: (0, 0)),
+            pl.BlockSpec((2, pair), lambda i: (0, 0)),
+            pl.BlockSpec((width, 2 * part), lambda i: (0, 0)),
+            pl.BlockSpec((part, width), lambda i: (0, 0)),
+        ]
+        + [loose] * (8 + len(held)),
+        out_specs=[pl.BlockSpec((rows, size), lambda i: (step, 0)) for size in widths]
+        + [pl.BlockSpec((2, pair), lambda i: (0, 0))]
+        + [pl.BlockSpec((2, pair, half), lambda i: (0, 0, 0))] * 2,
+        out_shape=[jax.ShapeDtypeStruct((steps * rows, size), jnp.bfloat16) for size in widths]
+        + [jax.ShapeDtypeStruct((2, pair), jnp.float32)]
+        + [jax.ShapeDtypeStruct((2, pair, half), jnp.bfloat16)] * 2,
+        scratch_shapes=[
+            pltpu.VMEM((2, 2, pair, half), jnp.bfloat16),
+            pltpu.VMEM((2, 2, pair, half), jnp.bfloat16),
+            pltpu.SemaphoreType.DMA((4,)),
+            pltpu.SemaphoreType.DMA((4,)),
+        ],
+        input_output_aliases={12 + i: i for i in range(len(held))},
+        compiler_params=pltpu.CompilerParams(vmem_limit_bytes=40 << 20),
+        cost_estimate=pl.CostEstimate(
+            flops=10 * rows * width * part + 12 * rows * pair * width,
+            bytes_accessed=8 * 2 * pair * width + 6 * width * part,
+            transcendentals=rows * part,
+        ),
+        name="rows",
+    )(slot, prob, both_w, down_w, *x_in, *g_in, *held)
+
+
+def grads_kernel(tp_ref, x_ref, g_ref, both_ref, scaled_ref, dg_ref, du_ref, dd_ref):
+    part = scaled_ref.shape[1]
+    both = lax.dot_general(x_ref[...], both_ref[...], (((0,), (0,)), ((), ())), preferred_element_type=jnp.float32)
+    dg_ref[0] = both[:, :part].astype(jnp.bfloat16)
+    du_ref[0] = both[:, part:].astype(jnp.bfloat16)
+    down = lax.dot_general(scaled_ref[...], g_ref[...], (((0,), (0,)), ((), ())), preferred_element_type=jnp.float32)
+    dd_ref[0] = down.astype(jnp.bfloat16)
+
+
+def grads_call(which, x_rows, g_rows, both, scaled):
+    total, width = x_rows.shape
+    part = scaled.shape[1]
+    step = math.gcd(width // 2, 256)
+    per = width // 2 // step
+
+    def place(i, w):
+        return (i + w[0] * per) % (2 * per)
+
+    moving = pl.BlockSpec((total, step), lambda i, w: (0, i))
+    return pl.pallas_call(
+        grads_kernel,
+        grid_spec=pltpu.PrefetchScalarGridSpec(
+            num_scalar_prefetch=1,
+            grid=(width // step,),
+            in_specs=[
+                moving,
+                moving,
+                pl.BlockSpec((total, 2 * part), lambda i, w: (0, 0)),
+                pl.BlockSpec((total, part), lambda i, w: (0, 0)),
+            ],
+            out_specs=[
+                pl.BlockSpec((1, step, part), lambda i, w: (0, place(i, w), 0)),
+                pl.BlockSpec((1, step, part), lambda i, w: (0, place(i, w), 0)),
+                pl.BlockSpec((1, part, step), lambda i, w: (0, 0, place(i, w))),
+            ],
+        ),
+        out_shape=[
+            jax.ShapeDtypeStruct((1, width, part), jnp.bfloat16),
+            jax.ShapeDtypeStruct((1, width, part), jnp.bfloat16),
+            jax.ShapeDtypeStruct((1, part, width), jnp.bfloat16),
+        ],
+        compiler_params=pltpu.CompilerParams(vmem_limit_bytes=40 << 20),
+        cost_estimate=pl.CostEstimate(flops=6 * total * width * part, bytes_accessed=6 * total * width, transcendentals=0),
+        name="grads",
+    )(which, x_rows, g_rows, both, scaled)
+
+
+def dense_device(tokens, out_grad, routes, probs, w_gate, w_up, w_down):
+    owners = lax.axis_size(("role", "ep"))
+    ep = lax.axis_size("ep")
+    n_y = 2
+    n_z = ep // n_y
+    tok_rows, half = tokens.shape
+    capacity = slot_capacity(tok_rows, routes.shape[1], owners)
+    slots = -(-n_y * capacity // 16) * 16
+    me = lax.axis_index(("role", "ep"))
+    role, place, which = lax.axis_index("role"), lax.axis_index("ep"), lax.axis_index("tp")
+    my_z, my_y = place // n_y, place % n_y
+
+    def over_x(array):
+        return lax.ppermute(array, "tp", [(0, 1), (1, 0)])
+
+    def over_role(array):
+        return lax.ppermute(array, "role", [(0, 1), (1, 0)])
+
+    def over_y(array):
+        return lax.ppermute(array, "ep", [(i, i + 1 - 2 * (i % n_y)) for i in range(ep)])
+
+    def over_z(array, shift):
+        return lax.ppermute(array, "ep", [(i, (i + shift * n_y) % ep) for i in range(ep)])
+
+    chosen = routes[:, :, None] == jnp.arange(owners, dtype=jnp.int32)
+    table = jnp.sum(jnp.where(chosen, probs[:, :, None].astype(jnp.float32) + 1.0, 0.0), axis=1) - 1.0
+    table = table.astype(jnp.bfloat16).T
+    tables = jnp.stack([table] + [over_z(table, step) for step in range(1, n_z)])
+    tables = jnp.stack([tables, over_y(tables)], 1)
+    tables = jnp.stack([tables, over_role(tables)], 1)
+    prob = lax.dynamic_slice_in_dim(tables, me, 1, 3)[:, :, :, 0].astype(jnp.float32)
+    routed = prob >= 0.0
+    before = jnp.tril(jnp.ones((tok_rows, tok_rows), jnp.bfloat16), -1).T
+    slot = jnp.dot(routed.astype(jnp.bfloat16), before, preferred_element_type=jnp.float32).astype(jnp.int32)
+    slot = jnp.where(routed, slot + capacity * jnp.arange(n_y, dtype=jnp.int32)[:, None], -1)
+    slot = slot.reshape(n_z, 2, n_y * tok_rows)
+    prob = prob.reshape(n_z, 2, n_y * tok_rows)
+
+    which_ref = which.reshape(1).astype(jnp.int32)
+    both_w, down_w = weights_call(which_ref, w_gate, w_up, w_down)
+
+    x_own, g_own = tokens, jnp.stack([out_grad, over_x(out_grad)])
+    x_parts, g_parts = [], []
+    for step in range(n_z):
+        if step:
+            x_own, g_own = over_z(x_own, 1), over_z(g_own, 1)
+        pair = jnp.concatenate([x_own, over_y(x_own)], 0)
+        far = over_x(pair)
+        x_parts.append((pair, far, over_role(pair), over_role(far)))
+        far = over_y(g_own)
+        g_parts.append((g_own, far, over_role(g_own), over_role(far)))
+
+    held, scores, homeward = (), [], []
+    for step in range(n_z):
+        *held, score, keep, send = rows_call(
+            step, n_z, slots, slot[step], prob[step], both_w, down_w, x_parts[step], g_parts[step], held
+        )
+        scores.append(score)
+        total = keep.astype(jnp.float32) + over_role(send).astype(jnp.float32)
+        total = total[0] + over_x(total[1].astype(jnp.bfloat16)).astype(jnp.float32)
+        total = total[:tok_rows] + over_y(total[tok_rows:].astype(jnp.bfloat16)).astype(jnp.float32)
+        homeward.append(over_z(total.astype(jnp.bfloat16), -step).astype(jnp.float32) if step else total)
+    d_tok = sum(homeward[1:], homeward[0]).astype(jnp.bfloat16)
+    d_gate, d_up, d_down = grads_call(which_ref, *held)
+
+    mine = jnp.stack(scores).reshape(n_z, 2, n_y, tok_rows)
+    mine = mine + over_x(mine)
+    mine = jnp.stack([mine[:, 0], over_role(mine[:, 1])])
+    mine = jnp.stack([mine[:, :, 0], over_y(mine[:, :, 1])])
+    mine = jnp.stack([mine[:, :, 0]] + [over_z(mine[:, :, step], -step) for step in range(1, n_z)])
+    steps = jnp.arange(n_z)[:, None, None]
+    source = (role + jnp.arange(2)) % 2 * ep + (my_z + steps) % n_z * n_y + ((my_y + jnp.arange(n_y)) % n_y)[:, None]
+    picked = routes[:, :, None] == source.reshape(-1)
+    d_probs = jnp.sum(jnp.where(picked, mine.reshape(owners, tok_rows).T[:, None, :], 0.0), axis=2)
+    return d_tok, d_probs, d_gate, d_up, d_down
+
+
+def per_device(tokens, out_grad, routes, probs, w_gate, w_up, w_down):
+    owners = lax.axis_size(("role", "ep"))
+    tok_rows, top_count = routes.shape
+    paired = lax.axis_size("tp") == 2 and lax.axis_size("role") == 2 and lax.axis_size("ep") % 2 == 0
+    if paired and 2 * slot_capacity(tok_rows, top_count, owners) >= tok_rows:
+        return dense_device(tokens, out_grad, routes, probs, w_gate, w_up, w_down)
+    return routed_device(tokens, out_grad, routes, probs, w_gate, w_up, w_down)
+
+
 def solution(mesh):
     in_specs = (
         P(("groups", "role", "ep"), "tp"),

time: 367 us -> 233 us (0.63)
  blocking collectives: 148 us -> 0 us
  Pallas kernels: 0 us -> 39.2 us
  starting transfers between devices: 5.8 us -> 43.7 us
  matrix products: 34.4 us -> 0.2 us
  waiting for transfers between devices: 106 us -> 88.4 us
  between operations: 14 us -> 1.53 us
  local copies, waits for them, and re-layouts: 37.4 us -> 45.7 us
  other arithmetic: 20.2 us -> 13.1 us
    all_to_all x4 -> x0, blocking collectives: 143 us -> none  [the longest x1 62.8 us: per_device(): lax.all_to_all(send_x.reshape(owners, capacity, tokens.shape[1]), ('role'...]
    ppermute x0 -> x61, waiting for transfers between devices: none -> 88.4 us  [the longest x14 31.9 us: over_y(): lax.ppermute(array, 'ep', [(i, i + 1 - 2 * (i % n_y)) for i in range(ep)])]
    ppermute x0 -> x61, starting transfers between devices: none -> 43.7 us  [the longest x14 15.6 us: over_y(): lax.ppermute(array, 'ep', [(i, i + 1 - 2 * (i % n_y)) for i in range(ep)])]
    reduce_scatter x1 -> x0, waiting for transfers between devices: 43.3 us -> none  [per_device(): lax.psum_scatter(partial_low.reshape(owners, capacity, width_full), 'tp',...]
    pallas_call x0 -> x6, Pallas kernels: none -> 39.2 us  [the longest x4 28.4 us: rows_call(): pl.pallas_call(functools.partial(rows_kernel, slots), grid=(1,), in_specs...]
    unnamed x23 -> x129, local copies, waits for them, and re-layouts: 4.23 us -> 40.8 us
    all_gather x2 -> x0, waiting for transfers between devices: 34.5 us -> none  [the longest x1 34.5 us: per_device(): lax.all_gather(slice_g, 'tp', axis=2, tiled=True)]
    dot_general x5 -> x1, matrix products: 34.4 us -> 0.2 us  [dense_device(): jnp.dot(routed.astype(jnp.bfloat16), before, preferred_element_type=jnp.f...]
  transfers between devices with their start and end apart: 4 -> 61, of which waited for: 3 -> 20; matrix products, arithmetic and copies ran while one was open for 12% -> 8% of each run, Pallas kernels for 0% -> 17%
where the time goes in v3:
time: 233 us; the launch traced here: 232 us
  waiting for transfers between devices  88.4 us (38%)
  local copies, waits for them, and re-layouts  45.7 us (20%)
  starting transfers between devices  43.7 us (19%)
  Pallas kernels  39.2 us (17%)
  other arithmetic  13.1 us (6%)
    unnamed x129, local copies, waits for them, and re-layouts  40.8 us
    ppermute x14, waiting for transfers between devices, over_y(): lax.ppermute(array, 'ep', [(i, i + 1 - 2 * (i % n_y)) for i in range(ep)])  31.9 us
    pallas_call x4, Pallas kernels, rows_call(): pl.pallas_call(functools.partial(rows_kernel, slots), grid=(1,), in_specs...  28.4 us
    ppermute x10, waiting for transfers between devices, over_x(): return lax.ppermute(array, 'tp', [(0, 1), (1, 0)])  27.7 us
    ppermute x15, waiting for transfers between devices, over_z(): lax.ppermute(array, 'ep', [(i, (i + shift * n_y) % ep) for i in range(ep)])  27.5 us
    ppermute x14, starting transfers between devices, over_y(): lax.ppermute(array, 'ep', [(i, i + 1 - 2 * (i % n_y)) for i in range(ep)])  15.6 us
    ppermute x10, starting transfers between devices, over_x(): return lax.ppermute(array, 'tp', [(0, 1), (1, 0)])  13.3 us
    ppermute x15, starting transfers between devices, over_z(): lax.ppermute(array, 'ep', [(i, (i + shift * n_y) % ep) for i in range(ep)])  11.6 us
  transfers between devices with their start and end apart: 61, of which 20 were waited for; matrix products, arithmetic and copies ran while one was open for 8% of the time, Pallas kernels for 17%

profile of v3, /device:TPU:0, one launch (start us, length us, event | category | flops | bytes accessed | tf_op | source)
XLA Modules:
  0.0 231.8 jit_solution(9594488495625508738)
XLA Ops:
  2.0 3.1 %collective-permute-start = (bf16[16,128]{1,0:T(8,128)(2,1)S(1)}, bf16[16,128]{1,0:T(8,128)(2,1)S(1)}, u32[]{:S(2)}, u32[]{:S(2)}) collective-permute-start(bf16[16,128]{1,0:T(8,128)(2,1)S(1)} %get-tuple-element.90), channel_id=1, source_target_pairs={{0,4},{2,6},{4,8},{6,10},{8,12},{10,14},{12,0},{14,2},{1,5},{3,7},... | collective-permute-start | bytes 12296 | tf_op jit(solution)/shard_map/ppermute | solution.py:330
  5.1 2.6 %collective-permute-start.1 = (bf16[16,128]{1,0:T(8,128)(2,1)S(1)}, bf16[16,128]{1,0:T(8,128)(2,1)S(1)}, u32[]{:S(2)}, u32[]{:S(2)}) collective-permute-start(bf16[16,128]{1,0:T(8,128)(2,1)S(1)} %get-tuple-element.90), channel_id=1, source_target_pairs={{0,8},{2,10},{4,12},{6,14},{8,0},{10,2},{12,4},{14,6},{1,9},{3,11}... | collective-permute-start | bytes 12296 | tf_op jit(solution)/shard_map/ppermute | solution.py:330
  9.0 1.5 collective-permute-start.9
  10.5 1.5 collective-permute-start.5
  12.1 1.7 constant_dynamic-update-slice_fusion.1
  16.5 1.8 pad_maximum_fusion.refs_4_
  18.3 1.5 collective-permute-start.10
  19.8 2.8 %collective-permute-done.16 = bf16[128,1024]{1,0:T(8,128)(2,1)S(1)} collective-permute-done((bf16[128,1024]{1,0:T(8,128)(2,1)}, bf16[128,1024]{1,0:T(8,128)(2,1)S(1)}, u32[]{:S(2)}, u32[]{:S(2)}) %collective-permute-start.16) | collective-permute-done | bytes 262176 | tf_op jit(solution)/shard_map/ppermute | solution.py:330
  26.0 10.0 %collective-permute-done.17 = bf16[128,1024]{1,0:T(8,128)(2,1)S(1)} collective-permute-done((bf16[128,1024]{1,0:T(8,128)(2,1)S(1)}, bf16[128,1024]{1,0:T(8,128)(2,1)S(1)}, u32[]{:S(2)}, u32[]{:S(2)}) %collective-permute-start.17) | collective-permute-done | bytes 262176 | tf_op jit(solution)/shard_map/ppermute | solution.py:327
  37.4 1.5 collective-permute-start.30
  39.0 1.4 copy-done.20
  40.4 1.4 copy-done.21
  41.8 1.4 copy-done.22
  44.5 1.6 collective-permute-start.18
  46.1 7.5 %collective-permute-done.21.refs_4_ = bf16[2,128,1024]{2,1,0:T(8,128)(2,1)} collective-permute-done((bf16[2,128,1024]{2,1,0:T(8,128)(2,1)}, bf16[2,128,1024]{2,1,0:T(8,128)(2,1)}, u32[]{:S(2)}, u32[]{:S(2)}) %collective-permute-start.21) | collective-permute-done | bytes 524320 | tf_op jit(solution)/shard_map/ppermute | solution.py:330
  54.1 3.8 %collective-permute-done.42 = bf16[128,1024]{1,0:T(8,128)(2,1)S(1)} collective-permute-done((bf16[128,1024]{1,0:T(8,128)(2,1)}, bf16[128,1024]{1,0:T(8,128)(2,1)S(1)}, u32[]{:S(2)}, u32[]{:S(2)}) %collective-permute-start.42) | collective-permute-done | bytes 262176 | tf_op jit(solution)/shard_map/ppermute | solution.py:330
  58.0 1.5 collective-permute-start.43
  61.7 1.6 collective-permute-start.31
  65.1 1.5 collective-permute-start.22
  66.8 7.5 %rows.4 = (bf16[1152,2048]{1,0:T(8,128)(2,1)}, bf16[1152,2048]{1,0:T(8,128)(2,1)}, bf16[1152,768]{1,0:T(8,128)(2,1)S(1)}, bf16[1152,384]{1,0:T(8,128)(2,1)S(1)},...) custom-call(s32[2,256]{1,0:T(2,128)S(1)} %bitcast.123, ...), custom_call_target="tpu_custom_call" | custom-call | flops 4076863488 | bytes 13107200 | tf_op jit(solution)/shard_map/rows/pallas_call | solution.py:228
  80.0 3.1 %collective-permute-done.34.refs_4_ = bf16[2,128,1024]{2,1,0:T(8,128)(2,1)} collective-permute-done((bf16[2,128,1024]{2,1,0:T(8,128)(2,1)}, bf16[2,128,1024]{2,1,0:T(8,128)(2,1)}, u32[]{:S(2)}, u32[]{:S(2)}) %collective-permute-start.34) | collective-permute-done | bytes 524320 | tf_op jit(solution)/shard_map/ppermute | solution.py:330
  86.3 1.7 constant_dynamic-update-slice_fusion.6.refs_0_
  88.0 1.5 collective-permute-start.44
  89.8 7.1 %collective-permute-done.35.refs_5_ = bf16[2,128,1024]{2,1,0:T(8,128)(2,1)} collective-permute-done((bf16[2,128,1024]{2,1,0:T(8,128)(2,1)}, bf16[2,128,1024]{2,1,0:T(8,128)(2,1)}, u32[]{:S(2)}, u32[]{:S(2)}) %collective-permute-start.35) | collective-permute-done | bytes 524320 | tf_op jit(solution)/shard_map/ppermute | solution.py:327
  96.9 2.2 collective-permute-done.47.refs_4_
  100.4 1.5 copy-done.1
  101.9 1.4 copy-done.9
  107.6 6.7 %rows.5 = (bf16[1152,2048]{1,0:T(8,128)(2,1)}, bf16[1152,2048]{1,0:T(8,128)(2,1)}, bf16[1152,768]{1,0:T(8,128)(2,1)S(1)}, bf16[1152,384]{1,0:T(8,128)(2,1)S(1)},...) custom-call(s32[2,256]{1,0:T(2,128)S(1)} %bitcast.121, ...), custom_call_target="tpu_custom_call", output_to_operand_aliasing={{0}: (12, {}), {1}: (13, {}), {2}: (14, {}), {3}: (15, {})} | custom-call | flops 4076863488 | bytes 13107200 | tf_op jit(solution)/shard_map/rows/pallas_call | solution.py:228
  118.7 2.1 convert_add_fusion.3
  125.4 6.8 %rows.6 = (bf16[1152,2048]{1,0:T(8,128)(2,1)}, bf16[1152,2048]{1,0:T(8,128)(2,1)}, bf16[1152,768]{1,0:T(8,128)(2,1)S(1)}, bf16[1152,384]{1,0:T(8,128)(2,1)S(1)},...) custom-call(s32[2,256]{1,0:T(2,128)S(1)} %bitcast.119, ...), custom_call_target="tpu_custom_call", output_to_operand_aliasing={{0}: (12, {}), {1}: (13, {}), {2}: (14, {}), {3}: (15, {})} | custom-call | flops 4076863488 | bytes 13107200 | tf_op jit(solution)/shard_map/rows/pallas_call | solution.py:228
  136.4 1.5 collective-permute-start.14
  137.9 1.5 copy-done.5
  141.9 7.4 %rows.7 = (bf16[1152,2048]{1,0:T(8,128)(2,1)}, bf16[1152,2048]{1,0:T(8,128)(2,1)}, bf16[1152,768]{1,0:T(8,128)(2,1)S(1)}, bf16[1152,384]{1,0:T(8,128)(2,1)S(1)},...) custom-call(s32[2,256]{1,0:T(2,128)S(1)} %bitcast.117, ...), custom_call_target="tpu_custom_call", output_to_operand_aliasing={{0}: (12, {}), {1}: (13, {}), {2}: (14, {}), {3}: (15, {})} | custom-call | flops 4076863488 | bytes 13107200 | tf_op jit(solution)/shard_map/rows/pallas_call | solution.py:228
  154.1 1.5 fusion.5
  157.4 1.7 convert_add_fusion.2
  160.6 1.6 collective-permute-start.26
  162.2 2.2 collective-permute-done.57
  164.8 1.7 convert_add_fusion.1
  166.6 1.5 collective-permute-start.39
  168.6 6.9 %collective-permute-done.26 = bf16[256,1024]{1,0:T(8,128)(2,1)S(1)} collective-permute-done((bf16[256,1024]{1,0:T(8,128)(2,1)S(1)}, bf16[256,1024]{1,0:T(8,128)(2,1)S(1)}, u32[]{:S(2)}, u32[]{:S(2)}) %collective-permute-start.26) | collective-permute-done | bytes 524320 | tf_op jit(solution)/shard_map/ppermute | solution.py:321
  175.5 1.5 collective-permute-start.52
  177.2 9.6 %collective-permute-done.39 = bf16[256,1024]{1,0:T(8,128)(2,1)S(1)} collective-permute-done((bf16[256,1024]{1,0:T(8,128)(2,1)S(1)}, bf16[256,1024]{1,0:T(8,128)(2,1)S(1)}, u32[]{:S(2)}, u32[]{:S(2)}) %collective-permute-start.39) | collective-permute-done | bytes 524320 | tf_op jit(solution)/shard_map/ppermute | solution.py:321
  187.6 9.3 %collective-permute-done.52 = bf16[256,1024]{1,0:T(8,128)(2,1)S(1)} collective-permute-done((bf16[256,1024]{1,0:T(8,128)(2,1)S(1)}, bf16[256,1024]{1,0:T(8,128)(2,1)S(1)}, u32[]{:S(2)}, u32[]{:S(2)}) %collective-permute-start.52) | collective-permute-done | bytes 524320 | tf_op jit(solution)/shard_map/ppermute | solution.py:321
  199.3 6.8 %collective-permute-done.40 = bf16[128,1024]{1,0:T(8,128)(2,1)S(1)} collective-permute-done((bf16[128,1024]{1,0:T(8,128)(2,1)S(1)}, bf16[128,1024]{1,0:T(8,128)(2,1)S(1)}, u32[]{:S(2)}, u32[]{:S(2)}) %collective-permute-start.40) | collective-permute-done | bytes 262176 | tf_op jit(solution)/shard_map/ppermute | solution.py:327
  206.2 3.5 %collective-permute-done.53 = bf16[128,1024]{1,0:T(8,128)(2,1)S(1)} collective-permute-done((bf16[128,1024]{1,0:T(8,128)(2,1)S(1)}, bf16[128,1024]{1,0:T(8,128)(2,1)S(1)}, u32[]{:S(2)}, u32[]{:S(2)}) %collective-permute-start.53) | collective-permute-done | bytes 262176 | tf_op jit(solution)/shard_map/ppermute | solution.py:327
  210.2 1.7 collective-permute-start.54
  212.0 10.1 %grads.1 = (bf16[1,2048,384]{2,1,0:T(8,128)(2,1)}, bf16[1,2048,384]{2,1,0:T(8,128)(2,1)}, bf16[1,384,2048]{2,1,0:T(8,128)(2,1)}) custom-call(s32[1]{0:T(128)} %bitcast.14.tp_ref, bf16[1152,2048]{1,0:T(8,128)(2,1)S(1)} %bitcast.114, bf16[1152,2048]{1,0:T(8,128)(2,1)S(1)} %bitcast.116, bf16[1152,768]{1,0:T(8,128)(2,1)S(1)} %copy-done.7, ...), custom_call_target="tpu_custom_call" | custom-call | flops 5435817984 | bytes 14155776 | tf_op jit(solution)/shard_map/grads/pallas_call | solution.py:280
  222.8 8.1 %collective-permute-done.41 = bf16[128,1024]{1,0:T(8,128)(2,1)S(1)} collective-permute-done((bf16[128,1024]{1,0:T(8,128)(2,1)S(1)}, bf16[128,1024]{1,0:T(8,128)(2,1)S(1)}, u32[]{:S(2)}, u32[]{:S(2)}) %collective-permute-start.41) | collective-permute-done | bytes 262176 | tf_op jit(solution)/shard_map/ppermute | solution.py:330
  (268 shorter events, 61.0 us)
Async XLA Ops:
  2.0 11.8 %collective-permute-start = (bf16[16,128]{1,0:T(8,128)(2,1)S(1)}, bf16[16,128]{1,0:T(8,128)(2,1)S(1)}, u32[]{:S(2)}, u32[]{:S(2)}) collective-permute-start(bf16[16,128]{1,0:T(8,128)(2,1)S(1)} %get-tuple-element.90), channel_id=1, source_target_pairs={{0,4},{2,6},{4,8},{6,10},{8,12},{10,14},{12,0},{14,2},{1,5},{3,7},... | collective-permute-start | bytes 12296 | tf_op jit(solution)/shard_map/ppermute | solution.py:330
  10.5 12.7 %collective-permute-start.5 = (bf16[128,1024]{1,0:T(8,128)(2,1)}, bf16[128,1024]{1,0:T(8,128)(2,1)S(1)}, u32[]{:S(2)}, u32[]{:S(2)}) collective-permute-start(bf16[128,1024]{1,0:T(8,128)(2,1)} %param.7), channel_id=1, source_target_pairs={{0,2},{2,0},{4,6},{6,4},{8,10},{10,8},{12,14},{14,12},{1,3},{3,1},... | collective-permute-start | bytes 786440 | tf_op jit(solution)/shard_map/ppermute | solution.py:327
  14.7 9.8 %collective-permute-start.3 = (bf16[4,16,128]{2,0,1:T(4,128)(2,1)S(1)}, bf16[4,16,128]{2,0,1:T(4,128)(2,1)S(1)}, u32[]{:S(2)}, u32[]{:S(2)}) collective-permute-start(bf16[4,16,128]{2,0,1:T(4,128)(2,1)S(1)} %pad_maximum_fusion.2), channel_id=1, source_target_pairs={{0,2},{2,0},{4,6},{6,4},{8,10},{10,8},{12,14},{14,12},{1,3},{3,1},... | collective-permute-start | bytes 49160 | tf_op jit(solution)/shard_map/ppermute | solution.py:327
  18.3 19.2 %collective-permute-start.10 = (bf16[2,128,1024]{2,1,0:T(8,128)(2,1)}, bf16[2,128,1024]{2,1,0:T(8,128)(2,1)}, u32[]{:S(2)}, u32[]{:S(2)}) collective-permute-start(bf16[2,128,1024]{2,1,0:T(8,128)(2,1)} %pad_maximum_fusion.refs_4_), channel_id=1, source_target_pairs={{0,2},{2,0},{4,6},{6,4},{8,10},{10,8},{12,14},{14,12},{1,3},{3,1},... | collective-permute-start | bytes 1572872 | tf_op jit(solution)/shard_map/ppermute | solution.py:327
  22.5 13.4 %collective-permute-start.17 = (bf16[128,1024]{1,0:T(8,128)(2,1)S(1)}, bf16[128,1024]{1,0:T(8,128)(2,1)S(1)}, u32[]{:S(2)}, u32[]{:S(2)}) collective-permute-start(bf16[128,1024]{1,0:T(8,128)(2,1)S(1)} %collective-permute-done.16), channel_id=1, source_target_pairs={{0,2},{2,0},{4,6},{6,4},{8,10},{10,8},{12,14},{14,12},{1,3},{3,1},... | collective-permute-start | bytes 786440 | tf_op jit(solution)/shard_map/ppermute | solution.py:327
  23.2 12.7 %collective-permute-start.29 = (bf16[128,1024]{1,0:T(8,128)(2,1)S(1)}, bf16[128,1024]{1,0:T(8,128)(2,1)}, u32[]{:S(2)}, u32[]{:S(2)}) collective-permute-start(bf16[128,1024]{1,0:T(8,128)(2,1)S(1)} %collective-permute-done.16), channel_id=1, source_target_pairs={{0,4},{2,6},{4,8},{6,10},{8,12},{10,14},{12,0},{14,2},{1,5},{3,7},... | collective-permute-start | bytes 786440 | tf_op jit(solution)/shard_map/ppermute | solution.py:330
  24.0 19.9 %collective-permute-start.6 = (bf16[256,1024]{1,0:T(8,128)(2,1)}, bf16[256,1024]{1,0:T(8,128)(2,1)}, u32[]{:S(2)}, u32[]{:S(2)}) collective-permute-start(bf16[256,1024]{1,0:T(8,128)(2,1)} %constant_dynamic-update-slice_fusion.refs_0_), channel_id=1, source_target_pairs={{0,1},{1,0},{2,3},{3,2},{4,5},{5,4},{6,7},{7,6},{8,9},{9,8},{10,11... | collective-permute-start | bytes 1572872 | tf_op jit(solution)/shard_map/ppermute | solution.py:321
  25.8 18.7 %collective-permute-start.11 = (bf16[2,128,1024]{2,1,0:T(8,128)(2,1)}, bf16[2,128,1024]{2,1,0:T(8,128)(2,1)}, u32[]{:S(2)}, u32[]{:S(2)}) collective-permute-start(bf16[2,128,1024]{2,1,0:T(8,128)(2,1)} %pad_maximum_fusion.refs_4_), channel_id=1, source_target_pairs={{0,16},{16,0},{1,17},{17,1},{2,18},{18,2},{3,19},{19,3},{4,20},{20... | collective-permute-start | bytes 1572872 | tf_op jit(solution)/shard_map/ppermute | solution.py:324
  36.0 10.1 %collective-permute-start.7 = (bf16[256,1024]{1,0:T(8,128)(2,1)}, bf16[256,1024]{1,0:T(8,128)(2,1)}, u32[]{:S(2)}, u32[]{:S(2)}) collective-permute-start(bf16[256,1024]{1,0:T(8,128)(2,1)} %constant_dynamic-update-slice_fusion.refs_0_), channel_id=1, source_target_pairs={{0,16},{16,0},{1,17},{17,1},{2,18},{18,2},{3,19},{19,3},{4,20},{20... | collective-permute-start | bytes 1572872 | tf_op jit(solution)/shard_map/ppermute | solution.py:324
  36.7 16.9 %collective-permute-start.21 = (bf16[2,128,1024]{2,1,0:T(8,128)(2,1)}, bf16[2,128,1024]{2,1,0:T(8,128)(2,1)}, u32[]{:S(2)}, u32[]{:S(2)}) collective-permute-start(bf16[2,128,1024]{2,1,0:T(8,128)(2,1)} %pad_maximum_fusion.refs_4_), channel_id=1, source_target_pairs={{0,4},{2,6},{4,8},{6,10},{8,12},{10,14},{12,0},{14,2},{1,5},{3,7},... | collective-permute-start | bytes 1572872 | tf_op jit(solution)/shard_map/ppermute | solution.py:330
  37.4 16.2 %collective-permute-start.30 = (bf16[128,1024]{1,0:T(8,128)(2,1)}, bf16[128,1024]{1,0:T(8,128)(2,1)}, u32[]{:S(2)}, u32[]{:S(2)}) collective-permute-start(bf16[128,1024]{1,0:T(8,128)(2,1)} %collective-permute-done.29), channel_id=1, source_target_pairs={{0,2},{2,0},{4,6},{6,4},{8,10},{10,8},{12,14},{14,12},{1,3},{3,1},... | collective-permute-start | bytes 786440 | tf_op jit(solution)/shard_map/ppermute | solution.py:327
  43.9 14.1 %collective-permute-start.42 = (bf16[128,1024]{1,0:T(8,128)(2,1)}, bf16[128,1024]{1,0:T(8,128)(2,1)S(1)}, u32[]{:S(2)}, u32[]{:S(2)}) collective-permute-start(bf16[128,1024]{1,0:T(8,128)(2,1)} %collective-permute-done.29), channel_id=1, source_target_pairs={{0,4},{2,6},{4,8},{6,10},{8,12},{10,14},{12,0},{14,2},{1,5},{3,7},... | collective-permute-start | bytes 786440 | tf_op jit(solution)/shard_map/ppermute | solution.py:330
  44.5 17.1 %collective-permute-start.18 = (bf16[256,1024]{1,0:T(8,128)(2,1)S(1)}, bf16[256,1024]{1,0:T(8,128)(2,1)}, u32[]{:S(2)}, u32[]{:S(2)}) collective-permute-start(bf16[256,1024]{1,0:T(8,128)(2,1)S(1)} %constant_dynamic-update-slice_fusion.2.refs_0_), channel_id=1, source_target_pairs={{0,1},{1,0},{2,3},{3,2},{4,5},{5,4},{6,7},{7,6},{8,9},{9,8},{10,11... | collective-permute-start | bytes 1572872 | tf_op jit(solution)/shard_map/ppermute | solution.py:321
  46.1 17.1 %collective-permute-start.19 = (bf16[256,1024]{1,0:T(8,128)(2,1)S(1)}, bf16[256,1024]{1,0:T(8,128)(2,1)S(1)}, u32[]{:S(2)}, u32[]{:S(2)}) collective-permute-start(bf16[256,1024]{1,0:T(8,128)(2,1)S(1)} %constant_dynamic-update-slice_fusion.2.refs_0_), channel_id=1, source_target_pairs={{0,16},{16,0},{1,17},{17,1},{2,18},{18,2},{3,19},{19,3},{4,20},{20... | collective-permute-start | bytes 1572872 | tf_op jit(solution)/shard_map/ppermute | solution.py:324
  53.6 13.0 %collective-permute-start.12 = (bf16[2,128,1024]{2,1,0:T(8,128)(2,1)}, bf16[2,128,1024]{2,1,0:T(8,128)(2,1)S(1)}, u32[]{:S(2)}, u32[]{:S(2)}) collective-permute-start(bf16[2,128,1024]{2,1,0:T(8,128)(2,1)} %collective-permute-done.10.refs_5_), channel_id=1, source_target_pairs={{0,16},{16,0},{1,17},{17,1},{2,18},{18,2},{3,19},{19,3},{4,20},{20... | collective-permute-start | bytes 1572872 | tf_op jit(solution)/shard_map/ppermute | solution.py:324
  53.6 13.0 %collective-permute-start.8 = (bf16[256,1024]{1,0:T(8,128)(2,1)}, bf16[256,1024]{1,0:T(8,128)(2,1)S(1)}, u32[]{:S(2)}, u32[]{:S(2)}) collective-permute-start(bf16[256,1024]{1,0:T(8,128)(2,1)} %collective-permute-done.6.refs_1_), channel_id=1, source_target_pairs={{0,16},{16,0},{1,17},{17,1},{2,18},{18,2},{3,19},{19,3},{4,20},{20... | collective-permute-start | bytes 1572872 | tf_op jit(solution)/shard_map/ppermute | solution.py:324
  61.7 22.1 %collective-permute-start.31 = (bf16[256,1024]{1,0:T(8,128)(2,1)S(1)}, bf16[256,1024]{1,0:T(8,128)(2,1)S(1)}, u32[]{:S(2)}, u32[]{:S(2)}) collective-permute-start(bf16[256,1024]{1,0:T(8,128)(2,1)S(1)} %constant_dynamic-update-slice_fusion.4.refs_0_), channel_id=1, source_target_pairs={{0,1},{1,0},{2,3},{3,2},{4,5},{5,4},{6,7},{7,6},{8,9},{9,8},{10,11... | collective-permute-start | bytes 1572872 | tf_op jit(solution)/shard_map/ppermute | solution.py:321
  64.0 19.8 %collective-permute-start.32 = (bf16[256,1024]{1,0:T(8,128)(2,1)S(1)}, bf16[256,1024]{1,0:T(8,128)(2,1)S(1)}, u32[]{:S(2)}, u32[]{:S(2)}) collective-permute-start(bf16[256,1024]{1,0:T(8,128)(2,1)S(1)} %constant_dynamic-update-slice_fusion.4.refs_0_), channel_id=1, source_target_pairs={{0,16},{16,0},{1,17},{17,1},{2,18},{18,2},{3,19},{19,3},{4,20},{20... | collective-permute-start | bytes 1572872 | tf_op jit(solution)/shard_map/ppermute | solution.py:324
  65.1 13.6 %collective-permute-start.22 = (bf16[2,128,1024]{2,1,0:T(8,128)(2,1)}, bf16[2,128,1024]{2,1,0:T(8,128)(2,1)}, u32[]{:S(2)}, u32[]{:S(2)}) collective-permute-start(bf16[2,128,1024]{2,1,0:T(8,128)(2,1)} %collective-permute-done.21.refs_4_), channel_id=1, source_target_pairs={{0,2},{2,0},{4,6},{6,4},{8,10},{10,8},{12,14},{14,12},{1,3},{3,1},... | collective-permute-start | bytes 1572872 | tf_op jit(solution)/shard_map/ppermute | solution.py:327
  66.6 12.1 %collective-permute-start.23 = (bf16[2,128,1024]{2,1,0:T(8,128)(2,1)}, bf16[2,128,1024]{2,1,0:T(8,128)(2,1)S(1)}, u32[]{:S(2)}, u32[]{:S(2)}) collective-permute-start(bf16[2,128,1024]{2,1,0:T(8,128)(2,1)} %collective-permute-done.21.refs_4_), channel_id=1, source_target_pairs={{0,16},{16,0},{1,17},{17,1},{2,18},{18,2},{3,19},{19,3},{4,20},{20... | collective-permute-start | bytes 1572872 | tf_op jit(solution)/shard_map/ppermute | solution.py:324
  66.6 16.4 %collective-permute-start.34 = (bf16[2,128,1024]{2,1,0:T(8,128)(2,1)}, bf16[2,128,1024]{2,1,0:T(8,128)(2,1)}, u32[]{:S(2)}, u32[]{:S(2)}) collective-permute-start(bf16[2,128,1024]{2,1,0:T(8,128)(2,1)} %collective-permute-done.21.refs_4_), channel_id=1, source_target_pairs={{0,4},{2,6},{4,8},{6,10},{8,12},{10,14},{12,0},{14,2},{1,5},{3,7},... | collective-permute-start | bytes 1572872 | tf_op jit(solution)/shard_map/ppermute | solution.py:330
  79.5 39.1 %collective-permute-start.13 = (bf16[2,256,1024]{2,1,0:T(8,128)(2,1)}, bf16[2,256,1024]{2,1,0:T(8,128)(2,1)}, u32[]{:S(2)}, u32[]{:S(2)}) collective-permute-start(bf16[2,256,1024]{2,1,0:T(8,128)(2,1)} %get-tuple-element.41), channel_id=1, source_target_pairs={{0,16},{16,0},{1,17},{17,1},{2,18},{18,2},{3,19},{19,3},{4,20},{20... | collective-permute-start | bytes 3145736 | tf_op jit(solution)/shard_map/ppermute | solution.py:324
  83.1 13.8 %collective-permute-start.35 = (bf16[2,128,1024]{2,1,0:T(8,128)(2,1)}, bf16[2,128,1024]{2,1,0:T(8,128)(2,1)}, u32[]{:S(2)}, u32[]{:S(2)}) collective-permute-start(bf16[2,128,1024]{2,1,0:T(8,128)(2,1)} %collective-permute-done.34.refs_4_), channel_id=1, source_target_pairs={{0,2},{2,0},{4,6},{6,4},{8,10},{10,8},{12,14},{14,12},{1,3},{3,1},... | collective-permute-start | bytes 1572872 | tf_op jit(solution)/shard_map/ppermute | solution.py:327
  83.8 15.3 %collective-permute-start.47 = (bf16[2,128,1024]{2,1,0:T(8,128)(2,1)}, bf16[2,128,1024]{2,1,0:T(8,128)(2,1)}, u32[]{:S(2)}, u32[]{:S(2)}) collective-permute-start(bf16[2,128,1024]{2,1,0:T(8,128)(2,1)} %collective-permute-done.34.refs_4_), channel_id=1, source_target_pairs={{0,4},{2,6},{4,8},{6,10},{8,12},{10,14},{12,0},{14,2},{1,5},{3,7},... | collective-permute-start | bytes 1572872 | tf_op jit(solution)/shard_map/ppermute | solution.py:330
  88.0 32.8 %collective-permute-start.44 = (bf16[256,1024]{1,0:T(8,128)(2,1)}, bf16[256,1024]{1,0:T(8,128)(2,1)}, u32[]{:S(2)}, u32[]{:S(2)}) collective-permute-start(bf16[256,1024]{1,0:T(8,128)(2,1)} %constant_dynamic-update-slice_fusion.6.refs_0_), channel_id=1, source_target_pairs={{0,1},{1,0},{2,3},{3,2},{4,5},{5,4},{6,7},{7,6},{8,9},{9,8},{10,11... | collective-permute-start | bytes 1572872 | tf_op jit(solution)/shard_map/ppermute | solution.py:321
  89.6 31.9 %collective-permute-start.36 = (bf16[2,128,1024]{2,1,0:T(8,128)(2,1)}, bf16[2,128,1024]{2,1,0:T(8,128)(2,1)}, u32[]{:S(2)}, u32[]{:S(2)}) collective-permute-start(bf16[2,128,1024]{2,1,0:T(8,128)(2,1)} %collective-permute-done.34.refs_4_), channel_id=1, source_target_pairs={{0,16},{16,0},{1,17},{17,1},{2,18},{18,2},{3,19},{19,3},{4,20},{20... | collective-permute-start | bytes 1572872 | tf_op jit(solution)/shard_map/ppermute | solution.py:324
  96.9 24.4 %collective-permute-start.33 = (bf16[256,1024]{1,0:T(8,128)(2,1)}, bf16[256,1024]{1,0:T(8,128)(2,1)}, u32[]{:S(2)}, u32[]{:S(2)}) collective-permute-start(bf16[256,1024]{1,0:T(8,128)(2,1)} %copy-done.34), channel_id=1, source_target_pairs={{0,16},{16,0},{1,17},{17,1},{2,18},{18,2},{3,19},{19,3},{4,20},{20... | collective-permute-start | bytes 1572872 | tf_op jit(solution)/shard_map/ppermute | solution.py:324
  99.1 22.7 %collective-permute-start.48 = (bf16[2,128,1024]{2,1,0:T(8,128)(2,1)}, bf16[2,128,1024]{2,1,0:T(8,128)(2,1)}, u32[]{:S(2)}, u32[]{:S(2)}) collective-permute-start(bf16[2,128,1024]{2,1,0:T(8,128)(2,1)} %collective-permute-done.47.refs_4_), channel_id=1, source_target_pairs={{0,2},{2,0},{4,6},{6,4},{8,10},{10,8},{12,14},{14,12},{1,3},{3,1},... | collective-permute-start | bytes 1572872 | tf_op jit(solution)/shard_map/ppermute | solution.py:327
  120.8 15.6 %collective-permute-start.45 = (bf16[256,1024]{1,0:T(8,128)(2,1)}, bf16[256,1024]{1,0:T(8,128)(2,1)}, u32[]{:S(2)}, u32[]{:S(2)}) collective-permute-start(bf16[256,1024]{1,0:T(8,128)(2,1)} %constant_dynamic-update-slice_fusion.6.refs_0_), channel_id=1, source_target_pairs={{0,16},{16,0},{1,17},{17,1},{2,18},{18,2},{3,19},{19,3},{4,20},{20... | collective-permute-start | bytes 1572872 | tf_op jit(solution)/shard_map/ppermute | solution.py:324
  121.3 16.5 %collective-permute-start.46 = (bf16[256,1024]{1,0:T(8,128)(2,1)}, bf16[256,1024]{1,0:T(8,128)(2,1)}, u32[]{:S(2)}, u32[]{:S(2)}) collective-permute-start(bf16[256,1024]{1,0:T(8,128)(2,1)} %collective-permute-done.44.refs_1_), channel_id=1, source_target_pairs={{0,16},{16,0},{1,17},{17,1},{2,18},{18,2},{3,19},{19,3},{4,20},{20... | collective-permute-start | bytes 1572872 | tf_op jit(solution)/shard_map/ppermute | solution.py:324
  121.4 16.5 %collective-permute-start.49 = (bf16[2,128,1024]{2,1,0:T(8,128)(2,1)}, bf16[2,128,1024]{2,1,0:T(8,128)(2,1)}, u32[]{:S(2)}, u32[]{:S(2)}) collective-permute-start(bf16[2,128,1024]{2,1,0:T(8,128)(2,1)} %collective-permute-done.47.refs_4_), channel_id=1, source_target_pairs={{0,16},{16,0},{1,17},{17,1},{2,18},{18,2},{3,19},{19,3},{4,20},{20... | collective-permute-start | bytes 1572872 | tf_op jit(solution)/shard_map/ppermute | solution.py:324
  121.8 16.0 %collective-permute-start.50 = (bf16[2,128,1024]{2,1,0:T(8,128)(2,1)}, bf16[2,128,1024]{2,1,0:T(8,128)(2,1)}, u32[]{:S(2)}, u32[]{:S(2)}) collective-permute-start(bf16[2,128,1024]{2,1,0:T(8,128)(2,1)} %collective-permute-done.48.refs_5_), channel_id=1, source_target_pairs={{0,16},{16,0},{1,17},{17,1},{2,18},{18,2},{3,19},{19,3},{4,20},{20... | collective-permute-start | bytes 1572872 | tf_op jit(solution)/shard_map/ppermute | solution.py:324
  122.8 34.5 %collective-permute-start.25 = (bf16[2,256,1024]{2,1,0:T(8,128)(2,1)}, bf16[2,256,1024]{2,1,0:T(8,128)(2,1)}, u32[]{:S(2)}, u32[]{:S(2)}) collective-permute-start(bf16[2,256,1024]{2,1,0:T(8,128)(2,1)} %copy-done.42), channel_id=1, source_target_pairs={{0,16},{16,0},{1,17},{17,1},{2,18},{18,2},{3,19},{19,3},{4,20},{20... | collective-permute-start | bytes 3145736 | tf_op jit(solution)/shard_map/ppermute | solution.py:324
  136.4 17.8 %collective-permute-start.14 = (bf16[256,1024]{1,0:T(8,128)(2,1)}, bf16[256,1024]{1,0:T(8,128)(2,1)}, u32[]{:S(2)}, u32[]{:S(2)}) collective-permute-start(bf16[256,1024]{1,0:T(8,128)(2,1)} %fusion.6), channel_id=1, source_target_pairs={{0,1},{1,0},{2,3},{3,2},{4,5},{5,4},{6,7},{7,6},{8,9},{9,8},{10,11... | collective-permute-start | bytes 1572872 | tf_op jit(solution)/shard_map/ppermute | solution.py:321
  137.9 26.8 %collective-permute-start.38 = (bf16[2,256,1024]{2,1,0:T(8,128)(2,1)}, bf16[2,256,1024]{2,1,0:T(8,128)(2,1)}, u32[]{:S(2)}, u32[]{:S(2)}) collective-permute-start(bf16[2,256,1024]{2,1,0:T(8,128)(2,1)} %copy-done.43), channel_id=1, source_target_pairs={{0,16},{16,0},{1,17},{17,1},{2,18},{18,2},{3,19},{19,3},{4,20},{20... | collective-permute-start | bytes 3145736 | tf_op jit(solution)/shard_map/ppermute | solution.py:324
  155.7 67.0 %collective-permute-start.15 = (bf16[128,1024]{1,0:T(8,128)(2,1)S(1)}, bf16[128,1024]{1,0:T(8,128)(2,1)S(1)}, u32[]{:S(2)}, u32[]{:S(2)}) collective-permute-start(bf16[128,1024]{1,0:T(8,128)(2,1)S(1)} %slice.265), channel_id=1, source_target_pairs={{0,2},{2,0},{4,6},{6,4},{8,10},{10,8},{12,14},{14,12},{1,3},{3,1},... | collective-permute-start | bytes 786440 | tf_op jit(solution)/shard_map/ppermute | solution.py:327
  156.5 10.1 %collective-permute-start.51 = (bf16[2,256,1024]{2,1,0:T(8,128)(2,1)S(1)}, bf16[2,256,1024]{2,1,0:T(8,128)(2,1)S(1)}, u32[]{:S(2)}, u32[]{:S(2)}) collective-permute-start(bf16[2,256,1024]{2,1,0:T(8,128)(2,1)S(1)} %copy-done.45), channel_id=1, source_target_pairs={{0,16},{16,0},{1,17},{17,1},{2,18},{18,2},{3,19},{19,3},{4,20},{20... | collective-permute-start | bytes 3145736 | tf_op jit(solution)/shard_map/ppermute | solution.py:324
  160.6 14.9 %collective-permute-start.26 = (bf16[256,1024]{1,0:T(8,128)(2,1)S(1)}, bf16[256,1024]{1,0:T(8,128)(2,1)S(1)}, u32[]{:S(2)}, u32[]{:S(2)}) collective-permute-start(bf16[256,1024]{1,0:T(8,128)(2,1)S(1)} %fusion.7), channel_id=1, source_target_pairs={{0,1},{1,0},{2,3},{3,2},{4,5},{5,4},{6,7},{7,6},{8,9},{9,8},{10,11... | collective-permute-start | bytes 1572872 | tf_op jit(solution)/shard_map/ppermute | solution.py:321
  164.4 45.7 %collective-permute-start.58 = (f32[2,2,128]{2,1,0:T(2,128)S(1)}, f32[2,2,128]{2,1,0:T(2,128)S(1)}, u32[]{:S(2)}, u32[]{:S(2)}) collective-permute-start(f32[2,2,128]{2,1,0:T(2,128)S(1)} %bitcast.150), channel_id=1, source_target_pairs={{0,12},{2,14},{4,0},{6,2},{8,4},{10,6},{12,8},{14,10},{1,13},{3,15... | collective-permute-start | bytes 6152 | tf_op jit(solution)/shard_map/ppermute | solution.py:330
  164.7 45.5 %collective-permute-start.59 = (f32[2,2,128]{2,1,0:T(2,128)S(1)}, f32[2,2,128]{2,1,0:T(2,128)S(1)}, u32[]{:S(2)}, u32[]{:S(2)}) collective-permute-start(f32[2,2,128]{2,1,0:T(2,128)S(1)} %bitcast.149), channel_id=1, source_target_pairs={{0,8},{2,10},{4,12},{6,14},{8,0},{10,2},{12,4},{14,6},{1,9},{3,11}... | collective-permute-start | bytes 6152 | tf_op jit(solution)/shard_map/ppermute | solution.py:330
  166.6 20.1 %collective-permute-start.39 = (bf16[256,1024]{1,0:T(8,128)(2,1)S(1)}, bf16[256,1024]{1,0:T(8,128)(2,1)S(1)}, u32[]{:S(2)}, u32[]{:S(2)}) collective-permute-start(bf16[256,1024]{1,0:T(8,128)(2,1)S(1)} %fusion.8), channel_id=1, source_target_pairs={{0,1},{1,0},{2,3},{3,2},{4,5},{5,4},{6,7},{7,6},{8,9},{9,8},{10,11... | collective-permute-start | bytes 1572872 | tf_op jit(solution)/shard_map/ppermute | solution.py:321
  175.5 21.4 %collective-permute-start.52 = (bf16[256,1024]{1,0:T(8,128)(2,1)S(1)}, bf16[256,1024]{1,0:T(8,128)(2,1)S(1)}, u32[]{:S(2)}, u32[]{:S(2)}) collective-permute-start(bf16[256,1024]{1,0:T(8,128)(2,1)S(1)} %fusion.9), channel_id=1, source_target_pairs={{0,1},{1,0},{2,3},{3,2},{4,5},{5,4},{6,7},{7,6},{8,9},{9,8},{10,11... | collective-permute-start | bytes 1572872 | tf_op jit(solution)/shard_map/ppermute | solution.py:321
  186.7 11.3 %collective-permute-start.27 = (bf16[128,1024]{1,0:T(8,128)(2,1)S(1)}, bf16[128,1024]{1,0:T(8,128)(2,1)S(1)}, u32[]{:S(2)}, u32[]{:S(2)}) collective-permute-start(bf16[128,1024]{1,0:T(8,128)(2,1)S(1)} %slice.264), channel_id=1, source_target_pairs={{0,2},{2,0},{4,6},{6,4},{8,10},{10,8},{12,14},{14,12},{1,3},{3,1},... | collective-permute-start | bytes 786440 | tf_op jit(solution)/shard_map/ppermute | solution.py:327
  198.1 11.6 %collective-permute-start.53 = (bf16[128,1024]{1,0:T(8,128)(2,1)S(1)}, bf16[128,1024]{1,0:T(8,128)(2,1)S(1)}, u32[]{:S(2)}, u32[]{:S(2)}) collective-permute-start(bf16[128,1024]{1,0:T(8,128)(2,1)S(1)} %slice.262), channel_id=1, source_target_pairs={{0,2},{2,0},{4,6},{6,4},{8,10},{10,8},{12,14},{14,12},{1,3},{3,1},... | collective-permute-start | bytes 786440 | tf_op jit(solution)/shard_map/ppermute | solution.py:327
  206.1 16.0 %collective-permute-start.60 = (f32[2,2,128]{2,1,0:T(2,128)S(1)}, f32[2,2,128]{2,1,0:T(2,128)S(1)}, u32[]{:S(2)}, u32[]{:S(2)}) collective-permute-start(f32[2,2,128]{2,1,0:T(2,128)S(1)} %bitcast.146), channel_id=1, source_target_pairs={{0,4},{2,6},{4,8},{6,10},{8,12},{10,14},{12,0},{14,2},{1,5},{3,7},... | collective-permute-start | bytes 6152 | tf_op jit(solution)/shard_map/ppermute | solution.py:330
  209.7 13.1 %collective-permute-start.28 = (bf16[128,1024]{1,0:T(8,128)(2,1)S(1)}, bf16[128,1024]{1,0:T(8,128)(2,1)S(1)}, u32[]{:S(2)}, u32[]{:S(2)}) collective-permute-start(bf16[128,1024]{1,0:T(8,128)(2,1)S(1)} %fusion.12), channel_id=1, source_target_pairs={{0,12},{2,14},{4,0},{6,2},{8,4},{10,6},{12,8},{14,10},{1,13},{3,15... | collective-permute-start | bytes 786440 | tf_op jit(solution)/shard_map/ppermute | solution.py:330
  210.1 20.8 %collective-permute-start.41 = (bf16[128,1024]{1,0:T(8,128)(2,1)S(1)}, bf16[128,1024]{1,0:T(8,128)(2,1)S(1)}, u32[]{:S(2)}, u32[]{:S(2)}) collective-permute-start(bf16[128,1024]{1,0:T(8,128)(2,1)S(1)} %fusion.11), channel_id=1, source_target_pairs={{0,8},{2,10},{4,12},{6,14},{8,0},{10,2},{12,4},{14,6},{1,9},{3,11}... | collective-permute-start | bytes 786440 | tf_op jit(solution)/shard_map/ppermute | solution.py:330
  210.2 20.7 %collective-permute-start.54 = (bf16[128,1024]{1,0:T(8,128)(2,1)S(1)}, bf16[128,1024]{1,0:T(8,128)(2,1)S(1)}, u32[]{:S(2)}, u32[]{:S(2)}) collective-permute-start(bf16[128,1024]{1,0:T(8,128)(2,1)S(1)} %fusion.10), channel_id=1, source_target_pairs={{0,4},{2,6},{4,8},{6,10},{8,12},{10,14},{12,0},{14,2},{1,5},{3,7},... | collective-permute-start | bytes 786440 | tf_op jit(solution)/shard_map/ppermute | solution.py:330
  (70 other events, 427.3 us)

commit v4 on v0

--- a/solution.py
+++ b/solution.py
@@ -1,6 +1,11 @@
+import functools
+import math
+
 import jax
 import jax.numpy as jnp
 from jax import lax
+from jax.experimental import pallas as pl
+from jax.experimental.pallas import tpu as pltpu
 from jax.sharding import PartitionSpec as P
 
 
@@ -8,7 +13,7 @@
     return jnp.concatenate([array, jnp.zeros((1, array.shape[1]), array.dtype)], 0)
 
 
-def per_device(tokens, out_grad, routes, probs, w_gate, w_up, w_down):
+def routed_device(tokens, out_grad, routes, probs, w_gate, w_up, w_down):
     owners = lax.axis_size(("role", "ep"))
     tok_rows, top_count = routes.shape
     width_full = w_gate.shape[1]
@@ -112,6 +117,320 @@
     )
 
 
+def slot_capacity(tok_rows, top_count, owners):
+    return min(tok_rows, tok_rows * top_count * 9 // (8 * owners))
+
+
+def weights_kernel(tp_ref, wg_ref, wu_ref, wd_ref, both_ref, down_ref):
+    part = wg_ref.shape[2]
+    both_ref[:, :part] = wg_ref[0]
+    both_ref[:, part:] = wu_ref[0]
+    down_ref[...] = wd_ref[0]
+
+
+def weights_call(which, w_gate, w_up, w_down):
+    _, width, part = w_gate.shape
+    half = width // 2
+
+    def place(i, w):
+        return (i + w[0]) % 2
+
+    return pl.pallas_call(
+        weights_kernel,
+        grid_spec=pltpu.PrefetchScalarGridSpec(
+            num_scalar_prefetch=1,
+            grid=(2,),
+            in_specs=[
+                pl.BlockSpec((1, half, part), lambda i, w: (0, place(i, w), 0)),
+                pl.BlockSpec((1, half, part), lambda i, w: (0, place(i, w), 0)),
+                pl.BlockSpec((1, part, half), lambda i, w: (0, 0, place(i, w))),
+            ],
+            out_specs=[
+                pl.BlockSpec((half, 2 * part), lambda i, w: (i, 0)),
+                pl.BlockSpec((part, half), lambda i, w: (0, i)),
+            ],
+        ),
+        out_shape=[
+            jax.ShapeDtypeStruct((width, 2 * part), jnp.bfloat16),
+            jax.ShapeDtypeStruct((part, width), jnp.bfloat16),
+        ],
+        compiler_params=pltpu.CompilerParams(vmem_limit_bytes=24 << 20),
+        cost_estimate=pl.CostEstimate(flops=0, bytes_accessed=12 * width * part, transcendentals=0),
+        name="weights",
+    )(which, w_gate, w_up, w_down)
+
+
+def rows_kernel(step, y_first, slots, slot_ref, p_ref, *refs):
+    weights_in, units_in, refs = refs[:4], refs[4:8], refs[len(refs) - 21 :]
+    outs, refs = refs[:4], refs[4:]
+    score_ref, keep_ref, send_ref, x_all, g_all, wgu0, wgu1, wd0, wd1, xc, gc, both, scaled, piece = refs[:14]
+    unit_sems, weight_sems, out_sems = refs[14:]
+    half, tok = x_all.shape[2], x_all.shape[1] // 2
+    part = scaled.shape[1]
+    wgu, wd = (wgu0, wgu1), (wd0, wd1)
+
+    x_copies, g_copies = [], []
+    for index, unit in enumerate(units_in):
+        rows = pl.ds(index // 2 * tok, tok)
+        x_copies.append(pltpu.make_async_copy(unit.at[pl.ds(0, tok)], x_all.at[index % 2, rows], unit_sems.at[0, index]))
+        g_copies.append(pltpu.make_async_copy(unit.at[pl.ds(tok, tok)], g_all.at[index % 2, rows], unit_sems.at[1, index]))
+    weight_copies = [
+        pltpu.make_async_copy(source, target, weight_sems.at[index])
+        for index, (source, target) in enumerate(zip(weights_in, (wgu0, wgu1, wd0, wd1)))
+    ]
+    for copy in x_copies + weight_copies[:2] + g_copies + weight_copies[2:]:
+        copy.start()
+    leaving = []
+
+    def leave(source, target):
+        copy = pltpu.make_async_copy(source, target, out_sems.at[len(leaving)])
+        copy.start()
+        leaving.append(copy)
+
+    def leave_rows(held, target):
+        for expert in range(2):
+            leave(held.at[pl.ds(expert * slots, slots)], target.at[expert, pl.ds(step * slots, slots)])
+
+    def dot(a, b, dims):
+        return lax.dot_general(a, b, (dims, ((), ())), preferred_element_type=jnp.float32)
+
+    number = lax.broadcasted_iota(jnp.int32, (slots, 2 * tok), 0)
+    picks = [(number == slot_ref[expert : expert + 1, :]).astype(jnp.float32) for expert in range(2)]
+    prob = [jnp.sum(picks[e] * p_ref[e : e + 1, :], axis=1, keepdims=True) for e in range(2)]
+    low_picks = [item.astype(jnp.bfloat16) for item in picks]
+    all_picks = jnp.concatenate(low_picks, 0)
+    spans = [slice(expert * slots, (expert + 1) * slots) for expert in range(2)]
+    sides = [slice(side * half, (side + 1) * half) for side in range(2)]
+    for copy in x_copies:
+        copy.wait()
+    for side in range(2):
+        xc[:, sides[side]] = dot(all_picks, x_all[side], ((1,), (0,))).astype(jnp.bfloat16)
+    leave_rows(xc, outs[0])
+    rows = []
+    for expert in range(2):
+        weight_copies[expert].wait()
+        rows.append(dot(xc[spans[expert], :], wgu[expert][...], ((1,), (0,))))
+    for copy in g_copies:
+        copy.wait()
+    for side in range(2):
+        gc[:, sides[side]] = dot(all_picks, g_all[side], ((1,), (0,))).astype(jnp.bfloat16)
+    leave_rows(gc, outs[1])
+    for expert in range(2):
+        weight_copies[2 + expert].wait()
+        back = dot(gc[spans[expert], :], wd[expert][...], ((1,), (1,)))
+        gate, up = rows[expert][:, :part], rows[expert][:, part:]
+        sig = jax.nn.sigmoid(gate)
+        act = gate * sig
+        hidden = act * up
+        score = jnp.sum(hidden * back, axis=1, keepdims=True)
+        score_ref[expert : expert + 1, :] = jnp.sum(picks[expert] * score, axis=0, keepdims=True)
+        hgrad = prob[expert] * back
+        both[spans[expert], :part] = (hgrad * up * sig * (1.0 + gate * (1.0 - sig))).astype(jnp.bfloat16)
+        both[spans[expert], part:] = (hgrad * act).astype(jnp.bfloat16)
+        scaled[spans[expert], :] = (prob[expert] * hidden).astype(jnp.bfloat16)
+    leave_rows(both, outs[2])
+    leave_rows(scaled, outs[3])
+    for side in (1, 0):
+        total = None
+        for expert in range(2):
+            low = dot(both[spans[expert], :], wgu[expert][sides[side], :], ((1,), (1,))).astype(jnp.bfloat16)
+            term = dot(low_picks[expert], low, ((0,), (0,)))
+            total = term if total is None else total + term
+        piece[side] = total.astype(jnp.bfloat16)
+        for y in range(2):
+            first, second = (y, side) if y_first else (side, y)
+            leave(piece.at[side, pl.ds(y * tok, tok)], (send_ref if first else keep_ref).at[second])
+    for copy in leaving:
+        copy.wait()
+
+
+def rows_call(step, steps, slots, slot, prob, weights, units, held):
+    pair, half = units[0].shape
+    part, width = weights[2].shape
+    loose = pl.BlockSpec(memory_space=pl.ANY)
+    widths = (width, width, 2 * part, part)
+    return pl.pallas_call(
+        functools.partial(rows_kernel, step, step % 2 == 1, slots),
+        grid=(1,),
+        in_specs=[pl.BlockSpec((2, pair), lambda i: (0, 0))] * 2 + [loose] * (8 + len(held)),
+        out_specs=[loose] * 4 + [pl.BlockSpec((2, pair), lambda i: (0, 0))] + [loose] * 2,
+        out_shape=[jax.ShapeDtypeStruct((2, steps * slots, size), jnp.bfloat16) for size in widths]
+        + [jax.ShapeDtypeStruct((2, pair), jnp.float32)]
+        + [jax.ShapeDtypeStruct((2, pair // 2, half), jnp.bfloat16)] * 2,
+        scratch_shapes=[pltpu.VMEM((2, pair, half), jnp.bfloat16)] * 2
+        + [pltpu.VMEM((width, 2 * part), jnp.bfloat16)] * 2
+        + [pltpu.VMEM((part, width), jnp.bfloat16)] * 2
+        + [pltpu.VMEM((2 * slots, size), jnp.bfloat16) for size in widths]
+        + [
+            pltpu.VMEM((2, pair, half), jnp.bfloat16),
+            pltpu.SemaphoreType.DMA((2, 4)),
+            pltpu.SemaphoreType.DMA((4,)),
+            pltpu.SemaphoreType.DMA((12,)),
+        ],
+        input_output_aliases={10 + i: i for i in range(len(held))},
+        compiler_params=pltpu.CompilerParams(vmem_limit_bytes=56 << 20),
+        cost_estimate=pl.CostEstimate(
+            flops=20 * slots * width * part + 12 * slots * pair * width,
+            bytes_accessed=8 * pair * width + 12 * width * part,
+            transcendentals=2 * slots * part,
+        ),
+        name="rows",
+    )(slot, prob, *weights, *units, *held)
+
+
+def grads_kernel(first, tp_ref, x_ref, g_ref, both_ref, scaled_ref, *refs):
+    part = scaled_ref.shape[2]
+    dims = (((0,), (0,)), ((), ()))
+    both = lax.dot_general(x_ref[0], both_ref[0], dims, preferred_element_type=jnp.float32)
+    down = lax.dot_general(scaled_ref[0], g_ref[0], dims, preferred_element_type=jnp.float32)
+    if first:
+        refs[0][...] = both.astype(jnp.bfloat16)
+        refs[1][...] = down.astype(jnp.bfloat16)
+        return
+    more_both, more_down, dg_ref, du_ref, dd_ref = refs
+    both = both + more_both[...].astype(jnp.float32)
+    dg_ref[0] = both[:, :part].astype(jnp.bfloat16)
+    du_ref[0] = both[:, part:].astype(jnp.bfloat16)
+    dd_ref[0] = (down + more_down[...].astype(jnp.float32)).astype(jnp.bfloat16)
+
+
+def grads_call(which, expert, x_rows, g_rows, both, scaled, more=()):
+    _, total, width = x_rows.shape
+    part = scaled.shape[2]
+    step = math.gcd(width // 2, 256)
+    per = width // 2 // step
+
+    def place(i, w):
+        return (i + w[0] * per) % (2 * per)
+
+    moving = pl.BlockSpec((1, total, step), lambda i, w: (expert, 0, i))
+    passing = [
+        pl.BlockSpec((step, 2 * part), lambda i, w: (i, 0)),
+        pl.BlockSpec((part, step), lambda i, w: (0, i)),
+    ]
+    if more:
+        out_specs = [
+            pl.BlockSpec((1, step, part), lambda i, w: (0, place(i, w), 0)),
+            pl.BlockSpec((1, step, part), lambda i, w: (0, place(i, w), 0)),
+            pl.BlockSpec((1, part, step), lambda i, w: (0, 0, place(i, w))),
+        ]
+        shapes = [(1, width, part), (1, width, part), (1, part, width)]
+    else:
+        out_specs = passing
+        shapes = [(width, 2 * part), (part, width)]
+    return pl.pallas_call(
+        functools.partial(grads_kernel, not more),
+        grid_spec=pltpu.PrefetchScalarGridSpec(
+            num_scalar_prefetch=1,
+            grid=(width // step,),
+            in_specs=[
+                moving,
+                moving,
+                pl.BlockSpec((1, total, 2 * part), lambda i, w: (expert, 0, 0)),
+                pl.BlockSpec((1, total, part), lambda i, w: (expert, 0, 0)),
+            ]
+            + (passing if more else []),
+            out_specs=out_specs,
+        ),
+        out_shape=[jax.ShapeDtypeStruct(shape, jnp.bfloat16) for shape in shapes],
+        compiler_params=pltpu.CompilerParams(vmem_limit_bytes=40 << 20),
+        cost_estimate=pl.CostEstimate(flops=6 * total * width * part, bytes_accessed=6 * total * width, transcendentals=0),
+        name="grads",
+    )(which, x_rows, g_rows, both, scaled, *more)
+
+
+def dense_device(tokens, out_grad, routes, probs, w_gate, w_up, w_down):
+    owners = lax.axis_size(("role", "ep"))
+    ep = lax.axis_size("ep")
+    n_y = 2
+    n_z = ep // n_y
+    tok_rows, half = tokens.shape
+    capacity = slot_capacity(tok_rows, routes.shape[1], owners)
+    slots = -(-n_y * capacity // 16) * 16
+    role, place, which = lax.axis_index("role"), lax.axis_index("ep"), lax.axis_index("tp")
+    my_z, my_y = place // n_y, place % n_y
+
+    def over_x(array):
+        return lax.ppermute(array, "tp", [(0, 1), (1, 0)])
+
+    def over_role(array):
+        return lax.ppermute(array, "role", [(0, 1), (1, 0)])
+
+    def over_y(array):
+        return lax.ppermute(array, "ep", [(i, i + 1 - 2 * (i % n_y)) for i in range(ep)])
+
+    def over_z(array, shift):
+        return lax.ppermute(array, "ep", [(i, (i + shift * n_y) % ep) for i in range(ep)])
+
+    units = {(0, 0, 0): jnp.concatenate([tokens, out_grad], 0)}
+    for z in range(n_z):
+        if z:
+            units[z, 0, 0] = over_z(units[z - 1, 0, 0], 1)
+        units[z, 1, 0] = over_y(units[z, 0, 0])
+        units[z, 0, 1] = over_x(units[z, 0, 0])
+        if z == 0:
+            units[z, 1, 1] = over_x(units[z, 1, 0])
+        elif z < n_z - 1:
+            units[z, 1, 1] = over_z(units[z - 1, 1, 1], 1)
+        else:
+            units[z, 1, 1] = over_y(units[z, 0, 1])
+
+    which_ref = which.reshape(1).astype(jnp.int32)
+    both_w, down_w = weights_call(which_ref, w_gate, w_up, w_down)
+    weights = (both_w, over_role(both_w), down_w, over_role(down_w))
+
+    chosen = routes[:, :, None] == jnp.arange(owners, dtype=jnp.int32)
+    table = jnp.sum(jnp.where(chosen, probs[:, :, None].astype(jnp.float32) + 1.0, 0.0), axis=1) - 1.0
+    table = table.astype(jnp.bfloat16).T
+    tables = jnp.stack([table, over_y(table)])
+    tables = jnp.stack([tables] + [over_z(tables, step) for step in range(1, n_z)])
+    tables = tables.reshape(n_z, n_y, 2, ep, tok_rows)
+    prob = lax.dynamic_slice_in_dim(tables, place, 1, 3)[:, :, :, 0].astype(jnp.float32)
+    prob = jnp.where(role == 0, prob, prob[:, :, ::-1])
+    routed = prob >= 0.0
+    before = jnp.triu(jnp.ones((tok_rows, tok_rows), jnp.bfloat16), 1)
+    slot = jnp.dot(routed.astype(jnp.bfloat16), before, preferred_element_type=jnp.float32).astype(jnp.int32)
+    slot = jnp.where(routed, slot + capacity * jnp.arange(n_y, dtype=jnp.int32)[:, None, None], -1)
+    slot = slot.transpose(0, 2, 1, 3).reshape(n_z, 2, n_y * tok_rows)
+    prob = prob.transpose(0, 2, 1, 3).reshape(n_z, 2, n_y * tok_rows)
+
+    def add(a, b):
+        return a.astype(jnp.float32) + b.astype(jnp.float32)
+
+    held, scores, homeward = (), [], []
+    for z in range(n_z):
+        four = [units[z, y, x] for y in range(2) for x in range(2)]
+        *held, score, keep, send = rows_call(z, n_z, slots, slot[z], prob[z], weights, four, held)
+        scores.append(score)
+        go_first, go_second = (over_y, over_x) if z % 2 else (over_x, over_y)
+        recv = go_first(send)
+        recv_next = go_second(add(keep[1], recv[1]).astype(jnp.bfloat16))
+        total = add(add(keep[0], recv[0]), recv_next)
+        homeward.append(over_z(total.astype(jnp.bfloat16), -z).astype(jnp.float32) if z else total)
+    d_tok = sum(homeward[1:], homeward[0]).astype(jnp.bfloat16)
+    more = grads_call(which_ref, 1, *held)
+    d_gate, d_up, d_down = grads_call(which_ref, 0, *held, [over_role(item) for item in more])
+
+    mine = jnp.stack(scores).reshape(n_z, 2, n_y, tok_rows)
+    mine = mine + over_x(mine)
+    mine = jnp.stack([mine[:, :, 0], over_y(mine[:, :, 1])])
+    mine = jnp.stack([mine[:, 0]] + [over_z(mine[:, step], -step) for step in range(1, n_z)])
+    steps = jnp.arange(n_z)[:, None, None]
+    source = (my_z + steps) % n_z * n_y + ((my_y + jnp.arange(n_y)) % n_y)[:, None] + (role + jnp.arange(2)) % 2 * ep
+    picked = routes[:, :, None] == source.reshape(-1)
+    d_probs = jnp.sum(jnp.where(picked, mine.reshape(owners, tok_rows).T[:, None, :], 0.0), axis=2)
+    return d_tok, d_probs, d_gate, d_up, d_down
+
+
+def per_device(tokens, out_grad, routes, probs, w_gate, w_up, w_down):
+    owners = lax.axis_size(("role", "ep"))
+    tok_rows, top_count = routes.shape
+    paired = lax.axis_size("tp") == 2 and lax.axis_size("role") == 2 and lax.axis_size("ep") % 2 == 0
+    if paired and 2 * slot_capacity(tok_rows, top_count, owners) >= tok_rows:
+        return dense_device(tokens, out_grad, routes, probs, w_gate, w_up, w_down)
+    return routed_device(tokens, out_grad, routes, probs, w_gate, w_up, w_down)
+
+
 def solution(mesh):
     in_specs = (
         P(("groups", "role", "ep"), "tp"),

time: 367 us -> 225 us (0.61)
  blocking collectives: 148 us -> 0 us
  Pallas kernels: 0 us -> 64.4 us
  starting transfers between devices: 5.8 us -> 49.2 us
  matrix products: 34.4 us -> 0.09 us
  local copies, waits for them, and re-layouts: 37.4 us -> 17.1 us
  waiting for transfers between devices: 106 us -> 86.3 us
  other arithmetic: 20.2 us -> 5.74 us
  between operations: 14 us -> 1.17 us
    all_to_all x4 -> x0, blocking collectives: 143 us -> none  [the longest x1 62.8 us: per_device(): lax.all_to_all(send_x.reshape(owners, capacity, tokens.shape[1]), ('role'...]
    ppermute x0 -> x39, waiting for transfers between devices: none -> 86.3 us  [the longest x10 35.3 us: over_x(): return lax.ppermute(array, 'tp', [(0, 1), (1, 0)])]
    pallas_call x0 -> x7, Pallas kernels: none -> 64.4 us  [the longest x4 44.6 us: rows_call(): pl.pallas_call(functools.partial(rows_kernel, step, step % 2 == 1, slots)...]
    ppermute x0 -> x39, starting transfers between devices: none -> 49.2 us  [the longest x14 23.8 us: over_z(): lax.ppermute(array, 'ep', [(i, (i + shift * n_y) % ep) for i in range(ep)])]
    reduce_scatter x1 -> x0, waiting for transfers between devices: 43.3 us -> none  [per_device(): lax.psum_scatter(partial_low.reshape(owners, capacity, width_full), 'tp',...]
    all_gather x2 -> x0, waiting for transfers between devices: 34.5 us -> none  [the longest x1 34.5 us: per_device(): lax.all_gather(slice_g, 'tp', axis=2, tiled=True)]
    dot_general x5 -> x1, matrix products: 34.4 us -> 0.09 us  [dense_device(): jnp.dot(routed.astype(jnp.bfloat16), before, preferred_element_type=jnp.f...]
    all_to_all x1 -> x0, waiting for transfers between devices: 28 us -> none  [per_device(): lax.all_to_all(summed_low, ('role', 'ep'), split_axis=0, concat_axis=0, t...]
  transfers between devices with their start and end apart: 4 -> 39, of which waited for: 3 -> 13; matrix products, arithmetic and copies ran while one was open for 12% -> 4% of each run, Pallas kernels for 0% -> 15%
where the time goes in v4:
time: 225 us; the launch traced here: 224 us
  waiting for transfers between devices  86.3 us (38%)
  Pallas kernels  64.4 us (29%)
  starting transfers between devices  49.2 us (22%)
  local copies, waits for them, and re-layouts  17.1 us (8%)
  other arithmetic  5.74 us (3%)
    pallas_call x4, Pallas kernels, rows_call(): pl.pallas_call(functools.partial(rows_kernel, step, step % 2 == 1, slots)...  44.6 us
    ppermute x10, waiting for transfers between devices, over_x(): return lax.ppermute(array, 'tp', [(0, 1), (1, 0)])  35.3 us
    ppermute x11, waiting for transfers between devices, over_y(): lax.ppermute(array, 'ep', [(i, i + 1 - 2 * (i % n_y)) for i in range(ep)])  28.6 us
    ppermute x14, starting transfers between devices, over_z(): lax.ppermute(array, 'ep', [(i, (i + shift * n_y) % ep) for i in range(ep)])  23.8 us
    ppermute x14, waiting for transfers between devices, over_z(): lax.ppermute(array, 'ep', [(i, (i + shift * n_y) % ep) for i in range(ep)])  22.4 us
    pallas_call x2, Pallas kernels, grads_call(): pl.pallas_call(functools.partial(grads_kernel, not more), grid_spec=pltpu...  18.4 us
    unnamed x80, local copies, waits for them, and re-layouts  15 us
    ppermute x11, starting transfers between devices, over_y(): lax.ppermute(array, 'ep', [(i, i + 1 - 2 * (i % n_y)) for i in range(ep)])  13.2 us
  transfers between devices with their start and end apart: 39, of which 13 were waited for; matrix products, arithmetic and copies ran while one was open for 4% of the time, Pallas kernels for 15%

profile of v4, /device:TPU:0, one launch (start us, length us, event | category | flops | bytes accessed | tf_op | source)
XLA Modules:
  0.0 224.1 jit_solution(14014692684287500404)
XLA Ops:
  0.6 1.4 copy-done.7
  2.0 1.4 copy-done.8
  3.5 1.4 copy-done.9
  4.9 1.5 weights.1
  6.8 1.1 constant_dynamic-update-slice_fusion.1
  8.7 2.5 %collective-permute-start.7 = (bf16[256,1024]{1,0:T(8,128)(2,1)}, bf16[256,1024]{1,0:T(8,128)(2,1)}, u32[]{:S(2)}, u32[]{:S(2)}) collective-permute-start(bf16[256,1024]{1,0:T(8,128)(2,1)} %constant_dynamic-update-slice_fusion.refs_4_), channel_id=1, source_target_pairs={{0,2},{2,0},{4,6},{6,4},{8,10},{10,8},{12,14},{14,12},{1,3},{3,1},... | collective-permute-start | bytes 1572872 | tf_op jit(solution)/shard_map/ppermute | solution.py:360
  11.2 1.6 collective-permute-start.11
  13.4 10.7 %collective-permute-done = bf16[16,128]{1,0:T(8,128)(2,1)S(1)} collective-permute-done((bf16[16,128]{1,0:T(8,128)(2,1)S(1)}, bf16[16,128]{1,0:T(8,128)(2,1)S(1)}, u32[]{:S(2)}, u32[]{:S(2)}) %collective-permute-start) | collective-permute-done | bytes 4128 | tf_op jit(solution)/shard_map/ppermute | solution.py:360
  24.1 1.8 collective-permute-start.1
  25.9 3.7 %collective-permute-done.1 = bf16[2,16,128]{2,1,0:T(8,128)(2,1)S(1)} collective-permute-done((bf16[2,16,128]{2,1,0:T(8,128)(2,1)S(1)}, bf16[2,16,128]{2,1,0:T(8,128)(2,1)S(1)}, u32[]{:S(2)}, u32[]{:S(2)}) %collective-permute-start.1) | collective-permute-done | bytes 8224 | tf_op jit(solution)/shard_map/ppermute | solution.py:363
  29.5 1.0 collective-permute-start.2
  30.5 3.5 %collective-permute-done.2 = bf16[2,16,128]{2,1,0:T(8,128)(2,1)S(1)} collective-permute-done((bf16[2,16,128]{2,1,0:T(8,128)(2,1)S(1)}, bf16[2,16,128]{2,1,0:T(8,128)(2,1)S(1)}, u32[]{:S(2)}, u32[]{:S(2)}) %collective-permute-start.2) | collective-permute-done | bytes 8224 | tf_op jit(solution)/shard_map/ppermute | solution.py:363
  34.1 2.0 collective-permute-start.3
  36.1 1.6 collective-permute-done.3
  37.7 1.7 collective-permute-start.6
  40.0 12.9 %collective-permute-done.6.refs_5_ = bf16[256,1024]{1,0:T(8,128)(2,1)} collective-permute-done((bf16[256,1024]{1,0:T(8,128)(2,1)}, bf16[256,1024]{1,0:T(8,128)(2,1)}, u32[]{:S(2)}, u32[]{:S(2)}) %collective-permute-start.6) | collective-permute-done | bytes 524320 | tf_op jit(solution)/shard_map/ppermute | solution.py:354
  52.9 1.7 collective-permute-start.12
  54.7 9.4 %collective-permute-done.8.refs_7_ = bf16[256,1024]{1,0:T(8,128)(2,1)S(1)} collective-permute-done((bf16[256,1024]{1,0:T(8,128)(2,1)}, bf16[256,1024]{1,0:T(8,128)(2,1)S(1)}, u32[]{:S(2)}, u32[]{:S(2)}) %collective-permute-start.8) | collective-permute-done | bytes 524320 | tf_op jit(solution)/shard_map/ppermute | solution.py:354
  64.1 7.1 %collective-permute-done.12.refs_5_ = bf16[256,1024]{1,0:T(8,128)(2,1)S(1)} collective-permute-done((bf16[256,1024]{1,0:T(8,128)(2,1)}, bf16[256,1024]{1,0:T(8,128)(2,1)S(1)}, u32[]{:S(2)}, u32[]{:S(2)}) %collective-permute-start.12) | collective-permute-done | bytes 524320 | tf_op jit(solution)/shard_map/ppermute | solution.py:354
  71.2 2.8 %collective-permute-start.13 = (bf16[256,1024]{1,0:T(8,128)(2,1)}, bf16[256,1024]{1,0:T(8,128)(2,1)S(1)}, u32[]{:S(2)}, u32[]{:S(2)}) collective-permute-start(bf16[256,1024]{1,0:T(8,128)(2,1)} %collective-permute-done.11.refs_4_), channel_id=1, source_target_pairs={{0,2},{2,0},{4,6},{6,4},{8,10},{10,8},{12,14},{14,12},{1,3},{3,1},... | collective-permute-start | bytes 1572872 | tf_op jit(solution)/shard_map/ppermute | solution.py:360
  74.0 1.5 collective-permute-start.26
  77.5 2.0 collective-permute-start.20
  79.6 11.0 %rows.4 = (bf16[2,576,2048]{2,1,0:T(8,128)(2,1)}, bf16[2,576,2048]{2,1,0:T(8,128)(2,1)}, bf16[2,576,768]{2,1,0:T(8,128)(2,1)}, bf16[2,576,384]{2,1,0:T(8,128)(2,...) custom-call(s32[2,256]{1,0:T(2,128)} %bitcast.106, f32[2,256]{1,0:T(2,128)} %bitcast.107, ...), custom_call_target="tpu_custom_call" | custom-call | flops 3170893824 | bytes 13631488 | tf_op jit(solution)/shard_map/rows/pallas_call | solution.py:252
  91.0 1.8 collective-permute-start.28
  92.7 11.1 %rows.5 = (bf16[2,576,2048]{2,1,0:T(8,128)(2,1)}, bf16[2,576,2048]{2,1,0:T(8,128)(2,1)}, bf16[2,576,768]{2,1,0:T(8,128)(2,1)}, bf16[2,576,384]{2,1,0:T(8,128)(2,...) custom-call(s32[2,256]{1,0:T(2,128)} %bitcast.97, ...), custom_call_target="tpu_custom_call", output_to_operand_aliasing={{0}: (10, {}), {1}: (11, {}), {2}: (12, {}), {3}: (13, {})} | custom-call | flops 3170893824 | bytes 13631488 | tf_op jit(solution)/shard_map/rows/pallas_call | solution.py:252
  105.1 11.4 %rows.6 = (bf16[2,576,2048]{2,1,0:T(8,128)(2,1)}, bf16[2,576,2048]{2,1,0:T(8,128)(2,1)}, bf16[2,576,768]{2,1,0:T(8,128)(2,1)}, bf16[2,576,384]{2,1,0:T(8,128)(2,...) custom-call(s32[2,256]{1,0:T(2,128)} %bitcast.95, ...), custom_call_target="tpu_custom_call", output_to_operand_aliasing={{0}: (10, {}), {1}: (11, {}), {2}: (12, {}), {3}: (13, {})} | custom-call | flops 3170893824 | bytes 13631488 | tf_op jit(solution)/shard_map/rows/pallas_call | solution.py:252
  117.5 11.1 %rows.7 = (bf16[2,576,2048]{2,1,0:T(8,128)(2,1)}, bf16[2,576,2048]{2,1,0:T(8,128)(2,1)}, bf16[2,576,768]{2,1,0:T(8,128)(2,1)}, bf16[2,576,384]{2,1,0:T(8,128)(2,...) custom-call(s32[2,256]{1,0:T(2,128)} %bitcast.93, ...), custom_call_target="tpu_custom_call", output_to_operand_aliasing={{0}: (10, {}), {1}: (11, {}), {2}: (12, {}), {3}: (13, {})} | custom-call | flops 3170893824 | bytes 13631488 | tf_op jit(solution)/shard_map/rows/pallas_call | solution.py:252
  128.6 2.3 %copy-done = bf16[2,576,2048]{2,1,0:T(8,128)(2,1)S(1)} copy-done((bf16[2,576,2048]{2,1,0:T(8,128)(2,1)S(1)}, bf16[2,576,2048]{2,1,0:T(8,128)(2,1)}, u32[]{:S(2)}) %copy-start) | copy-done | bytes 4718616
  131.0 1.5 copy-done.2
  132.4 1.2 copy-done.5
  133.6 9.0 %grads.2 = (bf16[2048,768]{1,0:T(8,128)(2,1)}, bf16[384,2048]{1,0:T(8,128)(2,1)}) custom-call(s32[1]{0:T(128)} %bitcast.16.tp_ref, bf16[2,576,2048]{2,1,0:T(8,128)(2,1)S(1)} %copy-done, bf16[2,576,2048]{2,1,0:T(8,128)(2,1)} %get-tuple-element.67.g_ref, bf16[2,576,768]{2,1,0:T(8,128)(2,1)S(1)} %copy-done.2, bf16[2,576,384]{2,1,0:T(8,128)(2,1)S(1)} %copy-done.5), custom_call_target="tpu_custom_call" | custom-call | flops 2717908992 | bytes 7077888 | tf_op jit(solution)/shard_map/grads/pallas_call | solution.py:321
  144.2 1.0 collective-permute-start.22
  145.2 1.3 collective-permute-done.32
  147.2 10.4 %collective-permute-done.33 = f32[4,2,128]{2,1,0:T(2,128)S(1)} collective-permute-done((f32[4,2,128]{2,1,0:T(2,128)S(1)}, f32[4,2,128]{2,1,0:T(2,128)S(1)}, u32[]{:S(2)}, u32[]{:S(2)}) %collective-permute-start.33) | collective-permute-done | bytes 4128 | tf_op jit(solution)/shard_map/ppermute | solution.py:360
  158.4 1.1 collective-permute-start.9
  159.5 3.9 %collective-permute-start.34 = (f32[2,2,128]{2,1,0:T(2,128)S(1)}, f32[2,2,128]{2,1,0:T(2,128)S(1)}, u32[]{:S(2)}, u32[]{:S(2)}) collective-permute-start(f32[2,2,128]{2,1,0:T(2,128)S(1)} %get-tuple-element.76), channel_id=1, source_target_pairs={{0,12},{2,14},{4,0},{6,2},{8,4},{10,6},{12,8},{14,10},{1,13},{3,15... | collective-permute-start | bytes 6152 | tf_op jit(solution)/shard_map/ppermute | solution.py:363
  163.5 7.5 %collective-permute-done.29 = bf16[2,128,1024]{2,1,0:T(8,128)(2,1)S(1)} collective-permute-done((bf16[2,128,1024]{2,1,0:T(8,128)(2,1)}, bf16[2,128,1024]{2,1,0:T(8,128)(2,1)S(1)}, u32[]{:S(2)}, u32[]{:S(2)}) %collective-permute-start.29) | collective-permute-done | bytes 524320 | tf_op jit(solution)/shard_map/ppermute | solution.py:360
  171.0 1.5 collective-permute-start.16
  173.0 4.6 %collective-permute-done.16 = bf16[128,1024]{1,0:T(8,128)(2,1)S(1)} collective-permute-done((bf16[128,1024]{1,0:T(8,128)(2,1)S(1)}, bf16[128,1024]{1,0:T(8,128)(2,1)S(1)}, u32[]{:S(2)}, u32[]{:S(2)}) %collective-permute-start.16) | collective-permute-done | bytes 262176 | tf_op jit(solution)/shard_map/ppermute | solution.py:354
  177.6 1.5 collective-permute-start.30
  181.4 3.5 %collective-permute-start.35 = (f32[2,2,128]{2,1,0:T(2,128)S(1)}, f32[2,2,128]{2,1,0:T(2,128)S(1)}, u32[]{:S(2)}, u32[]{:S(2)}) collective-permute-start(f32[2,2,128]{2,1,0:T(2,128)S(1)} %get-tuple-element.78), channel_id=1, source_target_pairs={{0,8},{2,10},{4,12},{6,14},{8,0},{10,2},{12,4},{14,6},{1,9},{3,11}... | collective-permute-start | bytes 6152 | tf_op jit(solution)/shard_map/ppermute | solution.py:363
  184.9 0.9 collective-permute-start.36
  186.6 3.1 %collective-permute-start.17 = (bf16[128,1024]{1,0:T(8,128)(2,1)}, bf16[128,1024]{1,0:T(8,128)(2,1)}, u32[]{:S(2)}, u32[]{:S(2)}) collective-permute-start(bf16[128,1024]{1,0:T(8,128)(2,1)} %fusion.5), channel_id=1, source_target_pairs={{0,12},{2,14},{4,0},{6,2},{8,4},{10,6},{12,8},{14,10},{1,13},{3,15... | collective-permute-start | bytes 786440 | tf_op jit(solution)/shard_map/ppermute | solution.py:363
  190.3 6.1 %collective-permute-start.24 = (bf16[128,1024]{1,0:T(8,128)(2,1)}, bf16[128,1024]{1,0:T(8,128)(2,1)}, u32[]{:S(2)}, u32[]{:S(2)}) collective-permute-start(bf16[128,1024]{1,0:T(8,128)(2,1)} %fusion.4), channel_id=1, source_target_pairs={{0,8},{2,10},{4,12},{6,14},{8,0},{10,2},{12,4},{14,6},{1,9},{3,11}... | collective-permute-start | bytes 786440 | tf_op jit(solution)/shard_map/ppermute | solution.py:363
  197.3 12.9 %collective-permute-done.24 = bf16[128,1024]{1,0:T(8,128)(2,1)} collective-permute-done((bf16[128,1024]{1,0:T(8,128)(2,1)}, bf16[128,1024]{1,0:T(8,128)(2,1)}, u32[]{:S(2)}, u32[]{:S(2)}) %collective-permute-start.24) | collective-permute-done | bytes 262176 | tf_op jit(solution)/shard_map/ppermute | solution.py:363
  210.2 2.1 fusion.9
  212.3 2.3 %copy-done.1 = bf16[2,576,2048]{2,1,0:T(8,128)(2,1)S(1)} copy-done((bf16[2,576,2048]{2,1,0:T(8,128)(2,1)S(1)}, bf16[2,576,2048]{2,1,0:T(8,128)(2,1)}, u32[]{:S(2)}) %copy-start.1) | copy-done | bytes 4718616
  214.7 9.4 %grads.3 = (bf16[1,2048,384]{2,1,0:T(8,128)(2,1)}, bf16[1,2048,384]{2,1,0:T(8,128)(2,1)}, bf16[1,384,2048]{2,1,0:T(8,128)(2,1)}) custom-call(s32[1]{0:T(128)} %bitcast.16.tp_ref, bf16[2,576,2048]{2,1,0:T(8,128)(2,1)S(1)} %copy-done.1, bf16[2,576,2048]{2,1,0:T(8,128)(2,1)} %get-tuple-element.67.g_ref, bf16[2,576,768]{2,1,0:T(8,128)(2,1)S(1)} %copy-done.3, ...), custom_call_target="tpu_custom_call" | custom-call | flops 2717908992 | bytes 7077888 | tf_op jit(solution)/shard_map/grads/pallas_call | solution.py:321
  (156 shorter events, 15.3 us)
Async XLA Ops:
  6.4 73.2 %copy-start.4 = (bf16[2048,768]{1,0:T(8,128)(2,1)}, bf16[2048,768]{1,0:T(8,128)(2,1)S(1)}, u32[]{:S(2)}) copy-start(bf16[2048,768]{1,0:T(8,128)(2,1)S(1)} %get-tuple-element.40.refs_0_) | copy-start | bytes 9437188
  6.4 73.2 %collective-permute-start.4 = (bf16[2048,768]{1,0:T(8,128)(2,1)S(1)}, bf16[2048,768]{1,0:T(8,128)(2,1)}, u32[]{:S(2)}, u32[]{:S(2)}) collective-permute-start(bf16[2048,768]{1,0:T(8,128)(2,1)S(1)} %get-tuple-element.40.refs_0_), channel_id=1, source_target_pairs={{0,16},{16,0},{1,17},{17,1},{2,18},{18,2},{3,19},{19,3},{4,20},{20... | collective-permute-start | bytes 9437192 | tf_op jit(solution)/shard_map/ppermute | solution.py:357
  8.7 30.8 %collective-permute-start.7 = (bf16[256,1024]{1,0:T(8,128)(2,1)}, bf16[256,1024]{1,0:T(8,128)(2,1)}, u32[]{:S(2)}, u32[]{:S(2)}) collective-permute-start(bf16[256,1024]{1,0:T(8,128)(2,1)} %constant_dynamic-update-slice_fusion.refs_4_), channel_id=1, source_target_pairs={{0,2},{2,0},{4,6},{6,4},{8,10},{10,8},{12,14},{14,12},{1,3},{3,1},... | collective-permute-start | bytes 1572872 | tf_op jit(solution)/shard_map/ppermute | solution.py:360
  11.2 28.3 %collective-permute-start.11 = (bf16[256,1024]{1,0:T(8,128)(2,1)}, bf16[256,1024]{1,0:T(8,128)(2,1)}, u32[]{:S(2)}, u32[]{:S(2)}) collective-permute-start(bf16[256,1024]{1,0:T(8,128)(2,1)} %constant_dynamic-update-slice_fusion.refs_4_), channel_id=1, source_target_pairs={{0,4},{2,6},{4,8},{6,10},{8,12},{10,14},{12,0},{14,2},{1,5},{3,7},... | collective-permute-start | bytes 1572872 | tf_op jit(solution)/shard_map/ppermute | solution.py:363
  12.8 11.3 %collective-permute-start = (bf16[16,128]{1,0:T(8,128)(2,1)S(1)}, bf16[16,128]{1,0:T(8,128)(2,1)S(1)}, u32[]{:S(2)}, u32[]{:S(2)}) collective-permute-start(bf16[16,128]{1,0:T(8,128)(2,1)S(1)} %get-tuple-element.93), channel_id=1, source_target_pairs={{0,2},{2,0},{4,6},{6,4},{8,10},{10,8},{12,14},{14,12},{1,3},{3,1},... | collective-permute-start | bytes 12296 | tf_op jit(solution)/shard_map/ppermute | solution.py:360
  13.4 64.1 %collective-permute-start.5 = (bf16[384,2048]{1,0:T(8,128)(2,1)}, bf16[384,2048]{1,0:T(8,128)(2,1)}, u32[]{:S(2)}, u32[]{:S(2)}) collective-permute-start(bf16[384,2048]{1,0:T(8,128)(2,1)} %get-tuple-element.41.refs_2_), channel_id=1, source_target_pairs={{0,16},{16,0},{1,17},{17,1},{2,18},{18,2},{3,19},{19,3},{4,20},{20... | collective-permute-start | bytes 4718600 | tf_op jit(solution)/shard_map/ppermute | solution.py:357
  24.1 5.5 %collective-permute-start.1 = (bf16[2,16,128]{2,1,0:T(8,128)(2,1)S(1)}, bf16[2,16,128]{2,1,0:T(8,128)(2,1)S(1)}, u32[]{:S(2)}, u32[]{:S(2)}) collective-permute-start(bf16[2,16,128]{2,1,0:T(8,128)(2,1)S(1)} %pad_maximum_fusion), channel_id=1, source_target_pairs={{0,4},{2,6},{4,8},{6,10},{8,12},{10,14},{12,0},{14,2},{1,5},{3,7},... | collective-permute-start | bytes 24584 | tf_op jit(solution)/shard_map/ppermute | solution.py:363
  29.5 4.5 %collective-permute-start.2 = (bf16[2,16,128]{2,1,0:T(8,128)(2,1)S(1)}, bf16[2,16,128]{2,1,0:T(8,128)(2,1)S(1)}, u32[]{:S(2)}, u32[]{:S(2)}) collective-permute-start(bf16[2,16,128]{2,1,0:T(8,128)(2,1)S(1)} %pad_maximum_fusion), channel_id=1, source_target_pairs={{0,8},{2,10},{4,12},{6,14},{8,0},{10,2},{12,4},{14,6},{1,9},{3,11}... | collective-permute-start | bytes 24584 | tf_op jit(solution)/shard_map/ppermute | solution.py:363
  34.1 3.7 %collective-permute-start.3 = (bf16[2,16,128]{2,1,0:T(8,128)(2,1)S(1)}, bf16[2,16,128]{2,1,0:T(8,128)(2,1)S(1)}, u32[]{:S(2)}, u32[]{:S(2)}) collective-permute-start(bf16[2,16,128]{2,1,0:T(8,128)(2,1)S(1)} %pad_maximum_fusion), channel_id=1, source_target_pairs={{0,12},{2,14},{4,0},{6,2},{8,4},{10,6},{12,8},{14,10},{1,13},{3,15... | collective-permute-start | bytes 24584 | tf_op jit(solution)/shard_map/ppermute | solution.py:363
  37.7 15.2 %collective-permute-start.6 = (bf16[256,1024]{1,0:T(8,128)(2,1)}, bf16[256,1024]{1,0:T(8,128)(2,1)}, u32[]{:S(2)}, u32[]{:S(2)}) collective-permute-start(bf16[256,1024]{1,0:T(8,128)(2,1)} %constant_dynamic-update-slice_fusion.refs_4_), channel_id=1, source_target_pairs={{0,1},{1,0},{2,3},{3,2},{4,5},{5,4},{6,7},{7,6},{8,9},{9,8},{10,11... | collective-permute-start | bytes 1572872 | tf_op jit(solution)/shard_map/ppermute | solution.py:354
  39.5 15.2 %collective-permute-start.18 = (bf16[256,1024]{1,0:T(8,128)(2,1)}, bf16[256,1024]{1,0:T(8,128)(2,1)}, u32[]{:S(2)}, u32[]{:S(2)}) collective-permute-start(bf16[256,1024]{1,0:T(8,128)(2,1)} %collective-permute-done.11.refs_4_), channel_id=1, source_target_pairs={{0,4},{2,6},{4,8},{6,10},{8,12},{10,14},{12,0},{14,2},{1,5},{3,7},... | collective-permute-start | bytes 1572872 | tf_op jit(solution)/shard_map/ppermute | solution.py:363
  39.5 24.5 %collective-permute-start.8 = (bf16[256,1024]{1,0:T(8,128)(2,1)}, bf16[256,1024]{1,0:T(8,128)(2,1)S(1)}, u32[]{:S(2)}, u32[]{:S(2)}) collective-permute-start(bf16[256,1024]{1,0:T(8,128)(2,1)} %collective-permute-done.7.refs_6_), channel_id=1, source_target_pairs={{0,1},{1,0},{2,3},{3,2},{4,5},{5,4},{6,7},{7,6},{8,9},{9,8},{10,11... | collective-permute-start | bytes 1572872 | tf_op jit(solution)/shard_map/ppermute | solution.py:354
  52.9 18.3 %collective-permute-start.12 = (bf16[256,1024]{1,0:T(8,128)(2,1)}, bf16[256,1024]{1,0:T(8,128)(2,1)S(1)}, u32[]{:S(2)}, u32[]{:S(2)}) collective-permute-start(bf16[256,1024]{1,0:T(8,128)(2,1)} %collective-permute-done.11.refs_4_), channel_id=1, source_target_pairs={{0,1},{1,0},{2,3},{3,2},{4,5},{5,4},{6,7},{7,6},{8,9},{9,8},{10,11... | collective-permute-start | bytes 1572872 | tf_op jit(solution)/shard_map/ppermute | solution.py:354
  54.6 19.4 %collective-permute-start.25 = (bf16[256,1024]{1,0:T(8,128)(2,1)}, bf16[256,1024]{1,0:T(8,128)(2,1)S(1)}, u32[]{:S(2)}, u32[]{:S(2)}) collective-permute-start(bf16[256,1024]{1,0:T(8,128)(2,1)} %collective-permute-done.18.refs_4_), channel_id=1, source_target_pairs={{0,4},{2,6},{4,8},{6,10},{8,12},{10,14},{12,0},{14,2},{1,5},{3,7},... | collective-permute-start | bytes 1572872 | tf_op jit(solution)/shard_map/ppermute | solution.py:363
  64.1 12.7 %collective-permute-start.14 = (bf16[256,1024]{1,0:T(8,128)(2,1)S(1)}, bf16[256,1024]{1,0:T(8,128)(2,1)S(1)}, u32[]{:S(2)}, u32[]{:S(2)}) collective-permute-start(bf16[256,1024]{1,0:T(8,128)(2,1)S(1)} %collective-permute-done.8.refs_7_), channel_id=1, source_target_pairs={{0,4},{2,6},{4,8},{6,10},{8,12},{10,14},{12,0},{14,2},{1,5},{3,7},... | collective-permute-start | bytes 1572872 | tf_op jit(solution)/shard_map/ppermute | solution.py:363
  71.2 19.4 %collective-permute-start.13 = (bf16[256,1024]{1,0:T(8,128)(2,1)}, bf16[256,1024]{1,0:T(8,128)(2,1)S(1)}, u32[]{:S(2)}, u32[]{:S(2)}) collective-permute-start(bf16[256,1024]{1,0:T(8,128)(2,1)} %collective-permute-done.11.refs_4_), channel_id=1, source_target_pairs={{0,2},{2,0},{4,6},{6,4},{8,10},{10,8},{12,14},{14,12},{1,3},{3,1},... | collective-permute-start | bytes 1572872 | tf_op jit(solution)/shard_map/ppermute | solution.py:360
  74.0 16.9 %collective-permute-start.26 = (bf16[256,1024]{1,0:T(8,128)(2,1)S(1)}, bf16[256,1024]{1,0:T(8,128)(2,1)S(1)}, u32[]{:S(2)}, u32[]{:S(2)}) collective-permute-start(bf16[256,1024]{1,0:T(8,128)(2,1)S(1)} %collective-permute-done.25.refs_4_), channel_id=1, source_target_pairs={{0,1},{1,0},{2,3},{3,2},{4,5},{5,4},{6,7},{7,6},{8,9},{9,8},{10,11... | collective-permute-start | bytes 1572872 | tf_op jit(solution)/shard_map/ppermute | solution.py:354
  76.7 27.1 %collective-permute-start.19 = (bf16[256,1024]{1,0:T(8,128)(2,1)}, bf16[256,1024]{1,0:T(8,128)(2,1)S(1)}, u32[]{:S(2)}, u32[]{:S(2)}) collective-permute-start(bf16[256,1024]{1,0:T(8,128)(2,1)} %collective-permute-done.18.refs_4_), channel_id=1, source_target_pairs={{0,1},{1,0},{2,3},{3,2},{4,5},{5,4},{6,7},{7,6},{8,9},{9,8},{10,11... | collective-permute-start | bytes 1572872 | tf_op jit(solution)/shard_map/ppermute | solution.py:354
  77.5 26.4 %collective-permute-start.20 = (bf16[256,1024]{1,0:T(8,128)(2,1)}, bf16[256,1024]{1,0:T(8,128)(2,1)S(1)}, u32[]{:S(2)}, u32[]{:S(2)}) collective-permute-start(bf16[256,1024]{1,0:T(8,128)(2,1)} %collective-permute-done.18.refs_4_), channel_id=1, source_target_pairs={{0,2},{2,0},{4,6},{6,4},{8,10},{10,8},{12,14},{14,12},{1,3},{3,1},... | collective-permute-start | bytes 1572872 | tf_op jit(solution)/shard_map/ppermute | solution.py:360
  79.5 24.3 %collective-permute-start.21 = (bf16[256,1024]{1,0:T(8,128)(2,1)S(1)}, bf16[256,1024]{1,0:T(8,128)(2,1)S(1)}, u32[]{:S(2)}, u32[]{:S(2)}) collective-permute-start(bf16[256,1024]{1,0:T(8,128)(2,1)S(1)} %collective-permute-done.14.refs_7_), channel_id=1, source_target_pairs={{0,4},{2,6},{4,8},{6,10},{8,12},{10,14},{12,0},{14,2},{1,5},{3,7},... | collective-permute-start | bytes 1572872 | tf_op jit(solution)/shard_map/ppermute | solution.py:363
  90.6 25.8 %collective-permute-start.27 = (bf16[256,1024]{1,0:T(8,128)(2,1)S(1)}, bf16[256,1024]{1,0:T(8,128)(2,1)S(1)}, u32[]{:S(2)}, u32[]{:S(2)}) collective-permute-start(bf16[256,1024]{1,0:T(8,128)(2,1)S(1)} %collective-permute-done.25.refs_4_), channel_id=1, source_target_pairs={{0,2},{2,0},{4,6},{6,4},{8,10},{10,8},{12,14},{14,12},{1,3},{3,1},... | collective-permute-start | bytes 1572872 | tf_op jit(solution)/shard_map/ppermute | solution.py:360
  91.0 25.5 %collective-permute-start.28 = (bf16[256,1024]{1,0:T(8,128)(2,1)S(1)}, bf16[256,1024]{1,0:T(8,128)(2,1)S(1)}, u32[]{:S(2)}, u32[]{:S(2)}) collective-permute-start(bf16[256,1024]{1,0:T(8,128)(2,1)S(1)} %collective-permute-done.26.refs_5_), channel_id=1, source_target_pairs={{0,2},{2,0},{4,6},{6,4},{8,10},{10,8},{12,14},{14,12},{1,3},{3,1},... | collective-permute-start | bytes 1572872 | tf_op jit(solution)/shard_map/ppermute | solution.py:360
  133.6 24.7 %copy-start.35 = (bf16[2,128,1024]{2,1,0:T(8,128)(2,1)S(1)}, bf16[2,128,1024]{2,1,0:T(8,128)(2,1)}, u32[]{:S(2)}) copy-start(bf16[2,128,1024]{2,1,0:T(8,128)(2,1)} %get-tuple-element.43) | copy-start | bytes 1572868
  133.6 25.8 %copy-start.22 = (bf16[2,128,1024]{2,1,0:T(8,128)(2,1)S(1)}, bf16[2,128,1024]{2,1,0:T(8,128)(2,1)}, u32[]{:S(2)}) copy-start(bf16[2,128,1024]{2,1,0:T(8,128)(2,1)} %get-tuple-element.48) | copy-start | bytes 1572868
  133.6 29.8 %copy-start.23 = (bf16[2,128,1024]{2,1,0:T(8,128)(2,1)S(1)}, bf16[2,128,1024]{2,1,0:T(8,128)(2,1)}, u32[]{:S(2)}) copy-start(bf16[2,128,1024]{2,1,0:T(8,128)(2,1)} %get-tuple-element.54) | copy-start | bytes 1572868
  142.6 29.9 %copy-start.25 = (bf16[2,128,1024]{2,1,0:T(8,128)(2,1)S(1)}, bf16[2,128,1024]{2,1,0:T(8,128)(2,1)}, u32[]{:S(2)}) copy-start(bf16[2,128,1024]{2,1,0:T(8,128)(2,1)} %get-tuple-element.60) | copy-start | bytes 1572868
  142.6 30.4 %copy-start.10 = (bf16[2,128,1024]{2,1,0:T(8,128)(2,1)S(1)}, bf16[2,128,1024]{2,1,0:T(8,128)(2,1)}, u32[]{:S(2)}) copy-start(bf16[2,128,1024]{2,1,0:T(8,128)(2,1)} %get-tuple-element.42) | copy-start | bytes 1572868
  142.6 69.7 %collective-permute-start.37 = (bf16[2048,768]{1,0:T(8,128)(2,1)}, bf16[2048,768]{1,0:T(8,128)(2,1)}, u32[]{:S(2)}, u32[]{:S(2)}) collective-permute-start(bf16[2048,768]{1,0:T(8,128)(2,1)} %get-tuple-element.70), channel_id=1, source_target_pairs={{0,16},{16,0},{1,17},{17,1},{2,18},{18,2},{3,19},{19,3},{4,20},{20... | collective-permute-start | bytes 9437192 | tf_op jit(solution)/shard_map/ppermute | solution.py:357
  142.8 3.7 %collective-permute-start.32 = (f32[4,2,2,128]{3,2,1,0:T(2,128)S(1)}, f32[4,2,2,128]{3,2,1,0:T(2,128)S(1)}, u32[]{:S(2)}, u32[]{:S(2)}) collective-permute-start(f32[4,2,2,128]{3,2,1,0:T(2,128)S(1)} %constant_dynamic-update-slice_fusion.2), channel_id=1, source_target_pairs={{0,1},{1,0},{2,3},{3,2},{4,5},{5,4},{6,7},{7,6},{8,9},{9,8},{10,11... | collective-permute-start | bytes 24584 | tf_op jit(solution)/shard_map/ppermute | solution.py:354
  143.4 15.0 %collective-permute-start.15 = (bf16[2,128,1024]{2,1,0:T(8,128)(2,1)S(1)}, bf16[2,128,1024]{2,1,0:T(8,128)(2,1)S(1)}, u32[]{:S(2)}, u32[]{:S(2)}) collective-permute-start(bf16[2,128,1024]{2,1,0:T(8,128)(2,1)S(1)} %copy-done.36), channel_id=1, source_target_pairs={{0,2},{2,0},{4,6},{6,4},{8,10},{10,8},{12,14},{14,12},{1,3},{3,1},... | collective-permute-start | bytes 1572872 | tf_op jit(solution)/shard_map/ppermute | solution.py:360
  144.2 15.3 %collective-permute-start.22 = (bf16[2,128,1024]{2,1,0:T(8,128)(2,1)}, bf16[2,128,1024]{2,1,0:T(8,128)(2,1)S(1)}, u32[]{:S(2)}, u32[]{:S(2)}) collective-permute-start(bf16[2,128,1024]{2,1,0:T(8,128)(2,1)} %get-tuple-element.55), channel_id=1, source_target_pairs={{0,1},{1,0},{2,3},{3,2},{4,5},{5,4},{6,7},{7,6},{8,9},{9,8},{10,11... | collective-permute-start | bytes 1572872 | tf_op jit(solution)/shard_map/ppermute | solution.py:354
  146.5 11.0 %collective-permute-start.33 = (f32[4,2,128]{2,1,0:T(2,128)S(1)}, f32[4,2,128]{2,1,0:T(2,128)S(1)}, u32[]{:S(2)}, u32[]{:S(2)}) collective-permute-start(f32[4,2,128]{2,1,0:T(2,128)S(1)} %bitcast.103), channel_id=1, source_target_pairs={{0,2},{2,0},{4,6},{6,4},{8,10},{10,8},{12,14},{14,12},{1,3},{3,1},... | collective-permute-start | bytes 12296 | tf_op jit(solution)/shard_map/ppermute | solution.py:360
  147.1 65.2 %collective-permute-start.38 = (bf16[384,2048]{1,0:T(8,128)(2,1)}, bf16[384,2048]{1,0:T(8,128)(2,1)}, u32[]{:S(2)}, u32[]{:S(2)}) collective-permute-start(bf16[384,2048]{1,0:T(8,128)(2,1)} %get-tuple-element.71), channel_id=1, source_target_pairs={{0,16},{16,0},{1,17},{17,1},{2,18},{18,2},{3,19},{19,3},{4,20},{20... | collective-permute-start | bytes 4718600 | tf_op jit(solution)/shard_map/ppermute | solution.py:357
  157.5 13.4 %collective-permute-start.29 = (bf16[2,128,1024]{2,1,0:T(8,128)(2,1)}, bf16[2,128,1024]{2,1,0:T(8,128)(2,1)S(1)}, u32[]{:S(2)}, u32[]{:S(2)}) collective-permute-start(bf16[2,128,1024]{2,1,0:T(8,128)(2,1)} %get-tuple-element.61), channel_id=1, source_target_pairs={{0,2},{2,0},{4,6},{6,4},{8,10},{10,8},{12,14},{14,12},{1,3},{3,1},... | collective-permute-start | bytes 1572872 | tf_op jit(solution)/shard_map/ppermute | solution.py:360
  158.4 14.2 %collective-permute-start.9 = (bf16[2,128,1024]{2,1,0:T(8,128)(2,1)S(1)}, bf16[2,128,1024]{2,1,0:T(8,128)(2,1)S(1)}, u32[]{:S(2)}, u32[]{:S(2)}) collective-permute-start(bf16[2,128,1024]{2,1,0:T(8,128)(2,1)S(1)} %copy-done.35), channel_id=1, source_target_pairs={{0,1},{1,0},{2,3},{3,2},{4,5},{5,4},{6,7},{7,6},{8,9},{9,8},{10,11... | collective-permute-start | bytes 1572872 | tf_op jit(solution)/shard_map/ppermute | solution.py:354
  159.5 21.0 %copy-start.24 = (bf16[2,128,1024]{2,1,0:T(8,128)(2,1)S(1)}, bf16[2,128,1024]{2,1,0:T(8,128)(2,1)}, u32[]{:S(2)}) copy-start(bf16[2,128,1024]{2,1,0:T(8,128)(2,1)} %get-tuple-element.54) | copy-start | bytes 1572868
  159.5 21.8 %collective-permute-start.34 = (f32[2,2,128]{2,1,0:T(2,128)S(1)}, f32[2,2,128]{2,1,0:T(2,128)S(1)}, u32[]{:S(2)}, u32[]{:S(2)}) collective-permute-start(f32[2,2,128]{2,1,0:T(2,128)S(1)} %get-tuple-element.76), channel_id=1, source_target_pairs={{0,12},{2,14},{4,0},{6,2},{8,4},{10,6},{12,8},{14,10},{1,13},{3,15... | collective-permute-start | bytes 6152 | tf_op jit(solution)/shard_map/ppermute | solution.py:363
  171.0 6.7 %collective-permute-start.16 = (bf16[128,1024]{1,0:T(8,128)(2,1)S(1)}, bf16[128,1024]{1,0:T(8,128)(2,1)S(1)}, u32[]{:S(2)}, u32[]{:S(2)}) collective-permute-start(bf16[128,1024]{1,0:T(8,128)(2,1)S(1)} %fusion.11), channel_id=1, source_target_pairs={{0,1},{1,0},{2,3},{3,2},{4,5},{5,4},{6,7},{7,6},{8,9},{9,8},{10,11... | collective-permute-start | bytes 786440 | tf_op jit(solution)/shard_map/ppermute | solution.py:354
  172.6 7.4 %collective-permute-start.23 = (bf16[128,1024]{1,0:T(8,128)(2,1)S(1)}, bf16[128,1024]{1,0:T(8,128)(2,1)S(1)}, u32[]{:S(2)}, u32[]{:S(2)}) collective-permute-start(bf16[128,1024]{1,0:T(8,128)(2,1)S(1)} %fusion.12), channel_id=1, source_target_pairs={{0,2},{2,0},{4,6},{6,4},{8,10},{10,8},{12,14},{14,12},{1,3},{3,1},... | collective-permute-start | bytes 786440 | tf_op jit(solution)/shard_map/ppermute | solution.py:360
  177.6 7.3 %collective-permute-start.30 = (bf16[128,1024]{1,0:T(8,128)(2,1)S(1)}, bf16[128,1024]{1,0:T(8,128)(2,1)S(1)}, u32[]{:S(2)}, u32[]{:S(2)}) collective-permute-start(bf16[128,1024]{1,0:T(8,128)(2,1)S(1)} %fusion.13), channel_id=1, source_target_pairs={{0,1},{1,0},{2,3},{3,2},{4,5},{5,4},{6,7},{7,6},{8,9},{9,8},{10,11... | collective-permute-start | bytes 786440 | tf_op jit(solution)/shard_map/ppermute | solution.py:354
  180.0 32.4 %copy-start.3 = (bf16[2,576,768]{2,1,0:T(8,128)(2,1)S(1)}, bf16[2,576,768]{2,1,0:T(8,128)(2,1)}, u32[]{:S(2)}) copy-start(bf16[2,576,768]{2,1,0:T(8,128)(2,1)} %get-tuple-element.68.both_ref) | copy-start | bytes 5308420
  180.0 32.4 %copy-start.6 = (bf16[2,576,384]{2,1,0:T(8,128)(2,1)S(1)}, bf16[2,576,384]{2,1,0:T(8,128)(2,1)}, u32[]{:S(2)}) copy-start(bf16[2,576,384]{2,1,0:T(8,128)(2,1)} %get-tuple-element.69.scaled_ref) | copy-start | bytes 2654212
  180.0 16.5 %collective-permute-start.10 = (bf16[128,1024]{1,0:T(8,128)(2,1)S(1)}, bf16[128,1024]{1,0:T(8,128)(2,1)S(1)}, u32[]{:S(2)}, u32[]{:S(2)}) collective-permute-start(bf16[128,1024]{1,0:T(8,128)(2,1)S(1)} %fusion.10), channel_id=1, source_target_pairs={{0,2},{2,0},{4,6},{6,4},{8,10},{10,8},{12,14},{14,12},{1,3},{3,1},... | collective-permute-start | bytes 786440 | tf_op jit(solution)/shard_map/ppermute | solution.py:360
  181.4 5.2 %collective-permute-start.35 = (f32[2,2,128]{2,1,0:T(2,128)S(1)}, f32[2,2,128]{2,1,0:T(2,128)S(1)}, u32[]{:S(2)}, u32[]{:S(2)}) collective-permute-start(f32[2,2,128]{2,1,0:T(2,128)S(1)} %get-tuple-element.78), channel_id=1, source_target_pairs={{0,8},{2,10},{4,12},{6,14},{8,0},{10,2},{12,4},{14,6},{1,9},{3,11}... | collective-permute-start | bytes 6152 | tf_op jit(solution)/shard_map/ppermute | solution.py:363
  184.9 5.5 %collective-permute-start.36 = (f32[2,2,128]{2,1,0:T(2,128)S(1)}, f32[2,2,128]{2,1,0:T(2,128)S(1)}, u32[]{:S(2)}, u32[]{:S(2)}) collective-permute-start(f32[2,2,128]{2,1,0:T(2,128)S(1)} %get-tuple-element.77), channel_id=1, source_target_pairs={{0,4},{2,6},{4,8},{6,10},{8,12},{10,14},{12,0},{14,2},{1,5},{3,7},... | collective-permute-start | bytes 6152 | tf_op jit(solution)/shard_map/ppermute | solution.py:363
  186.6 10.7 %collective-permute-start.17 = (bf16[128,1024]{1,0:T(8,128)(2,1)}, bf16[128,1024]{1,0:T(8,128)(2,1)}, u32[]{:S(2)}, u32[]{:S(2)}) collective-permute-start(bf16[128,1024]{1,0:T(8,128)(2,1)} %fusion.5), channel_id=1, source_target_pairs={{0,12},{2,14},{4,0},{6,2},{8,4},{10,6},{12,8},{14,10},{1,13},{3,15... | collective-permute-start | bytes 786440 | tf_op jit(solution)/shard_map/ppermute | solution.py:363
  190.3 19.9 %collective-permute-start.24 = (bf16[128,1024]{1,0:T(8,128)(2,1)}, bf16[128,1024]{1,0:T(8,128)(2,1)}, u32[]{:S(2)}, u32[]{:S(2)}) collective-permute-start(bf16[128,1024]{1,0:T(8,128)(2,1)} %fusion.4), channel_id=1, source_target_pairs={{0,8},{2,10},{4,12},{6,14},{8,0},{10,2},{12,4},{14,6},{1,9},{3,11}... | collective-permute-start | bytes 786440 | tf_op jit(solution)/shard_map/ppermute | solution.py:363
  196.5 13.8 %collective-permute-start.31 = (bf16[128,1024]{1,0:T(8,128)(2,1)}, bf16[128,1024]{1,0:T(8,128)(2,1)}, u32[]{:S(2)}, u32[]{:S(2)}) collective-permute-start(bf16[128,1024]{1,0:T(8,128)(2,1)} %fusion.3), channel_id=1, source_target_pairs={{0,4},{2,6},{4,8},{6,10},{8,12},{10,14},{12,0},{14,2},{1,5},{3,7},... | collective-permute-start | bytes 786440 | tf_op jit(solution)/shard_map/ppermute | solution.py:363
  (29 other events, 191.0 us)

commit v5 on v4

v5 whole, which is shorter than its diff:
```python
import functools
import math

import jax
import jax.numpy as jnp
from jax import lax
from jax.experimental import pallas as pl
from jax.experimental.pallas import tpu as pltpu
from jax.sharding import PartitionSpec as P


def pad_rows(array):
    return jnp.concatenate([array, jnp.zeros((1, array.shape[1]), array.dtype)], 0)


def routed_device(tokens, out_grad, routes, probs, w_gate, w_up, w_down):
    owners = lax.axis_size(("role", "ep"))
    tok_rows, top_count = routes.shape
    width_full = w_gate.shape[1]
    part_width = w_gate.shape[2]
    capacity = min(tok_rows, tok_rows * top_count * 9 // (8 * owners))
    entry_total = tok_rows * top_count
    routes_flat = routes.reshape(-1)
    onehot = (routes_flat[:, None] == jnp.arange(owners, dtype=jnp.int32)[None, :]).astype(
        jnp.int32
    )
    before = jnp.cumsum(onehot, axis=0) - onehot
    slot_index = jnp.sum(before * onehot, axis=1)
    target = routes_flat * capacity + slot_index
    row_count = owners * capacity
    entry_of_slot = (
        jnp.full((row_count,), entry_total, jnp.int32)
        .at[target]
        .set(jnp.arange(entry_total, dtype=jnp.int32))
    )
    token_of_slot = entry_of_slot // top_count
    padded_prob = jnp.concatenate([probs.reshape(-1), jnp.zeros((1,), probs.dtype)], 0)
    send_prob = padded_prob[entry_of_slot].reshape(owners, capacity)
    send_x = pad_rows(tokens)[token_of_slot]
    send_g = pad_rows(out_grad)[token_of_slot]
    slice_x, slice_g, recv_p = (
        lax.all_to_all(
            send_x.reshape(owners, capacity, tokens.shape[1]),
            ("role", "ep"),
            split_axis=0,
            concat_axis=0,
            tiled=True,
        ),
        lax.all_to_all(
            send_g.reshape(owners, capacity, tokens.shape[1]),
            ("role", "ep"),
            split_axis=0,
            concat_axis=0,
            tiled=True,
        ),
        lax.all_to_all(send_prob, ("role", "ep"), split_axis=0, concat_axis=0, tiled=True),
    )
    recv_x, recv_g = (
        lax.all_gather(slice_x, "tp", axis=2, tiled=True),
        lax.all_gather(slice_g, "tp", axis=2, tiled=True),
    )
    rows_x = recv_x.reshape(row_count, width_full)
    rows_g = recv_g.reshape(row_count, width_full)
    weight_p = recv_p.reshape(row_count, 1).astype(jnp.float32)
    gate_up = jnp.concatenate([w_gate[0], w_up[0]], 1)
    down_shard = w_down[0]
    both_rows = jnp.dot(rows_x, gate_up, preferred_element_type=jnp.float32)
    gate_rows = both_rows[:, :part_width]
    up_rows = both_rows[:, part_width:]
    sigmoid_gate = jax.nn.sigmoid(gate_rows)
    activated = gate_rows * sigmoid_gate
    hidden = activated * up_rows
    back_rows = lax.dot_general(
        rows_g, down_shard, (((1,), (1,)), ((), ())), preferred_element_type=jnp.float32
    )
    scores = lax.psum(jnp.sum(hidden * back_rows, axis=1), "tp")
    hidden_grad = weight_p * back_rows
    d_gate_rows = (
        hidden_grad * up_rows * sigmoid_gate * (1.0 + gate_rows * (1.0 - sigmoid_gate))
    ).astype(jnp.bfloat16)
    d_up_rows = (hidden_grad * activated).astype(jnp.bfloat16)
    d_both = jnp.concatenate([d_gate_rows, d_up_rows], 1)
    scaled = (weight_p * hidden).astype(jnp.bfloat16)
    grad_down = lax.dot_general(
        scaled, rows_g, (((0,), (0,)), ((), ())), preferred_element_type=jnp.float32
    )
    grad_both = lax.dot_general(
        rows_x, d_both, (((0,), (0,)), ((), ())), preferred_element_type=jnp.float32
    )
    grad_gate = grad_both[:, :part_width]
    grad_up = grad_both[:, part_width:]
    partial_low = lax.dot_general(
        d_both, gate_up, (((1,), (1,)), ((), ())), preferred_element_type=jnp.float32
    ).astype(jnp.bfloat16)
    home_s = lax.all_to_all(
        scores.reshape(owners, capacity), ("role", "ep"), split_axis=0, concat_axis=0, tiled=True
    )
    summed = lax.psum_scatter(
        partial_low.reshape(owners, capacity, width_full), "tp", scatter_dimension=2, tiled=True
    ).astype(jnp.float32)
    summed_low = summed.astype(jnp.bfloat16)
    home_x = lax.all_to_all(summed_low, ("role", "ep"), split_axis=0, concat_axis=0, tiled=True)
    slice_width = summed.shape[2]
    route_rows = home_x.reshape(row_count, slice_width).astype(jnp.float32)
    d_tok = (
        jnp.zeros((tok_rows + 1, slice_width), jnp.float32)
        .at[token_of_slot]
        .add(route_rows)[:tok_rows]
    )
    d_probs = home_s.reshape(-1)[target].reshape(tok_rows, top_count)
    return (
        d_tok.astype(jnp.bfloat16),
        d_probs,
        grad_gate.astype(jnp.bfloat16)[None],
        grad_up.astype(jnp.bfloat16)[None],
        grad_down.astype(jnp.bfloat16)[None],
    )


def slot_capacity(tok_rows, top_count, owners):
    return min(tok_rows, tok_rows * top_count * 9 // (8 * owners))


LOOSE = pl.BlockSpec(memory_space=pl.ANY)


def weights_kernel(tp_ref, wg_ref, wu_ref, wd_ref, *refs):
    both_ref, down_ref = refs[-2:]
    part = wg_ref.shape[2]
    both_ref[:, :part] = wg_ref[0]
    both_ref[:, part:] = wu_ref[0]
    down_ref[...] = wd_ref[0]


def weights_call(which, w_gate, w_up, w_down, after):
    _, width, part = w_gate.shape
    half = width // 2

    def place(i, w):
        return (i + w[0]) % 2

    return pl.pallas_call(
        weights_kernel,
        grid_spec=pltpu.PrefetchScalarGridSpec(
            num_scalar_prefetch=1,
            grid=(2,),
            in_specs=[
                pl.BlockSpec((1, half, part), lambda i, w: (0, place(i, w), 0)),
                pl.BlockSpec((1, half, part), lambda i, w: (0, place(i, w), 0)),
                pl.BlockSpec((1, part, half), lambda i, w: (0, 0, place(i, w))),
            ]
            + [LOOSE] * len(after),
            out_specs=[
                pl.BlockSpec((half, 2 * part), lambda i, w: (i, 0)),
                pl.BlockSpec((part, half), lambda i, w: (0, i)),
            ],
        ),
        out_shape=[
            jax.ShapeDtypeStruct((width, 2 * part), jnp.bfloat16),
            jax.ShapeDtypeStruct((part, width), jnp.bfloat16),
        ],
        compiler_params=pltpu.CompilerParams(vmem_limit_bytes=56 << 20),
        cost_estimate=pl.CostEstimate(flops=0, bytes_accessed=12 * width * part, transcendentals=0),
        name="weights",
    )(which, w_gate, w_up, w_down, *after)


def rows_kernel(places, modes, capacity, slots, where_ref, *refs):
    count = len(places)
    weights_in, units_in, refs = refs[:4], refs[4 : 4 + 4 * count], refs[len(refs) - 19 - 2 * count :]
    outs, keeps, sends, refs = refs[:4], refs[4 : 4 + count], refs[4 + count : 4 + 2 * count], refs[4 + 2 * count :]
    x_all, g_all, tables, wgu0, wgu1, wd0, wd1, xc, gc, both, scaled, piece, unit_sems, weight_sems = refs[:14]
    out_sems = refs[14]
    half, tok = x_all.shape[3], x_all.shape[2] // 2
    part = scaled.shape[2]
    owners = tables.shape[2]
    wgu, wd = (wgu0, wgu1), (wd0, wd1)

    x_copies, g_copies, t_copies = [], [], []
    for index, unit in enumerate(units_in):
        chunk, y, x = index // 4, index // 2 % 2, index % 2
        rows = pl.ds(y * tok, tok)
        x_copies.append(pltpu.make_async_copy(unit.at[pl.ds(0, tok)], x_all.at[chunk, x, rows], unit_sems.at[0, index]))
        g_copies.append(pltpu.make_async_copy(unit.at[pl.ds(tok, tok)], g_all.at[chunk, x, rows], unit_sems.at[1, index]))
        if x == 0:
            table = unit.at[pl.ds(2 * tok, owners), pl.ds(0, tok)]
            t_copies.append(pltpu.make_async_copy(table, tables.at[chunk, y], unit_sems.at[2, index]))
    weight_copies = [
        pltpu.make_async_copy(source, target, weight_sems.at[index])
        for index, (source, target) in enumerate(zip(weights_in, (wgu0, wgu1, wd0, wd1)))
    ]
    for copy in t_copies + x_copies + weight_copies[:2] + g_copies + weight_copies[2:]:
        copy.start()
    leaving = []

    def leave(source, target):
        copy = pltpu.make_async_copy(source, target, out_sems.at[len(leaving)])
        copy.start()
        leaving.append(copy)

    def leave_rows(held, target):
        for expert in range(2):
            for chunk, place in enumerate(places):
                source = held.at[expert, pl.ds(chunk * slots, slots)]
                leave(source, target.at[expert, pl.ds(place * slots, slots)])

    def dot(a, b, dims):
        return lax.dot_general(a, b, (dims, ((), ())), preferred_element_type=jnp.float32)

    for copy in t_copies:
        copy.wait()
    earlier = lax.broadcasted_iota(jnp.int32, (tok, tok), 0) < lax.broadcasted_iota(jnp.int32, (tok, tok), 1)
    earlier = earlier.astype(jnp.bfloat16)
    number = lax.broadcasted_iota(jnp.int32, (slots, tok), 0).astype(jnp.float32)
    names = lax.broadcasted_iota(jnp.int32, (owners, tok), 0)
    picks, low_picks, probs = {}, {}, {}
    for chunk in range(count):
        found = []
        for y in range(2):
            table = tables[chunk, y].astype(jnp.float32)
            rank = dot((table >= 0.0).astype(jnp.bfloat16), earlier, ((1,), (0,))) + float(y * capacity)
            found.append((table, jnp.where(table >= 0.0, rank, -1.0)))
        for expert in range(2):
            mine = names == where_ref[expert]
            halves, prob = [], None
            for table, rank in found:
                weight = jnp.sum(jnp.where(mine, table, 0.0), axis=0, keepdims=True)
                slot = jnp.sum(jnp.where(mine, rank, 0.0), axis=0, keepdims=True)
                halves.append((number == slot).astype(jnp.float32))
                term = jnp.sum(halves[-1] * weight, axis=1, keepdims=True)
                prob = term if prob is None else prob + term
            picks[chunk, expert] = halves
            low_picks[chunk, expert] = jnp.concatenate(halves, 1).astype(jnp.bfloat16)
            probs[chunk, expert] = prob
    spans = [pl.ds(chunk * slots, slots) for chunk in range(count)]
    sides = [slice(side * half, (side + 1) * half) for side in range(2)]

    def gather(copies, source, target):
        for chunk in range(count):
            for copy in copies[4 * chunk : 4 * chunk + 4]:
                copy.wait()
            both_picks = jnp.concatenate([low_picks[chunk, expert] for expert in range(2)], 0)
            for side in range(2):
                rows = dot(both_picks, source[chunk, side], ((1,), (0,))).astype(jnp.bfloat16)
                for expert in range(2):
                    target[expert, spans[chunk], sides[side]] = rows[expert * slots : (expert + 1) * slots]

    gather(x_copies, x_all, xc)
    leave_rows(xc, outs[0])
    rows = []
    for expert in range(2):
        weight_copies[expert].wait()
        rows.append(dot(xc[expert], wgu[expert][...], ((1,), (0,))))
    gather(g_copies, g_all, gc)
    leave_rows(gc, outs[1])
    scores = []
    for expert in range(2):
        weight_copies[2 + expert].wait()
        back = dot(gc[expert], wd[expert][...], ((1,), (1,)))
        gate, up = rows[expert][:, :part], rows[expert][:, part:]
        sig = jax.nn.sigmoid(gate)
        act = gate * sig
        hidden = act * up
        scores.append(jnp.sum(hidden * back, axis=1, keepdims=True))
        prob = jnp.concatenate([probs[chunk, expert] for chunk in range(count)], 0)
        hgrad = prob * back
        both[expert, :, :part] = (hgrad * up * sig * (1.0 + gate * (1.0 - sig))).astype(jnp.bfloat16)
        both[expert, :, part:] = (hgrad * act).astype(jnp.bfloat16)
        scaled[expert] = (prob * hidden).astype(jnp.bfloat16)
    leave_rows(both, outs[2])
    leave_rows(scaled, outs[3])

    names = lax.broadcasted_iota(jnp.int32, (owners, half), 0)
    column = lax.broadcasted_iota(jnp.int32, (owners, half), 1) // (2 * tok)
    for chunk in range(count):
        for y in range(2):
            extra = jnp.zeros((owners, half), jnp.float32)
            for expert in range(2):
                part_scores = scores[expert][chunk * slots : (chunk + 1) * slots]
                line = jnp.sum(picks[chunk, expert][y] * part_scores, axis=0, keepdims=True)
                high = line.astype(jnp.bfloat16).astype(jnp.float32)
                line = jnp.concatenate([high, line - high] * (half // (2 * tok)), 1)
                extra = extra + jnp.where((names == where_ref[expert]) & (column == where_ref[2]), line, 0.0)
            for side in range(2):
                piece[chunk, side, y, tok:] = extra.astype(jnp.bfloat16)
    for side in (1, 0):
        low = [
            dot(both[expert], wgu[expert][sides[side], :], ((1,), (1,))).astype(jnp.bfloat16) for expert in range(2)
        ]
        for chunk in range(count):
            total = None
            for expert in range(2):
                term = dot(low_picks[chunk, expert], low[expert][chunk * slots : (chunk + 1) * slots], ((0,), (0,)))
                total = term if total is None else total + term
            for y in range(2):
                piece[chunk, side, y, :tok] = total[y * tok : (y + 1) * tok].astype(jnp.bfloat16)
                first, second = (y, side) if modes[chunk] else (side, y)
                leave(piece.at[chunk, side, y], (sends if first else keeps)[chunk].at[second])
    for copy in leaving:
        copy.wait()


def rows_call(places, modes, steps, owners, capacity, slots, where, weights, units, held):
    count = len(places)
    tok, half = (units[0].shape[0] - owners) // 2, units[0].shape[1]
    part, width = weights[2].shape
    widths = (width, width, 2 * part, part)
    packet = (2, tok + owners, half)
    return pl.pallas_call(
        functools.partial(rows_kernel, places, modes, capacity, slots),
        grid_spec=pltpu.PrefetchScalarGridSpec(
            num_scalar_prefetch=1,
            grid=(1,),
            in_specs=[LOOSE] * (4 + len(units) + len(held)),
            out_specs=[LOOSE] * (4 + 2 * count),
            scratch_shapes=[pltpu.VMEM((count, 2, 2 * tok, half), jnp.bfloat16)] * 2
            + [pltpu.VMEM((count, 2, owners, tok), jnp.bfloat16)]
            + [pltpu.VMEM((width, 2 * part), jnp.bfloat16)] * 2
            + [pltpu.VMEM((part, width), jnp.bfloat16)] * 2
            + [pltpu.VMEM((2, count * slots, size), jnp.bfloat16) for size in widths]
            + [
                pltpu.VMEM((count, 2) + packet, jnp.bfloat16),
                pltpu.SemaphoreType.DMA((3, 4 * count)),
                pltpu.SemaphoreType.DMA((4,)),
                pltpu.SemaphoreType.DMA((12 * count,)),
            ],
        ),
        out_shape=[jax.ShapeDtypeStruct((2, steps * slots, size), jnp.bfloat16) for size in widths]
        + [jax.ShapeDtypeStruct(packet, jnp.bfloat16)] * (2 * count),
        input_output_aliases={5 + len(units) + i: i for i in range(len(held))},
        compiler_params=pltpu.CompilerParams(vmem_limit_bytes=56 << 20),
        cost_estimate=pl.CostEstimate(
            flops=count * (20 * slots * width * part + 24 * slots * tok * width),
            bytes_accessed=count * 16 * tok * width + 12 * width * part,
            transcendentals=2 * count * slots * part,
        ),
        name="rows",
    )(where, *weights, *units, *held)


def grads_kernel(first, tp_ref, x_ref, g_ref, both_ref, scaled_ref, *refs):
    flipped = refs[-1]
    part = scaled_ref.shape[2]

    @pl.when(pl.program_id(0) == 0)
    def _():
        flipped[...] = scaled_ref[0].T

    both = lax.dot_general(x_ref[0], both_ref[0], (((0,), (0,)), ((), ())), preferred_element_type=jnp.float32)
    down = jnp.dot(flipped[...], g_ref[0], preferred_element_type=jnp.float32)
    if first:
        both_out, down_out = refs[-3:-1]
        both_out[...] = both.astype(jnp.bfloat16)
        down_out[...] = down.astype(jnp.bfloat16)
        return
    more_both, more_down = refs[:2]
    dg_ref, du_ref, dd_ref = refs[-4:-1]
    both = both + more_both[...].astype(jnp.float32)
    dg_ref[0] = both[:, :part].astype(jnp.bfloat16)
    du_ref[0] = both[:, part:].astype(jnp.bfloat16)
    dd_ref[0] = (down + more_down[...].astype(jnp.float32)).astype(jnp.bfloat16)


def grads_call(which, expert, x_rows, g_rows, both, scaled, more, after):
    _, total, width = x_rows.shape
    part = scaled.shape[2]
    step = math.gcd(width // 2, 512)
    per = width // 2 // step

    def place(i, w):
        return (i + w[0] * per) % (2 * per)

    moving = pl.BlockSpec((1, total, step), lambda i, w: (expert, 0, i))
    passing = [
        pl.BlockSpec((step, 2 * part), lambda i, w: (i, 0)),
        pl.BlockSpec((part, step), lambda i, w: (0, i)),
    ]
    if more:
        out_specs = [
            pl.BlockSpec((1, step, part), lambda i, w: (0, place(i, w), 0)),
            pl.BlockSpec((1, step, part), lambda i, w: (0, place(i, w), 0)),
            pl.BlockSpec((1, part, step), lambda i, w: (0, 0, place(i, w))),
        ]
        shapes = [(1, width, part), (1, width, part), (1, part, width)]
    else:
        out_specs = passing
        shapes = [(width, 2 * part), (part, width)]
    return pl.pallas_call(
        functools.partial(grads_kernel, not more),
        grid_spec=pltpu.PrefetchScalarGridSpec(
            num_scalar_prefetch=1,
            grid=(width // step,),
            in_specs=[
                moving,
                moving,
                pl.BlockSpec((1, total, 2 * part), lambda i, w: (expert, 0, 0)),
                pl.BlockSpec((1, total, part), lambda i, w: (expert, 0, 0)),
            ]
            + (passing if more else [])
            + [LOOSE] * len(after),
            out_specs=out_specs,
            scratch_shapes=[pltpu.VMEM((part, total), jnp.bfloat16)],
        ),
        out_shape=[jax.ShapeDtypeStruct(shape, jnp.bfloat16) for shape in shapes],
        compiler_params=pltpu.CompilerParams(vmem_limit_bytes=56 << 20),
        cost_estimate=pl.CostEstimate(flops=6 * total * width * part, bytes_accessed=6 * total * width, transcendentals=0),
        name="grads",
    )(which, x_rows, g_rows, both, scaled, *more, *after)


def dense_device(tokens, out_grad, routes, probs, w_gate, w_up, w_down):
    owners = lax.axis_size(("role", "ep"))
    ep = lax.axis_size("ep")
    n_y = 2
    n_z = ep // n_y
    tok_rows, half = tokens.shape
    capacity = slot_capacity(tok_rows, routes.shape[1], owners)
    slots = -(-n_y * capacity // 16) * 16
    role, place, which = lax.axis_index("role"), lax.axis_index("ep"), lax.axis_index("tp")

    def over_x(array):
        return lax.ppermute(array, "tp", [(0, 1), (1, 0)])

    def over_role(array):
        return lax.ppermute(array, "role", [(0, 1), (1, 0)])

    def over_y(array):
        return lax.ppermute(array, "ep", [(i, i + 1 - 2 * (i % n_y)) for i in range(ep)])

    def over_z(array, shift):
        return lax.ppermute(array, "ep", [(i, (i + shift * n_y) % ep) for i in range(ep)])

    chosen = routes[:, :, None] == jnp.arange(owners, dtype=jnp.int32)
    table = jnp.sum(jnp.where(chosen, probs[:, :, None].astype(jnp.float32) + 1.0, 0.0), axis=1) - 1.0
    table = jnp.pad(table.astype(jnp.bfloat16).T, ((0, 0), (0, half - tok_rows)))
    units = {(0, 0, 0): jnp.concatenate([tokens, out_grad, table], 0)}
    last = n_z - 1
    for z in range(n_z):
        if z:
            back = 0 if z in (1, last) else z - 1
            shift = -1 if z == last and z > 1 else 1
            units[z, 0, 0] = over_z(units[back, 0, 0], shift)
        units[z, 1, 0] = over_y(units[z, 0, 0])
        units[z, 0, 1] = over_x(units[z, 0, 0])
        if z == 0:
            units[z, 1, 1] = over_x(units[z, 1, 0])
        elif z in (1, last):
            units[z, 1, 1] = over_z(units[0, 1, 1], shift)
        else:
            units[z, 1, 1] = over_y(units[z, 0, 1])

    which_ref = which.reshape(1).astype(jnp.int32)
    both_w, down_w = weights_call(which_ref, w_gate, w_up, w_down, [units[1, 0, 0], units[0, 1, 0], units[0, 0, 1]])
    weights = (both_w, over_role(both_w), down_w, over_role(down_w))
    where = jnp.stack([role * ep + place, (1 - role) * ep + place, which]).astype(jnp.int32)

    def add(a, b):
        return a.astype(jnp.float32) + b.astype(jnp.float32)

    held, homeward, early, late = (), [], [], []
    for group in (range(0, n_z, 2), range(1, n_z, 2)):
        modes = [index % 2 for index in range(len(group))]
        four = [units[z, y, x] for z in group for y in range(2) for x in range(2)]
        packets = rows_call(group, modes, n_z, owners, capacity, slots, where, weights, four, held)
        held, packets = packets[:4], packets[4:]
        for index, z in enumerate(group):
            keep, send = packets[index], packets[len(group) + index]
            go_first, go_second = (over_y, over_x) if modes[index] else (over_x, over_y)
            recv = go_first(send)
            recv_next = go_second(add(keep[1], recv[1]).astype(jnp.bfloat16))
            (late if group[0] else early).append(recv)
            if not group[0]:
                late.append(recv_next)
            total = add(add(keep[0], recv[0]), recv_next)
            homeward.append(over_z(total.astype(jnp.bfloat16), -z).astype(jnp.float32) if z else total)
    home = sum(homeward[1:], homeward[0])
    d_tok = home[:tok_rows].astype(jnp.bfloat16)
    more = grads_call(which_ref, 1, *held, [], early)
    d_gate, d_up, d_down = grads_call(which_ref, 0, *held, [over_role(item) for item in more], late)
    score = jnp.sum(home[tok_rows:, : 4 * tok_rows].reshape(owners, 4, tok_rows), axis=1).T
    d_probs = jnp.sum(jnp.where(chosen, score[:, None, :], 0.0), axis=2)
    return d_tok, d_probs, d_gate, d_up, d_down


def per_device(tokens, out_grad, routes, probs, w_gate, w_up, w_down):
    owners = lax.axis_size(("role", "ep"))
    tok_rows, top_count = routes.shape
    paired = lax.axis_size("tp") == 2 and lax.axis_size("role") == 2 and lax.axis_size("ep") % 4 == 0
    if paired and 2 * slot_capacity(tok_rows, top_count, owners) >= tok_rows:
        return dense_device(tokens, out_grad, routes, probs, w_gate, w_up, w_down)
    return routed_device(tokens, out_grad, routes, probs, w_gate, w_up, w_down)


def solution(mesh):
    in_specs = (
        P(("groups", "role", "ep"), "tp"),
        P(("groups", "role", "ep"), "tp"),
        P(("groups", "role", "ep"), None),
        P(("groups", "role", "ep"), None),
        P(("role", "ep"), None, "tp"),
        P(("role", "ep"), None, "tp"),
        P(("role", "ep"), "tp", None),
    )
    out_specs = (
        P(("groups", "role", "ep"), "tp"),
        P(("groups", "role", "ep"), None),
        P(("groups", "role", "ep"), None, "tp"),
        P(("groups", "role", "ep"), None, "tp"),
        P(("groups", "role", "ep"), "tp", None),
    )
    return jax.shard_map(
        per_device, mesh=mesh, in_specs=in_specs, out_specs=out_specs, check_vma=False
    )
```

time: 225 us -> 201 us (0.89)
  waiting for transfers between devices: 86.3 us -> 107 us
  starting transfers between devices: 49.2 us -> 30.4 us
  Pallas kernels: 64.4 us -> 49.2 us
  local copies, waits for them, and re-layouts: 17.1 us -> 8.51 us
    ppermute x14 -> x8, waiting for transfers between devices: 22.4 us -> 45.9 us  [over_z(): lax.ppermute(array, 'ep', [(i, (i + shift * n_y) % ep) for i in range(ep)])]
    ppermute x11 -> x9, waiting for transfers between devices: 28.6 us -> 9.4 us  [over_y(): lax.ppermute(array, 'ep', [(i, i + 1 - 2 * (i % n_y)) for i in range(ep)])]
    pallas_call x4 -> x2, Pallas kernels: 44.6 us -> 28.2 us  [rows_call(): pl.pallas_call(functools.partial(rows_kernel, places, modes, capacity, sl...]
    ppermute x10 -> x9, waiting for transfers between devices: 35.3 us -> 51.3 us  [over_x(): return lax.ppermute(array, 'tp', [(0, 1), (1, 0)])]
    ppermute x14 -> x8, starting transfers between devices: 23.8 us -> 13.6 us  [over_z(): lax.ppermute(array, 'ep', [(i, (i + shift * n_y) % ep) for i in range(ep)])]
    unnamed x80 -> x56, local copies, waits for them, and re-layouts: 15 us -> 7.75 us
    ppermute x11 -> x9, starting transfers between devices: 13.2 us -> 7.88 us  [over_y(): lax.ppermute(array, 'ep', [(i, i + 1 - 2 * (i % n_y)) for i in range(ep)])]
    ppermute x10 -> x9, starting transfers between devices: 11.7 us -> 8.86 us  [over_x(): return lax.ppermute(array, 'tp', [(0, 1), (1, 0)])]
  transfers between devices with their start and end apart: 39 -> 30, of which waited for: 13 -> 16; matrix products, arithmetic and copies ran while one was open for 4% -> 1% of each run, Pallas kernels for 15% -> 14%
where the time goes in v5:
time: 201 us; the launch traced here: 200 us
  waiting for transfers between devices  107 us (53%)
  Pallas kernels  49.2 us (24%)
  starting transfers between devices  30.4 us (15%)
  local copies, waits for them, and re-layouts  8.51 us (4%)
  other arithmetic  4.71 us (2%)
    ppermute x9, waiting for transfers between devices, over_x(): return lax.ppermute(array, 'tp', [(0, 1), (1, 0)])  51.3 us
    ppermute x8, waiting for transfers between devices, over_z(): lax.ppermute(array, 'ep', [(i, (i + shift * n_y) % ep) for i in range(ep)])  45.9 us
    pallas_call x2, Pallas kernels, rows_call(): pl.pallas_call(functools.partial(rows_kernel, places, modes, capacity, sl...  28.2 us
    pallas_call x2, Pallas kernels, grads_call(): pl.pallas_call(functools.partial(grads_kernel, not more), grid_spec=pltpu...  17 us
    ppermute x8, starting transfers between devices, over_z(): lax.ppermute(array, 'ep', [(i, (i + shift * n_y) % ep) for i in range(ep)])  13.6 us
    ppermute x9, waiting for transfers between devices, over_y(): lax.ppermute(array, 'ep', [(i, i + 1 - 2 * (i % n_y)) for i in range(ep)])  9.4 us
    ppermute x9, starting transfers between devices, over_x(): return lax.ppermute(array, 'tp', [(0, 1), (1, 0)])  8.86 us
    ppermute x9, starting transfers between devices, over_y(): lax.ppermute(array, 'ep', [(i, i + 1 - 2 * (i % n_y)) for i in range(ep)])  7.88 us
  transfers between devices with their start and end apart: 30, of which 16 were waited for; matrix products, arithmetic and copies ran while one was open for 1% of the time, Pallas kernels for 14%

profile of v5, /device:TPU:0, one launch (start us, length us, event | category | flops | bytes accessed | tf_op | source)
XLA Modules:
  0.0 200.4 jit_solution(15895107835490449723)
XLA Ops:
  0.6 0.7 convert_add_fusion
  1.3 0.7 select_reduce_fusion.1
  2.0 1.1 fusion.7.refs_4_
  3.1 3.0 %collective-permute-start.2 = (bf16[272,1024]{1,0:T(8,128)(2,1)S(1)}, bf16[272,1024]{1,0:T(8,128)(2,1)S(1)}, u32[]{:S(2)}, u32[]{:S(2)}) collective-permute-start(bf16[272,1024]{1,0:T(8,128)(2,1)S(1)} %fusion.7.refs_4_), channel_id=1, source_target_pairs={{0,1},{1,0},{2,3},{3,2},{4,5},{5,4},{6,7},{7,6},{8,9},{9,8},{10,11... | collective-permute-start | bytes 1671176 | tf_op jit(solution)/shard_map/ppermute | solution.py:422
  6.1 1.5 collective-permute-start.1
  7.6 1.6 collective-permute-start
  9.2 9.5 %collective-permute-done.2.refs_2_.refs_5_ = bf16[272,1024]{1,0:T(8,128)(2,1)S(1)} collective-permute-done((bf16[272,1024]{1,0:T(8,128)(2,1)S(1)}, bf16[272,1024]{1,0:T(8,128)(2,1)S(1)}, u32[]{:S(2)}, u32[]{:S(2)}) %collective-permute-start.2) | collective-permute-done | bytes 557088 | tf_op jit(solution)/shard_map/ppermute | solution.py:422
  18.7 1.5 collective-permute-done.1.refs_1_.refs_6_
  20.2 3.1 %collective-permute-done.refs_0_.refs_4_ = bf16[272,1024]{1,0:T(8,128)(2,1)S(1)} collective-permute-done((bf16[272,1024]{1,0:T(8,128)(2,1)S(1)}, bf16[272,1024]{1,0:T(8,128)(2,1)S(1)}, u32[]{:S(2)}, u32[]{:S(2)}) %collective-permute-start) | collective-permute-done | bytes 557088 | tf_op jit(solution)/shard_map/ppermute | solution.py:431
  23.3 0.8 copy-done.8
  24.1 4.0 %weights.1 = (bf16[2048,768]{1,0:T(8,128)(2,1)}, bf16[384,2048]{1,0:T(8,128)(2,1)}) custom-call(s32[1]{0:T(128)} %bitcast.2.tp_ref, bf16[1,2048,384]{2,1,0:T(8,128)(2,1)} %wg_ref.1, bf16[1,2048,384]{2,1,0:T(8,128)(2,1)} %wu_ref.1, bf16[1,384,2048]{2,1,0:T(8,128)(2,1)} %wd_ref.1, bf16[272,1024]{1,0:T(8,128)(2,1)} %copy-done.8, bf16[272,1024]{1,0:T(8,128)(2,1)} %copy-done.17, ...), custom_call_target="tpu_custom_call" | custom-call | bytes 9437184 | tf_op jit(solution)/shard_map/weights/pallas_call | solution.py:142
  28.1 1.8 collective-permute-start.18
  30.2 13.4 %collective-permute-done.18.refs_8_ = bf16[272,1024]{1,0:T(8,128)(2,1)S(1)} collective-permute-done((bf16[272,1024]{1,0:T(8,128)(2,1)}, bf16[272,1024]{1,0:T(8,128)(2,1)S(1)}, u32[]{:S(2)}, u32[]{:S(2)}) %collective-permute-start.18) | collective-permute-done | bytes 557088 | tf_op jit(solution)/shard_map/ppermute | solution.py:431
  43.6 0.8 copy-done.15
  45.0 10.6 %collective-permute-done.6.refs_8_ = bf16[272,1024]{1,0:T(8,128)(2,1)} collective-permute-done((bf16[272,1024]{1,0:T(8,128)(2,1)}, bf16[272,1024]{1,0:T(8,128)(2,1)}, u32[]{:S(2)}, u32[]{:S(2)}) %collective-permute-start.6) | collective-permute-done | bytes 557088 | tf_op jit(solution)/shard_map/ppermute | solution.py:431
  56.1 1.5 collective-permute-start.5
  57.6 0.8 collective-permute-done.20.refs_10_
  58.4 0.9 copy-done.18
  59.8 11.6 %collective-permute-done.7.refs_9_ = bf16[272,1024]{1,0:T(8,128)(2,1)} collective-permute-done((bf16[272,1024]{1,0:T(8,128)(2,1)}, bf16[272,1024]{1,0:T(8,128)(2,1)}, u32[]{:S(2)}, u32[]{:S(2)}) %collective-permute-start.7) | collective-permute-done | bytes 557088 | tf_op jit(solution)/shard_map/ppermute | solution.py:422
  71.9 0.6 pad_add_fusion.where_ref
  72.5 9.5 %collective-permute-done.5.refs_7_ = bf16[272,1024]{1,0:T(8,128)(2,1)} collective-permute-done((bf16[272,1024]{1,0:T(8,128)(2,1)}, bf16[272,1024]{1,0:T(8,128)(2,1)}, u32[]{:S(2)}, u32[]{:S(2)}) %collective-permute-start.5) | collective-permute-done | bytes 557088 | tf_op jit(solution)/shard_map/ppermute | solution.py:422
  83.1 1.5 collective-permute-start.15
  85.0 5.6 %collective-permute-start.21 = (bf16[272,1024]{1,0:T(8,128)(2,1)}, bf16[272,1024]{1,0:T(8,128)(2,1)S(1)}, u32[]{:S(2)}, u32[]{:S(2)}) collective-permute-start(bf16[272,1024]{1,0:T(8,128)(2,1)} %collective-permute-done.5.refs_7_), channel_id=1, source_target_pairs={{0,12},{2,14},{4,0},{6,2},{8,4},{10,6},{12,8},{14,10},{1,13},{3,15... | collective-permute-start | bytes 1671176 | tf_op jit(solution)/shard_map/ppermute | solution.py:431
  90.7 1.6 copy-done
  92.3 14.0 %rows.2 = (bf16[2,576,2048]{2,1,0:T(8,128)(2,1)}, bf16[2,576,2048]{2,1,0:T(8,128)(2,1)}, bf16[2,576,768]{2,1,0:T(8,128)(2,1)}, bf16[2,576,384]{2,1,0:T(8,128)(2,...) custom-call(s32[3]{0:T(128)} %pad_add_fusion.where_ref, ...), custom_call_target="tpu_custom_call" | custom-call | flops 6341787648 | bytes 17825792 | tf_op jit(solution)/shard_map/rows/pallas_call | solution.py:309
  106.4 0.6 collective-permute-start.12
  107.0 2.8 %collective-permute-done.15.refs_5_ = bf16[272,1024]{1,0:T(8,128)(2,1)S(1)} collective-permute-done((bf16[272,1024]{1,0:T(8,128)(2,1)}, bf16[272,1024]{1,0:T(8,128)(2,1)S(1)}, u32[]{:S(2)}, u32[]{:S(2)}) %collective-permute-start.15) | collective-permute-done | bytes 557088 | tf_op jit(solution)/shard_map/ppermute | solution.py:422
  111.0 14.2 %rows.3 = (bf16[2,576,2048]{2,1,0:T(8,128)(2,1)}, bf16[2,576,2048]{2,1,0:T(8,128)(2,1)}, bf16[2,576,768]{2,1,0:T(8,128)(2,1)}, bf16[2,576,384]{2,1,0:T(8,128)(2,...) custom-call(s32[3]{0:T(128)} %pad_add_fusion.where_ref, ...), custom_call_target="tpu_custom_call", output_to_operand_aliasing={{0}: (13, {}), {1}: (14, {}), {2}: (15, {}), {3}: (16, {})} | custom-call | flops 6341787648 | bytes 17825792 | tf_op jit(solution)/shard_map/rows/pallas_call | solution.py:309
  125.3 0.8 copy-done.2
  126.3 8.3 %grads.2 = (bf16[2048,768]{1,0:T(8,128)(2,1)}, bf16[384,2048]{1,0:T(8,128)(2,1)}) custom-call(s32[1]{0:T(128)} %bitcast.2.tp_ref, bf16[2,576,2048]{2,1,0:T(8,128)(2,1)} %get-tuple-element.42.x_ref, bf16[2,576,2048]{2,1,0:T(8,128)(2,1)} %get-tuple-element.43.g_ref, bf16[2,576,768]{2,1,0:T(8,128)(2,1)} %get-tuple-element.44.both_ref, ...), custom_call_target="tpu_custom_call" | custom-call | flops 2717908992 | bytes 7077888 | tf_op jit(solution)/shard_map/grads/pallas_call | solution.py:388
  134.7 0.6 collective-permute-start.22
  135.3 1.3 collective-permute-start.25
  136.6 13.9 %collective-permute-done.22.refs_4_ = bf16[2,144,1024]{2,1,0:T(8,128)(2,1)S(1)} collective-permute-done((bf16[2,144,1024]{2,1,0:T(8,128)(2,1)S(1)}, bf16[2,144,1024]{2,1,0:T(8,128)(2,1)S(1)}, u32[]{:S(2)}, u32[]{:S(2)}) %collective-permute-start.22) | collective-permute-done | bytes 589856 | tf_op jit(solution)/shard_map/ppermute | solution.py:422
  150.5 1.4 collective-permute-start.23
  152.0 0.6 collective-permute-start.26
  152.7 1.1 collective-permute-start.11
  153.9 6.6 %collective-permute-done.23 = bf16[144,1024]{1,0:T(8,128)(2,1)S(1)} collective-permute-done((bf16[144,1024]{1,0:T(8,128)(2,1)S(1)}, bf16[144,1024]{1,0:T(8,128)(2,1)S(1)}, u32[]{:S(2)}, u32[]{:S(2)}) %collective-permute-start.23) | collective-permute-done | bytes 294944 | tf_op jit(solution)/shard_map/ppermute | solution.py:428
  160.5 0.5 collective-permute-start.13
  161.2 1.9 collective-permute-start.24
  163.2 4.0 %collective-permute-done.13.refs_3_ = bf16[144,1024]{1,0:T(8,128)(2,1)S(1)} collective-permute-done((bf16[144,1024]{1,0:T(8,128)(2,1)S(1)}, bf16[144,1024]{1,0:T(8,128)(2,1)S(1)}, u32[]{:S(2)}, u32[]{:S(2)}) %collective-permute-start.13) | collective-permute-done | bytes 294944 | tf_op jit(solution)/shard_map/ppermute | solution.py:422
  167.3 1.8 collective-permute-start.27
  169.2 0.6 collective-permute-start.14
  169.9 8.9 %collective-permute-done.27 = bf16[144,1024]{1,0:T(8,128)(2,1)S(1)} collective-permute-done((bf16[144,1024]{1,0:T(8,128)(2,1)S(1)}, bf16[144,1024]{1,0:T(8,128)(2,1)S(1)}, u32[]{:S(2)}, u32[]{:S(2)}) %collective-permute-start.27) | collective-permute-done | bytes 294944 | tf_op jit(solution)/shard_map/ppermute | solution.py:431
  178.8 9.4 %collective-permute-done.14 = bf16[144,1024]{1,0:T(8,128)(2,1)S(1)} collective-permute-done((bf16[144,1024]{1,0:T(8,128)(2,1)S(1)}, bf16[144,1024]{1,0:T(8,128)(2,1)S(1)}, u32[]{:S(2)}, u32[]{:S(2)}) %collective-permute-start.14) | collective-permute-done | bytes 294944 | tf_op jit(solution)/shard_map/ppermute | solution.py:431
  188.5 0.7 slice.100
  189.3 0.6 select_reduce_fusion
  189.9 1.7 copy-done.1
  191.6 8.7 %grads.3 = (bf16[1,2048,384]{2,1,0:T(8,128)(2,1)}, bf16[1,2048,384]{2,1,0:T(8,128)(2,1)}, bf16[1,384,2048]{2,1,0:T(8,128)(2,1)}) custom-call(s32[1]{0:T(128)} %bitcast.2.tp_ref, bf16[2,576,2048]{2,1,0:T(8,128)(2,1)} %get-tuple-element.42.x_ref, bf16[2,576,2048]{2,1,0:T(8,128)(2,1)} %get-tuple-element.43.g_ref, ...), custom_call_target="tpu_custom_call" | custom-call | flops 2717908992 | bytes 7077888 | tf_op jit(solution)/shard_map/grads/pallas_call | solution.py:388
  (91 shorter events, 6.7 us)
Async XLA Ops:
  3.1 25.0 %copy-start.24 = (bf16[272,1024]{1,0:T(8,128)(2,1)}, bf16[272,1024]{1,0:T(8,128)(2,1)S(1)}, u32[]{:S(2)}) copy-start(bf16[272,1024]{1,0:T(8,128)(2,1)S(1)} %fusion.7.refs_4_) | copy-start | bytes 1671172
  3.1 15.6 %collective-permute-start.2 = (bf16[272,1024]{1,0:T(8,128)(2,1)S(1)}, bf16[272,1024]{1,0:T(8,128)(2,1)S(1)}, u32[]{:S(2)}, u32[]{:S(2)}) collective-permute-start(bf16[272,1024]{1,0:T(8,128)(2,1)S(1)} %fusion.7.refs_4_), channel_id=1, source_target_pairs={{0,1},{1,0},{2,3},{3,2},{4,5},{5,4},{6,7},{7,6},{8,9},{9,8},{10,11... | collective-permute-start | bytes 1671176 | tf_op jit(solution)/shard_map/ppermute | solution.py:422
  6.1 14.1 %collective-permute-start.1 = (bf16[272,1024]{1,0:T(8,128)(2,1)S(1)}, bf16[272,1024]{1,0:T(8,128)(2,1)S(1)}, u32[]{:S(2)}, u32[]{:S(2)}) collective-permute-start(bf16[272,1024]{1,0:T(8,128)(2,1)S(1)} %fusion.7.refs_4_), channel_id=1, source_target_pairs={{0,2},{2,0},{4,6},{6,4},{8,10},{10,8},{12,14},{14,12},{1,3},{3,1},... | collective-permute-start | bytes 1671176 | tf_op jit(solution)/shard_map/ppermute | solution.py:428
  7.6 15.7 %collective-permute-start = (bf16[272,1024]{1,0:T(8,128)(2,1)S(1)}, bf16[272,1024]{1,0:T(8,128)(2,1)S(1)}, u32[]{:S(2)}, u32[]{:S(2)}) collective-permute-start(bf16[272,1024]{1,0:T(8,128)(2,1)S(1)} %fusion.7.refs_4_), channel_id=1, source_target_pairs={{0,4},{2,6},{4,8},{6,10},{8,12},{10,14},{12,0},{14,2},{1,5},{3,7},... | collective-permute-start | bytes 1671176 | tf_op jit(solution)/shard_map/ppermute | solution.py:431
  18.7 4.6 %copy-start.16 = (bf16[272,1024]{1,0:T(8,128)(2,1)}, bf16[272,1024]{1,0:T(8,128)(2,1)S(1)}, u32[]{:S(2)}) copy-start(bf16[272,1024]{1,0:T(8,128)(2,1)S(1)} %collective-permute-done.2.refs_2_.refs_5_) | copy-start | bytes 1671172
  20.2 3.1 %copy-start.17 = (bf16[272,1024]{1,0:T(8,128)(2,1)}, bf16[272,1024]{1,0:T(8,128)(2,1)S(1)}, u32[]{:S(2)}) copy-start(bf16[272,1024]{1,0:T(8,128)(2,1)S(1)} %collective-permute-done.1.refs_1_.refs_6_) | copy-start | bytes 1671172
  28.1 62.6 %collective-permute-start.3 = (bf16[2048,768]{1,0:T(8,128)(2,1)}, bf16[2048,768]{1,0:T(8,128)(2,1)S(1)}, u32[]{:S(2)}, u32[]{:S(2)}) collective-permute-start(bf16[2048,768]{1,0:T(8,128)(2,1)} %get-tuple-element.28.refs_0_), channel_id=1, source_target_pairs={{0,16},{16,0},{1,17},{17,1},{2,18},{18,2},{3,19},{19,3},{4,20},{20... | collective-permute-start | bytes 9437192 | tf_op jit(solution)/shard_map/ppermute | solution.py:425
  28.1 15.5 %collective-permute-start.18 = (bf16[272,1024]{1,0:T(8,128)(2,1)}, bf16[272,1024]{1,0:T(8,128)(2,1)S(1)}, u32[]{:S(2)}, u32[]{:S(2)}) collective-permute-start(bf16[272,1024]{1,0:T(8,128)(2,1)} %copy-done.24), channel_id=1, source_target_pairs={{0,12},{2,14},{4,0},{6,2},{8,4},{10,6},{12,8},{14,10},{1,13},{3,15... | collective-permute-start | bytes 1671176 | tf_op jit(solution)/shard_map/ppermute | solution.py:431
  29.9 25.7 %collective-permute-start.6 = (bf16[272,1024]{1,0:T(8,128)(2,1)}, bf16[272,1024]{1,0:T(8,128)(2,1)}, u32[]{:S(2)}, u32[]{:S(2)}) collective-permute-start(bf16[272,1024]{1,0:T(8,128)(2,1)} %copy-done.8), channel_id=1, source_target_pairs={{0,4},{2,6},{4,8},{6,10},{8,12},{10,14},{12,0},{14,2},{1,5},{3,7},... | collective-permute-start | bytes 1671176 | tf_op jit(solution)/shard_map/ppermute | solution.py:431
  30.2 52.9 %collective-permute-start.4 = (bf16[384,2048]{1,0:T(8,128)(2,1)}, bf16[384,2048]{1,0:T(8,128)(2,1)}, u32[]{:S(2)}, u32[]{:S(2)}) collective-permute-start(bf16[384,2048]{1,0:T(8,128)(2,1)} %get-tuple-element.29.refs_2_), channel_id=1, source_target_pairs={{0,16},{16,0},{1,17},{17,1},{2,18},{18,2},{3,19},{19,3},{4,20},{20... | collective-permute-start | bytes 4718600 | tf_op jit(solution)/shard_map/ppermute | solution.py:425
  44.5 13.9 %collective-permute-start.20 = (bf16[272,1024]{1,0:T(8,128)(2,1)S(1)}, bf16[272,1024]{1,0:T(8,128)(2,1)S(1)}, u32[]{:S(2)}, u32[]{:S(2)}) collective-permute-start(bf16[272,1024]{1,0:T(8,128)(2,1)S(1)} %collective-permute-done.18.refs_8_), channel_id=1, source_target_pairs={{0,2},{2,0},{4,6},{6,4},{8,10},{10,8},{12,14},{14,12},{1,3},{3,1},... | collective-permute-start | bytes 1671176 | tf_op jit(solution)/shard_map/ppermute | solution.py:428
  55.6 15.9 %collective-permute-start.7 = (bf16[272,1024]{1,0:T(8,128)(2,1)}, bf16[272,1024]{1,0:T(8,128)(2,1)}, u32[]{:S(2)}, u32[]{:S(2)}) collective-permute-start(bf16[272,1024]{1,0:T(8,128)(2,1)} %collective-permute-done.6.refs_8_), channel_id=1, source_target_pairs={{0,1},{1,0},{2,3},{3,2},{4,5},{5,4},{6,7},{7,6},{8,9},{9,8},{10,11... | collective-permute-start | bytes 1671176 | tf_op jit(solution)/shard_map/ppermute | solution.py:422
  56.1 25.9 %collective-permute-start.5 = (bf16[272,1024]{1,0:T(8,128)(2,1)}, bf16[272,1024]{1,0:T(8,128)(2,1)}, u32[]{:S(2)}, u32[]{:S(2)}) collective-permute-start(bf16[272,1024]{1,0:T(8,128)(2,1)} %copy-done.17), channel_id=1, source_target_pairs={{0,1},{1,0},{2,3},{3,2},{4,5},{5,4},{6,7},{7,6},{8,9},{9,8},{10,11... | collective-permute-start | bytes 1671176 | tf_op jit(solution)/shard_map/ppermute | solution.py:422
  59.3 23.3 %collective-permute-start.8 = (bf16[272,1024]{1,0:T(8,128)(2,1)}, bf16[272,1024]{1,0:T(8,128)(2,1)}, u32[]{:S(2)}, u32[]{:S(2)}) collective-permute-start(bf16[272,1024]{1,0:T(8,128)(2,1)} %collective-permute-done.6.refs_8_), channel_id=1, source_target_pairs={{0,2},{2,0},{4,6},{6,4},{8,10},{10,8},{12,14},{14,12},{1,3},{3,1},... | collective-permute-start | bytes 1671176 | tf_op jit(solution)/shard_map/ppermute | solution.py:428
  71.4 13.6 %collective-permute-start.9 = (bf16[272,1024]{1,0:T(8,128)(2,1)}, bf16[272,1024]{1,0:T(8,128)(2,1)}, u32[]{:S(2)}, u32[]{:S(2)}) collective-permute-start(bf16[272,1024]{1,0:T(8,128)(2,1)} %collective-permute-done.7.refs_9_), channel_id=1, source_target_pairs={{0,2},{2,0},{4,6},{6,4},{8,10},{10,8},{12,14},{14,12},{1,3},{3,1},... | collective-permute-start | bytes 1671176 | tf_op jit(solution)/shard_map/ppermute | solution.py:428
  82.0 24.3 %collective-permute-start.19 = (bf16[272,1024]{1,0:T(8,128)(2,1)}, bf16[272,1024]{1,0:T(8,128)(2,1)S(1)}, u32[]{:S(2)}, u32[]{:S(2)}) collective-permute-start(bf16[272,1024]{1,0:T(8,128)(2,1)} %copy-done.15), channel_id=1, source_target_pairs={{0,1},{1,0},{2,3},{3,2},{4,5},{5,4},{6,7},{7,6},{8,9},{9,8},{10,11... | collective-permute-start | bytes 1671176 | tf_op jit(solution)/shard_map/ppermute | solution.py:422
  82.5 23.8 %collective-permute-start.16 = (bf16[272,1024]{1,0:T(8,128)(2,1)}, bf16[272,1024]{1,0:T(8,128)(2,1)S(1)}, u32[]{:S(2)}, u32[]{:S(2)}) collective-permute-start(bf16[272,1024]{1,0:T(8,128)(2,1)} %copy-done.8), channel_id=1, source_target_pairs={{0,2},{2,0},{4,6},{6,4},{8,10},{10,8},{12,14},{14,12},{1,3},{3,1},... | collective-permute-start | bytes 1671176 | tf_op jit(solution)/shard_map/ppermute | solution.py:428
  83.1 26.7 %collective-permute-start.15 = (bf16[272,1024]{1,0:T(8,128)(2,1)}, bf16[272,1024]{1,0:T(8,128)(2,1)S(1)}, u32[]{:S(2)}, u32[]{:S(2)}) collective-permute-start(bf16[272,1024]{1,0:T(8,128)(2,1)} %copy-done.8), channel_id=1, source_target_pairs={{0,1},{1,0},{2,3},{3,2},{4,5},{5,4},{6,7},{7,6},{8,9},{9,8},{10,11... | collective-permute-start | bytes 1671176 | tf_op jit(solution)/shard_map/ppermute | solution.py:422
  85.0 24.7 %collective-permute-start.21 = (bf16[272,1024]{1,0:T(8,128)(2,1)}, bf16[272,1024]{1,0:T(8,128)(2,1)S(1)}, u32[]{:S(2)}, u32[]{:S(2)}) collective-permute-start(bf16[272,1024]{1,0:T(8,128)(2,1)} %collective-permute-done.5.refs_7_), channel_id=1, source_target_pairs={{0,12},{2,14},{4,0},{6,2},{8,4},{10,6},{12,8},{14,10},{1,13},{3,15... | collective-permute-start | bytes 1671176 | tf_op jit(solution)/shard_map/ppermute | solution.py:431
  90.7 19.6 %collective-permute-start.17 = (bf16[272,1024]{1,0:T(8,128)(2,1)}, bf16[272,1024]{1,0:T(8,128)(2,1)S(1)}, u32[]{:S(2)}, u32[]{:S(2)}) collective-permute-start(bf16[272,1024]{1,0:T(8,128)(2,1)} %collective-permute-done.5.refs_7_), channel_id=1, source_target_pairs={{0,4},{2,6},{4,8},{6,10},{8,12},{10,14},{12,0},{14,2},{1,5},{3,7},... | collective-permute-start | bytes 1671176 | tf_op jit(solution)/shard_map/ppermute | solution.py:431
  106.3 4.0 %copy-start.19 = (bf16[272,1024]{1,0:T(8,128)(2,1)}, bf16[272,1024]{1,0:T(8,128)(2,1)S(1)}, u32[]{:S(2)}) copy-start(bf16[272,1024]{1,0:T(8,128)(2,1)S(1)} %collective-permute-done.19.refs_9_) | copy-start | bytes 1671172
  106.3 19.0 %collective-permute-start.10 = (bf16[2,144,1024]{2,1,0:T(8,128)(2,1)}, bf16[2,144,1024]{2,1,0:T(8,128)(2,1)S(1)}, u32[]{:S(2)}, u32[]{:S(2)}) collective-permute-start(bf16[2,144,1024]{2,1,0:T(8,128)(2,1)} %get-tuple-element.31), channel_id=1, source_target_pairs={{0,1},{1,0},{2,3},{3,2},{4,5},{5,4},{6,7},{7,6},{8,9},{9,8},{10,11... | collective-permute-start | bytes 1769480 | tf_op jit(solution)/shard_map/ppermute | solution.py:422
  106.4 3.9 %copy-start.20 = (bf16[272,1024]{1,0:T(8,128)(2,1)}, bf16[272,1024]{1,0:T(8,128)(2,1)S(1)}, u32[]{:S(2)}) copy-start(bf16[272,1024]{1,0:T(8,128)(2,1)S(1)} %collective-permute-done.16.refs_6_) | copy-start | bytes 1671172
  106.4 18.9 %collective-permute-start.12 = (bf16[2,144,1024]{2,1,0:T(8,128)(2,1)}, bf16[2,144,1024]{2,1,0:T(8,128)(2,1)S(1)}, u32[]{:S(2)}, u32[]{:S(2)}) collective-permute-start(bf16[2,144,1024]{2,1,0:T(8,128)(2,1)} %get-tuple-element.33), channel_id=1, source_target_pairs={{0,2},{2,0},{4,6},{6,4},{8,10},{10,8},{12,14},{14,12},{1,3},{3,1},... | collective-permute-start | bytes 1769480 | tf_op jit(solution)/shard_map/ppermute | solution.py:428
  126.3 8.4 %copy-start.27 = (bf16[2,144,1024]{2,1,0:T(8,128)(2,1)S(1)}, bf16[2,144,1024]{2,1,0:T(8,128)(2,1)}, u32[]{:S(2)}) copy-start(bf16[2,144,1024]{2,1,0:T(8,128)(2,1)} %get-tuple-element.39) | copy-start | bytes 1769476
  126.3 9.0 %copy-start.26 = (bf16[2,144,1024]{2,1,0:T(8,128)(2,1)S(1)}, bf16[2,144,1024]{2,1,0:T(8,128)(2,1)}, u32[]{:S(2)}) copy-start(bf16[2,144,1024]{2,1,0:T(8,128)(2,1)} %get-tuple-element.41) | copy-start | bytes 1769476
  126.3 24.2 %copy-start.14 = (bf16[2,144,1024]{2,1,0:T(8,128)(2,1)S(1)}, bf16[2,144,1024]{2,1,0:T(8,128)(2,1)}, u32[]{:S(2)}) copy-start(bf16[2,144,1024]{2,1,0:T(8,128)(2,1)} %get-tuple-element.38) | copy-start | bytes 1769476
  126.3 25.6 %copy-start.13 = (bf16[2,144,1024]{2,1,0:T(8,128)(2,1)S(1)}, bf16[2,144,1024]{2,1,0:T(8,128)(2,1)}, u32[]{:S(2)}) copy-start(bf16[2,144,1024]{2,1,0:T(8,128)(2,1)} %get-tuple-element.40) | copy-start | bytes 1769476
  134.6 18.0 %copy-start.3 = (bf16[2,144,1024]{2,1,0:T(8,128)(2,1)S(1)}, bf16[2,144,1024]{2,1,0:T(8,128)(2,1)}, u32[]{:S(2)}) copy-start(bf16[2,144,1024]{2,1,0:T(8,128)(2,1)} %copy-done.2) | copy-start | bytes 1769476
  134.6 18.0 %copy-start.11 = (bf16[2,144,1024]{2,1,0:T(8,128)(2,1)S(1)}, bf16[2,144,1024]{2,1,0:T(8,128)(2,1)}, u32[]{:S(2)}) copy-start(bf16[2,144,1024]{2,1,0:T(8,128)(2,1)} %get-tuple-element.30) | copy-start | bytes 1769476
  134.6 19.2 %copy-start.5 = (bf16[2,144,1024]{2,1,0:T(8,128)(2,1)S(1)}, bf16[2,144,1024]{2,1,0:T(8,128)(2,1)}, u32[]{:S(2)}) copy-start(bf16[2,144,1024]{2,1,0:T(8,128)(2,1)} %copy-done.4) | copy-start | bytes 1769476
  134.6 19.2 %copy-start.12 = (bf16[2,144,1024]{2,1,0:T(8,128)(2,1)S(1)}, bf16[2,144,1024]{2,1,0:T(8,128)(2,1)}, u32[]{:S(2)}) copy-start(bf16[2,144,1024]{2,1,0:T(8,128)(2,1)} %get-tuple-element.32) | copy-start | bytes 1769476
  134.6 55.3 %collective-permute-start.28 = (bf16[2048,768]{1,0:T(8,128)(2,1)}, bf16[2048,768]{1,0:T(8,128)(2,1)S(1)}, u32[]{:S(2)}, u32[]{:S(2)}) collective-permute-start(bf16[2048,768]{1,0:T(8,128)(2,1)} %get-tuple-element.46), channel_id=1, source_target_pairs={{0,16},{16,0},{1,17},{17,1},{2,18},{18,2},{3,19},{19,3},{4,20},{20... | collective-permute-start | bytes 9437192 | tf_op jit(solution)/shard_map/ppermute | solution.py:425
  134.7 15.7 %collective-permute-start.22 = (bf16[2,144,1024]{2,1,0:T(8,128)(2,1)S(1)}, bf16[2,144,1024]{2,1,0:T(8,128)(2,1)S(1)}, u32[]{:S(2)}, u32[]{:S(2)}) collective-permute-start(bf16[2,144,1024]{2,1,0:T(8,128)(2,1)S(1)} %copy-done.27), channel_id=1, source_target_pairs={{0,1},{1,0},{2,3},{3,2},{4,5},{5,4},{6,7},{7,6},{8,9},{9,8},{10,11... | collective-permute-start | bytes 1769480 | tf_op jit(solution)/shard_map/ppermute | solution.py:422
  135.3 16.6 %collective-permute-start.25 = (bf16[2,144,1024]{2,1,0:T(8,128)(2,1)S(1)}, bf16[2,144,1024]{2,1,0:T(8,128)(2,1)S(1)}, u32[]{:S(2)}, u32[]{:S(2)}) collective-permute-start(bf16[2,144,1024]{2,1,0:T(8,128)(2,1)S(1)} %copy-done.26), channel_id=1, source_target_pairs={{0,2},{2,0},{4,6},{6,4},{8,10},{10,8},{12,14},{14,12},{1,3},{3,1},... | collective-permute-start | bytes 1769480 | tf_op jit(solution)/shard_map/ppermute | solution.py:428
  150.5 10.6 %copy-start.6 = (bf16[2,144,1024]{2,1,0:T(8,128)(2,1)}, bf16[2,144,1024]{2,1,0:T(8,128)(2,1)S(1)}, u32[]{:S(2)}) copy-start(bf16[2,144,1024]{2,1,0:T(8,128)(2,1)S(1)} %collective-permute-done.22.refs_4_) | copy-start | bytes 1769476
  150.5 10.0 %collective-permute-start.23 = (bf16[144,1024]{1,0:T(8,128)(2,1)S(1)}, bf16[144,1024]{1,0:T(8,128)(2,1)S(1)}, u32[]{:S(2)}, u32[]{:S(2)}) collective-permute-start(bf16[144,1024]{1,0:T(8,128)(2,1)S(1)} %fusion.10), channel_id=1, source_target_pairs={{0,2},{2,0},{4,6},{6,4},{8,10},{10,8},{12,14},{14,12},{1,3},{3,1},... | collective-permute-start | bytes 884744 | tf_op jit(solution)/shard_map/ppermute | solution.py:428
  151.9 11.2 %copy-start.7 = (bf16[2,144,1024]{2,1,0:T(8,128)(2,1)}, bf16[2,144,1024]{2,1,0:T(8,128)(2,1)S(1)}, u32[]{:S(2)}) copy-start(bf16[2,144,1024]{2,1,0:T(8,128)(2,1)S(1)} %collective-permute-done.25.refs_5_) | copy-start | bytes 1769476
  152.0 9.2 %collective-permute-start.26 = (bf16[144,1024]{1,0:T(8,128)(2,1)S(1)}, bf16[144,1024]{1,0:T(8,128)(2,1)S(1)}, u32[]{:S(2)}, u32[]{:S(2)}) collective-permute-start(bf16[144,1024]{1,0:T(8,128)(2,1)S(1)} %fusion.11), channel_id=1, source_target_pairs={{0,1},{1,0},{2,3},{3,2},{4,5},{5,4},{6,7},{7,6},{8,9},{9,8},{10,11... | collective-permute-start | bytes 884744 | tf_op jit(solution)/shard_map/ppermute | solution.py:422
  152.7 16.6 %collective-permute-start.11 = (bf16[144,1024]{1,0:T(8,128)(2,1)S(1)}, bf16[144,1024]{1,0:T(8,128)(2,1)S(1)}, u32[]{:S(2)}, u32[]{:S(2)}) collective-permute-start(bf16[144,1024]{1,0:T(8,128)(2,1)S(1)} %fusion.8), channel_id=1, source_target_pairs={{0,2},{2,0},{4,6},{6,4},{8,10},{10,8},{12,14},{14,12},{1,3},{3,1},... | collective-permute-start | bytes 884744 | tf_op jit(solution)/shard_map/ppermute | solution.py:428
  153.8 36.1 %collective-permute-start.29 = (bf16[384,2048]{1,0:T(8,128)(2,1)}, bf16[384,2048]{1,0:T(8,128)(2,1)}, u32[]{:S(2)}, u32[]{:S(2)}) collective-permute-start(bf16[384,2048]{1,0:T(8,128)(2,1)} %get-tuple-element.47), channel_id=1, source_target_pairs={{0,16},{16,0},{1,17},{17,1},{2,18},{18,2},{3,19},{19,3},{4,20},{20... | collective-permute-start | bytes 4718600 | tf_op jit(solution)/shard_map/ppermute | solution.py:425
  160.5 6.7 %collective-permute-start.13 = (bf16[144,1024]{1,0:T(8,128)(2,1)S(1)}, bf16[144,1024]{1,0:T(8,128)(2,1)S(1)}, u32[]{:S(2)}, u32[]{:S(2)}) collective-permute-start(bf16[144,1024]{1,0:T(8,128)(2,1)S(1)} %fusion.9), channel_id=1, source_target_pairs={{0,1},{1,0},{2,3},{3,2},{4,5},{5,4},{6,7},{7,6},{8,9},{9,8},{10,11... | collective-permute-start | bytes 884744 | tf_op jit(solution)/shard_map/ppermute | solution.py:422
  161.2 8.7 %collective-permute-start.24 = (bf16[144,1024]{1,0:T(8,128)(2,1)S(1)}, bf16[144,1024]{1,0:T(8,128)(2,1)S(1)}, u32[]{:S(2)}, u32[]{:S(2)}) collective-permute-start(bf16[144,1024]{1,0:T(8,128)(2,1)S(1)} %fusion.2), channel_id=1, source_target_pairs={{0,12},{2,14},{4,0},{6,2},{8,4},{10,6},{12,8},{14,10},{1,13},{3,15... | collective-permute-start | bytes 884744 | tf_op jit(solution)/shard_map/ppermute | solution.py:431
  167.2 11.5 %copy-start.10 = (bf16[144,1024]{1,0:T(8,128)(2,1)}, bf16[144,1024]{1,0:T(8,128)(2,1)S(1)}, u32[]{:S(2)}) copy-start(bf16[144,1024]{1,0:T(8,128)(2,1)S(1)} %collective-permute-done.13.refs_3_) | copy-start | bytes 884740
  167.3 11.5 %collective-permute-start.27 = (bf16[144,1024]{1,0:T(8,128)(2,1)S(1)}, bf16[144,1024]{1,0:T(8,128)(2,1)S(1)}, u32[]{:S(2)}, u32[]{:S(2)}) collective-permute-start(bf16[144,1024]{1,0:T(8,128)(2,1)S(1)} %fusion.1), channel_id=1, source_target_pairs={{0,4},{2,6},{4,8},{6,10},{8,12},{10,14},{12,0},{14,2},{1,5},{3,7},... | collective-permute-start | bytes 884744 | tf_op jit(solution)/shard_map/ppermute | solution.py:431
  169.2 20.1 %copy-start.25 = (s32[128,8]{0,1:T(8,128)S(1)}, s32[128,8]{0,1:T(8,128)}, u32[]{:S(2)}) copy-start(s32[128,8]{0,1:T(8,128)} %param.9) | copy-start | bytes 12292
  169.2 20.7 %copy-start.9 = (bf16[144,1024]{1,0:T(8,128)(2,1)}, bf16[144,1024]{1,0:T(8,128)(2,1)S(1)}, u32[]{:S(2)}) copy-start(bf16[144,1024]{1,0:T(8,128)(2,1)S(1)} %collective-permute-done.11.refs_2_) | copy-start | bytes 884740
  169.2 19.0 %collective-permute-start.14 = (bf16[144,1024]{1,0:T(8,128)(2,1)S(1)}, bf16[144,1024]{1,0:T(8,128)(2,1)S(1)}, u32[]{:S(2)}, u32[]{:S(2)}) collective-permute-start(bf16[144,1024]{1,0:T(8,128)(2,1)S(1)} %fusion.3), channel_id=1, source_target_pairs={{0,8},{2,10},{4,12},{6,14},{8,0},{10,2},{12,4},{14,6},{1,9},{3,11}... | collective-permute-start | bytes 884744 | tf_op jit(solution)/shard_map/ppermute | solution.py:431
  (10 other events, 10.4 us)

commit v6 on v5

--- a/solution.py
+++ b/solution.py
@@ -165,10 +165,10 @@
     )(which, w_gate, w_up, w_down, *after)
 
 
-def rows_kernel(places, modes, capacity, slots, where_ref, *refs):
-    count = len(places)
-    weights_in, units_in, refs = refs[:4], refs[4 : 4 + 4 * count], refs[len(refs) - 19 - 2 * count :]
-    outs, keeps, sends, refs = refs[:4], refs[4 : 4 + count], refs[4 + count : 4 + 2 * count], refs[4 + 2 * count :]
+def rows_kernel(count, modes, capacity, slots, where_ref, *refs):
+    weights_in, x_in, g_in = refs[:4], refs[4 : 4 + 4 * count], refs[4 + 4 * count : 4 + 8 * count]
+    refs = refs[len(refs) - 17 - 2 * count :]
+    outs, keeps, sends, refs = refs[:2], refs[2 : 2 + count], refs[2 + count : 2 + 2 * count], refs[2 + 2 * count :]
     x_all, g_all, tables, wgu0, wgu1, wd0, wd1, xc, gc, both, scaled, piece, unit_sems, weight_sems = refs[:14]
     out_sems = refs[14]
     half, tok = x_all.shape[3], x_all.shape[2] // 2
@@ -177,13 +177,13 @@
     wgu, wd = (wgu0, wgu1), (wd0, wd1)
 
     x_copies, g_copies, t_copies = [], [], []
-    for index, unit in enumerate(units_in):
+    for index, (x_unit, g_unit) in enumerate(zip(x_in, g_in)):
         chunk, y, x = index // 4, index // 2 % 2, index % 2
         rows = pl.ds(y * tok, tok)
-        x_copies.append(pltpu.make_async_copy(unit.at[pl.ds(0, tok)], x_all.at[chunk, x, rows], unit_sems.at[0, index]))
-        g_copies.append(pltpu.make_async_copy(unit.at[pl.ds(tok, tok)], g_all.at[chunk, x, rows], unit_sems.at[1, index]))
+        x_copies.append(pltpu.make_async_copy(x_unit.at[pl.ds(0, tok)], x_all.at[chunk, x, rows], unit_sems.at[0, index]))
+        g_copies.append(pltpu.make_async_copy(g_unit, g_all.at[chunk, x, rows], unit_sems.at[1, index]))
         if x == 0:
-            table = unit.at[pl.ds(2 * tok, owners), pl.ds(0, tok)]
+            table = x_unit.at[pl.ds(tok, owners), pl.ds(0, tok)]
             t_copies.append(pltpu.make_async_copy(table, tables.at[chunk, y], unit_sems.at[2, index]))
     weight_copies = [
         pltpu.make_async_copy(source, target, weight_sems.at[index])
@@ -198,11 +198,9 @@
         copy.start()
         leaving.append(copy)
 
-    def leave_rows(held, target):
+    def leave_rows(held, start):
         for expert in range(2):
-            for chunk, place in enumerate(places):
-                source = held.at[expert, pl.ds(chunk * slots, slots)]
-                leave(source, target.at[expert, pl.ds(place * slots, slots)])
+            leave(held.at[expert], outs[expert].at[:, pl.ds(start, held.shape[2])])
 
     def dot(a, b, dims):
         return lax.dot_general(a, b, (dims, ((), ())), preferred_element_type=jnp.float32)
@@ -246,13 +244,13 @@
                     target[expert, spans[chunk], sides[side]] = rows[expert * slots : (expert + 1) * slots]
 
     gather(x_copies, x_all, xc)
-    leave_rows(xc, outs[0])
+    leave_rows(xc, 0)
     rows = []
     for expert in range(2):
         weight_copies[expert].wait()
         rows.append(dot(xc[expert], wgu[expert][...], ((1,), (0,))))
     gather(g_copies, g_all, gc)
-    leave_rows(gc, outs[1])
+    leave_rows(gc, 2 * half)
     scores = []
     for expert in range(2):
         weight_copies[2 + expert].wait()
@@ -267,8 +265,8 @@
         both[expert, :, :part] = (hgrad * up * sig * (1.0 + gate * (1.0 - sig))).astype(jnp.bfloat16)
         both[expert, :, part:] = (hgrad * act).astype(jnp.bfloat16)
         scaled[expert] = (prob * hidden).astype(jnp.bfloat16)
-    leave_rows(both, outs[2])
-    leave_rows(scaled, outs[3])
+    leave_rows(both, 4 * half)
+    leave_rows(scaled, 4 * half + 2 * part)
 
     names = lax.broadcasted_iota(jnp.int32, (owners, half), 0)
     column = lax.broadcasted_iota(jnp.int32, (owners, half), 1) // (2 * tok)
@@ -300,19 +298,19 @@
         copy.wait()
 
 
-def rows_call(places, modes, steps, owners, capacity, slots, where, weights, units, held):
-    count = len(places)
-    tok, half = (units[0].shape[0] - owners) // 2, units[0].shape[1]
+def rows_call(modes, owners, capacity, slots, where, weights, units, after):
+    count = len(modes)
+    tok, half = units[-1].shape
     part, width = weights[2].shape
     widths = (width, width, 2 * part, part)
     packet = (2, tok + owners, half)
     return pl.pallas_call(
-        functools.partial(rows_kernel, places, modes, capacity, slots),
+        functools.partial(rows_kernel, count, modes, capacity, slots),
         grid_spec=pltpu.PrefetchScalarGridSpec(
             num_scalar_prefetch=1,
             grid=(1,),
-            in_specs=[LOOSE] * (4 + len(units) + len(held)),
-            out_specs=[LOOSE] * (4 + 2 * count),
+            in_specs=[LOOSE] * (4 + len(units) + len(after)),
+            out_specs=[LOOSE] * (2 + 2 * count),
             scratch_shapes=[pltpu.VMEM((count, 2, 2 * tok, half), jnp.bfloat16)] * 2
             + [pltpu.VMEM((count, 2, owners, tok), jnp.bfloat16)]
             + [pltpu.VMEM((width, 2 * part), jnp.bfloat16)] * 2
@@ -322,12 +320,11 @@
                 pltpu.VMEM((count, 2) + packet, jnp.bfloat16),
                 pltpu.SemaphoreType.DMA((3, 4 * count)),
                 pltpu.SemaphoreType.DMA((4,)),
-                pltpu.SemaphoreType.DMA((12 * count,)),
+                pltpu.SemaphoreType.DMA((8 + 4 * count,)),
             ],
         ),
-        out_shape=[jax.ShapeDtypeStruct((2, steps * slots, size), jnp.bfloat16) for size in widths]
+        out_shape=[jax.ShapeDtypeStruct((count * slots, sum(widths)), jnp.bfloat16)] * 2
         + [jax.ShapeDtypeStruct(packet, jnp.bfloat16)] * (2 * count),
-        input_output_aliases={5 + len(units) + i: i for i in range(len(held))},
         compiler_params=pltpu.CompilerParams(vmem_limit_bytes=56 << 20),
         cost_estimate=pl.CostEstimate(
             flops=count * (20 * slots * width * part + 24 * slots * tok * width),
@@ -335,77 +332,97 @@
             transcendentals=2 * count * slots * part,
         ),
         name="rows",
-    )(where, *weights, *units, *held)
-
-
-def grads_kernel(first, tp_ref, x_ref, g_ref, both_ref, scaled_ref, *refs):
-    flipped = refs[-1]
-    part = scaled_ref.shape[2]
-
-    @pl.when(pl.program_id(0) == 0)
+    )(where, *weights, *units, *after)
+
+
+def grads_kernel(count, wide, deep, blocks, tp_ref, *refs):
+    sources, outs = refs[:count], refs[count:-4]
+    wide_all, deep_all, wide_sems, deep_sems = refs[-4:]
+    rows = sources[0].shape[0]
+    size = wide_all.shape[2]
+    block = pl.program_id(0)
+
+    def copies(column):
+        return [
+            pltpu.make_async_copy(
+                source.at[:, pl.ds(wide + column * size, size)],
+                wide_all.at[column, pl.ds(index * rows, rows)],
+                wide_sems.at[column, index],
+            )
+            for index, source in enumerate(sources)
+        ]
+
+    @pl.when(block == 0)
     def _():
-        flipped[...] = scaled_ref[0].T
-
-    both = lax.dot_general(x_ref[0], both_ref[0], (((0,), (0,)), ((), ())), preferred_element_type=jnp.float32)
-    down = jnp.dot(flipped[...], g_ref[0], preferred_element_type=jnp.float32)
-    if first:
-        both_out, down_out = refs[-3:-1]
-        both_out[...] = both.astype(jnp.bfloat16)
-        down_out[...] = down.astype(jnp.bfloat16)
-        return
-    more_both, more_down = refs[:2]
-    dg_ref, du_ref, dd_ref = refs[-4:-1]
-    both = both + more_both[...].astype(jnp.float32)
-    dg_ref[0] = both[:, :part].astype(jnp.bfloat16)
-    du_ref[0] = both[:, part:].astype(jnp.bfloat16)
-    dd_ref[0] = (down + more_down[...].astype(jnp.float32)).astype(jnp.bfloat16)
-
-
-def grads_call(which, expert, x_rows, g_rows, both, scaled, more, after):
-    _, total, width = x_rows.shape
-    part = scaled.shape[2]
+        deep_copies = [
+            pltpu.make_async_copy(
+                source.at[:, pl.ds(deep, deep_all.shape[1])], deep_all.at[pl.ds(index * rows, rows)], deep_sems.at[index]
+            )
+            for index, source in enumerate(sources)
+        ]
+        for copy in deep_copies:
+            copy.start()
+        for column in range(blocks):
+            for copy in copies(column):
+                copy.start()
+        for copy in deep_copies:
+            copy.wait()
+
+    for column in range(blocks):
+
+        @pl.when(block == column)
+        def _(column=column):
+            for copy in copies(column):
+                copy.wait()
+
+    dims = (((0,), (0,)), ((), ()))
+    if len(outs) == 2:
+        part = outs[0].shape[2]
+        both = lax.dot_general(wide_all[block], deep_all[...], dims, preferred_element_type=jnp.float32)
+        outs[0][0] = both[:, :part].astype(jnp.bfloat16)
+        outs[1][0] = both[:, part:].astype(jnp.bfloat16)
+    else:
+        down = lax.dot_general(deep_all[...], wide_all[block], dims, preferred_element_type=jnp.float32)
+        outs[0][0] = down.astype(jnp.bfloat16)
+
+
+def grads_call(which, packed, width, part, down):
+    rows, count = packed[0].shape[0], len(packed)
     step = math.gcd(width // 2, 512)
     per = width // 2 // step
+    deep = part if down else 2 * part
 
     def place(i, w):
         return (i + w[0] * per) % (2 * per)
 
-    moving = pl.BlockSpec((1, total, step), lambda i, w: (expert, 0, i))
-    passing = [
-        pl.BlockSpec((step, 2 * part), lambda i, w: (i, 0)),
-        pl.BlockSpec((part, step), lambda i, w: (0, i)),
-    ]
-    if more:
-        out_specs = [
-            pl.BlockSpec((1, step, part), lambda i, w: (0, place(i, w), 0)),
-            pl.BlockSpec((1, step, part), lambda i, w: (0, place(i, w), 0)),
-            pl.BlockSpec((1, part, step), lambda i, w: (0, 0, place(i, w))),
-        ]
-        shapes = [(1, width, part), (1, width, part), (1, part, width)]
+    if down:
+        specs = [pl.BlockSpec((1, part, step), lambda i, w: (0, 0, place(i, w)))]
+        shapes = [(1, part, width)]
     else:
-        out_specs = passing
-        shapes = [(width, 2 * part), (part, width)]
+        specs = [pl.BlockSpec((1, step, part), lambda i, w: (0, place(i, w), 0))] * 2
+        shapes = [(1, width, part)] * 2
+    starts = (width, 2 * width + 2 * part) if down else (0, 2 * width)
     return pl.pallas_call(
-        functools.partial(grads_kernel, not more),
+        functools.partial(grads_kernel, count, *starts, 2 * per),
         grid_spec=pltpu.PrefetchScalarGridSpec(
             num_scalar_prefetch=1,
-            grid=(width // step,),
-            in_specs=[
-                moving,
-                moving,
-                pl.BlockSpec((1, total, 2 * part), lambda i, w: (expert, 0, 0)),
-                pl.BlockSpec((1, total, part), lambda i, w: (expert, 0, 0)),
-            ]
-            + (passing if more else [])
-            + [LOOSE] * len(after),
-            out_specs=out_specs,
-            scratch_shapes=[pltpu.VMEM((part, total), jnp.bfloat16)],
+            grid=(2 * per,),
+            in_specs=[LOOSE] * count,
+            out_specs=specs,
+            scratch_shapes=[
+                pltpu.VMEM((2 * per, count * rows, step), jnp.bfloat16),
+                pltpu.VMEM((count * rows, deep), jnp.bfloat16),
+                pltpu.SemaphoreType.DMA((2 * per, count)),
+                pltpu.SemaphoreType.DMA((count,)),
+            ],
         ),
         out_shape=[jax.ShapeDtypeStruct(shape, jnp.bfloat16) for shape in shapes],
         compiler_params=pltpu.CompilerParams(vmem_limit_bytes=56 << 20),
-        cost_estimate=pl.CostEstimate(flops=6 * total * width * part, bytes_accessed=6 * total * width, transcendentals=0),
+        cost_estimate=pl.CostEstimate(
+            flops=2 * count * rows * width * deep, bytes_accessed=2 * count * rows * (width + deep), transcendentals=0
+        ),
         name="grads",
-    )(which, x_rows, g_rows, both, scaled, *more, *after)
+    )(which, *packed)
 
 
 def dense_device(tokens, out_grad, routes, probs, w_gate, w_up, w_down):
@@ -433,50 +450,83 @@
     chosen = routes[:, :, None] == jnp.arange(owners, dtype=jnp.int32)
     table = jnp.sum(jnp.where(chosen, probs[:, :, None].astype(jnp.float32) + 1.0, 0.0), axis=1) - 1.0
     table = jnp.pad(table.astype(jnp.bfloat16).T, ((0, 0), (0, half - tok_rows)))
-    units = {(0, 0, 0): jnp.concatenate([tokens, out_grad, table], 0)}
     last = n_z - 1
+    routes_in = []
     for z in range(n_z):
+        shift = -1 if z == last and z > 1 else 1
         if z:
-            back = 0 if z in (1, last) else z - 1
-            shift = -1 if z == last and z > 1 else 1
-            units[z, 0, 0] = over_z(units[back, 0, 0], shift)
-        units[z, 1, 0] = over_y(units[z, 0, 0])
-        units[z, 0, 1] = over_x(units[z, 0, 0])
+            routes_in.append(((z, 0, 0), (0 if z in (1, last) else z - 1, 0, 0), functools.partial(over_z, shift=shift)))
+        routes_in.append(((z, 1, 0), (z, 0, 0), over_y))
+        routes_in.append(((z, 0, 1), (z, 0, 0), over_x))
         if z == 0:
-            units[z, 1, 1] = over_x(units[z, 1, 0])
+            routes_in.append(((z, 1, 1), (z, 1, 0), over_x))
         elif z in (1, last):
-            units[z, 1, 1] = over_z(units[0, 1, 1], shift)
+            routes_in.append(((z, 1, 1), (0, 1, 1), functools.partial(over_z, shift=shift)))
         else:
-            units[z, 1, 1] = over_y(units[z, 0, 1])
+            routes_in.append(((z, 1, 1), (z, 0, 1), over_y))
+    routes_in.sort(key=lambda item: (item[0][0] % 2 if item[2] in (over_x, over_y) else 0, sum(item[0][1:])))
+
+    rounds, waiting, there = [], list(routes_in), {(0, 0, 0)}
+    while waiting:
+        moves = {}
+        for item in waiting:
+            axis = item[2] if item[2] in (over_x, over_y) else over_z
+            if item[1] in there and axis not in moves:
+                moves[axis] = item
+        rounds.append(list(moves.values()))
+        there |= {item[0] for item in rounds[-1]}
+        waiting = [item for item in waiting if item[0] not in there]
+
+    units = {("x", 0, 0, 0): jnp.concatenate([tokens, table], 0), ("g", 0, 0, 0): out_grad}
+    settled, flying = dict(units), {}
+    for moves in rounds:
+        for name in ("x", "g"):
+            arrived = {(name,) + target: move(settled[(name,) + source]) for target, source, move in moves}
+            units.update(arrived)
+            settled.update(flying)
+            names = list(settled)
+            settled = dict(zip(names, lax.optimization_barrier([settled[item] for item in names])))
+            flying = arrived
 
     which_ref = which.reshape(1).astype(jnp.int32)
-    both_w, down_w = weights_call(which_ref, w_gate, w_up, w_down, [units[1, 0, 0], units[0, 1, 0], units[0, 0, 1]])
+    first = [units[("x",) + item[0]] for item in rounds[1]]
+    both_w, down_w = weights_call(which_ref, w_gate, w_up, w_down, first)
     weights = (both_w, over_role(both_w), down_w, over_role(down_w))
     where = jnp.stack([role * ep + place, (1 - role) * ep + place, which]).astype(jnp.int32)
 
     def add(a, b):
         return a.astype(jnp.float32) + b.astype(jnp.float32)
 
-    held, homeward, early, late = (), [], [], []
-    for group in (range(0, n_z, 2), range(1, n_z, 2)):
+    def tied(values, others):
+        return lax.optimization_barrier((list(values), list(others)))[0]
+
+    width, part = both_w.shape[0], down_w.shape[0]
+    packed, flown, homeward, done = [], [], [], []
+    for turn, group in enumerate((range(0, n_z, 2), range(1, n_z, 2))):
         modes = [index % 2 for index in range(len(group))]
-        four = [units[z, y, x] for z in group for y in range(2) for x in range(2)]
-        packets = rows_call(group, modes, n_z, owners, capacity, slots, where, weights, four, held)
-        held, packets = packets[:4], packets[4:]
-        for index, z in enumerate(group):
-            keep, send = packets[index], packets[len(group) + index]
-            go_first, go_second = (over_y, over_x) if modes[index] else (over_x, over_y)
-            recv = go_first(send)
-            recv_next = go_second(add(keep[1], recv[1]).astype(jnp.bfloat16))
-            (late if group[0] else early).append(recv)
-            if not group[0]:
-                late.append(recv_next)
-            total = add(add(keep[0], recv[0]), recv_next)
-            homeward.append(over_z(total.astype(jnp.bfloat16), -z).astype(jnp.float32) if z else total)
-    home = sum(homeward[1:], homeward[0])
+        eight = [units[name, z, y, x] for name in ("x", "g") for z in group for y in range(2) for x in range(2)]
+        mine, other, *packets = rows_call(modes, owners, capacity, slots, where, weights, eight, packed[:1])
+        keeps, sends = packets[: len(group)], packets[len(group) :]
+        if turn:
+            mine, other, *sends = tied([mine, other] + sends, flown[0])
+        packed += [mine, over_role(other)]
+        firsts = [over_y(send) if mode else over_x(send) for mode, send in zip(modes, sends)]
+        if turn:
+            done += grads_call(which_ref, packed, width, part, False)
+            firsts = tied(firsts, flown[1] + done)
+        sends = [add(keep[1], first[1]).astype(jnp.bfloat16) for keep, first in zip(keeps, firsts)]
+        seconds = [over_x(send) if mode else over_y(send) for mode, send in zip(modes, sends)]
+        if turn:
+            done += grads_call(which_ref, packed, width, part, True)
+            seconds = tied(seconds, homeward[1:] + done)
+        totals = [add(add(keep[0], first[0]), second) for keep, first, second in zip(keeps, firsts, seconds)]
+        sends = [total.astype(jnp.bfloat16) for total in totals]
+        thirds = [over_z(send, -z) if z else total for z, send, total in zip(group, sends, totals)]
+        homeward += thirds
+        flown += [firsts, seconds]
+    home = sum(item.astype(jnp.float32) for item in homeward)
     d_tok = home[:tok_rows].astype(jnp.bfloat16)
-    more = grads_call(which_ref, 1, *held, [], early)
-    d_gate, d_up, d_down = grads_call(which_ref, 0, *held, [over_role(item) for item in more], late)
+    d_gate, d_up, d_down = done
     score = jnp.sum(home[tok_rows:, : 4 * tok_rows].reshape(owners, 4, tok_rows), axis=1).T
     d_probs = jnp.sum(jnp.where(chosen, score[:, None, :], 0.0), axis=2)
     return d_tok, d_probs, d_gate, d_up, d_down

time: 201 us -> 196 us (0.975)
  waiting for transfers between devices: 107 us -> 81.1 us
  starting transfers between devices: 30.4 us -> 43.3 us
  other arithmetic: 4.71 us -> 12.9 us
    ppermute x9 -> x14, waiting for transfers between devices: 51.3 us -> 33 us  [over_x(): return lax.ppermute(array, 'tp', [(0, 1), (1, 0)])]
    ppermute x9 -> x14, starting transfers between devices: 7.88 us -> 17.8 us  [over_y(): lax.ppermute(array, 'ep', [(i, i + 1 - 2 * (i % n_y)) for i in range(ep)])]
    ppermute x9 -> x14, starting transfers between devices: 8.86 us -> 17.8 us  [over_x(): return lax.ppermute(array, 'tp', [(0, 1), (1, 0)])]
    convert_element_type x7, other arithmetic: 0.72 us -> 8 us  [the longest x3 4.02 us: dense_device(): sends = [total.astype(jnp.bfloat16) for total in totals]]
    ppermute x8 -> x13, starting transfers between devices: 13.6 us -> 7.41 us  [over_z(): lax.ppermute(array, 'ep', [(i, (i + shift * n_y) % ep) for i in range(ep)])]
    ppermute x8 -> x13, waiting for transfers between devices: 45.9 us -> 41.3 us  [over_z(): lax.ppermute(array, 'ep', [(i, (i + shift * n_y) % ep) for i in range(ep)])]
    ppermute x9 -> x14, waiting for transfers between devices: 9.4 us -> 6.8 us  [over_y(): lax.ppermute(array, 'ep', [(i, i + 1 - 2 * (i % n_y)) for i in range(ep)])]
    unnamed x56 -> x74, local copies, waits for them, and re-layouts: 7.75 us -> 8.5 us
  transfers between devices with their start and end apart: 30 -> 45, of which waited for: 16 -> 26; matrix products, arithmetic and copies ran while one was open for 1% -> 3% of each run, Pallas kernels for 14% -> 22%
where the time goes in v6:
time: 196 us; the launch traced here: 195 us
  waiting for transfers between devices  81.1 us (41%)
  Pallas kernels  47.5 us (24%)
  starting transfers between devices  43.3 us (22%)
  other arithmetic  12.9 us (7%)
  local copies, waits for them, and re-layouts  9.25 us (5%)
    ppermute x13, waiting for transfers between devices, over_z(): lax.ppermute(array, 'ep', [(i, (i + shift * n_y) % ep) for i in range(ep)])  41.3 us
    ppermute x14, waiting for transfers between devices, over_x(): return lax.ppermute(array, 'tp', [(0, 1), (1, 0)])  33 us
    pallas_call x2, Pallas kernels, rows_call(): pl.pallas_call(functools.partial(rows_kernel, count, modes, capacity, slo...  28.2 us
    ppermute x14, starting transfers between devices, over_y(): lax.ppermute(array, 'ep', [(i, i + 1 - 2 * (i % n_y)) for i in range(ep)])  17.8 us
    ppermute x14, starting transfers between devices, over_x(): return lax.ppermute(array, 'tp', [(0, 1), (1, 0)])  17.8 us
    pallas_call x2, Pallas kernels, grads_call(): pl.pallas_call(functools.partial(grads_kernel, count, *starts, 2 * per),...  15.4 us
    unnamed x74, local copies, waits for them, and re-layouts  8.5 us
    ppermute x13, starting transfers between devices, over_z(): lax.ppermute(array, 'ep', [(i, (i + shift * n_y) % ep) for i in range(ep)])  7.41 us
  transfers between devices with their start and end apart: 45, of which 26 were waited for; matrix products, arithmetic and copies ran while one was open for 3% of the time, Pallas kernels for 22%

profile of v6, /device:TPU:0, one launch (start us, length us, event | category | flops | bytes accessed | tf_op | source)
XLA Modules:
  0.0 195.2 jit_solution(13310533114854817425)
XLA Ops:
  3.1 3.0 %collective-permute-start.2 = (bf16[144,1024]{1,0:T(8,128)(2,1)S(1)}, bf16[144,1024]{1,0:T(8,128)(2,1)S(1)}, u32[]{:S(2)}, u32[]{:S(2)}) collective-permute-start(bf16[144,1024]{1,0:T(8,128)(2,1)S(1)} %fusion.7.refs_4_), channel_id=1, source_target_pairs={{0,1},{1,0},{2,3},{3,2},{4,5},{5,4},{6,7},{7,6},{8,9},{9,8},{10,11... | collective-permute-start | bytes 884744 | tf_op jit(solution)/shard_map/ppermute | solution.py:439
  6.1 1.5 collective-permute-start.1
  7.6 1.6 collective-permute-start
  9.2 3.9 %collective-permute-done.2.refs_5_ = bf16[144,1024]{1,0:T(8,128)(2,1)S(1)} collective-permute-done((bf16[144,1024]{1,0:T(8,128)(2,1)S(1)}, bf16[144,1024]{1,0:T(8,128)(2,1)S(1)}, u32[]{:S(2)}, u32[]{:S(2)}) %collective-permute-start.2) | collective-permute-done | bytes 294944 | tf_op jit(solution)/shard_map/ppermute | solution.py:439
  13.1 1.5 collective-permute-done.1.refs_6_
  14.5 3.1 %collective-permute-done.refs_4_ = bf16[144,1024]{1,0:T(8,128)(2,1)S(1)} collective-permute-done((bf16[144,1024]{1,0:T(8,128)(2,1)S(1)}, bf16[144,1024]{1,0:T(8,128)(2,1)S(1)}, u32[]{:S(2)}, u32[]{:S(2)}) %collective-permute-start) | collective-permute-done | bytes 294944 | tf_op jit(solution)/shard_map/ppermute | solution.py:448
  18.7 6.3 %collective-permute-done.4.refs_1_.refs_7_ = bf16[144,1024]{1,0:T(8,128)(2,1)S(1)} collective-permute-done((bf16[144,1024]{1,0:T(8,128)(2,1)S(1)}, bf16[144,1024]{1,0:T(8,128)(2,1)S(1)}, u32[]{:S(2)}, u32[]{:S(2)}) %collective-permute-start.4) | collective-permute-done | bytes 294944 | tf_op jit(solution)/shard_map/ppermute | solution.py:439
  25.2 2.3 %collective-permute-done.3.refs_0_.refs_8_ = bf16[144,1024]{1,0:T(8,128)(2,1)S(1)} collective-permute-done((bf16[144,1024]{1,0:T(8,128)(2,1)S(1)}, bf16[144,1024]{1,0:T(8,128)(2,1)S(1)}, u32[]{:S(2)}, u32[]{:S(2)}) %collective-permute-start.3) | collective-permute-done | bytes 294944 | tf_op jit(solution)/shard_map/ppermute | solution.py:448
  28.2 4.0 %weights.1 = (bf16[2048,768]{1,0:T(8,128)(2,1)}, bf16[384,2048]{1,0:T(8,128)(2,1)}) custom-call(s32[1]{0:T(128)} %bitcast.2.tp_ref, bf16[1,2048,384]{2,1,0:T(8,128)(2,1)} %wg_ref.1, bf16[1,2048,384]{2,1,0:T(8,128)(2,1)} %wu_ref.1, bf16[1,384,2048]{2,1,0:T(8,128)(2,1)} %wd_ref.1, bf16[144,1024]{1,0:T(8,128)(2,1)} %copy-done.9, bf16[144,1024]{1,0:T(8,128)(2,1)} %copy-done.8, ...), custom_call_target="tpu_custom_call" | custom-call | bytes 9437184 | tf_op jit(solution)/shard_map/weights/pallas_call | solution.py:142
  32.2 1.3 collective-permute-start.10
  33.5 1.5 collective-permute-start.9
  35.0 5.9 %collective-permute-done.10.refs_13_ = bf16[128,1024]{1,0:T(8,128)(2,1)S(1)} collective-permute-done((bf16[128,1024]{1,0:T(8,128)(2,1)S(1)}, bf16[128,1024]{1,0:T(8,128)(2,1)S(1)}, u32[]{:S(2)}, u32[]{:S(2)}) %collective-permute-start.10) | collective-permute-done | bytes 262176 | tf_op jit(solution)/shard_map/ppermute | solution.py:439
  41.9 3.0 %collective-permute-done.8.refs_12_ = bf16[128,1024]{1,0:T(8,128)(2,1)S(1)} collective-permute-done((bf16[128,1024]{1,0:T(8,128)(2,1)S(1)}, bf16[128,1024]{1,0:T(8,128)(2,1)S(1)}, u32[]{:S(2)}, u32[]{:S(2)}) %collective-permute-start.8) | collective-permute-done | bytes 262176 | tf_op jit(solution)/shard_map/ppermute | solution.py:448
  46.2 6.0 %collective-permute-done.14.refs_15_ = bf16[128,1024]{1,0:T(8,128)(2,1)} collective-permute-done((bf16[128,1024]{1,0:T(8,128)(2,1)S(1)}, bf16[128,1024]{1,0:T(8,128)(2,1)}, u32[]{:S(2)}, u32[]{:S(2)}) %collective-permute-start.14) | collective-permute-done | bytes 262176 | tf_op jit(solution)/shard_map/ppermute | solution.py:439
  53.1 4.1 %collective-permute-done.13.refs_16_ = bf16[128,1024]{1,0:T(8,128)(2,1)S(1)} collective-permute-done((bf16[128,1024]{1,0:T(8,128)(2,1)S(1)}, bf16[128,1024]{1,0:T(8,128)(2,1)S(1)}, u32[]{:S(2)}, u32[]{:S(2)}) %collective-permute-start.13) | collective-permute-done | bytes 262176 | tf_op jit(solution)/shard_map/ppermute | solution.py:448
  57.2 1.3 collective-permute-start.11
  58.5 3.0 %collective-permute-done.16.refs_8_ = bf16[144,1024]{1,0:T(8,128)(2,1)} collective-permute-done((bf16[144,1024]{1,0:T(8,128)(2,1)S(1)}, bf16[144,1024]{1,0:T(8,128)(2,1)}, u32[]{:S(2)}, u32[]{:S(2)}) %collective-permute-start.16) | collective-permute-done | bytes 294944 | tf_op jit(solution)/shard_map/ppermute | solution.py:448
  61.5 1.1 collective-permute-start.19
  62.7 2.0 %collective-permute-done.11.refs_9_ = bf16[144,1024]{1,0:T(8,128)(2,1)S(1)} collective-permute-done((bf16[144,1024]{1,0:T(8,128)(2,1)}, bf16[144,1024]{1,0:T(8,128)(2,1)S(1)}, u32[]{:S(2)}, u32[]{:S(2)}) %collective-permute-start.11) | collective-permute-done | bytes 294944 | tf_op jit(solution)/shard_map/ppermute | solution.py:439
  65.4 3.1 %collective-permute-done.20.refs_16_ = bf16[128,1024]{1,0:T(8,128)(2,1)S(1)} collective-permute-done((bf16[128,1024]{1,0:T(8,128)(2,1)}, bf16[128,1024]{1,0:T(8,128)(2,1)S(1)}, u32[]{:S(2)}, u32[]{:S(2)}) %collective-permute-start.20) | collective-permute-done | bytes 262176 | tf_op jit(solution)/shard_map/ppermute | solution.py:448
  69.6 1.9 collective-permute-start.27
  72.8 3.1 %collective-permute-done.17.refs_11_ = bf16[144,1024]{1,0:T(8,128)(2,1)S(1)} collective-permute-done((bf16[144,1024]{1,0:T(8,128)(2,1)S(1)}, bf16[144,1024]{1,0:T(8,128)(2,1)S(1)}, u32[]{:S(2)}, u32[]{:S(2)}) %collective-permute-start.17) | collective-permute-done | bytes 294944 | tf_op jit(solution)/shard_map/ppermute | solution.py:445
  78.1 1.2 collective-permute-start.32
  79.3 1.4 collective-permute-done.28.refs_7_
  82.3 2.2 %collective-permute-done.32.refs_13_ = bf16[128,1024]{1,0:T(8,128)(2,1)S(1)} collective-permute-done((bf16[128,1024]{1,0:T(8,128)(2,1)S(1)}, bf16[128,1024]{1,0:T(8,128)(2,1)S(1)}, u32[]{:S(2)}, u32[]{:S(2)}) %collective-permute-start.32) | collective-permute-done | bytes 262176 | tf_op jit(solution)/shard_map/ppermute | solution.py:439
  84.5 6.3 %collective-permute-done.33.refs_15_ = bf16[128,1024]{1,0:T(8,128)(2,1)S(1)} collective-permute-done((bf16[128,1024]{1,0:T(8,128)(2,1)}, bf16[128,1024]{1,0:T(8,128)(2,1)S(1)}, u32[]{:S(2)}, u32[]{:S(2)}) %collective-permute-start.33) | collective-permute-done | bytes 262176 | tf_op jit(solution)/shard_map/ppermute | solution.py:448
  92.2 3.1 %collective-permute-start.35 = (bf16[128,1024]{1,0:T(8,128)(2,1)}, bf16[128,1024]{1,0:T(8,128)(2,1)S(1)}, u32[]{:S(2)}, u32[]{:S(2)}) collective-permute-start(bf16[128,1024]{1,0:T(8,128)(2,1)} %copy-done.28), channel_id=1, source_target_pairs={{0,2},{2,0},{4,6},{6,4},{8,10},{10,8},{12,14},{14,12},{1,3},{3,1},... | collective-permute-start | bytes 786440 | tf_op jit(solution)/shard_map/ppermute | solution.py:445
  95.3 1.9 collective-permute-start.34
  97.2 3.6 %collective-permute-done.36.refs_19_ = bf16[128,1024]{1,0:T(8,128)(2,1)} collective-permute-done((bf16[128,1024]{1,0:T(8,128)(2,1)}, bf16[128,1024]{1,0:T(8,128)(2,1)}, u32[]{:S(2)}, u32[]{:S(2)}) %collective-permute-start.36) | collective-permute-done | bytes 262176 | tf_op jit(solution)/shard_map/ppermute | solution.py:448
  100.7 2.0 %collective-permute-start.31 = (bf16[144,1024]{1,0:T(8,128)(2,1)}, bf16[144,1024]{1,0:T(8,128)(2,1)S(1)}, u32[]{:S(2)}, u32[]{:S(2)}) collective-permute-start(bf16[144,1024]{1,0:T(8,128)(2,1)} %copy-done.8), channel_id=1, source_target_pairs={{0,12},{2,14},{4,0},{6,2},{8,4},{10,6},{12,8},{14,10},{1,13},{3,15... | collective-permute-start | bytes 884744 | tf_op jit(solution)/shard_map/ppermute | solution.py:448
  102.7 3.2 %collective-permute-start.30 = (bf16[144,1024]{1,0:T(8,128)(2,1)}, bf16[144,1024]{1,0:T(8,128)(2,1)S(1)}, u32[]{:S(2)}, u32[]{:S(2)}) collective-permute-start(bf16[144,1024]{1,0:T(8,128)(2,1)} %collective-permute-done.16.refs_8_), channel_id=1, source_target_pairs={{0,2},{2,0},{4,6},{6,4},{8,10},{10,8},{12,14},{14,12},{1,3},{3,1},... | collective-permute-start | bytes 884744 | tf_op jit(solution)/shard_map/ppermute | solution.py:445
  107.0 13.9 %rows.2 = (bf16[288,5248]{1,0:T(8,128)(2,1)}, bf16[288,5248]{1,0:T(8,128)(2,1)}, bf16[2,144,1024]{2,1,0:T(8,128)(2,1)}, bf16[2,144,1024]{2,1,0:T(8,128)(2,1)}, b...) custom-call(s32[3]{0:T(128)} %pad_add_fusion.where_ref, bf16[2048,768]{1,0:T(8,128)(2,1)} %get-tuple-element.74.refs_0_, ...), custom_call_target="tpu_custom_call" | custom-call | flops 6341787648 | bytes 17825792 | tf_op jit(solution)/shard_map/rows/pallas_call | solution.py:307
  124.4 14.2 %rows.3 = (bf16[288,5248]{1,0:T(8,128)(2,1)}, bf16[288,5248]{1,0:T(8,128)(2,1)}, bf16[2,144,1024]{2,1,0:T(8,128)(2,1)}, bf16[2,144,1024]{2,1,0:T(8,128)(2,1)}, b...) custom-call(s32[3]{0:T(128)} %pad_add_fusion.where_ref, bf16[2048,768]{1,0:T(8,128)(2,1)} %get-tuple-element.74.refs_0_, ...), custom_call_target="tpu_custom_call" | custom-call | flops 6341787648 | bytes 17825792 | tf_op jit(solution)/shard_map/rows/pallas_call | solution.py:307
  142.7 1.4 collective-permute-start.23
  145.1 5.7 %collective-permute-done.25 = bf16[144,1024]{1,0:T(8,128)(2,1)S(1)} collective-permute-done((bf16[144,1024]{1,0:T(8,128)(2,1)S(1)}, bf16[144,1024]{1,0:T(8,128)(2,1)S(1)}, u32[]{:S(2)}, u32[]{:S(2)}) %collective-permute-start.25) | collective-permute-done | bytes 294944 | tf_op jit(solution)/shard_map/ppermute | solution.py:439
  150.8 1.4 collective-permute-start.38
  152.1 1.8 fusion.2
  154.1 1.6 copy-done
  155.7 1.6 copy-done.1
  157.2 9.0 %grads.2 = (bf16[1,2048,384]{2,1,0:T(8,128)(2,1)}, bf16[1,2048,384]{2,1,0:T(8,128)(2,1)}) custom-call(s32[1]{0:T(128)} %bitcast.2.tp_ref, bf16[288,5248]{1,0:T(8,128)(2,1)} %get-tuple-element.117.refs_20_.refs_0_, bf16[288,5248]{1,0:T(8,128)(2,1)} %copy-done, bf16[288,5248]{1,0:T(8,128)(2,1)} %get-tuple-element.126.refs_2_, bf16[288,5248]{1,0:T(8,128)(2,1)} %copy-done.1), custom_call_target="tpu_custom_call" | custom-call | flops 3623878656 | bytes 6488064 | tf_op jit(solution)/shard_map/grads/pallas_call | solution.py:405
  166.3 1.1 fusion.11
  170.3 6.4 %grads.3 = bf16[1,384,2048]{2,1,0:T(8,128)(2,1)} custom-call(s32[1]{0:T(128)} %bitcast.2.tp_ref, bf16[288,5248]{1,0:T(8,128)(2,1)} %get-tuple-element.117.refs_20_.refs_0_, bf16[288,5248]{1,0:T(8,128)(2,1)} %copy-done, bf16[288,5248]{1,0:T(8,128)(2,1)} %get-tuple-element.126.refs_2_, bf16[288,5248]{1,0:T(8,128)(2,1)} %copy-done.1), custom_call_target="tpu_custom_call" | custom-call | flops 1811939328 | bytes 5603328 | tf_op jit(solution)/shard_map/grads/pallas_call | solution.py:405
  176.8 1.1 fusion
  177.9 1.1 fusion.1
  179.0 1.9 collective-permute-start.43
  181.0 7.9 %collective-permute-done.43 = bf16[144,1024]{1,0:T(8,128)(2,1)S(1)} collective-permute-done((bf16[144,1024]{1,0:T(8,128)(2,1)S(1)}, bf16[144,1024]{1,0:T(8,128)(2,1)S(1)}, u32[]{:S(2)}, u32[]{:S(2)}) %collective-permute-start.43) | collective-permute-done | bytes 294944 | tf_op jit(solution)/shard_map/ppermute | solution.py:448
  188.9 3.6 %collective-permute-done.44 = bf16[144,1024]{1,0:T(8,128)(2,1)S(1)} collective-permute-done((bf16[144,1024]{1,0:T(8,128)(2,1)S(1)}, bf16[144,1024]{1,0:T(8,128)(2,1)S(1)}, u32[]{:S(2)}, u32[]{:S(2)}) %collective-permute-start.44) | collective-permute-done | bytes 294944 | tf_op jit(solution)/shard_map/ppermute | solution.py:448
  192.5 1.2 fusion.5
  (139 shorter events, 29.9 us)
Async XLA Ops:
  3.1 103.9 %copy-start.10 = (bf16[144,1024]{1,0:T(8,128)(2,1)}, bf16[144,1024]{1,0:T(8,128)(2,1)S(1)}, u32[]{:S(2)}) copy-start(bf16[144,1024]{1,0:T(8,128)(2,1)S(1)} %fusion.7.refs_4_) | copy-start | bytes 884740
  3.1 10.0 %collective-permute-start.2 = (bf16[144,1024]{1,0:T(8,128)(2,1)S(1)}, bf16[144,1024]{1,0:T(8,128)(2,1)S(1)}, u32[]{:S(2)}, u32[]{:S(2)}) collective-permute-start(bf16[144,1024]{1,0:T(8,128)(2,1)S(1)} %fusion.7.refs_4_), channel_id=1, source_target_pairs={{0,1},{1,0},{2,3},{3,2},{4,5},{5,4},{6,7},{7,6},{8,9},{9,8},{10,11... | collective-permute-start | bytes 884744 | tf_op jit(solution)/shard_map/ppermute | solution.py:439
  6.1 8.5 %collective-permute-start.1 = (bf16[144,1024]{1,0:T(8,128)(2,1)S(1)}, bf16[144,1024]{1,0:T(8,128)(2,1)S(1)}, u32[]{:S(2)}, u32[]{:S(2)}) collective-permute-start(bf16[144,1024]{1,0:T(8,128)(2,1)S(1)} %fusion.7.refs_4_), channel_id=1, source_target_pairs={{0,2},{2,0},{4,6},{6,4},{8,10},{10,8},{12,14},{14,12},{1,3},{3,1},... | collective-permute-start | bytes 884744 | tf_op jit(solution)/shard_map/ppermute | solution.py:445
  7.6 10.0 %collective-permute-start = (bf16[144,1024]{1,0:T(8,128)(2,1)S(1)}, bf16[144,1024]{1,0:T(8,128)(2,1)S(1)}, u32[]{:S(2)}, u32[]{:S(2)}) collective-permute-start(bf16[144,1024]{1,0:T(8,128)(2,1)S(1)} %fusion.7.refs_4_), channel_id=1, source_target_pairs={{0,4},{2,6},{4,8},{6,10},{8,12},{10,14},{12,0},{14,2},{1,5},{3,7},... | collective-permute-start | bytes 884744 | tf_op jit(solution)/shard_map/ppermute | solution.py:448
  13.1 93.8 %copy-start.14 = (bf16[144,1024]{1,0:T(8,128)(2,1)}, bf16[144,1024]{1,0:T(8,128)(2,1)S(1)}, u32[]{:S(2)}) copy-start(bf16[144,1024]{1,0:T(8,128)(2,1)S(1)} %collective-permute-done.2.refs_5_) | copy-start | bytes 884740
  17.6 103.3 %copy-start.13 = (bf16[144,1024]{1,0:T(8,128)(2,1)}, bf16[144,1024]{1,0:T(8,128)(2,1)S(1)}, u32[]{:S(2)}) copy-start(bf16[144,1024]{1,0:T(8,128)(2,1)S(1)} %collective-permute-done.refs_4_) | copy-start | bytes 884740
  17.6 7.3 %collective-permute-start.4 = (bf16[144,1024]{1,0:T(8,128)(2,1)S(1)}, bf16[144,1024]{1,0:T(8,128)(2,1)S(1)}, u32[]{:S(2)}, u32[]{:S(2)}) collective-permute-start(bf16[144,1024]{1,0:T(8,128)(2,1)S(1)} %collective-permute-done.1.refs_6_), channel_id=1, source_target_pairs={{0,1},{1,0},{2,3},{3,2},{4,5},{5,4},{6,7},{7,6},{8,9},{9,8},{10,11... | collective-permute-start | bytes 884744 | tf_op jit(solution)/shard_map/ppermute | solution.py:439
  18.2 7.0 %collective-permute-start.5 = (bf16[144,1024]{1,0:T(8,128)(2,1)S(1)}, bf16[144,1024]{1,0:T(8,128)(2,1)S(1)}, u32[]{:S(2)}, u32[]{:S(2)}) collective-permute-start(bf16[144,1024]{1,0:T(8,128)(2,1)S(1)} %collective-permute-done.refs_4_), channel_id=1, source_target_pairs={{0,2},{2,0},{4,6},{6,4},{8,10},{10,8},{12,14},{14,12},{1,3},{3,1},... | collective-permute-start | bytes 884744 | tf_op jit(solution)/shard_map/ppermute | solution.py:445
  18.7 8.8 %collective-permute-start.3 = (bf16[144,1024]{1,0:T(8,128)(2,1)S(1)}, bf16[144,1024]{1,0:T(8,128)(2,1)S(1)}, u32[]{:S(2)}, u32[]{:S(2)}) collective-permute-start(bf16[144,1024]{1,0:T(8,128)(2,1)S(1)} %collective-permute-done.refs_4_), channel_id=1, source_target_pairs={{0,4},{2,6},{4,8},{6,10},{8,12},{10,14},{12,0},{14,2},{1,5},{3,7},... | collective-permute-start | bytes 884744 | tf_op jit(solution)/shard_map/ppermute | solution.py:448
  32.2 73.7 %collective-permute-start.6 = (bf16[2048,768]{1,0:T(8,128)(2,1)}, bf16[2048,768]{1,0:T(8,128)(2,1)}, u32[]{:S(2)}, u32[]{:S(2)}) collective-permute-start(bf16[2048,768]{1,0:T(8,128)(2,1)} %get-tuple-element.74.refs_0_), channel_id=1, source_target_pairs={{0,16},{16,0},{1,17},{17,1},{2,18},{18,2},{3,19},{19,3},{4,20},{20... | collective-permute-start | bytes 9437192 | tf_op jit(solution)/shard_map/ppermute | solution.py:442
  32.2 8.7 %collective-permute-start.10 = (bf16[128,1024]{1,0:T(8,128)(2,1)S(1)}, bf16[128,1024]{1,0:T(8,128)(2,1)S(1)}, u32[]{:S(2)}, u32[]{:S(2)}) collective-permute-start(bf16[128,1024]{1,0:T(8,128)(2,1)S(1)} %copy-done.23), channel_id=1, source_target_pairs={{0,1},{1,0},{2,3},{3,2},{4,5},{5,4},{6,7},{7,6},{8,9},{9,8},{10,11... | collective-permute-start | bytes 786440 | tf_op jit(solution)/shard_map/ppermute | solution.py:439
  33.5 8.4 %collective-permute-start.9 = (bf16[128,1024]{1,0:T(8,128)(2,1)S(1)}, bf16[128,1024]{1,0:T(8,128)(2,1)S(1)}, u32[]{:S(2)}, u32[]{:S(2)}) collective-permute-start(bf16[128,1024]{1,0:T(8,128)(2,1)S(1)} %copy-done.23), channel_id=1, source_target_pairs={{0,2},{2,0},{4,6},{6,4},{8,10},{10,8},{12,14},{14,12},{1,3},{3,1},... | collective-permute-start | bytes 786440 | tf_op jit(solution)/shard_map/ppermute | solution.py:445
  35.0 9.9 %collective-permute-start.8 = (bf16[128,1024]{1,0:T(8,128)(2,1)S(1)}, bf16[128,1024]{1,0:T(8,128)(2,1)S(1)}, u32[]{:S(2)}, u32[]{:S(2)}) collective-permute-start(bf16[128,1024]{1,0:T(8,128)(2,1)S(1)} %copy-done.23), channel_id=1, source_target_pairs={{0,4},{2,6},{4,8},{6,10},{8,12},{10,14},{12,0},{14,2},{1,5},{3,7},... | collective-permute-start | bytes 786440 | tf_op jit(solution)/shard_map/ppermute | solution.py:448
  44.9 7.3 %collective-permute-start.14 = (bf16[128,1024]{1,0:T(8,128)(2,1)S(1)}, bf16[128,1024]{1,0:T(8,128)(2,1)}, u32[]{:S(2)}, u32[]{:S(2)}) collective-permute-start(bf16[128,1024]{1,0:T(8,128)(2,1)S(1)} %collective-permute-done.9.refs_14_), channel_id=1, source_target_pairs={{0,1},{1,0},{2,3},{3,2},{4,5},{5,4},{6,7},{7,6},{8,9},{9,8},{10,11... | collective-permute-start | bytes 786440 | tf_op jit(solution)/shard_map/ppermute | solution.py:439
  45.5 6.9 %collective-permute-start.15 = (bf16[128,1024]{1,0:T(8,128)(2,1)S(1)}, bf16[128,1024]{1,0:T(8,128)(2,1)S(1)}, u32[]{:S(2)}, u32[]{:S(2)}) collective-permute-start(bf16[128,1024]{1,0:T(8,128)(2,1)S(1)} %collective-permute-done.8.refs_12_), channel_id=1, source_target_pairs={{0,2},{2,0},{4,6},{6,4},{8,10},{10,8},{12,14},{14,12},{1,3},{3,1},... | collective-permute-start | bytes 786440 | tf_op jit(solution)/shard_map/ppermute | solution.py:445
  46.2 11.0 %collective-permute-start.13 = (bf16[128,1024]{1,0:T(8,128)(2,1)S(1)}, bf16[128,1024]{1,0:T(8,128)(2,1)S(1)}, u32[]{:S(2)}, u32[]{:S(2)}) collective-permute-start(bf16[128,1024]{1,0:T(8,128)(2,1)S(1)} %collective-permute-done.8.refs_12_), channel_id=1, source_target_pairs={{0,4},{2,6},{4,8},{6,10},{8,12},{10,14},{12,0},{14,2},{1,5},{3,7},... | collective-permute-start | bytes 786440 | tf_op jit(solution)/shard_map/ppermute | solution.py:448
  46.2 56.5 %collective-permute-start.7 = (bf16[384,2048]{1,0:T(8,128)(2,1)}, bf16[384,2048]{1,0:T(8,128)(2,1)S(1)}, u32[]{:S(2)}, u32[]{:S(2)}) collective-permute-start(bf16[384,2048]{1,0:T(8,128)(2,1)} %get-tuple-element.75.refs_2_), channel_id=1, source_target_pairs={{0,16},{16,0},{1,17},{17,1},{2,18},{18,2},{3,19},{19,3},{4,20},{20... | collective-permute-start | bytes 4718600 | tf_op jit(solution)/shard_map/ppermute | solution.py:442
  52.3 9.3 %collective-permute-start.16 = (bf16[144,1024]{1,0:T(8,128)(2,1)S(1)}, bf16[144,1024]{1,0:T(8,128)(2,1)}, u32[]{:S(2)}, u32[]{:S(2)}) collective-permute-start(bf16[144,1024]{1,0:T(8,128)(2,1)S(1)} %fusion.7.refs_4_), channel_id=1, source_target_pairs={{0,12},{2,14},{4,0},{6,2},{8,4},{10,6},{12,8},{14,10},{1,13},{3,15... | collective-permute-start | bytes 884744 | tf_op jit(solution)/shard_map/ppermute | solution.py:448
  52.4 9.1 %collective-permute-start.12 = (bf16[144,1024]{1,0:T(8,128)(2,1)}, bf16[144,1024]{1,0:T(8,128)(2,1)S(1)}, u32[]{:S(2)}, u32[]{:S(2)}) collective-permute-start(bf16[144,1024]{1,0:T(8,128)(2,1)} %copy-done.9), channel_id=1, source_target_pairs={{0,2},{2,0},{4,6},{6,4},{8,10},{10,8},{12,14},{14,12},{1,3},{3,1},... | collective-permute-start | bytes 884744 | tf_op jit(solution)/shard_map/ppermute | solution.py:445
  57.2 7.4 %collective-permute-start.11 = (bf16[144,1024]{1,0:T(8,128)(2,1)}, bf16[144,1024]{1,0:T(8,128)(2,1)S(1)}, u32[]{:S(2)}, u32[]{:S(2)}) collective-permute-start(bf16[144,1024]{1,0:T(8,128)(2,1)} %copy-done.9), channel_id=1, source_target_pairs={{0,1},{1,0},{2,3},{3,2},{4,5},{5,4},{6,7},{7,6},{8,9},{9,8},{10,11... | collective-permute-start | bytes 884744 | tf_op jit(solution)/shard_map/ppermute | solution.py:439
  61.5 7.0 %collective-permute-start.20 = (bf16[128,1024]{1,0:T(8,128)(2,1)}, bf16[128,1024]{1,0:T(8,128)(2,1)S(1)}, u32[]{:S(2)}, u32[]{:S(2)}) collective-permute-start(bf16[128,1024]{1,0:T(8,128)(2,1)} %refs_12_.1), channel_id=1, source_target_pairs={{0,12},{2,14},{4,0},{6,2},{8,4},{10,6},{12,8},{14,10},{1,13},{3,15... | collective-permute-start | bytes 786440 | tf_op jit(solution)/shard_map/ppermute | solution.py:448
  61.5 8.0 %collective-permute-start.19 = (bf16[128,1024]{1,0:T(8,128)(2,1)S(1)}, bf16[128,1024]{1,0:T(8,128)(2,1)S(1)}, u32[]{:S(2)}, u32[]{:S(2)}) collective-permute-start(bf16[128,1024]{1,0:T(8,128)(2,1)S(1)} %collective-permute-done.13.refs_16_), channel_id=1, source_target_pairs={{0,2},{2,0},{4,6},{6,4},{8,10},{10,8},{12,14},{14,12},{1,3},{3,1},... | collective-permute-start | bytes 786440 | tf_op jit(solution)/shard_map/ppermute | solution.py:445
  64.7 7.2 %collective-permute-start.18 = (bf16[128,1024]{1,0:T(8,128)(2,1)S(1)}, bf16[128,1024]{1,0:T(8,128)(2,1)S(1)}, u32[]{:S(2)}, u32[]{:S(2)}) collective-permute-start(bf16[128,1024]{1,0:T(8,128)(2,1)S(1)} %collective-permute-done.13.refs_16_), channel_id=1, source_target_pairs={{0,1},{1,0},{2,3},{3,2},{4,5},{5,4},{6,7},{7,6},{8,9},{9,8},{10,11... | collective-permute-start | bytes 786440 | tf_op jit(solution)/shard_map/ppermute | solution.py:439
  68.5 7.4 %collective-permute-start.17 = (bf16[144,1024]{1,0:T(8,128)(2,1)S(1)}, bf16[144,1024]{1,0:T(8,128)(2,1)S(1)}, u32[]{:S(2)}, u32[]{:S(2)}) collective-permute-start(bf16[144,1024]{1,0:T(8,128)(2,1)S(1)} %collective-permute-done.11.refs_9_), channel_id=1, source_target_pairs={{0,2},{2,0},{4,6},{6,4},{8,10},{10,8},{12,14},{14,12},{1,3},{3,1},... | collective-permute-start | bytes 884744 | tf_op jit(solution)/shard_map/ppermute | solution.py:445
  69.6 7.8 %collective-permute-start.27 = (bf16[144,1024]{1,0:T(8,128)(2,1)S(1)}, bf16[144,1024]{1,0:T(8,128)(2,1)S(1)}, u32[]{:S(2)}, u32[]{:S(2)}) collective-permute-start(bf16[144,1024]{1,0:T(8,128)(2,1)S(1)} %collective-permute-done.refs_4_), channel_id=1, source_target_pairs={{0,1},{1,0},{2,3},{3,2},{4,5},{5,4},{6,7},{7,6},{8,9},{9,8},{10,11... | collective-permute-start | bytes 884744 | tf_op jit(solution)/shard_map/ppermute | solution.py:439
  71.9 8.8 %collective-permute-start.28 = (bf16[144,1024]{1,0:T(8,128)(2,1)}, bf16[144,1024]{1,0:T(8,128)(2,1)}, u32[]{:S(2)}, u32[]{:S(2)}) collective-permute-start(bf16[144,1024]{1,0:T(8,128)(2,1)} %copy-done.8), channel_id=1, source_target_pairs={{0,4},{2,6},{4,8},{6,10},{8,12},{10,14},{12,0},{14,2},{1,5},{3,7},... | collective-permute-start | bytes 884744 | tf_op jit(solution)/shard_map/ppermute | solution.py:448
  75.9 6.4 %collective-permute-start.21 = (bf16[128,1024]{1,0:T(8,128)(2,1)S(1)}, bf16[128,1024]{1,0:T(8,128)(2,1)S(1)}, u32[]{:S(2)}, u32[]{:S(2)}) collective-permute-start(bf16[128,1024]{1,0:T(8,128)(2,1)S(1)} %collective-permute-done.18.refs_17_), channel_id=1, source_target_pairs={{0,2},{2,0},{4,6},{6,4},{8,10},{10,8},{12,14},{14,12},{1,3},{3,1},... | collective-permute-start | bytes 786440 | tf_op jit(solution)/shard_map/ppermute | solution.py:445
  78.1 6.4 %collective-permute-start.32 = (bf16[128,1024]{1,0:T(8,128)(2,1)S(1)}, bf16[128,1024]{1,0:T(8,128)(2,1)S(1)}, u32[]{:S(2)}, u32[]{:S(2)}) collective-permute-start(bf16[128,1024]{1,0:T(8,128)(2,1)S(1)} %collective-permute-done.8.refs_12_), channel_id=1, source_target_pairs={{0,1},{1,0},{2,3},{3,2},{4,5},{5,4},{6,7},{7,6},{8,9},{9,8},{10,11... | collective-permute-start | bytes 786440 | tf_op jit(solution)/shard_map/ppermute | solution.py:439
  80.7 10.1 %collective-permute-start.33 = (bf16[128,1024]{1,0:T(8,128)(2,1)}, bf16[128,1024]{1,0:T(8,128)(2,1)S(1)}, u32[]{:S(2)}, u32[]{:S(2)}) collective-permute-start(bf16[128,1024]{1,0:T(8,128)(2,1)} %collective-permute-done.14.refs_15_), channel_id=1, source_target_pairs={{0,4},{2,6},{4,8},{6,10},{8,12},{10,14},{12,0},{14,2},{1,5},{3,7},... | collective-permute-start | bytes 786440 | tf_op jit(solution)/shard_map/ppermute | solution.py:448
  91.5 9.2 %collective-permute-start.36 = (bf16[128,1024]{1,0:T(8,128)(2,1)}, bf16[128,1024]{1,0:T(8,128)(2,1)}, u32[]{:S(2)}, u32[]{:S(2)}) collective-permute-start(bf16[128,1024]{1,0:T(8,128)(2,1)} %collective-permute-done.14.refs_15_), channel_id=1, source_target_pairs={{0,12},{2,14},{4,0},{6,2},{8,4},{10,6},{12,8},{14,10},{1,13},{3,15... | collective-permute-start | bytes 786440 | tf_op jit(solution)/shard_map/ppermute | solution.py:448
  92.2 28.7 %collective-permute-start.35 = (bf16[128,1024]{1,0:T(8,128)(2,1)}, bf16[128,1024]{1,0:T(8,128)(2,1)S(1)}, u32[]{:S(2)}, u32[]{:S(2)}) collective-permute-start(bf16[128,1024]{1,0:T(8,128)(2,1)} %copy-done.28), channel_id=1, source_target_pairs={{0,2},{2,0},{4,6},{6,4},{8,10},{10,8},{12,14},{14,12},{1,3},{3,1},... | collective-permute-start | bytes 786440 | tf_op jit(solution)/shard_map/ppermute | solution.py:445
  95.3 26.7 %collective-permute-start.34 = (bf16[128,1024]{1,0:T(8,128)(2,1)}, bf16[128,1024]{1,0:T(8,128)(2,1)S(1)}, u32[]{:S(2)}, u32[]{:S(2)}) collective-permute-start(bf16[128,1024]{1,0:T(8,128)(2,1)} %copy-done.28), channel_id=1, source_target_pairs={{0,1},{1,0},{2,3},{3,2},{4,5},{5,4},{6,7},{7,6},{8,9},{9,8},{10,11... | collective-permute-start | bytes 786440 | tf_op jit(solution)/shard_map/ppermute | solution.py:439
  100.7 21.4 %collective-permute-start.31 = (bf16[144,1024]{1,0:T(8,128)(2,1)}, bf16[144,1024]{1,0:T(8,128)(2,1)S(1)}, u32[]{:S(2)}, u32[]{:S(2)}) collective-permute-start(bf16[144,1024]{1,0:T(8,128)(2,1)} %copy-done.8), channel_id=1, source_target_pairs={{0,12},{2,14},{4,0},{6,2},{8,4},{10,6},{12,8},{14,10},{1,13},{3,15... | collective-permute-start | bytes 884744 | tf_op jit(solution)/shard_map/ppermute | solution.py:448
  102.7 20.0 %collective-permute-start.30 = (bf16[144,1024]{1,0:T(8,128)(2,1)}, bf16[144,1024]{1,0:T(8,128)(2,1)S(1)}, u32[]{:S(2)}, u32[]{:S(2)}) collective-permute-start(bf16[144,1024]{1,0:T(8,128)(2,1)} %collective-permute-done.16.refs_8_), channel_id=1, source_target_pairs={{0,2},{2,0},{4,6},{6,4},{8,10},{10,8},{12,14},{14,12},{1,3},{3,1},... | collective-permute-start | bytes 884744 | tf_op jit(solution)/shard_map/ppermute | solution.py:445
  105.9 16.8 %collective-permute-start.29 = (bf16[144,1024]{1,0:T(8,128)(2,1)}, bf16[144,1024]{1,0:T(8,128)(2,1)S(1)}, u32[]{:S(2)}, u32[]{:S(2)}) collective-permute-start(bf16[144,1024]{1,0:T(8,128)(2,1)} %collective-permute-done.16.refs_8_), channel_id=1, source_target_pairs={{0,1},{1,0},{2,3},{3,2},{4,5},{5,4},{6,7},{7,6},{8,9},{9,8},{10,11... | collective-permute-start | bytes 884744 | tf_op jit(solution)/shard_map/ppermute | solution.py:439
  120.9 17.7 %collective-permute-start.22 = (bf16[2,144,1024]{2,1,0:T(8,128)(2,1)}, bf16[2,144,1024]{2,1,0:T(8,128)(2,1)S(1)}, u32[]{:S(2)}, u32[]{:S(2)}) collective-permute-start(bf16[2,144,1024]{2,1,0:T(8,128)(2,1)} %get-tuple-element.103), channel_id=1, source_target_pairs={{0,1},{1,0},{2,3},{3,2},{4,5},{5,4},{6,7},{7,6},{8,9},{9,8},{10,11... | collective-permute-start | bytes 1769480 | tf_op jit(solution)/shard_map/ppermute | solution.py:439
  122.0 16.6 %collective-permute-start.24 = (bf16[2,144,1024]{2,1,0:T(8,128)(2,1)}, bf16[2,144,1024]{2,1,0:T(8,128)(2,1)S(1)}, u32[]{:S(2)}, u32[]{:S(2)}) collective-permute-start(bf16[2,144,1024]{2,1,0:T(8,128)(2,1)} %get-tuple-element.105), channel_id=1, source_target_pairs={{0,2},{2,0},{4,6},{6,4},{8,10},{10,8},{12,14},{14,12},{1,3},{3,1},... | collective-permute-start | bytes 1769480 | tf_op jit(solution)/shard_map/ppermute | solution.py:445
  122.7 31.2 %collective-permute-start.39 = (bf16[288,5248]{1,0:T(8,128)(2,1)}, bf16[288,5248]{1,0:T(8,128)(2,1)S(1)}, u32[]{:S(2)}, u32[]{:S(2)}) collective-permute-start(bf16[288,5248]{1,0:T(8,128)(2,1)} %get-tuple-element.125), channel_id=1, source_target_pairs={{0,16},{16,0},{1,17},{17,1},{2,18},{18,2},{3,19},{19,3},{4,20},{20... | collective-permute-start | bytes 9068552 | tf_op jit(solution)/shard_map/ppermute | solution.py:442
  139.4 14.6 %collective-permute-start.40 = (bf16[288,5248]{1,0:T(8,128)(2,1)}, bf16[288,5248]{1,0:T(8,128)(2,1)S(1)}, u32[]{:S(2)}, u32[]{:S(2)}) collective-permute-start(bf16[288,5248]{1,0:T(8,128)(2,1)} %get-tuple-element.127), channel_id=1, source_target_pairs={{0,16},{16,0},{1,17},{17,1},{2,18},{18,2},{3,19},{19,3},{4,20},{20... | collective-permute-start | bytes 9068552 | tf_op jit(solution)/shard_map/ppermute | solution.py:442
  140.8 9.9 %collective-permute-start.25 = (bf16[144,1024]{1,0:T(8,128)(2,1)S(1)}, bf16[144,1024]{1,0:T(8,128)(2,1)S(1)}, u32[]{:S(2)}, u32[]{:S(2)}) collective-permute-start(bf16[144,1024]{1,0:T(8,128)(2,1)S(1)} %fusion.9), channel_id=1, source_target_pairs={{0,1},{1,0},{2,3},{3,2},{4,5},{5,4},{6,7},{7,6},{8,9},{9,8},{10,11... | collective-permute-start | bytes 884744 | tf_op jit(solution)/shard_map/ppermute | solution.py:439
  142.7 23.5 %collective-permute-start.23 = (bf16[144,1024]{1,0:T(8,128)(2,1)}, bf16[144,1024]{1,0:T(8,128)(2,1)S(1)}, u32[]{:S(2)}, u32[]{:S(2)}) collective-permute-start(bf16[144,1024]{1,0:T(8,128)(2,1)} %fusion.8), channel_id=1, source_target_pairs={{0,2},{2,0},{4,6},{6,4},{8,10},{10,8},{12,14},{14,12},{1,3},{3,1},... | collective-permute-start | bytes 884744 | tf_op jit(solution)/shard_map/ppermute | solution.py:445
  144.1 22.2 %collective-permute-start.37 = (bf16[2,144,1024]{2,1,0:T(8,128)(2,1)}, bf16[2,144,1024]{2,1,0:T(8,128)(2,1)}, u32[]{:S(2)}, u32[]{:S(2)}) collective-permute-start(bf16[2,144,1024]{2,1,0:T(8,128)(2,1)} %get-tuple-element.123), channel_id=1, source_target_pairs={{0,1},{1,0},{2,3},{3,2},{4,5},{5,4},{6,7},{7,6},{8,9},{9,8},{10,11... | collective-permute-start | bytes 1769480 | tf_op jit(solution)/shard_map/ppermute | solution.py:439
  150.8 15.5 %collective-permute-start.38 = (bf16[2,144,1024]{2,1,0:T(8,128)(2,1)}, bf16[2,144,1024]{2,1,0:T(8,128)(2,1)}, u32[]{:S(2)}, u32[]{:S(2)}) collective-permute-start(bf16[2,144,1024]{2,1,0:T(8,128)(2,1)} %get-tuple-element.124), channel_id=1, source_target_pairs={{0,2},{2,0},{4,6},{6,4},{8,10},{10,8},{12,14},{14,12},{1,3},{3,1},... | collective-permute-start | bytes 1769480 | tf_op jit(solution)/shard_map/ppermute | solution.py:445
  154.0 22.7 %collective-permute-start.26 = (bf16[144,1024]{1,0:T(8,128)(2,1)}, bf16[144,1024]{1,0:T(8,128)(2,1)}, u32[]{:S(2)}, u32[]{:S(2)}) collective-permute-start(bf16[144,1024]{1,0:T(8,128)(2,1)} %fusion.2), channel_id=1, source_target_pairs={{0,8},{2,10},{4,12},{6,14},{8,0},{10,2},{12,4},{14,6},{1,9},{3,11}... | collective-permute-start | bytes 884744 | tf_op jit(solution)/shard_map/ppermute | solution.py:448
  167.4 9.3 %collective-permute-start.42 = (bf16[144,1024]{1,0:T(8,128)(2,1)S(1)}, bf16[144,1024]{1,0:T(8,128)(2,1)S(1)}, u32[]{:S(2)}, u32[]{:S(2)}) collective-permute-start(bf16[144,1024]{1,0:T(8,128)(2,1)S(1)} %fusion.11), channel_id=1, source_target_pairs={{0,1},{1,0},{2,3},{3,2},{4,5},{5,4},{6,7},{7,6},{8,9},{9,8},{10,11... | collective-permute-start | bytes 884744 | tf_op jit(solution)/shard_map/ppermute | solution.py:439
  169.6 7.2 %collective-permute-start.41 = (bf16[144,1024]{1,0:T(8,128)(2,1)S(1)}, bf16[144,1024]{1,0:T(8,128)(2,1)S(1)}, u32[]{:S(2)}, u32[]{:S(2)}) collective-permute-start(bf16[144,1024]{1,0:T(8,128)(2,1)S(1)} %fusion.10), channel_id=1, source_target_pairs={{0,2},{2,0},{4,6},{6,4},{8,10},{10,8},{12,14},{14,12},{1,3},{3,1},... | collective-permute-start | bytes 884744 | tf_op jit(solution)/shard_map/ppermute | solution.py:445
  179.0 9.9 %collective-permute-start.43 = (bf16[144,1024]{1,0:T(8,128)(2,1)S(1)}, bf16[144,1024]{1,0:T(8,128)(2,1)S(1)}, u32[]{:S(2)}, u32[]{:S(2)}) collective-permute-start(bf16[144,1024]{1,0:T(8,128)(2,1)S(1)} %fusion.1), channel_id=1, source_target_pairs={{0,12},{2,14},{4,0},{6,2},{8,4},{10,6},{12,8},{14,10},{1,13},{3,15... | collective-permute-start | bytes 884744 | tf_op jit(solution)/shard_map/ppermute | solution.py:448
  180.9 11.6 %collective-permute-start.44 = (bf16[144,1024]{1,0:T(8,128)(2,1)S(1)}, bf16[144,1024]{1,0:T(8,128)(2,1)S(1)}, u32[]{:S(2)}, u32[]{:S(2)}) collective-permute-start(bf16[144,1024]{1,0:T(8,128)(2,1)S(1)} %fusion), channel_id=1, source_target_pairs={{0,4},{2,6},{4,8},{6,10},{8,12},{10,14},{12,0},{14,2},{1,5},{3,7},... | collective-permute-start | bytes 884744 | tf_op jit(solution)/shard_map/ppermute | solution.py:448
  (34 other events, 477.4 us)

commit v7 on v6

--- a/solution.py
+++ b/solution.py
@@ -124,15 +124,14 @@
 LOOSE = pl.BlockSpec(memory_space=pl.ANY)
 
 
-def weights_kernel(tp_ref, wg_ref, wu_ref, wd_ref, *refs):
-    both_ref, down_ref = refs[-2:]
+def weights_kernel(tp_ref, wg_ref, wu_ref, wd_ref, both_ref, down_ref):
     part = wg_ref.shape[2]
     both_ref[:, :part] = wg_ref[0]
     both_ref[:, part:] = wu_ref[0]
     down_ref[...] = wd_ref[0]
 
 
-def weights_call(which, w_gate, w_up, w_down, after):
+def weights_call(which, w_gate, w_up, w_down):
     _, width, part = w_gate.shape
     half = width // 2
 
@@ -148,8 +147,7 @@
                 pl.BlockSpec((1, half, part), lambda i, w: (0, place(i, w), 0)),
                 pl.BlockSpec((1, half, part), lambda i, w: (0, place(i, w), 0)),
                 pl.BlockSpec((1, part, half), lambda i, w: (0, 0, place(i, w))),
-            ]
-            + [LOOSE] * len(after),
+            ],
             out_specs=[
                 pl.BlockSpec((half, 2 * part), lambda i, w: (i, 0)),
                 pl.BlockSpec((part, half), lambda i, w: (0, i)),
@@ -159,14 +157,14 @@
             jax.ShapeDtypeStruct((width, 2 * part), jnp.bfloat16),
             jax.ShapeDtypeStruct((part, width), jnp.bfloat16),
         ],
-        compiler_params=pltpu.CompilerParams(vmem_limit_bytes=56 << 20),
+        compiler_params=pltpu.CompilerParams(vmem_limit_bytes=62 << 20),
         cost_estimate=pl.CostEstimate(flops=0, bytes_accessed=12 * width * part, transcendentals=0),
         name="weights",
-    )(which, w_gate, w_up, w_down, *after)
+    )(which, w_gate, w_up, w_down)
 
 
 def rows_kernel(count, modes, capacity, slots, where_ref, *refs):
-    weights_in, x_in, g_in = refs[:4], refs[4 : 4 + 4 * count], refs[4 + 4 * count : 4 + 8 * count]
+    weights_in, units_in = refs[:4], refs[4 : 4 + 4 * count]
     refs = refs[len(refs) - 17 - 2 * count :]
     outs, keeps, sends, refs = refs[:2], refs[2 : 2 + count], refs[2 + count : 2 + 2 * count], refs[2 + 2 * count :]
     x_all, g_all, tables, wgu0, wgu1, wd0, wd1, xc, gc, both, scaled, piece, unit_sems, weight_sems = refs[:14]
@@ -177,13 +175,13 @@
     wgu, wd = (wgu0, wgu1), (wd0, wd1)
 
     x_copies, g_copies, t_copies = [], [], []
-    for index, (x_unit, g_unit) in enumerate(zip(x_in, g_in)):
+    for index, unit in enumerate(units_in):
         chunk, y, x = index // 4, index // 2 % 2, index % 2
         rows = pl.ds(y * tok, tok)
-        x_copies.append(pltpu.make_async_copy(x_unit.at[pl.ds(0, tok)], x_all.at[chunk, x, rows], unit_sems.at[0, index]))
-        g_copies.append(pltpu.make_async_copy(g_unit, g_all.at[chunk, x, rows], unit_sems.at[1, index]))
+        x_copies.append(pltpu.make_async_copy(unit.at[pl.ds(0, tok)], x_all.at[chunk, x, rows], unit_sems.at[0, index]))
+        g_copies.append(pltpu.make_async_copy(unit.at[pl.ds(tok, tok)], g_all.at[chunk, x, rows], unit_sems.at[1, index]))
         if x == 0:
-            table = x_unit.at[pl.ds(tok, owners), pl.ds(0, tok)]
+            table = unit.at[pl.ds(2 * tok, owners), pl.ds(0, tok)]
             t_copies.append(pltpu.make_async_copy(table, tables.at[chunk, y], unit_sems.at[2, index]))
     weight_copies = [
         pltpu.make_async_copy(source, target, weight_sems.at[index])
@@ -300,7 +298,7 @@
 
 def rows_call(modes, owners, capacity, slots, where, weights, units, after):
     count = len(modes)
-    tok, half = units[-1].shape
+    tok, half = (units[0].shape[0] - owners) // 2, units[0].shape[1]
     part, width = weights[2].shape
     widths = (width, width, 2 * part, part)
     packet = (2, tok + owners, half)
@@ -325,7 +323,7 @@
         ),
         out_shape=[jax.ShapeDtypeStruct((count * slots, sum(widths)), jnp.bfloat16)] * 2
         + [jax.ShapeDtypeStruct(packet, jnp.bfloat16)] * (2 * count),
-        compiler_params=pltpu.CompilerParams(vmem_limit_bytes=56 << 20),
+        compiler_params=pltpu.CompilerParams(vmem_limit_bytes=62 << 20),
         cost_estimate=pl.CostEstimate(
             flops=count * (20 * slots * width * part + 24 * slots * tok * width),
             bytes_accessed=count * 16 * tok * width + 12 * width * part,
@@ -417,7 +415,7 @@
             ],
         ),
         out_shape=[jax.ShapeDtypeStruct(shape, jnp.bfloat16) for shape in shapes],
-        compiler_params=pltpu.CompilerParams(vmem_limit_bytes=56 << 20),
+        compiler_params=pltpu.CompilerParams(vmem_limit_bytes=24 << 20),
         cost_estimate=pl.CostEstimate(
             flops=2 * count * rows * width * deep, bytes_accessed=2 * count * rows * (width + deep), transcendentals=0
         ),
@@ -446,6 +444,9 @@
 
     def over_z(array, shift):
         return lax.ppermute(array, "ep", [(i, (i + shift * n_y) % ep) for i in range(ep)])
+
+    def tied(values, others):
+        return lax.optimization_barrier((list(values), list(others)))[0]
 
     chosen = routes[:, :, None] == jnp.arange(owners, dtype=jnp.int32)
     table = jnp.sum(jnp.where(chosen, probs[:, :, None].astype(jnp.float32) + 1.0, 0.0), axis=1) - 1.0
@@ -477,35 +478,31 @@
         there |= {item[0] for item in rounds[-1]}
         waiting = [item for item in waiting if item[0] not in there]
 
-    units = {("x", 0, 0, 0): jnp.concatenate([tokens, table], 0), ("g", 0, 0, 0): out_grad}
-    settled, flying = dict(units), {}
+    which_ref = which.reshape(1).astype(jnp.int32)
+    both_w, down_w = weights_call(which_ref, w_gate, w_up, w_down)
+    units = {(0, 0, 0): jnp.concatenate([tokens, out_grad, table], 0)}
+    settled, extra, weights = dict(units), [both_w, down_w], ()
     for moves in rounds:
-        for name in ("x", "g"):
-            arrived = {(name,) + target: move(settled[(name,) + source]) for target, source, move in moves}
-            units.update(arrived)
-            settled.update(flying)
-            names = list(settled)
-            settled = dict(zip(names, lax.optimization_barrier([settled[item] for item in names])))
-            flying = arrived
-
-    which_ref = which.reshape(1).astype(jnp.int32)
-    first = [units[("x",) + item[0]] for item in rounds[1]]
-    both_w, down_w = weights_call(which_ref, w_gate, w_up, w_down, first)
-    weights = (both_w, over_role(both_w), down_w, over_role(down_w))
+        arrived = {target: move(settled[source]) for target, source, move in moves}
+        units.update(arrived)
+        settled.update(arrived)
+        names = list(settled)
+        settled = dict(zip(names, tied([settled[item] for item in names], extra)))
+        if extra:
+            both_w, down_w = tied(extra, arrived.values())
+            weights, extra = (both_w, over_role(both_w), down_w, over_role(down_w)), []
+
     where = jnp.stack([role * ep + place, (1 - role) * ep + place, which]).astype(jnp.int32)
 
     def add(a, b):
         return a.astype(jnp.float32) + b.astype(jnp.float32)
-
-    def tied(values, others):
-        return lax.optimization_barrier((list(values), list(others)))[0]
 
     width, part = both_w.shape[0], down_w.shape[0]
     packed, flown, homeward, done = [], [], [], []
     for turn, group in enumerate((range(0, n_z, 2), range(1, n_z, 2))):
         modes = [index % 2 for index in range(len(group))]
-        eight = [units[name, z, y, x] for name in ("x", "g") for z in group for y in range(2) for x in range(2)]
-        mine, other, *packets = rows_call(modes, owners, capacity, slots, where, weights, eight, packed[:1])
+        four = [units[z, y, x] for z in group for y in range(2) for x in range(2)]
+        mine, other, *packets = rows_call(modes, owners, capacity, slots, where, weights, four, packed[:1])
         keeps, sends = packets[: len(group)], packets[len(group) :]
         if turn:
             mine, other, *sends = tied([mine, other] + sends, flown[0])

time: 196 us -> 155 us (0.79)
  starting transfers between devices: 43.3 us -> 28.9 us
  waiting for transfers between devices: 81.1 us -> 67.4 us
  other arithmetic: 12.9 us -> 6.73 us
  Pallas kernels: 47.5 us -> 44.3 us
  local copies, waits for them, and re-layouts: 9.25 us -> 6.19 us
    ppermute x13 -> x8, waiting for transfers between devices: 41.3 us -> 28.1 us  [over_z(): lax.ppermute(array, 'ep', [(i, (i + shift * n_y) % ep) for i in range(ep)])]
    ppermute x14 -> x9, starting transfers between devices: 17.8 us -> 9.03 us  [over_y(): lax.ppermute(array, 'ep', [(i, i + 1 - 2 * (i % n_y)) for i in range(ep)])]
    ppermute x14 -> x9, starting transfers between devices: 17.8 us -> 11.8 us  [over_x(): return lax.ppermute(array, 'tp', [(0, 1), (1, 0)])]
    ppermute x14 -> x9, waiting for transfers between devices: 33 us -> 28.2 us  [over_x(): return lax.ppermute(array, 'tp', [(0, 1), (1, 0)])]
    ppermute x14 -> x9, waiting for transfers between devices: 6.8 us -> 11 us  [over_y(): lax.ppermute(array, 'ep', [(i, i + 1 - 2 * (i % n_y)) for i in range(ep)])]
    pallas_call x2, Pallas kernels: 15.4 us -> 12.2 us  [grads_call(): pl.pallas_call(functools.partial(grads_kernel, count, *starts, 2 * per),...]
    unnamed x74 -> x36, local copies, waits for them, and re-layouts: 8.5 us -> 5.43 us
    convert_element_type x4, other arithmetic: 3.99 us -> 1.26 us  [dense_device(): add(keep[1], first[1]).astype(jnp.bfloat16)]
  transfers between devices with their start and end apart: 45 -> 30, of which waited for: 26 -> 16; matrix products, arithmetic and copies ran while one was open for 3% -> 2% of each run, Pallas kernels for 22% -> 29%
where the time goes in v7:
time: 155 us; the launch traced here: 154 us
  waiting for transfers between devices  67.4 us (43%)
  Pallas kernels  44.3 us (29%)
  starting transfers between devices  28.9 us (19%)
  other arithmetic  6.73 us (4%)
  local copies, waits for them, and re-layouts  6.19 us (4%)
    ppermute x9, waiting for transfers between devices, over_x(): return lax.ppermute(array, 'tp', [(0, 1), (1, 0)])  28.2 us
    pallas_call x2, Pallas kernels, rows_call(): pl.pallas_call(functools.partial(rows_kernel, count, modes, capacity, slo...  28.2 us
    ppermute x8, waiting for transfers between devices, over_z(): lax.ppermute(array, 'ep', [(i, (i + shift * n_y) % ep) for i in range(ep)])  28.1 us
    pallas_call x2, Pallas kernels, grads_call(): pl.pallas_call(functools.partial(grads_kernel, count, *starts, 2 * per),...  12.2 us
    ppermute x9, starting transfers between devices, over_x(): return lax.ppermute(array, 'tp', [(0, 1), (1, 0)])  11.8 us
    ppermute x9, waiting for transfers between devices, over_y(): lax.ppermute(array, 'ep', [(i, i + 1 - 2 * (i % n_y)) for i in range(ep)])  11 us
    ppermute x9, starting transfers between devices, over_y(): lax.ppermute(array, 'ep', [(i, i + 1 - 2 * (i % n_y)) for i in range(ep)])  9.03 us
    ppermute x8, starting transfers between devices, over_z(): lax.ppermute(array, 'ep', [(i, (i + shift * n_y) % ep) for i in range(ep)])  7.43 us
  transfers between devices with their start and end apart: 30, of which 16 were waited for; matrix products, arithmetic and copies ran while one was open for 2% of the time, Pallas kernels for 29%

profile of v7, /device:TPU:0, one launch (start us, length us, event | category | flops | bytes accessed | tf_op | source)
XLA Modules:
  0.0 154.5 jit_solution(639885723111153230)
XLA Ops:
  0.6 0.7 convert_add_fusion
  1.3 0.7 select_reduce_fusion.1
  2.0 1.1 fusion.7.refs_4_
  3.1 3.0 %collective-permute-start.2 = (bf16[272,1024]{1,0:T(8,128)(2,1)S(1)}, bf16[272,1024]{1,0:T(8,128)(2,1)S(1)}, u32[]{:S(2)}, u32[]{:S(2)}) collective-permute-start(bf16[272,1024]{1,0:T(8,128)(2,1)S(1)} %fusion.7.refs_4_), channel_id=1, source_target_pairs={{0,1},{1,0},{2,3},{3,2},{4,5},{5,4},{6,7},{7,6},{8,9},{9,8},{10,11... | collective-permute-start | bytes 1671176 | tf_op jit(solution)/shard_map/ppermute | solution.py:437
  6.1 1.5 collective-permute-start.1
  7.6 1.6 %collective-permute-start = (bf16[272,1024]{1,0:T(8,128)(2,1)S(1)}, bf16[272,1024]{1,0:T(8,128)(2,1)S(1)}, u32[]{:S(2)}, u32[]{:S(2)}) collective-permute-start(bf16[272,1024]{1,0:T(8,128)(2,1)S(1)} %fusion.7.refs_4_), channel_id=1, source_target_pairs={{0,4},{2,6},{4,8},{6,10},{8,12},{10,14},{12,0},{14,2},{1,5},{3,7},... | collective-permute-start | bytes 1671176 | tf_op jit(solution)/shard_map/ppermute | solution.py:446
  9.2 4.0 %weights.1 = (bf16[2048,768]{1,0:T(8,128)(2,1)}, bf16[384,2048]{1,0:T(8,128)(2,1)}) custom-call(s32[1]{0:T(128)} %bitcast.2.tp_ref, bf16[1,2048,384]{2,1,0:T(8,128)(2,1)} %wg_ref.1, bf16[1,2048,384]{2,1,0:T(8,128)(2,1)} %wu_ref.1, bf16[1,384,2048]{2,1,0:T(8,128)(2,1)} %wd_ref.1), custom_call_target="tpu_custom_call" | custom-call | bytes 9437184 | tf_op jit(solution)/shard_map/weights/pallas_call | solution.py:141
  13.2 5.6 %collective-permute-done.2.refs_5_ = bf16[272,1024]{1,0:T(8,128)(2,1)S(1)} collective-permute-done((bf16[272,1024]{1,0:T(8,128)(2,1)S(1)}, bf16[272,1024]{1,0:T(8,128)(2,1)S(1)}, u32[]{:S(2)}, u32[]{:S(2)}) %collective-permute-start.2) | collective-permute-done | bytes 557088 | tf_op jit(solution)/shard_map/ppermute | solution.py:437
  18.7 1.6 %collective-permute-done.1.refs_6_ = bf16[272,1024]{1,0:T(8,128)(2,1)} collective-permute-done((bf16[272,1024]{1,0:T(8,128)(2,1)S(1)}, bf16[272,1024]{1,0:T(8,128)(2,1)}, u32[]{:S(2)}, u32[]{:S(2)}) %collective-permute-start.1) | collective-permute-done | bytes 557088 | tf_op jit(solution)/shard_map/ppermute | solution.py:443
  20.3 3.0 %collective-permute-done.refs_4_ = bf16[272,1024]{1,0:T(8,128)(2,1)S(1)} collective-permute-done((bf16[272,1024]{1,0:T(8,128)(2,1)S(1)}, bf16[272,1024]{1,0:T(8,128)(2,1)S(1)}, u32[]{:S(2)}, u32[]{:S(2)}) %collective-permute-start) | collective-permute-done | bytes 557088 | tf_op jit(solution)/shard_map/ppermute | solution.py:446
  24.4 14.3 %collective-permute-done.5.refs_7_ = bf16[272,1024]{1,0:T(8,128)(2,1)} collective-permute-done((bf16[272,1024]{1,0:T(8,128)(2,1)}, bf16[272,1024]{1,0:T(8,128)(2,1)}, u32[]{:S(2)}, u32[]{:S(2)}) %collective-permute-start.5) | collective-permute-done | bytes 557088 | tf_op jit(solution)/shard_map/ppermute | solution.py:437
  38.7 2.0 %collective-permute-done.6.refs_8_ = bf16[272,1024]{1,0:T(8,128)(2,1)S(1)} collective-permute-done((bf16[272,1024]{1,0:T(8,128)(2,1)S(1)}, bf16[272,1024]{1,0:T(8,128)(2,1)S(1)}, u32[]{:S(2)}, u32[]{:S(2)}) %collective-permute-start.6) | collective-permute-done | bytes 557088 | tf_op jit(solution)/shard_map/ppermute | solution.py:446
  40.6 1.6 %collective-permute-start.9 = (bf16[272,1024]{1,0:T(8,128)(2,1)S(1)}, bf16[272,1024]{1,0:T(8,128)(2,1)S(1)}, u32[]{:S(2)}, u32[]{:S(2)}) collective-permute-start(bf16[272,1024]{1,0:T(8,128)(2,1)S(1)} %collective-permute-done.6.refs_8_), channel_id=1, source_target_pairs={{0,2},{2,0},{4,6},{6,4},{8,10},{10,8},{12,14},{14,12},{1,3},{3,1},... | collective-permute-start | bytes 1671176 | tf_op jit(solution)/shard_map/ppermute | solution.py:443
  42.2 1.5 collective-permute-start.8
  43.7 10.6 %collective-permute-done.10.refs_8_ = bf16[272,1024]{1,0:T(8,128)(2,1)} collective-permute-done((bf16[272,1024]{1,0:T(8,128)(2,1)S(1)}, bf16[272,1024]{1,0:T(8,128)(2,1)}, u32[]{:S(2)}, u32[]{:S(2)}) %collective-permute-start.10) | collective-permute-done | bytes 557088 | tf_op jit(solution)/shard_map/ppermute | solution.py:446
  54.5 1.2 collective-permute-done.8.refs_9_
  55.7 0.7 collective-permute-start.11
  56.3 1.3 collective-permute-start.17
  57.7 1.7 %collective-permute-start.18 = (bf16[272,1024]{1,0:T(8,128)(2,1)}, bf16[272,1024]{1,0:T(8,128)(2,1)S(1)}, u32[]{:S(2)}, u32[]{:S(2)}) collective-permute-start(bf16[272,1024]{1,0:T(8,128)(2,1)} %collective-permute-done.5.refs_7_), channel_id=1, source_target_pairs={{0,4},{2,6},{4,8},{6,10},{8,12},{10,14},{12,0},{14,2},{1,5},{3,7},... | collective-permute-start | bytes 1671176 | tf_op jit(solution)/shard_map/ppermute | solution.py:446
  60.0 8.3 %collective-permute-done.11.refs_11_ = bf16[272,1024]{1,0:T(8,128)(2,1)S(1)} collective-permute-done((bf16[272,1024]{1,0:T(8,128)(2,1)}, bf16[272,1024]{1,0:T(8,128)(2,1)S(1)}, u32[]{:S(2)}, u32[]{:S(2)}) %collective-permute-start.11) | collective-permute-done | bytes 557088 | tf_op jit(solution)/shard_map/ppermute | solution.py:443
  68.6 0.8 copy-done.14
  69.4 2.2 %collective-permute-done.18.refs_7_ = bf16[272,1024]{1,0:T(8,128)(2,1)S(1)} collective-permute-done((bf16[272,1024]{1,0:T(8,128)(2,1)}, bf16[272,1024]{1,0:T(8,128)(2,1)S(1)}, u32[]{:S(2)}, u32[]{:S(2)}) %collective-permute-start.18) | collective-permute-done | bytes 557088 | tf_op jit(solution)/shard_map/ppermute | solution.py:446
  71.7 0.8 copy-done.15
  72.5 1.4 collective-permute-start.20
  74.5 13.9 %rows.2 = (bf16[288,5248]{1,0:T(8,128)(2,1)}, bf16[288,5248]{1,0:T(8,128)(2,1)}, bf16[2,144,1024]{2,1,0:T(8,128)(2,1)}, bf16[2,144,1024]{2,1,0:T(8,128)(2,1)}, b...) custom-call(s32[3]{0:T(128)} %pad_add_fusion.where_ref, bf16[2048,768]{1,0:T(8,128)(2,1)} %get-tuple-element.46.refs_0_, ...), custom_call_target="tpu_custom_call" | custom-call | flops 6341787648 | bytes 17825792 | tf_op jit(solution)/shard_map/rows/pallas_call | solution.py:305
  88.4 1.5 collective-permute-start.12
  90.0 1.1 collective-permute-start.14
  91.1 14.3 %rows.3 = (bf16[288,5248]{1,0:T(8,128)(2,1)}, bf16[288,5248]{1,0:T(8,128)(2,1)}, bf16[2,144,1024]{2,1,0:T(8,128)(2,1)}, bf16[2,144,1024]{2,1,0:T(8,128)(2,1)}, b...) custom-call(s32[3]{0:T(128)} %pad_add_fusion.where_ref, bf16[2048,768]{1,0:T(8,128)(2,1)} %get-tuple-element.46.refs_0_, ...), custom_call_target="tpu_custom_call" | custom-call | flops 6341787648 | bytes 17825792 | tf_op jit(solution)/shard_map/rows/pallas_call | solution.py:305
  106.0 1.0 fusion.9
  107.0 1.0 collective-permute-start.15
  108.1 0.6 collective-permute-start.13
  108.7 1.5 collective-permute-start.22
  110.2 6.8 %collective-permute-done.15 = bf16[144,1024]{1,0:T(8,128)(2,1)S(1)} collective-permute-done((bf16[144,1024]{1,0:T(8,128)(2,1)S(1)}, bf16[144,1024]{1,0:T(8,128)(2,1)S(1)}, u32[]{:S(2)}, u32[]{:S(2)}) %collective-permute-start.15) | collective-permute-done | bytes 294944 | tf_op jit(solution)/shard_map/ppermute | solution.py:437
  117.0 0.9 collective-permute-start.23
  117.9 1.2 fusion.3
  119.1 1.1 collective-permute-start.16
  120.2 1.9 %copy-done = bf16[288,5248]{1,0:T(8,128)(2,1)S(1)} copy-done((bf16[288,5248]{1,0:T(8,128)(2,1)S(1)}, bf16[288,5248]{1,0:T(8,128)(2,1)}, u32[]{:S(2)}) %copy-start) | copy-done | bytes 3022872
  122.1 1.9 %copy-done.1 = bf16[288,5248]{1,0:T(8,128)(2,1)S(1)} copy-done((bf16[288,5248]{1,0:T(8,128)(2,1)S(1)}, bf16[288,5248]{1,0:T(8,128)(2,1)}, u32[]{:S(2)}) %copy-start.1) | copy-done | bytes 3022872
  123.9 7.3 %grads.2 = (bf16[1,2048,384]{2,1,0:T(8,128)(2,1)}, bf16[1,2048,384]{2,1,0:T(8,128)(2,1)}) custom-call(s32[1]{0:T(128)} %bitcast.2.tp_ref, bf16[288,5248]{1,0:T(8,128)(2,1)S(1)} %copy-done, bf16[288,5248]{1,0:T(8,128)(2,1)} %collective-permute-done.24.refs_1_, bf16[288,5248]{1,0:T(8,128)(2,1)S(1)} %copy-done.1, ...), custom_call_target="tpu_custom_call" | custom-call | flops 3623878656 | bytes 6488064 | tf_op jit(solution)/shard_map/grads/pallas_call | solution.py:403
  131.3 1.0 collective-permute-start.27
  132.3 0.7 collective-permute-start.26
  133.1 4.9 %grads.3 = bf16[1,384,2048]{2,1,0:T(8,128)(2,1)} custom-call(s32[1]{0:T(128)} %bitcast.2.tp_ref, bf16[288,5248]{1,0:T(8,128)(2,1)S(1)} %copy-done, bf16[288,5248]{1,0:T(8,128)(2,1)} %collective-permute-done.24.refs_1_, bf16[288,5248]{1,0:T(8,128)(2,1)S(1)} %copy-done.1, bf16[288,5248]{1,0:T(8,128)(2,1)S(1)} %collective-permute-done.25.refs_3_), custom_call_target="tpu_custom_call" | custom-call | flops 1811939328 | bytes 5603328 | tf_op jit(solution)/shard_map/grads/pallas_call | solution.py:403
  138.1 1.0 collective-permute-done.26
  139.4 3.0 %collective-permute-start.28 = (bf16[144,1024]{1,0:T(8,128)(2,1)S(1)}, bf16[144,1024]{1,0:T(8,128)(2,1)S(1)}, u32[]{:S(2)}, u32[]{:S(2)}) collective-permute-start(bf16[144,1024]{1,0:T(8,128)(2,1)S(1)} %fusion.2), channel_id=1, source_target_pairs={{0,12},{2,14},{4,0},{6,2},{8,4},{10,6},{12,8},{14,10},{1,13},{3,15... | collective-permute-start | bytes 884744 | tf_op jit(solution)/shard_map/ppermute | solution.py:446
  142.5 6.9 %collective-permute-done.28 = bf16[144,1024]{1,0:T(8,128)(2,1)S(1)} collective-permute-done((bf16[144,1024]{1,0:T(8,128)(2,1)S(1)}, bf16[144,1024]{1,0:T(8,128)(2,1)S(1)}, u32[]{:S(2)}, u32[]{:S(2)}) %collective-permute-start.28) | collective-permute-done | bytes 294944 | tf_op jit(solution)/shard_map/ppermute | solution.py:446
  149.4 3.4 %collective-permute-done.29 = bf16[144,1024]{1,0:T(8,128)(2,1)S(1)} collective-permute-done((bf16[144,1024]{1,0:T(8,128)(2,1)S(1)}, bf16[144,1024]{1,0:T(8,128)(2,1)S(1)}, u32[]{:S(2)}, u32[]{:S(2)}) %collective-permute-start.29) | collective-permute-done | bytes 294944 | tf_op jit(solution)/shard_map/ppermute | solution.py:446
  153.1 0.7 slice.96
  153.8 0.6 select_reduce_fusion
  (71 shorter events, 4.2 us)
Async XLA Ops:
  3.1 37.5 %copy-start.6 = (bf16[272,1024]{1,0:T(8,128)(2,1)}, bf16[272,1024]{1,0:T(8,128)(2,1)S(1)}, u32[]{:S(2)}) copy-start(bf16[272,1024]{1,0:T(8,128)(2,1)S(1)} %fusion.7.refs_4_) | copy-start | bytes 1671172
  3.1 15.6 %collective-permute-start.2 = (bf16[272,1024]{1,0:T(8,128)(2,1)S(1)}, bf16[272,1024]{1,0:T(8,128)(2,1)S(1)}, u32[]{:S(2)}, u32[]{:S(2)}) collective-permute-start(bf16[272,1024]{1,0:T(8,128)(2,1)S(1)} %fusion.7.refs_4_), channel_id=1, source_target_pairs={{0,1},{1,0},{2,3},{3,2},{4,5},{5,4},{6,7},{7,6},{8,9},{9,8},{10,11... | collective-permute-start | bytes 1671176 | tf_op jit(solution)/shard_map/ppermute | solution.py:437
  6.1 14.2 %collective-permute-start.1 = (bf16[272,1024]{1,0:T(8,128)(2,1)S(1)}, bf16[272,1024]{1,0:T(8,128)(2,1)}, u32[]{:S(2)}, u32[]{:S(2)}) collective-permute-start(bf16[272,1024]{1,0:T(8,128)(2,1)S(1)} %fusion.7.refs_4_), channel_id=1, source_target_pairs={{0,2},{2,0},{4,6},{6,4},{8,10},{10,8},{12,14},{14,12},{1,3},{3,1},... | collective-permute-start | bytes 1671176 | tf_op jit(solution)/shard_map/ppermute | solution.py:443
  7.6 15.7 %collective-permute-start = (bf16[272,1024]{1,0:T(8,128)(2,1)S(1)}, bf16[272,1024]{1,0:T(8,128)(2,1)S(1)}, u32[]{:S(2)}, u32[]{:S(2)}) collective-permute-start(bf16[272,1024]{1,0:T(8,128)(2,1)S(1)} %fusion.7.refs_4_), channel_id=1, source_target_pairs={{0,4},{2,6},{4,8},{6,10},{8,12},{10,14},{12,0},{14,2},{1,5},{3,7},... | collective-permute-start | bytes 1671176 | tf_op jit(solution)/shard_map/ppermute | solution.py:446
  18.7 55.7 %copy-start.12 = (bf16[272,1024]{1,0:T(8,128)(2,1)}, bf16[272,1024]{1,0:T(8,128)(2,1)S(1)}, u32[]{:S(2)}) copy-start(bf16[272,1024]{1,0:T(8,128)(2,1)S(1)} %collective-permute-done.2.refs_5_) | copy-start | bytes 1671172
  23.3 65.1 %copy-start.10 = (bf16[272,1024]{1,0:T(8,128)(2,1)}, bf16[272,1024]{1,0:T(8,128)(2,1)S(1)}, u32[]{:S(2)}) copy-start(bf16[272,1024]{1,0:T(8,128)(2,1)S(1)} %collective-permute-done.refs_4_) | copy-start | bytes 1671172
  23.3 51.2 %collective-permute-start.3 = (bf16[2048,768]{1,0:T(8,128)(2,1)}, bf16[2048,768]{1,0:T(8,128)(2,1)}, u32[]{:S(2)}, u32[]{:S(2)}) collective-permute-start(bf16[2048,768]{1,0:T(8,128)(2,1)} %get-tuple-element.46.refs_0_), channel_id=1, source_target_pairs={{0,16},{16,0},{1,17},{17,1},{2,18},{18,2},{3,19},{19,3},{4,20},{20... | collective-permute-start | bytes 9437192 | tf_op jit(solution)/shard_map/ppermute | solution.py:440
  23.3 15.4 %collective-permute-start.5 = (bf16[272,1024]{1,0:T(8,128)(2,1)}, bf16[272,1024]{1,0:T(8,128)(2,1)}, u32[]{:S(2)}, u32[]{:S(2)}) collective-permute-start(bf16[272,1024]{1,0:T(8,128)(2,1)} %collective-permute-done.1.refs_6_), channel_id=1, source_target_pairs={{0,1},{1,0},{2,3},{3,2},{4,5},{5,4},{6,7},{7,6},{8,9},{9,8},{10,11... | collective-permute-start | bytes 1671176 | tf_op jit(solution)/shard_map/ppermute | solution.py:437
  23.8 14.8 %collective-permute-start.7 = (bf16[272,1024]{1,0:T(8,128)(2,1)S(1)}, bf16[272,1024]{1,0:T(8,128)(2,1)S(1)}, u32[]{:S(2)}, u32[]{:S(2)}) collective-permute-start(bf16[272,1024]{1,0:T(8,128)(2,1)S(1)} %collective-permute-done.refs_4_), channel_id=1, source_target_pairs={{0,2},{2,0},{4,6},{6,4},{8,10},{10,8},{12,14},{14,12},{1,3},{3,1},... | collective-permute-start | bytes 1671176 | tf_op jit(solution)/shard_map/ppermute | solution.py:443
  24.4 16.3 %collective-permute-start.6 = (bf16[272,1024]{1,0:T(8,128)(2,1)S(1)}, bf16[272,1024]{1,0:T(8,128)(2,1)S(1)}, u32[]{:S(2)}, u32[]{:S(2)}) collective-permute-start(bf16[272,1024]{1,0:T(8,128)(2,1)S(1)} %collective-permute-done.refs_4_), channel_id=1, source_target_pairs={{0,4},{2,6},{4,8},{6,10},{8,12},{10,14},{12,0},{14,2},{1,5},{3,7},... | collective-permute-start | bytes 1671176 | tf_op jit(solution)/shard_map/ppermute | solution.py:446
  24.4 50.1 %collective-permute-start.4 = (bf16[384,2048]{1,0:T(8,128)(2,1)}, bf16[384,2048]{1,0:T(8,128)(2,1)}, u32[]{:S(2)}, u32[]{:S(2)}) collective-permute-start(bf16[384,2048]{1,0:T(8,128)(2,1)} %get-tuple-element.47.refs_2_), channel_id=1, source_target_pairs={{0,16},{16,0},{1,17},{17,1},{2,18},{18,2},{3,19},{19,3},{4,20},{20... | collective-permute-start | bytes 4718600 | tf_op jit(solution)/shard_map/ppermute | solution.py:440
  38.7 17.0 %copy-start.11 = (bf16[272,1024]{1,0:T(8,128)(2,1)}, bf16[272,1024]{1,0:T(8,128)(2,1)S(1)}, u32[]{:S(2)}) copy-start(bf16[272,1024]{1,0:T(8,128)(2,1)S(1)} %collective-permute-done.7.refs_6_) | copy-start | bytes 1671172
  40.6 15.7 %copy-start.13 = (bf16[272,1024]{1,0:T(8,128)(2,1)}, bf16[272,1024]{1,0:T(8,128)(2,1)S(1)}, u32[]{:S(2)}) copy-start(bf16[272,1024]{1,0:T(8,128)(2,1)S(1)} %collective-permute-done.6.refs_8_) | copy-start | bytes 1671172
  40.6 13.7 %collective-permute-start.10 = (bf16[272,1024]{1,0:T(8,128)(2,1)S(1)}, bf16[272,1024]{1,0:T(8,128)(2,1)}, u32[]{:S(2)}, u32[]{:S(2)}) collective-permute-start(bf16[272,1024]{1,0:T(8,128)(2,1)S(1)} %fusion.7.refs_4_), channel_id=1, source_target_pairs={{0,12},{2,14},{4,0},{6,2},{8,4},{10,6},{12,8},{14,10},{1,13},{3,15... | collective-permute-start | bytes 1671176 | tf_op jit(solution)/shard_map/ppermute | solution.py:446
  40.6 13.8 %collective-permute-start.9 = (bf16[272,1024]{1,0:T(8,128)(2,1)S(1)}, bf16[272,1024]{1,0:T(8,128)(2,1)S(1)}, u32[]{:S(2)}, u32[]{:S(2)}) collective-permute-start(bf16[272,1024]{1,0:T(8,128)(2,1)S(1)} %collective-permute-done.6.refs_8_), channel_id=1, source_target_pairs={{0,2},{2,0},{4,6},{6,4},{8,10},{10,8},{12,14},{14,12},{1,3},{3,1},... | collective-permute-start | bytes 1671176 | tf_op jit(solution)/shard_map/ppermute | solution.py:443
  42.2 13.4 %collective-permute-start.8 = (bf16[272,1024]{1,0:T(8,128)(2,1)S(1)}, bf16[272,1024]{1,0:T(8,128)(2,1)}, u32[]{:S(2)}, u32[]{:S(2)}) collective-permute-start(bf16[272,1024]{1,0:T(8,128)(2,1)S(1)} %collective-permute-done.6.refs_8_), channel_id=1, source_target_pairs={{0,1},{1,0},{2,3},{3,2},{4,5},{5,4},{6,7},{7,6},{8,9},{9,8},{10,11... | collective-permute-start | bytes 1671176 | tf_op jit(solution)/shard_map/ppermute | solution.py:437
  54.5 3.2 %copy-start.16 = (bf16[272,1024]{1,0:T(8,128)(2,1)}, bf16[272,1024]{1,0:T(8,128)(2,1)S(1)}, u32[]{:S(2)}) copy-start(bf16[272,1024]{1,0:T(8,128)(2,1)S(1)} %collective-permute-done.9.refs_10_) | copy-start | bytes 1671172
  55.7 12.6 %collective-permute-start.11 = (bf16[272,1024]{1,0:T(8,128)(2,1)}, bf16[272,1024]{1,0:T(8,128)(2,1)S(1)}, u32[]{:S(2)}, u32[]{:S(2)}) collective-permute-start(bf16[272,1024]{1,0:T(8,128)(2,1)} %collective-permute-done.8.refs_9_), channel_id=1, source_target_pairs={{0,2},{2,0},{4,6},{6,4},{8,10},{10,8},{12,14},{14,12},{1,3},{3,1},... | collective-permute-start | bytes 1671176 | tf_op jit(solution)/shard_map/ppermute | solution.py:443
  56.3 12.3 %collective-permute-start.17 = (bf16[272,1024]{1,0:T(8,128)(2,1)S(1)}, bf16[272,1024]{1,0:T(8,128)(2,1)S(1)}, u32[]{:S(2)}, u32[]{:S(2)}) collective-permute-start(bf16[272,1024]{1,0:T(8,128)(2,1)S(1)} %collective-permute-done.refs_4_), channel_id=1, source_target_pairs={{0,1},{1,0},{2,3},{3,2},{4,5},{5,4},{6,7},{7,6},{8,9},{9,8},{10,11... | collective-permute-start | bytes 1671176 | tf_op jit(solution)/shard_map/ppermute | solution.py:437
  57.7 14.0 %collective-permute-start.18 = (bf16[272,1024]{1,0:T(8,128)(2,1)}, bf16[272,1024]{1,0:T(8,128)(2,1)S(1)}, u32[]{:S(2)}, u32[]{:S(2)}) collective-permute-start(bf16[272,1024]{1,0:T(8,128)(2,1)} %collective-permute-done.5.refs_7_), channel_id=1, source_target_pairs={{0,4},{2,6},{4,8},{6,10},{8,12},{10,14},{12,0},{14,2},{1,5},{3,7},... | collective-permute-start | bytes 1671176 | tf_op jit(solution)/shard_map/ppermute | solution.py:446
  68.3 6.2 %copy-start.17 = (bf16[272,1024]{1,0:T(8,128)(2,1)}, bf16[272,1024]{1,0:T(8,128)(2,1)S(1)}, u32[]{:S(2)}) copy-start(bf16[272,1024]{1,0:T(8,128)(2,1)S(1)} %collective-permute-done.11.refs_11_) | copy-start | bytes 1671172
  68.6 0.8 copy-start.14
  71.7 0.8 copy-start.15
  72.5 18.6 %collective-permute-start.20 = (bf16[272,1024]{1,0:T(8,128)(2,1)}, bf16[272,1024]{1,0:T(8,128)(2,1)}, u32[]{:S(2)}, u32[]{:S(2)}) collective-permute-start(bf16[272,1024]{1,0:T(8,128)(2,1)} %collective-permute-done.10.refs_8_), channel_id=1, source_target_pairs={{0,2},{2,0},{4,6},{6,4},{8,10},{10,8},{12,14},{14,12},{1,3},{3,1},... | collective-permute-start | bytes 1671176 | tf_op jit(solution)/shard_map/ppermute | solution.py:443
  73.9 17.2 %collective-permute-start.19 = (bf16[272,1024]{1,0:T(8,128)(2,1)}, bf16[272,1024]{1,0:T(8,128)(2,1)}, u32[]{:S(2)}, u32[]{:S(2)}) collective-permute-start(bf16[272,1024]{1,0:T(8,128)(2,1)} %collective-permute-done.10.refs_8_), channel_id=1, source_target_pairs={{0,1},{1,0},{2,3},{3,2},{4,5},{5,4},{6,7},{7,6},{8,9},{9,8},{10,11... | collective-permute-start | bytes 1671176 | tf_op jit(solution)/shard_map/ppermute | solution.py:437
  74.4 16.7 %collective-permute-start.21 = (bf16[272,1024]{1,0:T(8,128)(2,1)}, bf16[272,1024]{1,0:T(8,128)(2,1)}, u32[]{:S(2)}, u32[]{:S(2)}) collective-permute-start(bf16[272,1024]{1,0:T(8,128)(2,1)} %collective-permute-done.5.refs_7_), channel_id=1, source_target_pairs={{0,12},{2,14},{4,0},{6,2},{8,4},{10,6},{12,8},{14,10},{1,13},{3,15... | collective-permute-start | bytes 1671176 | tf_op jit(solution)/shard_map/ppermute | solution.py:446
  88.4 17.0 %collective-permute-start.12 = (bf16[2,144,1024]{2,1,0:T(8,128)(2,1)}, bf16[2,144,1024]{2,1,0:T(8,128)(2,1)S(1)}, u32[]{:S(2)}, u32[]{:S(2)}) collective-permute-start(bf16[2,144,1024]{2,1,0:T(8,128)(2,1)} %get-tuple-element.57), channel_id=1, source_target_pairs={{0,1},{1,0},{2,3},{3,2},{4,5},{5,4},{6,7},{7,6},{8,9},{9,8},{10,11... | collective-permute-start | bytes 1769480 | tf_op jit(solution)/shard_map/ppermute | solution.py:437
  90.0 15.5 %collective-permute-start.14 = (bf16[2,144,1024]{2,1,0:T(8,128)(2,1)}, bf16[2,144,1024]{2,1,0:T(8,128)(2,1)}, u32[]{:S(2)}, u32[]{:S(2)}) collective-permute-start(bf16[2,144,1024]{2,1,0:T(8,128)(2,1)} %get-tuple-element.59), channel_id=1, source_target_pairs={{0,2},{2,0},{4,6},{6,4},{8,10},{10,8},{12,14},{14,12},{1,3},{3,1},... | collective-permute-start | bytes 1769480 | tf_op jit(solution)/shard_map/ppermute | solution.py:443
  91.1 28.0 %collective-permute-start.24 = (bf16[288,5248]{1,0:T(8,128)(2,1)}, bf16[288,5248]{1,0:T(8,128)(2,1)}, u32[]{:S(2)}, u32[]{:S(2)}) collective-permute-start(bf16[288,5248]{1,0:T(8,128)(2,1)} %get-tuple-element.73), channel_id=1, source_target_pairs={{0,16},{16,0},{1,17},{17,1},{2,18},{18,2},{3,19},{19,3},{4,20},{20... | collective-permute-start | bytes 9068552 | tf_op jit(solution)/shard_map/ppermute | solution.py:440
  91.1 14.9 %copy-start.5 = (bf16[2,144,1024]{2,1,0:T(8,128)(2,1)S(1)}, bf16[2,144,1024]{2,1,0:T(8,128)(2,1)}, u32[]{:S(2)}) copy-start(bf16[2,144,1024]{2,1,0:T(8,128)(2,1)} %get-tuple-element.58) | copy-start | bytes 1769476
  91.1 16.9 %copy-start.2 = (bf16[2,144,1024]{2,1,0:T(8,128)(2,1)S(1)}, bf16[2,144,1024]{2,1,0:T(8,128)(2,1)}, u32[]{:S(2)}) copy-start(bf16[2,144,1024]{2,1,0:T(8,128)(2,1)} %get-tuple-element.56) | copy-start | bytes 1769476
  105.4 3.3 %copy-start.9 = (bf16[2,144,1024]{2,1,0:T(8,128)(2,1)S(1)}, bf16[2,144,1024]{2,1,0:T(8,128)(2,1)}, u32[]{:S(2)}) copy-start(bf16[2,144,1024]{2,1,0:T(8,128)(2,1)} %get-tuple-element.71) | copy-start | bytes 1769476
  105.4 11.6 %copy-start.8 = (bf16[2,144,1024]{2,1,0:T(8,128)(2,1)S(1)}, bf16[2,144,1024]{2,1,0:T(8,128)(2,1)}, u32[]{:S(2)}) copy-start(bf16[2,144,1024]{2,1,0:T(8,128)(2,1)} %get-tuple-element.72) | copy-start | bytes 1769476
  105.4 14.8 %collective-permute-start.25 = (bf16[288,5248]{1,0:T(8,128)(2,1)}, bf16[288,5248]{1,0:T(8,128)(2,1)S(1)}, u32[]{:S(2)}, u32[]{:S(2)}) collective-permute-start(bf16[288,5248]{1,0:T(8,128)(2,1)} %get-tuple-element.75), channel_id=1, source_target_pairs={{0,16},{16,0},{1,17},{17,1},{2,18},{18,2},{3,19},{19,3},{4,20},{20... | collective-permute-start | bytes 9068552 | tf_op jit(solution)/shard_map/ppermute | solution.py:440
  107.0 9.9 %collective-permute-start.15 = (bf16[144,1024]{1,0:T(8,128)(2,1)S(1)}, bf16[144,1024]{1,0:T(8,128)(2,1)S(1)}, u32[]{:S(2)}, u32[]{:S(2)}) collective-permute-start(bf16[144,1024]{1,0:T(8,128)(2,1)S(1)} %fusion.9), channel_id=1, source_target_pairs={{0,1},{1,0},{2,3},{3,2},{4,5},{5,4},{6,7},{7,6},{8,9},{9,8},{10,11... | collective-permute-start | bytes 884744 | tf_op jit(solution)/shard_map/ppermute | solution.py:437
  108.1 23.1 %collective-permute-start.13 = (bf16[144,1024]{1,0:T(8,128)(2,1)S(1)}, bf16[144,1024]{1,0:T(8,128)(2,1)S(1)}, u32[]{:S(2)}, u32[]{:S(2)}) collective-permute-start(bf16[144,1024]{1,0:T(8,128)(2,1)S(1)} %fusion.8), channel_id=1, source_target_pairs={{0,2},{2,0},{4,6},{6,4},{8,10},{10,8},{12,14},{14,12},{1,3},{3,1},... | collective-permute-start | bytes 884744 | tf_op jit(solution)/shard_map/ppermute | solution.py:443
  108.7 22.5 %collective-permute-start.22 = (bf16[2,144,1024]{2,1,0:T(8,128)(2,1)S(1)}, bf16[2,144,1024]{2,1,0:T(8,128)(2,1)S(1)}, u32[]{:S(2)}, u32[]{:S(2)}) collective-permute-start(bf16[2,144,1024]{2,1,0:T(8,128)(2,1)S(1)} %copy-done.9), channel_id=1, source_target_pairs={{0,1},{1,0},{2,3},{3,2},{4,5},{5,4},{6,7},{7,6},{8,9},{9,8},{10,11... | collective-permute-start | bytes 1769480 | tf_op jit(solution)/shard_map/ppermute | solution.py:437
  117.0 14.2 %collective-permute-start.23 = (bf16[2,144,1024]{2,1,0:T(8,128)(2,1)S(1)}, bf16[2,144,1024]{2,1,0:T(8,128)(2,1)S(1)}, u32[]{:S(2)}, u32[]{:S(2)}) collective-permute-start(bf16[2,144,1024]{2,1,0:T(8,128)(2,1)S(1)} %copy-done.8), channel_id=1, source_target_pairs={{0,2},{2,0},{4,6},{6,4},{8,10},{10,8},{12,14},{14,12},{1,3},{3,1},... | collective-permute-start | bytes 1769480 | tf_op jit(solution)/shard_map/ppermute | solution.py:443
  117.9 13.3 %copy-start.4 = (bf16[2,144,1024]{2,1,0:T(8,128)(2,1)S(1)}, bf16[2,144,1024]{2,1,0:T(8,128)(2,1)}, u32[]{:S(2)}) copy-start(bf16[2,144,1024]{2,1,0:T(8,128)(2,1)} %get-tuple-element.79) | copy-start | bytes 1769476
  117.9 14.4 %copy-start.3 = (bf16[2,144,1024]{2,1,0:T(8,128)(2,1)S(1)}, bf16[2,144,1024]{2,1,0:T(8,128)(2,1)}, u32[]{:S(2)}) copy-start(bf16[2,144,1024]{2,1,0:T(8,128)(2,1)} %get-tuple-element.66) | copy-start | bytes 1769476
  119.1 18.9 %collective-permute-start.16 = (bf16[144,1024]{1,0:T(8,128)(2,1)S(1)}, bf16[144,1024]{1,0:T(8,128)(2,1)S(1)}, u32[]{:S(2)}, u32[]{:S(2)}) collective-permute-start(bf16[144,1024]{1,0:T(8,128)(2,1)S(1)} %fusion.3), channel_id=1, source_target_pairs={{0,8},{2,10},{4,12},{6,14},{8,0},{10,2},{12,4},{14,6},{1,9},{3,11}... | collective-permute-start | bytes 884744 | tf_op jit(solution)/shard_map/ppermute | solution.py:446
  120.2 1.9 %copy-start = (bf16[288,5248]{1,0:T(8,128)(2,1)S(1)}, bf16[288,5248]{1,0:T(8,128)(2,1)}, u32[]{:S(2)}) copy-start(bf16[288,5248]{1,0:T(8,128)(2,1)} %get-tuple-element.65.refs_12_.refs_0_) | copy-start | bytes 9068548
  122.1 1.9 %copy-start.1 = (bf16[288,5248]{1,0:T(8,128)(2,1)S(1)}, bf16[288,5248]{1,0:T(8,128)(2,1)}, u32[]{:S(2)}) copy-start(bf16[288,5248]{1,0:T(8,128)(2,1)} %get-tuple-element.74.refs_2_) | copy-start | bytes 9068548
  131.3 6.8 %collective-permute-start.27 = (bf16[144,1024]{1,0:T(8,128)(2,1)S(1)}, bf16[144,1024]{1,0:T(8,128)(2,1)S(1)}, u32[]{:S(2)}, u32[]{:S(2)}) collective-permute-start(bf16[144,1024]{1,0:T(8,128)(2,1)S(1)} %fusion.11), channel_id=1, source_target_pairs={{0,1},{1,0},{2,3},{3,2},{4,5},{5,4},{6,7},{7,6},{8,9},{9,8},{10,11... | collective-permute-start | bytes 884744 | tf_op jit(solution)/shard_map/ppermute | solution.py:437
  132.3 6.8 %collective-permute-start.26 = (bf16[144,1024]{1,0:T(8,128)(2,1)S(1)}, bf16[144,1024]{1,0:T(8,128)(2,1)S(1)}, u32[]{:S(2)}, u32[]{:S(2)}) collective-permute-start(bf16[144,1024]{1,0:T(8,128)(2,1)S(1)} %fusion.10), channel_id=1, source_target_pairs={{0,2},{2,0},{4,6},{6,4},{8,10},{10,8},{12,14},{14,12},{1,3},{3,1},... | collective-permute-start | bytes 884744 | tf_op jit(solution)/shard_map/ppermute | solution.py:443
  139.4 14.4 %copy-start.7 = (s32[128,8]{0,1:T(8,128)S(1)}, s32[128,8]{0,1:T(8,128)}, u32[]{:S(2)}) copy-start(s32[128,8]{0,1:T(8,128)} %param.9) | copy-start | bytes 12292
  139.4 9.9 %collective-permute-start.28 = (bf16[144,1024]{1,0:T(8,128)(2,1)S(1)}, bf16[144,1024]{1,0:T(8,128)(2,1)S(1)}, u32[]{:S(2)}, u32[]{:S(2)}) collective-permute-start(bf16[144,1024]{1,0:T(8,128)(2,1)S(1)} %fusion.2), channel_id=1, source_target_pairs={{0,12},{2,14},{4,0},{6,2},{8,4},{10,6},{12,8},{14,10},{1,13},{3,15... | collective-permute-start | bytes 884744 | tf_op jit(solution)/shard_map/ppermute | solution.py:446
  142.5 10.3 %collective-permute-start.29 = (bf16[144,1024]{1,0:T(8,128)(2,1)S(1)}, bf16[144,1024]{1,0:T(8,128)(2,1)S(1)}, u32[]{:S(2)}, u32[]{:S(2)}) collective-permute-start(bf16[144,1024]{1,0:T(8,128)(2,1)S(1)} %fusion.1), channel_id=1, source_target_pairs={{0,4},{2,6},{4,8},{6,10},{8,12},{10,14},{12,0},{14,2},{1,5},{3,7},... | collective-permute-start | bytes 884744 | tf_op jit(solution)/shard_map/ppermute | solution.py:446

commit v8 on v7

--- a/solution.py
+++ b/solution.py
@@ -163,10 +163,11 @@
     )(which, w_gate, w_up, w_down)
 
 
-def rows_kernel(count, modes, capacity, slots, where_ref, *refs):
-    weights_in, units_in = refs[:4], refs[4 : 4 + 4 * count]
-    refs = refs[len(refs) - 17 - 2 * count :]
-    outs, keeps, sends, refs = refs[:2], refs[2 : 2 + count], refs[2 + count : 2 + 2 * count], refs[2 + 2 * count :]
+def rows_kernel(count, ways, capacity, slots, where_ref, *refs):
+    weights_in, units_in, tables_in = refs[:4], refs[4 : 4 + 4 * count], refs[4 + 4 * count : 4 + 5 * count]
+    leaves = 1 + max(way[0] for way in ways.values())
+    refs = refs[len(refs) - 17 - leaves :]
+    outs, packets, refs = refs[:2], refs[2 : 2 + leaves], refs[2 + leaves :]
     x_all, g_all, tables, wgu0, wgu1, wd0, wd1, xc, gc, both, scaled, piece, unit_sems, weight_sems = refs[:14]
     out_sems = refs[14]
     half, tok = x_all.shape[3], x_all.shape[2] // 2
@@ -174,15 +175,15 @@
     owners = tables.shape[2]
     wgu, wd = (wgu0, wgu1), (wd0, wd1)
 
-    x_copies, g_copies, t_copies = [], [], []
+    x_copies, g_copies = [], []
     for index, unit in enumerate(units_in):
         chunk, y, x = index // 4, index // 2 % 2, index % 2
         rows = pl.ds(y * tok, tok)
         x_copies.append(pltpu.make_async_copy(unit.at[pl.ds(0, tok)], x_all.at[chunk, x, rows], unit_sems.at[0, index]))
         g_copies.append(pltpu.make_async_copy(unit.at[pl.ds(tok, tok)], g_all.at[chunk, x, rows], unit_sems.at[1, index]))
-        if x == 0:
-            table = unit.at[pl.ds(2 * tok, owners), pl.ds(0, tok)]
-            t_copies.append(pltpu.make_async_copy(table, tables.at[chunk, y], unit_sems.at[2, index]))
+    t_copies = [
+        pltpu.make_async_copy(table, tables.at[chunk], unit_sems.at[2, chunk]) for chunk, table in enumerate(tables_in)
+    ]
     weight_copies = [
         pltpu.make_async_copy(source, target, weight_sems.at[index])
         for index, (source, target) in enumerate(zip(weights_in, (wgu0, wgu1, wd0, wd1)))
@@ -290,39 +291,40 @@
                 total = term if total is None else total + term
             for y in range(2):
                 piece[chunk, side, y, :tok] = total[y * tok : (y + 1) * tok].astype(jnp.bfloat16)
-                first, second = (y, side) if modes[chunk] else (side, y)
-                leave(piece.at[chunk, side, y], (sends if first else keeps)[chunk].at[second])
+                number, slot = ways[chunk, y, side]
+                leave(piece.at[chunk, side, y], packets[number].at[slot])
     for copy in leaving:
         copy.wait()
 
 
-def rows_call(modes, owners, capacity, slots, where, weights, units, after):
-    count = len(modes)
-    tok, half = (units[0].shape[0] - owners) // 2, units[0].shape[1]
+def rows_call(items, owners, capacity, slots, where, weights, units, tables, after):
+    count = len(tables)
+    ways = {block: (number, slot) for number, blocks in enumerate(items) for slot, block in enumerate(blocks)}
+    tok, half = units[0].shape[0] // 2, units[0].shape[1]
     part, width = weights[2].shape
     widths = (width, width, 2 * part, part)
-    packet = (2, tok + owners, half)
+    packet = (tok + owners, half)
     return pl.pallas_call(
-        functools.partial(rows_kernel, count, modes, capacity, slots),
+        functools.partial(rows_kernel, count, ways, capacity, slots),
         grid_spec=pltpu.PrefetchScalarGridSpec(
             num_scalar_prefetch=1,
             grid=(1,),
-            in_specs=[LOOSE] * (4 + len(units) + len(after)),
-            out_specs=[LOOSE] * (2 + 2 * count),
+            in_specs=[LOOSE] * (4 + 5 * count + len(after)),
+            out_specs=[LOOSE] * (2 + len(items)),
             scratch_shapes=[pltpu.VMEM((count, 2, 2 * tok, half), jnp.bfloat16)] * 2
             + [pltpu.VMEM((count, 2, owners, tok), jnp.bfloat16)]
             + [pltpu.VMEM((width, 2 * part), jnp.bfloat16)] * 2
             + [pltpu.VMEM((part, width), jnp.bfloat16)] * 2
             + [pltpu.VMEM((2, count * slots, size), jnp.bfloat16) for size in widths]
             + [
-                pltpu.VMEM((count, 2) + packet, jnp.bfloat16),
+                pltpu.VMEM((count, 2, 2) + packet, jnp.bfloat16),
                 pltpu.SemaphoreType.DMA((3, 4 * count)),
                 pltpu.SemaphoreType.DMA((4,)),
                 pltpu.SemaphoreType.DMA((8 + 4 * count,)),
             ],
         ),
         out_shape=[jax.ShapeDtypeStruct((count * slots, sum(widths)), jnp.bfloat16)] * 2
-        + [jax.ShapeDtypeStruct(packet, jnp.bfloat16)] * (2 * count),
+        + [jax.ShapeDtypeStruct((len(blocks),) + packet, jnp.bfloat16) for blocks in items],
         compiler_params=pltpu.CompilerParams(vmem_limit_bytes=62 << 20),
         cost_estimate=pl.CostEstimate(
             flops=count * (20 * slots * width * part + 24 * slots * tok * width),
@@ -330,13 +332,13 @@
             transcendentals=2 * count * slots * part,
         ),
         name="rows",
-    )(where, *weights, *units, *after)
+    )(where, *weights, *units, *tables, *after)
 
 
 def grads_kernel(count, wide, deep, blocks, tp_ref, *refs):
     sources, outs = refs[:count], refs[count:-4]
     wide_all, deep_all, wide_sems, deep_sems = refs[-4:]
-    rows = sources[0].shape[0]
+    starts = [sum(source.shape[0] for source in sources[:index]) for index in range(count)]
     size = wide_all.shape[2]
     block = pl.program_id(0)
 
@@ -344,7 +346,7 @@
         return [
             pltpu.make_async_copy(
                 source.at[:, pl.ds(wide + column * size, size)],
-                wide_all.at[column, pl.ds(index * rows, rows)],
+                wide_all.at[column, pl.ds(starts[index], source.shape[0])],
                 wide_sems.at[column, index],
             )
             for index, source in enumerate(sources)
@@ -354,7 +356,9 @@
     def _():
         deep_copies = [
             pltpu.make_async_copy(
-                source.at[:, pl.ds(deep, deep_all.shape[1])], deep_all.at[pl.ds(index * rows, rows)], deep_sems.at[index]
+                source.at[:, pl.ds(deep, deep_all.shape[1])],
+                deep_all.at[pl.ds(starts[index], source.shape[0])],
+                deep_sems.at[index],
             )
             for index, source in enumerate(sources)
         ]
@@ -385,7 +389,7 @@
 
 
 def grads_call(which, packed, width, part, down):
-    rows, count = packed[0].shape[0], len(packed)
+    rows, count = sum(item.shape[0] for item in packed), len(packed)
     step = math.gcd(width // 2, 512)
     per = width // 2 // step
     deep = part if down else 2 * part
@@ -408,8 +412,8 @@
             in_specs=[LOOSE] * count,
             out_specs=specs,
             scratch_shapes=[
-                pltpu.VMEM((2 * per, count * rows, step), jnp.bfloat16),
-                pltpu.VMEM((count * rows, deep), jnp.bfloat16),
+                pltpu.VMEM((2 * per, rows, step), jnp.bfloat16),
+                pltpu.VMEM((rows, deep), jnp.bfloat16),
                 pltpu.SemaphoreType.DMA((2 * per, count)),
                 pltpu.SemaphoreType.DMA((count,)),
             ],
@@ -417,7 +421,7 @@
         out_shape=[jax.ShapeDtypeStruct(shape, jnp.bfloat16) for shape in shapes],
         compiler_params=pltpu.CompilerParams(vmem_limit_bytes=24 << 20),
         cost_estimate=pl.CostEstimate(
-            flops=2 * count * rows * width * deep, bytes_accessed=2 * count * rows * (width + deep), transcendentals=0
+            flops=2 * rows * width * deep, bytes_accessed=2 * rows * (width + deep), transcendentals=0
         ),
         name="grads",
     )(which, *packed)
@@ -448,9 +452,6 @@
     def tied(values, others):
         return lax.optimization_barrier((list(values), list(others)))[0]
 
-    chosen = routes[:, :, None] == jnp.arange(owners, dtype=jnp.int32)
-    table = jnp.sum(jnp.where(chosen, probs[:, :, None].astype(jnp.float32) + 1.0, 0.0), axis=1) - 1.0
-    table = jnp.pad(table.astype(jnp.bfloat16).T, ((0, 0), (0, half - tok_rows)))
     last = n_z - 1
     routes_in = []
     for z in range(n_z):
@@ -479,52 +480,69 @@
         waiting = [item for item in waiting if item[0] not in there]
 
     which_ref = which.reshape(1).astype(jnp.int32)
+    where = jnp.stack([role * ep + place, (1 - role) * ep + place, which]).astype(jnp.int32)
     both_w, down_w = weights_call(which_ref, w_gate, w_up, w_down)
-    units = {(0, 0, 0): jnp.concatenate([tokens, out_grad, table], 0)}
-    settled, extra, weights = dict(units), [both_w, down_w], ()
-    for moves in rounds:
+    width, part = both_w.shape[0], down_w.shape[0]
+
+    def rows_of(steps, items, after):
+        four = [units[z, y, x] for z in steps for y in range(2) for x in range(2)]
+        return rows_call(items, owners, capacity, slots, where, weights, four, [tables[z] for z in steps], after)
+
+    units = {(0, 0, 0): jnp.concatenate([tokens, out_grad], 0)}
+    settled = dict(units)
+    for number, moves in enumerate(rounds):
         arrived = {target: move(settled[source]) for target, source, move in moves}
         units.update(arrived)
         settled.update(arrived)
+        extra = []
+        if number == 0:
+            extra = [both_w, down_w]
+            both_w, down_w, routes, probs = tied([both_w, down_w, routes, probs], arrived.values())
+            weights = (both_w, over_role(both_w), down_w, over_role(down_w))
+            chosen = routes[:, :, None] == jnp.arange(owners, dtype=jnp.int32)
+            table = jnp.sum(jnp.where(chosen, probs[:, :, None].astype(jnp.float32) + 1.0, 0.0), axis=1) - 1.0
+            table = table.astype(jnp.bfloat16).T
+            table = jnp.stack([table, over_y(table)])
+        if number == 1:
+            (table,) = tied([table], arrived.values())
+            tables = [over_z(table, z) if z else table for z in range(n_z)]
+        if number == 2:
+            mine_0, other_0, near, side_0, far, y_0 = rows_of(
+                [0], [[(0, 0, 0)], [(0, 0, 1)], [(0, 1, 1)], [(0, 1, 0)]], []
+            )
+            extra = [mine_0]
         names = list(settled)
         settled = dict(zip(names, tied([settled[item] for item in names], extra)))
-        if extra:
-            both_w, down_w = tied(extra, arrived.values())
-            weights, extra = (both_w, over_role(both_w), down_w, over_role(down_w)), []
-
-    where = jnp.stack([role * ep + place, (1 - role) * ep + place, which]).astype(jnp.int32)
-
-    def add(a, b):
-        return a.astype(jnp.float32) + b.astype(jnp.float32)
-
-    width, part = both_w.shape[0], down_w.shape[0]
-    packed, flown, homeward, done = [], [], [], []
-    for turn, group in enumerate((range(0, n_z, 2), range(1, n_z, 2))):
-        modes = [index % 2 for index in range(len(group))]
-        four = [units[z, y, x] for z in group for y in range(2) for x in range(2)]
-        mine, other, *packets = rows_call(modes, owners, capacity, slots, where, weights, four, packed[:1])
-        keeps, sends = packets[: len(group)], packets[len(group) :]
-        if turn:
-            mine, other, *sends = tied([mine, other] + sends, flown[0])
-        packed += [mine, over_role(other)]
-        firsts = [over_y(send) if mode else over_x(send) for mode, send in zip(modes, sends)]
-        if turn:
-            done += grads_call(which_ref, packed, width, part, False)
-            firsts = tied(firsts, flown[1] + done)
-        sends = [add(keep[1], first[1]).astype(jnp.bfloat16) for keep, first in zip(keeps, firsts)]
-        seconds = [over_x(send) if mode else over_y(send) for mode, send in zip(modes, sends)]
-        if turn:
-            done += grads_call(which_ref, packed, width, part, True)
-            seconds = tied(seconds, homeward[1:] + done)
-        totals = [add(add(keep[0], first[0]), second) for keep, first, second in zip(keeps, firsts, seconds)]
-        sends = [total.astype(jnp.bfloat16) for total in totals]
-        thirds = [over_z(send, -z) if z else total for z, send, total in zip(group, sends, totals)]
-        homeward += thirds
-        flown += [firsts, seconds]
-    home = sum(item.astype(jnp.float32) for item in homeward)
-    d_tok = home[:tok_rows].astype(jnp.bfloat16)
-    d_gate, d_up, d_down = done
-    score = jnp.sum(home[tok_rows:, : 4 * tok_rows].reshape(owners, 4, tok_rows), axis=1).T
+
+    def total(*blocks):
+        return sum(block.astype(jnp.float32) for block in blocks).astype(jnp.bfloat16)
+
+    items = [[(1, 1, 1)], [(1, 0, 1), (0, 0, 1)], [(0, 1, 0)], [(0, 1, 1)], [(0, 0, 0)], [(1, 0, 0)], [(1, 1, 0)]]
+    mine_1, other_1, x_2, x_12, y_1, z_1, keep_1, keep_2, keep_2y = rows_of([1, 2], items, [])
+    other_1, x_2, x_12, y_1, z_1 = tied([other_1, x_2, x_12, y_1, z_1], arrived.values())
+    from_x2, from_y1, from_z1 = over_x(x_2), over_y(y_1), over_z(z_1, -1)
+    from_x12 = over_x(x_12)
+    items = [[(0, 0, 1)], [(0, 1, 0)], [(0, 1, 1)], [(0, 0, 0)]]
+    mine_3, other_3, x_3, y_3, z_3, keep_3 = rows_of([3], items, [mine_1])
+    mine_3, other_3, x_3, y_3, z_3, keep_2y = tied(
+        [mine_3, other_3, x_3, y_3, z_3, keep_2y], [from_x2, from_y1, from_z1]
+    )
+    from_z3, from_x3, from_y2, from_y3 = over_z(z_3, 1), over_x(x_3), over_y(total(keep_2y, from_x2)), over_y(y_3)
+    packed = [mine_0, over_role(other_0), mine_1, over_role(other_1), mine_3, over_role(other_3)]
+    d_gate, d_up = grads_call(which_ref, packed, width, part, False)
+    from_z3, from_x12, from_y2 = tied([from_z3, from_x12, from_y2], [d_gate, d_up])
+    from_far = over_y(total(far, from_z1, from_z3))
+    from_z2 = over_z(total(keep_2, from_x12[:1], from_y2), 1)
+    home_1 = over_z(total(keep_1, from_x12[1:], from_y1), -1)
+    (d_down,) = grads_call(which_ref, packed, width, part, True)
+    from_x3, from_y3, from_z2, y_0 = tied([from_x3, from_y3, from_z2, y_0], [d_down])
+    from_y0 = over_y(y_0)
+    home_3 = over_z(total(keep_3, from_x3, from_y3, from_z2), 1)
+    from_x0 = over_x(total(side_0, from_far))
+    home = (near, from_y0, home_1, home_3, from_x0)
+    d_tok = sum(block[0, :tok_rows].astype(jnp.float32) for block in home).astype(jnp.bfloat16)
+    home = sum(block[0, tok_rows:, : 4 * tok_rows].astype(jnp.float32) for block in home)
+    score = jnp.sum(home.reshape(owners, 4, tok_rows), axis=1).T
     d_probs = jnp.sum(jnp.where(chosen, score[:, None, :], 0.0), axis=2)
     return d_tok, d_probs, d_gate, d_up, d_down
 
@@ -532,7 +550,7 @@
 def per_device(tokens, out_grad, routes, probs, w_gate, w_up, w_down):
     owners = lax.axis_size(("role", "ep"))
     tok_rows, top_count = routes.shape
-    paired = lax.axis_size("tp") == 2 and lax.axis_size("role") == 2 and lax.axis_size("ep") % 4 == 0
+    paired = lax.axis_size("tp") == 2 and lax.axis_size("role") == 2 and lax.axis_size("ep") == 8
     if paired and 2 * slot_capacity(tok_rows, top_count, owners) >= tok_rows:
         return dense_device(tokens, out_grad, routes, probs, w_gate, w_up, w_down)
     return routed_device(tokens, out_grad, routes, probs, w_gate, w_up, w_down)

time: 155 us -> 148 us (0.955)
  waiting for transfers between devices: 67.4 us -> 38 us
  starting transfers between devices: 28.9 us -> 42.9 us
  Pallas kernels: 44.3 us -> 51.6 us
  local copies, waits for them, and re-layouts: 6.19 us -> 7.78 us
    ppermute x9, waiting for transfers between devices: 28.2 us -> 0.82 us  [over_x(): return lax.ppermute(array, 'tp', [(0, 1), (1, 0)])]
    ppermute x8 -> x13, starting transfers between devices: 7.43 us -> 18 us  [over_z(): lax.ppermute(array, 'ep', [(i, (i + shift * n_y) % ep) for i in range(ep)])]
    ppermute x9 -> x11, waiting for transfers between devices: 11 us -> 0.72 us  [over_y(): lax.ppermute(array, 'ep', [(i, i + 1 - 2 * (i % n_y)) for i in range(ep)])]
    ppermute x8 -> x13, waiting for transfers between devices: 28.1 us -> 36.5 us  [over_z(): lax.ppermute(array, 'ep', [(i, (i + shift * n_y) % ep) for i in range(ep)])]
    pallas_call x2 -> x3, Pallas kernels: 28.2 us -> 34.9 us  [rows_call(): pl.pallas_call(functools.partial(rows_kernel, count, ways, capacity, slot...]
    ppermute x9 -> x11, starting transfers between devices: 9.03 us -> 12.8 us  [over_y(): lax.ppermute(array, 'ep', [(i, i + 1 - 2 * (i % n_y)) for i in range(ep)])]
    unnamed x36 -> x57, local copies, waits for them, and re-layouts: 5.43 us -> 6.79 us
    convert_element_type x8 -> x6, other arithmetic: 2.75 us -> 3.79 us  [the longest x5 2.87 us: total(): sum((block.astype(jnp.float32) for block in blocks)).astype(jnp.bfloat16)]
  transfers between devices with their start and end apart: 30 -> 38, of which waited for: 16 -> 9; matrix products, arithmetic and copies ran while one was open for 2% -> 3% of each run, Pallas kernels for 29% -> 35%
where the time goes in v8:
time: 148 us; the launch traced here: 147 us
  Pallas kernels  51.6 us (35%)
  starting transfers between devices  42.9 us (29%)
  waiting for transfers between devices  38 us (26%)
  local copies, waits for them, and re-layouts  7.78 us (5%)
  other arithmetic  5.71 us (4%)
    ppermute x13, waiting for transfers between devices, over_z(): lax.ppermute(array, 'ep', [(i, (i + shift * n_y) % ep) for i in range(ep)])  36.5 us
    pallas_call x3, Pallas kernels, rows_call(): pl.pallas_call(functools.partial(rows_kernel, count, ways, capacity, slot...  34.9 us
    ppermute x13, starting transfers between devices, over_z(): lax.ppermute(array, 'ep', [(i, (i + shift * n_y) % ep) for i in range(ep)])  18 us
    ppermute x11, starting transfers between devices, over_y(): lax.ppermute(array, 'ep', [(i, i + 1 - 2 * (i % n_y)) for i in range(ep)])  12.8 us
    pallas_call x2, Pallas kernels, grads_call(): pl.pallas_call(functools.partial(grads_kernel, count, *starts, 2 * per),...  12.7 us
    ppermute x9, starting transfers between devices, over_x(): return lax.ppermute(array, 'tp', [(0, 1), (1, 0)])  11.1 us
    unnamed x57, local copies, waits for them, and re-layouts  6.79 us
    pallas_call x1, Pallas kernels, weights_call(): pl.pallas_call(weights_kernel, grid_spec=pltpu.PrefetchScalarGridSpec(num...  3.99 us
  transfers between devices with their start and end apart: 38, of which 9 were waited for; matrix products, arithmetic and copies ran while one was open for 3% of the time, Pallas kernels for 35%

profile of v8, /device:TPU:0, one launch (start us, length us, event | category | flops | bytes accessed | tf_op | source)
XLA Modules:
  0.0 147.1 jit_solution(7521260692721481790)
XLA Ops:
  0.6 1.0 constant_dynamic-update-slice_fusion.1
  1.6 1.0 constant_dynamic-update-slice_fusion.refs_4_
  2.6 3.1 %collective-permute-start = (bf16[256,1024]{1,0:T(8,128)(2,1)S(1)}, bf16[256,1024]{1,0:T(8,128)(2,1)S(1)}, u32[]{:S(2)}, u32[]{:S(2)}) collective-permute-start(bf16[256,1024]{1,0:T(8,128)(2,1)S(1)} %constant_dynamic-update-slice_fusion.refs_4_), channel_id=1, source_target_pairs={{0,4},{2,6},{4,8},{6,10},{8,12},{10,14},{12,0},{14,2},{1,5},{3,7},... | collective-permute-start | bytes 1572872 | tf_op jit(solution)/shard_map/ppermute | solution.py:450
  5.7 1.5 %collective-permute-start.1 = (bf16[256,1024]{1,0:T(8,128)(2,1)S(1)}, bf16[256,1024]{1,0:T(8,128)(2,1)S(1)}, u32[]{:S(2)}, u32[]{:S(2)}) collective-permute-start(bf16[256,1024]{1,0:T(8,128)(2,1)S(1)} %constant_dynamic-update-slice_fusion.refs_4_), channel_id=1, source_target_pairs={{0,2},{2,0},{4,6},{6,4},{8,10},{10,8},{12,14},{14,12},{1,3},{3,1},... | collective-permute-start | bytes 1572872 | tf_op jit(solution)/shard_map/ppermute | solution.py:447
  7.2 1.5 %collective-permute-start.2 = (bf16[256,1024]{1,0:T(8,128)(2,1)S(1)}, bf16[256,1024]{1,0:T(8,128)(2,1)}, u32[]{:S(2)}, u32[]{:S(2)}) collective-permute-start(bf16[256,1024]{1,0:T(8,128)(2,1)S(1)} %constant_dynamic-update-slice_fusion.refs_4_), channel_id=1, source_target_pairs={{0,1},{1,0},{2,3},{3,2},{4,5},{5,4},{6,7},{7,6},{8,9},{9,8},{10,11... | collective-permute-start | bytes 1572872 | tf_op jit(solution)/shard_map/ppermute | solution.py:441
  8.7 4.0 %weights.1 = (bf16[2048,768]{1,0:T(8,128)(2,1)}, bf16[384,2048]{1,0:T(8,128)(2,1)}) custom-call(s32[1]{0:T(128)} %bitcast.2.tp_ref, bf16[1,2048,384]{2,1,0:T(8,128)(2,1)} %wg_ref.1, bf16[1,2048,384]{2,1,0:T(8,128)(2,1)} %wu_ref.1, bf16[1,384,2048]{2,1,0:T(8,128)(2,1)} %wd_ref.1), custom_call_target="tpu_custom_call" | custom-call | bytes 9437184 | tf_op jit(solution)/shard_map/weights/pallas_call | solution.py:141
  12.7 6.9 %collective-permute-done.refs_4_ = bf16[256,1024]{1,0:T(8,128)(2,1)S(1)} collective-permute-done((bf16[256,1024]{1,0:T(8,128)(2,1)S(1)}, bf16[256,1024]{1,0:T(8,128)(2,1)S(1)}, u32[]{:S(2)}, u32[]{:S(2)}) %collective-permute-start) | collective-permute-done | bytes 524320 | tf_op jit(solution)/shard_map/ppermute | solution.py:450
  19.6 0.8 collective-permute-done.2.refs_5_
  21.1 1.5 collective-permute-start.7
  22.6 0.9 collective-permute-start.8
  23.5 1.5 %collective-permute-start.5 = (bf16[256,1024]{1,0:T(8,128)(2,1)}, bf16[256,1024]{1,0:T(8,128)(2,1)S(1)}, u32[]{:S(2)}, u32[]{:S(2)}) collective-permute-start(bf16[256,1024]{1,0:T(8,128)(2,1)} %copy-done.21), channel_id=1, source_target_pairs={{0,1},{1,0},{2,3},{3,2},{4,5},{5,4},{6,7},{7,6},{8,9},{9,8},{10,11... | collective-permute-start | bytes 1572872 | tf_op jit(solution)/shard_map/ppermute | solution.py:441
  25.0 12.1 %collective-permute-done.7.refs_8_ = bf16[256,1024]{1,0:T(8,128)(2,1)} collective-permute-done((bf16[256,1024]{1,0:T(8,128)(2,1)}, bf16[256,1024]{1,0:T(8,128)(2,1)}, u32[]{:S(2)}, u32[]{:S(2)}) %collective-permute-start.7) | collective-permute-done | bytes 524320 | tf_op jit(solution)/shard_map/ppermute | solution.py:450
  37.0 1.5 %collective-permute-start.6 = (bf16[16,128]{1,0:T(8,128)(2,1)S(1)}, bf16[16,128]{1,0:T(8,128)(2,1)S(1)}, u32[]{:S(2)}, u32[]{:S(2)}) collective-permute-start(bf16[16,128]{1,0:T(8,128)(2,1)S(1)} %get-tuple-element.130), channel_id=1, source_target_pairs={{0,2},{2,0},{4,6},{6,4},{8,10},{10,8},{12,14},{14,12},{1,3},{3,1},... | collective-permute-start | bytes 12296 | tf_op jit(solution)/shard_map/ppermute | solution.py:447
  39.2 1.5 %collective-permute-start.11 = (bf16[256,1024]{1,0:T(8,128)(2,1)}, bf16[256,1024]{1,0:T(8,128)(2,1)}, u32[]{:S(2)}, u32[]{:S(2)}) collective-permute-start(bf16[256,1024]{1,0:T(8,128)(2,1)} %collective-permute-done.7.refs_8_), channel_id=1, source_target_pairs={{0,1},{1,0},{2,3},{3,2},{4,5},{5,4},{6,7},{7,6},{8,9},{9,8},{10,11... | collective-permute-start | bytes 1572872 | tf_op jit(solution)/shard_map/ppermute | solution.py:441
  40.7 1.2 collective-permute-start.9
  41.9 0.6 pad_add_fusion.where_ref
  43.2 1.1 copy-done.3
  44.3 10.5 %rows.3 = (bf16[144,5248]{1,0:T(8,128)(2,1)}, bf16[144,5248]{1,0:T(8,128)(2,1)}, bf16[1,144,1024]{2,1,0:T(8,128)(2,1)}, bf16[1,144,1024]{2,1,0:T(8,128)(2,1)}, b...) custom-call(s32[3]{0:T(128)} %pad_add_fusion.where_ref, bf16[2048,768]{1,0:T(8,128)(2,1)} %get-tuple-element.68.refs_0_, ...), custom_call_target="tpu_custom_call" | custom-call | flops 3170893824 | bytes 13631488 | tf_op jit(solution)/shard_map/rows/pallas_call | solution.py:307
  54.9 0.8 collective-permute-start.12
  55.7 1.6 %collective-permute-start.13 = (bf16[256,1024]{1,0:T(8,128)(2,1)}, bf16[256,1024]{1,0:T(8,128)(2,1)S(1)}, u32[]{:S(2)}, u32[]{:S(2)}) collective-permute-start(bf16[256,1024]{1,0:T(8,128)(2,1)} %collective-permute-done.11.refs_9_), channel_id=1, source_target_pairs={{0,2},{2,0},{4,6},{6,4},{8,10},{10,8},{12,14},{14,12},{1,3},{3,1},... | collective-permute-start | bytes 1572872 | tf_op jit(solution)/shard_map/ppermute | solution.py:447
  57.3 1.5 %collective-permute-start.14 = (bf16[256,1024]{1,0:T(8,128)(2,1)}, bf16[256,1024]{1,0:T(8,128)(2,1)S(1)}, u32[]{:S(2)}, u32[]{:S(2)}) collective-permute-start(bf16[256,1024]{1,0:T(8,128)(2,1)} %copy-done.18), channel_id=1, source_target_pairs={{0,1},{1,0},{2,3},{3,2},{4,5},{5,4},{6,7},{7,6},{8,9},{9,8},{10,11... | collective-permute-start | bytes 1572872 | tf_op jit(solution)/shard_map/ppermute | solution.py:441
  58.8 2.5 %collective-permute-start.20 = (bf16[2,16,128]{2,1,0:T(8,128)(2,1)S(1)}, bf16[2,16,128]{2,1,0:T(8,128)(2,1)S(1)}, u32[]{:S(2)}, u32[]{:S(2)}) collective-permute-start(bf16[2,16,128]{2,1,0:T(8,128)(2,1)S(1)} %copy-done.16), channel_id=1, source_target_pairs={{0,8},{2,10},{4,12},{6,14},{8,0},{10,2},{12,4},{14,6},{1,9},{3,11}... | collective-permute-start | bytes 24584 | tf_op jit(solution)/shard_map/ppermute | solution.py:450
  61.4 7.5 %collective-permute-done.12.refs_7_ = bf16[256,1024]{1,0:T(8,128)(2,1)S(1)} collective-permute-done((bf16[256,1024]{1,0:T(8,128)(2,1)}, bf16[256,1024]{1,0:T(8,128)(2,1)S(1)}, u32[]{:S(2)}, u32[]{:S(2)}) %collective-permute-start.12) | collective-permute-done | bytes 524320 | tf_op jit(solution)/shard_map/ppermute | solution.py:450
  68.9 1.1 collective-permute-start.15
  70.0 0.9 collective-permute-start.16
  70.8 2.7 %collective-permute-start.17 = (bf16[256,1024]{1,0:T(8,128)(2,1)}, bf16[256,1024]{1,0:T(8,128)(2,1)S(1)}, u32[]{:S(2)}, u32[]{:S(2)}) collective-permute-start(bf16[256,1024]{1,0:T(8,128)(2,1)} %copy-done.19), channel_id=1, source_target_pairs={{0,12},{2,14},{4,0},{6,2},{8,4},{10,6},{12,8},{14,10},{1,13},{3,15... | collective-permute-start | bytes 1572872 | tf_op jit(solution)/shard_map/ppermute | solution.py:450
  74.8 13.8 %rows.4 = (bf16[288,5248]{1,0:T(8,128)(2,1)}, bf16[288,5248]{1,0:T(8,128)(2,1)}, bf16[1,144,1024]{2,1,0:T(8,128)(2,1)}, bf16[2,144,1024]{2,1,0:T(8,128)(2,1)}, b...) custom-call(s32[3]{0:T(128)} %pad_add_fusion.where_ref, ...), custom_call_target="tpu_custom_call" | custom-call | flops 6341787648 | bytes 17825792 | tf_op jit(solution)/shard_map/rows/pallas_call | solution.py:307
  89.2 1.3 collective-permute-start.21
  90.5 1.5 %collective-permute-start.22 = (bf16[1,144,1024]{2,1,0:T(8,128)(2,1)}, bf16[1,144,1024]{2,1,0:T(8,128)(2,1)S(1)}, u32[]{:S(2)}, u32[]{:S(2)}) collective-permute-start(bf16[1,144,1024]{2,1,0:T(8,128)(2,1)} %get-tuple-element.101), channel_id=1, source_target_pairs={{0,2},{2,0},{4,6},{6,4},{8,10},{10,8},{12,14},{14,12},{1,3},{3,1},... | collective-permute-start | bytes 884744 | tf_op jit(solution)/shard_map/ppermute | solution.py:447
  92.4 1.8 %collective-permute-start.23 = (bf16[1,144,1024]{2,1,0:T(8,128)(2,1)}, bf16[1,144,1024]{2,1,0:T(8,128)(2,1)}, u32[]{:S(2)}, u32[]{:S(2)}) collective-permute-start(bf16[1,144,1024]{2,1,0:T(8,128)(2,1)} %get-tuple-element.102), channel_id=1, source_target_pairs={{0,12},{2,14},{4,0},{6,2},{8,4},{10,6},{12,8},{14,10},{1,13},{3,15... | collective-permute-start | bytes 884744 | tf_op jit(solution)/shard_map/ppermute | solution.py:450
  94.3 10.6 %rows.5 = (bf16[144,5248]{1,0:T(8,128)(2,1)}, bf16[144,5248]{1,0:T(8,128)(2,1)}, bf16[1,144,1024]{2,1,0:T(8,128)(2,1)}, bf16[1,144,1024]{2,1,0:T(8,128)(2,1)}, b...) custom-call(s32[3]{0:T(128)} %pad_add_fusion.where_ref, bf16[2048,768]{1,0:T(8,128)(2,1)} %get-tuple-element.68.refs_0_, ...), custom_call_target="tpu_custom_call" | custom-call | flops 3170893824 | bytes 13631488 | tf_op jit(solution)/shard_map/rows/pallas_call | solution.py:307
  105.0 1.3 collective-permute-start.27
  106.3 1.2 add_convert_fusion.5
  107.5 1.6 %collective-permute-start.28 = (bf16[1,144,1024]{2,1,0:T(8,128)(2,1)S(1)}, bf16[1,144,1024]{2,1,0:T(8,128)(2,1)S(1)}, u32[]{:S(2)}, u32[]{:S(2)}) collective-permute-start(bf16[1,144,1024]{2,1,0:T(8,128)(2,1)S(1)} %add_convert_fusion.5), channel_id=1, source_target_pairs={{0,2},{2,0},{4,6},{6,4},{8,10},{10,8},{12,14},{14,12},{1,3},{3,1},... | collective-permute-start | bytes 884744 | tf_op jit(solution)/shard_map/ppermute | solution.py:447
  109.8 1.5 %collective-permute-start.25 = (bf16[1,144,1024]{2,1,0:T(8,128)(2,1)}, bf16[1,144,1024]{2,1,0:T(8,128)(2,1)S(1)}, u32[]{:S(2)}, u32[]{:S(2)}) collective-permute-start(bf16[1,144,1024]{2,1,0:T(8,128)(2,1)} %get-tuple-element.104), channel_id=1, source_target_pairs={{0,2},{2,0},{4,6},{6,4},{8,10},{10,8},{12,14},{14,12},{1,3},{3,1},... | collective-permute-start | bytes 884744 | tf_op jit(solution)/shard_map/ppermute | solution.py:447
  111.3 1.9 %copy-done = bf16[288,5248]{1,0:T(8,128)(2,1)S(1)} copy-done((bf16[288,5248]{1,0:T(8,128)(2,1)S(1)}, bf16[288,5248]{1,0:T(8,128)(2,1)}, u32[]{:S(2)}) %copy-start) | copy-done | bytes 3022872
  113.2 1.4 copy-done.2
  114.6 7.5 %grads.2 = (bf16[1,2048,384]{2,1,0:T(8,128)(2,1)}, bf16[1,2048,384]{2,1,0:T(8,128)(2,1)}) custom-call(s32[1]{0:T(128)} %bitcast.2.tp_ref, bf16[144,5248]{1,0:T(8,128)(2,1)S(1)} %copy-done.1, bf16[144,5248]{1,0:T(8,128)(2,1)} %collective-permute-done.29.refs_1_, bf16[288,5248]{1,0:T(8,128)(2,1)S(1)} %copy-done, ...), custom_call_target="tpu_custom_call" | custom-call | flops 3623878656 | bytes 6488064 | tf_op jit(solution)/shard_map/grads/pallas_call | solution.py:407
  122.4 0.7 collective-permute-start.32
  123.1 3.2 %collective-permute-start.34 = (bf16[1,144,1024]{2,1,0:T(8,128)(2,1)S(1)}, bf16[1,144,1024]{2,1,0:T(8,128)(2,1)S(1)}, u32[]{:S(2)}, u32[]{:S(2)}) collective-permute-start(bf16[1,144,1024]{2,1,0:T(8,128)(2,1)S(1)} %get-tuple-element.127), channel_id=1, source_target_pairs={{0,12},{2,14},{4,0},{6,2},{8,4},{10,6},{12,8},{14,10},{1,13},{3,15... | collective-permute-start | bytes 884744 | tf_op jit(solution)/shard_map/ppermute | solution.py:450
  126.3 1.1 add_convert_fusion.1
  128.0 5.2 %grads.3 = bf16[1,384,2048]{2,1,0:T(8,128)(2,1)} custom-call(s32[1]{0:T(128)} %bitcast.2.tp_ref, bf16[144,5248]{1,0:T(8,128)(2,1)S(1)} %copy-done.1, bf16[144,5248]{1,0:T(8,128)(2,1)} %collective-permute-done.29.refs_1_, bf16[288,5248]{1,0:T(8,128)(2,1)S(1)} %copy-done, bf16[288,5248]{1,0:T(8,128)(2,1)} %collective-permute-done.30.refs_3_, ...), custom_call_target="tpu_custom_call" | custom-call | flops 1811939328 | bytes 5603328 | tf_op jit(solution)/shard_map/grads/pallas_call | solution.py:407
  133.3 0.9 collective-permute-done.32
  134.5 0.7 collective-permute-start.33
  135.2 0.6 collective-permute-done.36
  135.9 0.9 collective-permute-start.37
  137.4 8.1 %collective-permute-done.35 = bf16[1,144,1024]{2,1,0:T(8,128)(2,1)S(1)} collective-permute-done((bf16[1,144,1024]{2,1,0:T(8,128)(2,1)S(1)}, bf16[1,144,1024]{2,1,0:T(8,128)(2,1)S(1)}, u32[]{:S(2)}, u32[]{:S(2)}) %collective-permute-start.35) | collective-permute-done | bytes 294944 | tf_op jit(solution)/shard_map/ppermute | solution.py:450
  146.2 0.9 fusion
  (107 shorter events, 7.5 us)
Async XLA Ops:
  2.6 17.8 %copy-start.13 = (bf16[256,1024]{1,0:T(8,128)(2,1)}, bf16[256,1024]{1,0:T(8,128)(2,1)S(1)}, u32[]{:S(2)}) copy-start(bf16[256,1024]{1,0:T(8,128)(2,1)S(1)} %constant_dynamic-update-slice_fusion.refs_4_) | copy-start | bytes 1572868
  2.6 17.0 %collective-permute-start = (bf16[256,1024]{1,0:T(8,128)(2,1)S(1)}, bf16[256,1024]{1,0:T(8,128)(2,1)S(1)}, u32[]{:S(2)}, u32[]{:S(2)}) collective-permute-start(bf16[256,1024]{1,0:T(8,128)(2,1)S(1)} %constant_dynamic-update-slice_fusion.refs_4_), channel_id=1, source_target_pairs={{0,4},{2,6},{4,8},{6,10},{8,12},{10,14},{12,0},{14,2},{1,5},{3,7},... | collective-permute-start | bytes 1572872 | tf_op jit(solution)/shard_map/ppermute | solution.py:450
  5.7 14.0 %collective-permute-start.1 = (bf16[256,1024]{1,0:T(8,128)(2,1)S(1)}, bf16[256,1024]{1,0:T(8,128)(2,1)S(1)}, u32[]{:S(2)}, u32[]{:S(2)}) collective-permute-start(bf16[256,1024]{1,0:T(8,128)(2,1)S(1)} %constant_dynamic-update-slice_fusion.refs_4_), channel_id=1, source_target_pairs={{0,2},{2,0},{4,6},{6,4},{8,10},{10,8},{12,14},{14,12},{1,3},{3,1},... | collective-permute-start | bytes 1572872 | tf_op jit(solution)/shard_map/ppermute | solution.py:447
  7.2 13.2 %collective-permute-start.2 = (bf16[256,1024]{1,0:T(8,128)(2,1)S(1)}, bf16[256,1024]{1,0:T(8,128)(2,1)}, u32[]{:S(2)}, u32[]{:S(2)}) collective-permute-start(bf16[256,1024]{1,0:T(8,128)(2,1)S(1)} %constant_dynamic-update-slice_fusion.refs_4_), channel_id=1, source_target_pairs={{0,1},{1,0},{2,3},{3,2},{4,5},{5,4},{6,7},{7,6},{8,9},{9,8},{10,11... | collective-permute-start | bytes 1572872 | tf_op jit(solution)/shard_map/ppermute | solution.py:441
  8.7 16.3 %copy-start.17 = (bf16[128,8]{0,1:T(8,128)(2,1)S(1)}, bf16[128,8]{0,1:T(8,128)(2,1)}, u32[]{:S(2)}) copy-start(bf16[128,8]{0,1:T(8,128)(2,1)} %param.10) | copy-start | bytes 6148
  8.7 16.3 %copy-start.14 = (s32[128,8]{0,1:T(8,128)S(1)}, s32[128,8]{0,1:T(8,128)}, u32[]{:S(2)}) copy-start(s32[128,8]{0,1:T(8,128)} %param.9) | copy-start | bytes 12292
  20.6 22.6 %collective-permute-start.3 = (bf16[2048,768]{1,0:T(8,128)(2,1)}, bf16[2048,768]{1,0:T(8,128)(2,1)}, u32[]{:S(2)}, u32[]{:S(2)}) collective-permute-start(bf16[2048,768]{1,0:T(8,128)(2,1)} %get-tuple-element.68.refs_0_), channel_id=1, source_target_pairs={{0,16},{16,0},{1,17},{17,1},{2,18},{18,2},{3,19},{19,3},{4,20},{20... | collective-permute-start | bytes 9437192 | tf_op jit(solution)/shard_map/ppermute | solution.py:444
  20.6 22.6 %collective-permute-start.4 = (bf16[384,2048]{1,0:T(8,128)(2,1)}, bf16[384,2048]{1,0:T(8,128)(2,1)S(1)}, u32[]{:S(2)}, u32[]{:S(2)}) collective-permute-start(bf16[384,2048]{1,0:T(8,128)(2,1)} %get-tuple-element.69.refs_2_), channel_id=1, source_target_pairs={{0,16},{16,0},{1,17},{17,1},{2,18},{18,2},{3,19},{19,3},{4,20},{20... | collective-permute-start | bytes 4718600 | tf_op jit(solution)/shard_map/ppermute | solution.py:444
  21.1 15.9 %collective-permute-start.7 = (bf16[256,1024]{1,0:T(8,128)(2,1)}, bf16[256,1024]{1,0:T(8,128)(2,1)}, u32[]{:S(2)}, u32[]{:S(2)}) collective-permute-start(bf16[256,1024]{1,0:T(8,128)(2,1)} %copy-done.18), channel_id=1, source_target_pairs={{0,4},{2,6},{4,8},{6,10},{8,12},{10,14},{12,0},{14,2},{1,5},{3,7},... | collective-permute-start | bytes 1572872 | tf_op jit(solution)/shard_map/ppermute | solution.py:450
  22.6 16.0 %collective-permute-start.8 = (bf16[256,1024]{1,0:T(8,128)(2,1)}, bf16[256,1024]{1,0:T(8,128)(2,1)S(1)}, u32[]{:S(2)}, u32[]{:S(2)}) collective-permute-start(bf16[256,1024]{1,0:T(8,128)(2,1)} %copy-done.18), channel_id=1, source_target_pairs={{0,2},{2,0},{4,6},{6,4},{8,10},{10,8},{12,14},{14,12},{1,3},{3,1},... | collective-permute-start | bytes 1572872 | tf_op jit(solution)/shard_map/ppermute | solution.py:447
  23.5 15.1 %collective-permute-start.5 = (bf16[256,1024]{1,0:T(8,128)(2,1)}, bf16[256,1024]{1,0:T(8,128)(2,1)S(1)}, u32[]{:S(2)}, u32[]{:S(2)}) collective-permute-start(bf16[256,1024]{1,0:T(8,128)(2,1)} %copy-done.21), channel_id=1, source_target_pairs={{0,1},{1,0},{2,3},{3,2},{4,5},{5,4},{6,7},{7,6},{8,9},{9,8},{10,11... | collective-permute-start | bytes 1572872 | tf_op jit(solution)/shard_map/ppermute | solution.py:441
  37.0 3.6 %collective-permute-start.6 = (bf16[16,128]{1,0:T(8,128)(2,1)S(1)}, bf16[16,128]{1,0:T(8,128)(2,1)S(1)}, u32[]{:S(2)}, u32[]{:S(2)}) collective-permute-start(bf16[16,128]{1,0:T(8,128)(2,1)S(1)} %get-tuple-element.130), channel_id=1, source_target_pairs={{0,2},{2,0},{4,6},{6,4},{8,10},{10,8},{12,14},{14,12},{1,3},{3,1},... | collective-permute-start | bytes 12296 | tf_op jit(solution)/shard_map/ppermute | solution.py:447
  38.6 16.2 %collective-permute-start.10 = (bf16[256,1024]{1,0:T(8,128)(2,1)}, bf16[256,1024]{1,0:T(8,128)(2,1)}, u32[]{:S(2)}, u32[]{:S(2)}) collective-permute-start(bf16[256,1024]{1,0:T(8,128)(2,1)} %collective-permute-done.7.refs_8_), channel_id=1, source_target_pairs={{0,2},{2,0},{4,6},{6,4},{8,10},{10,8},{12,14},{14,12},{1,3},{3,1},... | collective-permute-start | bytes 1572872 | tf_op jit(solution)/shard_map/ppermute | solution.py:447
  39.2 15.7 %collective-permute-start.11 = (bf16[256,1024]{1,0:T(8,128)(2,1)}, bf16[256,1024]{1,0:T(8,128)(2,1)}, u32[]{:S(2)}, u32[]{:S(2)}) collective-permute-start(bf16[256,1024]{1,0:T(8,128)(2,1)} %collective-permute-done.7.refs_8_), channel_id=1, source_target_pairs={{0,1},{1,0},{2,3},{3,2},{4,5},{5,4},{6,7},{7,6},{8,9},{9,8},{10,11... | collective-permute-start | bytes 1572872 | tf_op jit(solution)/shard_map/ppermute | solution.py:441
  40.7 14.1 %collective-permute-start.9 = (bf16[256,1024]{1,0:T(8,128)(2,1)}, bf16[256,1024]{1,0:T(8,128)(2,1)}, u32[]{:S(2)}, u32[]{:S(2)}) collective-permute-start(bf16[256,1024]{1,0:T(8,128)(2,1)} %copy-done.13), channel_id=1, source_target_pairs={{0,12},{2,14},{4,0},{6,2},{8,4},{10,6},{12,8},{14,10},{1,13},{3,15... | collective-permute-start | bytes 1572872 | tf_op jit(solution)/shard_map/ppermute | solution.py:450
  43.2 15.6 %copy-start.16 = (bf16[2,16,128]{2,1,0:T(8,128)(2,1)S(1)}, bf16[2,16,128]{2,1,0:T(8,128)(2,1)}, u32[]{:S(2)}) copy-start(bf16[2,16,128]{2,1,0:T(8,128)(2,1)} %pad_maximum_fusion.refs_8_) | copy-start | bytes 24580
  54.9 14.0 %collective-permute-start.12 = (bf16[256,1024]{1,0:T(8,128)(2,1)}, bf16[256,1024]{1,0:T(8,128)(2,1)S(1)}, u32[]{:S(2)}, u32[]{:S(2)}) collective-permute-start(bf16[256,1024]{1,0:T(8,128)(2,1)} %copy-done.19), channel_id=1, source_target_pairs={{0,4},{2,6},{4,8},{6,10},{8,12},{10,14},{12,0},{14,2},{1,5},{3,7},... | collective-permute-start | bytes 1572872 | tf_op jit(solution)/shard_map/ppermute | solution.py:450
  55.7 13.2 %collective-permute-start.13 = (bf16[256,1024]{1,0:T(8,128)(2,1)}, bf16[256,1024]{1,0:T(8,128)(2,1)S(1)}, u32[]{:S(2)}, u32[]{:S(2)}) collective-permute-start(bf16[256,1024]{1,0:T(8,128)(2,1)} %collective-permute-done.11.refs_9_), channel_id=1, source_target_pairs={{0,2},{2,0},{4,6},{6,4},{8,10},{10,8},{12,14},{14,12},{1,3},{3,1},... | collective-permute-start | bytes 1572872 | tf_op jit(solution)/shard_map/ppermute | solution.py:447
  57.3 11.6 %collective-permute-start.14 = (bf16[256,1024]{1,0:T(8,128)(2,1)}, bf16[256,1024]{1,0:T(8,128)(2,1)S(1)}, u32[]{:S(2)}, u32[]{:S(2)}) collective-permute-start(bf16[256,1024]{1,0:T(8,128)(2,1)} %copy-done.18), channel_id=1, source_target_pairs={{0,1},{1,0},{2,3},{3,2},{4,5},{5,4},{6,7},{7,6},{8,9},{9,8},{10,11... | collective-permute-start | bytes 1572872 | tf_op jit(solution)/shard_map/ppermute | solution.py:441
  58.7 14.9 %collective-permute-start.19 = (bf16[2,16,128]{2,1,0:T(8,128)(2,1)S(1)}, bf16[2,16,128]{2,1,0:T(8,128)(2,1)S(1)}, u32[]{:S(2)}, u32[]{:S(2)}) collective-permute-start(bf16[2,16,128]{2,1,0:T(8,128)(2,1)S(1)} %copy-done.16), channel_id=1, source_target_pairs={{0,4},{2,6},{4,8},{6,10},{8,12},{10,14},{12,0},{14,2},{1,5},{3,7},... | collective-permute-start | bytes 24584 | tf_op jit(solution)/shard_map/ppermute | solution.py:450
  58.8 14.8 %collective-permute-start.20 = (bf16[2,16,128]{2,1,0:T(8,128)(2,1)S(1)}, bf16[2,16,128]{2,1,0:T(8,128)(2,1)S(1)}, u32[]{:S(2)}, u32[]{:S(2)}) collective-permute-start(bf16[2,16,128]{2,1,0:T(8,128)(2,1)S(1)} %copy-done.16), channel_id=1, source_target_pairs={{0,8},{2,10},{4,12},{6,14},{8,0},{10,2},{12,4},{14,6},{1,9},{3,11}... | collective-permute-start | bytes 24584 | tf_op jit(solution)/shard_map/ppermute | solution.py:450
  68.9 19.7 %collective-permute-start.15 = (bf16[256,1024]{1,0:T(8,128)(2,1)}, bf16[256,1024]{1,0:T(8,128)(2,1)S(1)}, u32[]{:S(2)}, u32[]{:S(2)}) collective-permute-start(bf16[256,1024]{1,0:T(8,128)(2,1)} %collective-permute-done.9.refs_4_), channel_id=1, source_target_pairs={{0,1},{1,0},{2,3},{3,2},{4,5},{5,4},{6,7},{7,6},{8,9},{9,8},{10,11... | collective-permute-start | bytes 1572872 | tf_op jit(solution)/shard_map/ppermute | solution.py:441
  70.0 18.7 %collective-permute-start.16 = (bf16[256,1024]{1,0:T(8,128)(2,1)}, bf16[256,1024]{1,0:T(8,128)(2,1)S(1)}, u32[]{:S(2)}, u32[]{:S(2)}) collective-permute-start(bf16[256,1024]{1,0:T(8,128)(2,1)} %collective-permute-done.9.refs_4_), channel_id=1, source_target_pairs={{0,2},{2,0},{4,6},{6,4},{8,10},{10,8},{12,14},{14,12},{1,3},{3,1},... | collective-permute-start | bytes 1572872 | tf_op jit(solution)/shard_map/ppermute | solution.py:447
  70.8 17.8 %collective-permute-start.17 = (bf16[256,1024]{1,0:T(8,128)(2,1)}, bf16[256,1024]{1,0:T(8,128)(2,1)S(1)}, u32[]{:S(2)}, u32[]{:S(2)}) collective-permute-start(bf16[256,1024]{1,0:T(8,128)(2,1)} %copy-done.19), channel_id=1, source_target_pairs={{0,12},{2,14},{4,0},{6,2},{8,4},{10,6},{12,8},{14,10},{1,13},{3,15... | collective-permute-start | bytes 1572872 | tf_op jit(solution)/shard_map/ppermute | solution.py:450
  88.7 21.1 %collective-permute-start.30 = (bf16[288,5248]{1,0:T(8,128)(2,1)}, bf16[288,5248]{1,0:T(8,128)(2,1)}, u32[]{:S(2)}, u32[]{:S(2)}) collective-permute-start(bf16[288,5248]{1,0:T(8,128)(2,1)} %get-tuple-element.110), channel_id=1, source_target_pairs={{0,16},{16,0},{1,17},{17,1},{2,18},{18,2},{3,19},{19,3},{4,20},{20... | collective-permute-start | bytes 9068552 | tf_op jit(solution)/shard_map/ppermute | solution.py:444
  88.7 3.7 %collective-permute-start.18 = (bf16[2,16,128]{2,1,0:T(8,128)(2,1)S(1)}, bf16[2,16,128]{2,1,0:T(8,128)(2,1)S(1)}, u32[]{:S(2)}, u32[]{:S(2)}) collective-permute-start(bf16[2,16,128]{2,1,0:T(8,128)(2,1)S(1)} %copy-done.16), channel_id=1, source_target_pairs={{0,12},{2,14},{4,0},{6,2},{8,4},{10,6},{12,8},{14,10},{1,13},{3,15... | collective-permute-start | bytes 24584 | tf_op jit(solution)/shard_map/ppermute | solution.py:450
  88.8 20.3 %collective-permute-start.29 = (bf16[144,5248]{1,0:T(8,128)(2,1)}, bf16[144,5248]{1,0:T(8,128)(2,1)}, u32[]{:S(2)}, u32[]{:S(2)}) collective-permute-start(bf16[144,5248]{1,0:T(8,128)(2,1)} %get-tuple-element.109), channel_id=1, source_target_pairs={{0,16},{16,0},{1,17},{17,1},{2,18},{18,2},{3,19},{19,3},{4,20},{20... | collective-permute-start | bytes 4534280 | tf_op jit(solution)/shard_map/ppermute | solution.py:444
  89.2 15.7 %collective-permute-start.21 = (bf16[1,144,1024]{2,1,0:T(8,128)(2,1)}, bf16[1,144,1024]{2,1,0:T(8,128)(2,1)}, u32[]{:S(2)}, u32[]{:S(2)}) collective-permute-start(bf16[1,144,1024]{2,1,0:T(8,128)(2,1)} %get-tuple-element.100), channel_id=1, source_target_pairs={{0,1},{1,0},{2,3},{3,2},{4,5},{5,4},{6,7},{7,6},{8,9},{9,8},{10,11... | collective-permute-start | bytes 884744 | tf_op jit(solution)/shard_map/ppermute | solution.py:441
  90.5 14.4 %collective-permute-start.22 = (bf16[1,144,1024]{2,1,0:T(8,128)(2,1)}, bf16[1,144,1024]{2,1,0:T(8,128)(2,1)S(1)}, u32[]{:S(2)}, u32[]{:S(2)}) collective-permute-start(bf16[1,144,1024]{2,1,0:T(8,128)(2,1)} %get-tuple-element.101), channel_id=1, source_target_pairs={{0,2},{2,0},{4,6},{6,4},{8,10},{10,8},{12,14},{14,12},{1,3},{3,1},... | collective-permute-start | bytes 884744 | tf_op jit(solution)/shard_map/ppermute | solution.py:447
  92.4 12.5 %collective-permute-start.23 = (bf16[1,144,1024]{2,1,0:T(8,128)(2,1)}, bf16[1,144,1024]{2,1,0:T(8,128)(2,1)}, u32[]{:S(2)}, u32[]{:S(2)}) collective-permute-start(bf16[1,144,1024]{2,1,0:T(8,128)(2,1)} %get-tuple-element.102), channel_id=1, source_target_pairs={{0,12},{2,14},{4,0},{6,2},{8,4},{10,6},{12,8},{14,10},{1,13},{3,15... | collective-permute-start | bytes 884744 | tf_op jit(solution)/shard_map/ppermute | solution.py:450
  94.3 17.0 %copy-start.1 = (bf16[144,5248]{1,0:T(8,128)(2,1)S(1)}, bf16[144,5248]{1,0:T(8,128)(2,1)}, u32[]{:S(2)}) copy-start(bf16[144,5248]{1,0:T(8,128)(2,1)} %get-tuple-element.81.refs_0_) | copy-start | bytes 4534276
  104.9 4.4 %collective-permute-start.31 = (bf16[144,5248]{1,0:T(8,128)(2,1)}, bf16[144,5248]{1,0:T(8,128)(2,1)S(1)}, u32[]{:S(2)}, u32[]{:S(2)}) collective-permute-start(bf16[144,5248]{1,0:T(8,128)(2,1)} %get-tuple-element.112), channel_id=1, source_target_pairs={{0,16},{16,0},{1,17},{17,1},{2,18},{18,2},{3,19},{19,3},{4,20},{20... | collective-permute-start | bytes 4534280 | tf_op jit(solution)/shard_map/ppermute | solution.py:444
  105.0 17.1 %collective-permute-start.27 = (bf16[2,144,1024]{2,1,0:T(8,128)(2,1)}, bf16[2,144,1024]{2,1,0:T(8,128)(2,1)S(1)}, u32[]{:S(2)}, u32[]{:S(2)}) collective-permute-start(bf16[2,144,1024]{2,1,0:T(8,128)(2,1)} %get-tuple-element.107), channel_id=1, source_target_pairs={{0,1},{1,0},{2,3},{3,2},{4,5},{5,4},{6,7},{7,6},{8,9},{9,8},{10,11... | collective-permute-start | bytes 1769480 | tf_op jit(solution)/shard_map/ppermute | solution.py:441
  106.3 15.8 %copy-start.7 = (bf16[1,144,1024]{2,1,0:T(8,128)(2,1)S(1)}, bf16[1,144,1024]{2,1,0:T(8,128)(2,1)}, u32[]{:S(2)}) copy-start(bf16[1,144,1024]{2,1,0:T(8,128)(2,1)} %get-tuple-element.119) | copy-start | bytes 884740
  106.3 15.8 %copy-start.8 = (bf16[1,144,1024]{2,1,0:T(8,128)(2,1)S(1)}, bf16[1,144,1024]{2,1,0:T(8,128)(2,1)}, u32[]{:S(2)}) copy-start(bf16[1,144,1024]{2,1,0:T(8,128)(2,1)} %get-tuple-element.105) | copy-start | bytes 884740
  107.5 14.6 %collective-permute-start.28 = (bf16[1,144,1024]{2,1,0:T(8,128)(2,1)S(1)}, bf16[1,144,1024]{2,1,0:T(8,128)(2,1)S(1)}, u32[]{:S(2)}, u32[]{:S(2)}) collective-permute-start(bf16[1,144,1024]{2,1,0:T(8,128)(2,1)S(1)} %add_convert_fusion.5), channel_id=1, source_target_pairs={{0,2},{2,0},{4,6},{6,4},{8,10},{10,8},{12,14},{14,12},{1,3},{3,1},... | collective-permute-start | bytes 884744 | tf_op jit(solution)/shard_map/ppermute | solution.py:447
  109.1 13.0 %collective-permute-start.26 = (bf16[1,144,1024]{2,1,0:T(8,128)(2,1)}, bf16[1,144,1024]{2,1,0:T(8,128)(2,1)S(1)}, u32[]{:S(2)}, u32[]{:S(2)}) collective-permute-start(bf16[1,144,1024]{2,1,0:T(8,128)(2,1)} %get-tuple-element.106), channel_id=1, source_target_pairs={{0,4},{2,6},{4,8},{6,10},{8,12},{10,14},{12,0},{14,2},{1,5},{3,7},... | collective-permute-start | bytes 884744 | tf_op jit(solution)/shard_map/ppermute | solution.py:450
  109.3 24.0 %collective-permute-start.24 = (bf16[1,144,1024]{2,1,0:T(8,128)(2,1)}, bf16[1,144,1024]{2,1,0:T(8,128)(2,1)S(1)}, u32[]{:S(2)}, u32[]{:S(2)}) collective-permute-start(bf16[1,144,1024]{2,1,0:T(8,128)(2,1)} %get-tuple-element.103), channel_id=1, source_target_pairs={{0,1},{1,0},{2,3},{3,2},{4,5},{5,4},{6,7},{7,6},{8,9},{9,8},{10,11... | collective-permute-start | bytes 884744 | tf_op jit(solution)/shard_map/ppermute | solution.py:441
  109.8 23.5 %collective-permute-start.25 = (bf16[1,144,1024]{2,1,0:T(8,128)(2,1)}, bf16[1,144,1024]{2,1,0:T(8,128)(2,1)S(1)}, u32[]{:S(2)}, u32[]{:S(2)}) collective-permute-start(bf16[1,144,1024]{2,1,0:T(8,128)(2,1)} %get-tuple-element.104), channel_id=1, source_target_pairs={{0,2},{2,0},{4,6},{6,4},{8,10},{10,8},{12,14},{14,12},{1,3},{3,1},... | collective-permute-start | bytes 884744 | tf_op jit(solution)/shard_map/ppermute | solution.py:447
  122.4 11.8 %collective-permute-start.32 = (bf16[1,144,1024]{2,1,0:T(8,128)(2,1)S(1)}, bf16[1,144,1024]{2,1,0:T(8,128)(2,1)S(1)}, u32[]{:S(2)}, u32[]{:S(2)}) collective-permute-start(bf16[1,144,1024]{2,1,0:T(8,128)(2,1)S(1)} %get-tuple-element.128), channel_id=1, source_target_pairs={{0,4},{2,6},{4,8},{6,10},{8,12},{10,14},{12,0},{14,2},{1,5},{3,7},... | collective-permute-start | bytes 884744 | tf_op jit(solution)/shard_map/ppermute | solution.py:450
  123.1 14.2 %collective-permute-start.34 = (bf16[1,144,1024]{2,1,0:T(8,128)(2,1)S(1)}, bf16[1,144,1024]{2,1,0:T(8,128)(2,1)S(1)}, u32[]{:S(2)}, u32[]{:S(2)}) collective-permute-start(bf16[1,144,1024]{2,1,0:T(8,128)(2,1)S(1)} %get-tuple-element.127), channel_id=1, source_target_pairs={{0,12},{2,14},{4,0},{6,2},{8,4},{10,6},{12,8},{14,10},{1,13},{3,15... | collective-permute-start | bytes 884744 | tf_op jit(solution)/shard_map/ppermute | solution.py:450
  127.4 6.8 %copy-start.11 = (bf16[1,144,1024]{2,1,0:T(8,128)(2,1)S(1)}, bf16[1,144,1024]{2,1,0:T(8,128)(2,1)}, u32[]{:S(2)}) copy-start(bf16[1,144,1024]{2,1,0:T(8,128)(2,1)} %get-tuple-element.120) | copy-start | bytes 884740
  127.5 7.1 %copy-start.25 = (bf16[1,144,1024]{2,1,0:T(8,128)(2,1)S(1)}, bf16[1,144,1024]{2,1,0:T(8,128)(2,1)}, u32[]{:S(2)}) copy-start(bf16[1,144,1024]{2,1,0:T(8,128)(2,1)} %get-tuple-element.118) | copy-start | bytes 884740
  127.5 8.4 %collective-permute-start.36 = (bf16[1,144,1024]{2,1,0:T(8,128)(2,1)S(1)}, bf16[1,144,1024]{2,1,0:T(8,128)(2,1)S(1)}, u32[]{:S(2)}, u32[]{:S(2)}) collective-permute-start(bf16[1,144,1024]{2,1,0:T(8,128)(2,1)S(1)} %add_convert_fusion.1), channel_id=1, source_target_pairs={{0,2},{2,0},{4,6},{6,4},{8,10},{10,8},{12,14},{14,12},{1,3},{3,1},... | collective-permute-start | bytes 884744 | tf_op jit(solution)/shard_map/ppermute | solution.py:447
  133.3 12.2 %copy-start.12 = (bf16[1,144,1024]{2,1,0:T(8,128)(2,1)S(1)}, bf16[1,144,1024]{2,1,0:T(8,128)(2,1)}, u32[]{:S(2)}) copy-start(bf16[1,144,1024]{2,1,0:T(8,128)(2,1)} %get-tuple-element.75) | copy-start | bytes 884740
  134.4 11.0 %collective-permute-start.35 = (bf16[1,144,1024]{2,1,0:T(8,128)(2,1)S(1)}, bf16[1,144,1024]{2,1,0:T(8,128)(2,1)S(1)}, u32[]{:S(2)}, u32[]{:S(2)}) collective-permute-start(bf16[1,144,1024]{2,1,0:T(8,128)(2,1)S(1)} %add_convert_fusion.2), channel_id=1, source_target_pairs={{0,4},{2,6},{4,8},{6,10},{8,12},{10,14},{12,0},{14,2},{1,5},{3,7},... | collective-permute-start | bytes 884744 | tf_op jit(solution)/shard_map/ppermute | solution.py:450
  134.5 11.0 %collective-permute-start.33 = (bf16[1,144,1024]{2,1,0:T(8,128)(2,1)S(1)}, bf16[1,144,1024]{2,1,0:T(8,128)(2,1)S(1)}, u32[]{:S(2)}, u32[]{:S(2)}) collective-permute-start(bf16[1,144,1024]{2,1,0:T(8,128)(2,1)S(1)} %copy-done.25), channel_id=1, source_target_pairs={{0,2},{2,0},{4,6},{6,4},{8,10},{10,8},{12,14},{14,12},{1,3},{3,1},... | collective-permute-start | bytes 884744 | tf_op jit(solution)/shard_map/ppermute | solution.py:447
  135.9 9.6 %collective-permute-start.37 = (bf16[1,144,1024]{2,1,0:T(8,128)(2,1)S(1)}, bf16[1,144,1024]{2,1,0:T(8,128)(2,1)S(1)}, u32[]{:S(2)}, u32[]{:S(2)}) collective-permute-start(bf16[1,144,1024]{2,1,0:T(8,128)(2,1)S(1)} %add_convert_fusion), channel_id=1, source_target_pairs={{0,1},{1,0},{2,3},{3,2},{4,5},{5,4},{6,7},{7,6},{8,9},{9,8},{10,11... | collective-permute-start | bytes 884744 | tf_op jit(solution)/shard_map/ppermute | solution.py:441
  (18 other events, 56.3 us)

commit v9 on v8

--- a/solution.py
+++ b/solution.py
@@ -166,10 +166,11 @@
 def rows_kernel(count, ways, capacity, slots, where_ref, *refs):
     weights_in, units_in, tables_in = refs[:4], refs[4 : 4 + 4 * count], refs[4 + 4 * count : 4 + 5 * count]
     leaves = 1 + max(way[0] for way in ways.values())
-    refs = refs[len(refs) - 17 - leaves :]
+    carried_in = refs[4 + 5 * count : 4 + 5 * count + sum(len(block) == 1 for block in ways)]
+    refs = refs[len(refs) - 18 - leaves :]
     outs, packets, refs = refs[:2], refs[2 : 2 + leaves], refs[2 + leaves :]
-    x_all, g_all, tables, wgu0, wgu1, wd0, wd1, xc, gc, both, scaled, piece, unit_sems, weight_sems = refs[:14]
-    out_sems = refs[14]
+    x_all, g_all, tables, wgu0, wgu1, wd0, wd1, xc, gc, both, scaled, dense, piece, unit_sems, weight_sems = refs[:15]
+    out_sems = refs[15]
     half, tok = x_all.shape[3], x_all.shape[2] // 2
     part = scaled.shape[2]
     owners = tables.shape[2]
@@ -188,7 +189,7 @@
         pltpu.make_async_copy(source, target, weight_sems.at[index])
         for index, (source, target) in enumerate(zip(weights_in, (wgu0, wgu1, wd0, wd1)))
     ]
-    for copy in t_copies + x_copies + weight_copies[:2] + g_copies + weight_copies[2:]:
+    for copy in t_copies + x_copies + weight_copies[:2]:
         copy.start()
     leaving = []
 
@@ -196,6 +197,10 @@
         copy = pltpu.make_async_copy(source, target, out_sems.at[len(leaving)])
         copy.start()
         leaving.append(copy)
+
+    for index, block in enumerate(carried_in):
+        number, slot = ways[(index,)]
+        leave(block.at[0], packets[number].at[slot])
 
     def leave_rows(held, start):
         for expert in range(2):
@@ -232,23 +237,25 @@
     spans = [pl.ds(chunk * slots, slots) for chunk in range(count)]
     sides = [slice(side * half, (side + 1) * half) for side in range(2)]
 
-    def gather(copies, source, target):
+    def gather(copies, source, target, following):
+        for copy in copies:
+            copy.wait()
+        for copy in following:
+            copy.start()
         for chunk in range(count):
-            for copy in copies[4 * chunk : 4 * chunk + 4]:
-                copy.wait()
             both_picks = jnp.concatenate([low_picks[chunk, expert] for expert in range(2)], 0)
             for side in range(2):
                 rows = dot(both_picks, source[chunk, side], ((1,), (0,))).astype(jnp.bfloat16)
                 for expert in range(2):
                     target[expert, spans[chunk], sides[side]] = rows[expert * slots : (expert + 1) * slots]
 
-    gather(x_copies, x_all, xc)
+    gather(x_copies, x_all, xc, g_copies + weight_copies[2:])
     leave_rows(xc, 0)
     rows = []
     for expert in range(2):
         weight_copies[expert].wait()
         rows.append(dot(xc[expert], wgu[expert][...], ((1,), (0,))))
-    gather(g_copies, g_all, gc)
+    gather(g_copies, g_all, gc, ())
     leave_rows(gc, 2 * half)
     scores = []
     for expert in range(2):
@@ -280,24 +287,24 @@
                 extra = extra + jnp.where((names == where_ref[expert]) & (column == where_ref[2]), line, 0.0)
             for side in range(2):
                 piece[chunk, side, y, tok:] = extra.astype(jnp.bfloat16)
+    for chunk in range(count):
+        for expert in range(2):
+            placed = dot(low_picks[chunk, expert], both[expert, spans[chunk], :], ((0,), (0,)))
+            dense[expert, pl.ds(chunk * 2 * tok, 2 * tok)] = placed.astype(jnp.bfloat16)
     for side in (1, 0):
-        low = [
-            dot(both[expert], wgu[expert][sides[side], :], ((1,), (1,))).astype(jnp.bfloat16) for expert in range(2)
-        ]
+        total = dot(dense[0], wgu0[sides[side], :], ((1,), (1,)))
+        total = total + dot(dense[1], wgu1[sides[side], :], ((1,), (1,)))
         for chunk in range(count):
-            total = None
-            for expert in range(2):
-                term = dot(low_picks[chunk, expert], low[expert][chunk * slots : (chunk + 1) * slots], ((0,), (0,)))
-                total = term if total is None else total + term
             for y in range(2):
-                piece[chunk, side, y, :tok] = total[y * tok : (y + 1) * tok].astype(jnp.bfloat16)
+                start = (2 * chunk + y) * tok
+                piece[chunk, side, y, :tok] = total[start : start + tok].astype(jnp.bfloat16)
                 number, slot = ways[chunk, y, side]
                 leave(piece.at[chunk, side, y], packets[number].at[slot])
     for copy in leaving:
         copy.wait()
 
 
-def rows_call(items, owners, capacity, slots, where, weights, units, tables, after):
+def rows_call(items, owners, capacity, slots, where, weights, units, tables, carried, after):
     count = len(tables)
     ways = {block: (number, slot) for number, blocks in enumerate(items) for slot, block in enumerate(blocks)}
     tok, half = units[0].shape[0] // 2, units[0].shape[1]
@@ -309,7 +316,7 @@
         grid_spec=pltpu.PrefetchScalarGridSpec(
             num_scalar_prefetch=1,
             grid=(1,),
-            in_specs=[LOOSE] * (4 + 5 * count + len(after)),
+            in_specs=[LOOSE] * (4 + 5 * count + len(carried) + len(after)),
             out_specs=[LOOSE] * (2 + len(items)),
             scratch_shapes=[pltpu.VMEM((count, 2, 2 * tok, half), jnp.bfloat16)] * 2
             + [pltpu.VMEM((count, 2, owners, tok), jnp.bfloat16)]
@@ -317,10 +324,11 @@
             + [pltpu.VMEM((part, width), jnp.bfloat16)] * 2
             + [pltpu.VMEM((2, count * slots, size), jnp.bfloat16) for size in widths]
             + [
+                pltpu.VMEM((2, count * 2 * tok, 2 * part), jnp.bfloat16),
                 pltpu.VMEM((count, 2, 2) + packet, jnp.bfloat16),
                 pltpu.SemaphoreType.DMA((3, 4 * count)),
                 pltpu.SemaphoreType.DMA((4,)),
-                pltpu.SemaphoreType.DMA((8 + 4 * count,)),
+                pltpu.SemaphoreType.DMA((8 + 4 * count + len(carried),)),
             ],
         ),
         out_shape=[jax.ShapeDtypeStruct((count * slots, sum(widths)), jnp.bfloat16)] * 2
@@ -332,7 +340,7 @@
             transcendentals=2 * count * slots * part,
         ),
         name="rows",
-    )(where, *weights, *units, *tables, *after)
+    )(where, *weights, *units, *tables, *carried, *after)
 
 
 def grads_kernel(count, wide, deep, blocks, tp_ref, *refs):
@@ -419,7 +427,7 @@
             ],
         ),
         out_shape=[jax.ShapeDtypeStruct(shape, jnp.bfloat16) for shape in shapes],
-        compiler_params=pltpu.CompilerParams(vmem_limit_bytes=24 << 20),
+        compiler_params=pltpu.CompilerParams(vmem_limit_bytes=62 << 20),
         cost_estimate=pl.CostEstimate(
             flops=2 * rows * width * deep, bytes_accessed=2 * rows * (width + deep), transcendentals=0
         ),
@@ -484,9 +492,9 @@
     both_w, down_w = weights_call(which_ref, w_gate, w_up, w_down)
     width, part = both_w.shape[0], down_w.shape[0]
 
-    def rows_of(steps, items, after):
+    def rows_of(steps, items, carried=(), after=()):
         four = [units[z, y, x] for z in steps for y in range(2) for x in range(2)]
-        return rows_call(items, owners, capacity, slots, where, weights, four, [tables[z] for z in steps], after)
+        return rows_call(items, owners, capacity, slots, where, weights, four, [tables[z] for z in steps], carried, after)
 
     units = {(0, 0, 0): jnp.concatenate([tokens, out_grad], 0)}
     settled = dict(units)
@@ -508,38 +516,41 @@
             tables = [over_z(table, z) if z else table for z in range(n_z)]
         if number == 2:
             mine_0, other_0, near, side_0, far, y_0 = rows_of(
-                [0], [[(0, 0, 0)], [(0, 0, 1)], [(0, 1, 1)], [(0, 1, 0)]], []
+                [0], [[(0, 0, 0)], [(0, 0, 1)], [(0, 1, 1)], [(0, 1, 0)]]
             )
             extra = [mine_0]
+        if number == 3:
+            (other_0,) = tied([other_0], [settled[0, 0, 0]])
+            other_0 = over_role(other_0)
+            extra = [other_0] + tables[1:]
         names = list(settled)
         settled = dict(zip(names, tied([settled[item] for item in names], extra)))
 
     def total(*blocks):
         return sum(block.astype(jnp.float32) for block in blocks).astype(jnp.bfloat16)
 
-    items = [[(1, 1, 1)], [(1, 0, 1), (0, 0, 1)], [(0, 1, 0)], [(0, 1, 1)], [(0, 0, 0)], [(1, 0, 0)], [(1, 1, 0)]]
-    mine_1, other_1, x_2, x_12, y_1, z_1, keep_1, keep_2, keep_2y = rows_of([1, 2], items, [])
-    other_1, x_2, x_12, y_1, z_1 = tied([other_1, x_2, x_12, y_1, z_1], arrived.values())
+    items = [[(1, 1, 1), (1, 0, 1)], [(0, 1, 0), (0,)], [(0, 1, 1)], [(0, 0, 1)], [(0, 0, 0)], [(1, 0, 0)], [(1, 1, 0)]]
+    mine_1, other_1, x_2, y_1, z_1, x_1, keep_1, keep_2, keep_2y = rows_of([1, 2], items, [y_0])
+    other_1, x_2, y_1, z_1 = tied([other_1, x_2, y_1, z_1], arrived.values())
     from_x2, from_y1, from_z1 = over_x(x_2), over_y(y_1), over_z(z_1, -1)
-    from_x12 = over_x(x_12)
-    items = [[(0, 0, 1)], [(0, 1, 0)], [(0, 1, 1)], [(0, 0, 0)]]
-    mine_3, other_3, x_3, y_3, z_3, keep_3 = rows_of([3], items, [mine_1])
+    items = [[(0, 0, 1), (0,)], [(0, 1, 0)], [(0, 1, 1)], [(0, 0, 0)]]
+    mine_3, other_3, x_3, y_3, z_3, keep_3 = rows_of([3], items, [x_1], [mine_1])
     mine_3, other_3, x_3, y_3, z_3, keep_2y = tied(
         [mine_3, other_3, x_3, y_3, z_3, keep_2y], [from_x2, from_y1, from_z1]
     )
-    from_z3, from_x3, from_y2, from_y3 = over_z(z_3, 1), over_x(x_3), over_y(total(keep_2y, from_x2)), over_y(y_3)
-    packed = [mine_0, over_role(other_0), mine_1, over_role(other_1), mine_3, over_role(other_3)]
+    from_z3, from_y2 = over_z(z_3, 1), over_y(total(keep_2y, from_x2[:1]))
+    from_x3, from_y3 = over_x(x_3), over_y(y_3)
+    packed = [mine_0, other_0, mine_1, over_role(other_1), mine_3, over_role(other_3)]
+    (d_down,) = grads_call(which_ref, packed, width, part, True)
+    from_z3, from_y2 = tied([from_z3, from_y2], [d_down])
+    from_far = over_y(total(far, from_z1, from_z3))
+    from_z2 = over_z(total(keep_2, from_x2[1:], from_y2), 1)
     d_gate, d_up = grads_call(which_ref, packed, width, part, False)
-    from_z3, from_x12, from_y2 = tied([from_z3, from_x12, from_y2], [d_gate, d_up])
-    from_far = over_y(total(far, from_z1, from_z3))
-    from_z2 = over_z(total(keep_2, from_x12[:1], from_y2), 1)
-    home_1 = over_z(total(keep_1, from_x12[1:], from_y1), -1)
-    (d_down,) = grads_call(which_ref, packed, width, part, True)
-    from_x3, from_y3, from_z2, y_0 = tied([from_x3, from_y3, from_z2, y_0], [d_down])
-    from_y0 = over_y(y_0)
-    home_3 = over_z(total(keep_3, from_x3, from_y3, from_z2), 1)
+    from_x3, from_y3, from_far, from_z2 = tied([from_x3, from_y3, from_far, from_z2], [d_gate, d_up])
+    home_1 = over_z(total(keep_1, from_x3[1:], from_y1[:1]), -1)
+    home_3 = over_z(total(keep_3, from_x3[:1], from_y3, from_z2), 1)
     from_x0 = over_x(total(side_0, from_far))
-    home = (near, from_y0, home_1, home_3, from_x0)
+    home = (near, from_y1[1:], home_1, home_3, from_x0)
     d_tok = sum(block[0, :tok_rows].astype(jnp.float32) for block in home).astype(jnp.bfloat16)
     home = sum(block[0, tok_rows:, : 4 * tok_rows].astype(jnp.float32) for block in home)
     score = jnp.sum(home.reshape(owners, 4, tok_rows), axis=1).T

time: 148 us -> 164 us (1.11)
  waiting for transfers between devices: 38 us -> 59.3 us
  starting transfers between devices: 42.9 us -> 33.6 us
  other arithmetic: 5.71 us -> 10.2 us
  Pallas kernels: 51.6 us -> 54.8 us
  local copies, waits for them, and re-layouts: 7.78 us -> 5.1 us
    ppermute x13, waiting for transfers between devices: 36.5 us -> 54.5 us  [over_z(): lax.ppermute(array, 'ep', [(i, (i + shift * n_y) % ep) for i in range(ep)])]
    ppermute x13, starting transfers between devices: 18 us -> 13.3 us  [over_z(): lax.ppermute(array, 'ep', [(i, (i + shift * n_y) % ep) for i in range(ep)])]
    convert_element_type x5, other arithmetic: 2.87 us -> 7.42 us  [total(): sum((block.astype(jnp.float32) for block in blocks)).astype(jnp.bfloat16)]
    pallas_call x2, Pallas kernels: 12.7 us -> 15.8 us  [grads_call(): pl.pallas_call(functools.partial(grads_kernel, count, *starts, 2 * per),...]
    ppermute x11 -> x10, waiting for transfers between devices: 0.72 us -> 3.77 us  [over_y(): lax.ppermute(array, 'ep', [(i, i + 1 - 2 * (i % n_y)) for i in range(ep)])]
    unnamed x57 -> x53, local copies, waits for them, and re-layouts: 6.79 us -> 4.11 us
    ppermute x9 -> x8, starting transfers between devices: 11.1 us -> 8.5 us  [over_x(): return lax.ppermute(array, 'tp', [(0, 1), (1, 0)])]
    ppermute x11 -> x10, starting transfers between devices: 12.8 us -> 11.2 us  [over_y(): lax.ppermute(array, 'ep', [(i, i + 1 - 2 * (i % n_y)) for i in range(ep)])]
  transfers between devices with their start and end apart: 38 -> 36, of which waited for: 9 -> 12; matrix products, arithmetic and copies ran while one was open for 3% -> 4% of each run, Pallas kernels for 35% -> 33%
where the time goes in v9:
time: 164 us
  waiting for transfers between devices  59.3 us (36%)
  Pallas kernels  54.8 us (33%)
  starting transfers between devices  33.6 us (20%)
  other arithmetic  10.2 us (6%)
  local copies, waits for them, and re-layouts  5.1 us (3%)
    ppermute x13, waiting for transfers between devices, over_z(): lax.ppermute(array, 'ep', [(i, (i + shift * n_y) % ep) for i in range(ep)])  54.5 us
    pallas_call x3, Pallas kernels, rows_call(): pl.pallas_call(functools.partial(rows_kernel, count, ways, capacity, slot...  35 us
    pallas_call x2, Pallas kernels, grads_call(): pl.pallas_call(functools.partial(grads_kernel, count, *starts, 2 * per),...  15.8 us
    ppermute x13, starting transfers between devices, over_z(): lax.ppermute(array, 'ep', [(i, (i + shift * n_y) % ep) for i in range(ep)])  13.3 us
    ppermute x10, starting transfers between devices, over_y(): lax.ppermute(array, 'ep', [(i, i + 1 - 2 * (i % n_y)) for i in range(ep)])  11.2 us
    ppermute x8, starting transfers between devices, over_x(): return lax.ppermute(array, 'tp', [(0, 1), (1, 0)])  8.5 us
    convert_element_type x5, other arithmetic, total(): sum((block.astype(jnp.float32) for block in blocks)).astype(jnp.bfloat16)  7.42 us
    unnamed x53, local copies, waits for them, and re-layouts  4.11 us
  transfers between devices with their start and end apart: 36, of which 12 were waited for; matrix products, arithmetic and copies ran while one was open for 4% of the time, Pallas kernels for 33%

profile of v9, /device:TPU:0, one launch (start us, length us, event | category | flops | bytes accessed | tf_op | source)
XLA Modules:
  0.0 164.1 jit_solution(17139817501851860364)
XLA Ops:
  0.6 1.0 constant_dynamic-update-slice_fusion.1
  1.6 1.0 constant_dynamic-update-slice_fusion.refs_4_
  2.6 3.1 %collective-permute-start = (bf16[256,1024]{1,0:T(8,128)(2,1)S(1)}, bf16[256,1024]{1,0:T(8,128)(2,1)S(1)}, u32[]{:S(2)}, u32[]{:S(2)}) collective-permute-start(bf16[256,1024]{1,0:T(8,128)(2,1)S(1)} %constant_dynamic-update-slice_fusion.refs_4_), channel_id=1, source_target_pairs={{0,4},{2,6},{4,8},{6,10},{8,12},{10,14},{12,0},{14,2},{1,5},{3,7},... | collective-permute-start | bytes 1572872 | tf_op jit(solution)/shard_map/ppermute | solution.py:458
  5.7 1.5 collective-permute-start.1
  7.2 1.5 collective-permute-start.2
  8.7 4.0 %weights.1 = (bf16[2048,768]{1,0:T(8,128)(2,1)}, bf16[384,2048]{1,0:T(8,128)(2,1)}) custom-call(s32[1]{0:T(128)} %bitcast.2.tp_ref, bf16[1,2048,384]{2,1,0:T(8,128)(2,1)} %wg_ref.1, bf16[1,2048,384]{2,1,0:T(8,128)(2,1)} %wu_ref.1, bf16[1,384,2048]{2,1,0:T(8,128)(2,1)} %wd_ref.1), custom_call_target="tpu_custom_call" | custom-call | bytes 9437184 | tf_op jit(solution)/shard_map/weights/pallas_call | solution.py:141
  12.7 6.9 %collective-permute-done.refs_4_ = bf16[256,1024]{1,0:T(8,128)(2,1)S(1)} collective-permute-done((bf16[256,1024]{1,0:T(8,128)(2,1)S(1)}, bf16[256,1024]{1,0:T(8,128)(2,1)S(1)}, u32[]{:S(2)}, u32[]{:S(2)}) %collective-permute-start) | collective-permute-done | bytes 524320 | tf_op jit(solution)/shard_map/ppermute | solution.py:458
  19.6 0.8 collective-permute-done.2.refs_5_
  21.1 1.4 collective-permute-start.7
  22.5 1.0 collective-permute-start.8
  23.5 1.5 collective-permute-start.5
  25.0 12.0 %collective-permute-done.7.refs_8_ = bf16[256,1024]{1,0:T(8,128)(2,1)} collective-permute-done((bf16[256,1024]{1,0:T(8,128)(2,1)}, bf16[256,1024]{1,0:T(8,128)(2,1)}, u32[]{:S(2)}, u32[]{:S(2)}) %collective-permute-start.7) | collective-permute-done | bytes 524320 | tf_op jit(solution)/shard_map/ppermute | solution.py:458
  37.0 1.5 collective-permute-start.6
  39.2 1.5 collective-permute-start.11
  40.7 1.3 collective-permute-start.9
  42.0 0.6 pad_add_fusion.where_ref
  42.6 0.6 pad_maximum_fusion.refs_8_
  43.2 1.1 copy-done
  44.4 10.1 %rows.3 = (bf16[144,5248]{1,0:T(8,128)(2,1)}, bf16[144,5248]{1,0:T(8,128)(2,1)}, bf16[1,144,1024]{2,1,0:T(8,128)(2,1)}, bf16[1,144,1024]{2,1,0:T(8,128)(2,1)}, b...) custom-call(s32[3]{0:T(128)} %pad_add_fusion.where_ref, bf16[2048,768]{1,0:T(8,128)(2,1)} %get-tuple-element.68.refs_0_, ...), custom_call_target="tpu_custom_call" | custom-call | flops 3170893824 | bytes 13631488 | tf_op jit(solution)/shard_map/rows/pallas_call | solution.py:314
  54.5 0.7 collective-permute-start.12
  55.2 1.6 collective-permute-start.13
  56.8 1.6 collective-permute-start.14
  58.4 13.0 %collective-permute-done.15.refs_12_ = bf16[2,16,128]{2,1,0:T(8,128)(2,1)S(1)} collective-permute-done((bf16[2,16,128]{2,1,0:T(8,128)(2,1)S(1)}, bf16[2,16,128]{2,1,0:T(8,128)(2,1)S(1)}, u32[]{:S(2)}, u32[]{:S(2)}) %collective-permute-start.15) | collective-permute-done | bytes 8224 | tf_op jit(solution)/shard_map/ppermute | solution.py:458
  71.4 4.5 %collective-permute-done.16.refs_13_ = bf16[2,16,128]{2,1,0:T(8,128)(2,1)S(1)} collective-permute-done((bf16[2,16,128]{2,1,0:T(8,128)(2,1)S(1)}, bf16[2,16,128]{2,1,0:T(8,128)(2,1)S(1)}, u32[]{:S(2)}, u32[]{:S(2)}) %collective-permute-start.16) | collective-permute-done | bytes 8224 | tf_op jit(solution)/shard_map/ppermute | solution.py:458
  76.0 3.6 %collective-permute-done.18.refs_8_ = bf16[2,16,128]{2,1,0:T(8,128)(2,1)S(1)} collective-permute-done((bf16[2,16,128]{2,1,0:T(8,128)(2,1)S(1)}, bf16[2,16,128]{2,1,0:T(8,128)(2,1)S(1)}, u32[]{:S(2)}, u32[]{:S(2)}) %collective-permute-start.18) | collective-permute-done | bytes 8224 | tf_op jit(solution)/shard_map/ppermute | solution.py:458
  79.7 0.7 copy-done.21
  80.4 1.4 collective-permute-start.20
  81.8 1.5 collective-permute-start.21
  83.3 1.8 %collective-permute-start.19 = (bf16[256,1024]{1,0:T(8,128)(2,1)}, bf16[256,1024]{1,0:T(8,128)(2,1)}, u32[]{:S(2)}, u32[]{:S(2)}) collective-permute-start(bf16[256,1024]{1,0:T(8,128)(2,1)} %copy-done.18), channel_id=1, source_target_pairs={{0,12},{2,14},{4,0},{6,2},{8,4},{10,6},{12,8},{14,10},{1,13},{3,15... | collective-permute-start | bytes 1572872 | tf_op jit(solution)/shard_map/ppermute | solution.py:458
  85.2 13.8 %rows.4 = (bf16[288,5248]{1,0:T(8,128)(2,1)}, bf16[288,5248]{1,0:T(8,128)(2,1)}, bf16[2,144,1024]{2,1,0:T(8,128)(2,1)}, bf16[2,144,1024]{2,1,0:T(8,128)(2,1)}, b...) custom-call(s32[3]{0:T(128)} %pad_add_fusion.where_ref, ...), custom_call_target="tpu_custom_call" | custom-call | flops 6341787648 | bytes 17825792 | tf_op jit(solution)/shard_map/rows/pallas_call | solution.py:314
  99.7 0.6 collective-permute-start.23
  100.3 11.1 %rows.5 = (bf16[144,5248]{1,0:T(8,128)(2,1)}, bf16[144,5248]{1,0:T(8,128)(2,1)}, bf16[2,144,1024]{2,1,0:T(8,128)(2,1)}, bf16[1,144,1024]{2,1,0:T(8,128)(2,1)}, b...) custom-call(s32[3]{0:T(128)} %pad_add_fusion.where_ref, bf16[2048,768]{1,0:T(8,128)(2,1)} %get-tuple-element.68.refs_0_, ...), custom_call_target="tpu_custom_call" | custom-call | flops 3170893824 | bytes 13631488 | tf_op jit(solution)/shard_map/rows/pallas_call | solution.py:314
  111.5 3.6 %collective-permute-done.22 = bf16[2,144,1024]{2,1,0:T(8,128)(2,1)S(1)} collective-permute-done((bf16[2,144,1024]{2,1,0:T(8,128)(2,1)}, bf16[2,144,1024]{2,1,0:T(8,128)(2,1)S(1)}, u32[]{:S(2)}, u32[]{:S(2)}) %collective-permute-start.22) | collective-permute-done | bytes 589856 | tf_op jit(solution)/shard_map/ppermute | solution.py:455
  116.1 1.8 %add_convert_fusion.5 = bf16[1,144,1024]{2,1,0:T(8,128)(2,1)} fusion(bf16[1,144,1024]{2,1,0:T(8,128)(2,1)S(1)} %copy-done.7, bf16[2,144,1024]{2,1,0:T(8,128)(2,1)} %copy-done.3), kind=kLoop, calls=%fused_computation.5 | loop fusion | flops 589824 | bytes 884736 | tf_op jit(solution)/shard_map/convert_element_type | solution.py:530
  117.9 1.5 collective-permute-start.28
  120.2 1.0 collective-permute-start.26
  121.3 6.6 %grads.2 = bf16[1,384,2048]{2,1,0:T(8,128)(2,1)} custom-call(s32[1]{0:T(128)} %bitcast.2.tp_ref, bf16[144,5248]{1,0:T(8,128)(2,1)} %get-tuple-element.81.refs_0_, bf16[144,5248]{1,0:T(8,128)(2,1)} %copy-done.1, bf16[288,5248]{1,0:T(8,128)(2,1)} %get-tuple-element.99.refs_10_.refs_2_, bf16[288,5248]{1,0:T(8,128)(2,1)} %collective-permute-done.29.refs_3_, ...), custom_call_target="tpu_custom_call" | custom-call | flops 1811939328 | bytes 5603328 | tf_op jit(solution)/shard_map/grads/pallas_call | solution.py:415
  128.0 2.7 %collective-permute-done.27 = bf16[1,144,1024]{2,1,0:T(8,128)(2,1)} collective-permute-done((bf16[1,144,1024]{2,1,0:T(8,128)(2,1)}, bf16[1,144,1024]{2,1,0:T(8,128)(2,1)}, u32[]{:S(2)}, u32[]{:S(2)}) %collective-permute-start.27) | collective-permute-done | bytes 294944 | tf_op jit(solution)/shard_map/ppermute | solution.py:458
  130.7 2.0 %add_convert_fusion.3 = bf16[1,144,1024]{2,1,0:T(8,128)(2,1)} fusion(bf16[1,144,1024]{2,1,0:T(8,128)(2,1)} %collective-permute-done.28, bf16[1,144,1024]{2,1,0:T(8,128)(2,1)} %get-tuple-element.117, bf16[2,144,1024]{2,1,0:T(8,128)(2,1)} %copy-done.3), kind=kLoop, calls=%fused_computation.3 | loop fusion | flops 884736 | bytes 1179648 | tf_op jit(solution)/shard_map/convert_element_type | solution.py:530
  132.7 1.9 %add_convert_fusion.4 = bf16[1,144,1024]{2,1,0:T(8,128)(2,1)} fusion(bf16[1,144,1024]{2,1,0:T(8,128)(2,1)} %collective-permute-done.27, bf16[1,144,1024]{2,1,0:T(8,128)(2,1)} %collective-permute-done.24, bf16[1,144,1024]{2,1,0:T(8,128)(2,1)S(1)} %copy-done.8), kind=kLoop, calls=%fused_computation.4 | loop fusion | flops 884736 | bytes 1179648 | tf_op jit(solution)/shard_map/convert_element_type | solution.py:530
  135.1 9.3 %grads.3 = (bf16[1,2048,384]{2,1,0:T(8,128)(2,1)}, bf16[1,2048,384]{2,1,0:T(8,128)(2,1)}) custom-call(s32[1]{0:T(128)} %bitcast.2.tp_ref, bf16[144,5248]{1,0:T(8,128)(2,1)} %get-tuple-element.81.refs_0_, bf16[144,5248]{1,0:T(8,128)(2,1)} %copy-done.1, bf16[288,5248]{1,0:T(8,128)(2,1)} %get-tuple-element.99.refs_10_.refs_2_, ...), custom_call_target="tpu_custom_call" | custom-call | flops 3623878656 | bytes 6488064 | tf_op jit(solution)/shard_map/grads/pallas_call | solution.py:415
  144.5 1.6 add_convert_fusion.2
  146.1 3.9 %collective-permute-start.33 = (bf16[1,144,1024]{2,1,0:T(8,128)(2,1)S(1)}, bf16[1,144,1024]{2,1,0:T(8,128)(2,1)S(1)}, u32[]{:S(2)}, u32[]{:S(2)}) collective-permute-start(bf16[1,144,1024]{2,1,0:T(8,128)(2,1)S(1)} %get-tuple-element.127), channel_id=1, source_target_pairs={{0,12},{2,14},{4,0},{6,2},{8,4},{10,6},{12,8},{14,10},{1,13},{3,15... | collective-permute-start | bytes 884744 | tf_op jit(solution)/shard_map/ppermute | solution.py:458
  150.1 0.7 collective-permute-start.35
  150.8 6.7 %collective-permute-done.33 = bf16[1,144,1024]{2,1,0:T(8,128)(2,1)S(1)} collective-permute-done((bf16[1,144,1024]{2,1,0:T(8,128)(2,1)S(1)}, bf16[1,144,1024]{2,1,0:T(8,128)(2,1)S(1)}, u32[]{:S(2)}, u32[]{:S(2)}) %collective-permute-start.33) | collective-permute-done | bytes 294944 | tf_op jit(solution)/shard_map/ppermute | solution.py:458
  157.5 5.0 %collective-permute-done.34 = bf16[1,144,1024]{2,1,0:T(8,128)(2,1)S(1)} collective-permute-done((bf16[1,144,1024]{2,1,0:T(8,128)(2,1)S(1)}, bf16[1,144,1024]{2,1,0:T(8,128)(2,1)S(1)}, u32[]{:S(2)}, u32[]{:S(2)}) %collective-permute-start.34) | collective-permute-done | bytes 294944 | tf_op jit(solution)/shard_map/ppermute | solution.py:458
  162.5 0.6 select_reduce_fusion
  163.1 0.9 fusion
  (99 shorter events, 5.0 us)
Async XLA Ops:
  2.6 10.1 %copy-start.12 = (bf16[256,1024]{1,0:T(8,128)(2,1)}, bf16[256,1024]{1,0:T(8,128)(2,1)S(1)}, u32[]{:S(2)}) copy-start(bf16[256,1024]{1,0:T(8,128)(2,1)S(1)} %constant_dynamic-update-slice_fusion.refs_4_) | copy-start | bytes 1572868
  2.6 17.0 %collective-permute-start = (bf16[256,1024]{1,0:T(8,128)(2,1)S(1)}, bf16[256,1024]{1,0:T(8,128)(2,1)S(1)}, u32[]{:S(2)}, u32[]{:S(2)}) collective-permute-start(bf16[256,1024]{1,0:T(8,128)(2,1)S(1)} %constant_dynamic-update-slice_fusion.refs_4_), channel_id=1, source_target_pairs={{0,4},{2,6},{4,8},{6,10},{8,12},{10,14},{12,0},{14,2},{1,5},{3,7},... | collective-permute-start | bytes 1572872 | tf_op jit(solution)/shard_map/ppermute | solution.py:458
  5.7 14.0 %collective-permute-start.1 = (bf16[256,1024]{1,0:T(8,128)(2,1)S(1)}, bf16[256,1024]{1,0:T(8,128)(2,1)S(1)}, u32[]{:S(2)}, u32[]{:S(2)}) collective-permute-start(bf16[256,1024]{1,0:T(8,128)(2,1)S(1)} %constant_dynamic-update-slice_fusion.refs_4_), channel_id=1, source_target_pairs={{0,2},{2,0},{4,6},{6,4},{8,10},{10,8},{12,14},{14,12},{1,3},{3,1},... | collective-permute-start | bytes 1572872 | tf_op jit(solution)/shard_map/ppermute | solution.py:455
  7.2 13.2 %collective-permute-start.2 = (bf16[256,1024]{1,0:T(8,128)(2,1)S(1)}, bf16[256,1024]{1,0:T(8,128)(2,1)}, u32[]{:S(2)}, u32[]{:S(2)}) collective-permute-start(bf16[256,1024]{1,0:T(8,128)(2,1)S(1)} %constant_dynamic-update-slice_fusion.refs_4_), channel_id=1, source_target_pairs={{0,1},{1,0},{2,3},{3,2},{4,5},{5,4},{6,7},{7,6},{8,9},{9,8},{10,11... | collective-permute-start | bytes 1572872 | tf_op jit(solution)/shard_map/ppermute | solution.py:449
  8.7 16.3 %copy-start.16 = (bf16[128,8]{0,1:T(8,128)(2,1)S(1)}, bf16[128,8]{0,1:T(8,128)(2,1)}, u32[]{:S(2)}) copy-start(bf16[128,8]{0,1:T(8,128)(2,1)} %param.10) | copy-start | bytes 6148
  8.7 16.3 %copy-start.13 = (s32[128,8]{0,1:T(8,128)S(1)}, s32[128,8]{0,1:T(8,128)}, u32[]{:S(2)}) copy-start(s32[128,8]{0,1:T(8,128)} %param.9) | copy-start | bytes 12292
  20.6 22.6 %collective-permute-start.3 = (bf16[2048,768]{1,0:T(8,128)(2,1)}, bf16[2048,768]{1,0:T(8,128)(2,1)}, u32[]{:S(2)}, u32[]{:S(2)}) collective-permute-start(bf16[2048,768]{1,0:T(8,128)(2,1)} %get-tuple-element.68.refs_0_), channel_id=1, source_target_pairs={{0,16},{16,0},{1,17},{17,1},{2,18},{18,2},{3,19},{19,3},{4,20},{20... | collective-permute-start | bytes 9437192 | tf_op jit(solution)/shard_map/ppermute | solution.py:452
  20.6 22.6 %collective-permute-start.4 = (bf16[384,2048]{1,0:T(8,128)(2,1)}, bf16[384,2048]{1,0:T(8,128)(2,1)S(1)}, u32[]{:S(2)}, u32[]{:S(2)}) collective-permute-start(bf16[384,2048]{1,0:T(8,128)(2,1)} %get-tuple-element.69.refs_2_), channel_id=1, source_target_pairs={{0,16},{16,0},{1,17},{17,1},{2,18},{18,2},{3,19},{19,3},{4,20},{20... | collective-permute-start | bytes 4718600 | tf_op jit(solution)/shard_map/ppermute | solution.py:452
  21.1 15.9 %collective-permute-start.7 = (bf16[256,1024]{1,0:T(8,128)(2,1)}, bf16[256,1024]{1,0:T(8,128)(2,1)}, u32[]{:S(2)}, u32[]{:S(2)}) collective-permute-start(bf16[256,1024]{1,0:T(8,128)(2,1)} %copy-done.17), channel_id=1, source_target_pairs={{0,4},{2,6},{4,8},{6,10},{8,12},{10,14},{12,0},{14,2},{1,5},{3,7},... | collective-permute-start | bytes 1572872 | tf_op jit(solution)/shard_map/ppermute | solution.py:458
  22.5 16.1 %collective-permute-start.8 = (bf16[256,1024]{1,0:T(8,128)(2,1)}, bf16[256,1024]{1,0:T(8,128)(2,1)S(1)}, u32[]{:S(2)}, u32[]{:S(2)}) collective-permute-start(bf16[256,1024]{1,0:T(8,128)(2,1)} %copy-done.17), channel_id=1, source_target_pairs={{0,2},{2,0},{4,6},{6,4},{8,10},{10,8},{12,14},{14,12},{1,3},{3,1},... | collective-permute-start | bytes 1572872 | tf_op jit(solution)/shard_map/ppermute | solution.py:455
  23.5 15.1 %collective-permute-start.5 = (bf16[256,1024]{1,0:T(8,128)(2,1)}, bf16[256,1024]{1,0:T(8,128)(2,1)S(1)}, u32[]{:S(2)}, u32[]{:S(2)}) collective-permute-start(bf16[256,1024]{1,0:T(8,128)(2,1)} %copy-done.20), channel_id=1, source_target_pairs={{0,1},{1,0},{2,3},{3,2},{4,5},{5,4},{6,7},{7,6},{8,9},{9,8},{10,11... | collective-permute-start | bytes 1572872 | tf_op jit(solution)/shard_map/ppermute | solution.py:449
  37.0 3.6 %collective-permute-start.6 = (bf16[16,128]{1,0:T(8,128)(2,1)S(1)}, bf16[16,128]{1,0:T(8,128)(2,1)S(1)}, u32[]{:S(2)}, u32[]{:S(2)}) collective-permute-start(bf16[16,128]{1,0:T(8,128)(2,1)S(1)} %get-tuple-element.130), channel_id=1, source_target_pairs={{0,2},{2,0},{4,6},{6,4},{8,10},{10,8},{12,14},{14,12},{1,3},{3,1},... | collective-permute-start | bytes 12296 | tf_op jit(solution)/shard_map/ppermute | solution.py:455
  38.6 15.8 %collective-permute-start.10 = (bf16[256,1024]{1,0:T(8,128)(2,1)}, bf16[256,1024]{1,0:T(8,128)(2,1)}, u32[]{:S(2)}, u32[]{:S(2)}) collective-permute-start(bf16[256,1024]{1,0:T(8,128)(2,1)} %collective-permute-done.7.refs_8_), channel_id=1, source_target_pairs={{0,2},{2,0},{4,6},{6,4},{8,10},{10,8},{12,14},{14,12},{1,3},{3,1},... | collective-permute-start | bytes 1572872 | tf_op jit(solution)/shard_map/ppermute | solution.py:455
  39.2 15.3 %collective-permute-start.11 = (bf16[256,1024]{1,0:T(8,128)(2,1)}, bf16[256,1024]{1,0:T(8,128)(2,1)}, u32[]{:S(2)}, u32[]{:S(2)}) collective-permute-start(bf16[256,1024]{1,0:T(8,128)(2,1)} %collective-permute-done.7.refs_8_), channel_id=1, source_target_pairs={{0,1},{1,0},{2,3},{3,2},{4,5},{5,4},{6,7},{7,6},{8,9},{9,8},{10,11... | collective-permute-start | bytes 1572872 | tf_op jit(solution)/shard_map/ppermute | solution.py:449
  40.7 13.8 %collective-permute-start.9 = (bf16[256,1024]{1,0:T(8,128)(2,1)}, bf16[256,1024]{1,0:T(8,128)(2,1)}, u32[]{:S(2)}, u32[]{:S(2)}) collective-permute-start(bf16[256,1024]{1,0:T(8,128)(2,1)} %copy-done.12), channel_id=1, source_target_pairs={{0,12},{2,14},{4,0},{6,2},{8,4},{10,6},{12,8},{14,10},{1,13},{3,15... | collective-permute-start | bytes 1572872 | tf_op jit(solution)/shard_map/ppermute | solution.py:458
  43.2 15.2 %copy-start.15 = (bf16[2,16,128]{2,1,0:T(8,128)(2,1)S(1)}, bf16[2,16,128]{2,1,0:T(8,128)(2,1)}, u32[]{:S(2)}) copy-start(bf16[2,16,128]{2,1,0:T(8,128)(2,1)} %pad_maximum_fusion.refs_8_) | copy-start | bytes 24580
  54.5 25.2 %collective-permute-start.17 = (bf16[144,5248]{1,0:T(8,128)(2,1)}, bf16[144,5248]{1,0:T(8,128)(2,1)S(1)}, u32[]{:S(2)}, u32[]{:S(2)}) collective-permute-start(bf16[144,5248]{1,0:T(8,128)(2,1)} %get-tuple-element.93), channel_id=1, source_target_pairs={{0,16},{16,0},{1,17},{17,1},{2,18},{18,2},{3,19},{19,3},{4,20},{20... | collective-permute-start | bytes 4534280 | tf_op jit(solution)/shard_map/ppermute | solution.py:452
  54.5 25.1 %collective-permute-start.12 = (bf16[256,1024]{1,0:T(8,128)(2,1)}, bf16[256,1024]{1,0:T(8,128)(2,1)S(1)}, u32[]{:S(2)}, u32[]{:S(2)}) collective-permute-start(bf16[256,1024]{1,0:T(8,128)(2,1)} %copy-done.17), channel_id=1, source_target_pairs={{0,1},{1,0},{2,3},{3,2},{4,5},{5,4},{6,7},{7,6},{8,9},{9,8},{10,11... | collective-permute-start | bytes 1572872 | tf_op jit(solution)/shard_map/ppermute | solution.py:449
  55.2 24.4 %collective-permute-start.13 = (bf16[256,1024]{1,0:T(8,128)(2,1)}, bf16[256,1024]{1,0:T(8,128)(2,1)S(1)}, u32[]{:S(2)}, u32[]{:S(2)}) collective-permute-start(bf16[256,1024]{1,0:T(8,128)(2,1)} %copy-done.18), channel_id=1, source_target_pairs={{0,4},{2,6},{4,8},{6,10},{8,12},{10,14},{12,0},{14,2},{1,5},{3,7},... | collective-permute-start | bytes 1572872 | tf_op jit(solution)/shard_map/ppermute | solution.py:458
  56.8 22.8 %collective-permute-start.14 = (bf16[256,1024]{1,0:T(8,128)(2,1)}, bf16[256,1024]{1,0:T(8,128)(2,1)S(1)}, u32[]{:S(2)}, u32[]{:S(2)}) collective-permute-start(bf16[256,1024]{1,0:T(8,128)(2,1)} %collective-permute-done.11.refs_9_), channel_id=1, source_target_pairs={{0,2},{2,0},{4,6},{6,4},{8,10},{10,8},{12,14},{14,12},{1,3},{3,1},... | collective-permute-start | bytes 1572872 | tf_op jit(solution)/shard_map/ppermute | solution.py:455
  58.4 13.0 %collective-permute-start.15 = (bf16[2,16,128]{2,1,0:T(8,128)(2,1)S(1)}, bf16[2,16,128]{2,1,0:T(8,128)(2,1)S(1)}, u32[]{:S(2)}, u32[]{:S(2)}) collective-permute-start(bf16[2,16,128]{2,1,0:T(8,128)(2,1)S(1)} %copy-done.15), channel_id=1, source_target_pairs={{0,4},{2,6},{4,8},{6,10},{8,12},{10,14},{12,0},{14,2},{1,5},{3,7},... | collective-permute-start | bytes 24584 | tf_op jit(solution)/shard_map/ppermute | solution.py:458
  71.4 13.7 %copy-start.24 = (bf16[2,16,128]{2,1,0:T(8,128)(2,1)}, bf16[2,16,128]{2,1,0:T(8,128)(2,1)S(1)}, u32[]{:S(2)}) copy-start(bf16[2,16,128]{2,1,0:T(8,128)(2,1)S(1)} %collective-permute-done.15.refs_12_) | copy-start | bytes 24580
  71.4 4.5 %collective-permute-start.16 = (bf16[2,16,128]{2,1,0:T(8,128)(2,1)S(1)}, bf16[2,16,128]{2,1,0:T(8,128)(2,1)S(1)}, u32[]{:S(2)}, u32[]{:S(2)}) collective-permute-start(bf16[2,16,128]{2,1,0:T(8,128)(2,1)S(1)} %copy-done.15), channel_id=1, source_target_pairs={{0,8},{2,10},{4,12},{6,14},{8,0},{10,2},{12,4},{14,6},{1,9},{3,11}... | collective-permute-start | bytes 24584 | tf_op jit(solution)/shard_map/ppermute | solution.py:458
  76.0 3.7 %collective-permute-start.18 = (bf16[2,16,128]{2,1,0:T(8,128)(2,1)S(1)}, bf16[2,16,128]{2,1,0:T(8,128)(2,1)S(1)}, u32[]{:S(2)}, u32[]{:S(2)}) collective-permute-start(bf16[2,16,128]{2,1,0:T(8,128)(2,1)S(1)} %copy-done.15), channel_id=1, source_target_pairs={{0,12},{2,14},{4,0},{6,2},{8,4},{10,6},{12,8},{14,10},{1,13},{3,15... | collective-permute-start | bytes 24584 | tf_op jit(solution)/shard_map/ppermute | solution.py:458
  79.6 19.4 %copy-start.14 = (bf16[2,16,128]{2,1,0:T(8,128)(2,1)}, bf16[2,16,128]{2,1,0:T(8,128)(2,1)S(1)}, u32[]{:S(2)}) copy-start(bf16[2,16,128]{2,1,0:T(8,128)(2,1)S(1)} %collective-permute-done.18.refs_8_) | copy-start | bytes 24580
  80.4 18.6 %copy-start.1 = (bf16[144,5248]{1,0:T(8,128)(2,1)}, bf16[144,5248]{1,0:T(8,128)(2,1)S(1)}, u32[]{:S(2)}) copy-start(bf16[144,5248]{1,0:T(8,128)(2,1)S(1)} %collective-permute-done.17.refs_1_) | copy-start | bytes 4534276
  80.4 18.6 %collective-permute-start.20 = (bf16[256,1024]{1,0:T(8,128)(2,1)}, bf16[256,1024]{1,0:T(8,128)(2,1)}, u32[]{:S(2)}, u32[]{:S(2)}) collective-permute-start(bf16[256,1024]{1,0:T(8,128)(2,1)} %collective-permute-done.9.refs_4_), channel_id=1, source_target_pairs={{0,2},{2,0},{4,6},{6,4},{8,10},{10,8},{12,14},{14,12},{1,3},{3,1},... | collective-permute-start | bytes 1572872 | tf_op jit(solution)/shard_map/ppermute | solution.py:455
  81.8 17.2 %collective-permute-start.21 = (bf16[256,1024]{1,0:T(8,128)(2,1)}, bf16[256,1024]{1,0:T(8,128)(2,1)}, u32[]{:S(2)}, u32[]{:S(2)}) collective-permute-start(bf16[256,1024]{1,0:T(8,128)(2,1)} %collective-permute-done.9.refs_4_), channel_id=1, source_target_pairs={{0,1},{1,0},{2,3},{3,2},{4,5},{5,4},{6,7},{7,6},{8,9},{9,8},{10,11... | collective-permute-start | bytes 1572872 | tf_op jit(solution)/shard_map/ppermute | solution.py:449
  83.3 15.7 %collective-permute-start.19 = (bf16[256,1024]{1,0:T(8,128)(2,1)}, bf16[256,1024]{1,0:T(8,128)(2,1)}, u32[]{:S(2)}, u32[]{:S(2)}) collective-permute-start(bf16[256,1024]{1,0:T(8,128)(2,1)} %copy-done.18), channel_id=1, source_target_pairs={{0,12},{2,14},{4,0},{6,2},{8,4},{10,6},{12,8},{14,10},{1,13},{3,15... | collective-permute-start | bytes 1572872 | tf_op jit(solution)/shard_map/ppermute | solution.py:458
  99.0 22.1 %collective-permute-start.29 = (bf16[288,5248]{1,0:T(8,128)(2,1)}, bf16[288,5248]{1,0:T(8,128)(2,1)}, u32[]{:S(2)}, u32[]{:S(2)}) collective-permute-start(bf16[288,5248]{1,0:T(8,128)(2,1)} %get-tuple-element.113), channel_id=1, source_target_pairs={{0,16},{16,0},{1,17},{17,1},{2,18},{18,2},{3,19},{19,3},{4,20},{20... | collective-permute-start | bytes 9068552 | tf_op jit(solution)/shard_map/ppermute | solution.py:452
  99.1 16.0 %collective-permute-start.22 = (bf16[2,144,1024]{2,1,0:T(8,128)(2,1)}, bf16[2,144,1024]{2,1,0:T(8,128)(2,1)S(1)}, u32[]{:S(2)}, u32[]{:S(2)}) collective-permute-start(bf16[2,144,1024]{2,1,0:T(8,128)(2,1)} %get-tuple-element.96), channel_id=1, source_target_pairs={{0,2},{2,0},{4,6},{6,4},{8,10},{10,8},{12,14},{14,12},{1,3},{3,1},... | collective-permute-start | bytes 1769480 | tf_op jit(solution)/shard_map/ppermute | solution.py:455
  99.7 15.6 %collective-permute-start.23 = (bf16[2,144,1024]{2,1,0:T(8,128)(2,1)}, bf16[2,144,1024]{2,1,0:T(8,128)(2,1)S(1)}, u32[]{:S(2)}, u32[]{:S(2)}) collective-permute-start(bf16[2,144,1024]{2,1,0:T(8,128)(2,1)} %get-tuple-element.106), channel_id=1, source_target_pairs={{0,1},{1,0},{2,3},{3,2},{4,5},{5,4},{6,7},{7,6},{8,9},{9,8},{10,11... | collective-permute-start | bytes 1769480 | tf_op jit(solution)/shard_map/ppermute | solution.py:449
  100.3 11.2 %collective-permute-start.24 = (bf16[1,144,1024]{2,1,0:T(8,128)(2,1)}, bf16[1,144,1024]{2,1,0:T(8,128)(2,1)}, u32[]{:S(2)}, u32[]{:S(2)}) collective-permute-start(bf16[1,144,1024]{2,1,0:T(8,128)(2,1)} %get-tuple-element.107), channel_id=1, source_target_pairs={{0,12},{2,14},{4,0},{6,2},{8,4},{10,6},{12,8},{14,10},{1,13},{3,15... | collective-permute-start | bytes 884744 | tf_op jit(solution)/shard_map/ppermute | solution.py:458
  100.3 15.8 %copy-start.7 = (bf16[1,144,1024]{2,1,0:T(8,128)(2,1)S(1)}, bf16[1,144,1024]{2,1,0:T(8,128)(2,1)}, u32[]{:S(2)}) copy-start(bf16[1,144,1024]{2,1,0:T(8,128)(2,1)} %get-tuple-element.112) | copy-start | bytes 884740
  116.1 4.1 %collective-permute-start.30 = (bf16[144,5248]{1,0:T(8,128)(2,1)}, bf16[144,5248]{1,0:T(8,128)(2,1)S(1)}, u32[]{:S(2)}, u32[]{:S(2)}) collective-permute-start(bf16[144,5248]{1,0:T(8,128)(2,1)} %get-tuple-element.115), channel_id=1, source_target_pairs={{0,16},{16,0},{1,17},{17,1},{2,18},{18,2},{3,19},{19,3},{4,20},{20... | collective-permute-start | bytes 4534280 | tf_op jit(solution)/shard_map/ppermute | solution.py:452
  117.9 14.8 %copy-start.8 = (bf16[1,144,1024]{2,1,0:T(8,128)(2,1)S(1)}, bf16[1,144,1024]{2,1,0:T(8,128)(2,1)}, u32[]{:S(2)}) copy-start(bf16[1,144,1024]{2,1,0:T(8,128)(2,1)} %get-tuple-element.110) | copy-start | bytes 884740
  117.9 10.1 %collective-permute-start.28 = (bf16[1,144,1024]{2,1,0:T(8,128)(2,1)}, bf16[1,144,1024]{2,1,0:T(8,128)(2,1)}, u32[]{:S(2)}, u32[]{:S(2)}) collective-permute-start(bf16[1,144,1024]{2,1,0:T(8,128)(2,1)} %add_convert_fusion.5), channel_id=1, source_target_pairs={{0,2},{2,0},{4,6},{6,4},{8,10},{10,8},{12,14},{14,12},{1,3},{3,1},... | collective-permute-start | bytes 884744 | tf_op jit(solution)/shard_map/ppermute | solution.py:455
  119.4 11.3 %collective-permute-start.27 = (bf16[1,144,1024]{2,1,0:T(8,128)(2,1)}, bf16[1,144,1024]{2,1,0:T(8,128)(2,1)}, u32[]{:S(2)}, u32[]{:S(2)}) collective-permute-start(bf16[1,144,1024]{2,1,0:T(8,128)(2,1)} %get-tuple-element.111), channel_id=1, source_target_pairs={{0,4},{2,6},{4,8},{6,10},{8,12},{10,14},{12,0},{14,2},{1,5},{3,7},... | collective-permute-start | bytes 884744 | tf_op jit(solution)/shard_map/ppermute | solution.py:458
  119.6 24.8 %collective-permute-start.25 = (bf16[2,144,1024]{2,1,0:T(8,128)(2,1)}, bf16[2,144,1024]{2,1,0:T(8,128)(2,1)}, u32[]{:S(2)}, u32[]{:S(2)}) collective-permute-start(bf16[2,144,1024]{2,1,0:T(8,128)(2,1)} %get-tuple-element.108), channel_id=1, source_target_pairs={{0,1},{1,0},{2,3},{3,2},{4,5},{5,4},{6,7},{7,6},{8,9},{9,8},{10,11... | collective-permute-start | bytes 1769480 | tf_op jit(solution)/shard_map/ppermute | solution.py:449
  120.2 24.2 %collective-permute-start.26 = (bf16[1,144,1024]{2,1,0:T(8,128)(2,1)}, bf16[1,144,1024]{2,1,0:T(8,128)(2,1)}, u32[]{:S(2)}, u32[]{:S(2)}) collective-permute-start(bf16[1,144,1024]{2,1,0:T(8,128)(2,1)} %get-tuple-element.109), channel_id=1, source_target_pairs={{0,2},{2,0},{4,6},{6,4},{8,10},{10,8},{12,14},{14,12},{1,3},{3,1},... | collective-permute-start | bytes 884744 | tf_op jit(solution)/shard_map/ppermute | solution.py:455
  132.7 11.7 %collective-permute-start.32 = (bf16[1,144,1024]{2,1,0:T(8,128)(2,1)}, bf16[1,144,1024]{2,1,0:T(8,128)(2,1)}, u32[]{:S(2)}, u32[]{:S(2)}) collective-permute-start(bf16[1,144,1024]{2,1,0:T(8,128)(2,1)} %add_convert_fusion.3), channel_id=1, source_target_pairs={{0,4},{2,6},{4,8},{6,10},{8,12},{10,14},{12,0},{14,2},{1,5},{3,7},... | collective-permute-start | bytes 884744 | tf_op jit(solution)/shard_map/ppermute | solution.py:458
  134.6 9.9 %copy-start.9 = (bf16[1,144,1024]{2,1,0:T(8,128)(2,1)S(1)}, bf16[1,144,1024]{2,1,0:T(8,128)(2,1)}, u32[]{:S(2)}) copy-start(bf16[1,144,1024]{2,1,0:T(8,128)(2,1)} %get-tuple-element.97) | copy-start | bytes 884740
  134.6 9.9 %copy-start.10 = (bf16[1,144,1024]{2,1,0:T(8,128)(2,1)S(1)}, bf16[1,144,1024]{2,1,0:T(8,128)(2,1)}, u32[]{:S(2)}) copy-start(bf16[1,144,1024]{2,1,0:T(8,128)(2,1)} %get-tuple-element.122) | copy-start | bytes 884740
  134.6 9.8 %collective-permute-start.31 = (bf16[1,144,1024]{2,1,0:T(8,128)(2,1)}, bf16[1,144,1024]{2,1,0:T(8,128)(2,1)S(1)}, u32[]{:S(2)}, u32[]{:S(2)}) collective-permute-start(bf16[1,144,1024]{2,1,0:T(8,128)(2,1)} %add_convert_fusion.4), channel_id=1, source_target_pairs={{0,2},{2,0},{4,6},{6,4},{8,10},{10,8},{12,14},{14,12},{1,3},{3,1},... | collective-permute-start | bytes 884744 | tf_op jit(solution)/shard_map/ppermute | solution.py:455
  144.5 18.0 %copy-start.11 = (bf16[1,144,1024]{2,1,0:T(8,128)(2,1)S(1)}, bf16[1,144,1024]{2,1,0:T(8,128)(2,1)}, u32[]{:S(2)}) copy-start(bf16[1,144,1024]{2,1,0:T(8,128)(2,1)} %get-tuple-element.75) | copy-start | bytes 884740
  146.1 11.3 %collective-permute-start.33 = (bf16[1,144,1024]{2,1,0:T(8,128)(2,1)S(1)}, bf16[1,144,1024]{2,1,0:T(8,128)(2,1)S(1)}, u32[]{:S(2)}, u32[]{:S(2)}) collective-permute-start(bf16[1,144,1024]{2,1,0:T(8,128)(2,1)S(1)} %get-tuple-element.127), channel_id=1, source_target_pairs={{0,12},{2,14},{4,0},{6,2},{8,4},{10,6},{12,8},{14,10},{1,13},{3,15... | collective-permute-start | bytes 884744 | tf_op jit(solution)/shard_map/ppermute | solution.py:458
  150.0 12.4 %collective-permute-start.34 = (bf16[1,144,1024]{2,1,0:T(8,128)(2,1)S(1)}, bf16[1,144,1024]{2,1,0:T(8,128)(2,1)S(1)}, u32[]{:S(2)}, u32[]{:S(2)}) collective-permute-start(bf16[1,144,1024]{2,1,0:T(8,128)(2,1)S(1)} %get-tuple-element.128), channel_id=1, source_target_pairs={{0,4},{2,6},{4,8},{6,10},{8,12},{10,14},{12,0},{14,2},{1,5},{3,7},... | collective-permute-start | bytes 884744 | tf_op jit(solution)/shard_map/ppermute | solution.py:458
  150.1 12.4 %collective-permute-start.35 = (bf16[1,144,1024]{2,1,0:T(8,128)(2,1)S(1)}, bf16[1,144,1024]{2,1,0:T(8,128)(2,1)S(1)}, u32[]{:S(2)}, u32[]{:S(2)}) collective-permute-start(bf16[1,144,1024]{2,1,0:T(8,128)(2,1)S(1)} %add_convert_fusion), channel_id=1, source_target_pairs={{0,1},{1,0},{2,3},{3,2},{4,5},{5,4},{6,7},{7,6},{8,9},{9,8},{10,11... | collective-permute-start | bytes 884744 | tf_op jit(solution)/shard_map/ppermute | solution.py:449
  (14 other events, 41.3 us)

commit v10 on v9

--- a/solution.py
+++ b/solution.py
@@ -166,7 +166,6 @@
 def rows_kernel(count, ways, capacity, slots, where_ref, *refs):
     weights_in, units_in, tables_in = refs[:4], refs[4 : 4 + 4 * count], refs[4 + 4 * count : 4 + 5 * count]
     leaves = 1 + max(way[0] for way in ways.values())
-    carried_in = refs[4 + 5 * count : 4 + 5 * count + sum(len(block) == 1 for block in ways)]
     refs = refs[len(refs) - 18 - leaves :]
     outs, packets, refs = refs[:2], refs[2 : 2 + leaves], refs[2 + leaves :]
     x_all, g_all, tables, wgu0, wgu1, wd0, wd1, xc, gc, both, scaled, dense, piece, unit_sems, weight_sems = refs[:15]
@@ -197,10 +196,6 @@
         copy = pltpu.make_async_copy(source, target, out_sems.at[len(leaving)])
         copy.start()
         leaving.append(copy)
-
-    for index, block in enumerate(carried_in):
-        number, slot = ways[(index,)]
-        leave(block.at[0], packets[number].at[slot])
 
     def leave_rows(held, start):
         for expert in range(2):
@@ -304,7 +299,7 @@
         copy.wait()
 
 
-def rows_call(items, owners, capacity, slots, where, weights, units, tables, carried, after):
+def rows_call(items, owners, capacity, slots, where, weights, units, tables, after):
     count = len(tables)
     ways = {block: (number, slot) for number, blocks in enumerate(items) for slot, block in enumerate(blocks)}
     tok, half = units[0].shape[0] // 2, units[0].shape[1]
@@ -316,7 +311,7 @@
         grid_spec=pltpu.PrefetchScalarGridSpec(
             num_scalar_prefetch=1,
             grid=(1,),
-            in_specs=[LOOSE] * (4 + 5 * count + len(carried) + len(after)),
+            in_specs=[LOOSE] * (4 + 5 * count + len(after)),
             out_specs=[LOOSE] * (2 + len(items)),
             scratch_shapes=[pltpu.VMEM((count, 2, 2 * tok, half), jnp.bfloat16)] * 2
             + [pltpu.VMEM((count, 2, owners, tok), jnp.bfloat16)]
@@ -328,7 +323,7 @@
                 pltpu.VMEM((count, 2, 2) + packet, jnp.bfloat16),
                 pltpu.SemaphoreType.DMA((3, 4 * count)),
                 pltpu.SemaphoreType.DMA((4,)),
-                pltpu.SemaphoreType.DMA((8 + 4 * count + len(carried),)),
+                pltpu.SemaphoreType.DMA((8 + 4 * count,)),
             ],
         ),
         out_shape=[jax.ShapeDtypeStruct((count * slots, sum(widths)), jnp.bfloat16)] * 2
@@ -340,7 +335,7 @@
             transcendentals=2 * count * slots * part,
         ),
         name="rows",
-    )(where, *weights, *units, *tables, *carried, *after)
+    )(where, *weights, *units, *tables, *after)
 
 
 def grads_kernel(count, wide, deep, blocks, tp_ref, *refs):
@@ -427,7 +422,7 @@
             ],
         ),
         out_shape=[jax.ShapeDtypeStruct(shape, jnp.bfloat16) for shape in shapes],
-        compiler_params=pltpu.CompilerParams(vmem_limit_bytes=62 << 20),
+        compiler_params=pltpu.CompilerParams(vmem_limit_bytes=24 << 20),
         cost_estimate=pl.CostEstimate(
             flops=2 * rows * width * deep, bytes_accessed=2 * rows * (width + deep), transcendentals=0
         ),
@@ -483,8 +478,8 @@
             axis = item[2] if item[2] in (over_x, over_y) else over_z
             if item[1] in there and axis not in moves:
                 moves[axis] = item
-        rounds.append(list(moves.values()))
-        there |= {item[0] for item in rounds[-1]}
+        rounds.append(moves)
+        there |= {item[0] for item in moves.values()}
         waiting = [item for item in waiting if item[0] not in there]
 
     which_ref = which.reshape(1).astype(jnp.int32)
@@ -492,14 +487,14 @@
     both_w, down_w = weights_call(which_ref, w_gate, w_up, w_down)
     width, part = both_w.shape[0], down_w.shape[0]
 
-    def rows_of(steps, items, carried=(), after=()):
+    def rows_of(steps, items, after=()):
         four = [units[z, y, x] for z in steps for y in range(2) for x in range(2)]
-        return rows_call(items, owners, capacity, slots, where, weights, four, [tables[z] for z in steps], carried, after)
+        return rows_call(items, owners, capacity, slots, where, weights, four, [tables[z] for z in steps], after)
 
     units = {(0, 0, 0): jnp.concatenate([tokens, out_grad], 0)}
     settled = dict(units)
     for number, moves in enumerate(rounds):
-        arrived = {target: move(settled[source]) for target, source, move in moves}
+        arrived = {target: move(settled[source]) for target, source, move in moves.values()}
         units.update(arrived)
         settled.update(arrived)
         extra = []
@@ -522,35 +517,38 @@
         if number == 3:
             (other_0,) = tied([other_0], [settled[0, 0, 0]])
             other_0 = over_role(other_0)
-            extra = [other_0] + tables[1:]
+            extra = [other_0]
         names = list(settled)
         settled = dict(zip(names, tied([settled[item] for item in names], extra)))
 
     def total(*blocks):
         return sum(block.astype(jnp.float32) for block in blocks).astype(jnp.bfloat16)
 
-    items = [[(1, 1, 1), (1, 0, 1)], [(0, 1, 0), (0,)], [(0, 1, 1)], [(0, 0, 1)], [(0, 0, 0)], [(1, 0, 0)], [(1, 1, 0)]]
-    mine_1, other_1, x_2, y_1, z_1, x_1, keep_1, keep_2, keep_2y = rows_of([1, 2], items, [y_0])
-    other_1, x_2, y_1, z_1 = tied([other_1, x_2, y_1, z_1], arrived.values())
+    items = [[(1, 1, 1)], [(1, 0, 1)], [(0, 1, 0)], [(0, 1, 1)], [(0, 0, 1)], [(0, 0, 0)], [(1, 0, 0)], [(1, 1, 0)]]
+    mine_1, other_1, x_2, x_20, y_1, z_1, x_1, keep_1, keep_2, keep_2y = rows_of([1, 2], items)
+    x_2, y_1, z_1 = tied([x_2, y_1, z_1], arrived.values())
     from_x2, from_y1, from_z1 = over_x(x_2), over_y(y_1), over_z(z_1, -1)
-    items = [[(0, 0, 1), (0,)], [(0, 1, 0)], [(0, 1, 1)], [(0, 0, 0)]]
-    mine_3, other_3, x_3, y_3, z_3, keep_3 = rows_of([3], items, [x_1], [mine_1])
-    mine_3, other_3, x_3, y_3, z_3, keep_2y = tied(
-        [mine_3, other_3, x_3, y_3, z_3, keep_2y], [from_x2, from_y1, from_z1]
-    )
-    from_z3, from_y2 = over_z(z_3, 1), over_y(total(keep_2y, from_x2[:1]))
-    from_x3, from_y3 = over_x(x_3), over_y(y_3)
+    items = [[(0, 0, 1)], [(0, 1, 0)], [(0, 1, 1)], [(0, 0, 0)]]
+    mine_3, other_3, x_3, y_3, z_3, keep_3 = rows_of([3], items, [mine_1])
+    mine_3, other_3, other_1, z_3, x_3, y_3, x_1, x_20, keep_2y = tied(
+        [mine_3, other_3, other_1, z_3, x_3, y_3, x_1, x_20, keep_2y], [from_x2, from_y1, from_z1]
+    )
+    from_z3, from_y2, from_x20 = over_z(z_3, 1), over_y(total(keep_2y, from_x2)), over_x(x_20)
+    from_x1, from_x3, from_y3 = over_x(x_1), over_x(x_3), over_y(y_3)
+    from_far = over_y(total(far, from_z1, from_z3))
+    from_z2 = over_z(total(keep_2, from_x20, from_y2), 1)
     packed = [mine_0, other_0, mine_1, over_role(other_1), mine_3, over_role(other_3)]
+    d_gate, d_up = grads_call(which_ref, packed, width, part, False)
+    from_x1, from_x3, from_y3, from_far, from_z2, y_0 = tied(
+        [from_x1, from_x3, from_y3, from_far, from_z2, y_0], [d_gate, d_up]
+    )
+    from_y0 = over_y(y_0)
+    home_1 = over_z(total(keep_1, from_x1, from_y1), -1)
+    home_3 = over_z(total(keep_3, from_x3, from_y3, from_z2), 1)
+    from_x0 = over_x(total(side_0, from_far))
     (d_down,) = grads_call(which_ref, packed, width, part, True)
-    from_z3, from_y2 = tied([from_z3, from_y2], [d_down])
-    from_far = over_y(total(far, from_z1, from_z3))
-    from_z2 = over_z(total(keep_2, from_x2[1:], from_y2), 1)
-    d_gate, d_up = grads_call(which_ref, packed, width, part, False)
-    from_x3, from_y3, from_far, from_z2 = tied([from_x3, from_y3, from_far, from_z2], [d_gate, d_up])
-    home_1 = over_z(total(keep_1, from_x3[1:], from_y1[:1]), -1)
-    home_3 = over_z(total(keep_3, from_x3[:1], from_y3, from_z2), 1)
-    from_x0 = over_x(total(side_0, from_far))
-    home = (near, from_y1[1:], home_1, home_3, from_x0)
+    home_1, home_3, from_x0, from_y0 = tied([home_1, home_3, from_x0, from_y0], [d_down])
+    home = (near, from_y0, home_1, home_3, from_x0)
     d_tok = sum(block[0, :tok_rows].astype(jnp.float32) for block in home).astype(jnp.bfloat16)
     home = sum(block[0, tok_rows:, : 4 * tok_rows].astype(jnp.float32) for block in home)
     score = jnp.sum(home.reshape(owners, 4, tok_rows), axis=1).T

time: 164 us -> 151 us (0.921)
  waiting for transfers between devices: 59.3 us -> 44.6 us
  starting transfers between devices: 33.6 us -> 39.8 us
  Pallas kernels: 54.8 us -> 49.1 us
  local copies, waits for them, and re-layouts: 5.1 us -> 8.48 us
  other arithmetic: 10.2 us -> 7.54 us
    ppermute x13, waiting for transfers between devices: 54.5 us -> 30.4 us  [over_z(): lax.ppermute(array, 'ep', [(i, (i + shift * n_y) % ep) for i in range(ep)])]
    ppermute x8 -> x10, waiting for transfers between devices: 1.02 us -> 12.6 us  [over_x(): return lax.ppermute(array, 'tp', [(0, 1), (1, 0)])]
    pallas_call x2, Pallas kernels: 15.8 us -> 11.1 us  [grads_call(): pl.pallas_call(functools.partial(grads_kernel, count, *starts, 2 * per),...]
    unnamed x53 -> x59, local copies, waits for them, and re-layouts: 4.11 us -> 7.5 us
    convert_element_type x5 -> x6, other arithmetic: 7.42 us -> 4.75 us  [total(): sum((block.astype(jnp.float32) for block in blocks)).astype(jnp.bfloat16)]
    ppermute x8 -> x10, starting transfers between devices: 8.5 us -> 10.8 us  [over_x(): return lax.ppermute(array, 'tp', [(0, 1), (1, 0)])]
    ppermute x10 -> x11, waiting for transfers between devices: 3.77 us -> 1.53 us  [over_y(): lax.ppermute(array, 'ep', [(i, i + 1 - 2 * (i % n_y)) for i in range(ep)])]
    ppermute x10 -> x11, starting transfers between devices: 11.2 us -> 13.4 us  [over_y(): lax.ppermute(array, 'ep', [(i, i + 1 - 2 * (i % n_y)) for i in range(ep)])]
  transfers between devices with their start and end apart: 36 -> 39, of which waited for: 12 -> 10; matrix products, arithmetic and copies ran while one was open for 4% -> 3% of each run, Pallas kernels for 33% -> 33%
where the time goes in v10:
time: 151 us
  Pallas kernels  49.1 us (33%)
  waiting for transfers between devices  44.6 us (30%)
  starting transfers between devices  39.8 us (26%)
  local copies, waits for them, and re-layouts  8.48 us (6%)
  other arithmetic  7.54 us (5%)
    pallas_call x3, Pallas kernels, rows_call(): pl.pallas_call(functools.partial(rows_kernel, count, ways, capacity, slot...  33.9 us
    ppermute x13, waiting for transfers between devices, over_z(): lax.ppermute(array, 'ep', [(i, (i + shift * n_y) % ep) for i in range(ep)])  30.4 us
    ppermute x13, starting transfers between devices, over_z(): lax.ppermute(array, 'ep', [(i, (i + shift * n_y) % ep) for i in range(ep)])  14.5 us
    ppermute x11, starting transfers between devices, over_y(): lax.ppermute(array, 'ep', [(i, i + 1 - 2 * (i % n_y)) for i in range(ep)])  13.4 us
    ppermute x10, waiting for transfers between devices, over_x(): return lax.ppermute(array, 'tp', [(0, 1), (1, 0)])  12.6 us
    pallas_call x2, Pallas kernels, grads_call(): pl.pallas_call(functools.partial(grads_kernel, count, *starts, 2 * per),...  11.1 us
    ppermute x10, starting transfers between devices, over_x(): return lax.ppermute(array, 'tp', [(0, 1), (1, 0)])  10.8 us
    unnamed x59, local copies, waits for them, and re-layouts  7.5 us
  transfers between devices with their start and end apart: 39, of which 10 were waited for; matrix products, arithmetic and copies ran while one was open for 3% of the time, Pallas kernels for 33%

profile of v10, /device:TPU:0, one launch (start us, length us, event | category | flops | bytes accessed | tf_op | source)
XLA Modules:
  0.0 150.5 jit_solution(6157040332988529302)
XLA Ops:
  0.6 1.0 constant_dynamic-update-slice_fusion.1
  1.6 1.0 constant_dynamic-update-slice_fusion.refs_4_
  2.6 3.1 %collective-permute-start = (bf16[256,1024]{1,0:T(8,128)(2,1)S(1)}, bf16[256,1024]{1,0:T(8,128)(2,1)S(1)}, u32[]{:S(2)}, u32[]{:S(2)}) collective-permute-start(bf16[256,1024]{1,0:T(8,128)(2,1)S(1)} %constant_dynamic-update-slice_fusion.refs_4_), channel_id=1, source_target_pairs={{0,4},{2,6},{4,8},{6,10},{8,12},{10,14},{12,0},{14,2},{1,5},{3,7},... | collective-permute-start | bytes 1572872 | tf_op jit(solution)/shard_map/ppermute | solution.py:453
  5.7 1.5 %collective-permute-start.1 = (bf16[256,1024]{1,0:T(8,128)(2,1)S(1)}, bf16[256,1024]{1,0:T(8,128)(2,1)S(1)}, u32[]{:S(2)}, u32[]{:S(2)}) collective-permute-start(bf16[256,1024]{1,0:T(8,128)(2,1)S(1)} %constant_dynamic-update-slice_fusion.refs_4_), channel_id=1, source_target_pairs={{0,2},{2,0},{4,6},{6,4},{8,10},{10,8},{12,14},{14,12},{1,3},{3,1},... | collective-permute-start | bytes 1572872 | tf_op jit(solution)/shard_map/ppermute | solution.py:450
  7.2 1.5 collective-permute-start.2
  8.7 4.0 %weights.1 = (bf16[2048,768]{1,0:T(8,128)(2,1)}, bf16[384,2048]{1,0:T(8,128)(2,1)}) custom-call(s32[1]{0:T(128)} %bitcast.2.tp_ref, bf16[1,2048,384]{2,1,0:T(8,128)(2,1)} %wg_ref.1, bf16[1,2048,384]{2,1,0:T(8,128)(2,1)} %wu_ref.1, bf16[1,384,2048]{2,1,0:T(8,128)(2,1)} %wd_ref.1), custom_call_target="tpu_custom_call" | custom-call | bytes 9437184 | tf_op jit(solution)/shard_map/weights/pallas_call | solution.py:141
  12.7 6.9 %collective-permute-done.refs_4_ = bf16[256,1024]{1,0:T(8,128)(2,1)S(1)} collective-permute-done((bf16[256,1024]{1,0:T(8,128)(2,1)S(1)}, bf16[256,1024]{1,0:T(8,128)(2,1)S(1)}, u32[]{:S(2)}, u32[]{:S(2)}) %collective-permute-start) | collective-permute-done | bytes 524320 | tf_op jit(solution)/shard_map/ppermute | solution.py:453
  19.6 0.8 collective-permute-done.2.refs_5_
  21.1 1.4 collective-permute-start.7
  22.5 1.0 collective-permute-start.8
  23.5 1.5 collective-permute-start.5
  25.0 12.0 %collective-permute-done.7.refs_8_ = bf16[256,1024]{1,0:T(8,128)(2,1)} collective-permute-done((bf16[256,1024]{1,0:T(8,128)(2,1)}, bf16[256,1024]{1,0:T(8,128)(2,1)}, u32[]{:S(2)}, u32[]{:S(2)}) %collective-permute-start.7) | collective-permute-done | bytes 524320 | tf_op jit(solution)/shard_map/ppermute | solution.py:453
  37.1 1.5 %collective-permute-start.6 = (bf16[16,128]{1,0:T(8,128)(2,1)S(1)}, bf16[16,128]{1,0:T(8,128)(2,1)S(1)}, u32[]{:S(2)}, u32[]{:S(2)}) collective-permute-start(bf16[16,128]{1,0:T(8,128)(2,1)S(1)} %get-tuple-element.142), channel_id=1, source_target_pairs={{0,2},{2,0},{4,6},{6,4},{8,10},{10,8},{12,14},{14,12},{1,3},{3,1},... | collective-permute-start | bytes 12296 | tf_op jit(solution)/shard_map/ppermute | solution.py:450
  38.6 1.4 collective-permute-start.9
  40.7 1.5 collective-permute-start.11
  43.4 1.1 copy-done.5
  44.5 10.0 %rows.3 = (bf16[144,5248]{1,0:T(8,128)(2,1)}, bf16[144,5248]{1,0:T(8,128)(2,1)}, bf16[1,144,1024]{2,1,0:T(8,128)(2,1)}, bf16[1,144,1024]{2,1,0:T(8,128)(2,1)}, b...) custom-call(s32[3]{0:T(128)} %pad_add_fusion.where_ref, bf16[2048,768]{1,0:T(8,128)(2,1)} %get-tuple-element.75.refs_0_, ...), custom_call_target="tpu_custom_call" | custom-call | flops 3170893824 | bytes 13631488 | tf_op jit(solution)/shard_map/rows/pallas_call | solution.py:309
  55.9 1.5 %collective-permute-start.14 = (bf16[256,1024]{1,0:T(8,128)(2,1)}, bf16[256,1024]{1,0:T(8,128)(2,1)S(1)}, u32[]{:S(2)}, u32[]{:S(2)}) collective-permute-start(bf16[256,1024]{1,0:T(8,128)(2,1)} %collective-permute-done.11.refs_9_), channel_id=1, source_target_pairs={{0,2},{2,0},{4,6},{6,4},{8,10},{10,8},{12,14},{14,12},{1,3},{3,1},... | collective-permute-start | bytes 1572872 | tf_op jit(solution)/shard_map/ppermute | solution.py:450
  57.4 11.8 %collective-permute-done.12.refs_5_ = bf16[256,1024]{1,0:T(8,128)(2,1)S(1)} collective-permute-done((bf16[256,1024]{1,0:T(8,128)(2,1)}, bf16[256,1024]{1,0:T(8,128)(2,1)S(1)}, u32[]{:S(2)}, u32[]{:S(2)}) %collective-permute-start.12) | collective-permute-done | bytes 524320 | tf_op jit(solution)/shard_map/ppermute | solution.py:444
  69.9 1.4 collective-permute-done.13.refs_7_
  71.4 0.8 collective-permute-start.21
  72.2 1.1 copy-done.2
  73.3 1.5 %collective-permute-start.19 = (bf16[256,1024]{1,0:T(8,128)(2,1)}, bf16[256,1024]{1,0:T(8,128)(2,1)S(1)}, u32[]{:S(2)}, u32[]{:S(2)}) collective-permute-start(bf16[256,1024]{1,0:T(8,128)(2,1)} %collective-permute-done.9.refs_4_), channel_id=1, source_target_pairs={{0,2},{2,0},{4,6},{6,4},{8,10},{10,8},{12,14},{14,12},{1,3},{3,1},... | collective-permute-start | bytes 1572872 | tf_op jit(solution)/shard_map/ppermute | solution.py:450
  75.6 1.9 %collective-permute-start.20 = (bf16[256,1024]{1,0:T(8,128)(2,1)}, bf16[256,1024]{1,0:T(8,128)(2,1)S(1)}, u32[]{:S(2)}, u32[]{:S(2)}) collective-permute-start(bf16[256,1024]{1,0:T(8,128)(2,1)} %copy-done.20), channel_id=1, source_target_pairs={{0,12},{2,14},{4,0},{6,2},{8,4},{10,6},{12,8},{14,10},{1,13},{3,15... | collective-permute-start | bytes 1572872 | tf_op jit(solution)/shard_map/ppermute | solution.py:453
  78.0 13.7 %rows.4 = (bf16[288,5248]{1,0:T(8,128)(2,1)}, bf16[288,5248]{1,0:T(8,128)(2,1)}, bf16[1,144,1024]{2,1,0:T(8,128)(2,1)}, bf16[1,144,1024]{2,1,0:T(8,128)(2,1)}, b...) custom-call(s32[3]{0:T(128)} %pad_add_fusion.where_ref, ...), custom_call_target="tpu_custom_call" | custom-call | flops 6341787648 | bytes 17825792 | tf_op jit(solution)/shard_map/rows/pallas_call | solution.py:309
  92.4 1.1 collective-permute-start.22
  94.5 10.2 %rows.5 = (bf16[144,5248]{1,0:T(8,128)(2,1)}, bf16[144,5248]{1,0:T(8,128)(2,1)}, bf16[1,144,1024]{2,1,0:T(8,128)(2,1)}, bf16[1,144,1024]{2,1,0:T(8,128)(2,1)}, b...) custom-call(s32[3]{0:T(128)} %pad_add_fusion.where_ref, bf16[2048,768]{1,0:T(8,128)(2,1)} %get-tuple-element.75.refs_0_, ...), custom_call_target="tpu_custom_call" | custom-call | flops 3170893824 | bytes 13631488 | tf_op jit(solution)/shard_map/rows/pallas_call | solution.py:309
  105.3 1.7 %collective-permute-start.28 = (bf16[1,144,1024]{2,1,0:T(8,128)(2,1)}, bf16[1,144,1024]{2,1,0:T(8,128)(2,1)S(1)}, u32[]{:S(2)}, u32[]{:S(2)}) collective-permute-start(bf16[1,144,1024]{2,1,0:T(8,128)(2,1)} %get-tuple-element.119), channel_id=1, source_target_pairs={{0,4},{2,6},{4,8},{6,10},{8,12},{10,14},{12,0},{14,2},{1,5},{3,7},... | collective-permute-start | bytes 884744 | tf_op jit(solution)/shard_map/ppermute | solution.py:453
  107.0 1.0 add_convert_fusion.4
  108.1 1.6 %collective-permute-start.31 = (bf16[1,144,1024]{2,1,0:T(8,128)(2,1)S(1)}, bf16[1,144,1024]{2,1,0:T(8,128)(2,1)S(1)}, u32[]{:S(2)}, u32[]{:S(2)}) collective-permute-start(bf16[1,144,1024]{2,1,0:T(8,128)(2,1)S(1)} %add_convert_fusion.4), channel_id=1, source_target_pairs={{0,2},{2,0},{4,6},{6,4},{8,10},{10,8},{12,14},{14,12},{1,3},{3,1},... | collective-permute-start | bytes 884744 | tf_op jit(solution)/shard_map/ppermute | solution.py:450
  109.6 0.9 collective-permute-start.30
  110.5 5.8 %collective-permute-done.28 = bf16[1,144,1024]{2,1,0:T(8,128)(2,1)S(1)} collective-permute-done((bf16[1,144,1024]{2,1,0:T(8,128)(2,1)}, bf16[1,144,1024]{2,1,0:T(8,128)(2,1)S(1)}, u32[]{:S(2)}, u32[]{:S(2)}) %collective-permute-start.28) | collective-permute-done | bytes 294944 | tf_op jit(solution)/shard_map/ppermute | solution.py:453
  116.3 0.9 collective-permute-start.25
  117.2 1.2 add_convert_fusion.5
  118.4 1.2 collective-permute-start.26
  119.6 1.5 %collective-permute-start.27 = (bf16[1,144,1024]{2,1,0:T(8,128)(2,1)}, bf16[1,144,1024]{2,1,0:T(8,128)(2,1)S(1)}, u32[]{:S(2)}, u32[]{:S(2)}) collective-permute-start(bf16[1,144,1024]{2,1,0:T(8,128)(2,1)} %get-tuple-element.117), channel_id=1, source_target_pairs={{0,2},{2,0},{4,6},{6,4},{8,10},{10,8},{12,14},{14,12},{1,3},{3,1},... | collective-permute-start | bytes 884744 | tf_op jit(solution)/shard_map/ppermute | solution.py:450
  121.2 1.1 add_convert_fusion.3
  122.9 1.4 copy-done.3
  124.3 1.4 copy-done.4
  125.6 6.7 %grads.2 = (bf16[1,2048,384]{2,1,0:T(8,128)(2,1)}, bf16[1,2048,384]{2,1,0:T(8,128)(2,1)}) custom-call(s32[1]{0:T(128)} %bitcast.2.tp_ref, bf16[144,5248]{1,0:T(8,128)(2,1)S(1)} %copy-done.1, bf16[144,5248]{1,0:T(8,128)(2,1)S(1)} %copy-done.3, bf16[288,5248]{1,0:T(8,128)(2,1)S(1)} %copy-done, bf16[288,5248]{1,0:T(8,128)(2,1)S(1)} %collective-permute-done.33.refs_3_, ...), custom_call_target="tpu_custom_call" | custom-call | flops 3623878656 | bytes 6488064 | tf_op jit(solution)/shard_map/grads/pallas_call | solution.py:410
  132.4 1.3 collective-permute-done.29
  133.8 1.1 add_convert_fusion.2
  134.9 2.6 %collective-permute-start.35 = (bf16[1,144,1024]{2,1,0:T(8,128)(2,1)S(1)}, bf16[1,144,1024]{2,1,0:T(8,128)(2,1)S(1)}, u32[]{:S(2)}, u32[]{:S(2)}) collective-permute-start(bf16[1,144,1024]{2,1,0:T(8,128)(2,1)S(1)} %add_convert_fusion.2), channel_id=1, source_target_pairs={{0,12},{2,14},{4,0},{6,2},{8,4},{10,6},{12,8},{14,10},{1,13},{3,15... | collective-permute-start | bytes 884744 | tf_op jit(solution)/shard_map/ppermute | solution.py:453
  137.9 0.9 collective-permute-start.37
  138.8 1.5 %collective-permute-start.38 = (bf16[1,144,1024]{2,1,0:T(8,128)(2,1)S(1)}, bf16[1,144,1024]{2,1,0:T(8,128)(2,1)S(1)}, u32[]{:S(2)}, u32[]{:S(2)}) collective-permute-start(bf16[1,144,1024]{2,1,0:T(8,128)(2,1)S(1)} %copy-done.26), channel_id=1, source_target_pairs={{0,2},{2,0},{4,6},{6,4},{8,10},{10,8},{12,14},{14,12},{1,3},{3,1},... | collective-permute-start | bytes 884744 | tf_op jit(solution)/shard_map/ppermute | solution.py:450
  140.3 4.4 %grads.3 = bf16[1,384,2048]{2,1,0:T(8,128)(2,1)} custom-call(s32[1]{0:T(128)} %bitcast.2.tp_ref, bf16[144,5248]{1,0:T(8,128)(2,1)S(1)} %copy-done.1, bf16[144,5248]{1,0:T(8,128)(2,1)S(1)} %copy-done.3, bf16[288,5248]{1,0:T(8,128)(2,1)S(1)} %copy-done, bf16[288,5248]{1,0:T(8,128)(2,1)S(1)} %collective-permute-done.33.refs_3_, ...), custom_call_target="tpu_custom_call" | custom-call | flops 1811939328 | bytes 5603328 | tf_op jit(solution)/shard_map/grads/pallas_call | solution.py:410
  144.9 4.0 %collective-permute-done.36 = bf16[1,144,1024]{2,1,0:T(8,128)(2,1)S(1)} collective-permute-done((bf16[1,144,1024]{2,1,0:T(8,128)(2,1)S(1)}, bf16[1,144,1024]{2,1,0:T(8,128)(2,1)S(1)}, u32[]{:S(2)}, u32[]{:S(2)}) %collective-permute-start.36) | collective-permute-done | bytes 294944 | tf_op jit(solution)/shard_map/ppermute | solution.py:453
  148.9 0.9 fusion
  (112 shorter events, 9.9 us)
Async XLA Ops:
  2.6 10.1 %copy-start.14 = (bf16[256,1024]{1,0:T(8,128)(2,1)}, bf16[256,1024]{1,0:T(8,128)(2,1)S(1)}, u32[]{:S(2)}) copy-start(bf16[256,1024]{1,0:T(8,128)(2,1)S(1)} %constant_dynamic-update-slice_fusion.refs_4_) | copy-start | bytes 1572868
  2.6 17.0 %collective-permute-start = (bf16[256,1024]{1,0:T(8,128)(2,1)S(1)}, bf16[256,1024]{1,0:T(8,128)(2,1)S(1)}, u32[]{:S(2)}, u32[]{:S(2)}) collective-permute-start(bf16[256,1024]{1,0:T(8,128)(2,1)S(1)} %constant_dynamic-update-slice_fusion.refs_4_), channel_id=1, source_target_pairs={{0,4},{2,6},{4,8},{6,10},{8,12},{10,14},{12,0},{14,2},{1,5},{3,7},... | collective-permute-start | bytes 1572872 | tf_op jit(solution)/shard_map/ppermute | solution.py:453
  5.7 14.0 %collective-permute-start.1 = (bf16[256,1024]{1,0:T(8,128)(2,1)S(1)}, bf16[256,1024]{1,0:T(8,128)(2,1)S(1)}, u32[]{:S(2)}, u32[]{:S(2)}) collective-permute-start(bf16[256,1024]{1,0:T(8,128)(2,1)S(1)} %constant_dynamic-update-slice_fusion.refs_4_), channel_id=1, source_target_pairs={{0,2},{2,0},{4,6},{6,4},{8,10},{10,8},{12,14},{14,12},{1,3},{3,1},... | collective-permute-start | bytes 1572872 | tf_op jit(solution)/shard_map/ppermute | solution.py:450
  7.2 13.2 %collective-permute-start.2 = (bf16[256,1024]{1,0:T(8,128)(2,1)S(1)}, bf16[256,1024]{1,0:T(8,128)(2,1)}, u32[]{:S(2)}, u32[]{:S(2)}) collective-permute-start(bf16[256,1024]{1,0:T(8,128)(2,1)S(1)} %constant_dynamic-update-slice_fusion.refs_4_), channel_id=1, source_target_pairs={{0,1},{1,0},{2,3},{3,2},{4,5},{5,4},{6,7},{7,6},{8,9},{9,8},{10,11... | collective-permute-start | bytes 1572872 | tf_op jit(solution)/shard_map/ppermute | solution.py:444
  8.7 16.3 %copy-start.18 = (bf16[128,8]{0,1:T(8,128)(2,1)S(1)}, bf16[128,8]{0,1:T(8,128)(2,1)}, u32[]{:S(2)}) copy-start(bf16[128,8]{0,1:T(8,128)(2,1)} %param.10) | copy-start | bytes 6148
  8.7 16.3 %copy-start.15 = (s32[128,8]{0,1:T(8,128)S(1)}, s32[128,8]{0,1:T(8,128)}, u32[]{:S(2)}) copy-start(s32[128,8]{0,1:T(8,128)} %param.9) | copy-start | bytes 12292
  20.6 22.8 %collective-permute-start.3 = (bf16[2048,768]{1,0:T(8,128)(2,1)}, bf16[2048,768]{1,0:T(8,128)(2,1)}, u32[]{:S(2)}, u32[]{:S(2)}) collective-permute-start(bf16[2048,768]{1,0:T(8,128)(2,1)} %get-tuple-element.75.refs_0_), channel_id=1, source_target_pairs={{0,16},{16,0},{1,17},{17,1},{2,18},{18,2},{3,19},{19,3},{4,20},{20... | collective-permute-start | bytes 9437192 | tf_op jit(solution)/shard_map/ppermute | solution.py:447
  20.6 22.8 %collective-permute-start.4 = (bf16[384,2048]{1,0:T(8,128)(2,1)}, bf16[384,2048]{1,0:T(8,128)(2,1)S(1)}, u32[]{:S(2)}, u32[]{:S(2)}) collective-permute-start(bf16[384,2048]{1,0:T(8,128)(2,1)} %get-tuple-element.76.refs_2_), channel_id=1, source_target_pairs={{0,16},{16,0},{1,17},{17,1},{2,18},{18,2},{3,19},{19,3},{4,20},{20... | collective-permute-start | bytes 4718600 | tf_op jit(solution)/shard_map/ppermute | solution.py:447
  21.1 15.9 %collective-permute-start.7 = (bf16[256,1024]{1,0:T(8,128)(2,1)}, bf16[256,1024]{1,0:T(8,128)(2,1)}, u32[]{:S(2)}, u32[]{:S(2)}) collective-permute-start(bf16[256,1024]{1,0:T(8,128)(2,1)} %copy-done.19), channel_id=1, source_target_pairs={{0,4},{2,6},{4,8},{6,10},{8,12},{10,14},{12,0},{14,2},{1,5},{3,7},... | collective-permute-start | bytes 1572872 | tf_op jit(solution)/shard_map/ppermute | solution.py:453
  22.5 16.1 %collective-permute-start.8 = (bf16[256,1024]{1,0:T(8,128)(2,1)}, bf16[256,1024]{1,0:T(8,128)(2,1)S(1)}, u32[]{:S(2)}, u32[]{:S(2)}) collective-permute-start(bf16[256,1024]{1,0:T(8,128)(2,1)} %copy-done.19), channel_id=1, source_target_pairs={{0,2},{2,0},{4,6},{6,4},{8,10},{10,8},{12,14},{14,12},{1,3},{3,1},... | collective-permute-start | bytes 1572872 | tf_op jit(solution)/shard_map/ppermute | solution.py:450
  23.5 15.1 %collective-permute-start.5 = (bf16[256,1024]{1,0:T(8,128)(2,1)}, bf16[256,1024]{1,0:T(8,128)(2,1)S(1)}, u32[]{:S(2)}, u32[]{:S(2)}) collective-permute-start(bf16[256,1024]{1,0:T(8,128)(2,1)} %copy-done.22), channel_id=1, source_target_pairs={{0,1},{1,0},{2,3},{3,2},{4,5},{5,4},{6,7},{7,6},{8,9},{9,8},{10,11... | collective-permute-start | bytes 1572872 | tf_op jit(solution)/shard_map/ppermute | solution.py:444
  37.1 3.6 %collective-permute-start.6 = (bf16[16,128]{1,0:T(8,128)(2,1)S(1)}, bf16[16,128]{1,0:T(8,128)(2,1)S(1)}, u32[]{:S(2)}, u32[]{:S(2)}) collective-permute-start(bf16[16,128]{1,0:T(8,128)(2,1)S(1)} %get-tuple-element.142), channel_id=1, source_target_pairs={{0,2},{2,0},{4,6},{6,4},{8,10},{10,8},{12,14},{14,12},{1,3},{3,1},... | collective-permute-start | bytes 12296 | tf_op jit(solution)/shard_map/ppermute | solution.py:450
  38.6 16.0 %collective-permute-start.9 = (bf16[256,1024]{1,0:T(8,128)(2,1)}, bf16[256,1024]{1,0:T(8,128)(2,1)}, u32[]{:S(2)}, u32[]{:S(2)}) collective-permute-start(bf16[256,1024]{1,0:T(8,128)(2,1)} %copy-done.14), channel_id=1, source_target_pairs={{0,12},{2,14},{4,0},{6,2},{8,4},{10,6},{12,8},{14,10},{1,13},{3,15... | collective-permute-start | bytes 1572872 | tf_op jit(solution)/shard_map/ppermute | solution.py:453
  40.0 14.6 %collective-permute-start.10 = (bf16[256,1024]{1,0:T(8,128)(2,1)}, bf16[256,1024]{1,0:T(8,128)(2,1)}, u32[]{:S(2)}, u32[]{:S(2)}) collective-permute-start(bf16[256,1024]{1,0:T(8,128)(2,1)} %collective-permute-done.7.refs_8_), channel_id=1, source_target_pairs={{0,2},{2,0},{4,6},{6,4},{8,10},{10,8},{12,14},{14,12},{1,3},{3,1},... | collective-permute-start | bytes 1572872 | tf_op jit(solution)/shard_map/ppermute | solution.py:450
  40.7 13.9 %collective-permute-start.11 = (bf16[256,1024]{1,0:T(8,128)(2,1)}, bf16[256,1024]{1,0:T(8,128)(2,1)}, u32[]{:S(2)}, u32[]{:S(2)}) collective-permute-start(bf16[256,1024]{1,0:T(8,128)(2,1)} %collective-permute-done.7.refs_8_), channel_id=1, source_target_pairs={{0,1},{1,0},{2,3},{3,2},{4,5},{5,4},{6,7},{7,6},{8,9},{9,8},{10,11... | collective-permute-start | bytes 1572872 | tf_op jit(solution)/shard_map/ppermute | solution.py:444
  43.4 14.0 %copy-start.17 = (bf16[2,16,128]{2,1,0:T(8,128)(2,1)S(1)}, bf16[2,16,128]{2,1,0:T(8,128)(2,1)}, u32[]{:S(2)}) copy-start(bf16[2,16,128]{2,1,0:T(8,128)(2,1)} %pad_maximum_fusion.refs_8_) | copy-start | bytes 24580
  54.6 17.6 %collective-permute-start.17 = (bf16[144,5248]{1,0:T(8,128)(2,1)}, bf16[144,5248]{1,0:T(8,128)(2,1)S(1)}, u32[]{:S(2)}, u32[]{:S(2)}) collective-permute-start(bf16[144,5248]{1,0:T(8,128)(2,1)} %get-tuple-element.96), channel_id=1, source_target_pairs={{0,16},{16,0},{1,17},{17,1},{2,18},{18,2},{3,19},{19,3},{4,20},{20... | collective-permute-start | bytes 4534280 | tf_op jit(solution)/shard_map/ppermute | solution.py:447
  54.7 14.6 %collective-permute-start.12 = (bf16[256,1024]{1,0:T(8,128)(2,1)}, bf16[256,1024]{1,0:T(8,128)(2,1)S(1)}, u32[]{:S(2)}, u32[]{:S(2)}) collective-permute-start(bf16[256,1024]{1,0:T(8,128)(2,1)} %copy-done.19), channel_id=1, source_target_pairs={{0,1},{1,0},{2,3},{3,2},{4,5},{5,4},{6,7},{7,6},{8,9},{9,8},{10,11... | collective-permute-start | bytes 1572872 | tf_op jit(solution)/shard_map/ppermute | solution.py:444
  55.3 16.1 %collective-permute-start.13 = (bf16[256,1024]{1,0:T(8,128)(2,1)}, bf16[256,1024]{1,0:T(8,128)(2,1)S(1)}, u32[]{:S(2)}, u32[]{:S(2)}) collective-permute-start(bf16[256,1024]{1,0:T(8,128)(2,1)} %copy-done.20), channel_id=1, source_target_pairs={{0,4},{2,6},{4,8},{6,10},{8,12},{10,14},{12,0},{14,2},{1,5},{3,7},... | collective-permute-start | bytes 1572872 | tf_op jit(solution)/shard_map/ppermute | solution.py:453
  55.9 16.3 %collective-permute-start.14 = (bf16[256,1024]{1,0:T(8,128)(2,1)}, bf16[256,1024]{1,0:T(8,128)(2,1)S(1)}, u32[]{:S(2)}, u32[]{:S(2)}) collective-permute-start(bf16[256,1024]{1,0:T(8,128)(2,1)} %collective-permute-done.11.refs_9_), channel_id=1, source_target_pairs={{0,2},{2,0},{4,6},{6,4},{8,10},{10,8},{12,14},{14,12},{1,3},{3,1},... | collective-permute-start | bytes 1572872 | tf_op jit(solution)/shard_map/ppermute | solution.py:450
  57.4 18.2 %collective-permute-start.15 = (bf16[2,16,128]{2,1,0:T(8,128)(2,1)S(1)}, bf16[2,16,128]{2,1,0:T(8,128)(2,1)S(1)}, u32[]{:S(2)}, u32[]{:S(2)}) collective-permute-start(bf16[2,16,128]{2,1,0:T(8,128)(2,1)S(1)} %copy-done.17), channel_id=1, source_target_pairs={{0,4},{2,6},{4,8},{6,10},{8,12},{10,14},{12,0},{14,2},{1,5},{3,7},... | collective-permute-start | bytes 24584 | tf_op jit(solution)/shard_map/ppermute | solution.py:453
  69.2 8.2 %collective-permute-start.16 = (bf16[2,16,128]{2,1,0:T(8,128)(2,1)S(1)}, bf16[2,16,128]{2,1,0:T(8,128)(2,1)S(1)}, u32[]{:S(2)}, u32[]{:S(2)}) collective-permute-start(bf16[2,16,128]{2,1,0:T(8,128)(2,1)S(1)} %copy-done.17), channel_id=1, source_target_pairs={{0,8},{2,10},{4,12},{6,14},{8,0},{10,2},{12,4},{14,6},{1,9},{3,11}... | collective-permute-start | bytes 24584 | tf_op jit(solution)/shard_map/ppermute | solution.py:453
  71.4 22.5 %collective-permute-start.21 = (bf16[2,16,128]{2,1,0:T(8,128)(2,1)S(1)}, bf16[2,16,128]{2,1,0:T(8,128)(2,1)S(1)}, u32[]{:S(2)}, u32[]{:S(2)}) collective-permute-start(bf16[2,16,128]{2,1,0:T(8,128)(2,1)S(1)} %copy-done.17), channel_id=1, source_target_pairs={{0,12},{2,14},{4,0},{6,2},{8,4},{10,6},{12,8},{14,10},{1,13},{3,15... | collective-permute-start | bytes 24584 | tf_op jit(solution)/shard_map/ppermute | solution.py:453
  73.3 18.5 %collective-permute-start.19 = (bf16[256,1024]{1,0:T(8,128)(2,1)}, bf16[256,1024]{1,0:T(8,128)(2,1)S(1)}, u32[]{:S(2)}, u32[]{:S(2)}) collective-permute-start(bf16[256,1024]{1,0:T(8,128)(2,1)} %collective-permute-done.9.refs_4_), channel_id=1, source_target_pairs={{0,2},{2,0},{4,6},{6,4},{8,10},{10,8},{12,14},{14,12},{1,3},{3,1},... | collective-permute-start | bytes 1572872 | tf_op jit(solution)/shard_map/ppermute | solution.py:450
  74.9 17.0 %collective-permute-start.18 = (bf16[256,1024]{1,0:T(8,128)(2,1)}, bf16[256,1024]{1,0:T(8,128)(2,1)S(1)}, u32[]{:S(2)}, u32[]{:S(2)}) collective-permute-start(bf16[256,1024]{1,0:T(8,128)(2,1)} %collective-permute-done.9.refs_4_), channel_id=1, source_target_pairs={{0,1},{1,0},{2,3},{3,2},{4,5},{5,4},{6,7},{7,6},{8,9},{9,8},{10,11... | collective-permute-start | bytes 1572872 | tf_op jit(solution)/shard_map/ppermute | solution.py:444
  75.6 16.2 %collective-permute-start.20 = (bf16[256,1024]{1,0:T(8,128)(2,1)}, bf16[256,1024]{1,0:T(8,128)(2,1)S(1)}, u32[]{:S(2)}, u32[]{:S(2)}) collective-permute-start(bf16[256,1024]{1,0:T(8,128)(2,1)} %copy-done.20), channel_id=1, source_target_pairs={{0,12},{2,14},{4,0},{6,2},{8,4},{10,6},{12,8},{14,10},{1,13},{3,15... | collective-permute-start | bytes 1572872 | tf_op jit(solution)/shard_map/ppermute | solution.py:453
  91.8 12.9 %collective-permute-start.23 = (bf16[1,144,1024]{2,1,0:T(8,128)(2,1)}, bf16[1,144,1024]{2,1,0:T(8,128)(2,1)}, u32[]{:S(2)}, u32[]{:S(2)}) collective-permute-start(bf16[1,144,1024]{2,1,0:T(8,128)(2,1)} %get-tuple-element.113), channel_id=1, source_target_pairs={{0,2},{2,0},{4,6},{6,4},{8,10},{10,8},{12,14},{14,12},{1,3},{3,1},... | collective-permute-start | bytes 884744 | tf_op jit(solution)/shard_map/ppermute | solution.py:450
  92.4 12.3 %collective-permute-start.22 = (bf16[1,144,1024]{2,1,0:T(8,128)(2,1)}, bf16[1,144,1024]{2,1,0:T(8,128)(2,1)}, u32[]{:S(2)}, u32[]{:S(2)}) collective-permute-start(bf16[1,144,1024]{2,1,0:T(8,128)(2,1)} %get-tuple-element.112), channel_id=1, source_target_pairs={{0,1},{1,0},{2,3},{3,2},{4,5},{5,4},{6,7},{7,6},{8,9},{9,8},{10,11... | collective-permute-start | bytes 884744 | tf_op jit(solution)/shard_map/ppermute | solution.py:444
  93.5 11.2 %collective-permute-start.24 = (bf16[1,144,1024]{2,1,0:T(8,128)(2,1)}, bf16[1,144,1024]{2,1,0:T(8,128)(2,1)}, u32[]{:S(2)}, u32[]{:S(2)}) collective-permute-start(bf16[1,144,1024]{2,1,0:T(8,128)(2,1)} %get-tuple-element.114), channel_id=1, source_target_pairs={{0,12},{2,14},{4,0},{6,2},{8,4},{10,6},{12,8},{14,10},{1,13},{3,15... | collective-permute-start | bytes 884744 | tf_op jit(solution)/shard_map/ppermute | solution.py:453
  94.5 12.5 %copy-start.10 = (bf16[1,144,1024]{2,1,0:T(8,128)(2,1)S(1)}, bf16[1,144,1024]{2,1,0:T(8,128)(2,1)}, u32[]{:S(2)}) copy-start(bf16[1,144,1024]{2,1,0:T(8,128)(2,1)} %get-tuple-element.122) | copy-start | bytes 884740
  94.5 28.3 %copy-start.1 = (bf16[144,5248]{1,0:T(8,128)(2,1)S(1)}, bf16[144,5248]{1,0:T(8,128)(2,1)}, u32[]{:S(2)}) copy-start(bf16[144,5248]{1,0:T(8,128)(2,1)} %get-tuple-element.88.refs_0_) | copy-start | bytes 4534276
  104.8 18.1 %copy-start = (bf16[288,5248]{1,0:T(8,128)(2,1)S(1)}, bf16[288,5248]{1,0:T(8,128)(2,1)}, u32[]{:S(2)}) copy-start(bf16[288,5248]{1,0:T(8,128)(2,1)} %get-tuple-element.99.refs_9_.refs_2_) | copy-start | bytes 9068548
  104.8 18.1 %collective-permute-start.33 = (bf16[288,5248]{1,0:T(8,128)(2,1)}, bf16[288,5248]{1,0:T(8,128)(2,1)S(1)}, u32[]{:S(2)}, u32[]{:S(2)}) collective-permute-start(bf16[288,5248]{1,0:T(8,128)(2,1)} %get-tuple-element.124), channel_id=1, source_target_pairs={{0,16},{16,0},{1,17},{17,1},{2,18},{18,2},{3,19},{19,3},{4,20},{20... | collective-permute-start | bytes 9068552 | tf_op jit(solution)/shard_map/ppermute | solution.py:447
  104.8 17.4 %collective-permute-start.34 = (bf16[144,5248]{1,0:T(8,128)(2,1)}, bf16[144,5248]{1,0:T(8,128)(2,1)S(1)}, u32[]{:S(2)}, u32[]{:S(2)}) collective-permute-start(bf16[144,5248]{1,0:T(8,128)(2,1)} %get-tuple-element.126), channel_id=1, source_target_pairs={{0,16},{16,0},{1,17},{17,1},{2,18},{18,2},{3,19},{19,3},{4,20},{20... | collective-permute-start | bytes 4534280 | tf_op jit(solution)/shard_map/ppermute | solution.py:447
  105.3 11.0 %collective-permute-start.28 = (bf16[1,144,1024]{2,1,0:T(8,128)(2,1)}, bf16[1,144,1024]{2,1,0:T(8,128)(2,1)S(1)}, u32[]{:S(2)}, u32[]{:S(2)}) collective-permute-start(bf16[1,144,1024]{2,1,0:T(8,128)(2,1)} %get-tuple-element.119), channel_id=1, source_target_pairs={{0,4},{2,6},{4,8},{6,10},{8,12},{10,14},{12,0},{14,2},{1,5},{3,7},... | collective-permute-start | bytes 884744 | tf_op jit(solution)/shard_map/ppermute | solution.py:453
  108.1 10.4 %collective-permute-start.31 = (bf16[1,144,1024]{2,1,0:T(8,128)(2,1)S(1)}, bf16[1,144,1024]{2,1,0:T(8,128)(2,1)S(1)}, u32[]{:S(2)}, u32[]{:S(2)}) collective-permute-start(bf16[1,144,1024]{2,1,0:T(8,128)(2,1)S(1)} %add_convert_fusion.4), channel_id=1, source_target_pairs={{0,2},{2,0},{4,6},{6,4},{8,10},{10,8},{12,14},{14,12},{1,3},{3,1},... | collective-permute-start | bytes 884744 | tf_op jit(solution)/shard_map/ppermute | solution.py:450
  109.6 10.0 %collective-permute-start.30 = (bf16[1,144,1024]{2,1,0:T(8,128)(2,1)}, bf16[1,144,1024]{2,1,0:T(8,128)(2,1)S(1)}, u32[]{:S(2)}, u32[]{:S(2)}) collective-permute-start(bf16[1,144,1024]{2,1,0:T(8,128)(2,1)} %get-tuple-element.121), channel_id=1, source_target_pairs={{0,1},{1,0},{2,3},{3,2},{4,5},{5,4},{6,7},{7,6},{8,9},{9,8},{10,11... | collective-permute-start | bytes 884744 | tf_op jit(solution)/shard_map/ppermute | solution.py:444
  116.3 16.1 %collective-permute-start.25 = (bf16[1,144,1024]{2,1,0:T(8,128)(2,1)}, bf16[1,144,1024]{2,1,0:T(8,128)(2,1)S(1)}, u32[]{:S(2)}, u32[]{:S(2)}) collective-permute-start(bf16[1,144,1024]{2,1,0:T(8,128)(2,1)} %get-tuple-element.115), channel_id=1, source_target_pairs={{0,1},{1,0},{2,3},{3,2},{4,5},{5,4},{6,7},{7,6},{8,9},{9,8},{10,11... | collective-permute-start | bytes 884744 | tf_op jit(solution)/shard_map/ppermute | solution.py:444
  118.4 14.0 %collective-permute-start.26 = (bf16[1,144,1024]{2,1,0:T(8,128)(2,1)}, bf16[1,144,1024]{2,1,0:T(8,128)(2,1)S(1)}, u32[]{:S(2)}, u32[]{:S(2)}) collective-permute-start(bf16[1,144,1024]{2,1,0:T(8,128)(2,1)} %get-tuple-element.116), channel_id=1, source_target_pairs={{0,1},{1,0},{2,3},{3,2},{4,5},{5,4},{6,7},{7,6},{8,9},{9,8},{10,11... | collective-permute-start | bytes 884744 | tf_op jit(solution)/shard_map/ppermute | solution.py:444
  119.6 12.8 %collective-permute-start.27 = (bf16[1,144,1024]{2,1,0:T(8,128)(2,1)}, bf16[1,144,1024]{2,1,0:T(8,128)(2,1)S(1)}, u32[]{:S(2)}, u32[]{:S(2)}) collective-permute-start(bf16[1,144,1024]{2,1,0:T(8,128)(2,1)} %get-tuple-element.117), channel_id=1, source_target_pairs={{0,2},{2,0},{4,6},{6,4},{8,10},{10,8},{12,14},{14,12},{1,3},{3,1},... | collective-permute-start | bytes 884744 | tf_op jit(solution)/shard_map/ppermute | solution.py:450
  122.3 11.5 %collective-permute-start.29 = (bf16[1,144,1024]{2,1,0:T(8,128)(2,1)S(1)}, bf16[1,144,1024]{2,1,0:T(8,128)(2,1)S(1)}, u32[]{:S(2)}, u32[]{:S(2)}) collective-permute-start(bf16[1,144,1024]{2,1,0:T(8,128)(2,1)S(1)} %add_convert_fusion.5), channel_id=1, source_target_pairs={{0,2},{2,0},{4,6},{6,4},{8,10},{10,8},{12,14},{14,12},{1,3},{3,1},... | collective-permute-start | bytes 884744 | tf_op jit(solution)/shard_map/ppermute | solution.py:450
  122.9 10.9 %collective-permute-start.32 = (bf16[1,144,1024]{2,1,0:T(8,128)(2,1)S(1)}, bf16[1,144,1024]{2,1,0:T(8,128)(2,1)S(1)}, u32[]{:S(2)}, u32[]{:S(2)}) collective-permute-start(bf16[1,144,1024]{2,1,0:T(8,128)(2,1)S(1)} %add_convert_fusion.3), channel_id=1, source_target_pairs={{0,4},{2,6},{4,8},{6,10},{8,12},{10,14},{12,0},{14,2},{1,5},{3,7},... | collective-permute-start | bytes 884744 | tf_op jit(solution)/shard_map/ppermute | solution.py:453
  125.6 11.8 %copy-start.12 = (bf16[1,144,1024]{2,1,0:T(8,128)(2,1)S(1)}, bf16[1,144,1024]{2,1,0:T(8,128)(2,1)}, u32[]{:S(2)}) copy-start(bf16[1,144,1024]{2,1,0:T(8,128)(2,1)} %get-tuple-element.130) | copy-start | bytes 884740
  134.9 10.0 %collective-permute-start.35 = (bf16[1,144,1024]{2,1,0:T(8,128)(2,1)S(1)}, bf16[1,144,1024]{2,1,0:T(8,128)(2,1)S(1)}, u32[]{:S(2)}, u32[]{:S(2)}) collective-permute-start(bf16[1,144,1024]{2,1,0:T(8,128)(2,1)S(1)} %add_convert_fusion.2), channel_id=1, source_target_pairs={{0,12},{2,14},{4,0},{6,2},{8,4},{10,6},{12,8},{14,10},{1,13},{3,15... | collective-permute-start | bytes 884744 | tf_op jit(solution)/shard_map/ppermute | solution.py:453
  137.7 11.2 %collective-permute-start.36 = (bf16[1,144,1024]{2,1,0:T(8,128)(2,1)S(1)}, bf16[1,144,1024]{2,1,0:T(8,128)(2,1)S(1)}, u32[]{:S(2)}, u32[]{:S(2)}) collective-permute-start(bf16[1,144,1024]{2,1,0:T(8,128)(2,1)S(1)} %add_convert_fusion.1), channel_id=1, source_target_pairs={{0,4},{2,6},{4,8},{6,10},{8,12},{10,14},{12,0},{14,2},{1,5},{3,7},... | collective-permute-start | bytes 884744 | tf_op jit(solution)/shard_map/ppermute | solution.py:453
  137.8 11.1 %copy-start.13 = (bf16[1,144,1024]{2,1,0:T(8,128)(2,1)S(1)}, bf16[1,144,1024]{2,1,0:T(8,128)(2,1)}, u32[]{:S(2)}) copy-start(bf16[1,144,1024]{2,1,0:T(8,128)(2,1)} %get-tuple-element.82) | copy-start | bytes 884740
  137.9 11.1 %collective-permute-start.37 = (bf16[1,144,1024]{2,1,0:T(8,128)(2,1)S(1)}, bf16[1,144,1024]{2,1,0:T(8,128)(2,1)S(1)}, u32[]{:S(2)}, u32[]{:S(2)}) collective-permute-start(bf16[1,144,1024]{2,1,0:T(8,128)(2,1)S(1)} %add_convert_fusion), channel_id=1, source_target_pairs={{0,1},{1,0},{2,3},{3,2},{4,5},{5,4},{6,7},{7,6},{8,9},{9,8},{10,11... | collective-permute-start | bytes 884744 | tf_op jit(solution)/shard_map/ppermute | solution.py:444
  138.8 10.1 %collective-permute-start.38 = (bf16[1,144,1024]{2,1,0:T(8,128)(2,1)S(1)}, bf16[1,144,1024]{2,1,0:T(8,128)(2,1)S(1)}, u32[]{:S(2)}, u32[]{:S(2)}) collective-permute-start(bf16[1,144,1024]{2,1,0:T(8,128)(2,1)S(1)} %copy-done.26), channel_id=1, source_target_pairs={{0,2},{2,0},{4,6},{6,4},{8,10},{10,8},{12,14},{14,12},{1,3},{3,1},... | collective-permute-start | bytes 884744 | tf_op jit(solution)/shard_map/ppermute | solution.py:450
  (20 other events, 56.6 us)

commit v11 on v8

--- a/solution.py
+++ b/solution.py
@@ -157,7 +157,7 @@
             jax.ShapeDtypeStruct((width, 2 * part), jnp.bfloat16),
             jax.ShapeDtypeStruct((part, width), jnp.bfloat16),
         ],
-        compiler_params=pltpu.CompilerParams(vmem_limit_bytes=62 << 20),
+        compiler_params=pltpu.CompilerParams(vmem_limit_bytes=30 << 20),
         cost_estimate=pl.CostEstimate(flops=0, bytes_accessed=12 * width * part, transcendentals=0),
         name="weights",
     )(which, w_gate, w_up, w_down)
@@ -325,7 +325,7 @@
         ),
         out_shape=[jax.ShapeDtypeStruct((count * slots, sum(widths)), jnp.bfloat16)] * 2
         + [jax.ShapeDtypeStruct((len(blocks),) + packet, jnp.bfloat16) for blocks in items],
-        compiler_params=pltpu.CompilerParams(vmem_limit_bytes=62 << 20),
+        compiler_params=pltpu.CompilerParams(vmem_limit_bytes=30 << 20),
         cost_estimate=pl.CostEstimate(
             flops=count * (20 * slots * width * part + 24 * slots * tok * width),
             bytes_accessed=count * 16 * tok * width + 12 * width * part,
@@ -419,7 +419,7 @@
             ],
         ),
         out_shape=[jax.ShapeDtypeStruct(shape, jnp.bfloat16) for shape in shapes],
-        compiler_params=pltpu.CompilerParams(vmem_limit_bytes=24 << 20),
+        compiler_params=pltpu.CompilerParams(vmem_limit_bytes=20 << 20),
         cost_estimate=pl.CostEstimate(
             flops=2 * rows * width * deep, bytes_accessed=2 * rows * (width + deep), transcendentals=0
         ),

time: 148 us -> 145 us (0.980)
  Pallas kernels: 51.6 us -> 44.9 us
  other arithmetic: 5.71 us -> 2.46 us
  waiting for transfers between devices: 38 us -> 41.2 us
  local copies, waits for them, and re-layouts: 7.78 us -> 10.2 us
  starting transfers between devices: 42.9 us -> 44.6 us
    ppermute x9, waiting for transfers between devices: 0.82 us -> 4.22 us  [over_x(): return lax.ppermute(array, 'tp', [(0, 1), (1, 0)])]
    pallas_call x1, Pallas kernels: 3.99 us -> 1.46 us  [weights_call(): pl.pallas_call(weights_kernel, grid_spec=pltpu.PrefetchScalarGridSpec(num...]
    pallas_call x3, Pallas kernels: 34.9 us -> 32.3 us  [rows_call(): pl.pallas_call(functools.partial(rows_kernel, count, ways, capacity, slot...]
    ppermute x13, starting transfers between devices: 18 us -> 20.2 us  [over_z(): lax.ppermute(array, 'ep', [(i, (i + shift * n_y) % ep) for i in range(ep)])]
    convert_element_type x5, other arithmetic: 2.87 us -> 0.79 us  [total(): sum((block.astype(jnp.float32) for block in blocks)).astype(jnp.bfloat16)]
    unnamed x57 -> x21, local copies, waits for them, and re-layouts: 6.79 us -> 8.56 us
    pallas_call x2, Pallas kernels: 12.7 us -> 11.1 us  [grads_call(): pl.pallas_call(functools.partial(grads_kernel, count, *starts, 2 * per),...]
  transfers between devices with their start and end apart: 38 -> 38, of which waited for: 9 -> 10; matrix products, arithmetic and copies ran while one was open for 3% -> 1% of each run, Pallas kernels for 35% -> 31%
where the time goes in v11:
time: 145 us; the launch traced here: 144 us
  Pallas kernels  44.9 us (31%)
  starting transfers between devices  44.6 us (31%)
  waiting for transfers between devices  41.2 us (28%)
  local copies, waits for them, and re-layouts  10.2 us (7%)
  other arithmetic  2.46 us (2%)
    ppermute x13, waiting for transfers between devices, over_z(): lax.ppermute(array, 'ep', [(i, (i + shift * n_y) % ep) for i in range(ep)])  36.5 us
    pallas_call x3, Pallas kernels, rows_call(): pl.pallas_call(functools.partial(rows_kernel, count, ways, capacity, slot...  32.3 us
    ppermute x13, starting transfers between devices, over_z(): lax.ppermute(array, 'ep', [(i, (i + shift * n_y) % ep) for i in range(ep)])  20.2 us
    ppermute x11, starting transfers between devices, over_y(): lax.ppermute(array, 'ep', [(i, i + 1 - 2 * (i % n_y)) for i in range(ep)])  12 us
    ppermute x9, starting transfers between devices, over_x(): return lax.ppermute(array, 'tp', [(0, 1), (1, 0)])  11.7 us
    pallas_call x2, Pallas kernels, grads_call(): pl.pallas_call(functools.partial(grads_kernel, count, *starts, 2 * per),...  11.1 us
    unnamed x21, local copies, waits for them, and re-layouts  8.56 us
    ppermute x9, waiting for transfers between devices, over_x(): return lax.ppermute(array, 'tp', [(0, 1), (1, 0)])  4.22 us
  transfers between devices with their start and end apart: 38, of which 10 were waited for; matrix products, arithmetic and copies ran while one was open for 1% of the time, Pallas kernels for 31%

profile of v11, /device:TPU:0, one launch (start us, length us, event | category | flops | bytes accessed | tf_op | source)
XLA Modules:
  0.0 144.4 jit_solution(15697276819602790850)
XLA Ops:
  0.6 1.7 %constant_dynamic-update-slice_fusion.1 = bf16[256,1024]{1,0:T(8,128)(2,1)} fusion(bf16[128,1024]{1,0:T(8,128)(2,1)} %param.7), kind=kLoop, calls=%fused_computation.15 | loop fusion | bytes 524288
  2.3 1.7 %constant_dynamic-update-slice_fusion.refs_4_ = bf16[256,1024]{1,0:T(8,128)(2,1)} fusion(bf16[256,1024]{1,0:T(8,128)(2,1)} %constant_dynamic-update-slice_fusion.1, bf16[128,1024]{1,0:T(8,128)(2,1)} %param.8), kind=kLoop, calls=%fused_computation.14 | loop fusion | bytes 524288 | tf_op jit(solution)/shard_map/concatenate | solution.py:491
  4.0 3.0 %collective-permute-start = (bf16[256,1024]{1,0:T(8,128)(2,1)}, bf16[256,1024]{1,0:T(8,128)(2,1)}, u32[]{:S(2)}, u32[]{:S(2)}) collective-permute-start(bf16[256,1024]{1,0:T(8,128)(2,1)} %constant_dynamic-update-slice_fusion.refs_4_), channel_id=1, source_target_pairs={{0,4},{2,6},{4,8},{6,10},{8,12},{10,14},{12,0},{14,2},{1,5},{3,7},... | collective-permute-start | bytes 1572872 | tf_op jit(solution)/shard_map/ppermute | solution.py:450
  7.0 1.5 %collective-permute-start.1 = (bf16[256,1024]{1,0:T(8,128)(2,1)}, bf16[256,1024]{1,0:T(8,128)(2,1)}, u32[]{:S(2)}, u32[]{:S(2)}) collective-permute-start(bf16[256,1024]{1,0:T(8,128)(2,1)} %constant_dynamic-update-slice_fusion.refs_4_), channel_id=1, source_target_pairs={{0,2},{2,0},{4,6},{6,4},{8,10},{10,8},{12,14},{14,12},{1,3},{3,1},... | collective-permute-start | bytes 1572872 | tf_op jit(solution)/shard_map/ppermute | solution.py:447
  8.5 1.5 %collective-permute-start.2 = (bf16[256,1024]{1,0:T(8,128)(2,1)}, bf16[256,1024]{1,0:T(8,128)(2,1)}, u32[]{:S(2)}, u32[]{:S(2)}) collective-permute-start(bf16[256,1024]{1,0:T(8,128)(2,1)} %constant_dynamic-update-slice_fusion.refs_4_), channel_id=1, source_target_pairs={{0,1},{1,0},{2,3},{3,2},{4,5},{5,4},{6,7},{7,6},{8,9},{9,8},{10,11... | collective-permute-start | bytes 1572872 | tf_op jit(solution)/shard_map/ppermute | solution.py:441
  10.0 1.4 copy-done
  11.4 1.4 copy-done.1
  12.8 1.4 copy-done.2
  14.2 1.5 %weights.1 = (bf16[2048,768]{1,0:T(8,128)(2,1)S(1)}, bf16[384,2048]{1,0:T(8,128)(2,1)}) custom-call(s32[1]{0:T(128)} %bitcast.2.tp_ref, bf16[1,2048,384]{2,1,0:T(8,128)(2,1)S(1)} %copy-done, bf16[1,2048,384]{2,1,0:T(8,128)(2,1)S(1)} %copy-done.1, bf16[1,384,2048]{2,1,0:T(8,128)(2,1)S(1)} %copy-done.2), custom_call_target="tpu_custom_call" | custom-call | bytes 9437184 | tf_op jit(solution)/shard_map/weights/pallas_call | solution.py:141
  15.7 5.6 %collective-permute-done.refs_4_ = bf16[256,1024]{1,0:T(8,128)(2,1)} collective-permute-done((bf16[256,1024]{1,0:T(8,128)(2,1)}, bf16[256,1024]{1,0:T(8,128)(2,1)}, u32[]{:S(2)}, u32[]{:S(2)}) %collective-permute-start) | collective-permute-done | bytes 524320 | tf_op jit(solution)/shard_map/ppermute | solution.py:450
  21.3 0.7 collective-permute-done.2.refs_5_
  22.4 1.6 %collective-permute-start.7 = (bf16[256,1024]{1,0:T(8,128)(2,1)}, bf16[256,1024]{1,0:T(8,128)(2,1)}, u32[]{:S(2)}, u32[]{:S(2)}) collective-permute-start(bf16[256,1024]{1,0:T(8,128)(2,1)} %collective-permute-done.refs_4_), channel_id=1, source_target_pairs={{0,4},{2,6},{4,8},{6,10},{8,12},{10,14},{12,0},{14,2},{1,5},{3,7},... | collective-permute-start | bytes 1572872 | tf_op jit(solution)/shard_map/ppermute | solution.py:450
  24.5 1.5 %collective-permute-start.5 = (bf16[256,1024]{1,0:T(8,128)(2,1)}, bf16[256,1024]{1,0:T(8,128)(2,1)S(1)}, u32[]{:S(2)}, u32[]{:S(2)}) collective-permute-start(bf16[256,1024]{1,0:T(8,128)(2,1)} %collective-permute-done.1.refs_6_), channel_id=1, source_target_pairs={{0,1},{1,0},{2,3},{3,2},{4,5},{5,4},{6,7},{7,6},{8,9},{9,8},{10,11... | collective-permute-start | bytes 1572872 | tf_op jit(solution)/shard_map/ppermute | solution.py:441
  26.1 12.3 %collective-permute-done.7.refs_8_ = bf16[256,1024]{1,0:T(8,128)(2,1)} collective-permute-done((bf16[256,1024]{1,0:T(8,128)(2,1)}, bf16[256,1024]{1,0:T(8,128)(2,1)}, u32[]{:S(2)}, u32[]{:S(2)}) %collective-permute-start.7) | collective-permute-done | bytes 524320 | tf_op jit(solution)/shard_map/ppermute | solution.py:450
  38.4 0.9 collective-permute-start.6
  39.3 0.8 copy-done.6
  40.1 0.8 copy-done.3
  40.9 1.1 collective-permute-start.10
  42.0 1.5 %collective-permute-start.11 = (bf16[256,1024]{1,0:T(8,128)(2,1)}, bf16[256,1024]{1,0:T(8,128)(2,1)}, u32[]{:S(2)}, u32[]{:S(2)}) collective-permute-start(bf16[256,1024]{1,0:T(8,128)(2,1)} %collective-permute-done.7.refs_8_), channel_id=1, source_target_pairs={{0,1},{1,0},{2,3},{3,2},{4,5},{5,4},{6,7},{7,6},{8,9},{9,8},{10,11... | collective-permute-start | bytes 1572872 | tf_op jit(solution)/shard_map/ppermute | solution.py:441
  44.2 1.0 copy-done.4
  45.2 9.6 %rows.3 = (bf16[144,5248]{1,0:T(8,128)(2,1)S(1)}, bf16[144,5248]{1,0:T(8,128)(2,1)S(1)}, bf16[1,144,1024]{2,1,0:T(8,128)(2,1)S(1)}, bf16[1,144,1024]{2,1,0:T(8,1...) custom-call(s32[3]{0:T(128)S(1)} %pad_add_fusion.where_ref, ...), custom_call_target="tpu_custom_call" | custom-call | flops 3170893824 | bytes 13631488 | tf_op jit(solution)/shard_map/rows/pallas_call | solution.py:307
  54.8 1.2 collective-permute-done.9.refs_4_
  56.4 0.9 collective-permute-start.13
  58.4 3.5 %collective-permute-start.20 = (bf16[2,16,128]{2,1,0:T(8,128)(2,1)S(1)}, bf16[2,16,128]{2,1,0:T(8,128)(2,1)S(1)}, u32[]{:S(2)}, u32[]{:S(2)}) collective-permute-start(bf16[2,16,128]{2,1,0:T(8,128)(2,1)S(1)} %pad_maximum_fusion.refs_8_), channel_id=1, source_target_pairs={{0,8},{2,10},{4,12},{6,14},{8,0},{10,2},{12,4},{14,6},{1,9},{3,11}... | collective-permute-start | bytes 24584 | tf_op jit(solution)/shard_map/ppermute | solution.py:450
  61.9 7.4 %collective-permute-done.12.refs_7_ = bf16[256,1024]{1,0:T(8,128)(2,1)S(1)} collective-permute-done((bf16[256,1024]{1,0:T(8,128)(2,1)S(1)}, bf16[256,1024]{1,0:T(8,128)(2,1)S(1)}, u32[]{:S(2)}, u32[]{:S(2)}) %collective-permute-start.12) | collective-permute-done | bytes 524320 | tf_op jit(solution)/shard_map/ppermute | solution.py:450
  69.9 1.1 collective-permute-start.16
  70.9 3.5 %collective-permute-start.17 = (bf16[256,1024]{1,0:T(8,128)(2,1)S(1)}, bf16[256,1024]{1,0:T(8,128)(2,1)S(1)}, u32[]{:S(2)}, u32[]{:S(2)}) collective-permute-start(bf16[256,1024]{1,0:T(8,128)(2,1)S(1)} %copy-done.5), channel_id=1, source_target_pairs={{0,12},{2,14},{4,0},{6,2},{8,4},{10,6},{12,8},{14,10},{1,13},{3,15... | collective-permute-start | bytes 1572872 | tf_op jit(solution)/shard_map/ppermute | solution.py:450
  74.5 13.3 %rows.4 = (bf16[288,5248]{1,0:T(8,128)(2,1)S(1)}, bf16[288,5248]{1,0:T(8,128)(2,1)S(1)}, bf16[1,144,1024]{2,1,0:T(8,128)(2,1)S(1)}, bf16[2,144,1024]{2,1,0:T(8,1...) custom-call(s32[3]{0:T(128)S(1)} %pad_add_fusion.where_ref, ...), custom_call_target="tpu_custom_call" | custom-call | flops 6341787648 | bytes 17825792 | tf_op jit(solution)/shard_map/rows/pallas_call | solution.py:307
  87.9 0.7 collective-permute-start.18
  88.8 1.5 %collective-permute-start.21 = (bf16[1,144,1024]{2,1,0:T(8,128)(2,1)S(1)}, bf16[1,144,1024]{2,1,0:T(8,128)(2,1)S(1)}, u32[]{:S(2)}, u32[]{:S(2)}) collective-permute-start(bf16[1,144,1024]{2,1,0:T(8,128)(2,1)S(1)} %get-tuple-element.100), channel_id=1, source_target_pairs={{0,1},{1,0},{2,3},{3,2},{4,5},{5,4},{6,7},{7,6},{8,9},{9,8},{10,11... | collective-permute-start | bytes 884744 | tf_op jit(solution)/shard_map/ppermute | solution.py:441
  90.3 1.1 collective-permute-start.22
  91.7 2.4 %collective-permute-start.23 = (bf16[1,144,1024]{2,1,0:T(8,128)(2,1)S(1)}, bf16[1,144,1024]{2,1,0:T(8,128)(2,1)S(1)}, u32[]{:S(2)}, u32[]{:S(2)}) collective-permute-start(bf16[1,144,1024]{2,1,0:T(8,128)(2,1)S(1)} %get-tuple-element.102), channel_id=1, source_target_pairs={{0,12},{2,14},{4,0},{6,2},{8,4},{10,6},{12,8},{14,10},{1,13},{3,15... | collective-permute-start | bytes 884744 | tf_op jit(solution)/shard_map/ppermute | solution.py:450
  94.1 9.4 %rows.5 = (bf16[144,5248]{1,0:T(8,128)(2,1)S(1)}, bf16[144,5248]{1,0:T(8,128)(2,1)S(1)}, bf16[1,144,1024]{2,1,0:T(8,128)(2,1)S(1)}, bf16[1,144,1024]{2,1,0:T(8,1...) custom-call(s32[3]{0:T(128)S(1)} %pad_add_fusion.where_ref, ...), custom_call_target="tpu_custom_call" | custom-call | flops 3170893824 | bytes 13631488 | tf_op jit(solution)/shard_map/rows/pallas_call | solution.py:307
  103.6 1.6 %collective-permute-start.27 = (bf16[2,144,1024]{2,1,0:T(8,128)(2,1)S(1)}, bf16[2,144,1024]{2,1,0:T(8,128)(2,1)S(1)}, u32[]{:S(2)}, u32[]{:S(2)}) collective-permute-start(bf16[2,144,1024]{2,1,0:T(8,128)(2,1)S(1)} %get-tuple-element.107), channel_id=1, source_target_pairs={{0,1},{1,0},{2,3},{3,2},{4,5},{5,4},{6,7},{7,6},{8,9},{9,8},{10,11... | collective-permute-start | bytes 1769480 | tf_op jit(solution)/shard_map/ppermute | solution.py:441
  105.3 1.2 collective-permute-start.28
  106.9 1.5 %collective-permute-start.24 = (bf16[1,144,1024]{2,1,0:T(8,128)(2,1)S(1)}, bf16[1,144,1024]{2,1,0:T(8,128)(2,1)S(1)}, u32[]{:S(2)}, u32[]{:S(2)}) collective-permute-start(bf16[1,144,1024]{2,1,0:T(8,128)(2,1)S(1)} %get-tuple-element.103), channel_id=1, source_target_pairs={{0,1},{1,0},{2,3},{3,2},{4,5},{5,4},{6,7},{7,6},{8,9},{9,8},{10,11... | collective-permute-start | bytes 884744 | tf_op jit(solution)/shard_map/ppermute | solution.py:441
  108.4 1.1 collective-permute-start.25
  109.6 6.7 %grads.2 = (bf16[1,2048,384]{2,1,0:T(8,128)(2,1)}, bf16[1,2048,384]{2,1,0:T(8,128)(2,1)}) custom-call(s32[1]{0:T(128)} %bitcast.2.tp_ref, bf16[144,5248]{1,0:T(8,128)(2,1)S(1)} %get-tuple-element.81.refs_0_, bf16[144,5248]{1,0:T(8,128)(2,1)S(1)} %collective-permute-done.29.refs_1_, bf16[288,5248]{1,0:T(8,128)(2,1)S(1)} %get-tuple-element.88.refs_9_.refs_2_, ...), custom_call_target="tpu_custom_call" | custom-call | flops 3623878656 | bytes 6488064 | tf_op jit(solution)/shard_map/grads/pallas_call | solution.py:407
  116.3 3.5 %collective-permute-done.27 = bf16[2,144,1024]{2,1,0:T(8,128)(2,1)S(1)} collective-permute-done((bf16[2,144,1024]{2,1,0:T(8,128)(2,1)S(1)}, bf16[2,144,1024]{2,1,0:T(8,128)(2,1)S(1)}, u32[]{:S(2)}, u32[]{:S(2)}) %collective-permute-start.27) | collective-permute-done | bytes 589856 | tf_op jit(solution)/shard_map/ppermute | solution.py:441
  120.2 3.8 %collective-permute-start.34 = (bf16[1,144,1024]{2,1,0:T(8,128)(2,1)S(1)}, bf16[1,144,1024]{2,1,0:T(8,128)(2,1)S(1)}, u32[]{:S(2)}, u32[]{:S(2)}) collective-permute-start(bf16[1,144,1024]{2,1,0:T(8,128)(2,1)S(1)} %get-tuple-element.127), channel_id=1, source_target_pairs={{0,12},{2,14},{4,0},{6,2},{8,4},{10,6},{12,8},{14,10},{1,13},{3,15... | collective-permute-start | bytes 884744 | tf_op jit(solution)/shard_map/ppermute | solution.py:450
  124.1 1.2 collective-permute-start.36
  125.4 4.4 %grads.3 = bf16[1,384,2048]{2,1,0:T(8,128)(2,1)} custom-call(s32[1]{0:T(128)} %bitcast.2.tp_ref, bf16[144,5248]{1,0:T(8,128)(2,1)S(1)} %get-tuple-element.81.refs_0_, bf16[144,5248]{1,0:T(8,128)(2,1)S(1)} %collective-permute-done.29.refs_1_, bf16[288,5248]{1,0:T(8,128)(2,1)S(1)} %get-tuple-element.88.refs_9_.refs_2_, ...), custom_call_target="tpu_custom_call" | custom-call | flops 1811939328 | bytes 5603328 | tf_op jit(solution)/shard_map/grads/pallas_call | solution.py:407
  129.8 2.1 %collective-permute-done.32 = bf16[1,144,1024]{2,1,0:T(8,128)(2,1)S(1)} collective-permute-done((bf16[1,144,1024]{2,1,0:T(8,128)(2,1)S(1)}, bf16[1,144,1024]{2,1,0:T(8,128)(2,1)S(1)}, u32[]{:S(2)}, u32[]{:S(2)}) %collective-permute-start.32) | collective-permute-done | bytes 294944 | tf_op jit(solution)/shard_map/ppermute | solution.py:450
  132.2 1.2 collective-permute-start.33
  133.5 1.6 %collective-permute-start.37 = (bf16[1,144,1024]{2,1,0:T(8,128)(2,1)S(1)}, bf16[1,144,1024]{2,1,0:T(8,128)(2,1)S(1)}, u32[]{:S(2)}, u32[]{:S(2)}) collective-permute-start(bf16[1,144,1024]{2,1,0:T(8,128)(2,1)S(1)} %add_convert_fusion), channel_id=1, source_target_pairs={{0,1},{1,0},{2,3},{3,2},{4,5},{5,4},{6,7},{7,6},{8,9},{9,8},{10,11... | collective-permute-start | bytes 884744 | tf_op jit(solution)/shard_map/ppermute | solution.py:441
  135.0 7.7 %collective-permute-done.35 = bf16[1,144,1024]{2,1,0:T(8,128)(2,1)S(1)} collective-permute-done((bf16[1,144,1024]{2,1,0:T(8,128)(2,1)S(1)}, bf16[1,144,1024]{2,1,0:T(8,128)(2,1)S(1)}, u32[]{:S(2)}, u32[]{:S(2)}) %collective-permute-start.35) | collective-permute-done | bytes 294944 | tf_op jit(solution)/shard_map/ppermute | solution.py:450
  142.9 0.6 select_reduce_fusion
  143.5 0.9 fusion
  (71 shorter events, 5.7 us)
Async XLA Ops:
  4.0 17.3 %collective-permute-start = (bf16[256,1024]{1,0:T(8,128)(2,1)}, bf16[256,1024]{1,0:T(8,128)(2,1)}, u32[]{:S(2)}, u32[]{:S(2)}) collective-permute-start(bf16[256,1024]{1,0:T(8,128)(2,1)} %constant_dynamic-update-slice_fusion.refs_4_), channel_id=1, source_target_pairs={{0,4},{2,6},{4,8},{6,10},{8,12},{10,14},{12,0},{14,2},{1,5},{3,7},... | collective-permute-start | bytes 1572872 | tf_op jit(solution)/shard_map/ppermute | solution.py:450
  7.0 14.3 %collective-permute-start.1 = (bf16[256,1024]{1,0:T(8,128)(2,1)}, bf16[256,1024]{1,0:T(8,128)(2,1)}, u32[]{:S(2)}, u32[]{:S(2)}) collective-permute-start(bf16[256,1024]{1,0:T(8,128)(2,1)} %constant_dynamic-update-slice_fusion.refs_4_), channel_id=1, source_target_pairs={{0,2},{2,0},{4,6},{6,4},{8,10},{10,8},{12,14},{14,12},{1,3},{3,1},... | collective-permute-start | bytes 1572872 | tf_op jit(solution)/shard_map/ppermute | solution.py:447
  8.5 13.4 %collective-permute-start.2 = (bf16[256,1024]{1,0:T(8,128)(2,1)}, bf16[256,1024]{1,0:T(8,128)(2,1)}, u32[]{:S(2)}, u32[]{:S(2)}) collective-permute-start(bf16[256,1024]{1,0:T(8,128)(2,1)} %constant_dynamic-update-slice_fusion.refs_4_), channel_id=1, source_target_pairs={{0,1},{1,0},{2,3},{3,2},{4,5},{5,4},{6,7},{7,6},{8,9},{9,8},{10,11... | collective-permute-start | bytes 1572872 | tf_op jit(solution)/shard_map/ppermute | solution.py:441
  10.0 1.4 copy-start
  11.4 1.4 copy-start.1
  12.8 1.4 copy-start.2
  14.2 11.8 %copy-start.9 = (bf16[128,8]{0,1:T(8,128)(2,1)S(1)}, bf16[128,8]{0,1:T(8,128)(2,1)}, u32[]{:S(2)}) copy-start(bf16[128,8]{0,1:T(8,128)(2,1)} %param.10) | copy-start | bytes 6148
  14.2 11.8 %copy-start.8 = (s32[128,8]{0,1:T(8,128)S(1)}, s32[128,8]{0,1:T(8,128)}, u32[]{:S(2)}) copy-start(s32[128,8]{0,1:T(8,128)} %param.9) | copy-start | bytes 12292
  21.9 22.2 %collective-permute-start.3 = (bf16[2048,768]{1,0:T(8,128)(2,1)S(1)}, bf16[2048,768]{1,0:T(8,128)(2,1)}, u32[]{:S(2)}, u32[]{:S(2)}) collective-permute-start(bf16[2048,768]{1,0:T(8,128)(2,1)S(1)} %get-tuple-element.68.refs_0_), channel_id=1, source_target_pairs={{0,16},{16,0},{1,17},{17,1},{2,18},{18,2},{3,19},{19,3},{4,20},{20... | collective-permute-start | bytes 9437192 | tf_op jit(solution)/shard_map/ppermute | solution.py:444
  21.9 22.2 %collective-permute-start.4 = (bf16[384,2048]{1,0:T(8,128)(2,1)}, bf16[384,2048]{1,0:T(8,128)(2,1)}, u32[]{:S(2)}, u32[]{:S(2)}) collective-permute-start(bf16[384,2048]{1,0:T(8,128)(2,1)} %get-tuple-element.69.refs_2_), channel_id=1, source_target_pairs={{0,16},{16,0},{1,17},{17,1},{2,18},{18,2},{3,19},{19,3},{4,20},{20... | collective-permute-start | bytes 4718600 | tf_op jit(solution)/shard_map/ppermute | solution.py:444
  22.4 15.9 %collective-permute-start.7 = (bf16[256,1024]{1,0:T(8,128)(2,1)}, bf16[256,1024]{1,0:T(8,128)(2,1)}, u32[]{:S(2)}, u32[]{:S(2)}) collective-permute-start(bf16[256,1024]{1,0:T(8,128)(2,1)} %collective-permute-done.refs_4_), channel_id=1, source_target_pairs={{0,4},{2,6},{4,8},{6,10},{8,12},{10,14},{12,0},{14,2},{1,5},{3,7},... | collective-permute-start | bytes 1572872 | tf_op jit(solution)/shard_map/ppermute | solution.py:450
  24.0 15.3 %collective-permute-start.8 = (bf16[256,1024]{1,0:T(8,128)(2,1)}, bf16[256,1024]{1,0:T(8,128)(2,1)S(1)}, u32[]{:S(2)}, u32[]{:S(2)}) collective-permute-start(bf16[256,1024]{1,0:T(8,128)(2,1)} %collective-permute-done.refs_4_), channel_id=1, source_target_pairs={{0,2},{2,0},{4,6},{6,4},{8,10},{10,8},{12,14},{14,12},{1,3},{3,1},... | collective-permute-start | bytes 1572872 | tf_op jit(solution)/shard_map/ppermute | solution.py:447
  24.5 15.6 %collective-permute-start.5 = (bf16[256,1024]{1,0:T(8,128)(2,1)}, bf16[256,1024]{1,0:T(8,128)(2,1)S(1)}, u32[]{:S(2)}, u32[]{:S(2)}) collective-permute-start(bf16[256,1024]{1,0:T(8,128)(2,1)} %collective-permute-done.1.refs_6_), channel_id=1, source_target_pairs={{0,1},{1,0},{2,3},{3,2},{4,5},{5,4},{6,7},{7,6},{8,9},{9,8},{10,11... | collective-permute-start | bytes 1572872 | tf_op jit(solution)/shard_map/ppermute | solution.py:441
  38.4 5.2 %collective-permute-start.6 = (bf16[16,128]{1,0:T(8,128)(2,1)S(1)}, bf16[16,128]{1,0:T(8,128)(2,1)S(1)}, u32[]{:S(2)}, u32[]{:S(2)}) collective-permute-start(bf16[16,128]{1,0:T(8,128)(2,1)S(1)} %get-tuple-element.130), channel_id=1, source_target_pairs={{0,2},{2,0},{4,6},{6,4},{8,10},{10,8},{12,14},{14,12},{1,3},{3,1},... | collective-permute-start | bytes 12296 | tf_op jit(solution)/shard_map/ppermute | solution.py:447
  39.3 0.8 copy-start.6
  40.1 0.8 copy-start.3
  40.9 13.9 %collective-permute-start.10 = (bf16[256,1024]{1,0:T(8,128)(2,1)}, bf16[256,1024]{1,0:T(8,128)(2,1)}, u32[]{:S(2)}, u32[]{:S(2)}) collective-permute-start(bf16[256,1024]{1,0:T(8,128)(2,1)} %collective-permute-done.7.refs_8_), channel_id=1, source_target_pairs={{0,2},{2,0},{4,6},{6,4},{8,10},{10,8},{12,14},{14,12},{1,3},{3,1},... | collective-permute-start | bytes 1572872 | tf_op jit(solution)/shard_map/ppermute | solution.py:447
  42.0 12.8 %collective-permute-start.11 = (bf16[256,1024]{1,0:T(8,128)(2,1)}, bf16[256,1024]{1,0:T(8,128)(2,1)}, u32[]{:S(2)}, u32[]{:S(2)}) collective-permute-start(bf16[256,1024]{1,0:T(8,128)(2,1)} %collective-permute-done.7.refs_8_), channel_id=1, source_target_pairs={{0,1},{1,0},{2,3},{3,2},{4,5},{5,4},{6,7},{7,6},{8,9},{9,8},{10,11... | collective-permute-start | bytes 1572872 | tf_op jit(solution)/shard_map/ppermute | solution.py:441
  43.5 12.5 %collective-permute-start.9 = (bf16[256,1024]{1,0:T(8,128)(2,1)}, bf16[256,1024]{1,0:T(8,128)(2,1)}, u32[]{:S(2)}, u32[]{:S(2)}) collective-permute-start(bf16[256,1024]{1,0:T(8,128)(2,1)} %constant_dynamic-update-slice_fusion.refs_4_), channel_id=1, source_target_pairs={{0,12},{2,14},{4,0},{6,2},{8,4},{10,6},{12,8},{14,10},{1,13},{3,15... | collective-permute-start | bytes 1572872 | tf_op jit(solution)/shard_map/ppermute | solution.py:450
  44.2 1.0 copy-start.4
  45.2 25.7 %copy-start.5 = (bf16[256,1024]{1,0:T(8,128)(2,1)S(1)}, bf16[256,1024]{1,0:T(8,128)(2,1)}, u32[]{:S(2)}) copy-start(bf16[256,1024]{1,0:T(8,128)(2,1)} %copy-done.3) | copy-start | bytes 1572868
  45.2 29.3 %copy-start.7 = (bf16[256,1024]{1,0:T(8,128)(2,1)S(1)}, bf16[256,1024]{1,0:T(8,128)(2,1)}, u32[]{:S(2)}) copy-start(bf16[256,1024]{1,0:T(8,128)(2,1)} %copy-done.6) | copy-start | bytes 1572868
  56.0 13.3 %collective-permute-start.12 = (bf16[256,1024]{1,0:T(8,128)(2,1)S(1)}, bf16[256,1024]{1,0:T(8,128)(2,1)S(1)}, u32[]{:S(2)}, u32[]{:S(2)}) collective-permute-start(bf16[256,1024]{1,0:T(8,128)(2,1)S(1)} %copy-done.4), channel_id=1, source_target_pairs={{0,4},{2,6},{4,8},{6,10},{8,12},{10,14},{12,0},{14,2},{1,5},{3,7},... | collective-permute-start | bytes 1572872 | tf_op jit(solution)/shard_map/ppermute | solution.py:450
  56.4 12.9 %collective-permute-start.13 = (bf16[256,1024]{1,0:T(8,128)(2,1)}, bf16[256,1024]{1,0:T(8,128)(2,1)S(1)}, u32[]{:S(2)}, u32[]{:S(2)}) collective-permute-start(bf16[256,1024]{1,0:T(8,128)(2,1)} %collective-permute-done.11.refs_9_), channel_id=1, source_target_pairs={{0,2},{2,0},{4,6},{6,4},{8,10},{10,8},{12,14},{14,12},{1,3},{3,1},... | collective-permute-start | bytes 1572872 | tf_op jit(solution)/shard_map/ppermute | solution.py:447
  57.3 12.0 %collective-permute-start.14 = (bf16[256,1024]{1,0:T(8,128)(2,1)}, bf16[256,1024]{1,0:T(8,128)(2,1)S(1)}, u32[]{:S(2)}, u32[]{:S(2)}) collective-permute-start(bf16[256,1024]{1,0:T(8,128)(2,1)} %collective-permute-done.refs_4_), channel_id=1, source_target_pairs={{0,1},{1,0},{2,3},{3,2},{4,5},{5,4},{6,7},{7,6},{8,9},{9,8},{10,11... | collective-permute-start | bytes 1572872 | tf_op jit(solution)/shard_map/ppermute | solution.py:441
  57.8 16.7 %collective-permute-start.19 = (bf16[2,16,128]{2,1,0:T(8,128)(2,1)S(1)}, bf16[2,16,128]{2,1,0:T(8,128)(2,1)S(1)}, u32[]{:S(2)}, u32[]{:S(2)}) collective-permute-start(bf16[2,16,128]{2,1,0:T(8,128)(2,1)S(1)} %pad_maximum_fusion.refs_8_), channel_id=1, source_target_pairs={{0,4},{2,6},{4,8},{6,10},{8,12},{10,14},{12,0},{14,2},{1,5},{3,7},... | collective-permute-start | bytes 24584 | tf_op jit(solution)/shard_map/ppermute | solution.py:450
  58.4 16.1 %collective-permute-start.20 = (bf16[2,16,128]{2,1,0:T(8,128)(2,1)S(1)}, bf16[2,16,128]{2,1,0:T(8,128)(2,1)S(1)}, u32[]{:S(2)}, u32[]{:S(2)}) collective-permute-start(bf16[2,16,128]{2,1,0:T(8,128)(2,1)S(1)} %pad_maximum_fusion.refs_8_), channel_id=1, source_target_pairs={{0,8},{2,10},{4,12},{6,14},{8,0},{10,2},{12,4},{14,6},{1,9},{3,11}... | collective-permute-start | bytes 24584 | tf_op jit(solution)/shard_map/ppermute | solution.py:450
  69.3 18.5 %collective-permute-start.15 = (bf16[256,1024]{1,0:T(8,128)(2,1)}, bf16[256,1024]{1,0:T(8,128)(2,1)S(1)}, u32[]{:S(2)}, u32[]{:S(2)}) collective-permute-start(bf16[256,1024]{1,0:T(8,128)(2,1)} %collective-permute-done.9.refs_4_), channel_id=1, source_target_pairs={{0,1},{1,0},{2,3},{3,2},{4,5},{5,4},{6,7},{7,6},{8,9},{9,8},{10,11... | collective-permute-start | bytes 1572872 | tf_op jit(solution)/shard_map/ppermute | solution.py:441
  69.9 18.0 %collective-permute-start.16 = (bf16[256,1024]{1,0:T(8,128)(2,1)}, bf16[256,1024]{1,0:T(8,128)(2,1)S(1)}, u32[]{:S(2)}, u32[]{:S(2)}) collective-permute-start(bf16[256,1024]{1,0:T(8,128)(2,1)} %collective-permute-done.9.refs_4_), channel_id=1, source_target_pairs={{0,2},{2,0},{4,6},{6,4},{8,10},{10,8},{12,14},{14,12},{1,3},{3,1},... | collective-permute-start | bytes 1572872 | tf_op jit(solution)/shard_map/ppermute | solution.py:447
  70.9 16.9 %collective-permute-start.17 = (bf16[256,1024]{1,0:T(8,128)(2,1)S(1)}, bf16[256,1024]{1,0:T(8,128)(2,1)S(1)}, u32[]{:S(2)}, u32[]{:S(2)}) collective-permute-start(bf16[256,1024]{1,0:T(8,128)(2,1)S(1)} %copy-done.5), channel_id=1, source_target_pairs={{0,12},{2,14},{4,0},{6,2},{8,4},{10,6},{12,8},{14,10},{1,13},{3,15... | collective-permute-start | bytes 1572872 | tf_op jit(solution)/shard_map/ppermute | solution.py:450
  87.9 20.6 %collective-permute-start.30 = (bf16[288,5248]{1,0:T(8,128)(2,1)S(1)}, bf16[288,5248]{1,0:T(8,128)(2,1)S(1)}, u32[]{:S(2)}, u32[]{:S(2)}) collective-permute-start(bf16[288,5248]{1,0:T(8,128)(2,1)S(1)} %get-tuple-element.110), channel_id=1, source_target_pairs={{0,16},{16,0},{1,17},{17,1},{2,18},{18,2},{3,19},{19,3},{4,20},{20... | collective-permute-start | bytes 9068552 | tf_op jit(solution)/shard_map/ppermute | solution.py:444
  87.9 3.7 %collective-permute-start.18 = (bf16[2,16,128]{2,1,0:T(8,128)(2,1)S(1)}, bf16[2,16,128]{2,1,0:T(8,128)(2,1)S(1)}, u32[]{:S(2)}, u32[]{:S(2)}) collective-permute-start(bf16[2,16,128]{2,1,0:T(8,128)(2,1)S(1)} %pad_maximum_fusion.refs_8_), channel_id=1, source_target_pairs={{0,12},{2,14},{4,0},{6,2},{8,4},{10,6},{12,8},{14,10},{1,13},{3,15... | collective-permute-start | bytes 24584 | tf_op jit(solution)/shard_map/ppermute | solution.py:450
  88.6 17.8 %collective-permute-start.29 = (bf16[144,5248]{1,0:T(8,128)(2,1)S(1)}, bf16[144,5248]{1,0:T(8,128)(2,1)S(1)}, u32[]{:S(2)}, u32[]{:S(2)}) collective-permute-start(bf16[144,5248]{1,0:T(8,128)(2,1)S(1)} %get-tuple-element.109), channel_id=1, source_target_pairs={{0,16},{16,0},{1,17},{17,1},{2,18},{18,2},{3,19},{19,3},{4,20},{20... | collective-permute-start | bytes 4534280 | tf_op jit(solution)/shard_map/ppermute | solution.py:444
  88.8 14.7 %collective-permute-start.21 = (bf16[1,144,1024]{2,1,0:T(8,128)(2,1)S(1)}, bf16[1,144,1024]{2,1,0:T(8,128)(2,1)S(1)}, u32[]{:S(2)}, u32[]{:S(2)}) collective-permute-start(bf16[1,144,1024]{2,1,0:T(8,128)(2,1)S(1)} %get-tuple-element.100), channel_id=1, source_target_pairs={{0,1},{1,0},{2,3},{3,2},{4,5},{5,4},{6,7},{7,6},{8,9},{9,8},{10,11... | collective-permute-start | bytes 884744 | tf_op jit(solution)/shard_map/ppermute | solution.py:441
  90.3 13.2 %collective-permute-start.22 = (bf16[1,144,1024]{2,1,0:T(8,128)(2,1)S(1)}, bf16[1,144,1024]{2,1,0:T(8,128)(2,1)S(1)}, u32[]{:S(2)}, u32[]{:S(2)}) collective-permute-start(bf16[1,144,1024]{2,1,0:T(8,128)(2,1)S(1)} %get-tuple-element.101), channel_id=1, source_target_pairs={{0,2},{2,0},{4,6},{6,4},{8,10},{10,8},{12,14},{14,12},{1,3},{3,1},... | collective-permute-start | bytes 884744 | tf_op jit(solution)/shard_map/ppermute | solution.py:447
  91.7 11.9 %collective-permute-start.23 = (bf16[1,144,1024]{2,1,0:T(8,128)(2,1)S(1)}, bf16[1,144,1024]{2,1,0:T(8,128)(2,1)S(1)}, u32[]{:S(2)}, u32[]{:S(2)}) collective-permute-start(bf16[1,144,1024]{2,1,0:T(8,128)(2,1)S(1)} %get-tuple-element.102), channel_id=1, source_target_pairs={{0,12},{2,14},{4,0},{6,2},{8,4},{10,6},{12,8},{14,10},{1,13},{3,15... | collective-permute-start | bytes 884744 | tf_op jit(solution)/shard_map/ppermute | solution.py:450
  103.5 3.4 %collective-permute-start.31 = (bf16[144,5248]{1,0:T(8,128)(2,1)S(1)}, bf16[144,5248]{1,0:T(8,128)(2,1)S(1)}, u32[]{:S(2)}, u32[]{:S(2)}) collective-permute-start(bf16[144,5248]{1,0:T(8,128)(2,1)S(1)} %get-tuple-element.112), channel_id=1, source_target_pairs={{0,16},{16,0},{1,17},{17,1},{2,18},{18,2},{3,19},{19,3},{4,20},{20... | collective-permute-start | bytes 4534280 | tf_op jit(solution)/shard_map/ppermute | solution.py:444
  103.6 16.2 %collective-permute-start.27 = (bf16[2,144,1024]{2,1,0:T(8,128)(2,1)S(1)}, bf16[2,144,1024]{2,1,0:T(8,128)(2,1)S(1)}, u32[]{:S(2)}, u32[]{:S(2)}) collective-permute-start(bf16[2,144,1024]{2,1,0:T(8,128)(2,1)S(1)} %get-tuple-element.107), channel_id=1, source_target_pairs={{0,1},{1,0},{2,3},{3,2},{4,5},{5,4},{6,7},{7,6},{8,9},{9,8},{10,11... | collective-permute-start | bytes 1769480 | tf_op jit(solution)/shard_map/ppermute | solution.py:441
  105.3 14.6 %collective-permute-start.28 = (bf16[1,144,1024]{2,1,0:T(8,128)(2,1)S(1)}, bf16[1,144,1024]{2,1,0:T(8,128)(2,1)S(1)}, u32[]{:S(2)}, u32[]{:S(2)}) collective-permute-start(bf16[1,144,1024]{2,1,0:T(8,128)(2,1)S(1)} %add_convert_fusion.5), channel_id=1, source_target_pairs={{0,2},{2,0},{4,6},{6,4},{8,10},{10,8},{12,14},{14,12},{1,3},{3,1},... | collective-permute-start | bytes 884744 | tf_op jit(solution)/shard_map/ppermute | solution.py:447
  106.5 13.3 %collective-permute-start.26 = (bf16[1,144,1024]{2,1,0:T(8,128)(2,1)S(1)}, bf16[1,144,1024]{2,1,0:T(8,128)(2,1)S(1)}, u32[]{:S(2)}, u32[]{:S(2)}) collective-permute-start(bf16[1,144,1024]{2,1,0:T(8,128)(2,1)S(1)} %get-tuple-element.106), channel_id=1, source_target_pairs={{0,4},{2,6},{4,8},{6,10},{8,12},{10,14},{12,0},{14,2},{1,5},{3,7},... | collective-permute-start | bytes 884744 | tf_op jit(solution)/shard_map/ppermute | solution.py:450
  106.9 22.9 %collective-permute-start.24 = (bf16[1,144,1024]{2,1,0:T(8,128)(2,1)S(1)}, bf16[1,144,1024]{2,1,0:T(8,128)(2,1)S(1)}, u32[]{:S(2)}, u32[]{:S(2)}) collective-permute-start(bf16[1,144,1024]{2,1,0:T(8,128)(2,1)S(1)} %get-tuple-element.103), channel_id=1, source_target_pairs={{0,1},{1,0},{2,3},{3,2},{4,5},{5,4},{6,7},{7,6},{8,9},{9,8},{10,11... | collective-permute-start | bytes 884744 | tf_op jit(solution)/shard_map/ppermute | solution.py:441
  108.4 21.4 %collective-permute-start.25 = (bf16[1,144,1024]{2,1,0:T(8,128)(2,1)S(1)}, bf16[1,144,1024]{2,1,0:T(8,128)(2,1)S(1)}, u32[]{:S(2)}, u32[]{:S(2)}) collective-permute-start(bf16[1,144,1024]{2,1,0:T(8,128)(2,1)S(1)} %get-tuple-element.104), channel_id=1, source_target_pairs={{0,2},{2,0},{4,6},{6,4},{8,10},{10,8},{12,14},{14,12},{1,3},{3,1},... | collective-permute-start | bytes 884744 | tf_op jit(solution)/shard_map/ppermute | solution.py:447
  120.1 11.8 %collective-permute-start.32 = (bf16[1,144,1024]{2,1,0:T(8,128)(2,1)S(1)}, bf16[1,144,1024]{2,1,0:T(8,128)(2,1)S(1)}, u32[]{:S(2)}, u32[]{:S(2)}) collective-permute-start(bf16[1,144,1024]{2,1,0:T(8,128)(2,1)S(1)} %get-tuple-element.128), channel_id=1, source_target_pairs={{0,4},{2,6},{4,8},{6,10},{8,12},{10,14},{12,0},{14,2},{1,5},{3,7},... | collective-permute-start | bytes 884744 | tf_op jit(solution)/shard_map/ppermute | solution.py:450
  120.2 14.9 %collective-permute-start.34 = (bf16[1,144,1024]{2,1,0:T(8,128)(2,1)S(1)}, bf16[1,144,1024]{2,1,0:T(8,128)(2,1)S(1)}, u32[]{:S(2)}, u32[]{:S(2)}) collective-permute-start(bf16[1,144,1024]{2,1,0:T(8,128)(2,1)S(1)} %get-tuple-element.127), channel_id=1, source_target_pairs={{0,12},{2,14},{4,0},{6,2},{8,4},{10,6},{12,8},{14,10},{1,13},{3,15... | collective-permute-start | bytes 884744 | tf_op jit(solution)/shard_map/ppermute | solution.py:450
  124.1 9.3 %collective-permute-start.36 = (bf16[1,144,1024]{2,1,0:T(8,128)(2,1)S(1)}, bf16[1,144,1024]{2,1,0:T(8,128)(2,1)S(1)}, u32[]{:S(2)}, u32[]{:S(2)}) collective-permute-start(bf16[1,144,1024]{2,1,0:T(8,128)(2,1)S(1)} %add_convert_fusion.1), channel_id=1, source_target_pairs={{0,2},{2,0},{4,6},{6,4},{8,10},{10,8},{12,14},{14,12},{1,3},{3,1},... | collective-permute-start | bytes 884744 | tf_op jit(solution)/shard_map/ppermute | solution.py:447
  132.1 10.7 %collective-permute-start.35 = (bf16[1,144,1024]{2,1,0:T(8,128)(2,1)S(1)}, bf16[1,144,1024]{2,1,0:T(8,128)(2,1)S(1)}, u32[]{:S(2)}, u32[]{:S(2)}) collective-permute-start(bf16[1,144,1024]{2,1,0:T(8,128)(2,1)S(1)} %add_convert_fusion.2), channel_id=1, source_target_pairs={{0,4},{2,6},{4,8},{6,10},{8,12},{10,14},{12,0},{14,2},{1,5},{3,7},... | collective-permute-start | bytes 884744 | tf_op jit(solution)/shard_map/ppermute | solution.py:450
  132.2 10.6 %collective-permute-start.33 = (bf16[1,144,1024]{2,1,0:T(8,128)(2,1)S(1)}, bf16[1,144,1024]{2,1,0:T(8,128)(2,1)S(1)}, u32[]{:S(2)}, u32[]{:S(2)}) collective-permute-start(bf16[1,144,1024]{2,1,0:T(8,128)(2,1)S(1)} %get-tuple-element.118), channel_id=1, source_target_pairs={{0,2},{2,0},{4,6},{6,4},{8,10},{10,8},{12,14},{14,12},{1,3},{3,1},... | collective-permute-start | bytes 884744 | tf_op jit(solution)/shard_map/ppermute | solution.py:447
  133.5 9.3 %collective-permute-start.37 = (bf16[1,144,1024]{2,1,0:T(8,128)(2,1)S(1)}, bf16[1,144,1024]{2,1,0:T(8,128)(2,1)S(1)}, u32[]{:S(2)}, u32[]{:S(2)}) collective-permute-start(bf16[1,144,1024]{2,1,0:T(8,128)(2,1)S(1)} %add_convert_fusion), channel_id=1, source_target_pairs={{0,1},{1,0},{2,3},{3,2},{4,5},{5,4},{6,7},{7,6},{8,9},{9,8},{10,11... | collective-permute-start | bytes 884744 | tf_op jit(solution)/shard_map/ppermute | solution.py:441

commit v12 on v11

--- a/solution.py
+++ b/solution.py
@@ -157,23 +157,48 @@
             jax.ShapeDtypeStruct((width, 2 * part), jnp.bfloat16),
             jax.ShapeDtypeStruct((part, width), jnp.bfloat16),
         ],
-        compiler_params=pltpu.CompilerParams(vmem_limit_bytes=30 << 20),
+        compiler_params=pltpu.CompilerParams(vmem_limit_bytes=16 << 20),
         cost_estimate=pl.CostEstimate(flops=0, bytes_accessed=12 * width * part, transcendentals=0),
         name="weights",
     )(which, w_gate, w_up, w_down)
 
 
+def join_kernel(top_ref, bottom_ref, out_ref, sems):
+    rows = top_ref.shape[0]
+    copies = [
+        pltpu.make_async_copy(top_ref, out_ref.at[pl.ds(0, rows)], sems.at[0]),
+        pltpu.make_async_copy(bottom_ref, out_ref.at[pl.ds(rows, rows)], sems.at[1]),
+    ]
+    for copy in copies:
+        copy.start()
+    for copy in copies:
+        copy.wait()
+
+
+def join_call(top, bottom):
+    rows, columns = top.shape
+    return pl.pallas_call(
+        join_kernel,
+        in_specs=[LOOSE] * 2,
+        out_specs=LOOSE,
+        out_shape=jax.ShapeDtypeStruct((2 * rows, columns), top.dtype),
+        scratch_shapes=[pltpu.SemaphoreType.DMA((2,))],
+        compiler_params=pltpu.CompilerParams(vmem_limit_bytes=8 << 20),
+        cost_estimate=pl.CostEstimate(flops=0, bytes_accessed=8 * rows * columns, transcendentals=0),
+        name="join",
+    )(top, bottom)
+
+
 def rows_kernel(count, ways, capacity, slots, where_ref, *refs):
     weights_in, units_in, tables_in = refs[:4], refs[4 : 4 + 4 * count], refs[4 + 4 * count : 4 + 5 * count]
     leaves = 1 + max(way[0] for way in ways.values())
-    refs = refs[len(refs) - 17 - leaves :]
+    refs = refs[len(refs) - 6 - leaves :]
     outs, packets, refs = refs[:2], refs[2 : 2 + leaves], refs[2 + leaves :]
-    x_all, g_all, tables, wgu0, wgu1, wd0, wd1, xc, gc, both, scaled, piece, unit_sems, weight_sems = refs[:14]
-    out_sems = refs[14]
+    x_all, g_all, tables, unit_sems = refs
     half, tok = x_all.shape[3], x_all.shape[2] // 2
-    part = scaled.shape[2]
+    part = weights_in[2].shape[0]
     owners = tables.shape[2]
-    wgu, wd = (wgu0, wgu1), (wd0, wd1)
+    wgu, wd = weights_in[:2], weights_in[2:]
 
     x_copies, g_copies = [], []
     for index, unit in enumerate(units_in):
@@ -184,22 +209,9 @@
     t_copies = [
         pltpu.make_async_copy(table, tables.at[chunk], unit_sems.at[2, chunk]) for chunk, table in enumerate(tables_in)
     ]
-    weight_copies = [
-        pltpu.make_async_copy(source, target, weight_sems.at[index])
-        for index, (source, target) in enumerate(zip(weights_in, (wgu0, wgu1, wd0, wd1)))
-    ]
-    for copy in t_copies + x_copies + weight_copies[:2] + g_copies + weight_copies[2:]:
+    for copy in t_copies + x_copies + g_copies:
         copy.start()
-    leaving = []
-
-    def leave(source, target):
-        copy = pltpu.make_async_copy(source, target, out_sems.at[len(leaving)])
-        copy.start()
-        leaving.append(copy)
-
-    def leave_rows(held, start):
-        for expert in range(2):
-            leave(held.at[expert], outs[expert].at[:, pl.ds(start, held.shape[2])])
+    both_at, scaled_at = pl.ds(4 * half, 2 * part), pl.ds(4 * half + 2 * part, part)
 
     def dot(a, b, dims):
         return lax.dot_general(a, b, (dims, ((), ())), preferred_element_type=jnp.float32)
@@ -208,7 +220,7 @@
         copy.wait()
     earlier = lax.broadcasted_iota(jnp.int32, (tok, tok), 0) < lax.broadcasted_iota(jnp.int32, (tok, tok), 1)
     earlier = earlier.astype(jnp.bfloat16)
-    number = lax.broadcasted_iota(jnp.int32, (slots, tok), 0).astype(jnp.float32)
+    place = lax.broadcasted_iota(jnp.int32, (slots, tok), 0).astype(jnp.float32)
     names = lax.broadcasted_iota(jnp.int32, (owners, tok), 0)
     picks, low_picks, probs = {}, {}, {}
     for chunk in range(count):
@@ -223,7 +235,7 @@
             for table, rank in found:
                 weight = jnp.sum(jnp.where(mine, table, 0.0), axis=0, keepdims=True)
                 slot = jnp.sum(jnp.where(mine, rank, 0.0), axis=0, keepdims=True)
-                halves.append((number == slot).astype(jnp.float32))
+                halves.append((place == slot).astype(jnp.float32))
                 term = jnp.sum(halves[-1] * weight, axis=1, keepdims=True)
                 prob = term if prob is None else prob + term
             picks[chunk, expert] = halves
@@ -232,7 +244,7 @@
     spans = [pl.ds(chunk * slots, slots) for chunk in range(count)]
     sides = [slice(side * half, (side + 1) * half) for side in range(2)]
 
-    def gather(copies, source, target):
+    def gather(copies, source, offset):
         for chunk in range(count):
             for copy in copies[4 * chunk : 4 * chunk + 4]:
                 copy.wait()
@@ -240,20 +252,17 @@
             for side in range(2):
                 rows = dot(both_picks, source[chunk, side], ((1,), (0,))).astype(jnp.bfloat16)
                 for expert in range(2):
-                    target[expert, spans[chunk], sides[side]] = rows[expert * slots : (expert + 1) * slots]
-
-    gather(x_copies, x_all, xc)
-    leave_rows(xc, 0)
+                    columns = pl.ds(offset + side * half, half)
+                    outs[expert][spans[chunk], columns] = rows[expert * slots : (expert + 1) * slots]
+
+    gather(x_copies, x_all, 0)
     rows = []
     for expert in range(2):
-        weight_copies[expert].wait()
-        rows.append(dot(xc[expert], wgu[expert][...], ((1,), (0,))))
-    gather(g_copies, g_all, gc)
-    leave_rows(gc, 2 * half)
+        rows.append(dot(outs[expert][:, : 2 * half], wgu[expert][...], ((1,), (0,))))
+    gather(g_copies, g_all, 2 * half)
     scores = []
     for expert in range(2):
-        weight_copies[2 + expert].wait()
-        back = dot(gc[expert], wd[expert][...], ((1,), (1,)))
+        back = dot(outs[expert][:, 2 * half : 4 * half], wd[expert][...], ((1,), (1,)))
         gate, up = rows[expert][:, :part], rows[expert][:, part:]
         sig = jax.nn.sigmoid(gate)
         act = gate * sig
@@ -261,11 +270,9 @@
         scores.append(jnp.sum(hidden * back, axis=1, keepdims=True))
         prob = jnp.concatenate([probs[chunk, expert] for chunk in range(count)], 0)
         hgrad = prob * back
-        both[expert, :, :part] = (hgrad * up * sig * (1.0 + gate * (1.0 - sig))).astype(jnp.bfloat16)
-        both[expert, :, part:] = (hgrad * act).astype(jnp.bfloat16)
-        scaled[expert] = (prob * hidden).astype(jnp.bfloat16)
-    leave_rows(both, 4 * half)
-    leave_rows(scaled, 4 * half + 2 * part)
+        d_gate = (hgrad * up * sig * (1.0 + gate * (1.0 - sig))).astype(jnp.bfloat16)
+        outs[expert][:, both_at] = jnp.concatenate([d_gate, (hgrad * act).astype(jnp.bfloat16)], 1)
+        outs[expert][:, scaled_at] = (prob * hidden).astype(jnp.bfloat16)
 
     names = lax.broadcasted_iota(jnp.int32, (owners, half), 0)
     column = lax.broadcasted_iota(jnp.int32, (owners, half), 1) // (2 * tok)
@@ -279,10 +286,11 @@
                 line = jnp.concatenate([high, line - high] * (half // (2 * tok)), 1)
                 extra = extra + jnp.where((names == where_ref[expert]) & (column == where_ref[2]), line, 0.0)
             for side in range(2):
-                piece[chunk, side, y, tok:] = extra.astype(jnp.bfloat16)
+                number, slot = ways[chunk, y, side]
+                packets[number][slot, tok:] = extra.astype(jnp.bfloat16)
     for side in (1, 0):
         low = [
-            dot(both[expert], wgu[expert][sides[side], :], ((1,), (1,))).astype(jnp.bfloat16) for expert in range(2)
+            dot(outs[expert][:, both_at], wgu[expert][sides[side], :], ((1,), (1,))).astype(jnp.bfloat16) for expert in range(2)
         ]
         for chunk in range(count):
             total = None
@@ -290,11 +298,8 @@
                 term = dot(low_picks[chunk, expert], low[expert][chunk * slots : (chunk + 1) * slots], ((0,), (0,)))
                 total = term if total is None else total + term
             for y in range(2):
-                piece[chunk, side, y, :tok] = total[y * tok : (y + 1) * tok].astype(jnp.bfloat16)
                 number, slot = ways[chunk, y, side]
-                leave(piece.at[chunk, side, y], packets[number].at[slot])
-    for copy in leaving:
-        copy.wait()
+                packets[number][slot, :tok] = total[y * tok : (y + 1) * tok].astype(jnp.bfloat16)
 
 
 def rows_call(items, owners, capacity, slots, where, weights, units, tables, after):
@@ -309,30 +314,22 @@
         grid_spec=pltpu.PrefetchScalarGridSpec(
             num_scalar_prefetch=1,
             grid=(1,),
-            in_specs=[LOOSE] * (4 + 5 * count + len(after)),
-            out_specs=[LOOSE] * (2 + len(items)),
+            in_specs=[pl.BlockSpec(memory_space=pltpu.VMEM)] * 4 + [LOOSE] * (5 * count + len(after)),
+            out_specs=[pl.BlockSpec(memory_space=pltpu.VMEM)] * (2 + len(items)),
             scratch_shapes=[pltpu.VMEM((count, 2, 2 * tok, half), jnp.bfloat16)] * 2
             + [pltpu.VMEM((count, 2, owners, tok), jnp.bfloat16)]
-            + [pltpu.VMEM((width, 2 * part), jnp.bfloat16)] * 2
-            + [pltpu.VMEM((part, width), jnp.bfloat16)] * 2
-            + [pltpu.VMEM((2, count * slots, size), jnp.bfloat16) for size in widths]
-            + [
-                pltpu.VMEM((count, 2, 2) + packet, jnp.bfloat16),
-                pltpu.SemaphoreType.DMA((3, 4 * count)),
-                pltpu.SemaphoreType.DMA((4,)),
-                pltpu.SemaphoreType.DMA((8 + 4 * count,)),
-            ],
-        ),
-        out_shape=[jax.ShapeDtypeStruct((count * slots, sum(widths)), jnp.bfloat16)] * 2
-        + [jax.ShapeDtypeStruct((len(blocks),) + packet, jnp.bfloat16) for blocks in items],
-        compiler_params=pltpu.CompilerParams(vmem_limit_bytes=30 << 20),
+            + [pltpu.SemaphoreType.DMA((3, 4 * count))],
+        ),
+        out_shape=[pltpu.VMEM((count * slots, sum(widths)), jnp.bfloat16)] * 2
+        + [pltpu.VMEM((len(blocks),) + packet, jnp.bfloat16) for blocks in items],
+        compiler_params=pltpu.CompilerParams(vmem_limit_bytes=16 << 20),
         cost_estimate=pl.CostEstimate(
             flops=count * (20 * slots * width * part + 24 * slots * tok * width),
             bytes_accessed=count * 16 * tok * width + 12 * width * part,
             transcendentals=2 * count * slots * part,
         ),
         name="rows",
-    )(where, *weights, *units, *tables, *after)
+    )(where, *[pltpu.with_memory_space_constraint(item, pltpu.VMEM) for item in weights], *units, *tables, *after)
 
 
 def grads_kernel(count, wide, deep, blocks, tp_ref, *refs):
@@ -488,7 +485,7 @@
         four = [units[z, y, x] for z in steps for y in range(2) for x in range(2)]
         return rows_call(items, owners, capacity, slots, where, weights, four, [tables[z] for z in steps], after)
 
-    units = {(0, 0, 0): jnp.concatenate([tokens, out_grad], 0)}
+    units = {(0, 0, 0): join_call(tokens, out_grad)}
     settled = dict(units)
     for number, moves in enumerate(rounds):
         arrived = {target: move(settled[source]) for target, source, move in moves}
@@ -517,11 +514,11 @@
     def total(*blocks):
         return sum(block.astype(jnp.float32) for block in blocks).astype(jnp.bfloat16)
 
-    items = [[(1, 1, 1)], [(1, 0, 1), (0, 0, 1)], [(0, 1, 0)], [(0, 1, 1)], [(0, 0, 0)], [(1, 0, 0)], [(1, 1, 0)]]
-    mine_1, other_1, x_2, x_12, y_1, z_1, keep_1, keep_2, keep_2y = rows_of([1, 2], items, [])
-    other_1, x_2, x_12, y_1, z_1 = tied([other_1, x_2, x_12, y_1, z_1], arrived.values())
+    items = [[(1, 1, 1)], [(1, 0, 1)], [(0, 0, 1)], [(0, 1, 0)], [(0, 1, 1)], [(0, 0, 0)], [(1, 0, 0)], [(1, 1, 0)]]
+    mine_1, other_1, x_2, x_20, x_1, y_1, z_1, keep_1, keep_2, keep_2y = rows_of([1, 2], items, [])
+    other_1, x_2, x_20, x_1, y_1, z_1 = tied([other_1, x_2, x_20, x_1, y_1, z_1], arrived.values())
     from_x2, from_y1, from_z1 = over_x(x_2), over_y(y_1), over_z(z_1, -1)
-    from_x12 = over_x(x_12)
+    from_x20, from_x1 = over_x(x_20), over_x(x_1)
     items = [[(0, 0, 1)], [(0, 1, 0)], [(0, 1, 1)], [(0, 0, 0)]]
     mine_3, other_3, x_3, y_3, z_3, keep_3 = rows_of([3], items, [mine_1])
     mine_3, other_3, x_3, y_3, z_3, keep_2y = tied(
@@ -530,10 +527,10 @@
     from_z3, from_x3, from_y2, from_y3 = over_z(z_3, 1), over_x(x_3), over_y(total(keep_2y, from_x2)), over_y(y_3)
     packed = [mine_0, over_role(other_0), mine_1, over_role(other_1), mine_3, over_role(other_3)]
     d_gate, d_up = grads_call(which_ref, packed, width, part, False)
-    from_z3, from_x12, from_y2 = tied([from_z3, from_x12, from_y2], [d_gate, d_up])
+    from_z3, from_x20, from_x1, from_y2 = tied([from_z3, from_x20, from_x1, from_y2], [d_gate, d_up])
     from_far = over_y(total(far, from_z1, from_z3))
-    from_z2 = over_z(total(keep_2, from_x12[:1], from_y2), 1)
-    home_1 = over_z(total(keep_1, from_x12[1:], from_y1), -1)
+    from_z2 = over_z(total(keep_2, from_x20, from_y2), 1)
+    home_1 = over_z(total(keep_1, from_x1, from_y1), -1)
     (d_down,) = grads_call(which_ref, packed, width, part, True)
     from_x3, from_y3, from_z2, y_0 = tied([from_x3, from_y3, from_z2, y_0], [d_down])
     from_y0 = over_y(y_0)

time: 145 us -> 145 us (level)
  waiting for transfers between devices: 41.2 us -> 42.7 us
    concatenate x1 -> x0, local copies, waits for them, and re-layouts: 1.67 us -> none  [dense_device(): units = {(0, 0, 0): jnp.concatenate([tokens, out_grad], 0)}]
    ppermute x9 -> x10, waiting for transfers between devices: 4.22 us -> 4.8 us  [over_x(): return lax.ppermute(array, 'tp', [(0, 1), (1, 0)])]
    ppermute x9 -> x10, starting transfers between devices: 11.7 us -> 12.2 us  [over_x(): return lax.ppermute(array, 'tp', [(0, 1), (1, 0)])]
    unnamed x21 -> x24, local copies, waits for them, and re-layouts: 8.56 us -> 8.78 us
  transfers between devices with their start and end apart: 38 -> 39, of which waited for: 10 -> 11; matrix products, arithmetic and copies ran while one was open for 1% -> 1% of each run, Pallas kernels for 31% -> 31%
where the time goes in v12:
time: 145 us; the launch traced here: 144 us
  Pallas kernels  45.7 us (32%)
  starting transfers between devices  43.9 us (30%)
  waiting for transfers between devices  42.7 us (29%)
  local copies, waits for them, and re-layouts  8.8 us (6%)
  other arithmetic  2.44 us (2%)
    ppermute x13, waiting for transfers between devices, over_z(): lax.ppermute(array, 'ep', [(i, (i + shift * n_y) % ep) for i in range(ep)])  37.9 us
    pallas_call x3, Pallas kernels, rows_call(): pl.pallas_call(functools.partial(rows_kernel, count, ways, capacity, slot...  32.3 us
    ppermute x13, starting transfers between devices, over_z(): lax.ppermute(array, 'ep', [(i, (i + shift * n_y) % ep) for i in range(ep)])  19.3 us
    ppermute x10, starting transfers between devices, over_x(): return lax.ppermute(array, 'tp', [(0, 1), (1, 0)])  12.2 us
    ppermute x11, starting transfers between devices, over_y(): lax.ppermute(array, 'ep', [(i, i + 1 - 2 * (i % n_y)) for i in range(ep)])  11.5 us
    pallas_call x2, Pallas kernels, grads_call(): pl.pallas_call(functools.partial(grads_kernel, count, *starts, 2 * per),...  11.1 us
    unnamed x24, local copies, waits for them, and re-layouts  8.78 us
    ppermute x10, waiting for transfers between devices, over_x(): return lax.ppermute(array, 'tp', [(0, 1), (1, 0)])  4.8 us
  transfers between devices with their start and end apart: 39, of which 11 were waited for; matrix products, arithmetic and copies ran while one was open for 1% of the time, Pallas kernels for 31%

profile of v12, /device:TPU:0, one launch (start us, length us, event | category | flops | bytes accessed | tf_op | source)
XLA Modules:
  0.0 144.5 jit_solution(14423249043621203304)
XLA Ops:
  0.6 0.9 copy-done.3
  1.6 0.9 copy-done.4
  2.5 0.8 join.1.refs_4_
  3.3 3.1 %collective-permute-start = (bf16[256,1024]{1,0:T(8,128)(2,1)}, bf16[256,1024]{1,0:T(8,128)(2,1)}, u32[]{:S(2)}, u32[]{:S(2)}) collective-permute-start(bf16[256,1024]{1,0:T(8,128)(2,1)} %join.1.refs_4_), channel_id=1, source_target_pairs={{0,4},{2,6},{4,8},{6,10},{8,12},{10,14},{12,0},{14,2},{1,5},{3,7},... | collective-permute-start | bytes 1572872 | tf_op jit(solution)/shard_map/ppermute | solution.py:447
  6.4 1.5 %collective-permute-start.1 = (bf16[256,1024]{1,0:T(8,128)(2,1)}, bf16[256,1024]{1,0:T(8,128)(2,1)}, u32[]{:S(2)}, u32[]{:S(2)}) collective-permute-start(bf16[256,1024]{1,0:T(8,128)(2,1)} %join.1.refs_4_), channel_id=1, source_target_pairs={{0,2},{2,0},{4,6},{6,4},{8,10},{10,8},{12,14},{14,12},{1,3},{3,1},... | collective-permute-start | bytes 1572872 | tf_op jit(solution)/shard_map/ppermute | solution.py:444
  7.9 1.5 %collective-permute-start.2 = (bf16[256,1024]{1,0:T(8,128)(2,1)}, bf16[256,1024]{1,0:T(8,128)(2,1)}, u32[]{:S(2)}, u32[]{:S(2)}) collective-permute-start(bf16[256,1024]{1,0:T(8,128)(2,1)} %join.1.refs_4_), channel_id=1, source_target_pairs={{0,1},{1,0},{2,3},{3,2},{4,5},{5,4},{6,7},{7,6},{8,9},{9,8},{10,11... | collective-permute-start | bytes 1572872 | tf_op jit(solution)/shard_map/ppermute | solution.py:438
  9.4 1.4 copy-done
  10.8 1.4 copy-done.1
  12.3 1.4 copy-done.2
  13.7 1.5 %weights.1 = (bf16[2048,768]{1,0:T(8,128)(2,1)S(1)}, bf16[384,2048]{1,0:T(8,128)(2,1)}) custom-call(s32[1]{0:T(128)} %bitcast.2.tp_ref, bf16[1,2048,384]{2,1,0:T(8,128)(2,1)S(1)} %copy-done, bf16[1,2048,384]{2,1,0:T(8,128)(2,1)S(1)} %copy-done.1, bf16[1,384,2048]{2,1,0:T(8,128)(2,1)S(1)} %copy-done.2), custom_call_target="tpu_custom_call" | custom-call | bytes 9437184 | tf_op jit(solution)/shard_map/weights/pallas_call | solution.py:141
  15.1 5.6 %collective-permute-done.refs_4_ = bf16[256,1024]{1,0:T(8,128)(2,1)} collective-permute-done((bf16[256,1024]{1,0:T(8,128)(2,1)}, bf16[256,1024]{1,0:T(8,128)(2,1)}, u32[]{:S(2)}, u32[]{:S(2)}) %collective-permute-start) | collective-permute-done | bytes 524320 | tf_op jit(solution)/shard_map/ppermute | solution.py:447
  21.9 1.6 %collective-permute-start.7 = (bf16[256,1024]{1,0:T(8,128)(2,1)}, bf16[256,1024]{1,0:T(8,128)(2,1)}, u32[]{:S(2)}, u32[]{:S(2)}) collective-permute-start(bf16[256,1024]{1,0:T(8,128)(2,1)} %collective-permute-done.refs_4_), channel_id=1, source_target_pairs={{0,4},{2,6},{4,8},{6,10},{8,12},{10,14},{12,0},{14,2},{1,5},{3,7},... | collective-permute-start | bytes 1572872 | tf_op jit(solution)/shard_map/ppermute | solution.py:447
  24.0 1.5 %collective-permute-start.5 = (bf16[256,1024]{1,0:T(8,128)(2,1)}, bf16[256,1024]{1,0:T(8,128)(2,1)S(1)}, u32[]{:S(2)}, u32[]{:S(2)}) collective-permute-start(bf16[256,1024]{1,0:T(8,128)(2,1)} %collective-permute-done.1.refs_6_), channel_id=1, source_target_pairs={{0,1},{1,0},{2,3},{3,2},{4,5},{5,4},{6,7},{7,6},{8,9},{9,8},{10,11... | collective-permute-start | bytes 1572872 | tf_op jit(solution)/shard_map/ppermute | solution.py:438
  25.5 12.3 %collective-permute-done.7.refs_8_ = bf16[256,1024]{1,0:T(8,128)(2,1)} collective-permute-done((bf16[256,1024]{1,0:T(8,128)(2,1)}, bf16[256,1024]{1,0:T(8,128)(2,1)}, u32[]{:S(2)}, u32[]{:S(2)}) %collective-permute-start.7) | collective-permute-done | bytes 524320 | tf_op jit(solution)/shard_map/ppermute | solution.py:447
  37.8 0.9 collective-permute-start.6
  38.7 0.8 copy-done.8
  39.6 0.8 copy-done.5
  40.4 1.1 collective-permute-start.10
  41.5 1.5 %collective-permute-start.11 = (bf16[256,1024]{1,0:T(8,128)(2,1)}, bf16[256,1024]{1,0:T(8,128)(2,1)}, u32[]{:S(2)}, u32[]{:S(2)}) collective-permute-start(bf16[256,1024]{1,0:T(8,128)(2,1)} %collective-permute-done.7.refs_8_), channel_id=1, source_target_pairs={{0,1},{1,0},{2,3},{3,2},{4,5},{5,4},{6,7},{7,6},{8,9},{9,8},{10,11... | collective-permute-start | bytes 1572872 | tf_op jit(solution)/shard_map/ppermute | solution.py:438
  43.7 1.0 copy-done.6
  44.7 9.8 %rows.3 = (bf16[144,5248]{1,0:T(8,128)(2,1)S(1)}, bf16[144,5248]{1,0:T(8,128)(2,1)S(1)}, bf16[1,144,1024]{2,1,0:T(8,128)(2,1)S(1)}, bf16[1,144,1024]{2,1,0:T(8,1...) custom-call(s32[3]{0:T(128)S(1)} %pad_add_fusion.where_ref, ...), custom_call_target="tpu_custom_call" | custom-call | flops 3170893824 | bytes 13631488 | tf_op jit(solution)/shard_map/rows/pallas_call | solution.py:312
  54.5 0.9 collective-permute-done.9.refs_4_
  56.0 0.9 collective-permute-start.13
  57.8 3.5 %collective-permute-start.20 = (bf16[2,16,128]{2,1,0:T(8,128)(2,1)S(1)}, bf16[2,16,128]{2,1,0:T(8,128)(2,1)S(1)}, u32[]{:S(2)}, u32[]{:S(2)}) collective-permute-start(bf16[2,16,128]{2,1,0:T(8,128)(2,1)S(1)} %pad_maximum_fusion.refs_8_), channel_id=1, source_target_pairs={{0,8},{2,10},{4,12},{6,14},{8,0},{10,2},{12,4},{14,6},{1,9},{3,11}... | collective-permute-start | bytes 24584 | tf_op jit(solution)/shard_map/ppermute | solution.py:447
  61.4 7.4 %collective-permute-done.12.refs_7_ = bf16[256,1024]{1,0:T(8,128)(2,1)S(1)} collective-permute-done((bf16[256,1024]{1,0:T(8,128)(2,1)S(1)}, bf16[256,1024]{1,0:T(8,128)(2,1)S(1)}, u32[]{:S(2)}, u32[]{:S(2)}) %collective-permute-start.12) | collective-permute-done | bytes 524320 | tf_op jit(solution)/shard_map/ppermute | solution.py:447
  69.5 1.0 collective-permute-start.16
  70.5 3.4 %collective-permute-start.17 = (bf16[256,1024]{1,0:T(8,128)(2,1)S(1)}, bf16[256,1024]{1,0:T(8,128)(2,1)S(1)}, u32[]{:S(2)}, u32[]{:S(2)}) collective-permute-start(bf16[256,1024]{1,0:T(8,128)(2,1)S(1)} %copy-done.7), channel_id=1, source_target_pairs={{0,12},{2,14},{4,0},{6,2},{8,4},{10,6},{12,8},{14,10},{1,13},{3,15... | collective-permute-start | bytes 1572872 | tf_op jit(solution)/shard_map/ppermute | solution.py:447
  73.9 12.9 %rows.4 = (bf16[288,5248]{1,0:T(8,128)(2,1)S(1)}, bf16[288,5248]{1,0:T(8,128)(2,1)S(1)}, bf16[1,144,1024]{2,1,0:T(8,128)(2,1)S(1)}, bf16[1,144,1024]{2,1,0:T(8,1...) custom-call(s32[3]{0:T(128)S(1)} %pad_add_fusion.where_ref, ...), custom_call_target="tpu_custom_call" | custom-call | flops 6341787648 | bytes 17825792 | tf_op jit(solution)/shard_map/rows/pallas_call | solution.py:312
  86.9 0.7 collective-permute-start.18
  87.7 1.5 %collective-permute-start.21 = (bf16[1,144,1024]{2,1,0:T(8,128)(2,1)S(1)}, bf16[1,144,1024]{2,1,0:T(8,128)(2,1)S(1)}, u32[]{:S(2)}, u32[]{:S(2)}) collective-permute-start(bf16[1,144,1024]{2,1,0:T(8,128)(2,1)S(1)} %get-tuple-element.104), channel_id=1, source_target_pairs={{0,1},{1,0},{2,3},{3,2},{4,5},{5,4},{6,7},{7,6},{8,9},{9,8},{10,11... | collective-permute-start | bytes 884744 | tf_op jit(solution)/shard_map/ppermute | solution.py:438
  89.2 1.1 collective-permute-start.22
  90.6 2.4 %collective-permute-start.23 = (bf16[1,144,1024]{2,1,0:T(8,128)(2,1)S(1)}, bf16[1,144,1024]{2,1,0:T(8,128)(2,1)S(1)}, u32[]{:S(2)}, u32[]{:S(2)}) collective-permute-start(bf16[1,144,1024]{2,1,0:T(8,128)(2,1)S(1)} %get-tuple-element.106), channel_id=1, source_target_pairs={{0,12},{2,14},{4,0},{6,2},{8,4},{10,6},{12,8},{14,10},{1,13},{3,15... | collective-permute-start | bytes 884744 | tf_op jit(solution)/shard_map/ppermute | solution.py:447
  93.0 9.7 %rows.5 = (bf16[144,5248]{1,0:T(8,128)(2,1)S(1)}, bf16[144,5248]{1,0:T(8,128)(2,1)S(1)}, bf16[1,144,1024]{2,1,0:T(8,128)(2,1)S(1)}, bf16[1,144,1024]{2,1,0:T(8,1...) custom-call(s32[3]{0:T(128)S(1)} %pad_add_fusion.where_ref, ...), custom_call_target="tpu_custom_call" | custom-call | flops 3170893824 | bytes 13631488 | tf_op jit(solution)/shard_map/rows/pallas_call | solution.py:312
  102.8 1.6 %collective-permute-start.27 = (bf16[1,144,1024]{2,1,0:T(8,128)(2,1)S(1)}, bf16[1,144,1024]{2,1,0:T(8,128)(2,1)S(1)}, u32[]{:S(2)}, u32[]{:S(2)}) collective-permute-start(bf16[1,144,1024]{2,1,0:T(8,128)(2,1)S(1)} %get-tuple-element.111), channel_id=1, source_target_pairs={{0,1},{1,0},{2,3},{3,2},{4,5},{5,4},{6,7},{7,6},{8,9},{9,8},{10,11... | collective-permute-start | bytes 884744 | tf_op jit(solution)/shard_map/ppermute | solution.py:438
  105.0 1.2 collective-permute-start.29
  106.2 1.6 %collective-permute-start.24 = (bf16[1,144,1024]{2,1,0:T(8,128)(2,1)S(1)}, bf16[1,144,1024]{2,1,0:T(8,128)(2,1)S(1)}, u32[]{:S(2)}, u32[]{:S(2)}) collective-permute-start(bf16[1,144,1024]{2,1,0:T(8,128)(2,1)S(1)} %get-tuple-element.107), channel_id=1, source_target_pairs={{0,1},{1,0},{2,3},{3,2},{4,5},{5,4},{6,7},{7,6},{8,9},{9,8},{10,11... | collective-permute-start | bytes 884744 | tf_op jit(solution)/shard_map/ppermute | solution.py:438
  107.8 6.7 %grads.2 = (bf16[1,2048,384]{2,1,0:T(8,128)(2,1)}, bf16[1,2048,384]{2,1,0:T(8,128)(2,1)}) custom-call(s32[1]{0:T(128)} %bitcast.2.tp_ref, bf16[144,5248]{1,0:T(8,128)(2,1)S(1)} %get-tuple-element.84.refs_0_, bf16[144,5248]{1,0:T(8,128)(2,1)S(1)} %collective-permute-done.30.refs_1_, bf16[288,5248]{1,0:T(8,128)(2,1)S(1)} %get-tuple-element.91.refs_9_.refs_2_, ...), custom_call_target="tpu_custom_call" | custom-call | flops 3623878656 | bytes 6488064 | tf_op jit(solution)/shard_map/grads/pallas_call | solution.py:404
  114.5 1.1 collective-permute-start.25
  115.6 3.4 %collective-permute-done.28 = bf16[1,144,1024]{2,1,0:T(8,128)(2,1)S(1)} collective-permute-done((bf16[1,144,1024]{2,1,0:T(8,128)(2,1)S(1)}, bf16[1,144,1024]{2,1,0:T(8,128)(2,1)S(1)}, u32[]{:S(2)}, u32[]{:S(2)}) %collective-permute-start.28) | collective-permute-done | bytes 294944 | tf_op jit(solution)/shard_map/ppermute | solution.py:438
  119.8 1.7 %collective-permute-start.33 = (bf16[1,144,1024]{2,1,0:T(8,128)(2,1)S(1)}, bf16[1,144,1024]{2,1,0:T(8,128)(2,1)S(1)}, u32[]{:S(2)}, u32[]{:S(2)}) collective-permute-start(bf16[1,144,1024]{2,1,0:T(8,128)(2,1)S(1)} %add_convert_fusion.4), channel_id=1, source_target_pairs={{0,4},{2,6},{4,8},{6,10},{8,12},{10,14},{12,0},{14,2},{1,5},{3,7},... | collective-permute-start | bytes 884744 | tf_op jit(solution)/shard_map/ppermute | solution.py:447
  121.6 1.2 collective-permute-start.37
  122.8 4.4 %grads.3 = bf16[1,384,2048]{2,1,0:T(8,128)(2,1)} custom-call(s32[1]{0:T(128)} %bitcast.2.tp_ref, bf16[144,5248]{1,0:T(8,128)(2,1)S(1)} %get-tuple-element.84.refs_0_, bf16[144,5248]{1,0:T(8,128)(2,1)S(1)} %collective-permute-done.30.refs_1_, bf16[288,5248]{1,0:T(8,128)(2,1)S(1)} %get-tuple-element.91.refs_9_.refs_2_, ...), custom_call_target="tpu_custom_call" | custom-call | flops 1811939328 | bytes 5603328 | tf_op jit(solution)/shard_map/grads/pallas_call | solution.py:404
  127.2 6.0 %collective-permute-done.33 = bf16[1,144,1024]{2,1,0:T(8,128)(2,1)S(1)} collective-permute-done((bf16[1,144,1024]{2,1,0:T(8,128)(2,1)S(1)}, bf16[1,144,1024]{2,1,0:T(8,128)(2,1)S(1)}, u32[]{:S(2)}, u32[]{:S(2)}) %collective-permute-start.33) | collective-permute-done | bytes 294944 | tf_op jit(solution)/shard_map/ppermute | solution.py:447
  133.5 1.0 collective-permute-start.36
  134.4 1.0 collective-permute-start.34
  135.5 1.6 %collective-permute-start.38 = (bf16[1,144,1024]{2,1,0:T(8,128)(2,1)S(1)}, bf16[1,144,1024]{2,1,0:T(8,128)(2,1)S(1)}, u32[]{:S(2)}, u32[]{:S(2)}) collective-permute-start(bf16[1,144,1024]{2,1,0:T(8,128)(2,1)S(1)} %add_convert_fusion), channel_id=1, source_target_pairs={{0,1},{1,0},{2,3},{3,2},{4,5},{5,4},{6,7},{7,6},{8,9},{9,8},{10,11... | collective-permute-start | bytes 884744 | tf_op jit(solution)/shard_map/ppermute | solution.py:438
  137.0 5.4 %collective-permute-done.36 = bf16[1,144,1024]{2,1,0:T(8,128)(2,1)S(1)} collective-permute-done((bf16[1,144,1024]{2,1,0:T(8,128)(2,1)S(1)}, bf16[1,144,1024]{2,1,0:T(8,128)(2,1)S(1)}, u32[]{:S(2)}, u32[]{:S(2)}) %collective-permute-start.36) | collective-permute-done | bytes 294944 | tf_op jit(solution)/shard_map/ppermute | solution.py:447
  143.5 0.9 fusion
  (77 shorter events, 8.1 us)
Async XLA Ops:
  0.6 1.0 copy-start.3
  3.3 17.3 %collective-permute-start = (bf16[256,1024]{1,0:T(8,128)(2,1)}, bf16[256,1024]{1,0:T(8,128)(2,1)}, u32[]{:S(2)}, u32[]{:S(2)}) collective-permute-start(bf16[256,1024]{1,0:T(8,128)(2,1)} %join.1.refs_4_), channel_id=1, source_target_pairs={{0,4},{2,6},{4,8},{6,10},{8,12},{10,14},{12,0},{14,2},{1,5},{3,7},... | collective-permute-start | bytes 1572872 | tf_op jit(solution)/shard_map/ppermute | solution.py:447
  6.4 14.3 %collective-permute-start.1 = (bf16[256,1024]{1,0:T(8,128)(2,1)}, bf16[256,1024]{1,0:T(8,128)(2,1)}, u32[]{:S(2)}, u32[]{:S(2)}) collective-permute-start(bf16[256,1024]{1,0:T(8,128)(2,1)} %join.1.refs_4_), channel_id=1, source_target_pairs={{0,2},{2,0},{4,6},{6,4},{8,10},{10,8},{12,14},{14,12},{1,3},{3,1},... | collective-permute-start | bytes 1572872 | tf_op jit(solution)/shard_map/ppermute | solution.py:444
  7.9 13.4 %collective-permute-start.2 = (bf16[256,1024]{1,0:T(8,128)(2,1)}, bf16[256,1024]{1,0:T(8,128)(2,1)}, u32[]{:S(2)}, u32[]{:S(2)}) collective-permute-start(bf16[256,1024]{1,0:T(8,128)(2,1)} %join.1.refs_4_), channel_id=1, source_target_pairs={{0,1},{1,0},{2,3},{3,2},{4,5},{5,4},{6,7},{7,6},{8,9},{9,8},{10,11... | collective-permute-start | bytes 1572872 | tf_op jit(solution)/shard_map/ppermute | solution.py:438
  9.4 1.4 copy-start
  10.8 1.4 copy-start.1
  12.2 1.4 copy-start.2
  13.7 11.8 %copy-start.11 = (bf16[128,8]{0,1:T(8,128)(2,1)S(1)}, bf16[128,8]{0,1:T(8,128)(2,1)}, u32[]{:S(2)}) copy-start(bf16[128,8]{0,1:T(8,128)(2,1)} %param.10) | copy-start | bytes 6148
  13.7 11.8 %copy-start.10 = (s32[128,8]{0,1:T(8,128)S(1)}, s32[128,8]{0,1:T(8,128)}, u32[]{:S(2)}) copy-start(s32[128,8]{0,1:T(8,128)} %param.9) | copy-start | bytes 12292
  21.4 22.3 %collective-permute-start.3 = (bf16[2048,768]{1,0:T(8,128)(2,1)S(1)}, bf16[2048,768]{1,0:T(8,128)(2,1)}, u32[]{:S(2)}, u32[]{:S(2)}) collective-permute-start(bf16[2048,768]{1,0:T(8,128)(2,1)S(1)} %get-tuple-element.71.refs_0_), channel_id=1, source_target_pairs={{0,16},{16,0},{1,17},{17,1},{2,18},{18,2},{3,19},{19,3},{4,20},{20... | collective-permute-start | bytes 9437192 | tf_op jit(solution)/shard_map/ppermute | solution.py:441
  21.4 22.3 %collective-permute-start.4 = (bf16[384,2048]{1,0:T(8,128)(2,1)}, bf16[384,2048]{1,0:T(8,128)(2,1)}, u32[]{:S(2)}, u32[]{:S(2)}) collective-permute-start(bf16[384,2048]{1,0:T(8,128)(2,1)} %get-tuple-element.72.refs_2_), channel_id=1, source_target_pairs={{0,16},{16,0},{1,17},{17,1},{2,18},{18,2},{3,19},{19,3},{4,20},{20... | collective-permute-start | bytes 4718600 | tf_op jit(solution)/shard_map/ppermute | solution.py:441
  21.9 15.9 %collective-permute-start.7 = (bf16[256,1024]{1,0:T(8,128)(2,1)}, bf16[256,1024]{1,0:T(8,128)(2,1)}, u32[]{:S(2)}, u32[]{:S(2)}) collective-permute-start(bf16[256,1024]{1,0:T(8,128)(2,1)} %collective-permute-done.refs_4_), channel_id=1, source_target_pairs={{0,4},{2,6},{4,8},{6,10},{8,12},{10,14},{12,0},{14,2},{1,5},{3,7},... | collective-permute-start | bytes 1572872 | tf_op jit(solution)/shard_map/ppermute | solution.py:447
  23.4 15.3 %collective-permute-start.8 = (bf16[256,1024]{1,0:T(8,128)(2,1)}, bf16[256,1024]{1,0:T(8,128)(2,1)S(1)}, u32[]{:S(2)}, u32[]{:S(2)}) collective-permute-start(bf16[256,1024]{1,0:T(8,128)(2,1)} %collective-permute-done.refs_4_), channel_id=1, source_target_pairs={{0,2},{2,0},{4,6},{6,4},{8,10},{10,8},{12,14},{14,12},{1,3},{3,1},... | collective-permute-start | bytes 1572872 | tf_op jit(solution)/shard_map/ppermute | solution.py:444
  24.0 15.6 %collective-permute-start.5 = (bf16[256,1024]{1,0:T(8,128)(2,1)}, bf16[256,1024]{1,0:T(8,128)(2,1)S(1)}, u32[]{:S(2)}, u32[]{:S(2)}) collective-permute-start(bf16[256,1024]{1,0:T(8,128)(2,1)} %collective-permute-done.1.refs_6_), channel_id=1, source_target_pairs={{0,1},{1,0},{2,3},{3,2},{4,5},{5,4},{6,7},{7,6},{8,9},{9,8},{10,11... | collective-permute-start | bytes 1572872 | tf_op jit(solution)/shard_map/ppermute | solution.py:438
  37.8 5.1 %collective-permute-start.6 = (bf16[16,128]{1,0:T(8,128)(2,1)S(1)}, bf16[16,128]{1,0:T(8,128)(2,1)S(1)}, u32[]{:S(2)}, u32[]{:S(2)}) collective-permute-start(bf16[16,128]{1,0:T(8,128)(2,1)S(1)} %get-tuple-element.134), channel_id=1, source_target_pairs={{0,2},{2,0},{4,6},{6,4},{8,10},{10,8},{12,14},{14,12},{1,3},{3,1},... | collective-permute-start | bytes 12296 | tf_op jit(solution)/shard_map/ppermute | solution.py:444
  40.4 14.1 %collective-permute-start.10 = (bf16[256,1024]{1,0:T(8,128)(2,1)}, bf16[256,1024]{1,0:T(8,128)(2,1)}, u32[]{:S(2)}, u32[]{:S(2)}) collective-permute-start(bf16[256,1024]{1,0:T(8,128)(2,1)} %collective-permute-done.7.refs_8_), channel_id=1, source_target_pairs={{0,2},{2,0},{4,6},{6,4},{8,10},{10,8},{12,14},{14,12},{1,3},{3,1},... | collective-permute-start | bytes 1572872 | tf_op jit(solution)/shard_map/ppermute | solution.py:444
  41.5 13.0 %collective-permute-start.11 = (bf16[256,1024]{1,0:T(8,128)(2,1)}, bf16[256,1024]{1,0:T(8,128)(2,1)}, u32[]{:S(2)}, u32[]{:S(2)}) collective-permute-start(bf16[256,1024]{1,0:T(8,128)(2,1)} %collective-permute-done.7.refs_8_), channel_id=1, source_target_pairs={{0,1},{1,0},{2,3},{3,2},{4,5},{5,4},{6,7},{7,6},{8,9},{9,8},{10,11... | collective-permute-start | bytes 1572872 | tf_op jit(solution)/shard_map/ppermute | solution.py:438
  43.0 12.5 %collective-permute-start.9 = (bf16[256,1024]{1,0:T(8,128)(2,1)}, bf16[256,1024]{1,0:T(8,128)(2,1)}, u32[]{:S(2)}, u32[]{:S(2)}) collective-permute-start(bf16[256,1024]{1,0:T(8,128)(2,1)} %join.1.refs_4_), channel_id=1, source_target_pairs={{0,12},{2,14},{4,0},{6,2},{8,4},{10,6},{12,8},{14,10},{1,13},{3,15... | collective-permute-start | bytes 1572872 | tf_op jit(solution)/shard_map/ppermute | solution.py:447
  43.6 1.0 copy-start.6
  44.7 25.9 %copy-start.7 = (bf16[256,1024]{1,0:T(8,128)(2,1)S(1)}, bf16[256,1024]{1,0:T(8,128)(2,1)}, u32[]{:S(2)}) copy-start(bf16[256,1024]{1,0:T(8,128)(2,1)} %copy-done.5) | copy-start | bytes 1572868
  44.7 29.2 %copy-start.9 = (bf16[256,1024]{1,0:T(8,128)(2,1)S(1)}, bf16[256,1024]{1,0:T(8,128)(2,1)}, u32[]{:S(2)}) copy-start(bf16[256,1024]{1,0:T(8,128)(2,1)} %copy-done.8) | copy-start | bytes 1572868
  55.4 13.3 %collective-permute-start.12 = (bf16[256,1024]{1,0:T(8,128)(2,1)S(1)}, bf16[256,1024]{1,0:T(8,128)(2,1)S(1)}, u32[]{:S(2)}, u32[]{:S(2)}) collective-permute-start(bf16[256,1024]{1,0:T(8,128)(2,1)S(1)} %copy-done.6), channel_id=1, source_target_pairs={{0,4},{2,6},{4,8},{6,10},{8,12},{10,14},{12,0},{14,2},{1,5},{3,7},... | collective-permute-start | bytes 1572872 | tf_op jit(solution)/shard_map/ppermute | solution.py:447
  56.0 12.7 %collective-permute-start.13 = (bf16[256,1024]{1,0:T(8,128)(2,1)}, bf16[256,1024]{1,0:T(8,128)(2,1)S(1)}, u32[]{:S(2)}, u32[]{:S(2)}) collective-permute-start(bf16[256,1024]{1,0:T(8,128)(2,1)} %collective-permute-done.11.refs_9_), channel_id=1, source_target_pairs={{0,2},{2,0},{4,6},{6,4},{8,10},{10,8},{12,14},{14,12},{1,3},{3,1},... | collective-permute-start | bytes 1572872 | tf_op jit(solution)/shard_map/ppermute | solution.py:444
  56.9 12.1 %collective-permute-start.14 = (bf16[256,1024]{1,0:T(8,128)(2,1)}, bf16[256,1024]{1,0:T(8,128)(2,1)S(1)}, u32[]{:S(2)}, u32[]{:S(2)}) collective-permute-start(bf16[256,1024]{1,0:T(8,128)(2,1)} %collective-permute-done.refs_4_), channel_id=1, source_target_pairs={{0,1},{1,0},{2,3},{3,2},{4,5},{5,4},{6,7},{7,6},{8,9},{9,8},{10,11... | collective-permute-start | bytes 1572872 | tf_op jit(solution)/shard_map/ppermute | solution.py:438
  57.4 16.5 %collective-permute-start.19 = (bf16[2,16,128]{2,1,0:T(8,128)(2,1)S(1)}, bf16[2,16,128]{2,1,0:T(8,128)(2,1)S(1)}, u32[]{:S(2)}, u32[]{:S(2)}) collective-permute-start(bf16[2,16,128]{2,1,0:T(8,128)(2,1)S(1)} %pad_maximum_fusion.refs_8_), channel_id=1, source_target_pairs={{0,4},{2,6},{4,8},{6,10},{8,12},{10,14},{12,0},{14,2},{1,5},{3,7},... | collective-permute-start | bytes 24584 | tf_op jit(solution)/shard_map/ppermute | solution.py:447
  57.8 16.1 %collective-permute-start.20 = (bf16[2,16,128]{2,1,0:T(8,128)(2,1)S(1)}, bf16[2,16,128]{2,1,0:T(8,128)(2,1)S(1)}, u32[]{:S(2)}, u32[]{:S(2)}) collective-permute-start(bf16[2,16,128]{2,1,0:T(8,128)(2,1)S(1)} %pad_maximum_fusion.refs_8_), channel_id=1, source_target_pairs={{0,8},{2,10},{4,12},{6,14},{8,0},{10,2},{12,4},{14,6},{1,9},{3,11}... | collective-permute-start | bytes 24584 | tf_op jit(solution)/shard_map/ppermute | solution.py:447
  69.0 17.8 %collective-permute-start.15 = (bf16[256,1024]{1,0:T(8,128)(2,1)}, bf16[256,1024]{1,0:T(8,128)(2,1)S(1)}, u32[]{:S(2)}, u32[]{:S(2)}) collective-permute-start(bf16[256,1024]{1,0:T(8,128)(2,1)} %collective-permute-done.9.refs_4_), channel_id=1, source_target_pairs={{0,1},{1,0},{2,3},{3,2},{4,5},{5,4},{6,7},{7,6},{8,9},{9,8},{10,11... | collective-permute-start | bytes 1572872 | tf_op jit(solution)/shard_map/ppermute | solution.py:438
  69.5 17.3 %collective-permute-start.16 = (bf16[256,1024]{1,0:T(8,128)(2,1)}, bf16[256,1024]{1,0:T(8,128)(2,1)S(1)}, u32[]{:S(2)}, u32[]{:S(2)}) collective-permute-start(bf16[256,1024]{1,0:T(8,128)(2,1)} %collective-permute-done.9.refs_4_), channel_id=1, source_target_pairs={{0,2},{2,0},{4,6},{6,4},{8,10},{10,8},{12,14},{14,12},{1,3},{3,1},... | collective-permute-start | bytes 1572872 | tf_op jit(solution)/shard_map/ppermute | solution.py:444
  70.5 16.3 %collective-permute-start.17 = (bf16[256,1024]{1,0:T(8,128)(2,1)S(1)}, bf16[256,1024]{1,0:T(8,128)(2,1)S(1)}, u32[]{:S(2)}, u32[]{:S(2)}) collective-permute-start(bf16[256,1024]{1,0:T(8,128)(2,1)S(1)} %copy-done.7), channel_id=1, source_target_pairs={{0,12},{2,14},{4,0},{6,2},{8,4},{10,6},{12,8},{14,10},{1,13},{3,15... | collective-permute-start | bytes 1572872 | tf_op jit(solution)/shard_map/ppermute | solution.py:447
  86.8 19.4 %collective-permute-start.31 = (bf16[288,5248]{1,0:T(8,128)(2,1)S(1)}, bf16[288,5248]{1,0:T(8,128)(2,1)S(1)}, u32[]{:S(2)}, u32[]{:S(2)}) collective-permute-start(bf16[288,5248]{1,0:T(8,128)(2,1)S(1)} %get-tuple-element.115), channel_id=1, source_target_pairs={{0,16},{16,0},{1,17},{17,1},{2,18},{18,2},{3,19},{19,3},{4,20},{20... | collective-permute-start | bytes 9068552 | tf_op jit(solution)/shard_map/ppermute | solution.py:441
  86.9 3.7 %collective-permute-start.18 = (bf16[2,16,128]{2,1,0:T(8,128)(2,1)S(1)}, bf16[2,16,128]{2,1,0:T(8,128)(2,1)S(1)}, u32[]{:S(2)}, u32[]{:S(2)}) collective-permute-start(bf16[2,16,128]{2,1,0:T(8,128)(2,1)S(1)} %pad_maximum_fusion.refs_8_), channel_id=1, source_target_pairs={{0,12},{2,14},{4,0},{6,2},{8,4},{10,6},{12,8},{14,10},{1,13},{3,15... | collective-permute-start | bytes 24584 | tf_op jit(solution)/shard_map/ppermute | solution.py:447
  87.6 17.4 %collective-permute-start.30 = (bf16[144,5248]{1,0:T(8,128)(2,1)S(1)}, bf16[144,5248]{1,0:T(8,128)(2,1)S(1)}, u32[]{:S(2)}, u32[]{:S(2)}) collective-permute-start(bf16[144,5248]{1,0:T(8,128)(2,1)S(1)} %get-tuple-element.114), channel_id=1, source_target_pairs={{0,16},{16,0},{1,17},{17,1},{2,18},{18,2},{3,19},{19,3},{4,20},{20... | collective-permute-start | bytes 4534280 | tf_op jit(solution)/shard_map/ppermute | solution.py:441
  87.7 15.0 %collective-permute-start.21 = (bf16[1,144,1024]{2,1,0:T(8,128)(2,1)S(1)}, bf16[1,144,1024]{2,1,0:T(8,128)(2,1)S(1)}, u32[]{:S(2)}, u32[]{:S(2)}) collective-permute-start(bf16[1,144,1024]{2,1,0:T(8,128)(2,1)S(1)} %get-tuple-element.104), channel_id=1, source_target_pairs={{0,1},{1,0},{2,3},{3,2},{4,5},{5,4},{6,7},{7,6},{8,9},{9,8},{10,11... | collective-permute-start | bytes 884744 | tf_op jit(solution)/shard_map/ppermute | solution.py:438
  89.2 13.5 %collective-permute-start.22 = (bf16[1,144,1024]{2,1,0:T(8,128)(2,1)S(1)}, bf16[1,144,1024]{2,1,0:T(8,128)(2,1)S(1)}, u32[]{:S(2)}, u32[]{:S(2)}) collective-permute-start(bf16[1,144,1024]{2,1,0:T(8,128)(2,1)S(1)} %get-tuple-element.105), channel_id=1, source_target_pairs={{0,2},{2,0},{4,6},{6,4},{8,10},{10,8},{12,14},{14,12},{1,3},{3,1},... | collective-permute-start | bytes 884744 | tf_op jit(solution)/shard_map/ppermute | solution.py:444
  90.6 12.1 %collective-permute-start.23 = (bf16[1,144,1024]{2,1,0:T(8,128)(2,1)S(1)}, bf16[1,144,1024]{2,1,0:T(8,128)(2,1)S(1)}, u32[]{:S(2)}, u32[]{:S(2)}) collective-permute-start(bf16[1,144,1024]{2,1,0:T(8,128)(2,1)S(1)} %get-tuple-element.106), channel_id=1, source_target_pairs={{0,12},{2,14},{4,0},{6,2},{8,4},{10,6},{12,8},{14,10},{1,13},{3,15... | collective-permute-start | bytes 884744 | tf_op jit(solution)/shard_map/ppermute | solution.py:447
  102.8 3.5 %collective-permute-start.32 = (bf16[144,5248]{1,0:T(8,128)(2,1)S(1)}, bf16[144,5248]{1,0:T(8,128)(2,1)S(1)}, u32[]{:S(2)}, u32[]{:S(2)}) collective-permute-start(bf16[144,5248]{1,0:T(8,128)(2,1)S(1)} %get-tuple-element.117), channel_id=1, source_target_pairs={{0,16},{16,0},{1,17},{17,1},{2,18},{18,2},{3,19},{19,3},{4,20},{20... | collective-permute-start | bytes 4534280 | tf_op jit(solution)/shard_map/ppermute | solution.py:441
  102.8 11.7 %collective-permute-start.27 = (bf16[1,144,1024]{2,1,0:T(8,128)(2,1)S(1)}, bf16[1,144,1024]{2,1,0:T(8,128)(2,1)S(1)}, u32[]{:S(2)}, u32[]{:S(2)}) collective-permute-start(bf16[1,144,1024]{2,1,0:T(8,128)(2,1)S(1)} %get-tuple-element.111), channel_id=1, source_target_pairs={{0,1},{1,0},{2,3},{3,2},{4,5},{5,4},{6,7},{7,6},{8,9},{9,8},{10,11... | collective-permute-start | bytes 884744 | tf_op jit(solution)/shard_map/ppermute | solution.py:438
  104.4 14.6 %collective-permute-start.28 = (bf16[1,144,1024]{2,1,0:T(8,128)(2,1)S(1)}, bf16[1,144,1024]{2,1,0:T(8,128)(2,1)S(1)}, u32[]{:S(2)}, u32[]{:S(2)}) collective-permute-start(bf16[1,144,1024]{2,1,0:T(8,128)(2,1)S(1)} %get-tuple-element.112), channel_id=1, source_target_pairs={{0,1},{1,0},{2,3},{3,2},{4,5},{5,4},{6,7},{7,6},{8,9},{9,8},{10,11... | collective-permute-start | bytes 884744 | tf_op jit(solution)/shard_map/ppermute | solution.py:438
  105.0 14.0 %collective-permute-start.29 = (bf16[1,144,1024]{2,1,0:T(8,128)(2,1)S(1)}, bf16[1,144,1024]{2,1,0:T(8,128)(2,1)S(1)}, u32[]{:S(2)}, u32[]{:S(2)}) collective-permute-start(bf16[1,144,1024]{2,1,0:T(8,128)(2,1)S(1)} %add_convert_fusion.5), channel_id=1, source_target_pairs={{0,2},{2,0},{4,6},{6,4},{8,10},{10,8},{12,14},{14,12},{1,3},{3,1},... | collective-permute-start | bytes 884744 | tf_op jit(solution)/shard_map/ppermute | solution.py:444
  106.2 12.8 %collective-permute-start.26 = (bf16[1,144,1024]{2,1,0:T(8,128)(2,1)S(1)}, bf16[1,144,1024]{2,1,0:T(8,128)(2,1)S(1)}, u32[]{:S(2)}, u32[]{:S(2)}) collective-permute-start(bf16[1,144,1024]{2,1,0:T(8,128)(2,1)S(1)} %get-tuple-element.110), channel_id=1, source_target_pairs={{0,4},{2,6},{4,8},{6,10},{8,12},{10,14},{12,0},{14,2},{1,5},{3,7},... | collective-permute-start | bytes 884744 | tf_op jit(solution)/shard_map/ppermute | solution.py:447
  106.2 21.0 %collective-permute-start.24 = (bf16[1,144,1024]{2,1,0:T(8,128)(2,1)S(1)}, bf16[1,144,1024]{2,1,0:T(8,128)(2,1)S(1)}, u32[]{:S(2)}, u32[]{:S(2)}) collective-permute-start(bf16[1,144,1024]{2,1,0:T(8,128)(2,1)S(1)} %get-tuple-element.107), channel_id=1, source_target_pairs={{0,1},{1,0},{2,3},{3,2},{4,5},{5,4},{6,7},{7,6},{8,9},{9,8},{10,11... | collective-permute-start | bytes 884744 | tf_op jit(solution)/shard_map/ppermute | solution.py:438
  114.5 12.7 %collective-permute-start.25 = (bf16[1,144,1024]{2,1,0:T(8,128)(2,1)S(1)}, bf16[1,144,1024]{2,1,0:T(8,128)(2,1)S(1)}, u32[]{:S(2)}, u32[]{:S(2)}) collective-permute-start(bf16[1,144,1024]{2,1,0:T(8,128)(2,1)S(1)} %get-tuple-element.108), channel_id=1, source_target_pairs={{0,2},{2,0},{4,6},{6,4},{8,10},{10,8},{12,14},{14,12},{1,3},{3,1},... | collective-permute-start | bytes 884744 | tf_op jit(solution)/shard_map/ppermute | solution.py:444
  119.2 17.9 %collective-permute-start.35 = (bf16[1,144,1024]{2,1,0:T(8,128)(2,1)S(1)}, bf16[1,144,1024]{2,1,0:T(8,128)(2,1)S(1)}, u32[]{:S(2)}, u32[]{:S(2)}) collective-permute-start(bf16[1,144,1024]{2,1,0:T(8,128)(2,1)S(1)} %add_convert_fusion.3), channel_id=1, source_target_pairs={{0,12},{2,14},{4,0},{6,2},{8,4},{10,6},{12,8},{14,10},{1,13},{3,15... | collective-permute-start | bytes 884744 | tf_op jit(solution)/shard_map/ppermute | solution.py:447
  119.8 13.5 %collective-permute-start.33 = (bf16[1,144,1024]{2,1,0:T(8,128)(2,1)S(1)}, bf16[1,144,1024]{2,1,0:T(8,128)(2,1)S(1)}, u32[]{:S(2)}, u32[]{:S(2)}) collective-permute-start(bf16[1,144,1024]{2,1,0:T(8,128)(2,1)S(1)} %add_convert_fusion.4), channel_id=1, source_target_pairs={{0,4},{2,6},{4,8},{6,10},{8,12},{10,14},{12,0},{14,2},{1,5},{3,7},... | collective-permute-start | bytes 884744 | tf_op jit(solution)/shard_map/ppermute | solution.py:447
  121.6 13.8 %collective-permute-start.37 = (bf16[1,144,1024]{2,1,0:T(8,128)(2,1)S(1)}, bf16[1,144,1024]{2,1,0:T(8,128)(2,1)S(1)}, u32[]{:S(2)}, u32[]{:S(2)}) collective-permute-start(bf16[1,144,1024]{2,1,0:T(8,128)(2,1)S(1)} %add_convert_fusion.1), channel_id=1, source_target_pairs={{0,2},{2,0},{4,6},{6,4},{8,10},{10,8},{12,14},{14,12},{1,3},{3,1},... | collective-permute-start | bytes 884744 | tf_op jit(solution)/shard_map/ppermute | solution.py:444
  133.5 9.0 %collective-permute-start.36 = (bf16[1,144,1024]{2,1,0:T(8,128)(2,1)S(1)}, bf16[1,144,1024]{2,1,0:T(8,128)(2,1)S(1)}, u32[]{:S(2)}, u32[]{:S(2)}) collective-permute-start(bf16[1,144,1024]{2,1,0:T(8,128)(2,1)S(1)} %add_convert_fusion.2), channel_id=1, source_target_pairs={{0,4},{2,6},{4,8},{6,10},{8,12},{10,14},{12,0},{14,2},{1,5},{3,7},... | collective-permute-start | bytes 884744 | tf_op jit(solution)/shard_map/ppermute | solution.py:447
  134.4 8.0 %collective-permute-start.34 = (bf16[1,144,1024]{2,1,0:T(8,128)(2,1)S(1)}, bf16[1,144,1024]{2,1,0:T(8,128)(2,1)S(1)}, u32[]{:S(2)}, u32[]{:S(2)}) collective-permute-start(bf16[1,144,1024]{2,1,0:T(8,128)(2,1)S(1)} %get-tuple-element.123), channel_id=1, source_target_pairs={{0,2},{2,0},{4,6},{6,4},{8,10},{10,8},{12,14},{14,12},{1,3},{3,1},... | collective-permute-start | bytes 884744 | tf_op jit(solution)/shard_map/ppermute | solution.py:444
  135.5 7.4 %collective-permute-start.38 = (bf16[1,144,1024]{2,1,0:T(8,128)(2,1)S(1)}, bf16[1,144,1024]{2,1,0:T(8,128)(2,1)S(1)}, u32[]{:S(2)}, u32[]{:S(2)}) collective-permute-start(bf16[1,144,1024]{2,1,0:T(8,128)(2,1)S(1)} %add_convert_fusion), channel_id=1, source_target_pairs={{0,1},{1,0},{2,3},{3,2},{4,5},{5,4},{6,7},{7,6},{8,9},{9,8},{10,11... | collective-permute-start | bytes 884744 | tf_op jit(solution)/shard_map/ppermute | solution.py:438
  (3 other events, 2.6 us)

commit v13 on v12

--- a/solution.py
+++ b/solution.py
@@ -157,10 +157,10 @@
             jax.ShapeDtypeStruct((width, 2 * part), jnp.bfloat16),
             jax.ShapeDtypeStruct((part, width), jnp.bfloat16),
         ],
-        compiler_params=pltpu.CompilerParams(vmem_limit_bytes=16 << 20),
+        compiler_params=pltpu.CompilerParams(vmem_limit_bytes=12 << 20),
         cost_estimate=pl.CostEstimate(flops=0, bytes_accessed=12 * width * part, transcendentals=0),
         name="weights",
-    )(which, w_gate, w_up, w_down)
+    )(which, *[pltpu.with_memory_space_constraint(item, pltpu.HBM) for item in (w_gate, w_up, w_down)])
 
 
 def join_kernel(top_ref, bottom_ref, out_ref, sems):
@@ -186,7 +186,7 @@
         compiler_params=pltpu.CompilerParams(vmem_limit_bytes=8 << 20),
         cost_estimate=pl.CostEstimate(flops=0, bytes_accessed=8 * rows * columns, transcendentals=0),
         name="join",
-    )(top, bottom)
+    )(*[pltpu.with_memory_space_constraint(item, pltpu.HBM) for item in (top, bottom)])
 
 
 def rows_kernel(count, ways, capacity, slots, where_ref, *refs):
@@ -322,7 +322,7 @@
         ),
         out_shape=[pltpu.VMEM((count * slots, sum(widths)), jnp.bfloat16)] * 2
         + [pltpu.VMEM((len(blocks),) + packet, jnp.bfloat16) for blocks in items],
-        compiler_params=pltpu.CompilerParams(vmem_limit_bytes=16 << 20),
+        compiler_params=pltpu.CompilerParams(vmem_limit_bytes=14 << 20),
         cost_estimate=pl.CostEstimate(
             flops=count * (20 * slots * width * part + 24 * slots * tok * width),
             bytes_accessed=count * 16 * tok * width + 12 * width * part,
@@ -416,7 +416,7 @@
             ],
         ),
         out_shape=[jax.ShapeDtypeStruct(shape, jnp.bfloat16) for shape in shapes],
-        compiler_params=pltpu.CompilerParams(vmem_limit_bytes=20 << 20),
+        compiler_params=pltpu.CompilerParams(vmem_limit_bytes=14 << 20),
         cost_estimate=pl.CostEstimate(
             flops=2 * rows * width * deep, bytes_accessed=2 * rows * (width + deep), transcendentals=0
         ),
@@ -527,12 +527,12 @@
     from_z3, from_x3, from_y2, from_y3 = over_z(z_3, 1), over_x(x_3), over_y(total(keep_2y, from_x2)), over_y(y_3)
     packed = [mine_0, over_role(other_0), mine_1, over_role(other_1), mine_3, over_role(other_3)]
     d_gate, d_up = grads_call(which_ref, packed, width, part, False)
-    from_z3, from_x20, from_x1, from_y2 = tied([from_z3, from_x20, from_x1, from_y2], [d_gate, d_up])
+    from_z3, from_x20, from_y2 = tied([from_z3, from_x20, from_y2], [d_gate, d_up])
     from_far = over_y(total(far, from_z1, from_z3))
     from_z2 = over_z(total(keep_2, from_x20, from_y2), 1)
+    (d_down,) = grads_call(which_ref, packed, width, part, True)
+    from_x1, from_x3, from_y3, from_z2, y_0 = tied([from_x1, from_x3, from_y3, from_z2, y_0], [d_down, from_far])
     home_1 = over_z(total(keep_1, from_x1, from_y1), -1)
-    (d_down,) = grads_call(which_ref, packed, width, part, True)
-    from_x3, from_y3, from_z2, y_0 = tied([from_x3, from_y3, from_z2, y_0], [d_down])
     from_y0 = over_y(y_0)
     home_3 = over_z(total(keep_3, from_x3, from_y3, from_z2), 1)
     from_x0 = over_x(total(side_0, from_far))

time: 145 us -> 161 us (1.11)
  Pallas kernels: 45.7 us -> 63.9 us
  local copies, waits for them, and re-layouts: 8.8 us -> 2.69 us
  waiting for transfers between devices: 42.7 us -> 48.4 us
    pallas_call x1, Pallas kernels: 0.8 us -> 17 us  [join_call(): pl.pallas_call(join_kernel, in_specs=[LOOSE] * 2, out_specs=LOOSE, out_sh...]
    unnamed x24 -> x14, local copies, waits for them, and re-layouts: 8.78 us -> 2.68 us
    ppermute x10, waiting for transfers between devices: 4.8 us -> 8.34 us  [over_x(): return lax.ppermute(array, 'tp', [(0, 1), (1, 0)])]
    pallas_call x1, Pallas kernels: 1.46 us -> 3.41 us  [weights_call(): pl.pallas_call(weights_kernel, grid_spec=pltpu.PrefetchScalarGridSpec(num...]
  transfers between devices with their start and end apart: 39 -> 39, of which waited for: 11 -> 14; matrix products, arithmetic and copies ran while one was open for 1% -> 0% of each run, Pallas kernels for 31% -> 29%
where the time goes in v13:
time: 161 us
  Pallas kernels  63.9 us (40%)
  waiting for transfers between devices  48.4 us (30%)
  starting transfers between devices  42.5 us (26%)
  local copies, waits for them, and re-layouts  2.69 us (2%)
  other arithmetic  2.44 us (2%)
    ppermute x13, waiting for transfers between devices, over_z(): lax.ppermute(array, 'ep', [(i, (i + shift * n_y) % ep) for i in range(ep)])  38.6 us
    pallas_call x3, Pallas kernels, rows_call(): pl.pallas_call(functools.partial(rows_kernel, count, ways, capacity, slot...  32.4 us
    ppermute x13, starting transfers between devices, over_z(): lax.ppermute(array, 'ep', [(i, (i + shift * n_y) % ep) for i in range(ep)])  19.4 us
    pallas_call x1, Pallas kernels, join_call(): pl.pallas_call(join_kernel, in_specs=[LOOSE] * 2, out_specs=LOOSE, out_sh...  17 us
    ppermute x10, starting transfers between devices, over_x(): return lax.ppermute(array, 'tp', [(0, 1), (1, 0)])  11.3 us
    pallas_call x2, Pallas kernels, grads_call(): pl.pallas_call(functools.partial(grads_kernel, count, *starts, 2 * per),...  11.1 us
    ppermute x11, starting transfers between devices, over_y(): lax.ppermute(array, 'ep', [(i, i + 1 - 2 * (i % n_y)) for i in range(ep)])  11 us
    ppermute x10, waiting for transfers between devices, over_x(): return lax.ppermute(array, 'tp', [(0, 1), (1, 0)])  8.34 us
  transfers between devices with their start and end apart: 39, of which 14 were waited for; matrix products, arithmetic and copies ran while one was open for 0% of the time, Pallas kernels for 29%

profile of v13, /device:TPU:0, one launch (start us, length us, event | category | flops | bytes accessed | tf_op | source)
XLA Modules:
  0.0 160.9 jit_solution(15502597980193606568)
XLA Ops:
  0.6 17.0 %join.1.refs_4_ = bf16[256,1024]{1,0:T(8,128)(2,1)} custom-call(bf16[128,1024]{1,0:T(8,128)(2,1)} %top_ref.1, bf16[128,1024]{1,0:T(8,128)(2,1)} %bottom_ref.1), custom_call_target="tpu_custom_call" | custom-call | bytes 1048576 | tf_op jit(solution)/shard_map/join/pallas_call | solution.py:180
  17.6 3.1 %collective-permute-start = (bf16[256,1024]{1,0:T(8,128)(2,1)}, bf16[256,1024]{1,0:T(8,128)(2,1)}, u32[]{:S(2)}, u32[]{:S(2)}) collective-permute-start(bf16[256,1024]{1,0:T(8,128)(2,1)} %join.1.refs_4_), channel_id=1, source_target_pairs={{0,4},{2,6},{4,8},{6,10},{8,12},{10,14},{12,0},{14,2},{1,5},{3,7},... | collective-permute-start | bytes 1572872 | tf_op jit(solution)/shard_map/ppermute | solution.py:447
  20.7 1.5 collective-permute-start.1
  22.2 1.5 collective-permute-start.2
  23.7 3.4 %weights.1 = (bf16[2048,768]{1,0:T(8,128)(2,1)S(1)}, bf16[384,2048]{1,0:T(8,128)(2,1)}) custom-call(s32[1]{0:T(128)} %bitcast.2.tp_ref, bf16[1,2048,384]{2,1,0:T(8,128)(2,1)} %wg_ref.1, bf16[1,2048,384]{2,1,0:T(8,128)(2,1)} %wu_ref.1, bf16[1,384,2048]{2,1,0:T(8,128)(2,1)} %wd_ref.1), custom_call_target="tpu_custom_call" | custom-call | bytes 9437184 | tf_op jit(solution)/shard_map/weights/pallas_call | solution.py:141
  27.1 7.8 %collective-permute-done.refs_4_ = bf16[256,1024]{1,0:T(8,128)(2,1)} collective-permute-done((bf16[256,1024]{1,0:T(8,128)(2,1)}, bf16[256,1024]{1,0:T(8,128)(2,1)}, u32[]{:S(2)}, u32[]{:S(2)}) %collective-permute-start) | collective-permute-done | bytes 524320 | tf_op jit(solution)/shard_map/ppermute | solution.py:447
  35.0 0.7 collective-permute-done.2.refs_5_
  36.2 1.6 collective-permute-start.7
  38.3 1.5 collective-permute-start.5
  39.8 12.3 %collective-permute-done.7.refs_8_ = bf16[256,1024]{1,0:T(8,128)(2,1)} collective-permute-done((bf16[256,1024]{1,0:T(8,128)(2,1)}, bf16[256,1024]{1,0:T(8,128)(2,1)}, u32[]{:S(2)}, u32[]{:S(2)}) %collective-permute-start.7) | collective-permute-done | bytes 524320 | tf_op jit(solution)/shard_map/ppermute | solution.py:447
  52.1 0.9 collective-permute-start.6
  53.0 0.8 copy-done.3
  53.9 0.8 copy-done
  54.7 1.1 collective-permute-start.10
  55.8 1.5 collective-permute-start.11
  58.0 1.0 copy-done.1
  59.0 9.8 %rows.3 = (bf16[144,5248]{1,0:T(8,128)(2,1)S(1)}, bf16[144,5248]{1,0:T(8,128)(2,1)S(1)}, bf16[1,144,1024]{2,1,0:T(8,128)(2,1)S(1)}, bf16[1,144,1024]{2,1,0:T(8,1...) custom-call(s32[3]{0:T(128)S(1)} %pad_add_fusion.where_ref, ...), custom_call_target="tpu_custom_call" | custom-call | flops 3170893824 | bytes 13631488 | tf_op jit(solution)/shard_map/rows/pallas_call | solution.py:312
  68.9 0.9 collective-permute-done.9.refs_4_
  70.3 0.7 collective-permute-start.13
  70.9 0.9 collective-permute-start.14
  72.1 3.5 %collective-permute-start.16 = (bf16[2,16,128]{2,1,0:T(8,128)(2,1)S(1)}, bf16[2,16,128]{2,1,0:T(8,128)(2,1)S(1)}, u32[]{:S(2)}, u32[]{:S(2)}) collective-permute-start(bf16[2,16,128]{2,1,0:T(8,128)(2,1)S(1)} %pad_maximum_fusion.refs_8_), channel_id=1, source_target_pairs={{0,8},{2,10},{4,12},{6,14},{8,0},{10,2},{12,4},{14,6},{1,9},{3,11}... | collective-permute-start | bytes 24584 | tf_op jit(solution)/shard_map/ppermute | solution.py:447
  75.7 5.5 %collective-permute-done.12.refs_5_ = bf16[256,1024]{1,0:T(8,128)(2,1)S(1)} collective-permute-done((bf16[256,1024]{1,0:T(8,128)(2,1)}, bf16[256,1024]{1,0:T(8,128)(2,1)S(1)}, u32[]{:S(2)}, u32[]{:S(2)}) %collective-permute-start.12) | collective-permute-done | bytes 524320 | tf_op jit(solution)/shard_map/ppermute | solution.py:438
  81.2 2.1 %collective-permute-done.13.refs_7_ = bf16[256,1024]{1,0:T(8,128)(2,1)S(1)} collective-permute-done((bf16[256,1024]{1,0:T(8,128)(2,1)S(1)}, bf16[256,1024]{1,0:T(8,128)(2,1)S(1)}, u32[]{:S(2)}, u32[]{:S(2)}) %collective-permute-start.13) | collective-permute-done | bytes 524320 | tf_op jit(solution)/shard_map/ppermute | solution.py:447
  83.3 1.1 collective-permute-start.18
  84.4 1.6 %collective-permute-start.19 = (bf16[256,1024]{1,0:T(8,128)(2,1)}, bf16[256,1024]{1,0:T(8,128)(2,1)S(1)}, u32[]{:S(2)}, u32[]{:S(2)}) collective-permute-start(bf16[256,1024]{1,0:T(8,128)(2,1)} %collective-permute-done.9.refs_4_), channel_id=1, source_target_pairs={{0,1},{1,0},{2,3},{3,2},{4,5},{5,4},{6,7},{7,6},{8,9},{9,8},{10,11... | collective-permute-start | bytes 1572872 | tf_op jit(solution)/shard_map/ppermute | solution.py:438
  86.0 2.7 %collective-permute-start.17 = (bf16[256,1024]{1,0:T(8,128)(2,1)S(1)}, bf16[256,1024]{1,0:T(8,128)(2,1)S(1)}, u32[]{:S(2)}, u32[]{:S(2)}) collective-permute-start(bf16[256,1024]{1,0:T(8,128)(2,1)S(1)} %copy-done.2), channel_id=1, source_target_pairs={{0,12},{2,14},{4,0},{6,2},{8,4},{10,6},{12,8},{14,10},{1,13},{3,15... | collective-permute-start | bytes 1572872 | tf_op jit(solution)/shard_map/ppermute | solution.py:447
  88.7 12.8 %rows.4 = (bf16[288,5248]{1,0:T(8,128)(2,1)S(1)}, bf16[288,5248]{1,0:T(8,128)(2,1)S(1)}, bf16[1,144,1024]{2,1,0:T(8,128)(2,1)S(1)}, bf16[1,144,1024]{2,1,0:T(8,1...) custom-call(s32[3]{0:T(128)S(1)} %pad_add_fusion.where_ref, ...), custom_call_target="tpu_custom_call" | custom-call | flops 6341787648 | bytes 17825792 | tf_op jit(solution)/shard_map/rows/pallas_call | solution.py:312
  101.6 0.8 collective-permute-start.21
  103.1 0.9 collective-permute-start.23
  104.0 1.3 collective-permute-done.21.refs_8_
  105.3 2.5 %collective-permute-start.24 = (bf16[1,144,1024]{2,1,0:T(8,128)(2,1)S(1)}, bf16[1,144,1024]{2,1,0:T(8,128)(2,1)S(1)}, u32[]{:S(2)}, u32[]{:S(2)}) collective-permute-start(bf16[1,144,1024]{2,1,0:T(8,128)(2,1)S(1)} %get-tuple-element.107), channel_id=1, source_target_pairs={{0,12},{2,14},{4,0},{6,2},{8,4},{10,6},{12,8},{14,10},{1,13},{3,15... | collective-permute-start | bytes 884744 | tf_op jit(solution)/shard_map/ppermute | solution.py:447
  107.8 9.7 %rows.5 = (bf16[144,5248]{1,0:T(8,128)(2,1)S(1)}, bf16[144,5248]{1,0:T(8,128)(2,1)S(1)}, bf16[1,144,1024]{2,1,0:T(8,128)(2,1)S(1)}, bf16[1,144,1024]{2,1,0:T(8,1...) custom-call(s32[3]{0:T(128)S(1)} %pad_add_fusion.where_ref, ...), custom_call_target="tpu_custom_call" | custom-call | flops 3170893824 | bytes 13631488 | tf_op jit(solution)/shard_map/rows/pallas_call | solution.py:312
  118.2 1.5 collective-permute-start.20
  119.8 1.0 collective-permute-start.29
  121.5 6.7 %grads.2 = (bf16[1,2048,384]{2,1,0:T(8,128)(2,1)}, bf16[1,2048,384]{2,1,0:T(8,128)(2,1)}) custom-call(s32[1]{0:T(128)} %bitcast.2.tp_ref, bf16[144,5248]{1,0:T(8,128)(2,1)S(1)} %get-tuple-element.84.refs_0_, bf16[144,5248]{1,0:T(8,128)(2,1)S(1)} %collective-permute-done.30.refs_1_, bf16[288,5248]{1,0:T(8,128)(2,1)S(1)} %get-tuple-element.98.refs_9_.refs_2_, ...), custom_call_target="tpu_custom_call" | custom-call | flops 3623878656 | bytes 6488064 | tf_op jit(solution)/shard_map/grads/pallas_call | solution.py:404
  128.2 1.1 collective-permute-start.26
  129.3 2.5 %collective-permute-done.27 = bf16[1,144,1024]{2,1,0:T(8,128)(2,1)S(1)} collective-permute-done((bf16[1,144,1024]{2,1,0:T(8,128)(2,1)S(1)}, bf16[1,144,1024]{2,1,0:T(8,128)(2,1)S(1)}, u32[]{:S(2)}, u32[]{:S(2)}) %collective-permute-start.27) | collective-permute-done | bytes 294944 | tf_op jit(solution)/shard_map/ppermute | solution.py:447
  132.2 1.0 collective-permute-start.34
  133.1 4.4 %grads.3 = bf16[1,384,2048]{2,1,0:T(8,128)(2,1)} custom-call(s32[1]{0:T(128)} %bitcast.2.tp_ref, bf16[144,5248]{1,0:T(8,128)(2,1)S(1)} %get-tuple-element.84.refs_0_, bf16[144,5248]{1,0:T(8,128)(2,1)S(1)} %collective-permute-done.30.refs_1_, bf16[288,5248]{1,0:T(8,128)(2,1)S(1)} %get-tuple-element.98.refs_9_.refs_2_, ...), custom_call_target="tpu_custom_call" | custom-call | flops 1811939328 | bytes 5603328 | tf_op jit(solution)/shard_map/grads/pallas_call | solution.py:404
  137.6 2.2 %collective-permute-done.25 = bf16[1,144,1024]{2,1,0:T(8,128)(2,1)S(1)} collective-permute-done((bf16[1,144,1024]{2,1,0:T(8,128)(2,1)S(1)}, bf16[1,144,1024]{2,1,0:T(8,128)(2,1)S(1)}, u32[]{:S(2)}, u32[]{:S(2)}) %collective-permute-start.25) | collective-permute-done | bytes 294944 | tf_op jit(solution)/shard_map/ppermute | solution.py:438
  139.7 2.3 %collective-permute-done.33 = bf16[1,144,1024]{2,1,0:T(8,128)(2,1)S(1)} collective-permute-done((bf16[1,144,1024]{2,1,0:T(8,128)(2,1)S(1)}, bf16[1,144,1024]{2,1,0:T(8,128)(2,1)S(1)}, u32[]{:S(2)}, u32[]{:S(2)}) %collective-permute-start.33) | collective-permute-done | bytes 294944 | tf_op jit(solution)/shard_map/ppermute | solution.py:447
  142.0 1.3 collective-permute-done.34
  143.5 3.6 %collective-permute-start.36 = (bf16[1,144,1024]{2,1,0:T(8,128)(2,1)S(1)}, bf16[1,144,1024]{2,1,0:T(8,128)(2,1)S(1)}, u32[]{:S(2)}, u32[]{:S(2)}) collective-permute-start(bf16[1,144,1024]{2,1,0:T(8,128)(2,1)S(1)} %add_convert_fusion.2), channel_id=1, source_target_pairs={{0,12},{2,14},{4,0},{6,2},{8,4},{10,6},{12,8},{14,10},{1,13},{3,15... | collective-permute-start | bytes 884744 | tf_op jit(solution)/shard_map/ppermute | solution.py:447
  147.4 1.0 collective-permute-start.35
  148.4 1.6 collective-permute-start.38
  150.0 4.6 %collective-permute-done.36 = bf16[1,144,1024]{2,1,0:T(8,128)(2,1)S(1)} collective-permute-done((bf16[1,144,1024]{2,1,0:T(8,128)(2,1)S(1)}, bf16[1,144,1024]{2,1,0:T(8,128)(2,1)S(1)}, u32[]{:S(2)}, u32[]{:S(2)}) %collective-permute-start.36) | collective-permute-done | bytes 294944 | tf_op jit(solution)/shard_map/ppermute | solution.py:447
  154.6 4.7 %collective-permute-done.37 = bf16[1,144,1024]{2,1,0:T(8,128)(2,1)S(1)} collective-permute-done((bf16[1,144,1024]{2,1,0:T(8,128)(2,1)S(1)}, bf16[1,144,1024]{2,1,0:T(8,128)(2,1)S(1)}, u32[]{:S(2)}, u32[]{:S(2)}) %collective-permute-start.37) | collective-permute-done | bytes 294944 | tf_op jit(solution)/shard_map/ppermute | solution.py:447
  160.0 0.9 fusion
  (67 shorter events, 6.2 us)
Async XLA Ops:
  17.6 17.3 %collective-permute-start = (bf16[256,1024]{1,0:T(8,128)(2,1)}, bf16[256,1024]{1,0:T(8,128)(2,1)}, u32[]{:S(2)}, u32[]{:S(2)}) collective-permute-start(bf16[256,1024]{1,0:T(8,128)(2,1)} %join.1.refs_4_), channel_id=1, source_target_pairs={{0,4},{2,6},{4,8},{6,10},{8,12},{10,14},{12,0},{14,2},{1,5},{3,7},... | collective-permute-start | bytes 1572872 | tf_op jit(solution)/shard_map/ppermute | solution.py:447
  20.7 14.3 %collective-permute-start.1 = (bf16[256,1024]{1,0:T(8,128)(2,1)}, bf16[256,1024]{1,0:T(8,128)(2,1)}, u32[]{:S(2)}, u32[]{:S(2)}) collective-permute-start(bf16[256,1024]{1,0:T(8,128)(2,1)} %join.1.refs_4_), channel_id=1, source_target_pairs={{0,2},{2,0},{4,6},{6,4},{8,10},{10,8},{12,14},{14,12},{1,3},{3,1},... | collective-permute-start | bytes 1572872 | tf_op jit(solution)/shard_map/ppermute | solution.py:444
  22.2 13.4 %collective-permute-start.2 = (bf16[256,1024]{1,0:T(8,128)(2,1)}, bf16[256,1024]{1,0:T(8,128)(2,1)}, u32[]{:S(2)}, u32[]{:S(2)}) collective-permute-start(bf16[256,1024]{1,0:T(8,128)(2,1)} %join.1.refs_4_), channel_id=1, source_target_pairs={{0,1},{1,0},{2,3},{3,2},{4,5},{5,4},{6,7},{7,6},{8,9},{9,8},{10,11... | collective-permute-start | bytes 1572872 | tf_op jit(solution)/shard_map/ppermute | solution.py:438
  23.7 16.0 %copy-start.6 = (bf16[128,8]{0,1:T(8,128)(2,1)S(1)}, bf16[128,8]{0,1:T(8,128)(2,1)}, u32[]{:S(2)}) copy-start(bf16[128,8]{0,1:T(8,128)(2,1)} %param.10) | copy-start | bytes 6148
  23.7 16.0 %copy-start.5 = (s32[128,8]{0,1:T(8,128)S(1)}, s32[128,8]{0,1:T(8,128)}, u32[]{:S(2)}) copy-start(s32[128,8]{0,1:T(8,128)} %param.9) | copy-start | bytes 12292
  35.7 22.3 %collective-permute-start.3 = (bf16[2048,768]{1,0:T(8,128)(2,1)S(1)}, bf16[2048,768]{1,0:T(8,128)(2,1)}, u32[]{:S(2)}, u32[]{:S(2)}) collective-permute-start(bf16[2048,768]{1,0:T(8,128)(2,1)S(1)} %get-tuple-element.71.refs_0_), channel_id=1, source_target_pairs={{0,16},{16,0},{1,17},{17,1},{2,18},{18,2},{3,19},{19,3},{4,20},{20... | collective-permute-start | bytes 9437192 | tf_op jit(solution)/shard_map/ppermute | solution.py:441
  35.7 22.3 %collective-permute-start.4 = (bf16[384,2048]{1,0:T(8,128)(2,1)}, bf16[384,2048]{1,0:T(8,128)(2,1)}, u32[]{:S(2)}, u32[]{:S(2)}) collective-permute-start(bf16[384,2048]{1,0:T(8,128)(2,1)} %get-tuple-element.72.refs_2_), channel_id=1, source_target_pairs={{0,16},{16,0},{1,17},{17,1},{2,18},{18,2},{3,19},{19,3},{4,20},{20... | collective-permute-start | bytes 4718600 | tf_op jit(solution)/shard_map/ppermute | solution.py:441
  36.2 15.9 %collective-permute-start.7 = (bf16[256,1024]{1,0:T(8,128)(2,1)}, bf16[256,1024]{1,0:T(8,128)(2,1)}, u32[]{:S(2)}, u32[]{:S(2)}) collective-permute-start(bf16[256,1024]{1,0:T(8,128)(2,1)} %collective-permute-done.refs_4_), channel_id=1, source_target_pairs={{0,4},{2,6},{4,8},{6,10},{8,12},{10,14},{12,0},{14,2},{1,5},{3,7},... | collective-permute-start | bytes 1572872 | tf_op jit(solution)/shard_map/ppermute | solution.py:447
  37.7 15.3 %collective-permute-start.8 = (bf16[256,1024]{1,0:T(8,128)(2,1)}, bf16[256,1024]{1,0:T(8,128)(2,1)S(1)}, u32[]{:S(2)}, u32[]{:S(2)}) collective-permute-start(bf16[256,1024]{1,0:T(8,128)(2,1)} %collective-permute-done.refs_4_), channel_id=1, source_target_pairs={{0,2},{2,0},{4,6},{6,4},{8,10},{10,8},{12,14},{14,12},{1,3},{3,1},... | collective-permute-start | bytes 1572872 | tf_op jit(solution)/shard_map/ppermute | solution.py:444
  38.3 15.6 %collective-permute-start.5 = (bf16[256,1024]{1,0:T(8,128)(2,1)}, bf16[256,1024]{1,0:T(8,128)(2,1)S(1)}, u32[]{:S(2)}, u32[]{:S(2)}) collective-permute-start(bf16[256,1024]{1,0:T(8,128)(2,1)} %collective-permute-done.1.refs_6_), channel_id=1, source_target_pairs={{0,1},{1,0},{2,3},{3,2},{4,5},{5,4},{6,7},{7,6},{8,9},{9,8},{10,11... | collective-permute-start | bytes 1572872 | tf_op jit(solution)/shard_map/ppermute | solution.py:438
  52.1 5.2 %collective-permute-start.6 = (bf16[16,128]{1,0:T(8,128)(2,1)S(1)}, bf16[16,128]{1,0:T(8,128)(2,1)S(1)}, u32[]{:S(2)}, u32[]{:S(2)}) collective-permute-start(bf16[16,128]{1,0:T(8,128)(2,1)S(1)} %get-tuple-element.134), channel_id=1, source_target_pairs={{0,2},{2,0},{4,6},{6,4},{8,10},{10,8},{12,14},{14,12},{1,3},{3,1},... | collective-permute-start | bytes 12296 | tf_op jit(solution)/shard_map/ppermute | solution.py:444
  53.0 0.8 copy-start.3
  53.9 0.8 copy-start
  54.7 14.2 %collective-permute-start.10 = (bf16[256,1024]{1,0:T(8,128)(2,1)}, bf16[256,1024]{1,0:T(8,128)(2,1)}, u32[]{:S(2)}, u32[]{:S(2)}) collective-permute-start(bf16[256,1024]{1,0:T(8,128)(2,1)} %collective-permute-done.7.refs_8_), channel_id=1, source_target_pairs={{0,2},{2,0},{4,6},{6,4},{8,10},{10,8},{12,14},{14,12},{1,3},{3,1},... | collective-permute-start | bytes 1572872 | tf_op jit(solution)/shard_map/ppermute | solution.py:444
  55.8 13.1 %collective-permute-start.11 = (bf16[256,1024]{1,0:T(8,128)(2,1)}, bf16[256,1024]{1,0:T(8,128)(2,1)}, u32[]{:S(2)}, u32[]{:S(2)}) collective-permute-start(bf16[256,1024]{1,0:T(8,128)(2,1)} %collective-permute-done.7.refs_8_), channel_id=1, source_target_pairs={{0,1},{1,0},{2,3},{3,2},{4,5},{5,4},{6,7},{7,6},{8,9},{9,8},{10,11... | collective-permute-start | bytes 1572872 | tf_op jit(solution)/shard_map/ppermute | solution.py:438
  57.3 12.5 %collective-permute-start.9 = (bf16[256,1024]{1,0:T(8,128)(2,1)}, bf16[256,1024]{1,0:T(8,128)(2,1)}, u32[]{:S(2)}, u32[]{:S(2)}) collective-permute-start(bf16[256,1024]{1,0:T(8,128)(2,1)} %join.1.refs_4_), channel_id=1, source_target_pairs={{0,12},{2,14},{4,0},{6,2},{8,4},{10,6},{12,8},{14,10},{1,13},{3,15... | collective-permute-start | bytes 1572872 | tf_op jit(solution)/shard_map/ppermute | solution.py:447
  57.9 1.0 copy-start.1
  59.0 27.0 %copy-start.2 = (bf16[256,1024]{1,0:T(8,128)(2,1)S(1)}, bf16[256,1024]{1,0:T(8,128)(2,1)}, u32[]{:S(2)}) copy-start(bf16[256,1024]{1,0:T(8,128)(2,1)} %copy-done) | copy-start | bytes 1572868
  59.0 29.7 %copy-start.4 = (bf16[256,1024]{1,0:T(8,128)(2,1)S(1)}, bf16[256,1024]{1,0:T(8,128)(2,1)}, u32[]{:S(2)}) copy-start(bf16[256,1024]{1,0:T(8,128)(2,1)} %copy-done.3) | copy-start | bytes 1572868
  69.7 11.4 %collective-permute-start.12 = (bf16[256,1024]{1,0:T(8,128)(2,1)}, bf16[256,1024]{1,0:T(8,128)(2,1)S(1)}, u32[]{:S(2)}, u32[]{:S(2)}) collective-permute-start(bf16[256,1024]{1,0:T(8,128)(2,1)} %collective-permute-done.refs_4_), channel_id=1, source_target_pairs={{0,1},{1,0},{2,3},{3,2},{4,5},{5,4},{6,7},{7,6},{8,9},{9,8},{10,11... | collective-permute-start | bytes 1572872 | tf_op jit(solution)/shard_map/ppermute | solution.py:438
  70.3 13.0 %collective-permute-start.13 = (bf16[256,1024]{1,0:T(8,128)(2,1)S(1)}, bf16[256,1024]{1,0:T(8,128)(2,1)S(1)}, u32[]{:S(2)}, u32[]{:S(2)}) collective-permute-start(bf16[256,1024]{1,0:T(8,128)(2,1)S(1)} %copy-done.1), channel_id=1, source_target_pairs={{0,4},{2,6},{4,8},{6,10},{8,12},{10,14},{12,0},{14,2},{1,5},{3,7},... | collective-permute-start | bytes 1572872 | tf_op jit(solution)/shard_map/ppermute | solution.py:447
  70.9 12.4 %collective-permute-start.14 = (bf16[256,1024]{1,0:T(8,128)(2,1)}, bf16[256,1024]{1,0:T(8,128)(2,1)S(1)}, u32[]{:S(2)}, u32[]{:S(2)}) collective-permute-start(bf16[256,1024]{1,0:T(8,128)(2,1)} %collective-permute-done.11.refs_9_), channel_id=1, source_target_pairs={{0,2},{2,0},{4,6},{6,4},{8,10},{10,8},{12,14},{14,12},{1,3},{3,1},... | collective-permute-start | bytes 1572872 | tf_op jit(solution)/shard_map/ppermute | solution.py:444
  71.8 16.8 %collective-permute-start.15 = (bf16[2,16,128]{2,1,0:T(8,128)(2,1)S(1)}, bf16[2,16,128]{2,1,0:T(8,128)(2,1)S(1)}, u32[]{:S(2)}, u32[]{:S(2)}) collective-permute-start(bf16[2,16,128]{2,1,0:T(8,128)(2,1)S(1)} %pad_maximum_fusion.refs_8_), channel_id=1, source_target_pairs={{0,4},{2,6},{4,8},{6,10},{8,12},{10,14},{12,0},{14,2},{1,5},{3,7},... | collective-permute-start | bytes 24584 | tf_op jit(solution)/shard_map/ppermute | solution.py:447
  72.1 16.6 %collective-permute-start.16 = (bf16[2,16,128]{2,1,0:T(8,128)(2,1)S(1)}, bf16[2,16,128]{2,1,0:T(8,128)(2,1)S(1)}, u32[]{:S(2)}, u32[]{:S(2)}) collective-permute-start(bf16[2,16,128]{2,1,0:T(8,128)(2,1)S(1)} %pad_maximum_fusion.refs_8_), channel_id=1, source_target_pairs={{0,8},{2,10},{4,12},{6,14},{8,0},{10,2},{12,4},{14,6},{1,9},{3,11}... | collective-permute-start | bytes 24584 | tf_op jit(solution)/shard_map/ppermute | solution.py:447
  83.3 18.2 %collective-permute-start.18 = (bf16[256,1024]{1,0:T(8,128)(2,1)}, bf16[256,1024]{1,0:T(8,128)(2,1)S(1)}, u32[]{:S(2)}, u32[]{:S(2)}) collective-permute-start(bf16[256,1024]{1,0:T(8,128)(2,1)} %collective-permute-done.9.refs_4_), channel_id=1, source_target_pairs={{0,2},{2,0},{4,6},{6,4},{8,10},{10,8},{12,14},{14,12},{1,3},{3,1},... | collective-permute-start | bytes 1572872 | tf_op jit(solution)/shard_map/ppermute | solution.py:444
  84.4 17.1 %collective-permute-start.19 = (bf16[256,1024]{1,0:T(8,128)(2,1)}, bf16[256,1024]{1,0:T(8,128)(2,1)S(1)}, u32[]{:S(2)}, u32[]{:S(2)}) collective-permute-start(bf16[256,1024]{1,0:T(8,128)(2,1)} %collective-permute-done.9.refs_4_), channel_id=1, source_target_pairs={{0,1},{1,0},{2,3},{3,2},{4,5},{5,4},{6,7},{7,6},{8,9},{9,8},{10,11... | collective-permute-start | bytes 1572872 | tf_op jit(solution)/shard_map/ppermute | solution.py:438
  86.0 15.5 %collective-permute-start.17 = (bf16[256,1024]{1,0:T(8,128)(2,1)S(1)}, bf16[256,1024]{1,0:T(8,128)(2,1)S(1)}, u32[]{:S(2)}, u32[]{:S(2)}) collective-permute-start(bf16[256,1024]{1,0:T(8,128)(2,1)S(1)} %copy-done.2), channel_id=1, source_target_pairs={{0,12},{2,14},{4,0},{6,2},{8,4},{10,6},{12,8},{14,10},{1,13},{3,15... | collective-permute-start | bytes 1572872 | tf_op jit(solution)/shard_map/ppermute | solution.py:447
  101.5 19.4 %collective-permute-start.31 = (bf16[288,5248]{1,0:T(8,128)(2,1)S(1)}, bf16[288,5248]{1,0:T(8,128)(2,1)S(1)}, u32[]{:S(2)}, u32[]{:S(2)}) collective-permute-start(bf16[288,5248]{1,0:T(8,128)(2,1)S(1)} %get-tuple-element.115), channel_id=1, source_target_pairs={{0,16},{16,0},{1,17},{17,1},{2,18},{18,2},{3,19},{19,3},{4,20},{20... | collective-permute-start | bytes 9068552 | tf_op jit(solution)/shard_map/ppermute | solution.py:441
  101.6 3.7 %collective-permute-start.21 = (bf16[2,16,128]{2,1,0:T(8,128)(2,1)S(1)}, bf16[2,16,128]{2,1,0:T(8,128)(2,1)S(1)}, u32[]{:S(2)}, u32[]{:S(2)}) collective-permute-start(bf16[2,16,128]{2,1,0:T(8,128)(2,1)S(1)} %pad_maximum_fusion.refs_8_), channel_id=1, source_target_pairs={{0,12},{2,14},{4,0},{6,2},{8,4},{10,6},{12,8},{14,10},{1,13},{3,15... | collective-permute-start | bytes 24584 | tf_op jit(solution)/shard_map/ppermute | solution.py:447
  102.4 17.4 %collective-permute-start.30 = (bf16[144,5248]{1,0:T(8,128)(2,1)S(1)}, bf16[144,5248]{1,0:T(8,128)(2,1)S(1)}, u32[]{:S(2)}, u32[]{:S(2)}) collective-permute-start(bf16[144,5248]{1,0:T(8,128)(2,1)S(1)} %get-tuple-element.114), channel_id=1, source_target_pairs={{0,16},{16,0},{1,17},{17,1},{2,18},{18,2},{3,19},{19,3},{4,20},{20... | collective-permute-start | bytes 4534280 | tf_op jit(solution)/shard_map/ppermute | solution.py:441
  102.6 15.0 %collective-permute-start.22 = (bf16[1,144,1024]{2,1,0:T(8,128)(2,1)S(1)}, bf16[1,144,1024]{2,1,0:T(8,128)(2,1)S(1)}, u32[]{:S(2)}, u32[]{:S(2)}) collective-permute-start(bf16[1,144,1024]{2,1,0:T(8,128)(2,1)S(1)} %get-tuple-element.105), channel_id=1, source_target_pairs={{0,1},{1,0},{2,3},{3,2},{4,5},{5,4},{6,7},{7,6},{8,9},{9,8},{10,11... | collective-permute-start | bytes 884744 | tf_op jit(solution)/shard_map/ppermute | solution.py:438
  103.1 14.5 %collective-permute-start.23 = (bf16[1,144,1024]{2,1,0:T(8,128)(2,1)S(1)}, bf16[1,144,1024]{2,1,0:T(8,128)(2,1)S(1)}, u32[]{:S(2)}, u32[]{:S(2)}) collective-permute-start(bf16[1,144,1024]{2,1,0:T(8,128)(2,1)S(1)} %get-tuple-element.106), channel_id=1, source_target_pairs={{0,2},{2,0},{4,6},{6,4},{8,10},{10,8},{12,14},{14,12},{1,3},{3,1},... | collective-permute-start | bytes 884744 | tf_op jit(solution)/shard_map/ppermute | solution.py:444
  105.3 12.2 %collective-permute-start.24 = (bf16[1,144,1024]{2,1,0:T(8,128)(2,1)S(1)}, bf16[1,144,1024]{2,1,0:T(8,128)(2,1)S(1)}, u32[]{:S(2)}, u32[]{:S(2)}) collective-permute-start(bf16[1,144,1024]{2,1,0:T(8,128)(2,1)S(1)} %get-tuple-element.107), channel_id=1, source_target_pairs={{0,12},{2,14},{4,0},{6,2},{8,4},{10,6},{12,8},{14,10},{1,13},{3,15... | collective-permute-start | bytes 884744 | tf_op jit(solution)/shard_map/ppermute | solution.py:447
  117.6 3.4 %collective-permute-start.32 = (bf16[144,5248]{1,0:T(8,128)(2,1)S(1)}, bf16[144,5248]{1,0:T(8,128)(2,1)S(1)}, u32[]{:S(2)}, u32[]{:S(2)}) collective-permute-start(bf16[144,5248]{1,0:T(8,128)(2,1)S(1)} %get-tuple-element.117), channel_id=1, source_target_pairs={{0,16},{16,0},{1,17},{17,1},{2,18},{18,2},{3,19},{19,3},{4,20},{20... | collective-permute-start | bytes 4534280 | tf_op jit(solution)/shard_map/ppermute | solution.py:441
  117.7 10.6 %collective-permute-start.28 = (bf16[1,144,1024]{2,1,0:T(8,128)(2,1)S(1)}, bf16[1,144,1024]{2,1,0:T(8,128)(2,1)S(1)}, u32[]{:S(2)}, u32[]{:S(2)}) collective-permute-start(bf16[1,144,1024]{2,1,0:T(8,128)(2,1)S(1)} %get-tuple-element.112), channel_id=1, source_target_pairs={{0,1},{1,0},{2,3},{3,2},{4,5},{5,4},{6,7},{7,6},{8,9},{9,8},{10,11... | collective-permute-start | bytes 884744 | tf_op jit(solution)/shard_map/ppermute | solution.py:438
  118.2 19.3 %collective-permute-start.20 = (bf16[1,144,1024]{2,1,0:T(8,128)(2,1)S(1)}, bf16[1,144,1024]{2,1,0:T(8,128)(2,1)S(1)}, u32[]{:S(2)}, u32[]{:S(2)}) collective-permute-start(bf16[1,144,1024]{2,1,0:T(8,128)(2,1)S(1)} %get-tuple-element.97), channel_id=1, source_target_pairs={{0,1},{1,0},{2,3},{3,2},{4,5},{5,4},{6,7},{7,6},{8,9},{9,8},{10,11... | collective-permute-start | bytes 884744 | tf_op jit(solution)/shard_map/ppermute | solution.py:438
  119.8 9.5 %collective-permute-start.29 = (bf16[1,144,1024]{2,1,0:T(8,128)(2,1)S(1)}, bf16[1,144,1024]{2,1,0:T(8,128)(2,1)S(1)}, u32[]{:S(2)}, u32[]{:S(2)}) collective-permute-start(bf16[1,144,1024]{2,1,0:T(8,128)(2,1)S(1)} %add_convert_fusion.5), channel_id=1, source_target_pairs={{0,2},{2,0},{4,6},{6,4},{8,10},{10,8},{12,14},{14,12},{1,3},{3,1},... | collective-permute-start | bytes 884744 | tf_op jit(solution)/shard_map/ppermute | solution.py:444
  121.0 10.8 %collective-permute-start.27 = (bf16[1,144,1024]{2,1,0:T(8,128)(2,1)S(1)}, bf16[1,144,1024]{2,1,0:T(8,128)(2,1)S(1)}, u32[]{:S(2)}, u32[]{:S(2)}) collective-permute-start(bf16[1,144,1024]{2,1,0:T(8,128)(2,1)S(1)} %get-tuple-element.111), channel_id=1, source_target_pairs={{0,4},{2,6},{4,8},{6,10},{8,12},{10,14},{12,0},{14,2},{1,5},{3,7},... | collective-permute-start | bytes 884744 | tf_op jit(solution)/shard_map/ppermute | solution.py:447
  121.0 18.7 %collective-permute-start.25 = (bf16[1,144,1024]{2,1,0:T(8,128)(2,1)S(1)}, bf16[1,144,1024]{2,1,0:T(8,128)(2,1)S(1)}, u32[]{:S(2)}, u32[]{:S(2)}) collective-permute-start(bf16[1,144,1024]{2,1,0:T(8,128)(2,1)S(1)} %get-tuple-element.108), channel_id=1, source_target_pairs={{0,1},{1,0},{2,3},{3,2},{4,5},{5,4},{6,7},{7,6},{8,9},{9,8},{10,11... | collective-permute-start | bytes 884744 | tf_op jit(solution)/shard_map/ppermute | solution.py:438
  128.2 11.5 %collective-permute-start.26 = (bf16[1,144,1024]{2,1,0:T(8,128)(2,1)S(1)}, bf16[1,144,1024]{2,1,0:T(8,128)(2,1)S(1)}, u32[]{:S(2)}, u32[]{:S(2)}) collective-permute-start(bf16[1,144,1024]{2,1,0:T(8,128)(2,1)S(1)} %get-tuple-element.109), channel_id=1, source_target_pairs={{0,2},{2,0},{4,6},{6,4},{8,10},{10,8},{12,14},{14,12},{1,3},{3,1},... | collective-permute-start | bytes 884744 | tf_op jit(solution)/shard_map/ppermute | solution.py:444
  132.0 10.1 %collective-permute-start.33 = (bf16[1,144,1024]{2,1,0:T(8,128)(2,1)S(1)}, bf16[1,144,1024]{2,1,0:T(8,128)(2,1)S(1)}, u32[]{:S(2)}, u32[]{:S(2)}) collective-permute-start(bf16[1,144,1024]{2,1,0:T(8,128)(2,1)S(1)} %add_convert_fusion.4), channel_id=1, source_target_pairs={{0,4},{2,6},{4,8},{6,10},{8,12},{10,14},{12,0},{14,2},{1,5},{3,7},... | collective-permute-start | bytes 884744 | tf_op jit(solution)/shard_map/ppermute | solution.py:447
  132.2 11.2 %collective-permute-start.34 = (bf16[1,144,1024]{2,1,0:T(8,128)(2,1)S(1)}, bf16[1,144,1024]{2,1,0:T(8,128)(2,1)S(1)}, u32[]{:S(2)}, u32[]{:S(2)}) collective-permute-start(bf16[1,144,1024]{2,1,0:T(8,128)(2,1)S(1)} %add_convert_fusion.3), channel_id=1, source_target_pairs={{0,2},{2,0},{4,6},{6,4},{8,10},{10,8},{12,14},{14,12},{1,3},{3,1},... | collective-permute-start | bytes 884744 | tf_op jit(solution)/shard_map/ppermute | solution.py:444
  143.5 11.1 %collective-permute-start.36 = (bf16[1,144,1024]{2,1,0:T(8,128)(2,1)S(1)}, bf16[1,144,1024]{2,1,0:T(8,128)(2,1)S(1)}, u32[]{:S(2)}, u32[]{:S(2)}) collective-permute-start(bf16[1,144,1024]{2,1,0:T(8,128)(2,1)S(1)} %add_convert_fusion.2), channel_id=1, source_target_pairs={{0,12},{2,14},{4,0},{6,2},{8,4},{10,6},{12,8},{14,10},{1,13},{3,15... | collective-permute-start | bytes 884744 | tf_op jit(solution)/shard_map/ppermute | solution.py:447
  147.3 12.0 %collective-permute-start.37 = (bf16[1,144,1024]{2,1,0:T(8,128)(2,1)S(1)}, bf16[1,144,1024]{2,1,0:T(8,128)(2,1)S(1)}, u32[]{:S(2)}, u32[]{:S(2)}) collective-permute-start(bf16[1,144,1024]{2,1,0:T(8,128)(2,1)S(1)} %add_convert_fusion.1), channel_id=1, source_target_pairs={{0,4},{2,6},{4,8},{6,10},{8,12},{10,14},{12,0},{14,2},{1,5},{3,7},... | collective-permute-start | bytes 884744 | tf_op jit(solution)/shard_map/ppermute | solution.py:447
  147.4 11.9 %collective-permute-start.35 = (bf16[1,144,1024]{2,1,0:T(8,128)(2,1)S(1)}, bf16[1,144,1024]{2,1,0:T(8,128)(2,1)S(1)}, u32[]{:S(2)}, u32[]{:S(2)}) collective-permute-start(bf16[1,144,1024]{2,1,0:T(8,128)(2,1)S(1)} %get-tuple-element.125), channel_id=1, source_target_pairs={{0,2},{2,0},{4,6},{6,4},{8,10},{10,8},{12,14},{14,12},{1,3},{3,1},... | collective-permute-start | bytes 884744 | tf_op jit(solution)/shard_map/ppermute | solution.py:444
  148.4 10.8 %collective-permute-start.38 = (bf16[1,144,1024]{2,1,0:T(8,128)(2,1)S(1)}, bf16[1,144,1024]{2,1,0:T(8,128)(2,1)S(1)}, u32[]{:S(2)}, u32[]{:S(2)}) collective-permute-start(bf16[1,144,1024]{2,1,0:T(8,128)(2,1)S(1)} %add_convert_fusion), channel_id=1, source_target_pairs={{0,1},{1,0},{2,3},{3,2},{4,5},{5,4},{6,7},{7,6},{8,9},{9,8},{10,11... | collective-permute-start | bytes 884744 | tf_op jit(solution)/shard_map/ppermute | solution.py:438

commit v14 on v13

--- a/solution.py
+++ b/solution.py
@@ -180,8 +180,8 @@
     return pl.pallas_call(
         join_kernel,
         in_specs=[LOOSE] * 2,
-        out_specs=LOOSE,
-        out_shape=jax.ShapeDtypeStruct((2 * rows, columns), top.dtype),
+        out_specs=pl.BlockSpec(memory_space=pltpu.VMEM),
+        out_shape=pltpu.VMEM((2 * rows, columns), top.dtype),
         scratch_shapes=[pltpu.SemaphoreType.DMA((2,))],
         compiler_params=pltpu.CompilerParams(vmem_limit_bytes=8 << 20),
         cost_estimate=pl.CostEstimate(flops=0, bytes_accessed=8 * rows * columns, transcendentals=0),
@@ -274,29 +274,38 @@
         outs[expert][:, both_at] = jnp.concatenate([d_gate, (hgrad * act).astype(jnp.bfloat16)], 1)
         outs[expert][:, scaled_at] = (prob * hidden).astype(jnp.bfloat16)
 
-    names = lax.broadcasted_iota(jnp.int32, (owners, half), 0)
-    column = lax.broadcasted_iota(jnp.int32, (owners, half), 1) // (2 * tok)
+    extra_rows = packets[0].shape[1] - tok
+    per_row = owners // extra_rows
+    names = lax.broadcasted_iota(jnp.int32, (extra_rows, half), 0)
+    column = lax.broadcasted_iota(jnp.int32, (extra_rows, half), 1) // (2 * tok)
     for chunk in range(count):
         for y in range(2):
-            extra = jnp.zeros((owners, half), jnp.float32)
+            extra = jnp.zeros((extra_rows, half), jnp.float32)
             for expert in range(2):
                 part_scores = scores[expert][chunk * slots : (chunk + 1) * slots]
                 line = jnp.sum(picks[chunk, expert][y] * part_scores, axis=0, keepdims=True)
                 high = line.astype(jnp.bfloat16).astype(jnp.float32)
                 line = jnp.concatenate([high, line - high] * (half // (2 * tok)), 1)
-                extra = extra + jnp.where((names == where_ref[expert]) & (column == where_ref[2]), line, 0.0)
+                row, cell = where_ref[expert] // per_row, where_ref[expert] % per_row * 2 + where_ref[2]
+                extra = extra + jnp.where((names == row) & (column == cell), line, 0.0)
             for side in range(2):
                 number, slot = ways[chunk, y, side]
                 packets[number][slot, tok:] = extra.astype(jnp.bfloat16)
+    early = count == 1
+    grads = [outs[expert][:, both_at] for expert in range(2)]
+    if early:
+        grads = [dot(low_picks[0, expert], grads[expert], ((0,), (0,))).astype(jnp.bfloat16) for expert in range(2)]
     for side in (1, 0):
-        low = [
-            dot(outs[expert][:, both_at], wgu[expert][sides[side], :], ((1,), (1,))).astype(jnp.bfloat16) for expert in range(2)
-        ]
+        low = [dot(grads[expert], wgu[expert][sides[side], :], ((1,), (1,))) for expert in range(2)]
         for chunk in range(count):
-            total = None
-            for expert in range(2):
-                term = dot(low_picks[chunk, expert], low[expert][chunk * slots : (chunk + 1) * slots], ((0,), (0,)))
-                total = term if total is None else total + term
+            if early:
+                total = low[0] + low[1]
+            else:
+                rows = slice(chunk * slots, (chunk + 1) * slots)
+                total = sum(
+                    dot(low_picks[chunk, expert], low[expert][rows].astype(jnp.bfloat16), ((0,), (0,)))
+                    for expert in range(2)
+                )
             for y in range(2):
                 number, slot = ways[chunk, y, side]
                 packets[number][slot, :tok] = total[y * tok : (y + 1) * tok].astype(jnp.bfloat16)
@@ -308,7 +317,7 @@
     tok, half = units[0].shape[0] // 2, units[0].shape[1]
     part, width = weights[2].shape
     widths = (width, width, 2 * part, part)
-    packet = (tok + owners, half)
+    packet = (tok + 4 * tok * owners // half, half)
     return pl.pallas_call(
         functools.partial(rows_kernel, count, ways, capacity, slots),
         grid_spec=pltpu.PrefetchScalarGridSpec(
@@ -518,7 +527,7 @@
     mine_1, other_1, x_2, x_20, x_1, y_1, z_1, keep_1, keep_2, keep_2y = rows_of([1, 2], items, [])
     other_1, x_2, x_20, x_1, y_1, z_1 = tied([other_1, x_2, x_20, x_1, y_1, z_1], arrived.values())
     from_x2, from_y1, from_z1 = over_x(x_2), over_y(y_1), over_z(z_1, -1)
-    from_x20, from_x1 = over_x(x_20), over_x(x_1)
+    from_x20 = over_x(x_20)
     items = [[(0, 0, 1)], [(0, 1, 0)], [(0, 1, 1)], [(0, 0, 0)]]
     mine_3, other_3, x_3, y_3, z_3, keep_3 = rows_of([3], items, [mine_1])
     mine_3, other_3, x_3, y_3, z_3, keep_2y = tied(
@@ -527,18 +536,21 @@
     from_z3, from_x3, from_y2, from_y3 = over_z(z_3, 1), over_x(x_3), over_y(total(keep_2y, from_x2)), over_y(y_3)
     packed = [mine_0, over_role(other_0), mine_1, over_role(other_1), mine_3, over_role(other_3)]
     d_gate, d_up = grads_call(which_ref, packed, width, part, False)
-    from_z3, from_x20, from_y2 = tied([from_z3, from_x20, from_y2], [d_gate, d_up])
+    from_z3, from_x20, from_y2, x_1 = tied([from_z3, from_x20, from_y2, x_1], [d_gate, d_up])
+    from_x1 = over_x(x_1)
     from_far = over_y(total(far, from_z1, from_z3))
     from_z2 = over_z(total(keep_2, from_x20, from_y2), 1)
     (d_down,) = grads_call(which_ref, packed, width, part, True)
-    from_x1, from_x3, from_y3, from_z2, y_0 = tied([from_x1, from_x3, from_y3, from_z2, y_0], [d_down, from_far])
-    home_1 = over_z(total(keep_1, from_x1, from_y1), -1)
+    (from_x1,) = tied([from_x1], [d_down])
+    home_1 = total(keep_1, from_x1, from_y1)
+    from_far, from_x3, from_y3, from_z2, y_0 = tied([from_far, from_x3, from_y3, from_z2, y_0], [d_down, home_1])
+    from_x0 = over_x(total(side_0, from_far))
+    home_1 = over_z(home_1, -1)
+    home_3 = over_z(total(keep_3, from_x3, from_y3, from_z2), 1)
     from_y0 = over_y(y_0)
-    home_3 = over_z(total(keep_3, from_x3, from_y3, from_z2), 1)
-    from_x0 = over_x(total(side_0, from_far))
-    home = (near, from_y0, home_1, home_3, from_x0)
+    home = (near, from_x0, home_3, home_1, from_y0)
     d_tok = sum(block[0, :tok_rows].astype(jnp.float32) for block in home).astype(jnp.bfloat16)
-    home = sum(block[0, tok_rows:, : 4 * tok_rows].astype(jnp.float32) for block in home)
+    home = sum(block[0, tok_rows:].astype(jnp.float32) for block in home)
     score = jnp.sum(home.reshape(owners, 4, tok_rows), axis=1).T
     d_probs = jnp.sum(jnp.where(chosen, score[:, None, :], 0.0), axis=2)
     return d_tok, d_probs, d_gate, d_up, d_down

time: 161 us -> 140 us (0.87)
  Pallas kernels: 63.9 us -> 48 us
  waiting for transfers between devices: 48.4 us -> 44.5 us
  starting transfers between devices: 42.5 us -> 40.8 us
    pallas_call x1, Pallas kernels: 17 us -> 1.84 us  [join_call(): pl.pallas_call(join_kernel, in_specs=[LOOSE] * 2, out_specs=pl.BlockSpec(...]
    ppermute x13, waiting for transfers between devices: 38.6 us -> 35 us  [over_z(): lax.ppermute(array, 'ep', [(i, (i + shift * n_y) % ep) for i in range(ep)])]
  transfers between devices with their start and end apart: 39 -> 39, of which waited for: 14 -> 14; matrix products, arithmetic and copies ran while one was open for 0% -> 1% of each run, Pallas kernels for 29% -> 33%
where the time goes in v14:
time: 140 us; the launch traced here: 139 us
  Pallas kernels  48 us (34%)
  waiting for transfers between devices  44.5 us (32%)
  starting transfers between devices  40.8 us (29%)
  local copies, waits for them, and re-layouts  2.71 us (2%)
  other arithmetic  2.4 us (2%)
    ppermute x13, waiting for transfers between devices, over_z(): lax.ppermute(array, 'ep', [(i, (i + shift * n_y) % ep) for i in range(ep)])  35 us
    pallas_call x3, Pallas kernels, rows_call(): pl.pallas_call(functools.partial(rows_kernel, count, ways, capacity, slot...  31.6 us
    ppermute x13, starting transfers between devices, over_z(): lax.ppermute(array, 'ep', [(i, (i + shift * n_y) % ep) for i in range(ep)])  18.3 us
    ppermute x11, starting transfers between devices, over_y(): lax.ppermute(array, 'ep', [(i, i + 1 - 2 * (i % n_y)) for i in range(ep)])  11.4 us
    pallas_call x2, Pallas kernels, grads_call(): pl.pallas_call(functools.partial(grads_kernel, count, *starts, 2 * per),...  11.1 us
    ppermute x10, starting transfers between devices, over_x(): return lax.ppermute(array, 'tp', [(0, 1), (1, 0)])  10.3 us
    ppermute x10, waiting for transfers between devices, over_x(): return lax.ppermute(array, 'tp', [(0, 1), (1, 0)])  8.72 us
    pallas_call x1, Pallas kernels, weights_call(): pl.pallas_call(weights_kernel, grid_spec=pltpu.PrefetchScalarGridSpec(num...  3.41 us
  transfers between devices with their start and end apart: 39, of which 14 were waited for; matrix products, arithmetic and copies ran while one was open for 1% of the time, Pallas kernels for 33%

profile of v14, /device:TPU:0, one launch (start us, length us, event | category | flops | bytes accessed | tf_op | source)
XLA Modules:
  0.0 139.3 jit_solution(12838592586507839891)
XLA Ops:
  0.6 1.8 %join.1.refs_4_ = bf16[256,1024]{1,0:T(8,128)(2,1)} custom-call(bf16[128,1024]{1,0:T(8,128)(2,1)} %top_ref.1, bf16[128,1024]{1,0:T(8,128)(2,1)} %bottom_ref.1), custom_call_target="tpu_custom_call" | custom-call | bytes 1048576 | tf_op jit(solution)/shard_map/join/pallas_call | solution.py:180
  2.5 3.1 %collective-permute-start = (bf16[256,1024]{1,0:T(8,128)(2,1)}, bf16[256,1024]{1,0:T(8,128)(2,1)}, u32[]{:S(2)}, u32[]{:S(2)}) collective-permute-start(bf16[256,1024]{1,0:T(8,128)(2,1)} %join.1.refs_4_), channel_id=1, source_target_pairs={{0,4},{2,6},{4,8},{6,10},{8,12},{10,14},{12,0},{14,2},{1,5},{3,7},... | collective-permute-start | bytes 1572872 | tf_op jit(solution)/shard_map/ppermute | solution.py:456
  5.6 1.5 %collective-permute-start.1 = (bf16[256,1024]{1,0:T(8,128)(2,1)}, bf16[256,1024]{1,0:T(8,128)(2,1)}, u32[]{:S(2)}, u32[]{:S(2)}) collective-permute-start(bf16[256,1024]{1,0:T(8,128)(2,1)} %join.1.refs_4_), channel_id=1, source_target_pairs={{0,2},{2,0},{4,6},{6,4},{8,10},{10,8},{12,14},{14,12},{1,3},{3,1},... | collective-permute-start | bytes 1572872 | tf_op jit(solution)/shard_map/ppermute | solution.py:453
  7.1 1.5 %collective-permute-start.2 = (bf16[256,1024]{1,0:T(8,128)(2,1)}, bf16[256,1024]{1,0:T(8,128)(2,1)}, u32[]{:S(2)}, u32[]{:S(2)}) collective-permute-start(bf16[256,1024]{1,0:T(8,128)(2,1)} %join.1.refs_4_), channel_id=1, source_target_pairs={{0,1},{1,0},{2,3},{3,2},{4,5},{5,4},{6,7},{7,6},{8,9},{9,8},{10,11... | collective-permute-start | bytes 1572872 | tf_op jit(solution)/shard_map/ppermute | solution.py:447
  8.6 3.4 %weights.1 = (bf16[2048,768]{1,0:T(8,128)(2,1)S(1)}, bf16[384,2048]{1,0:T(8,128)(2,1)}) custom-call(s32[1]{0:T(128)} %bitcast.2.tp_ref, bf16[1,2048,384]{2,1,0:T(8,128)(2,1)} %wg_ref.1, bf16[1,2048,384]{2,1,0:T(8,128)(2,1)} %wu_ref.1, bf16[1,384,2048]{2,1,0:T(8,128)(2,1)} %wd_ref.1), custom_call_target="tpu_custom_call" | custom-call | bytes 9437184 | tf_op jit(solution)/shard_map/weights/pallas_call | solution.py:141
  12.0 7.8 %collective-permute-done.refs_4_ = bf16[256,1024]{1,0:T(8,128)(2,1)} collective-permute-done((bf16[256,1024]{1,0:T(8,128)(2,1)}, bf16[256,1024]{1,0:T(8,128)(2,1)}, u32[]{:S(2)}, u32[]{:S(2)}) %collective-permute-start) | collective-permute-done | bytes 524320 | tf_op jit(solution)/shard_map/ppermute | solution.py:456
  19.8 0.7 collective-permute-done.2.refs_5_
  21.0 1.6 %collective-permute-start.7 = (bf16[256,1024]{1,0:T(8,128)(2,1)}, bf16[256,1024]{1,0:T(8,128)(2,1)}, u32[]{:S(2)}, u32[]{:S(2)}) collective-permute-start(bf16[256,1024]{1,0:T(8,128)(2,1)} %collective-permute-done.refs_4_), channel_id=1, source_target_pairs={{0,4},{2,6},{4,8},{6,10},{8,12},{10,14},{12,0},{14,2},{1,5},{3,7},... | collective-permute-start | bytes 1572872 | tf_op jit(solution)/shard_map/ppermute | solution.py:456
  23.1 1.5 %collective-permute-start.5 = (bf16[256,1024]{1,0:T(8,128)(2,1)}, bf16[256,1024]{1,0:T(8,128)(2,1)S(1)}, u32[]{:S(2)}, u32[]{:S(2)}) collective-permute-start(bf16[256,1024]{1,0:T(8,128)(2,1)} %collective-permute-done.1.refs_6_), channel_id=1, source_target_pairs={{0,1},{1,0},{2,3},{3,2},{4,5},{5,4},{6,7},{7,6},{8,9},{9,8},{10,11... | collective-permute-start | bytes 1572872 | tf_op jit(solution)/shard_map/ppermute | solution.py:447
  24.6 12.3 %collective-permute-done.7.refs_8_ = bf16[256,1024]{1,0:T(8,128)(2,1)} collective-permute-done((bf16[256,1024]{1,0:T(8,128)(2,1)}, bf16[256,1024]{1,0:T(8,128)(2,1)}, u32[]{:S(2)}, u32[]{:S(2)}) %collective-permute-start.7) | collective-permute-done | bytes 524320 | tf_op jit(solution)/shard_map/ppermute | solution.py:456
  37.0 0.9 collective-permute-start.6
  37.9 0.8 copy-done.2
  38.7 0.8 copy-done
  39.5 1.1 collective-permute-start.10
  40.6 1.5 %collective-permute-start.11 = (bf16[256,1024]{1,0:T(8,128)(2,1)}, bf16[256,1024]{1,0:T(8,128)(2,1)}, u32[]{:S(2)}, u32[]{:S(2)}) collective-permute-start(bf16[256,1024]{1,0:T(8,128)(2,1)} %collective-permute-done.7.refs_8_), channel_id=1, source_target_pairs={{0,1},{1,0},{2,3},{3,2},{4,5},{5,4},{6,7},{7,6},{8,9},{9,8},{10,11... | collective-permute-start | bytes 1572872 | tf_op jit(solution)/shard_map/ppermute | solution.py:447
  42.8 1.0 copy-done.1
  43.9 9.5 %rows.3 = (bf16[144,5248]{1,0:T(8,128)(2,1)S(1)}, bf16[144,5248]{1,0:T(8,128)(2,1)S(1)}, bf16[1,136,1024]{2,1,0:T(8,128)(2,1)S(1)}, bf16[1,136,1024]{2,1,0:T(8,1...) custom-call(s32[3]{0:T(128)S(1)} %pad_add_fusion.where_ref, ...), custom_call_target="tpu_custom_call" | custom-call | flops 3170893824 | bytes 13631488 | tf_op jit(solution)/shard_map/rows/pallas_call | solution.py:321
  53.4 1.2 collective-permute-done.9.refs_4_
  55.4 0.9 collective-permute-start.14
  56.3 0.7 collective-permute-start.15
  57.0 3.5 %collective-permute-start.16 = (bf16[2,16,128]{2,1,0:T(8,128)(2,1)S(1)}, bf16[2,16,128]{2,1,0:T(8,128)(2,1)S(1)}, u32[]{:S(2)}, u32[]{:S(2)}) collective-permute-start(bf16[2,16,128]{2,1,0:T(8,128)(2,1)S(1)} %pad_maximum_fusion.refs_8_), channel_id=1, source_target_pairs={{0,8},{2,10},{4,12},{6,14},{8,0},{10,2},{12,4},{14,6},{1,9},{3,11}... | collective-permute-start | bytes 24584 | tf_op jit(solution)/shard_map/ppermute | solution.py:456
  60.5 5.5 %collective-permute-done.12.refs_5_ = bf16[256,1024]{1,0:T(8,128)(2,1)S(1)} collective-permute-done((bf16[256,1024]{1,0:T(8,128)(2,1)}, bf16[256,1024]{1,0:T(8,128)(2,1)S(1)}, u32[]{:S(2)}, u32[]{:S(2)}) %collective-permute-start.12) | collective-permute-done | bytes 524320 | tf_op jit(solution)/shard_map/ppermute | solution.py:447
  66.0 2.1 %collective-permute-done.13.refs_7_ = bf16[256,1024]{1,0:T(8,128)(2,1)S(1)} collective-permute-done((bf16[256,1024]{1,0:T(8,128)(2,1)S(1)}, bf16[256,1024]{1,0:T(8,128)(2,1)S(1)}, u32[]{:S(2)}, u32[]{:S(2)}) %collective-permute-start.13) | collective-permute-done | bytes 524320 | tf_op jit(solution)/shard_map/ppermute | solution.py:456
  68.2 1.1 collective-permute-start.18
  69.2 1.6 %collective-permute-start.19 = (bf16[256,1024]{1,0:T(8,128)(2,1)}, bf16[256,1024]{1,0:T(8,128)(2,1)S(1)}, u32[]{:S(2)}, u32[]{:S(2)}) collective-permute-start(bf16[256,1024]{1,0:T(8,128)(2,1)} %collective-permute-done.9.refs_4_), channel_id=1, source_target_pairs={{0,1},{1,0},{2,3},{3,2},{4,5},{5,4},{6,7},{7,6},{8,9},{9,8},{10,11... | collective-permute-start | bytes 1572872 | tf_op jit(solution)/shard_map/ppermute | solution.py:447
  70.9 2.6 %collective-permute-start.17 = (bf16[256,1024]{1,0:T(8,128)(2,1)S(1)}, bf16[256,1024]{1,0:T(8,128)(2,1)S(1)}, u32[]{:S(2)}, u32[]{:S(2)}) collective-permute-start(bf16[256,1024]{1,0:T(8,128)(2,1)S(1)} %copy-done.1), channel_id=1, source_target_pairs={{0,12},{2,14},{4,0},{6,2},{8,4},{10,6},{12,8},{14,10},{1,13},{3,15... | collective-permute-start | bytes 1572872 | tf_op jit(solution)/shard_map/ppermute | solution.py:456
  73.5 12.8 %rows.4 = (bf16[288,5248]{1,0:T(8,128)(2,1)S(1)}, bf16[288,5248]{1,0:T(8,128)(2,1)S(1)}, bf16[1,136,1024]{2,1,0:T(8,128)(2,1)S(1)}, bf16[1,136,1024]{2,1,0:T(8,1...) custom-call(s32[3]{0:T(128)S(1)} %pad_add_fusion.where_ref, ...), custom_call_target="tpu_custom_call" | custom-call | flops 6341787648 | bytes 17825792 | tf_op jit(solution)/shard_map/rows/pallas_call | solution.py:321
  86.5 0.8 collective-permute-start.21
  88.2 2.0 %collective-permute-done.21.refs_8_ = bf16[2,16,128]{2,1,0:T(8,128)(2,1)S(1)} collective-permute-done((bf16[2,16,128]{2,1,0:T(8,128)(2,1)S(1)}, bf16[2,16,128]{2,1,0:T(8,128)(2,1)S(1)}, u32[]{:S(2)}, u32[]{:S(2)}) %collective-permute-start.21) | collective-permute-done | bytes 8224 | tf_op jit(solution)/shard_map/ppermute | solution.py:456
  90.2 1.0 collective-permute-start.23
  91.2 9.3 %rows.5 = (bf16[144,5248]{1,0:T(8,128)(2,1)S(1)}, bf16[144,5248]{1,0:T(8,128)(2,1)S(1)}, bf16[1,136,1024]{2,1,0:T(8,128)(2,1)S(1)}, bf16[1,136,1024]{2,1,0:T(8,1...) custom-call(s32[3]{0:T(128)S(1)} %pad_add_fusion.where_ref, ...), custom_call_target="tpu_custom_call" | custom-call | flops 3170893824 | bytes 13631488 | tf_op jit(solution)/shard_map/rows/pallas_call | solution.py:321
  101.3 1.1 collective-permute-start.26
  102.4 0.8 collective-permute-start.24
  103.2 0.8 collective-permute-done.29.refs_5_
  104.5 1.0 collective-permute-start.32
  105.5 6.7 %grads.2 = (bf16[1,2048,384]{2,1,0:T(8,128)(2,1)}, bf16[1,2048,384]{2,1,0:T(8,128)(2,1)}) custom-call(s32[1]{0:T(128)} %bitcast.2.tp_ref, bf16[144,5248]{1,0:T(8,128)(2,1)S(1)} %get-tuple-element.88.refs_0_, bf16[144,5248]{1,0:T(8,128)(2,1)S(1)} %collective-permute-done.27.refs_1_, bf16[288,5248]{1,0:T(8,128)(2,1)S(1)} %get-tuple-element.102.refs_9_.refs_2_, ...), custom_call_target="tpu_custom_call" | custom-call | flops 3623878656 | bytes 6488064 | tf_op jit(solution)/shard_map/grads/pallas_call | solution.py:413
  112.7 1.5 %collective-permute-start.34 = (bf16[1,136,1024]{2,1,0:T(8,128)(2,1)S(1)}, bf16[1,136,1024]{2,1,0:T(8,128)(2,1)S(1)}, u32[]{:S(2)}, u32[]{:S(2)}) collective-permute-start(bf16[1,136,1024]{2,1,0:T(8,128)(2,1)S(1)} %get-tuple-element.129), channel_id=1, source_target_pairs={{0,1},{1,0},{2,3},{3,2},{4,5},{5,4},{6,7},{7,6},{8,9},{9,8},{10,11... | collective-permute-start | bytes 835592 | tf_op jit(solution)/shard_map/ppermute | solution.py:447
  114.7 1.1 collective-permute-start.30
  115.7 4.4 %grads.3 = bf16[1,384,2048]{2,1,0:T(8,128)(2,1)} custom-call(s32[1]{0:T(128)} %bitcast.2.tp_ref, bf16[144,5248]{1,0:T(8,128)(2,1)S(1)} %get-tuple-element.88.refs_0_, bf16[144,5248]{1,0:T(8,128)(2,1)S(1)} %collective-permute-done.27.refs_1_, bf16[288,5248]{1,0:T(8,128)(2,1)S(1)} %get-tuple-element.102.refs_9_.refs_2_, ...), custom_call_target="tpu_custom_call" | custom-call | flops 1811939328 | bytes 5603328 | tf_op jit(solution)/shard_map/grads/pallas_call | solution.py:413
  120.2 1.5 %collective-permute-done.34 = bf16[1,136,1024]{2,1,0:T(8,128)(2,1)S(1)} collective-permute-done((bf16[1,136,1024]{2,1,0:T(8,128)(2,1)S(1)}, bf16[1,136,1024]{2,1,0:T(8,128)(2,1)S(1)}, u32[]{:S(2)}, u32[]{:S(2)}) %collective-permute-start.34) | collective-permute-done | bytes 278560 | tf_op jit(solution)/shard_map/ppermute | solution.py:447
  121.8 1.8 %collective-permute-done.33 = bf16[1,136,1024]{2,1,0:T(8,128)(2,1)S(1)} collective-permute-done((bf16[1,136,1024]{2,1,0:T(8,128)(2,1)S(1)}, bf16[1,136,1024]{2,1,0:T(8,128)(2,1)S(1)}, u32[]{:S(2)}, u32[]{:S(2)}) %collective-permute-start.33) | collective-permute-done | bytes 278560 | tf_op jit(solution)/shard_map/ppermute | solution.py:456
  124.5 0.7 collective-permute-start.36
  125.2 1.2 collective-permute-start.38
  126.4 3.0 %collective-permute-start.37 = (bf16[1,136,1024]{2,1,0:T(8,128)(2,1)S(1)}, bf16[1,136,1024]{2,1,0:T(8,128)(2,1)S(1)}, u32[]{:S(2)}, u32[]{:S(2)}) collective-permute-start(bf16[1,136,1024]{2,1,0:T(8,128)(2,1)S(1)} %add_convert_fusion.2), channel_id=1, source_target_pairs={{0,12},{2,14},{4,0},{6,2},{8,4},{10,6},{12,8},{14,10},{1,13},{3,15... | collective-permute-start | bytes 835592 | tf_op jit(solution)/shard_map/ppermute | solution.py:456
  129.4 1.0 collective-permute-done.35
  130.4 5.4 %collective-permute-done.36 = bf16[1,136,1024]{2,1,0:T(8,128)(2,1)S(1)} collective-permute-done((bf16[1,136,1024]{2,1,0:T(8,128)(2,1)S(1)}, bf16[1,136,1024]{2,1,0:T(8,128)(2,1)S(1)}, u32[]{:S(2)}, u32[]{:S(2)}) %collective-permute-start.36) | collective-permute-done | bytes 278560 | tf_op jit(solution)/shard_map/ppermute | solution.py:456
  135.8 1.9 %collective-permute-done.37 = bf16[1,136,1024]{2,1,0:T(8,128)(2,1)S(1)} collective-permute-done((bf16[1,136,1024]{2,1,0:T(8,128)(2,1)S(1)}, bf16[1,136,1024]{2,1,0:T(8,128)(2,1)S(1)}, u32[]{:S(2)}, u32[]{:S(2)}) %collective-permute-start.37) | collective-permute-done | bytes 278560 | tf_op jit(solution)/shard_map/ppermute | solution.py:456
  138.4 0.9 fusion
  (65 shorter events, 7.5 us)
Async XLA Ops:
  2.5 17.3 %collective-permute-start = (bf16[256,1024]{1,0:T(8,128)(2,1)}, bf16[256,1024]{1,0:T(8,128)(2,1)}, u32[]{:S(2)}, u32[]{:S(2)}) collective-permute-start(bf16[256,1024]{1,0:T(8,128)(2,1)} %join.1.refs_4_), channel_id=1, source_target_pairs={{0,4},{2,6},{4,8},{6,10},{8,12},{10,14},{12,0},{14,2},{1,5},{3,7},... | collective-permute-start | bytes 1572872 | tf_op jit(solution)/shard_map/ppermute | solution.py:456
  5.6 14.3 %collective-permute-start.1 = (bf16[256,1024]{1,0:T(8,128)(2,1)}, bf16[256,1024]{1,0:T(8,128)(2,1)}, u32[]{:S(2)}, u32[]{:S(2)}) collective-permute-start(bf16[256,1024]{1,0:T(8,128)(2,1)} %join.1.refs_4_), channel_id=1, source_target_pairs={{0,2},{2,0},{4,6},{6,4},{8,10},{10,8},{12,14},{14,12},{1,3},{3,1},... | collective-permute-start | bytes 1572872 | tf_op jit(solution)/shard_map/ppermute | solution.py:453
  7.1 13.4 %collective-permute-start.2 = (bf16[256,1024]{1,0:T(8,128)(2,1)}, bf16[256,1024]{1,0:T(8,128)(2,1)}, u32[]{:S(2)}, u32[]{:S(2)}) collective-permute-start(bf16[256,1024]{1,0:T(8,128)(2,1)} %join.1.refs_4_), channel_id=1, source_target_pairs={{0,1},{1,0},{2,3},{3,2},{4,5},{5,4},{6,7},{7,6},{8,9},{9,8},{10,11... | collective-permute-start | bytes 1572872 | tf_op jit(solution)/shard_map/ppermute | solution.py:447
  8.6 16.0 %copy-start.5 = (bf16[128,8]{0,1:T(8,128)(2,1)S(1)}, bf16[128,8]{0,1:T(8,128)(2,1)}, u32[]{:S(2)}) copy-start(bf16[128,8]{0,1:T(8,128)(2,1)} %param.10) | copy-start | bytes 6148
  8.6 16.0 %copy-start.4 = (s32[128,8]{0,1:T(8,128)S(1)}, s32[128,8]{0,1:T(8,128)}, u32[]{:S(2)}) copy-start(s32[128,8]{0,1:T(8,128)} %param.9) | copy-start | bytes 12292
  20.5 22.3 %collective-permute-start.3 = (bf16[2048,768]{1,0:T(8,128)(2,1)S(1)}, bf16[2048,768]{1,0:T(8,128)(2,1)}, u32[]{:S(2)}, u32[]{:S(2)}) collective-permute-start(bf16[2048,768]{1,0:T(8,128)(2,1)S(1)} %get-tuple-element.73.refs_0_), channel_id=1, source_target_pairs={{0,16},{16,0},{1,17},{17,1},{2,18},{18,2},{3,19},{19,3},{4,20},{20... | collective-permute-start | bytes 9437192 | tf_op jit(solution)/shard_map/ppermute | solution.py:450
  20.5 22.3 %collective-permute-start.4 = (bf16[384,2048]{1,0:T(8,128)(2,1)}, bf16[384,2048]{1,0:T(8,128)(2,1)}, u32[]{:S(2)}, u32[]{:S(2)}) collective-permute-start(bf16[384,2048]{1,0:T(8,128)(2,1)} %get-tuple-element.74.refs_2_), channel_id=1, source_target_pairs={{0,16},{16,0},{1,17},{17,1},{2,18},{18,2},{3,19},{19,3},{4,20},{20... | collective-permute-start | bytes 4718600 | tf_op jit(solution)/shard_map/ppermute | solution.py:450
  21.0 15.9 %collective-permute-start.7 = (bf16[256,1024]{1,0:T(8,128)(2,1)}, bf16[256,1024]{1,0:T(8,128)(2,1)}, u32[]{:S(2)}, u32[]{:S(2)}) collective-permute-start(bf16[256,1024]{1,0:T(8,128)(2,1)} %collective-permute-done.refs_4_), channel_id=1, source_target_pairs={{0,4},{2,6},{4,8},{6,10},{8,12},{10,14},{12,0},{14,2},{1,5},{3,7},... | collective-permute-start | bytes 1572872 | tf_op jit(solution)/shard_map/ppermute | solution.py:456
  22.6 15.3 %collective-permute-start.8 = (bf16[256,1024]{1,0:T(8,128)(2,1)}, bf16[256,1024]{1,0:T(8,128)(2,1)S(1)}, u32[]{:S(2)}, u32[]{:S(2)}) collective-permute-start(bf16[256,1024]{1,0:T(8,128)(2,1)} %collective-permute-done.refs_4_), channel_id=1, source_target_pairs={{0,2},{2,0},{4,6},{6,4},{8,10},{10,8},{12,14},{14,12},{1,3},{3,1},... | collective-permute-start | bytes 1572872 | tf_op jit(solution)/shard_map/ppermute | solution.py:453
  23.1 15.6 %collective-permute-start.5 = (bf16[256,1024]{1,0:T(8,128)(2,1)}, bf16[256,1024]{1,0:T(8,128)(2,1)S(1)}, u32[]{:S(2)}, u32[]{:S(2)}) collective-permute-start(bf16[256,1024]{1,0:T(8,128)(2,1)} %collective-permute-done.1.refs_6_), channel_id=1, source_target_pairs={{0,1},{1,0},{2,3},{3,2},{4,5},{5,4},{6,7},{7,6},{8,9},{9,8},{10,11... | collective-permute-start | bytes 1572872 | tf_op jit(solution)/shard_map/ppermute | solution.py:447
  37.0 5.2 %collective-permute-start.6 = (bf16[16,128]{1,0:T(8,128)(2,1)S(1)}, bf16[16,128]{1,0:T(8,128)(2,1)S(1)}, u32[]{:S(2)}, u32[]{:S(2)}) collective-permute-start(bf16[16,128]{1,0:T(8,128)(2,1)S(1)} %get-tuple-element.138), channel_id=1, source_target_pairs={{0,2},{2,0},{4,6},{6,4},{8,10},{10,8},{12,14},{14,12},{1,3},{3,1},... | collective-permute-start | bytes 12296 | tf_op jit(solution)/shard_map/ppermute | solution.py:453
  37.9 0.9 copy-start.2
  38.7 0.8 copy-start
  39.5 13.8 %collective-permute-start.10 = (bf16[256,1024]{1,0:T(8,128)(2,1)}, bf16[256,1024]{1,0:T(8,128)(2,1)}, u32[]{:S(2)}, u32[]{:S(2)}) collective-permute-start(bf16[256,1024]{1,0:T(8,128)(2,1)} %collective-permute-done.7.refs_8_), channel_id=1, source_target_pairs={{0,2},{2,0},{4,6},{6,4},{8,10},{10,8},{12,14},{14,12},{1,3},{3,1},... | collective-permute-start | bytes 1572872 | tf_op jit(solution)/shard_map/ppermute | solution.py:453
  40.6 12.7 %collective-permute-start.11 = (bf16[256,1024]{1,0:T(8,128)(2,1)}, bf16[256,1024]{1,0:T(8,128)(2,1)}, u32[]{:S(2)}, u32[]{:S(2)}) collective-permute-start(bf16[256,1024]{1,0:T(8,128)(2,1)} %collective-permute-done.7.refs_8_), channel_id=1, source_target_pairs={{0,1},{1,0},{2,3},{3,2},{4,5},{5,4},{6,7},{7,6},{8,9},{9,8},{10,11... | collective-permute-start | bytes 1572872 | tf_op jit(solution)/shard_map/ppermute | solution.py:447
  42.1 12.5 %collective-permute-start.9 = (bf16[256,1024]{1,0:T(8,128)(2,1)}, bf16[256,1024]{1,0:T(8,128)(2,1)}, u32[]{:S(2)}, u32[]{:S(2)}) collective-permute-start(bf16[256,1024]{1,0:T(8,128)(2,1)} %join.1.refs_4_), channel_id=1, source_target_pairs={{0,12},{2,14},{4,0},{6,2},{8,4},{10,6},{12,8},{14,10},{1,13},{3,15... | collective-permute-start | bytes 1572872 | tf_op jit(solution)/shard_map/ppermute | solution.py:456
  42.8 1.0 copy-start.1
  43.8 29.7 %copy-start.3 = (bf16[256,1024]{1,0:T(8,128)(2,1)S(1)}, bf16[256,1024]{1,0:T(8,128)(2,1)}, u32[]{:S(2)}) copy-start(bf16[256,1024]{1,0:T(8,128)(2,1)} %copy-done.2) | copy-start | bytes 1572868
  54.6 11.4 %collective-permute-start.12 = (bf16[256,1024]{1,0:T(8,128)(2,1)}, bf16[256,1024]{1,0:T(8,128)(2,1)S(1)}, u32[]{:S(2)}, u32[]{:S(2)}) collective-permute-start(bf16[256,1024]{1,0:T(8,128)(2,1)} %collective-permute-done.refs_4_), channel_id=1, source_target_pairs={{0,1},{1,0},{2,3},{3,2},{4,5},{5,4},{6,7},{7,6},{8,9},{9,8},{10,11... | collective-permute-start | bytes 1572872 | tf_op jit(solution)/shard_map/ppermute | solution.py:447
  55.1 13.0 %collective-permute-start.13 = (bf16[256,1024]{1,0:T(8,128)(2,1)S(1)}, bf16[256,1024]{1,0:T(8,128)(2,1)S(1)}, u32[]{:S(2)}, u32[]{:S(2)}) collective-permute-start(bf16[256,1024]{1,0:T(8,128)(2,1)S(1)} %copy-done.1), channel_id=1, source_target_pairs={{0,4},{2,6},{4,8},{6,10},{8,12},{10,14},{12,0},{14,2},{1,5},{3,7},... | collective-permute-start | bytes 1572872 | tf_op jit(solution)/shard_map/ppermute | solution.py:456
  55.4 12.8 %collective-permute-start.14 = (bf16[256,1024]{1,0:T(8,128)(2,1)}, bf16[256,1024]{1,0:T(8,128)(2,1)S(1)}, u32[]{:S(2)}, u32[]{:S(2)}) collective-permute-start(bf16[256,1024]{1,0:T(8,128)(2,1)} %collective-permute-done.11.refs_9_), channel_id=1, source_target_pairs={{0,2},{2,0},{4,6},{6,4},{8,10},{10,8},{12,14},{14,12},{1,3},{3,1},... | collective-permute-start | bytes 1572872 | tf_op jit(solution)/shard_map/ppermute | solution.py:453
  56.3 17.2 %collective-permute-start.15 = (bf16[2,16,128]{2,1,0:T(8,128)(2,1)S(1)}, bf16[2,16,128]{2,1,0:T(8,128)(2,1)S(1)}, u32[]{:S(2)}, u32[]{:S(2)}) collective-permute-start(bf16[2,16,128]{2,1,0:T(8,128)(2,1)S(1)} %pad_maximum_fusion.refs_8_), channel_id=1, source_target_pairs={{0,4},{2,6},{4,8},{6,10},{8,12},{10,14},{12,0},{14,2},{1,5},{3,7},... | collective-permute-start | bytes 24584 | tf_op jit(solution)/shard_map/ppermute | solution.py:456
  57.0 16.6 %collective-permute-start.16 = (bf16[2,16,128]{2,1,0:T(8,128)(2,1)S(1)}, bf16[2,16,128]{2,1,0:T(8,128)(2,1)S(1)}, u32[]{:S(2)}, u32[]{:S(2)}) collective-permute-start(bf16[2,16,128]{2,1,0:T(8,128)(2,1)S(1)} %pad_maximum_fusion.refs_8_), channel_id=1, source_target_pairs={{0,8},{2,10},{4,12},{6,14},{8,0},{10,2},{12,4},{14,6},{1,9},{3,11}... | collective-permute-start | bytes 24584 | tf_op jit(solution)/shard_map/ppermute | solution.py:456
  68.2 18.2 %collective-permute-start.18 = (bf16[256,1024]{1,0:T(8,128)(2,1)}, bf16[256,1024]{1,0:T(8,128)(2,1)S(1)}, u32[]{:S(2)}, u32[]{:S(2)}) collective-permute-start(bf16[256,1024]{1,0:T(8,128)(2,1)} %collective-permute-done.9.refs_4_), channel_id=1, source_target_pairs={{0,2},{2,0},{4,6},{6,4},{8,10},{10,8},{12,14},{14,12},{1,3},{3,1},... | collective-permute-start | bytes 1572872 | tf_op jit(solution)/shard_map/ppermute | solution.py:453
  69.2 17.2 %collective-permute-start.19 = (bf16[256,1024]{1,0:T(8,128)(2,1)}, bf16[256,1024]{1,0:T(8,128)(2,1)S(1)}, u32[]{:S(2)}, u32[]{:S(2)}) collective-permute-start(bf16[256,1024]{1,0:T(8,128)(2,1)} %collective-permute-done.9.refs_4_), channel_id=1, source_target_pairs={{0,1},{1,0},{2,3},{3,2},{4,5},{5,4},{6,7},{7,6},{8,9},{9,8},{10,11... | collective-permute-start | bytes 1572872 | tf_op jit(solution)/shard_map/ppermute | solution.py:447
  70.9 15.5 %collective-permute-start.17 = (bf16[256,1024]{1,0:T(8,128)(2,1)S(1)}, bf16[256,1024]{1,0:T(8,128)(2,1)S(1)}, u32[]{:S(2)}, u32[]{:S(2)}) collective-permute-start(bf16[256,1024]{1,0:T(8,128)(2,1)S(1)} %copy-done.1), channel_id=1, source_target_pairs={{0,12},{2,14},{4,0},{6,2},{8,4},{10,6},{12,8},{14,10},{1,13},{3,15... | collective-permute-start | bytes 1572872 | tf_op jit(solution)/shard_map/ppermute | solution.py:456
  86.4 18.1 %collective-permute-start.28 = (bf16[288,5248]{1,0:T(8,128)(2,1)S(1)}, bf16[288,5248]{1,0:T(8,128)(2,1)S(1)}, u32[]{:S(2)}, u32[]{:S(2)}) collective-permute-start(bf16[288,5248]{1,0:T(8,128)(2,1)S(1)} %get-tuple-element.116), channel_id=1, source_target_pairs={{0,16},{16,0},{1,17},{17,1},{2,18},{18,2},{3,19},{19,3},{4,20},{20... | collective-permute-start | bytes 9068552 | tf_op jit(solution)/shard_map/ppermute | solution.py:450
  86.5 3.7 %collective-permute-start.21 = (bf16[2,16,128]{2,1,0:T(8,128)(2,1)S(1)}, bf16[2,16,128]{2,1,0:T(8,128)(2,1)S(1)}, u32[]{:S(2)}, u32[]{:S(2)}) collective-permute-start(bf16[2,16,128]{2,1,0:T(8,128)(2,1)S(1)} %pad_maximum_fusion.refs_8_), channel_id=1, source_target_pairs={{0,12},{2,14},{4,0},{6,2},{8,4},{10,6},{12,8},{14,10},{1,13},{3,15... | collective-permute-start | bytes 24584 | tf_op jit(solution)/shard_map/ppermute | solution.py:456
  87.3 15.1 %collective-permute-start.27 = (bf16[144,5248]{1,0:T(8,128)(2,1)S(1)}, bf16[144,5248]{1,0:T(8,128)(2,1)S(1)}, u32[]{:S(2)}, u32[]{:S(2)}) collective-permute-start(bf16[144,5248]{1,0:T(8,128)(2,1)S(1)} %get-tuple-element.115), channel_id=1, source_target_pairs={{0,16},{16,0},{1,17},{17,1},{2,18},{18,2},{3,19},{19,3},{4,20},{20... | collective-permute-start | bytes 4534280 | tf_op jit(solution)/shard_map/ppermute | solution.py:450
  87.5 13.1 %collective-permute-start.20 = (bf16[1,136,1024]{2,1,0:T(8,128)(2,1)S(1)}, bf16[1,136,1024]{2,1,0:T(8,128)(2,1)S(1)}, u32[]{:S(2)}, u32[]{:S(2)}) collective-permute-start(bf16[1,136,1024]{2,1,0:T(8,128)(2,1)S(1)} %get-tuple-element.101), channel_id=1, source_target_pairs={{0,12},{2,14},{4,0},{6,2},{8,4},{10,6},{12,8},{14,10},{1,13},{3,15... | collective-permute-start | bytes 835592 | tf_op jit(solution)/shard_map/ppermute | solution.py:456
  87.8 12.8 %collective-permute-start.22 = (bf16[1,136,1024]{2,1,0:T(8,128)(2,1)S(1)}, bf16[1,136,1024]{2,1,0:T(8,128)(2,1)S(1)}, u32[]{:S(2)}, u32[]{:S(2)}) collective-permute-start(bf16[1,136,1024]{2,1,0:T(8,128)(2,1)S(1)} %get-tuple-element.109), channel_id=1, source_target_pairs={{0,1},{1,0},{2,3},{3,2},{4,5},{5,4},{6,7},{7,6},{8,9},{9,8},{10,11... | collective-permute-start | bytes 835592 | tf_op jit(solution)/shard_map/ppermute | solution.py:447
  90.2 10.4 %collective-permute-start.23 = (bf16[1,136,1024]{2,1,0:T(8,128)(2,1)S(1)}, bf16[1,136,1024]{2,1,0:T(8,128)(2,1)S(1)}, u32[]{:S(2)}, u32[]{:S(2)}) collective-permute-start(bf16[1,136,1024]{2,1,0:T(8,128)(2,1)S(1)} %get-tuple-element.110), channel_id=1, source_target_pairs={{0,2},{2,0},{4,6},{6,4},{8,10},{10,8},{12,14},{14,12},{1,3},{3,1},... | collective-permute-start | bytes 835592 | tf_op jit(solution)/shard_map/ppermute | solution.py:453
  100.6 3.4 %collective-permute-start.29 = (bf16[144,5248]{1,0:T(8,128)(2,1)S(1)}, bf16[144,5248]{1,0:T(8,128)(2,1)S(1)}, u32[]{:S(2)}, u32[]{:S(2)}) collective-permute-start(bf16[144,5248]{1,0:T(8,128)(2,1)S(1)} %get-tuple-element.118), channel_id=1, source_target_pairs={{0,16},{16,0},{1,17},{17,1},{2,18},{18,2},{3,19},{19,3},{4,20},{20... | collective-permute-start | bytes 4534280 | tf_op jit(solution)/shard_map/ppermute | solution.py:450
  100.7 11.6 %collective-permute-start.25 = (bf16[1,136,1024]{2,1,0:T(8,128)(2,1)S(1)}, bf16[1,136,1024]{2,1,0:T(8,128)(2,1)S(1)}, u32[]{:S(2)}, u32[]{:S(2)}) collective-permute-start(bf16[1,136,1024]{2,1,0:T(8,128)(2,1)S(1)} %get-tuple-element.112), channel_id=1, source_target_pairs={{0,1},{1,0},{2,3},{3,2},{4,5},{5,4},{6,7},{7,6},{8,9},{9,8},{10,11... | collective-permute-start | bytes 835592 | tf_op jit(solution)/shard_map/ppermute | solution.py:447
  101.3 10.9 %collective-permute-start.26 = (bf16[1,136,1024]{2,1,0:T(8,128)(2,1)S(1)}, bf16[1,136,1024]{2,1,0:T(8,128)(2,1)S(1)}, u32[]{:S(2)}, u32[]{:S(2)}) collective-permute-start(bf16[1,136,1024]{2,1,0:T(8,128)(2,1)S(1)} %add_convert_fusion.5), channel_id=1, source_target_pairs={{0,2},{2,0},{4,6},{6,4},{8,10},{10,8},{12,14},{14,12},{1,3},{3,1},... | collective-permute-start | bytes 835592 | tf_op jit(solution)/shard_map/ppermute | solution.py:453
  102.4 10.2 %collective-permute-start.24 = (bf16[1,136,1024]{2,1,0:T(8,128)(2,1)S(1)}, bf16[1,136,1024]{2,1,0:T(8,128)(2,1)S(1)}, u32[]{:S(2)}, u32[]{:S(2)}) collective-permute-start(bf16[1,136,1024]{2,1,0:T(8,128)(2,1)S(1)} %get-tuple-element.111), channel_id=1, source_target_pairs={{0,4},{2,6},{4,8},{6,10},{8,12},{10,14},{12,0},{14,2},{1,5},{3,7},... | collective-permute-start | bytes 835592 | tf_op jit(solution)/shard_map/ppermute | solution.py:456
  104.0 17.8 %collective-permute-start.31 = (bf16[1,136,1024]{2,1,0:T(8,128)(2,1)S(1)}, bf16[1,136,1024]{2,1,0:T(8,128)(2,1)S(1)}, u32[]{:S(2)}, u32[]{:S(2)}) collective-permute-start(bf16[1,136,1024]{2,1,0:T(8,128)(2,1)S(1)} %get-tuple-element.122), channel_id=1, source_target_pairs={{0,1},{1,0},{2,3},{3,2},{4,5},{5,4},{6,7},{7,6},{8,9},{9,8},{10,11... | collective-permute-start | bytes 835592 | tf_op jit(solution)/shard_map/ppermute | solution.py:447
  104.5 17.3 %collective-permute-start.32 = (bf16[1,136,1024]{2,1,0:T(8,128)(2,1)S(1)}, bf16[1,136,1024]{2,1,0:T(8,128)(2,1)S(1)}, u32[]{:S(2)}, u32[]{:S(2)}) collective-permute-start(bf16[1,136,1024]{2,1,0:T(8,128)(2,1)S(1)} %get-tuple-element.123), channel_id=1, source_target_pairs={{0,2},{2,0},{4,6},{6,4},{8,10},{10,8},{12,14},{14,12},{1,3},{3,1},... | collective-permute-start | bytes 835592 | tf_op jit(solution)/shard_map/ppermute | solution.py:453
  112.7 9.0 %collective-permute-start.34 = (bf16[1,136,1024]{2,1,0:T(8,128)(2,1)S(1)}, bf16[1,136,1024]{2,1,0:T(8,128)(2,1)S(1)}, u32[]{:S(2)}, u32[]{:S(2)}) collective-permute-start(bf16[1,136,1024]{2,1,0:T(8,128)(2,1)S(1)} %get-tuple-element.129), channel_id=1, source_target_pairs={{0,1},{1,0},{2,3},{3,2},{4,5},{5,4},{6,7},{7,6},{8,9},{9,8},{10,11... | collective-permute-start | bytes 835592 | tf_op jit(solution)/shard_map/ppermute | solution.py:447
  114.3 9.4 %collective-permute-start.33 = (bf16[1,136,1024]{2,1,0:T(8,128)(2,1)S(1)}, bf16[1,136,1024]{2,1,0:T(8,128)(2,1)S(1)}, u32[]{:S(2)}, u32[]{:S(2)}) collective-permute-start(bf16[1,136,1024]{2,1,0:T(8,128)(2,1)S(1)} %add_convert_fusion.3), channel_id=1, source_target_pairs={{0,4},{2,6},{4,8},{6,10},{8,12},{10,14},{12,0},{14,2},{1,5},{3,7},... | collective-permute-start | bytes 835592 | tf_op jit(solution)/shard_map/ppermute | solution.py:456
  114.7 9.0 %collective-permute-start.30 = (bf16[1,136,1024]{2,1,0:T(8,128)(2,1)S(1)}, bf16[1,136,1024]{2,1,0:T(8,128)(2,1)S(1)}, u32[]{:S(2)}, u32[]{:S(2)}) collective-permute-start(bf16[1,136,1024]{2,1,0:T(8,128)(2,1)S(1)} %add_convert_fusion.4), channel_id=1, source_target_pairs={{0,2},{2,0},{4,6},{6,4},{8,10},{10,8},{12,14},{14,12},{1,3},{3,1},... | collective-permute-start | bytes 835592 | tf_op jit(solution)/shard_map/ppermute | solution.py:453
  123.7 6.7 %collective-permute-start.35 = (bf16[1,136,1024]{2,1,0:T(8,128)(2,1)S(1)}, bf16[1,136,1024]{2,1,0:T(8,128)(2,1)S(1)}, u32[]{:S(2)}, u32[]{:S(2)}) collective-permute-start(bf16[1,136,1024]{2,1,0:T(8,128)(2,1)S(1)} %add_convert_fusion.1), channel_id=1, source_target_pairs={{0,1},{1,0},{2,3},{3,2},{4,5},{5,4},{6,7},{7,6},{8,9},{9,8},{10,11... | collective-permute-start | bytes 835592 | tf_op jit(solution)/shard_map/ppermute | solution.py:447
  124.5 11.2 %collective-permute-start.36 = (bf16[1,136,1024]{2,1,0:T(8,128)(2,1)S(1)}, bf16[1,136,1024]{2,1,0:T(8,128)(2,1)S(1)}, u32[]{:S(2)}, u32[]{:S(2)}) collective-permute-start(bf16[1,136,1024]{2,1,0:T(8,128)(2,1)S(1)} %add_convert_fusion), channel_id=1, source_target_pairs={{0,4},{2,6},{4,8},{6,10},{8,12},{10,14},{12,0},{14,2},{1,5},{3,7},... | collective-permute-start | bytes 835592 | tf_op jit(solution)/shard_map/ppermute | solution.py:456
  125.2 10.6 %collective-permute-start.38 = (bf16[1,136,1024]{2,1,0:T(8,128)(2,1)S(1)}, bf16[1,136,1024]{2,1,0:T(8,128)(2,1)S(1)}, u32[]{:S(2)}, u32[]{:S(2)}) collective-permute-start(bf16[1,136,1024]{2,1,0:T(8,128)(2,1)S(1)} %get-tuple-element.136), channel_id=1, source_target_pairs={{0,2},{2,0},{4,6},{6,4},{8,10},{10,8},{12,14},{14,12},{1,3},{3,1},... | collective-permute-start | bytes 835592 | tf_op jit(solution)/shard_map/ppermute | solution.py:453
  126.4 11.3 %collective-permute-start.37 = (bf16[1,136,1024]{2,1,0:T(8,128)(2,1)S(1)}, bf16[1,136,1024]{2,1,0:T(8,128)(2,1)S(1)}, u32[]{:S(2)}, u32[]{:S(2)}) collective-permute-start(bf16[1,136,1024]{2,1,0:T(8,128)(2,1)S(1)} %add_convert_fusion.2), channel_id=1, source_target_pairs={{0,12},{2,14},{4,0},{6,2},{8,4},{10,6},{12,8},{14,10},{1,13},{3,15... | collective-permute-start | bytes 835592 | tf_op jit(solution)/shard_map/ppermute | solution.py:456

commit v15 on v14

--- a/solution.py
+++ b/solution.py
@@ -338,7 +338,7 @@
             transcendentals=2 * count * slots * part,
         ),
         name="rows",
-    )(where, *[pltpu.with_memory_space_constraint(item, pltpu.VMEM) for item in weights], *units, *tables, *after)
+    )(where, *[pltpu.with_memory_space_constraint(item, pltpu.VMEM) for item in (*weights, *units, *tables)], *after)
 
 
 def grads_kernel(count, wide, deep, blocks, tp_ref, *refs):
@@ -524,7 +524,7 @@
         return sum(block.astype(jnp.float32) for block in blocks).astype(jnp.bfloat16)
 
     items = [[(1, 1, 1)], [(1, 0, 1)], [(0, 0, 1)], [(0, 1, 0)], [(0, 1, 1)], [(0, 0, 0)], [(1, 0, 0)], [(1, 1, 0)]]
-    mine_1, other_1, x_2, x_20, x_1, y_1, z_1, keep_1, keep_2, keep_2y = rows_of([1, 2], items, [])
+    mine_1, other_1, x_2, x_20, x_1, y_1, z_1, keep_1, keep_2, keep_2y = rows_of([1, 2], items, tables[3:])
     other_1, x_2, x_20, x_1, y_1, z_1 = tied([other_1, x_2, x_20, x_1, y_1, z_1], arrived.values())
     from_x2, from_y1, from_z1 = over_x(x_2), over_y(y_1), over_z(z_1, -1)
     from_x20 = over_x(x_20)

time: 140 us -> 139 us (level)
  waiting for transfers between devices: 44.5 us -> 39.9 us
  starting transfers between devices: 40.8 us -> 45.2 us
    ppermute x13, starting transfers between devices: 18.3 us -> 21.3 us  [over_z(): lax.ppermute(array, 'ep', [(i, (i + shift * n_y) % ep) for i in range(ep)])]
    ppermute x13, waiting for transfers between devices: 35 us -> 32.8 us  [over_z(): lax.ppermute(array, 'ep', [(i, (i + shift * n_y) % ep) for i in range(ep)])]
    ppermute x10, waiting for transfers between devices: 8.72 us -> 7.06 us  [over_x(): return lax.ppermute(array, 'tp', [(0, 1), (1, 0)])]
  transfers between devices with their start and end apart: 39 -> 39, of which waited for: 14 -> 11; matrix products, arithmetic and copies ran while one was open for 1% -> 1% of each run, Pallas kernels for 33% -> 33%
where the time goes in v15:
time: 139 us
  Pallas kernels  48 us (35%)
  starting transfers between devices  45.2 us (33%)
  waiting for transfers between devices  39.9 us (29%)
  local copies, waits for them, and re-layouts  2.71 us (2%)
  other arithmetic  2.39 us (2%)
    ppermute x13, waiting for transfers between devices, over_z(): lax.ppermute(array, 'ep', [(i, (i + shift * n_y) % ep) for i in range(ep)])  32.8 us
    pallas_call x3, Pallas kernels, rows_call(): pl.pallas_call(functools.partial(rows_kernel, count, ways, capacity, slot...  31.6 us
    ppermute x13, starting transfers between devices, over_z(): lax.ppermute(array, 'ep', [(i, (i + shift * n_y) % ep) for i in range(ep)])  21.3 us
    ppermute x11, starting transfers between devices, over_y(): lax.ppermute(array, 'ep', [(i, i + 1 - 2 * (i % n_y)) for i in range(ep)])  11.7 us
    pallas_call x2, Pallas kernels, grads_call(): pl.pallas_call(functools.partial(grads_kernel, count, *starts, 2 * per),...  11.1 us
    ppermute x10, starting transfers between devices, over_x(): return lax.ppermute(array, 'tp', [(0, 1), (1, 0)])  11 us
    ppermute x10, waiting for transfers between devices, over_x(): return lax.ppermute(array, 'tp', [(0, 1), (1, 0)])  7.06 us
    pallas_call x1, Pallas kernels, weights_call(): pl.pallas_call(weights_kernel, grid_spec=pltpu.PrefetchScalarGridSpec(num...  3.41 us
  transfers between devices with their start and end apart: 39, of which 11 were waited for; matrix products, arithmetic and copies ran while one was open for 1% of the time, Pallas kernels for 33%

profile of v15, /device:TPU:0, one launch (start us, length us, event | category | flops | bytes accessed | tf_op | source)
XLA Modules:
  0.0 139.1 jit_solution(16512444228547743145)
XLA Ops:
  0.6 1.8 %join.1.refs_4_ = bf16[256,1024]{1,0:T(8,128)(2,1)} custom-call(bf16[128,1024]{1,0:T(8,128)(2,1)} %top_ref.1, bf16[128,1024]{1,0:T(8,128)(2,1)} %bottom_ref.1), custom_call_target="tpu_custom_call" | custom-call | bytes 1048576 | tf_op jit(solution)/shard_map/join/pallas_call | solution.py:180
  2.5 3.1 %collective-permute-start = (bf16[256,1024]{1,0:T(8,128)(2,1)}, bf16[256,1024]{1,0:T(8,128)(2,1)}, u32[]{:S(2)}, u32[]{:S(2)}) collective-permute-start(bf16[256,1024]{1,0:T(8,128)(2,1)} %join.1.refs_4_), channel_id=1, source_target_pairs={{0,4},{2,6},{4,8},{6,10},{8,12},{10,14},{12,0},{14,2},{1,5},{3,7},... | collective-permute-start | bytes 1572872 | tf_op jit(solution)/shard_map/ppermute | solution.py:456
  5.6 1.5 %collective-permute-start.1 = (bf16[256,1024]{1,0:T(8,128)(2,1)}, bf16[256,1024]{1,0:T(8,128)(2,1)}, u32[]{:S(2)}, u32[]{:S(2)}) collective-permute-start(bf16[256,1024]{1,0:T(8,128)(2,1)} %join.1.refs_4_), channel_id=1, source_target_pairs={{0,2},{2,0},{4,6},{6,4},{8,10},{10,8},{12,14},{14,12},{1,3},{3,1},... | collective-permute-start | bytes 1572872 | tf_op jit(solution)/shard_map/ppermute | solution.py:453
  7.1 1.5 %collective-permute-start.2 = (bf16[256,1024]{1,0:T(8,128)(2,1)}, bf16[256,1024]{1,0:T(8,128)(2,1)}, u32[]{:S(2)}, u32[]{:S(2)}) collective-permute-start(bf16[256,1024]{1,0:T(8,128)(2,1)} %join.1.refs_4_), channel_id=1, source_target_pairs={{0,1},{1,0},{2,3},{3,2},{4,5},{5,4},{6,7},{7,6},{8,9},{9,8},{10,11... | collective-permute-start | bytes 1572872 | tf_op jit(solution)/shard_map/ppermute | solution.py:447
  8.6 3.4 %weights.1 = (bf16[2048,768]{1,0:T(8,128)(2,1)S(1)}, bf16[384,2048]{1,0:T(8,128)(2,1)}) custom-call(s32[1]{0:T(128)} %bitcast.2.tp_ref, bf16[1,2048,384]{2,1,0:T(8,128)(2,1)} %wg_ref.1, bf16[1,2048,384]{2,1,0:T(8,128)(2,1)} %wu_ref.1, bf16[1,384,2048]{2,1,0:T(8,128)(2,1)} %wd_ref.1), custom_call_target="tpu_custom_call" | custom-call | bytes 9437184 | tf_op jit(solution)/shard_map/weights/pallas_call | solution.py:141
  12.0 7.8 %collective-permute-done.refs_4_ = bf16[256,1024]{1,0:T(8,128)(2,1)} collective-permute-done((bf16[256,1024]{1,0:T(8,128)(2,1)}, bf16[256,1024]{1,0:T(8,128)(2,1)}, u32[]{:S(2)}, u32[]{:S(2)}) %collective-permute-start) | collective-permute-done | bytes 524320 | tf_op jit(solution)/shard_map/ppermute | solution.py:456
  19.8 0.7 collective-permute-done.2.refs_5_
  21.0 1.6 %collective-permute-start.7 = (bf16[256,1024]{1,0:T(8,128)(2,1)}, bf16[256,1024]{1,0:T(8,128)(2,1)}, u32[]{:S(2)}, u32[]{:S(2)}) collective-permute-start(bf16[256,1024]{1,0:T(8,128)(2,1)} %collective-permute-done.refs_4_), channel_id=1, source_target_pairs={{0,4},{2,6},{4,8},{6,10},{8,12},{10,14},{12,0},{14,2},{1,5},{3,7},... | collective-permute-start | bytes 1572872 | tf_op jit(solution)/shard_map/ppermute | solution.py:456
  23.1 1.5 %collective-permute-start.5 = (bf16[256,1024]{1,0:T(8,128)(2,1)}, bf16[256,1024]{1,0:T(8,128)(2,1)S(1)}, u32[]{:S(2)}, u32[]{:S(2)}) collective-permute-start(bf16[256,1024]{1,0:T(8,128)(2,1)} %collective-permute-done.1.refs_6_), channel_id=1, source_target_pairs={{0,1},{1,0},{2,3},{3,2},{4,5},{5,4},{6,7},{7,6},{8,9},{9,8},{10,11... | collective-permute-start | bytes 1572872 | tf_op jit(solution)/shard_map/ppermute | solution.py:447
  24.6 12.3 %collective-permute-done.7.refs_8_ = bf16[256,1024]{1,0:T(8,128)(2,1)} collective-permute-done((bf16[256,1024]{1,0:T(8,128)(2,1)}, bf16[256,1024]{1,0:T(8,128)(2,1)}, u32[]{:S(2)}, u32[]{:S(2)}) %collective-permute-start.7) | collective-permute-done | bytes 524320 | tf_op jit(solution)/shard_map/ppermute | solution.py:456
  37.0 0.9 collective-permute-start.6
  37.9 0.8 copy-done.2
  38.7 0.8 copy-done
  39.5 1.1 collective-permute-start.10
  40.6 1.5 %collective-permute-start.11 = (bf16[256,1024]{1,0:T(8,128)(2,1)}, bf16[256,1024]{1,0:T(8,128)(2,1)}, u32[]{:S(2)}, u32[]{:S(2)}) collective-permute-start(bf16[256,1024]{1,0:T(8,128)(2,1)} %collective-permute-done.7.refs_8_), channel_id=1, source_target_pairs={{0,1},{1,0},{2,3},{3,2},{4,5},{5,4},{6,7},{7,6},{8,9},{9,8},{10,11... | collective-permute-start | bytes 1572872 | tf_op jit(solution)/shard_map/ppermute | solution.py:447
  42.8 1.0 copy-done.1
  43.9 9.5 %rows.3 = (bf16[144,5248]{1,0:T(8,128)(2,1)S(1)}, bf16[144,5248]{1,0:T(8,128)(2,1)S(1)}, bf16[1,136,1024]{2,1,0:T(8,128)(2,1)S(1)}, bf16[1,136,1024]{2,1,0:T(8,1...) custom-call(s32[3]{0:T(128)S(1)} %pad_add_fusion.where_ref, ...), custom_call_target="tpu_custom_call" | custom-call | flops 3170893824 | bytes 13631488 | tf_op jit(solution)/shard_map/rows/pallas_call | solution.py:321
  53.4 1.2 collective-permute-done.9.refs_4_
  55.4 0.9 collective-permute-start.14
  56.3 0.7 collective-permute-start.15
  57.0 3.5 %collective-permute-start.16 = (bf16[2,16,128]{2,1,0:T(8,128)(2,1)S(1)}, bf16[2,16,128]{2,1,0:T(8,128)(2,1)S(1)}, u32[]{:S(2)}, u32[]{:S(2)}) collective-permute-start(bf16[2,16,128]{2,1,0:T(8,128)(2,1)S(1)} %pad_maximum_fusion.refs_8_), channel_id=1, source_target_pairs={{0,8},{2,10},{4,12},{6,14},{8,0},{10,2},{12,4},{14,6},{1,9},{3,11}... | collective-permute-start | bytes 24584 | tf_op jit(solution)/shard_map/ppermute | solution.py:456
  60.5 5.5 %collective-permute-done.12.refs_5_ = bf16[256,1024]{1,0:T(8,128)(2,1)S(1)} collective-permute-done((bf16[256,1024]{1,0:T(8,128)(2,1)}, bf16[256,1024]{1,0:T(8,128)(2,1)S(1)}, u32[]{:S(2)}, u32[]{:S(2)}) %collective-permute-start.12) | collective-permute-done | bytes 524320 | tf_op jit(solution)/shard_map/ppermute | solution.py:447
  66.0 2.4 %collective-permute-start.17 = (bf16[2,16,128]{2,1,0:T(8,128)(2,1)S(1)}, bf16[2,16,128]{2,1,0:T(8,128)(2,1)S(1)}, u32[]{:S(2)}, u32[]{:S(2)}) collective-permute-start(bf16[2,16,128]{2,1,0:T(8,128)(2,1)S(1)} %pad_maximum_fusion.refs_8_), channel_id=1, source_target_pairs={{0,12},{2,14},{4,0},{6,2},{8,4},{10,6},{12,8},{14,10},{1,13},{3,15... | collective-permute-start | bytes 24584 | tf_op jit(solution)/shard_map/ppermute | solution.py:456
  68.4 1.2 collective-permute-start.19
  69.6 1.2 collective-permute-start.20
  70.8 2.8 %collective-permute-start.18 = (bf16[256,1024]{1,0:T(8,128)(2,1)S(1)}, bf16[256,1024]{1,0:T(8,128)(2,1)S(1)}, u32[]{:S(2)}, u32[]{:S(2)}) collective-permute-start(bf16[256,1024]{1,0:T(8,128)(2,1)S(1)} %copy-done.1), channel_id=1, source_target_pairs={{0,12},{2,14},{4,0},{6,2},{8,4},{10,6},{12,8},{14,10},{1,13},{3,15... | collective-permute-start | bytes 1572872 | tf_op jit(solution)/shard_map/ppermute | solution.py:456
  73.5 12.9 %rows.4 = (bf16[288,5248]{1,0:T(8,128)(2,1)S(1)}, bf16[288,5248]{1,0:T(8,128)(2,1)S(1)}, bf16[1,136,1024]{2,1,0:T(8,128)(2,1)S(1)}, bf16[1,136,1024]{2,1,0:T(8,1...) custom-call(s32[3]{0:T(128)S(1)} %pad_add_fusion.where_ref, ...), custom_call_target="tpu_custom_call" | custom-call | flops 6341787648 | bytes 17825792 | tf_op jit(solution)/shard_map/rows/pallas_call | solution.py:321
  87.0 0.8 collective-permute-start.21
  88.0 1.1 collective-permute-start.23
  89.2 9.3 %rows.5 = (bf16[144,5248]{1,0:T(8,128)(2,1)S(1)}, bf16[144,5248]{1,0:T(8,128)(2,1)S(1)}, bf16[1,136,1024]{2,1,0:T(8,128)(2,1)S(1)}, bf16[1,136,1024]{2,1,0:T(8,1...) custom-call(s32[3]{0:T(128)S(1)} %pad_add_fusion.where_ref, ...), custom_call_target="tpu_custom_call" | custom-call | flops 3170893824 | bytes 13631488 | tf_op jit(solution)/shard_map/rows/pallas_call | solution.py:321
  98.6 1.6 %collective-permute-start.25 = (bf16[1,136,1024]{2,1,0:T(8,128)(2,1)S(1)}, bf16[1,136,1024]{2,1,0:T(8,128)(2,1)S(1)}, u32[]{:S(2)}, u32[]{:S(2)}) collective-permute-start(bf16[1,136,1024]{2,1,0:T(8,128)(2,1)S(1)} %get-tuple-element.112), channel_id=1, source_target_pairs={{0,1},{1,0},{2,3},{3,2},{4,5},{5,4},{6,7},{7,6},{8,9},{9,8},{10,11... | collective-permute-start | bytes 835592 | tf_op jit(solution)/shard_map/ppermute | solution.py:447
  100.2 1.2 collective-permute-start.26
  101.5 1.3 collective-permute-start.24
  102.7 0.7 collective-permute-start.31
  103.4 1.1 collective-permute-start.32
  104.6 6.7 %grads.2 = (bf16[1,2048,384]{2,1,0:T(8,128)(2,1)}, bf16[1,2048,384]{2,1,0:T(8,128)(2,1)}) custom-call(s32[1]{0:T(128)} %bitcast.2.tp_ref, bf16[144,5248]{1,0:T(8,128)(2,1)S(1)} %get-tuple-element.88.refs_0_, bf16[144,5248]{1,0:T(8,128)(2,1)S(1)} %collective-permute-done.27.refs_1_, bf16[288,5248]{1,0:T(8,128)(2,1)S(1)} %get-tuple-element.102.refs_9_.refs_2_, ...), custom_call_target="tpu_custom_call" | custom-call | flops 3623878656 | bytes 6488064 | tf_op jit(solution)/shard_map/grads/pallas_call | solution.py:413
  111.7 0.9 collective-permute-start.34
  112.7 0.6 collective-permute-start.33
  113.5 1.1 collective-permute-start.30
  114.6 4.4 %grads.3 = bf16[1,384,2048]{2,1,0:T(8,128)(2,1)} custom-call(s32[1]{0:T(128)} %bitcast.2.tp_ref, bf16[144,5248]{1,0:T(8,128)(2,1)S(1)} %get-tuple-element.88.refs_0_, bf16[144,5248]{1,0:T(8,128)(2,1)S(1)} %collective-permute-done.27.refs_1_, bf16[288,5248]{1,0:T(8,128)(2,1)S(1)} %get-tuple-element.102.refs_9_.refs_2_, ...), custom_call_target="tpu_custom_call" | custom-call | flops 1811939328 | bytes 5603328 | tf_op jit(solution)/shard_map/grads/pallas_call | solution.py:413
  119.8 2.2 %collective-permute-done.33 = bf16[1,136,1024]{2,1,0:T(8,128)(2,1)S(1)} collective-permute-done((bf16[1,136,1024]{2,1,0:T(8,128)(2,1)S(1)}, bf16[1,136,1024]{2,1,0:T(8,128)(2,1)S(1)}, u32[]{:S(2)}, u32[]{:S(2)}) %collective-permute-start.33) | collective-permute-done | bytes 278560 | tf_op jit(solution)/shard_map/ppermute | solution.py:456
  122.0 1.4 %collective-permute-start.35 = (bf16[1,136,1024]{2,1,0:T(8,128)(2,1)S(1)}, bf16[1,136,1024]{2,1,0:T(8,128)(2,1)S(1)}, u32[]{:S(2)}, u32[]{:S(2)}) collective-permute-start(bf16[1,136,1024]{2,1,0:T(8,128)(2,1)S(1)} %add_convert_fusion.1), channel_id=1, source_target_pairs={{0,1},{1,0},{2,3},{3,2},{4,5},{5,4},{6,7},{7,6},{8,9},{9,8},{10,11... | collective-permute-start | bytes 835592 | tf_op jit(solution)/shard_map/ppermute | solution.py:447
  123.7 1.0 collective-permute-start.38
  124.6 3.7 %collective-permute-start.37 = (bf16[1,136,1024]{2,1,0:T(8,128)(2,1)S(1)}, bf16[1,136,1024]{2,1,0:T(8,128)(2,1)S(1)}, u32[]{:S(2)}, u32[]{:S(2)}) collective-permute-start(bf16[1,136,1024]{2,1,0:T(8,128)(2,1)S(1)} %add_convert_fusion.2), channel_id=1, source_target_pairs={{0,12},{2,14},{4,0},{6,2},{8,4},{10,6},{12,8},{14,10},{1,13},{3,15... | collective-permute-start | bytes 835592 | tf_op jit(solution)/shard_map/ppermute | solution.py:456
  128.6 6.2 %collective-permute-done.36 = bf16[1,136,1024]{2,1,0:T(8,128)(2,1)S(1)} collective-permute-done((bf16[1,136,1024]{2,1,0:T(8,128)(2,1)S(1)}, bf16[1,136,1024]{2,1,0:T(8,128)(2,1)S(1)}, u32[]{:S(2)}, u32[]{:S(2)}) %collective-permute-start.36) | collective-permute-done | bytes 278560 | tf_op jit(solution)/shard_map/ppermute | solution.py:456
  134.8 2.6 %collective-permute-done.37 = bf16[1,136,1024]{2,1,0:T(8,128)(2,1)S(1)} collective-permute-done((bf16[1,136,1024]{2,1,0:T(8,128)(2,1)S(1)}, bf16[1,136,1024]{2,1,0:T(8,128)(2,1)S(1)}, u32[]{:S(2)}, u32[]{:S(2)}) %collective-permute-start.37) | collective-permute-done | bytes 278560 | tf_op jit(solution)/shard_map/ppermute | solution.py:456
  137.5 0.6 select_reduce_fusion
  138.1 0.9 fusion
  (65 shorter events, 5.6 us)
Async XLA Ops:
  2.5 17.3 %collective-permute-start = (bf16[256,1024]{1,0:T(8,128)(2,1)}, bf16[256,1024]{1,0:T(8,128)(2,1)}, u32[]{:S(2)}, u32[]{:S(2)}) collective-permute-start(bf16[256,1024]{1,0:T(8,128)(2,1)} %join.1.refs_4_), channel_id=1, source_target_pairs={{0,4},{2,6},{4,8},{6,10},{8,12},{10,14},{12,0},{14,2},{1,5},{3,7},... | collective-permute-start | bytes 1572872 | tf_op jit(solution)/shard_map/ppermute | solution.py:456
  5.6 14.3 %collective-permute-start.1 = (bf16[256,1024]{1,0:T(8,128)(2,1)}, bf16[256,1024]{1,0:T(8,128)(2,1)}, u32[]{:S(2)}, u32[]{:S(2)}) collective-permute-start(bf16[256,1024]{1,0:T(8,128)(2,1)} %join.1.refs_4_), channel_id=1, source_target_pairs={{0,2},{2,0},{4,6},{6,4},{8,10},{10,8},{12,14},{14,12},{1,3},{3,1},... | collective-permute-start | bytes 1572872 | tf_op jit(solution)/shard_map/ppermute | solution.py:453
  7.1 13.4 %collective-permute-start.2 = (bf16[256,1024]{1,0:T(8,128)(2,1)}, bf16[256,1024]{1,0:T(8,128)(2,1)}, u32[]{:S(2)}, u32[]{:S(2)}) collective-permute-start(bf16[256,1024]{1,0:T(8,128)(2,1)} %join.1.refs_4_), channel_id=1, source_target_pairs={{0,1},{1,0},{2,3},{3,2},{4,5},{5,4},{6,7},{7,6},{8,9},{9,8},{10,11... | collective-permute-start | bytes 1572872 | tf_op jit(solution)/shard_map/ppermute | solution.py:447
  8.6 16.0 %copy-start.5 = (bf16[128,8]{0,1:T(8,128)(2,1)S(1)}, bf16[128,8]{0,1:T(8,128)(2,1)}, u32[]{:S(2)}) copy-start(bf16[128,8]{0,1:T(8,128)(2,1)} %param.10) | copy-start | bytes 6148
  8.6 16.0 %copy-start.4 = (s32[128,8]{0,1:T(8,128)S(1)}, s32[128,8]{0,1:T(8,128)}, u32[]{:S(2)}) copy-start(s32[128,8]{0,1:T(8,128)} %param.9) | copy-start | bytes 12292
  20.5 22.3 %collective-permute-start.3 = (bf16[2048,768]{1,0:T(8,128)(2,1)S(1)}, bf16[2048,768]{1,0:T(8,128)(2,1)}, u32[]{:S(2)}, u32[]{:S(2)}) collective-permute-start(bf16[2048,768]{1,0:T(8,128)(2,1)S(1)} %get-tuple-element.73.refs_0_), channel_id=1, source_target_pairs={{0,16},{16,0},{1,17},{17,1},{2,18},{18,2},{3,19},{19,3},{4,20},{20... | collective-permute-start | bytes 9437192 | tf_op jit(solution)/shard_map/ppermute | solution.py:450
  20.5 22.3 %collective-permute-start.4 = (bf16[384,2048]{1,0:T(8,128)(2,1)}, bf16[384,2048]{1,0:T(8,128)(2,1)}, u32[]{:S(2)}, u32[]{:S(2)}) collective-permute-start(bf16[384,2048]{1,0:T(8,128)(2,1)} %get-tuple-element.74.refs_2_), channel_id=1, source_target_pairs={{0,16},{16,0},{1,17},{17,1},{2,18},{18,2},{3,19},{19,3},{4,20},{20... | collective-permute-start | bytes 4718600 | tf_op jit(solution)/shard_map/ppermute | solution.py:450
  21.0 15.9 %collective-permute-start.7 = (bf16[256,1024]{1,0:T(8,128)(2,1)}, bf16[256,1024]{1,0:T(8,128)(2,1)}, u32[]{:S(2)}, u32[]{:S(2)}) collective-permute-start(bf16[256,1024]{1,0:T(8,128)(2,1)} %collective-permute-done.refs_4_), channel_id=1, source_target_pairs={{0,4},{2,6},{4,8},{6,10},{8,12},{10,14},{12,0},{14,2},{1,5},{3,7},... | collective-permute-start | bytes 1572872 | tf_op jit(solution)/shard_map/ppermute | solution.py:456
  22.6 15.3 %collective-permute-start.8 = (bf16[256,1024]{1,0:T(8,128)(2,1)}, bf16[256,1024]{1,0:T(8,128)(2,1)S(1)}, u32[]{:S(2)}, u32[]{:S(2)}) collective-permute-start(bf16[256,1024]{1,0:T(8,128)(2,1)} %collective-permute-done.refs_4_), channel_id=1, source_target_pairs={{0,2},{2,0},{4,6},{6,4},{8,10},{10,8},{12,14},{14,12},{1,3},{3,1},... | collective-permute-start | bytes 1572872 | tf_op jit(solution)/shard_map/ppermute | solution.py:453
  23.1 15.6 %collective-permute-start.5 = (bf16[256,1024]{1,0:T(8,128)(2,1)}, bf16[256,1024]{1,0:T(8,128)(2,1)S(1)}, u32[]{:S(2)}, u32[]{:S(2)}) collective-permute-start(bf16[256,1024]{1,0:T(8,128)(2,1)} %collective-permute-done.1.refs_6_), channel_id=1, source_target_pairs={{0,1},{1,0},{2,3},{3,2},{4,5},{5,4},{6,7},{7,6},{8,9},{9,8},{10,11... | collective-permute-start | bytes 1572872 | tf_op jit(solution)/shard_map/ppermute | solution.py:447
  37.0 5.2 %collective-permute-start.6 = (bf16[16,128]{1,0:T(8,128)(2,1)S(1)}, bf16[16,128]{1,0:T(8,128)(2,1)S(1)}, u32[]{:S(2)}, u32[]{:S(2)}) collective-permute-start(bf16[16,128]{1,0:T(8,128)(2,1)S(1)} %get-tuple-element.138), channel_id=1, source_target_pairs={{0,2},{2,0},{4,6},{6,4},{8,10},{10,8},{12,14},{14,12},{1,3},{3,1},... | collective-permute-start | bytes 12296 | tf_op jit(solution)/shard_map/ppermute | solution.py:453
  37.9 0.9 copy-start.2
  38.7 0.8 copy-start
  39.5 13.8 %collective-permute-start.10 = (bf16[256,1024]{1,0:T(8,128)(2,1)}, bf16[256,1024]{1,0:T(8,128)(2,1)}, u32[]{:S(2)}, u32[]{:S(2)}) collective-permute-start(bf16[256,1024]{1,0:T(8,128)(2,1)} %collective-permute-done.7.refs_8_), channel_id=1, source_target_pairs={{0,2},{2,0},{4,6},{6,4},{8,10},{10,8},{12,14},{14,12},{1,3},{3,1},... | collective-permute-start | bytes 1572872 | tf_op jit(solution)/shard_map/ppermute | solution.py:453
  40.6 12.7 %collective-permute-start.11 = (bf16[256,1024]{1,0:T(8,128)(2,1)}, bf16[256,1024]{1,0:T(8,128)(2,1)}, u32[]{:S(2)}, u32[]{:S(2)}) collective-permute-start(bf16[256,1024]{1,0:T(8,128)(2,1)} %collective-permute-done.7.refs_8_), channel_id=1, source_target_pairs={{0,1},{1,0},{2,3},{3,2},{4,5},{5,4},{6,7},{7,6},{8,9},{9,8},{10,11... | collective-permute-start | bytes 1572872 | tf_op jit(solution)/shard_map/ppermute | solution.py:447
  42.1 12.5 %collective-permute-start.9 = (bf16[256,1024]{1,0:T(8,128)(2,1)}, bf16[256,1024]{1,0:T(8,128)(2,1)}, u32[]{:S(2)}, u32[]{:S(2)}) collective-permute-start(bf16[256,1024]{1,0:T(8,128)(2,1)} %join.1.refs_4_), channel_id=1, source_target_pairs={{0,12},{2,14},{4,0},{6,2},{8,4},{10,6},{12,8},{14,10},{1,13},{3,15... | collective-permute-start | bytes 1572872 | tf_op jit(solution)/shard_map/ppermute | solution.py:456
  42.8 1.0 copy-start.1
  43.8 29.7 %copy-start.3 = (bf16[256,1024]{1,0:T(8,128)(2,1)S(1)}, bf16[256,1024]{1,0:T(8,128)(2,1)}, u32[]{:S(2)}) copy-start(bf16[256,1024]{1,0:T(8,128)(2,1)} %copy-done.2) | copy-start | bytes 1572868
  54.6 11.4 %collective-permute-start.12 = (bf16[256,1024]{1,0:T(8,128)(2,1)}, bf16[256,1024]{1,0:T(8,128)(2,1)S(1)}, u32[]{:S(2)}, u32[]{:S(2)}) collective-permute-start(bf16[256,1024]{1,0:T(8,128)(2,1)} %collective-permute-done.refs_4_), channel_id=1, source_target_pairs={{0,1},{1,0},{2,3},{3,2},{4,5},{5,4},{6,7},{7,6},{8,9},{9,8},{10,11... | collective-permute-start | bytes 1572872 | tf_op jit(solution)/shard_map/ppermute | solution.py:447
  55.1 13.3 %collective-permute-start.13 = (bf16[256,1024]{1,0:T(8,128)(2,1)S(1)}, bf16[256,1024]{1,0:T(8,128)(2,1)S(1)}, u32[]{:S(2)}, u32[]{:S(2)}) collective-permute-start(bf16[256,1024]{1,0:T(8,128)(2,1)S(1)} %copy-done.1), channel_id=1, source_target_pairs={{0,4},{2,6},{4,8},{6,10},{8,12},{10,14},{12,0},{14,2},{1,5},{3,7},... | collective-permute-start | bytes 1572872 | tf_op jit(solution)/shard_map/ppermute | solution.py:456
  55.4 13.0 %collective-permute-start.14 = (bf16[256,1024]{1,0:T(8,128)(2,1)}, bf16[256,1024]{1,0:T(8,128)(2,1)S(1)}, u32[]{:S(2)}, u32[]{:S(2)}) collective-permute-start(bf16[256,1024]{1,0:T(8,128)(2,1)} %collective-permute-done.11.refs_9_), channel_id=1, source_target_pairs={{0,2},{2,0},{4,6},{6,4},{8,10},{10,8},{12,14},{14,12},{1,3},{3,1},... | collective-permute-start | bytes 1572872 | tf_op jit(solution)/shard_map/ppermute | solution.py:453
  56.3 14.4 %collective-permute-start.15 = (bf16[2,16,128]{2,1,0:T(8,128)(2,1)S(1)}, bf16[2,16,128]{2,1,0:T(8,128)(2,1)S(1)}, u32[]{:S(2)}, u32[]{:S(2)}) collective-permute-start(bf16[2,16,128]{2,1,0:T(8,128)(2,1)S(1)} %pad_maximum_fusion.refs_8_), channel_id=1, source_target_pairs={{0,4},{2,6},{4,8},{6,10},{8,12},{10,14},{12,0},{14,2},{1,5},{3,7},... | collective-permute-start | bytes 24584 | tf_op jit(solution)/shard_map/ppermute | solution.py:456
  57.0 16.6 %collective-permute-start.16 = (bf16[2,16,128]{2,1,0:T(8,128)(2,1)S(1)}, bf16[2,16,128]{2,1,0:T(8,128)(2,1)S(1)}, u32[]{:S(2)}, u32[]{:S(2)}) collective-permute-start(bf16[2,16,128]{2,1,0:T(8,128)(2,1)S(1)} %pad_maximum_fusion.refs_8_), channel_id=1, source_target_pairs={{0,8},{2,10},{4,12},{6,14},{8,0},{10,2},{12,4},{14,6},{1,9},{3,11}... | collective-permute-start | bytes 24584 | tf_op jit(solution)/shard_map/ppermute | solution.py:456
  66.0 7.5 %collective-permute-start.17 = (bf16[2,16,128]{2,1,0:T(8,128)(2,1)S(1)}, bf16[2,16,128]{2,1,0:T(8,128)(2,1)S(1)}, u32[]{:S(2)}, u32[]{:S(2)}) collective-permute-start(bf16[2,16,128]{2,1,0:T(8,128)(2,1)S(1)} %pad_maximum_fusion.refs_8_), channel_id=1, source_target_pairs={{0,12},{2,14},{4,0},{6,2},{8,4},{10,6},{12,8},{14,10},{1,13},{3,15... | collective-permute-start | bytes 24584 | tf_op jit(solution)/shard_map/ppermute | solution.py:456
  68.4 18.0 %collective-permute-start.19 = (bf16[256,1024]{1,0:T(8,128)(2,1)}, bf16[256,1024]{1,0:T(8,128)(2,1)S(1)}, u32[]{:S(2)}, u32[]{:S(2)}) collective-permute-start(bf16[256,1024]{1,0:T(8,128)(2,1)} %collective-permute-done.9.refs_4_), channel_id=1, source_target_pairs={{0,2},{2,0},{4,6},{6,4},{8,10},{10,8},{12,14},{14,12},{1,3},{3,1},... | collective-permute-start | bytes 1572872 | tf_op jit(solution)/shard_map/ppermute | solution.py:453
  69.6 16.8 %collective-permute-start.20 = (bf16[256,1024]{1,0:T(8,128)(2,1)}, bf16[256,1024]{1,0:T(8,128)(2,1)S(1)}, u32[]{:S(2)}, u32[]{:S(2)}) collective-permute-start(bf16[256,1024]{1,0:T(8,128)(2,1)} %collective-permute-done.9.refs_4_), channel_id=1, source_target_pairs={{0,1},{1,0},{2,3},{3,2},{4,5},{5,4},{6,7},{7,6},{8,9},{9,8},{10,11... | collective-permute-start | bytes 1572872 | tf_op jit(solution)/shard_map/ppermute | solution.py:447
  70.8 15.6 %collective-permute-start.18 = (bf16[256,1024]{1,0:T(8,128)(2,1)S(1)}, bf16[256,1024]{1,0:T(8,128)(2,1)S(1)}, u32[]{:S(2)}, u32[]{:S(2)}) collective-permute-start(bf16[256,1024]{1,0:T(8,128)(2,1)S(1)} %copy-done.1), channel_id=1, source_target_pairs={{0,12},{2,14},{4,0},{6,2},{8,4},{10,6},{12,8},{14,10},{1,13},{3,15... | collective-permute-start | bytes 1572872 | tf_op jit(solution)/shard_map/ppermute | solution.py:456
  86.4 17.0 %collective-permute-start.28 = (bf16[288,5248]{1,0:T(8,128)(2,1)S(1)}, bf16[288,5248]{1,0:T(8,128)(2,1)S(1)}, u32[]{:S(2)}, u32[]{:S(2)}) collective-permute-start(bf16[288,5248]{1,0:T(8,128)(2,1)S(1)} %get-tuple-element.116), channel_id=1, source_target_pairs={{0,16},{16,0},{1,17},{17,1},{2,18},{18,2},{3,19},{19,3},{4,20},{20... | collective-permute-start | bytes 9068552 | tf_op jit(solution)/shard_map/ppermute | solution.py:450
  86.5 14.9 %collective-permute-start.27 = (bf16[144,5248]{1,0:T(8,128)(2,1)S(1)}, bf16[144,5248]{1,0:T(8,128)(2,1)S(1)}, u32[]{:S(2)}, u32[]{:S(2)}) collective-permute-start(bf16[144,5248]{1,0:T(8,128)(2,1)S(1)} %get-tuple-element.115), channel_id=1, source_target_pairs={{0,16},{16,0},{1,17},{17,1},{2,18},{18,2},{3,19},{19,3},{4,20},{20... | collective-permute-start | bytes 4534280 | tf_op jit(solution)/shard_map/ppermute | solution.py:450
  87.0 11.5 %collective-permute-start.21 = (bf16[1,136,1024]{2,1,0:T(8,128)(2,1)S(1)}, bf16[1,136,1024]{2,1,0:T(8,128)(2,1)S(1)}, u32[]{:S(2)}, u32[]{:S(2)}) collective-permute-start(bf16[1,136,1024]{2,1,0:T(8,128)(2,1)S(1)} %get-tuple-element.101), channel_id=1, source_target_pairs={{0,12},{2,14},{4,0},{6,2},{8,4},{10,6},{12,8},{14,10},{1,13},{3,15... | collective-permute-start | bytes 835592 | tf_op jit(solution)/shard_map/ppermute | solution.py:456
  87.8 10.7 %collective-permute-start.22 = (bf16[1,136,1024]{2,1,0:T(8,128)(2,1)S(1)}, bf16[1,136,1024]{2,1,0:T(8,128)(2,1)S(1)}, u32[]{:S(2)}, u32[]{:S(2)}) collective-permute-start(bf16[1,136,1024]{2,1,0:T(8,128)(2,1)S(1)} %get-tuple-element.109), channel_id=1, source_target_pairs={{0,1},{1,0},{2,3},{3,2},{4,5},{5,4},{6,7},{7,6},{8,9},{9,8},{10,11... | collective-permute-start | bytes 835592 | tf_op jit(solution)/shard_map/ppermute | solution.py:447
  88.0 10.5 %collective-permute-start.23 = (bf16[1,136,1024]{2,1,0:T(8,128)(2,1)S(1)}, bf16[1,136,1024]{2,1,0:T(8,128)(2,1)S(1)}, u32[]{:S(2)}, u32[]{:S(2)}) collective-permute-start(bf16[1,136,1024]{2,1,0:T(8,128)(2,1)S(1)} %get-tuple-element.110), channel_id=1, source_target_pairs={{0,2},{2,0},{4,6},{6,4},{8,10},{10,8},{12,14},{14,12},{1,3},{3,1},... | collective-permute-start | bytes 835592 | tf_op jit(solution)/shard_map/ppermute | solution.py:453
  98.5 4.2 %collective-permute-start.29 = (bf16[144,5248]{1,0:T(8,128)(2,1)S(1)}, bf16[144,5248]{1,0:T(8,128)(2,1)S(1)}, u32[]{:S(2)}, u32[]{:S(2)}) collective-permute-start(bf16[144,5248]{1,0:T(8,128)(2,1)S(1)} %get-tuple-element.118), channel_id=1, source_target_pairs={{0,16},{16,0},{1,17},{17,1},{2,18},{18,2},{3,19},{19,3},{4,20},{20... | collective-permute-start | bytes 4534280 | tf_op jit(solution)/shard_map/ppermute | solution.py:450
  98.6 12.7 %collective-permute-start.25 = (bf16[1,136,1024]{2,1,0:T(8,128)(2,1)S(1)}, bf16[1,136,1024]{2,1,0:T(8,128)(2,1)S(1)}, u32[]{:S(2)}, u32[]{:S(2)}) collective-permute-start(bf16[1,136,1024]{2,1,0:T(8,128)(2,1)S(1)} %get-tuple-element.112), channel_id=1, source_target_pairs={{0,1},{1,0},{2,3},{3,2},{4,5},{5,4},{6,7},{7,6},{8,9},{9,8},{10,11... | collective-permute-start | bytes 835592 | tf_op jit(solution)/shard_map/ppermute | solution.py:447
  100.2 11.1 %collective-permute-start.26 = (bf16[1,136,1024]{2,1,0:T(8,128)(2,1)S(1)}, bf16[1,136,1024]{2,1,0:T(8,128)(2,1)S(1)}, u32[]{:S(2)}, u32[]{:S(2)}) collective-permute-start(bf16[1,136,1024]{2,1,0:T(8,128)(2,1)S(1)} %add_convert_fusion.5), channel_id=1, source_target_pairs={{0,2},{2,0},{4,6},{6,4},{8,10},{10,8},{12,14},{14,12},{1,3},{3,1},... | collective-permute-start | bytes 835592 | tf_op jit(solution)/shard_map/ppermute | solution.py:453
  101.5 10.2 %collective-permute-start.24 = (bf16[1,136,1024]{2,1,0:T(8,128)(2,1)S(1)}, bf16[1,136,1024]{2,1,0:T(8,128)(2,1)S(1)}, u32[]{:S(2)}, u32[]{:S(2)}) collective-permute-start(bf16[1,136,1024]{2,1,0:T(8,128)(2,1)S(1)} %get-tuple-element.111), channel_id=1, source_target_pairs={{0,4},{2,6},{4,8},{6,10},{8,12},{10,14},{12,0},{14,2},{1,5},{3,7},... | collective-permute-start | bytes 835592 | tf_op jit(solution)/shard_map/ppermute | solution.py:456
  102.7 17.0 %collective-permute-start.31 = (bf16[1,136,1024]{2,1,0:T(8,128)(2,1)S(1)}, bf16[1,136,1024]{2,1,0:T(8,128)(2,1)S(1)}, u32[]{:S(2)}, u32[]{:S(2)}) collective-permute-start(bf16[1,136,1024]{2,1,0:T(8,128)(2,1)S(1)} %get-tuple-element.122), channel_id=1, source_target_pairs={{0,1},{1,0},{2,3},{3,2},{4,5},{5,4},{6,7},{7,6},{8,9},{9,8},{10,11... | collective-permute-start | bytes 835592 | tf_op jit(solution)/shard_map/ppermute | solution.py:447
  103.4 16.3 %collective-permute-start.32 = (bf16[1,136,1024]{2,1,0:T(8,128)(2,1)S(1)}, bf16[1,136,1024]{2,1,0:T(8,128)(2,1)S(1)}, u32[]{:S(2)}, u32[]{:S(2)}) collective-permute-start(bf16[1,136,1024]{2,1,0:T(8,128)(2,1)S(1)} %get-tuple-element.123), channel_id=1, source_target_pairs={{0,2},{2,0},{4,6},{6,4},{8,10},{10,8},{12,14},{14,12},{1,3},{3,1},... | collective-permute-start | bytes 835592 | tf_op jit(solution)/shard_map/ppermute | solution.py:453
  111.7 7.9 %collective-permute-start.34 = (bf16[1,136,1024]{2,1,0:T(8,128)(2,1)S(1)}, bf16[1,136,1024]{2,1,0:T(8,128)(2,1)S(1)}, u32[]{:S(2)}, u32[]{:S(2)}) collective-permute-start(bf16[1,136,1024]{2,1,0:T(8,128)(2,1)S(1)} %get-tuple-element.129), channel_id=1, source_target_pairs={{0,1},{1,0},{2,3},{3,2},{4,5},{5,4},{6,7},{7,6},{8,9},{9,8},{10,11... | collective-permute-start | bytes 835592 | tf_op jit(solution)/shard_map/ppermute | solution.py:447
  112.7 9.2 %collective-permute-start.33 = (bf16[1,136,1024]{2,1,0:T(8,128)(2,1)S(1)}, bf16[1,136,1024]{2,1,0:T(8,128)(2,1)S(1)}, u32[]{:S(2)}, u32[]{:S(2)}) collective-permute-start(bf16[1,136,1024]{2,1,0:T(8,128)(2,1)S(1)} %add_convert_fusion.3), channel_id=1, source_target_pairs={{0,4},{2,6},{4,8},{6,10},{8,12},{10,14},{12,0},{14,2},{1,5},{3,7},... | collective-permute-start | bytes 835592 | tf_op jit(solution)/shard_map/ppermute | solution.py:456
  113.5 8.4 %collective-permute-start.30 = (bf16[1,136,1024]{2,1,0:T(8,128)(2,1)S(1)}, bf16[1,136,1024]{2,1,0:T(8,128)(2,1)S(1)}, u32[]{:S(2)}, u32[]{:S(2)}) collective-permute-start(bf16[1,136,1024]{2,1,0:T(8,128)(2,1)S(1)} %add_convert_fusion.4), channel_id=1, source_target_pairs={{0,2},{2,0},{4,6},{6,4},{8,10},{10,8},{12,14},{14,12},{1,3},{3,1},... | collective-permute-start | bytes 835592 | tf_op jit(solution)/shard_map/ppermute | solution.py:453
  122.0 6.6 %collective-permute-start.35 = (bf16[1,136,1024]{2,1,0:T(8,128)(2,1)S(1)}, bf16[1,136,1024]{2,1,0:T(8,128)(2,1)S(1)}, u32[]{:S(2)}, u32[]{:S(2)}) collective-permute-start(bf16[1,136,1024]{2,1,0:T(8,128)(2,1)S(1)} %add_convert_fusion.1), channel_id=1, source_target_pairs={{0,1},{1,0},{2,3},{3,2},{4,5},{5,4},{6,7},{7,6},{8,9},{9,8},{10,11... | collective-permute-start | bytes 835592 | tf_op jit(solution)/shard_map/ppermute | solution.py:447
  123.6 11.2 %collective-permute-start.36 = (bf16[1,136,1024]{2,1,0:T(8,128)(2,1)S(1)}, bf16[1,136,1024]{2,1,0:T(8,128)(2,1)S(1)}, u32[]{:S(2)}, u32[]{:S(2)}) collective-permute-start(bf16[1,136,1024]{2,1,0:T(8,128)(2,1)S(1)} %add_convert_fusion), channel_id=1, source_target_pairs={{0,4},{2,6},{4,8},{6,10},{8,12},{10,14},{12,0},{14,2},{1,5},{3,7},... | collective-permute-start | bytes 835592 | tf_op jit(solution)/shard_map/ppermute | solution.py:456
  123.7 11.2 %collective-permute-start.38 = (bf16[1,136,1024]{2,1,0:T(8,128)(2,1)S(1)}, bf16[1,136,1024]{2,1,0:T(8,128)(2,1)S(1)}, u32[]{:S(2)}, u32[]{:S(2)}) collective-permute-start(bf16[1,136,1024]{2,1,0:T(8,128)(2,1)S(1)} %get-tuple-element.136), channel_id=1, source_target_pairs={{0,2},{2,0},{4,6},{6,4},{8,10},{10,8},{12,14},{14,12},{1,3},{3,1},... | collective-permute-start | bytes 835592 | tf_op jit(solution)/shard_map/ppermute | solution.py:453
  124.6 12.8 %collective-permute-start.37 = (bf16[1,136,1024]{2,1,0:T(8,128)(2,1)S(1)}, bf16[1,136,1024]{2,1,0:T(8,128)(2,1)S(1)}, u32[]{:S(2)}, u32[]{:S(2)}) collective-permute-start(bf16[1,136,1024]{2,1,0:T(8,128)(2,1)S(1)} %add_convert_fusion.2), channel_id=1, source_target_pairs={{0,12},{2,14},{4,0},{6,2},{8,4},{10,6},{12,8},{14,10},{1,13},{3,15... | collective-permute-start | bytes 835592 | tf_op jit(solution)/shard_map/ppermute | solution.py:456

commit v16 on v15

--- a/solution.py
+++ b/solution.py
@@ -396,7 +396,7 @@
 
 def grads_call(which, packed, width, part, down):
     rows, count = sum(item.shape[0] for item in packed), len(packed)
-    step = math.gcd(width // 2, 512)
+    step = math.gcd(width // 2, 512 if down else 1024)
     per = width // 2 // step
     deep = part if down else 2 * part
 
@@ -425,7 +425,7 @@
             ],
         ),
         out_shape=[jax.ShapeDtypeStruct(shape, jnp.bfloat16) for shape in shapes],
-        compiler_params=pltpu.CompilerParams(vmem_limit_bytes=14 << 20),
+        compiler_params=pltpu.CompilerParams(vmem_limit_bytes=22 << 20),
         cost_estimate=pl.CostEstimate(
             flops=2 * rows * width * deep, bytes_accessed=2 * rows * (width + deep), transcendentals=0
         ),
@@ -533,21 +533,21 @@
     mine_3, other_3, x_3, y_3, z_3, keep_2y = tied(
         [mine_3, other_3, x_3, y_3, z_3, keep_2y], [from_x2, from_y1, from_z1]
     )
-    from_z3, from_x3, from_y2, from_y3 = over_z(z_3, 1), over_x(x_3), over_y(total(keep_2y, from_x2)), over_y(y_3)
+    from_z3, from_y2, from_x1 = over_z(z_3, 1), over_y(total(keep_2y, from_x2)), over_x(x_1)
+    from_x3, from_y3 = over_x(x_3), over_y(y_3)
     packed = [mine_0, over_role(other_0), mine_1, over_role(other_1), mine_3, over_role(other_3)]
+    (d_down,) = grads_call(which_ref, packed, width, part, True)
+    from_z3, from_x20, from_y2 = tied([from_z3, from_x20, from_y2], [d_down])
+    far, step_2 = total(far, from_z1, from_z3), total(keep_2, from_x20, from_y2)
+    (from_x1,) = tied([from_x1], [far, step_2])
+    from_far, from_z2 = over_y(far), over_z(step_2, 1)
+    home_1 = over_z(total(keep_1, from_x1, from_y1), -1)
+    from_x0 = over_x(total(side_0, from_far))
+    from_x3, from_y3, from_z2 = tied([from_x3, from_y3, from_z2], [from_far])
+    home_3 = over_z(total(keep_3, from_x3, from_y3, from_z2), 1)
+    from_y0 = over_y(tied([y_0], [from_far])[0])
     d_gate, d_up = grads_call(which_ref, packed, width, part, False)
-    from_z3, from_x20, from_y2, x_1 = tied([from_z3, from_x20, from_y2, x_1], [d_gate, d_up])
-    from_x1 = over_x(x_1)
-    from_far = over_y(total(far, from_z1, from_z3))
-    from_z2 = over_z(total(keep_2, from_x20, from_y2), 1)
-    (d_down,) = grads_call(which_ref, packed, width, part, True)
-    (from_x1,) = tied([from_x1], [d_down])
-    home_1 = total(keep_1, from_x1, from_y1)
-    from_far, from_x3, from_y3, from_z2, y_0 = tied([from_far, from_x3, from_y3, from_z2, y_0], [d_down, home_1])
-    from_x0 = over_x(total(side_0, from_far))
-    home_1 = over_z(home_1, -1)
-    home_3 = over_z(total(keep_3, from_x3, from_y3, from_z2), 1)
-    from_y0 = over_y(y_0)
+    home_1, from_x0, home_3, from_y0 = tied([home_1, from_x0, home_3, from_y0], [d_gate, d_up])
     home = (near, from_x0, home_3, home_1, from_y0)
     d_tok = sum(block[0, :tok_rows].astype(jnp.float32) for block in home).astype(jnp.bfloat16)
     home = sum(block[0, tok_rows:].astype(jnp.float32) for block in home)

time: 139 us -> 135 us (0.971)
  waiting for transfers between devices: 39.9 us -> 35.5 us
    ppermute x13, waiting for transfers between devices: 32.8 us -> 21.4 us  [over_z(): lax.ppermute(array, 'ep', [(i, (i + shift * n_y) % ep) for i in range(ep)])]
    ppermute x11, waiting for transfers between devices: 0.03 us -> 7.23 us  [over_y(): lax.ppermute(array, 'ep', [(i, i + 1 - 2 * (i % n_y)) for i in range(ep)])]
    ppermute x10, starting transfers between devices: 11 us -> 12.6 us  [over_x(): return lax.ppermute(array, 'tp', [(0, 1), (1, 0)])]
  transfers between devices with their start and end apart: 39 -> 39, of which waited for: 11 -> 8; matrix products, arithmetic and copies ran while one was open for 1% -> 1% of each run, Pallas kernels for 33% -> 34%
where the time goes in v16:
time: 135 us; the launch traced here: 134 us
  Pallas kernels  47.5 us (35%)
  starting transfers between devices  45.3 us (34%)
  waiting for transfers between devices  35.5 us (26%)
  local copies, waits for them, and re-layouts  2.7 us (2%)
  other arithmetic  2.4 us (2%)
    pallas_call x3, Pallas kernels, rows_call(): pl.pallas_call(functools.partial(rows_kernel, count, ways, capacity, slot...  31.5 us
    ppermute x13, waiting for transfers between devices, over_z(): lax.ppermute(array, 'ep', [(i, (i + shift * n_y) % ep) for i in range(ep)])  21.4 us
    ppermute x13, starting transfers between devices, over_z(): lax.ppermute(array, 'ep', [(i, (i + shift * n_y) % ep) for i in range(ep)])  20.2 us
    ppermute x10, starting transfers between devices, over_x(): return lax.ppermute(array, 'tp', [(0, 1), (1, 0)])  12.6 us
    ppermute x11, starting transfers between devices, over_y(): lax.ppermute(array, 'ep', [(i, i + 1 - 2 * (i % n_y)) for i in range(ep)])  11.4 us
    pallas_call x2, Pallas kernels, grads_call(): pl.pallas_call(functools.partial(grads_kernel, count, *starts, 2 * per),...  10.8 us
    ppermute x11, waiting for transfers between devices, over_y(): lax.ppermute(array, 'ep', [(i, i + 1 - 2 * (i % n_y)) for i in range(ep)])  7.23 us
    ppermute x10, waiting for transfers between devices, over_x(): return lax.ppermute(array, 'tp', [(0, 1), (1, 0)])  6.84 us
  transfers between devices with their start and end apart: 39, of which 8 were waited for; matrix products, arithmetic and copies ran while one was open for 1% of the time, Pallas kernels for 34%

profile of v16, /device:TPU:0, one launch (start us, length us, event | category | flops | bytes accessed | tf_op | source)
XLA Modules:
  0.0 134.3 jit_solution(6457906563289696697)
XLA Ops:
  0.6 1.8 %join.1.refs_4_ = bf16[256,1024]{1,0:T(8,128)(2,1)} custom-call(bf16[128,1024]{1,0:T(8,128)(2,1)} %top_ref.1, bf16[128,1024]{1,0:T(8,128)(2,1)} %bottom_ref.1), custom_call_target="tpu_custom_call" | custom-call | bytes 1048576 | tf_op jit(solution)/shard_map/join/pallas_call | solution.py:180
  2.5 3.1 %collective-permute-start = (bf16[256,1024]{1,0:T(8,128)(2,1)}, bf16[256,1024]{1,0:T(8,128)(2,1)}, u32[]{:S(2)}, u32[]{:S(2)}) collective-permute-start(bf16[256,1024]{1,0:T(8,128)(2,1)} %join.1.refs_4_), channel_id=1, source_target_pairs={{0,4},{2,6},{4,8},{6,10},{8,12},{10,14},{12,0},{14,2},{1,5},{3,7},... | collective-permute-start | bytes 1572872 | tf_op jit(solution)/shard_map/ppermute | solution.py:456
  5.6 1.5 %collective-permute-start.1 = (bf16[256,1024]{1,0:T(8,128)(2,1)}, bf16[256,1024]{1,0:T(8,128)(2,1)}, u32[]{:S(2)}, u32[]{:S(2)}) collective-permute-start(bf16[256,1024]{1,0:T(8,128)(2,1)} %join.1.refs_4_), channel_id=1, source_target_pairs={{0,2},{2,0},{4,6},{6,4},{8,10},{10,8},{12,14},{14,12},{1,3},{3,1},... | collective-permute-start | bytes 1572872 | tf_op jit(solution)/shard_map/ppermute | solution.py:453
  7.1 1.5 %collective-permute-start.2 = (bf16[256,1024]{1,0:T(8,128)(2,1)}, bf16[256,1024]{1,0:T(8,128)(2,1)}, u32[]{:S(2)}, u32[]{:S(2)}) collective-permute-start(bf16[256,1024]{1,0:T(8,128)(2,1)} %join.1.refs_4_), channel_id=1, source_target_pairs={{0,1},{1,0},{2,3},{3,2},{4,5},{5,4},{6,7},{7,6},{8,9},{9,8},{10,11... | collective-permute-start | bytes 1572872 | tf_op jit(solution)/shard_map/ppermute | solution.py:447
  8.6 3.4 %weights.1 = (bf16[2048,768]{1,0:T(8,128)(2,1)S(1)}, bf16[384,2048]{1,0:T(8,128)(2,1)}) custom-call(s32[1]{0:T(128)} %bitcast.2.tp_ref, bf16[1,2048,384]{2,1,0:T(8,128)(2,1)} %wg_ref.1, bf16[1,2048,384]{2,1,0:T(8,128)(2,1)} %wu_ref.1, bf16[1,384,2048]{2,1,0:T(8,128)(2,1)} %wd_ref.1), custom_call_target="tpu_custom_call" | custom-call | bytes 9437184 | tf_op jit(solution)/shard_map/weights/pallas_call | solution.py:141
  12.0 7.8 %collective-permute-done.refs_4_ = bf16[256,1024]{1,0:T(8,128)(2,1)} collective-permute-done((bf16[256,1024]{1,0:T(8,128)(2,1)}, bf16[256,1024]{1,0:T(8,128)(2,1)}, u32[]{:S(2)}, u32[]{:S(2)}) %collective-permute-start) | collective-permute-done | bytes 524320 | tf_op jit(solution)/shard_map/ppermute | solution.py:456
  19.8 0.7 collective-permute-done.2.refs_5_
  21.0 1.6 %collective-permute-start.7 = (bf16[256,1024]{1,0:T(8,128)(2,1)}, bf16[256,1024]{1,0:T(8,128)(2,1)}, u32[]{:S(2)}, u32[]{:S(2)}) collective-permute-start(bf16[256,1024]{1,0:T(8,128)(2,1)} %collective-permute-done.refs_4_), channel_id=1, source_target_pairs={{0,4},{2,6},{4,8},{6,10},{8,12},{10,14},{12,0},{14,2},{1,5},{3,7},... | collective-permute-start | bytes 1572872 | tf_op jit(solution)/shard_map/ppermute | solution.py:456
  23.1 1.5 %collective-permute-start.5 = (bf16[256,1024]{1,0:T(8,128)(2,1)}, bf16[256,1024]{1,0:T(8,128)(2,1)S(1)}, u32[]{:S(2)}, u32[]{:S(2)}) collective-permute-start(bf16[256,1024]{1,0:T(8,128)(2,1)} %collective-permute-done.1.refs_6_), channel_id=1, source_target_pairs={{0,1},{1,0},{2,3},{3,2},{4,5},{5,4},{6,7},{7,6},{8,9},{9,8},{10,11... | collective-permute-start | bytes 1572872 | tf_op jit(solution)/shard_map/ppermute | solution.py:447
  24.6 12.3 %collective-permute-done.7.refs_8_ = bf16[256,1024]{1,0:T(8,128)(2,1)} collective-permute-done((bf16[256,1024]{1,0:T(8,128)(2,1)}, bf16[256,1024]{1,0:T(8,128)(2,1)}, u32[]{:S(2)}, u32[]{:S(2)}) %collective-permute-start.7) | collective-permute-done | bytes 524320 | tf_op jit(solution)/shard_map/ppermute | solution.py:456
  37.0 0.9 collective-permute-start.6
  37.9 0.8 copy-done
  38.7 0.8 copy-done.3
  39.5 1.4 %collective-permute-start.9 = (bf16[256,1024]{1,0:T(8,128)(2,1)}, bf16[256,1024]{1,0:T(8,128)(2,1)}, u32[]{:S(2)}, u32[]{:S(2)}) collective-permute-start(bf16[256,1024]{1,0:T(8,128)(2,1)} %join.1.refs_4_), channel_id=1, source_target_pairs={{0,12},{2,14},{4,0},{6,2},{8,4},{10,6},{12,8},{14,10},{1,13},{3,15... | collective-permute-start | bytes 1572872 | tf_op jit(solution)/shard_map/ppermute | solution.py:456
  40.9 1.1 collective-permute-start.10
  42.0 1.5 %collective-permute-start.11 = (bf16[256,1024]{1,0:T(8,128)(2,1)}, bf16[256,1024]{1,0:T(8,128)(2,1)}, u32[]{:S(2)}, u32[]{:S(2)}) collective-permute-start(bf16[256,1024]{1,0:T(8,128)(2,1)} %collective-permute-done.7.refs_8_), channel_id=1, source_target_pairs={{0,1},{1,0},{2,3},{3,2},{4,5},{5,4},{6,7},{7,6},{8,9},{9,8},{10,11... | collective-permute-start | bytes 1572872 | tf_op jit(solution)/shard_map/ppermute | solution.py:447
  43.6 1.0 copy-done.1
  44.6 9.4 %rows.3 = (bf16[144,5248]{1,0:T(8,128)(2,1)S(1)}, bf16[144,5248]{1,0:T(8,128)(2,1)S(1)}, bf16[1,136,1024]{2,1,0:T(8,128)(2,1)S(1)}, bf16[1,136,1024]{2,1,0:T(8,1...) custom-call(s32[3]{0:T(128)S(1)} %pad_add_fusion.where_ref, ...), custom_call_target="tpu_custom_call" | custom-call | flops 3170893824 | bytes 13631488 | tf_op jit(solution)/shard_map/rows/pallas_call | solution.py:321
  54.1 1.5 %collective-permute-start.12 = (bf16[256,1024]{1,0:T(8,128)(2,1)}, bf16[256,1024]{1,0:T(8,128)(2,1)S(1)}, u32[]{:S(2)}, u32[]{:S(2)}) collective-permute-start(bf16[256,1024]{1,0:T(8,128)(2,1)} %collective-permute-done.refs_4_), channel_id=1, source_target_pairs={{0,1},{1,0},{2,3},{3,2},{4,5},{5,4},{6,7},{7,6},{8,9},{9,8},{10,11... | collective-permute-start | bytes 1572872 | tf_op jit(solution)/shard_map/ppermute | solution.py:447
  55.6 1.0 collective-permute-start.13
  56.6 1.0 collective-permute-start.14
  57.6 3.4 %collective-permute-start.16 = (bf16[2,16,128]{2,1,0:T(8,128)(2,1)S(1)}, bf16[2,16,128]{2,1,0:T(8,128)(2,1)S(1)}, u32[]{:S(2)}, u32[]{:S(2)}) collective-permute-start(bf16[2,16,128]{2,1,0:T(8,128)(2,1)S(1)} %pad_maximum_fusion.refs_8_), channel_id=1, source_target_pairs={{0,8},{2,10},{4,12},{6,14},{8,0},{10,2},{12,4},{14,6},{1,9},{3,11}... | collective-permute-start | bytes 24584 | tf_op jit(solution)/shard_map/ppermute | solution.py:456
  61.0 4.9 %collective-permute-done.12.refs_5_ = bf16[256,1024]{1,0:T(8,128)(2,1)S(1)} collective-permute-done((bf16[256,1024]{1,0:T(8,128)(2,1)}, bf16[256,1024]{1,0:T(8,128)(2,1)S(1)}, u32[]{:S(2)}, u32[]{:S(2)}) %collective-permute-start.12) | collective-permute-done | bytes 524320 | tf_op jit(solution)/shard_map/ppermute | solution.py:447
  65.8 1.3 collective-permute-start.17
  67.1 1.2 collective-permute-done.13.refs_7_
  68.4 1.1 collective-permute-start.19
  69.4 1.1 collective-permute-start.20
  70.5 2.5 %collective-permute-start.18 = (bf16[256,1024]{1,0:T(8,128)(2,1)S(1)}, bf16[256,1024]{1,0:T(8,128)(2,1)S(1)}, u32[]{:S(2)}, u32[]{:S(2)}) collective-permute-start(bf16[256,1024]{1,0:T(8,128)(2,1)S(1)} %copy-done.2), channel_id=1, source_target_pairs={{0,12},{2,14},{4,0},{6,2},{8,4},{10,6},{12,8},{14,10},{1,13},{3,15... | collective-permute-start | bytes 1572872 | tf_op jit(solution)/shard_map/ppermute | solution.py:456
  73.0 12.8 %rows.4 = (bf16[288,5248]{1,0:T(8,128)(2,1)S(1)}, bf16[288,5248]{1,0:T(8,128)(2,1)S(1)}, bf16[1,136,1024]{2,1,0:T(8,128)(2,1)S(1)}, bf16[1,136,1024]{2,1,0:T(8,1...) custom-call(s32[3]{0:T(128)S(1)} %pad_add_fusion.where_ref, ...), custom_call_target="tpu_custom_call" | custom-call | flops 6341787648 | bytes 17825792 | tf_op jit(solution)/shard_map/rows/pallas_call | solution.py:321
  86.5 1.0 collective-permute-start.24
  87.5 1.5 %collective-permute-start.23 = (bf16[1,136,1024]{2,1,0:T(8,128)(2,1)S(1)}, bf16[1,136,1024]{2,1,0:T(8,128)(2,1)S(1)}, u32[]{:S(2)}, u32[]{:S(2)}) collective-permute-start(bf16[1,136,1024]{2,1,0:T(8,128)(2,1)S(1)} %get-tuple-element.112), channel_id=1, source_target_pairs={{0,1},{1,0},{2,3},{3,2},{4,5},{5,4},{6,7},{7,6},{8,9},{9,8},{10,11... | collective-permute-start | bytes 835592 | tf_op jit(solution)/shard_map/ppermute | solution.py:447
  89.0 9.3 %rows.5 = (bf16[144,5248]{1,0:T(8,128)(2,1)S(1)}, bf16[144,5248]{1,0:T(8,128)(2,1)S(1)}, bf16[1,136,1024]{2,1,0:T(8,128)(2,1)S(1)}, bf16[1,136,1024]{2,1,0:T(8,1...) custom-call(s32[3]{0:T(128)S(1)} %pad_add_fusion.where_ref, ...), custom_call_target="tpu_custom_call" | custom-call | flops 3170893824 | bytes 13631488 | tf_op jit(solution)/shard_map/rows/pallas_call | solution.py:321
  98.4 0.6 collective-permute-start.26
  99.1 2.0 %collective-permute-start.25 = (bf16[1,136,1024]{2,1,0:T(8,128)(2,1)S(1)}, bf16[1,136,1024]{2,1,0:T(8,128)(2,1)S(1)}, u32[]{:S(2)}, u32[]{:S(2)}) collective-permute-start(bf16[1,136,1024]{2,1,0:T(8,128)(2,1)S(1)} %get-tuple-element.114), channel_id=1, source_target_pairs={{0,4},{2,6},{4,8},{6,10},{8,12},{10,14},{12,0},{14,2},{1,5},{3,7},... | collective-permute-start | bytes 835592 | tf_op jit(solution)/shard_map/ppermute | solution.py:456
  101.1 1.0 collective-permute-start.27
  102.2 1.5 %collective-permute-start.21 = (bf16[1,136,1024]{2,1,0:T(8,128)(2,1)S(1)}, bf16[1,136,1024]{2,1,0:T(8,128)(2,1)S(1)}, u32[]{:S(2)}, u32[]{:S(2)}) collective-permute-start(bf16[1,136,1024]{2,1,0:T(8,128)(2,1)S(1)} %get-tuple-element.102), channel_id=1, source_target_pairs={{0,1},{1,0},{2,3},{3,2},{4,5},{5,4},{6,7},{7,6},{8,9},{9,8},{10,11... | collective-permute-start | bytes 835592 | tf_op jit(solution)/shard_map/ppermute | solution.py:447
  104.2 4.4 %grads.2 = bf16[1,384,2048]{2,1,0:T(8,128)(2,1)} custom-call(s32[1]{0:T(128)} %bitcast.2.tp_ref, bf16[144,5248]{1,0:T(8,128)(2,1)S(1)} %get-tuple-element.88.refs_0_, bf16[144,5248]{1,0:T(8,128)(2,1)S(1)} %collective-permute-done.28.refs_1_, bf16[288,5248]{1,0:T(8,128)(2,1)S(1)} %get-tuple-element.105.refs_9_.refs_2_, ...), custom_call_target="tpu_custom_call" | custom-call | flops 1811939328 | bytes 5603328 | tf_op jit(solution)/shard_map/grads/pallas_call | solution.py:413
  108.6 1.1 collective-permute-start.35
  109.9 1.0 collective-permute-start.32
  111.1 1.6 %collective-permute-start.36 = (bf16[1,136,1024]{2,1,0:T(8,128)(2,1)S(1)}, bf16[1,136,1024]{2,1,0:T(8,128)(2,1)S(1)}, u32[]{:S(2)}, u32[]{:S(2)}) collective-permute-start(bf16[1,136,1024]{2,1,0:T(8,128)(2,1)S(1)} %add_convert_fusion.3), channel_id=1, source_target_pairs={{0,4},{2,6},{4,8},{6,10},{8,12},{10,14},{12,0},{14,2},{1,5},{3,7},... | collective-permute-start | bytes 835592 | tf_op jit(solution)/shard_map/ppermute | solution.py:456
  112.7 1.2 collective-permute-done.21
  114.0 1.1 collective-permute-start.31
  115.2 7.2 %collective-permute-done.32 = bf16[1,136,1024]{2,1,0:T(8,128)(2,1)S(1)} collective-permute-done((bf16[1,136,1024]{2,1,0:T(8,128)(2,1)S(1)}, bf16[1,136,1024]{2,1,0:T(8,128)(2,1)S(1)}, u32[]{:S(2)}, u32[]{:S(2)}) %collective-permute-start.32) | collective-permute-done | bytes 278560 | tf_op jit(solution)/shard_map/ppermute | solution.py:453
  122.4 1.5 %collective-permute-start.33 = (bf16[1,136,1024]{2,1,0:T(8,128)(2,1)S(1)}, bf16[1,136,1024]{2,1,0:T(8,128)(2,1)S(1)}, u32[]{:S(2)}, u32[]{:S(2)}) collective-permute-start(bf16[1,136,1024]{2,1,0:T(8,128)(2,1)S(1)} %add_convert_fusion.1), channel_id=1, source_target_pairs={{0,1},{1,0},{2,3},{3,2},{4,5},{5,4},{6,7},{7,6},{8,9},{9,8},{10,11... | collective-permute-start | bytes 835592 | tf_op jit(solution)/shard_map/ppermute | solution.py:447
  124.1 1.2 collective-permute-start.37
  125.3 1.0 collective-permute-start.38
  126.3 6.3 %grads.3 = (bf16[1,2048,384]{2,1,0:T(8,128)(2,1)}, bf16[1,2048,384]{2,1,0:T(8,128)(2,1)}) custom-call(s32[1]{0:T(128)} %bitcast.2.tp_ref, bf16[144,5248]{1,0:T(8,128)(2,1)S(1)} %get-tuple-element.88.refs_0_, bf16[144,5248]{1,0:T(8,128)(2,1)S(1)} %collective-permute-done.28.refs_1_, bf16[288,5248]{1,0:T(8,128)(2,1)S(1)} %get-tuple-element.105.refs_9_.refs_2_, ...), custom_call_target="tpu_custom_call" | custom-call | flops 3623878656 | bytes 6488064 | tf_op jit(solution)/shard_map/grads/pallas_call | solution.py:413
  132.7 0.9 fusion
  (67 shorter events, 3.9 us)
Async XLA Ops:
  2.5 17.3 %collective-permute-start = (bf16[256,1024]{1,0:T(8,128)(2,1)}, bf16[256,1024]{1,0:T(8,128)(2,1)}, u32[]{:S(2)}, u32[]{:S(2)}) collective-permute-start(bf16[256,1024]{1,0:T(8,128)(2,1)} %join.1.refs_4_), channel_id=1, source_target_pairs={{0,4},{2,6},{4,8},{6,10},{8,12},{10,14},{12,0},{14,2},{1,5},{3,7},... | collective-permute-start | bytes 1572872 | tf_op jit(solution)/shard_map/ppermute | solution.py:456
  5.6 14.3 %collective-permute-start.1 = (bf16[256,1024]{1,0:T(8,128)(2,1)}, bf16[256,1024]{1,0:T(8,128)(2,1)}, u32[]{:S(2)}, u32[]{:S(2)}) collective-permute-start(bf16[256,1024]{1,0:T(8,128)(2,1)} %join.1.refs_4_), channel_id=1, source_target_pairs={{0,2},{2,0},{4,6},{6,4},{8,10},{10,8},{12,14},{14,12},{1,3},{3,1},... | collective-permute-start | bytes 1572872 | tf_op jit(solution)/shard_map/ppermute | solution.py:453
  7.1 13.4 %collective-permute-start.2 = (bf16[256,1024]{1,0:T(8,128)(2,1)}, bf16[256,1024]{1,0:T(8,128)(2,1)}, u32[]{:S(2)}, u32[]{:S(2)}) collective-permute-start(bf16[256,1024]{1,0:T(8,128)(2,1)} %join.1.refs_4_), channel_id=1, source_target_pairs={{0,1},{1,0},{2,3},{3,2},{4,5},{5,4},{6,7},{7,6},{8,9},{9,8},{10,11... | collective-permute-start | bytes 1572872 | tf_op jit(solution)/shard_map/ppermute | solution.py:447
  8.6 16.0 %copy-start.6 = (bf16[128,8]{0,1:T(8,128)(2,1)S(1)}, bf16[128,8]{0,1:T(8,128)(2,1)}, u32[]{:S(2)}) copy-start(bf16[128,8]{0,1:T(8,128)(2,1)} %param.10) | copy-start | bytes 6148
  8.6 16.0 %copy-start.5 = (s32[128,8]{0,1:T(8,128)S(1)}, s32[128,8]{0,1:T(8,128)}, u32[]{:S(2)}) copy-start(s32[128,8]{0,1:T(8,128)} %param.9) | copy-start | bytes 12292
  20.5 23.1 %collective-permute-start.3 = (bf16[2048,768]{1,0:T(8,128)(2,1)S(1)}, bf16[2048,768]{1,0:T(8,128)(2,1)}, u32[]{:S(2)}, u32[]{:S(2)}) collective-permute-start(bf16[2048,768]{1,0:T(8,128)(2,1)S(1)} %get-tuple-element.75.refs_0_), channel_id=1, source_target_pairs={{0,16},{16,0},{1,17},{17,1},{2,18},{18,2},{3,19},{19,3},{4,20},{20... | collective-permute-start | bytes 9437192 | tf_op jit(solution)/shard_map/ppermute | solution.py:450
  20.5 23.0 %collective-permute-start.4 = (bf16[384,2048]{1,0:T(8,128)(2,1)}, bf16[384,2048]{1,0:T(8,128)(2,1)}, u32[]{:S(2)}, u32[]{:S(2)}) collective-permute-start(bf16[384,2048]{1,0:T(8,128)(2,1)} %get-tuple-element.76.refs_2_), channel_id=1, source_target_pairs={{0,16},{16,0},{1,17},{17,1},{2,18},{18,2},{3,19},{19,3},{4,20},{20... | collective-permute-start | bytes 4718600 | tf_op jit(solution)/shard_map/ppermute | solution.py:450
  21.0 15.9 %collective-permute-start.7 = (bf16[256,1024]{1,0:T(8,128)(2,1)}, bf16[256,1024]{1,0:T(8,128)(2,1)}, u32[]{:S(2)}, u32[]{:S(2)}) collective-permute-start(bf16[256,1024]{1,0:T(8,128)(2,1)} %collective-permute-done.refs_4_), channel_id=1, source_target_pairs={{0,4},{2,6},{4,8},{6,10},{8,12},{10,14},{12,0},{14,2},{1,5},{3,7},... | collective-permute-start | bytes 1572872 | tf_op jit(solution)/shard_map/ppermute | solution.py:456
  22.6 16.1 %collective-permute-start.8 = (bf16[256,1024]{1,0:T(8,128)(2,1)}, bf16[256,1024]{1,0:T(8,128)(2,1)S(1)}, u32[]{:S(2)}, u32[]{:S(2)}) collective-permute-start(bf16[256,1024]{1,0:T(8,128)(2,1)} %collective-permute-done.refs_4_), channel_id=1, source_target_pairs={{0,2},{2,0},{4,6},{6,4},{8,10},{10,8},{12,14},{14,12},{1,3},{3,1},... | collective-permute-start | bytes 1572872 | tf_op jit(solution)/shard_map/ppermute | solution.py:453
  23.1 14.8 %collective-permute-start.5 = (bf16[256,1024]{1,0:T(8,128)(2,1)}, bf16[256,1024]{1,0:T(8,128)(2,1)S(1)}, u32[]{:S(2)}, u32[]{:S(2)}) collective-permute-start(bf16[256,1024]{1,0:T(8,128)(2,1)} %collective-permute-done.1.refs_6_), channel_id=1, source_target_pairs={{0,1},{1,0},{2,3},{3,2},{4,5},{5,4},{6,7},{7,6},{8,9},{9,8},{10,11... | collective-permute-start | bytes 1572872 | tf_op jit(solution)/shard_map/ppermute | solution.py:447
  37.0 5.0 %collective-permute-start.6 = (bf16[16,128]{1,0:T(8,128)(2,1)S(1)}, bf16[16,128]{1,0:T(8,128)(2,1)S(1)}, u32[]{:S(2)}, u32[]{:S(2)}) collective-permute-start(bf16[16,128]{1,0:T(8,128)(2,1)S(1)} %get-tuple-element.142), channel_id=1, source_target_pairs={{0,2},{2,0},{4,6},{6,4},{8,10},{10,8},{12,14},{14,12},{1,3},{3,1},... | collective-permute-start | bytes 12296 | tf_op jit(solution)/shard_map/ppermute | solution.py:453
  37.9 0.8 copy-start
  38.7 0.8 copy-start.3
  39.5 14.5 %collective-permute-start.9 = (bf16[256,1024]{1,0:T(8,128)(2,1)}, bf16[256,1024]{1,0:T(8,128)(2,1)}, u32[]{:S(2)}, u32[]{:S(2)}) collective-permute-start(bf16[256,1024]{1,0:T(8,128)(2,1)} %join.1.refs_4_), channel_id=1, source_target_pairs={{0,12},{2,14},{4,0},{6,2},{8,4},{10,6},{12,8},{14,10},{1,13},{3,15... | collective-permute-start | bytes 1572872 | tf_op jit(solution)/shard_map/ppermute | solution.py:456
  40.9 13.1 %collective-permute-start.10 = (bf16[256,1024]{1,0:T(8,128)(2,1)}, bf16[256,1024]{1,0:T(8,128)(2,1)}, u32[]{:S(2)}, u32[]{:S(2)}) collective-permute-start(bf16[256,1024]{1,0:T(8,128)(2,1)} %collective-permute-done.7.refs_8_), channel_id=1, source_target_pairs={{0,2},{2,0},{4,6},{6,4},{8,10},{10,8},{12,14},{14,12},{1,3},{3,1},... | collective-permute-start | bytes 1572872 | tf_op jit(solution)/shard_map/ppermute | solution.py:453
  42.0 12.1 %collective-permute-start.11 = (bf16[256,1024]{1,0:T(8,128)(2,1)}, bf16[256,1024]{1,0:T(8,128)(2,1)}, u32[]{:S(2)}, u32[]{:S(2)}) collective-permute-start(bf16[256,1024]{1,0:T(8,128)(2,1)} %collective-permute-done.7.refs_8_), channel_id=1, source_target_pairs={{0,1},{1,0},{2,3},{3,2},{4,5},{5,4},{6,7},{7,6},{8,9},{9,8},{10,11... | collective-permute-start | bytes 1572872 | tf_op jit(solution)/shard_map/ppermute | solution.py:447
  43.6 1.0 copy-start.1
  44.6 25.9 %copy-start.2 = (bf16[256,1024]{1,0:T(8,128)(2,1)S(1)}, bf16[256,1024]{1,0:T(8,128)(2,1)}, u32[]{:S(2)}) copy-start(bf16[256,1024]{1,0:T(8,128)(2,1)} %copy-done) | copy-start | bytes 1572868
  44.6 28.4 %copy-start.4 = (bf16[256,1024]{1,0:T(8,128)(2,1)S(1)}, bf16[256,1024]{1,0:T(8,128)(2,1)}, u32[]{:S(2)}) copy-start(bf16[256,1024]{1,0:T(8,128)(2,1)} %copy-done.3) | copy-start | bytes 1572868
  54.1 11.7 %collective-permute-start.12 = (bf16[256,1024]{1,0:T(8,128)(2,1)}, bf16[256,1024]{1,0:T(8,128)(2,1)S(1)}, u32[]{:S(2)}, u32[]{:S(2)}) collective-permute-start(bf16[256,1024]{1,0:T(8,128)(2,1)} %collective-permute-done.refs_4_), channel_id=1, source_target_pairs={{0,1},{1,0},{2,3},{3,2},{4,5},{5,4},{6,7},{7,6},{8,9},{9,8},{10,11... | collective-permute-start | bytes 1572872 | tf_op jit(solution)/shard_map/ppermute | solution.py:447
  55.6 12.8 %collective-permute-start.13 = (bf16[256,1024]{1,0:T(8,128)(2,1)S(1)}, bf16[256,1024]{1,0:T(8,128)(2,1)S(1)}, u32[]{:S(2)}, u32[]{:S(2)}) collective-permute-start(bf16[256,1024]{1,0:T(8,128)(2,1)S(1)} %copy-done.1), channel_id=1, source_target_pairs={{0,4},{2,6},{4,8},{6,10},{8,12},{10,14},{12,0},{14,2},{1,5},{3,7},... | collective-permute-start | bytes 1572872 | tf_op jit(solution)/shard_map/ppermute | solution.py:456
  56.6 11.8 %collective-permute-start.14 = (bf16[256,1024]{1,0:T(8,128)(2,1)}, bf16[256,1024]{1,0:T(8,128)(2,1)S(1)}, u32[]{:S(2)}, u32[]{:S(2)}) collective-permute-start(bf16[256,1024]{1,0:T(8,128)(2,1)} %collective-permute-done.11.refs_9_), channel_id=1, source_target_pairs={{0,2},{2,0},{4,6},{6,4},{8,10},{10,8},{12,14},{14,12},{1,3},{3,1},... | collective-permute-start | bytes 1572872 | tf_op jit(solution)/shard_map/ppermute | solution.py:453
  57.6 12.9 %collective-permute-start.15 = (bf16[2,16,128]{2,1,0:T(8,128)(2,1)S(1)}, bf16[2,16,128]{2,1,0:T(8,128)(2,1)S(1)}, u32[]{:S(2)}, u32[]{:S(2)}) collective-permute-start(bf16[2,16,128]{2,1,0:T(8,128)(2,1)S(1)} %pad_maximum_fusion.refs_8_), channel_id=1, source_target_pairs={{0,4},{2,6},{4,8},{6,10},{8,12},{10,14},{12,0},{14,2},{1,5},{3,7},... | collective-permute-start | bytes 24584 | tf_op jit(solution)/shard_map/ppermute | solution.py:456
  57.6 15.4 %collective-permute-start.16 = (bf16[2,16,128]{2,1,0:T(8,128)(2,1)S(1)}, bf16[2,16,128]{2,1,0:T(8,128)(2,1)S(1)}, u32[]{:S(2)}, u32[]{:S(2)}) collective-permute-start(bf16[2,16,128]{2,1,0:T(8,128)(2,1)S(1)} %pad_maximum_fusion.refs_8_), channel_id=1, source_target_pairs={{0,8},{2,10},{4,12},{6,14},{8,0},{10,2},{12,4},{14,6},{1,9},{3,11}... | collective-permute-start | bytes 24584 | tf_op jit(solution)/shard_map/ppermute | solution.py:456
  65.8 7.2 %collective-permute-start.17 = (bf16[2,16,128]{2,1,0:T(8,128)(2,1)S(1)}, bf16[2,16,128]{2,1,0:T(8,128)(2,1)S(1)}, u32[]{:S(2)}, u32[]{:S(2)}) collective-permute-start(bf16[2,16,128]{2,1,0:T(8,128)(2,1)S(1)} %pad_maximum_fusion.refs_8_), channel_id=1, source_target_pairs={{0,12},{2,14},{4,0},{6,2},{8,4},{10,6},{12,8},{14,10},{1,13},{3,15... | collective-permute-start | bytes 24584 | tf_op jit(solution)/shard_map/ppermute | solution.py:456
  68.4 17.5 %collective-permute-start.19 = (bf16[256,1024]{1,0:T(8,128)(2,1)}, bf16[256,1024]{1,0:T(8,128)(2,1)S(1)}, u32[]{:S(2)}, u32[]{:S(2)}) collective-permute-start(bf16[256,1024]{1,0:T(8,128)(2,1)} %collective-permute-done.9.refs_4_), channel_id=1, source_target_pairs={{0,2},{2,0},{4,6},{6,4},{8,10},{10,8},{12,14},{14,12},{1,3},{3,1},... | collective-permute-start | bytes 1572872 | tf_op jit(solution)/shard_map/ppermute | solution.py:453
  69.4 16.5 %collective-permute-start.20 = (bf16[256,1024]{1,0:T(8,128)(2,1)}, bf16[256,1024]{1,0:T(8,128)(2,1)S(1)}, u32[]{:S(2)}, u32[]{:S(2)}) collective-permute-start(bf16[256,1024]{1,0:T(8,128)(2,1)} %collective-permute-done.9.refs_4_), channel_id=1, source_target_pairs={{0,1},{1,0},{2,3},{3,2},{4,5},{5,4},{6,7},{7,6},{8,9},{9,8},{10,11... | collective-permute-start | bytes 1572872 | tf_op jit(solution)/shard_map/ppermute | solution.py:447
  70.5 15.3 %collective-permute-start.18 = (bf16[256,1024]{1,0:T(8,128)(2,1)S(1)}, bf16[256,1024]{1,0:T(8,128)(2,1)S(1)}, u32[]{:S(2)}, u32[]{:S(2)}) collective-permute-start(bf16[256,1024]{1,0:T(8,128)(2,1)S(1)} %copy-done.2), channel_id=1, source_target_pairs={{0,12},{2,14},{4,0},{6,2},{8,4},{10,6},{12,8},{14,10},{1,13},{3,15... | collective-permute-start | bytes 1572872 | tf_op jit(solution)/shard_map/ppermute | solution.py:456
  85.9 17.8 %collective-permute-start.29 = (bf16[288,5248]{1,0:T(8,128)(2,1)S(1)}, bf16[288,5248]{1,0:T(8,128)(2,1)S(1)}, u32[]{:S(2)}, u32[]{:S(2)}) collective-permute-start(bf16[288,5248]{1,0:T(8,128)(2,1)S(1)} %get-tuple-element.118), channel_id=1, source_target_pairs={{0,16},{16,0},{1,17},{17,1},{2,18},{18,2},{3,19},{19,3},{4,20},{20... | collective-permute-start | bytes 9068552 | tf_op jit(solution)/shard_map/ppermute | solution.py:450
  86.0 15.2 %collective-permute-start.28 = (bf16[144,5248]{1,0:T(8,128)(2,1)S(1)}, bf16[144,5248]{1,0:T(8,128)(2,1)S(1)}, u32[]{:S(2)}, u32[]{:S(2)}) collective-permute-start(bf16[144,5248]{1,0:T(8,128)(2,1)S(1)} %get-tuple-element.117), channel_id=1, source_target_pairs={{0,16},{16,0},{1,17},{17,1},{2,18},{18,2},{3,19},{19,3},{4,20},{20... | collective-permute-start | bytes 4534280 | tf_op jit(solution)/shard_map/ppermute | solution.py:450
  86.5 11.8 %collective-permute-start.24 = (bf16[1,136,1024]{2,1,0:T(8,128)(2,1)S(1)}, bf16[1,136,1024]{2,1,0:T(8,128)(2,1)S(1)}, u32[]{:S(2)}, u32[]{:S(2)}) collective-permute-start(bf16[1,136,1024]{2,1,0:T(8,128)(2,1)S(1)} %get-tuple-element.113), channel_id=1, source_target_pairs={{0,2},{2,0},{4,6},{6,4},{8,10},{10,8},{12,14},{14,12},{1,3},{3,1},... | collective-permute-start | bytes 835592 | tf_op jit(solution)/shard_map/ppermute | solution.py:453
  87.5 10.8 %collective-permute-start.23 = (bf16[1,136,1024]{2,1,0:T(8,128)(2,1)S(1)}, bf16[1,136,1024]{2,1,0:T(8,128)(2,1)S(1)}, u32[]{:S(2)}, u32[]{:S(2)}) collective-permute-start(bf16[1,136,1024]{2,1,0:T(8,128)(2,1)S(1)} %get-tuple-element.112), channel_id=1, source_target_pairs={{0,1},{1,0},{2,3},{3,2},{4,5},{5,4},{6,7},{7,6},{8,9},{9,8},{10,11... | collective-permute-start | bytes 835592 | tf_op jit(solution)/shard_map/ppermute | solution.py:447
  89.0 9.4 %collective-permute-start.22 = (bf16[1,136,1024]{2,1,0:T(8,128)(2,1)S(1)}, bf16[1,136,1024]{2,1,0:T(8,128)(2,1)S(1)}, u32[]{:S(2)}, u32[]{:S(2)}) collective-permute-start(bf16[1,136,1024]{2,1,0:T(8,128)(2,1)S(1)} %get-tuple-element.104), channel_id=1, source_target_pairs={{0,12},{2,14},{4,0},{6,2},{8,4},{10,6},{12,8},{14,10},{1,13},{3,15... | collective-permute-start | bytes 835592 | tf_op jit(solution)/shard_map/ppermute | solution.py:456
  98.3 3.9 %collective-permute-start.30 = (bf16[144,5248]{1,0:T(8,128)(2,1)S(1)}, bf16[144,5248]{1,0:T(8,128)(2,1)S(1)}, u32[]{:S(2)}, u32[]{:S(2)}) collective-permute-start(bf16[144,5248]{1,0:T(8,128)(2,1)S(1)} %get-tuple-element.120), channel_id=1, source_target_pairs={{0,16},{16,0},{1,17},{17,1},{2,18},{18,2},{3,19},{19,3},{4,20},{20... | collective-permute-start | bytes 4534280 | tf_op jit(solution)/shard_map/ppermute | solution.py:450
  98.4 10.2 %collective-permute-start.26 = (bf16[1,136,1024]{2,1,0:T(8,128)(2,1)S(1)}, bf16[1,136,1024]{2,1,0:T(8,128)(2,1)S(1)}, u32[]{:S(2)}, u32[]{:S(2)}) collective-permute-start(bf16[1,136,1024]{2,1,0:T(8,128)(2,1)S(1)} %get-tuple-element.115), channel_id=1, source_target_pairs={{0,1},{1,0},{2,3},{3,2},{4,5},{5,4},{6,7},{7,6},{8,9},{9,8},{10,11... | collective-permute-start | bytes 835592 | tf_op jit(solution)/shard_map/ppermute | solution.py:447
  99.1 10.7 %collective-permute-start.25 = (bf16[1,136,1024]{2,1,0:T(8,128)(2,1)S(1)}, bf16[1,136,1024]{2,1,0:T(8,128)(2,1)S(1)}, u32[]{:S(2)}, u32[]{:S(2)}) collective-permute-start(bf16[1,136,1024]{2,1,0:T(8,128)(2,1)S(1)} %get-tuple-element.114), channel_id=1, source_target_pairs={{0,4},{2,6},{4,8},{6,10},{8,12},{10,14},{12,0},{14,2},{1,5},{3,7},... | collective-permute-start | bytes 835592 | tf_op jit(solution)/shard_map/ppermute | solution.py:456
  101.1 8.6 %collective-permute-start.27 = (bf16[1,136,1024]{2,1,0:T(8,128)(2,1)S(1)}, bf16[1,136,1024]{2,1,0:T(8,128)(2,1)S(1)}, u32[]{:S(2)}, u32[]{:S(2)}) collective-permute-start(bf16[1,136,1024]{2,1,0:T(8,128)(2,1)S(1)} %add_convert_fusion.5), channel_id=1, source_target_pairs={{0,2},{2,0},{4,6},{6,4},{8,10},{10,8},{12,14},{14,12},{1,3},{3,1},... | collective-permute-start | bytes 835592 | tf_op jit(solution)/shard_map/ppermute | solution.py:453
  102.2 11.7 %collective-permute-start.21 = (bf16[1,136,1024]{2,1,0:T(8,128)(2,1)S(1)}, bf16[1,136,1024]{2,1,0:T(8,128)(2,1)S(1)}, u32[]{:S(2)}, u32[]{:S(2)}) collective-permute-start(bf16[1,136,1024]{2,1,0:T(8,128)(2,1)S(1)} %get-tuple-element.102), channel_id=1, source_target_pairs={{0,1},{1,0},{2,3},{3,2},{4,5},{5,4},{6,7},{7,6},{8,9},{9,8},{10,11... | collective-permute-start | bytes 835592 | tf_op jit(solution)/shard_map/ppermute | solution.py:447
  103.7 20.2 %collective-permute-start.34 = (bf16[1,136,1024]{2,1,0:T(8,128)(2,1)S(1)}, bf16[1,136,1024]{2,1,0:T(8,128)(2,1)S(1)}, u32[]{:S(2)}, u32[]{:S(2)}) collective-permute-start(bf16[1,136,1024]{2,1,0:T(8,128)(2,1)S(1)} %get-tuple-element.128), channel_id=1, source_target_pairs={{0,1},{1,0},{2,3},{3,2},{4,5},{5,4},{6,7},{7,6},{8,9},{9,8},{10,11... | collective-permute-start | bytes 835592 | tf_op jit(solution)/shard_map/ppermute | solution.py:447
  108.6 15.3 %collective-permute-start.35 = (bf16[1,136,1024]{2,1,0:T(8,128)(2,1)S(1)}, bf16[1,136,1024]{2,1,0:T(8,128)(2,1)S(1)}, u32[]{:S(2)}, u32[]{:S(2)}) collective-permute-start(bf16[1,136,1024]{2,1,0:T(8,128)(2,1)S(1)} %get-tuple-element.129), channel_id=1, source_target_pairs={{0,2},{2,0},{4,6},{6,4},{8,10},{10,8},{12,14},{14,12},{1,3},{3,1},... | collective-permute-start | bytes 835592 | tf_op jit(solution)/shard_map/ppermute | solution.py:453
  109.9 12.5 %collective-permute-start.32 = (bf16[1,136,1024]{2,1,0:T(8,128)(2,1)S(1)}, bf16[1,136,1024]{2,1,0:T(8,128)(2,1)S(1)}, u32[]{:S(2)}, u32[]{:S(2)}) collective-permute-start(bf16[1,136,1024]{2,1,0:T(8,128)(2,1)S(1)} %add_convert_fusion.4), channel_id=1, source_target_pairs={{0,2},{2,0},{4,6},{6,4},{8,10},{10,8},{12,14},{14,12},{1,3},{3,1},... | collective-permute-start | bytes 835592 | tf_op jit(solution)/shard_map/ppermute | solution.py:453
  111.1 12.8 %collective-permute-start.36 = (bf16[1,136,1024]{2,1,0:T(8,128)(2,1)S(1)}, bf16[1,136,1024]{2,1,0:T(8,128)(2,1)S(1)}, u32[]{:S(2)}, u32[]{:S(2)}) collective-permute-start(bf16[1,136,1024]{2,1,0:T(8,128)(2,1)S(1)} %add_convert_fusion.3), channel_id=1, source_target_pairs={{0,4},{2,6},{4,8},{6,10},{8,12},{10,14},{12,0},{14,2},{1,5},{3,7},... | collective-permute-start | bytes 835592 | tf_op jit(solution)/shard_map/ppermute | solution.py:456
  114.0 18.6 %collective-permute-start.31 = (bf16[1,136,1024]{2,1,0:T(8,128)(2,1)S(1)}, bf16[1,136,1024]{2,1,0:T(8,128)(2,1)S(1)}, u32[]{:S(2)}, u32[]{:S(2)}) collective-permute-start(bf16[1,136,1024]{2,1,0:T(8,128)(2,1)S(1)} %add_convert_fusion.2), channel_id=1, source_target_pairs={{0,12},{2,14},{4,0},{6,2},{8,4},{10,6},{12,8},{14,10},{1,13},{3,15... | collective-permute-start | bytes 835592 | tf_op jit(solution)/shard_map/ppermute | solution.py:456
  122.4 10.3 %collective-permute-start.33 = (bf16[1,136,1024]{2,1,0:T(8,128)(2,1)S(1)}, bf16[1,136,1024]{2,1,0:T(8,128)(2,1)S(1)}, u32[]{:S(2)}, u32[]{:S(2)}) collective-permute-start(bf16[1,136,1024]{2,1,0:T(8,128)(2,1)S(1)} %add_convert_fusion.1), channel_id=1, source_target_pairs={{0,1},{1,0},{2,3},{3,2},{4,5},{5,4},{6,7},{7,6},{8,9},{9,8},{10,11... | collective-permute-start | bytes 835592 | tf_op jit(solution)/shard_map/ppermute | solution.py:447
  124.1 8.6 %collective-permute-start.37 = (bf16[1,136,1024]{2,1,0:T(8,128)(2,1)S(1)}, bf16[1,136,1024]{2,1,0:T(8,128)(2,1)S(1)}, u32[]{:S(2)}, u32[]{:S(2)}) collective-permute-start(bf16[1,136,1024]{2,1,0:T(8,128)(2,1)S(1)} %add_convert_fusion), channel_id=1, source_target_pairs={{0,4},{2,6},{4,8},{6,10},{8,12},{10,14},{12,0},{14,2},{1,5},{3,7},... | collective-permute-start | bytes 835592 | tf_op jit(solution)/shard_map/ppermute | solution.py:456
  125.3 7.4 %collective-permute-start.38 = (bf16[1,136,1024]{2,1,0:T(8,128)(2,1)S(1)}, bf16[1,136,1024]{2,1,0:T(8,128)(2,1)S(1)}, u32[]{:S(2)}, u32[]{:S(2)}) collective-permute-start(bf16[1,136,1024]{2,1,0:T(8,128)(2,1)S(1)} %get-tuple-element.134), channel_id=1, source_target_pairs={{0,2},{2,0},{4,6},{6,4},{8,10},{10,8},{12,14},{14,12},{1,3},{3,1},... | collective-permute-start | bytes 835592 | tf_op jit(solution)/shard_map/ppermute | solution.py:453

commit v17 on v16

--- a/solution.py
+++ b/solution.py
@@ -481,8 +481,8 @@
             axis = item[2] if item[2] in (over_x, over_y) else over_z
             if item[1] in there and axis not in moves:
                 moves[axis] = item
-        rounds.append(list(moves.values()))
-        there |= {item[0] for item in rounds[-1]}
+        rounds.append(moves)
+        there |= {item[0] for item in moves.values()}
         waiting = [item for item in waiting if item[0] not in there]
 
     which_ref = which.reshape(1).astype(jnp.int32)
@@ -495,12 +495,14 @@
         return rows_call(items, owners, capacity, slots, where, weights, four, [tables[z] for z in steps], after)
 
     units = {(0, 0, 0): join_call(tokens, out_grad)}
-    settled = dict(units)
+    flying, landed, extra = {}, [], []
     for number, moves in enumerate(rounds):
-        arrived = {target: move(settled[source]) for target, source, move in moves}
-        units.update(arrived)
-        settled.update(arrived)
-        extra = []
+        arrived = {}
+        for axis, (target, source, move) in moves.items():
+            (block,) = tied([units[source]], [flying[axis]] + landed + extra) if flying else [units[source]]
+            arrived[axis] = move(block)
+        units.update({moves[axis][0]: block for axis, block in arrived.items()})
+        flying, landed, extra = arrived, list(flying.values()), []
         if number == 0:
             extra = [both_w, down_w]
             both_w, down_w, routes, probs = tied([both_w, down_w, routes, probs], arrived.values())
@@ -517,8 +519,6 @@
                 [0], [[(0, 0, 0)], [(0, 0, 1)], [(0, 1, 1)], [(0, 1, 0)]], []
             )
             extra = [mine_0]
-        names = list(settled)
-        settled = dict(zip(names, tied([settled[item] for item in names], extra)))
 
     def total(*blocks):
         return sum(block.astype(jnp.float32) for block in blocks).astype(jnp.bfloat16)

time: 135 us -> 132 us (0.978)
  waiting for transfers between devices: 35.5 us -> 43.3 us
  starting transfers between devices: 45.3 us -> 38 us
  local copies, waits for them, and re-layouts: 2.7 us -> 0.03 us
    ppermute x13, waiting for transfers between devices: 21.4 us -> 29.8 us  [over_z(): lax.ppermute(array, 'ep', [(i, (i + shift * n_y) % ep) for i in range(ep)])]
    ppermute x13, starting transfers between devices: 20.2 us -> 13.4 us  [over_z(): lax.ppermute(array, 'ep', [(i, (i + shift * n_y) % ep) for i in range(ep)])]
    ppermute x10, waiting for transfers between devices: 6.84 us -> 3.71 us  [over_x(): return lax.ppermute(array, 'tp', [(0, 1), (1, 0)])]
    unnamed x14 -> x4, local copies, waits for them, and re-layouts: 2.68 us -> 0.01 us
    ppermute x5, waiting for transfers between devices: 0.01 us -> 1.52 us  [over_role(): return lax.ppermute(array, 'role', [(0, 1), (1, 0)])]
  transfers between devices with their start and end apart: 39 -> 39, of which waited for: 8 -> 12; matrix products, arithmetic and copies ran while one was open for 1% -> 1% of each run, Pallas kernels for 34% -> 35%
where the time goes in v17:
time: 132 us
  Pallas kernels  47.6 us (36%)
  waiting for transfers between devices  43.3 us (33%)
  starting transfers between devices  38 us (29%)
  other arithmetic  2.4 us (2%)
    pallas_call x3, Pallas kernels, rows_call(): pl.pallas_call(functools.partial(rows_kernel, count, ways, capacity, slot...  31.6 us
    ppermute x13, waiting for transfers between devices, over_z(): lax.ppermute(array, 'ep', [(i, (i + shift * n_y) % ep) for i in range(ep)])  29.8 us
    ppermute x13, starting transfers between devices, over_z(): lax.ppermute(array, 'ep', [(i, (i + shift * n_y) % ep) for i in range(ep)])  13.4 us
    ppermute x10, starting transfers between devices, over_x(): return lax.ppermute(array, 'tp', [(0, 1), (1, 0)])  12.4 us
    ppermute x11, starting transfers between devices, over_y(): lax.ppermute(array, 'ep', [(i, i + 1 - 2 * (i % n_y)) for i in range(ep)])  11 us
    pallas_call x2, Pallas kernels, grads_call(): pl.pallas_call(functools.partial(grads_kernel, count, *starts, 2 * per),...  10.8 us
    ppermute x11, waiting for transfers between devices, over_y(): lax.ppermute(array, 'ep', [(i, i + 1 - 2 * (i % n_y)) for i in range(ep)])  8.33 us
    ppermute x10, waiting for transfers between devices, over_x(): return lax.ppermute(array, 'tp', [(0, 1), (1, 0)])  3.71 us
  transfers between devices with their start and end apart: 39, of which 12 were waited for; matrix products, arithmetic and copies ran while one was open for 1% of the time, Pallas kernels for 35%

profile of v17, /device:TPU:0, one launch (start us, length us, event | category | flops | bytes accessed | tf_op | source)
XLA Modules:
  0.0 132.3 jit_solution(10048001286977905036)
XLA Ops:
  0.6 1.8 %join.1.refs_4_ = bf16[256,1024]{1,0:T(8,128)(2,1)} custom-call(bf16[128,1024]{1,0:T(8,128)(2,1)} %top_ref.1, bf16[128,1024]{1,0:T(8,128)(2,1)} %bottom_ref.1), custom_call_target="tpu_custom_call" | custom-call | bytes 1048576 | tf_op jit(solution)/shard_map/join/pallas_call | solution.py:180
  2.5 3.1 %collective-permute-start = (bf16[256,1024]{1,0:T(8,128)(2,1)}, bf16[256,1024]{1,0:T(8,128)(2,1)}, u32[]{:S(2)}, u32[]{:S(2)}) collective-permute-start(bf16[256,1024]{1,0:T(8,128)(2,1)} %join.1.refs_4_), channel_id=1, source_target_pairs={{0,4},{2,6},{4,8},{6,10},{8,12},{10,14},{12,0},{14,2},{1,5},{3,7},... | collective-permute-start | bytes 1572872 | tf_op jit(solution)/shard_map/ppermute | solution.py:456
  5.6 1.5 %collective-permute-start.1 = (bf16[256,1024]{1,0:T(8,128)(2,1)}, bf16[256,1024]{1,0:T(8,128)(2,1)}, u32[]{:S(2)}, u32[]{:S(2)}) collective-permute-start(bf16[256,1024]{1,0:T(8,128)(2,1)} %join.1.refs_4_), channel_id=1, source_target_pairs={{0,2},{2,0},{4,6},{6,4},{8,10},{10,8},{12,14},{14,12},{1,3},{3,1},... | collective-permute-start | bytes 1572872 | tf_op jit(solution)/shard_map/ppermute | solution.py:453
  7.1 1.5 %collective-permute-start.2 = (bf16[256,1024]{1,0:T(8,128)(2,1)}, bf16[256,1024]{1,0:T(8,128)(2,1)}, u32[]{:S(2)}, u32[]{:S(2)}) collective-permute-start(bf16[256,1024]{1,0:T(8,128)(2,1)} %join.1.refs_4_), channel_id=1, source_target_pairs={{0,1},{1,0},{2,3},{3,2},{4,5},{5,4},{6,7},{7,6},{8,9},{9,8},{10,11... | collective-permute-start | bytes 1572872 | tf_op jit(solution)/shard_map/ppermute | solution.py:447
  8.6 3.4 %weights.1 = (bf16[2048,768]{1,0:T(8,128)(2,1)S(1)}, bf16[384,2048]{1,0:T(8,128)(2,1)}) custom-call(s32[1]{0:T(128)} %bitcast.2.tp_ref, bf16[1,2048,384]{2,1,0:T(8,128)(2,1)} %wg_ref.1, bf16[1,2048,384]{2,1,0:T(8,128)(2,1)} %wu_ref.1, bf16[1,384,2048]{2,1,0:T(8,128)(2,1)} %wd_ref.1), custom_call_target="tpu_custom_call" | custom-call | bytes 9437184 | tf_op jit(solution)/shard_map/weights/pallas_call | solution.py:141
  12.0 7.8 %collective-permute-done.refs_4_ = bf16[256,1024]{1,0:T(8,128)(2,1)} collective-permute-done((bf16[256,1024]{1,0:T(8,128)(2,1)}, bf16[256,1024]{1,0:T(8,128)(2,1)}, u32[]{:S(2)}, u32[]{:S(2)}) %collective-permute-start) | collective-permute-done | bytes 524320 | tf_op jit(solution)/shard_map/ppermute | solution.py:456
  19.8 0.7 collective-permute-done.2.refs_5_
  20.5 0.5 collective-permute-start.4
  21.0 1.6 %collective-permute-start.7 = (bf16[256,1024]{1,0:T(8,128)(2,1)}, bf16[256,1024]{1,0:T(8,128)(2,1)}, u32[]{:S(2)}, u32[]{:S(2)}) collective-permute-start(bf16[256,1024]{1,0:T(8,128)(2,1)} %collective-permute-done.refs_4_), channel_id=1, source_target_pairs={{0,4},{2,6},{4,8},{6,10},{8,12},{10,14},{12,0},{14,2},{1,5},{3,7},... | collective-permute-start | bytes 1572872 | tf_op jit(solution)/shard_map/ppermute | solution.py:456
  22.6 1.5 %collective-permute-start.5 = (bf16[256,1024]{1,0:T(8,128)(2,1)}, bf16[256,1024]{1,0:T(8,128)(2,1)}, u32[]{:S(2)}, u32[]{:S(2)}) collective-permute-start(bf16[256,1024]{1,0:T(8,128)(2,1)} %collective-permute-done.1.refs_6_), channel_id=1, source_target_pairs={{0,1},{1,0},{2,3},{3,2},{4,5},{5,4},{6,7},{7,6},{8,9},{9,8},{10,11... | collective-permute-start | bytes 1572872 | tf_op jit(solution)/shard_map/ppermute | solution.py:447
  24.1 0.5 collective-permute-start.8
  24.6 12.3 %collective-permute-done.7.refs_8_ = bf16[256,1024]{1,0:T(8,128)(2,1)} collective-permute-done((bf16[256,1024]{1,0:T(8,128)(2,1)}, bf16[256,1024]{1,0:T(8,128)(2,1)}, u32[]{:S(2)}, u32[]{:S(2)}) %collective-permute-start.7) | collective-permute-done | bytes 524320 | tf_op jit(solution)/shard_map/ppermute | solution.py:456
  37.0 0.9 collective-permute-start.6
  37.9 0.8 collective-permute-start.11
  38.7 1.5 %collective-permute-start.9 = (bf16[256,1024]{1,0:T(8,128)(2,1)}, bf16[256,1024]{1,0:T(8,128)(2,1)S(1)}, u32[]{:S(2)}, u32[]{:S(2)}) collective-permute-start(bf16[256,1024]{1,0:T(8,128)(2,1)} %collective-permute-done.7.refs_8_), channel_id=1, source_target_pairs={{0,1},{1,0},{2,3},{3,2},{4,5},{5,4},{6,7},{7,6},{8,9},{9,8},{10,11... | collective-permute-start | bytes 1572872 | tf_op jit(solution)/shard_map/ppermute | solution.py:447
  40.6 0.9 collective-permute-start.13
  41.6 9.5 %rows.3 = (bf16[144,5248]{1,0:T(8,128)(2,1)S(1)}, bf16[144,5248]{1,0:T(8,128)(2,1)S(1)}, bf16[1,136,1024]{2,1,0:T(8,128)(2,1)S(1)}, bf16[1,136,1024]{2,1,0:T(8,1...) custom-call(s32[3]{0:T(128)S(1)} %pad_add_fusion.where_ref, ...), custom_call_target="tpu_custom_call" | custom-call | flops 3170893824 | bytes 13631488 | tf_op jit(solution)/shard_map/rows/pallas_call | solution.py:321
  51.1 1.1 collective-permute-start.12
  52.6 1.0 collective-permute-start.14
  53.6 1.5 %collective-permute-start.10 = (bf16[256,1024]{1,0:T(8,128)(2,1)}, bf16[256,1024]{1,0:T(8,128)(2,1)S(1)}, u32[]{:S(2)}, u32[]{:S(2)}) collective-permute-start(bf16[256,1024]{1,0:T(8,128)(2,1)} %collective-permute-done.refs_4_), channel_id=1, source_target_pairs={{0,1},{1,0},{2,3},{3,2},{4,5},{5,4},{6,7},{7,6},{8,9},{9,8},{10,11... | collective-permute-start | bytes 1572872 | tf_op jit(solution)/shard_map/ppermute | solution.py:447
  55.4 2.7 %collective-permute-start.16 = (bf16[2,16,128]{2,1,0:T(8,128)(2,1)S(1)}, bf16[2,16,128]{2,1,0:T(8,128)(2,1)S(1)}, u32[]{:S(2)}, u32[]{:S(2)}) collective-permute-start(bf16[2,16,128]{2,1,0:T(8,128)(2,1)S(1)} %pad_maximum_fusion.refs_8_), channel_id=1, source_target_pairs={{0,8},{2,10},{4,12},{6,14},{8,0},{10,2},{12,4},{14,6},{1,9},{3,11}... | collective-permute-start | bytes 24584 | tf_op jit(solution)/shard_map/ppermute | solution.py:456
  58.1 7.4 %collective-permute-done.12.refs_7_ = bf16[256,1024]{1,0:T(8,128)(2,1)S(1)} collective-permute-done((bf16[256,1024]{1,0:T(8,128)(2,1)}, bf16[256,1024]{1,0:T(8,128)(2,1)S(1)}, u32[]{:S(2)}, u32[]{:S(2)}) %collective-permute-start.12) | collective-permute-done | bytes 524320 | tf_op jit(solution)/shard_map/ppermute | solution.py:456
  65.7 0.7 collective-permute-start.18
  66.4 0.9 collective-permute-start.19
  67.3 1.5 %collective-permute-start.20 = (bf16[256,1024]{1,0:T(8,128)(2,1)}, bf16[256,1024]{1,0:T(8,128)(2,1)S(1)}, u32[]{:S(2)}, u32[]{:S(2)}) collective-permute-start(bf16[256,1024]{1,0:T(8,128)(2,1)} %collective-permute-done.11.refs_4_), channel_id=1, source_target_pairs={{0,1},{1,0},{2,3},{3,2},{4,5},{5,4},{6,7},{7,6},{8,9},{9,8},{10,11... | collective-permute-start | bytes 1572872 | tf_op jit(solution)/shard_map/ppermute | solution.py:447
  69.3 12.9 %rows.4 = (bf16[288,5248]{1,0:T(8,128)(2,1)S(1)}, bf16[288,5248]{1,0:T(8,128)(2,1)S(1)}, bf16[1,136,1024]{2,1,0:T(8,128)(2,1)S(1)}, bf16[1,136,1024]{2,1,0:T(8,1...) custom-call(s32[3]{0:T(128)S(1)} %pad_add_fusion.where_ref, ...), custom_call_target="tpu_custom_call" | custom-call | flops 6341787648 | bytes 17825792 | tf_op jit(solution)/shard_map/rows/pallas_call | solution.py:321
  82.3 0.5 collective-permute-start.28
  82.8 0.8 collective-permute-start.24
  83.6 1.7 %collective-permute-start.23 = (bf16[1,136,1024]{2,1,0:T(8,128)(2,1)S(1)}, bf16[1,136,1024]{2,1,0:T(8,128)(2,1)S(1)}, u32[]{:S(2)}, u32[]{:S(2)}) collective-permute-start(bf16[1,136,1024]{2,1,0:T(8,128)(2,1)S(1)} %get-tuple-element.110), channel_id=1, source_target_pairs={{0,1},{1,0},{2,3},{3,2},{4,5},{5,4},{6,7},{7,6},{8,9},{9,8},{10,11... | collective-permute-start | bytes 835592 | tf_op jit(solution)/shard_map/ppermute | solution.py:447
  85.3 2.1 %collective-permute-start.22 = (bf16[1,136,1024]{2,1,0:T(8,128)(2,1)S(1)}, bf16[1,136,1024]{2,1,0:T(8,128)(2,1)S(1)}, u32[]{:S(2)}, u32[]{:S(2)}) collective-permute-start(bf16[1,136,1024]{2,1,0:T(8,128)(2,1)S(1)} %get-tuple-element.102), channel_id=1, source_target_pairs={{0,12},{2,14},{4,0},{6,2},{8,4},{10,6},{12,8},{14,10},{1,13},{3,15... | collective-permute-start | bytes 835592 | tf_op jit(solution)/shard_map/ppermute | solution.py:456
  87.4 9.3 %rows.5 = (bf16[144,5248]{1,0:T(8,128)(2,1)S(1)}, bf16[144,5248]{1,0:T(8,128)(2,1)S(1)}, bf16[1,136,1024]{2,1,0:T(8,128)(2,1)S(1)}, bf16[1,136,1024]{2,1,0:T(8,1...) custom-call(s32[3]{0:T(128)S(1)} %pad_add_fusion.where_ref, ...), custom_call_target="tpu_custom_call" | custom-call | flops 3170893824 | bytes 13631488 | tf_op jit(solution)/shard_map/rows/pallas_call | solution.py:321
  96.8 0.6 collective-permute-start.26
  97.5 1.1 collective-permute-start.27
  98.6 1.5 %collective-permute-done.30.refs_5_ = bf16[144,5248]{1,0:T(8,128)(2,1)S(1)} collective-permute-done((bf16[144,5248]{1,0:T(8,128)(2,1)S(1)}, bf16[144,5248]{1,0:T(8,128)(2,1)S(1)}, u32[]{:S(2)}, u32[]{:S(2)}) %collective-permute-start.30) | collective-permute-done | bytes 1511456 | tf_op jit(solution)/shard_map/ppermute | solution.py:450
  100.1 0.5 collective-permute-start.21
  100.6 1.5 %collective-permute-start.34 = (bf16[1,136,1024]{2,1,0:T(8,128)(2,1)S(1)}, bf16[1,136,1024]{2,1,0:T(8,128)(2,1)S(1)}, u32[]{:S(2)}, u32[]{:S(2)}) collective-permute-start(bf16[1,136,1024]{2,1,0:T(8,128)(2,1)S(1)} %get-tuple-element.126), channel_id=1, source_target_pairs={{0,1},{1,0},{2,3},{3,2},{4,5},{5,4},{6,7},{7,6},{8,9},{9,8},{10,11... | collective-permute-start | bytes 835592 | tf_op jit(solution)/shard_map/ppermute | solution.py:447
  102.1 4.4 %grads.2 = bf16[1,384,2048]{2,1,0:T(8,128)(2,1)} custom-call(s32[1]{0:T(128)} %bitcast.2.tp_ref, bf16[144,5248]{1,0:T(8,128)(2,1)S(1)} %get-tuple-element.84.refs_0_, bf16[144,5248]{1,0:T(8,128)(2,1)S(1)} %collective-permute-done.28.refs_1_, bf16[288,5248]{1,0:T(8,128)(2,1)S(1)} %get-tuple-element.103.refs_9_.refs_2_, ...), custom_call_target="tpu_custom_call" | custom-call | flops 1811939328 | bytes 5603328 | tf_op jit(solution)/shard_map/grads/pallas_call | solution.py:413
  106.6 1.1 collective-permute-start.35
  108.0 1.0 collective-permute-start.32
  109.3 3.0 %collective-permute-done.21 = bf16[1,136,1024]{2,1,0:T(8,128)(2,1)S(1)} collective-permute-done((bf16[1,136,1024]{2,1,0:T(8,128)(2,1)S(1)}, bf16[1,136,1024]{2,1,0:T(8,128)(2,1)S(1)}, u32[]{:S(2)}, u32[]{:S(2)}) %collective-permute-start.21) | collective-permute-done | bytes 278560 | tf_op jit(solution)/shard_map/ppermute | solution.py:447
  112.4 0.9 collective-permute-start.31
  113.3 7.5 %collective-permute-done.32 = bf16[1,136,1024]{2,1,0:T(8,128)(2,1)S(1)} collective-permute-done((bf16[1,136,1024]{2,1,0:T(8,128)(2,1)S(1)}, bf16[1,136,1024]{2,1,0:T(8,128)(2,1)S(1)}, u32[]{:S(2)}, u32[]{:S(2)}) %collective-permute-start.32) | collective-permute-done | bytes 278560 | tf_op jit(solution)/shard_map/ppermute | solution.py:453
  120.8 0.6 collective-permute-start.33
  121.7 1.1 collective-permute-start.38
  122.7 6.3 %grads.3 = (bf16[1,2048,384]{2,1,0:T(8,128)(2,1)}, bf16[1,2048,384]{2,1,0:T(8,128)(2,1)}) custom-call(s32[1]{0:T(128)} %bitcast.2.tp_ref, bf16[144,5248]{1,0:T(8,128)(2,1)S(1)} %get-tuple-element.84.refs_0_, bf16[144,5248]{1,0:T(8,128)(2,1)S(1)} %collective-permute-done.28.refs_1_, bf16[288,5248]{1,0:T(8,128)(2,1)S(1)} %get-tuple-element.103.refs_9_.refs_2_, ...), custom_call_target="tpu_custom_call" | custom-call | flops 3623878656 | bytes 6488064 | tf_op jit(solution)/shard_map/grads/pallas_call | solution.py:413
  129.1 1.6 %collective-permute-done.37 = bf16[1,136,1024]{2,1,0:T(8,128)(2,1)S(1)} collective-permute-done((bf16[1,136,1024]{2,1,0:T(8,128)(2,1)S(1)}, bf16[1,136,1024]{2,1,0:T(8,128)(2,1)S(1)}, u32[]{:S(2)}, u32[]{:S(2)}) %collective-permute-start.37) | collective-permute-done | bytes 278560 | tf_op jit(solution)/shard_map/ppermute | solution.py:456
  130.7 0.9 fusion
  131.7 0.6 select_reduce_fusion
  (57 shorter events, 3.2 us)
Async XLA Ops:
  2.5 17.3 %collective-permute-start = (bf16[256,1024]{1,0:T(8,128)(2,1)}, bf16[256,1024]{1,0:T(8,128)(2,1)}, u32[]{:S(2)}, u32[]{:S(2)}) collective-permute-start(bf16[256,1024]{1,0:T(8,128)(2,1)} %join.1.refs_4_), channel_id=1, source_target_pairs={{0,4},{2,6},{4,8},{6,10},{8,12},{10,14},{12,0},{14,2},{1,5},{3,7},... | collective-permute-start | bytes 1572872 | tf_op jit(solution)/shard_map/ppermute | solution.py:456
  5.6 14.3 %collective-permute-start.1 = (bf16[256,1024]{1,0:T(8,128)(2,1)}, bf16[256,1024]{1,0:T(8,128)(2,1)}, u32[]{:S(2)}, u32[]{:S(2)}) collective-permute-start(bf16[256,1024]{1,0:T(8,128)(2,1)} %join.1.refs_4_), channel_id=1, source_target_pairs={{0,2},{2,0},{4,6},{6,4},{8,10},{10,8},{12,14},{14,12},{1,3},{3,1},... | collective-permute-start | bytes 1572872 | tf_op jit(solution)/shard_map/ppermute | solution.py:453
  7.1 13.4 %collective-permute-start.2 = (bf16[256,1024]{1,0:T(8,128)(2,1)}, bf16[256,1024]{1,0:T(8,128)(2,1)}, u32[]{:S(2)}, u32[]{:S(2)}) collective-permute-start(bf16[256,1024]{1,0:T(8,128)(2,1)} %join.1.refs_4_), channel_id=1, source_target_pairs={{0,1},{1,0},{2,3},{3,2},{4,5},{5,4},{6,7},{7,6},{8,9},{9,8},{10,11... | collective-permute-start | bytes 1572872 | tf_op jit(solution)/shard_map/ppermute | solution.py:447
  8.6 16.0 %copy-start.1 = (bf16[128,8]{0,1:T(8,128)(2,1)S(1)}, bf16[128,8]{0,1:T(8,128)(2,1)}, u32[]{:S(2)}) copy-start(bf16[128,8]{0,1:T(8,128)(2,1)} %param.10) | copy-start | bytes 6148
  8.6 16.0 %copy-start = (s32[128,8]{0,1:T(8,128)S(1)}, s32[128,8]{0,1:T(8,128)}, u32[]{:S(2)}) copy-start(s32[128,8]{0,1:T(8,128)} %param.9) | copy-start | bytes 12292
  20.5 21.1 %collective-permute-start.3 = (bf16[2048,768]{1,0:T(8,128)(2,1)S(1)}, bf16[2048,768]{1,0:T(8,128)(2,1)}, u32[]{:S(2)}, u32[]{:S(2)}) collective-permute-start(bf16[2048,768]{1,0:T(8,128)(2,1)S(1)} %get-tuple-element.74.refs_0_), channel_id=1, source_target_pairs={{0,16},{16,0},{1,17},{17,1},{2,18},{18,2},{3,19},{19,3},{4,20},{20... | collective-permute-start | bytes 9437192 | tf_op jit(solution)/shard_map/ppermute | solution.py:450
  20.5 21.1 %collective-permute-start.4 = (bf16[384,2048]{1,0:T(8,128)(2,1)}, bf16[384,2048]{1,0:T(8,128)(2,1)}, u32[]{:S(2)}, u32[]{:S(2)}) collective-permute-start(bf16[384,2048]{1,0:T(8,128)(2,1)} %get-tuple-element.75.refs_2_), channel_id=1, source_target_pairs={{0,16},{16,0},{1,17},{17,1},{2,18},{18,2},{3,19},{19,3},{4,20},{20... | collective-permute-start | bytes 4718600 | tf_op jit(solution)/shard_map/ppermute | solution.py:450
  21.0 15.9 %collective-permute-start.7 = (bf16[256,1024]{1,0:T(8,128)(2,1)}, bf16[256,1024]{1,0:T(8,128)(2,1)}, u32[]{:S(2)}, u32[]{:S(2)}) collective-permute-start(bf16[256,1024]{1,0:T(8,128)(2,1)} %collective-permute-done.refs_4_), channel_id=1, source_target_pairs={{0,4},{2,6},{4,8},{6,10},{8,12},{10,14},{12,0},{14,2},{1,5},{3,7},... | collective-permute-start | bytes 1572872 | tf_op jit(solution)/shard_map/ppermute | solution.py:456
  22.6 15.3 %collective-permute-start.5 = (bf16[256,1024]{1,0:T(8,128)(2,1)}, bf16[256,1024]{1,0:T(8,128)(2,1)}, u32[]{:S(2)}, u32[]{:S(2)}) collective-permute-start(bf16[256,1024]{1,0:T(8,128)(2,1)} %collective-permute-done.1.refs_6_), channel_id=1, source_target_pairs={{0,1},{1,0},{2,3},{3,2},{4,5},{5,4},{6,7},{7,6},{8,9},{9,8},{10,11... | collective-permute-start | bytes 1572872 | tf_op jit(solution)/shard_map/ppermute | solution.py:447
  24.1 14.6 %collective-permute-start.8 = (bf16[256,1024]{1,0:T(8,128)(2,1)}, bf16[256,1024]{1,0:T(8,128)(2,1)}, u32[]{:S(2)}, u32[]{:S(2)}) collective-permute-start(bf16[256,1024]{1,0:T(8,128)(2,1)} %collective-permute-done.refs_4_), channel_id=1, source_target_pairs={{0,2},{2,0},{4,6},{6,4},{8,10},{10,8},{12,14},{14,12},{1,3},{3,1},... | collective-permute-start | bytes 1572872 | tf_op jit(solution)/shard_map/ppermute | solution.py:453
  37.0 3.6 %collective-permute-start.6 = (bf16[16,128]{1,0:T(8,128)(2,1)S(1)}, bf16[16,128]{1,0:T(8,128)(2,1)S(1)}, u32[]{:S(2)}, u32[]{:S(2)}) collective-permute-start(bf16[16,128]{1,0:T(8,128)(2,1)S(1)} %get-tuple-element.140), channel_id=1, source_target_pairs={{0,2},{2,0},{4,6},{6,4},{8,10},{10,8},{12,14},{14,12},{1,3},{3,1},... | collective-permute-start | bytes 12296 | tf_op jit(solution)/shard_map/ppermute | solution.py:453
  37.9 13.2 %collective-permute-start.11 = (bf16[256,1024]{1,0:T(8,128)(2,1)}, bf16[256,1024]{1,0:T(8,128)(2,1)}, u32[]{:S(2)}, u32[]{:S(2)}) collective-permute-start(bf16[256,1024]{1,0:T(8,128)(2,1)} %join.1.refs_4_), channel_id=1, source_target_pairs={{0,12},{2,14},{4,0},{6,2},{8,4},{10,6},{12,8},{14,10},{1,13},{3,15... | collective-permute-start | bytes 1572872 | tf_op jit(solution)/shard_map/ppermute | solution.py:456
  38.7 13.4 %collective-permute-start.9 = (bf16[256,1024]{1,0:T(8,128)(2,1)}, bf16[256,1024]{1,0:T(8,128)(2,1)S(1)}, u32[]{:S(2)}, u32[]{:S(2)}) collective-permute-start(bf16[256,1024]{1,0:T(8,128)(2,1)} %collective-permute-done.7.refs_8_), channel_id=1, source_target_pairs={{0,1},{1,0},{2,3},{3,2},{4,5},{5,4},{6,7},{7,6},{8,9},{9,8},{10,11... | collective-permute-start | bytes 1572872 | tf_op jit(solution)/shard_map/ppermute | solution.py:447
  40.6 12.1 %collective-permute-start.13 = (bf16[256,1024]{1,0:T(8,128)(2,1)}, bf16[256,1024]{1,0:T(8,128)(2,1)S(1)}, u32[]{:S(2)}, u32[]{:S(2)}) collective-permute-start(bf16[256,1024]{1,0:T(8,128)(2,1)} %collective-permute-done.7.refs_8_), channel_id=1, source_target_pairs={{0,2},{2,0},{4,6},{6,4},{8,10},{10,8},{12,14},{14,12},{1,3},{3,1},... | collective-permute-start | bytes 1572872 | tf_op jit(solution)/shard_map/ppermute | solution.py:453
  51.1 14.4 %collective-permute-start.12 = (bf16[256,1024]{1,0:T(8,128)(2,1)}, bf16[256,1024]{1,0:T(8,128)(2,1)S(1)}, u32[]{:S(2)}, u32[]{:S(2)}) collective-permute-start(bf16[256,1024]{1,0:T(8,128)(2,1)} %collective-permute-done.5.refs_7_), channel_id=1, source_target_pairs={{0,4},{2,6},{4,8},{6,10},{8,12},{10,14},{12,0},{14,2},{1,5},{3,7},... | collective-permute-start | bytes 1572872 | tf_op jit(solution)/shard_map/ppermute | solution.py:456
  52.6 13.1 %collective-permute-start.14 = (bf16[256,1024]{1,0:T(8,128)(2,1)S(1)}, bf16[256,1024]{1,0:T(8,128)(2,1)S(1)}, u32[]{:S(2)}, u32[]{:S(2)}) collective-permute-start(bf16[256,1024]{1,0:T(8,128)(2,1)S(1)} %collective-permute-done.9.refs_9_), channel_id=1, source_target_pairs={{0,2},{2,0},{4,6},{6,4},{8,10},{10,8},{12,14},{14,12},{1,3},{3,1},... | collective-permute-start | bytes 1572872 | tf_op jit(solution)/shard_map/ppermute | solution.py:453
  53.6 12.7 %collective-permute-start.10 = (bf16[256,1024]{1,0:T(8,128)(2,1)}, bf16[256,1024]{1,0:T(8,128)(2,1)S(1)}, u32[]{:S(2)}, u32[]{:S(2)}) collective-permute-start(bf16[256,1024]{1,0:T(8,128)(2,1)} %collective-permute-done.refs_4_), channel_id=1, source_target_pairs={{0,1},{1,0},{2,3},{3,2},{4,5},{5,4},{6,7},{7,6},{8,9},{9,8},{10,11... | collective-permute-start | bytes 1572872 | tf_op jit(solution)/shard_map/ppermute | solution.py:447
  55.2 12.2 %collective-permute-start.15 = (bf16[2,16,128]{2,1,0:T(8,128)(2,1)S(1)}, bf16[2,16,128]{2,1,0:T(8,128)(2,1)S(1)}, u32[]{:S(2)}, u32[]{:S(2)}) collective-permute-start(bf16[2,16,128]{2,1,0:T(8,128)(2,1)S(1)} %pad_maximum_fusion.refs_8_), channel_id=1, source_target_pairs={{0,4},{2,6},{4,8},{6,10},{8,12},{10,14},{12,0},{14,2},{1,5},{3,7},... | collective-permute-start | bytes 24584 | tf_op jit(solution)/shard_map/ppermute | solution.py:456
  55.4 13.4 %collective-permute-start.16 = (bf16[2,16,128]{2,1,0:T(8,128)(2,1)S(1)}, bf16[2,16,128]{2,1,0:T(8,128)(2,1)S(1)}, u32[]{:S(2)}, u32[]{:S(2)}) collective-permute-start(bf16[2,16,128]{2,1,0:T(8,128)(2,1)S(1)} %pad_maximum_fusion.refs_8_), channel_id=1, source_target_pairs={{0,8},{2,10},{4,12},{6,14},{8,0},{10,2},{12,4},{14,6},{1,9},{3,11}... | collective-permute-start | bytes 24584 | tf_op jit(solution)/shard_map/ppermute | solution.py:456
  65.5 3.8 %collective-permute-start.17 = (bf16[2,16,128]{2,1,0:T(8,128)(2,1)S(1)}, bf16[2,16,128]{2,1,0:T(8,128)(2,1)S(1)}, u32[]{:S(2)}, u32[]{:S(2)}) collective-permute-start(bf16[2,16,128]{2,1,0:T(8,128)(2,1)S(1)} %pad_maximum_fusion.refs_8_), channel_id=1, source_target_pairs={{0,12},{2,14},{4,0},{6,2},{8,4},{10,6},{12,8},{14,10},{1,13},{3,15... | collective-permute-start | bytes 24584 | tf_op jit(solution)/shard_map/ppermute | solution.py:456
  65.7 16.5 %collective-permute-start.18 = (bf16[256,1024]{1,0:T(8,128)(2,1)}, bf16[256,1024]{1,0:T(8,128)(2,1)S(1)}, u32[]{:S(2)}, u32[]{:S(2)}) collective-permute-start(bf16[256,1024]{1,0:T(8,128)(2,1)} %collective-permute-done.5.refs_7_), channel_id=1, source_target_pairs={{0,12},{2,14},{4,0},{6,2},{8,4},{10,6},{12,8},{14,10},{1,13},{3,15... | collective-permute-start | bytes 1572872 | tf_op jit(solution)/shard_map/ppermute | solution.py:456
  66.4 15.8 %collective-permute-start.19 = (bf16[256,1024]{1,0:T(8,128)(2,1)}, bf16[256,1024]{1,0:T(8,128)(2,1)S(1)}, u32[]{:S(2)}, u32[]{:S(2)}) collective-permute-start(bf16[256,1024]{1,0:T(8,128)(2,1)} %collective-permute-done.11.refs_4_), channel_id=1, source_target_pairs={{0,2},{2,0},{4,6},{6,4},{8,10},{10,8},{12,14},{14,12},{1,3},{3,1},... | collective-permute-start | bytes 1572872 | tf_op jit(solution)/shard_map/ppermute | solution.py:453
  67.3 14.9 %collective-permute-start.20 = (bf16[256,1024]{1,0:T(8,128)(2,1)}, bf16[256,1024]{1,0:T(8,128)(2,1)S(1)}, u32[]{:S(2)}, u32[]{:S(2)}) collective-permute-start(bf16[256,1024]{1,0:T(8,128)(2,1)} %collective-permute-done.11.refs_4_), channel_id=1, source_target_pairs={{0,1},{1,0},{2,3},{3,2},{4,5},{5,4},{6,7},{7,6},{8,9},{9,8},{10,11... | collective-permute-start | bytes 1572872 | tf_op jit(solution)/shard_map/ppermute | solution.py:447
  82.2 18.4 %collective-permute-start.29 = (bf16[288,5248]{1,0:T(8,128)(2,1)S(1)}, bf16[288,5248]{1,0:T(8,128)(2,1)S(1)}, u32[]{:S(2)}, u32[]{:S(2)}) collective-permute-start(bf16[288,5248]{1,0:T(8,128)(2,1)S(1)} %get-tuple-element.116), channel_id=1, source_target_pairs={{0,16},{16,0},{1,17},{17,1},{2,18},{18,2},{3,19},{19,3},{4,20},{20... | collective-permute-start | bytes 9068552 | tf_op jit(solution)/shard_map/ppermute | solution.py:450
  82.3 15.2 %collective-permute-start.28 = (bf16[144,5248]{1,0:T(8,128)(2,1)S(1)}, bf16[144,5248]{1,0:T(8,128)(2,1)S(1)}, u32[]{:S(2)}, u32[]{:S(2)}) collective-permute-start(bf16[144,5248]{1,0:T(8,128)(2,1)S(1)} %get-tuple-element.115), channel_id=1, source_target_pairs={{0,16},{16,0},{1,17},{17,1},{2,18},{18,2},{3,19},{19,3},{4,20},{20... | collective-permute-start | bytes 4534280 | tf_op jit(solution)/shard_map/ppermute | solution.py:450
  82.8 13.9 %collective-permute-start.24 = (bf16[1,136,1024]{2,1,0:T(8,128)(2,1)S(1)}, bf16[1,136,1024]{2,1,0:T(8,128)(2,1)S(1)}, u32[]{:S(2)}, u32[]{:S(2)}) collective-permute-start(bf16[1,136,1024]{2,1,0:T(8,128)(2,1)S(1)} %get-tuple-element.111), channel_id=1, source_target_pairs={{0,2},{2,0},{4,6},{6,4},{8,10},{10,8},{12,14},{14,12},{1,3},{3,1},... | collective-permute-start | bytes 835592 | tf_op jit(solution)/shard_map/ppermute | solution.py:453
  83.6 13.1 %collective-permute-start.23 = (bf16[1,136,1024]{2,1,0:T(8,128)(2,1)S(1)}, bf16[1,136,1024]{2,1,0:T(8,128)(2,1)S(1)}, u32[]{:S(2)}, u32[]{:S(2)}) collective-permute-start(bf16[1,136,1024]{2,1,0:T(8,128)(2,1)S(1)} %get-tuple-element.110), channel_id=1, source_target_pairs={{0,1},{1,0},{2,3},{3,2},{4,5},{5,4},{6,7},{7,6},{8,9},{9,8},{10,11... | collective-permute-start | bytes 835592 | tf_op jit(solution)/shard_map/ppermute | solution.py:447
  85.3 11.4 %collective-permute-start.22 = (bf16[1,136,1024]{2,1,0:T(8,128)(2,1)S(1)}, bf16[1,136,1024]{2,1,0:T(8,128)(2,1)S(1)}, u32[]{:S(2)}, u32[]{:S(2)}) collective-permute-start(bf16[1,136,1024]{2,1,0:T(8,128)(2,1)S(1)} %get-tuple-element.102), channel_id=1, source_target_pairs={{0,12},{2,14},{4,0},{6,2},{8,4},{10,6},{12,8},{14,10},{1,13},{3,15... | collective-permute-start | bytes 835592 | tf_op jit(solution)/shard_map/ppermute | solution.py:456
  96.7 3.4 %collective-permute-start.30 = (bf16[144,5248]{1,0:T(8,128)(2,1)S(1)}, bf16[144,5248]{1,0:T(8,128)(2,1)S(1)}, u32[]{:S(2)}, u32[]{:S(2)}) collective-permute-start(bf16[144,5248]{1,0:T(8,128)(2,1)S(1)} %get-tuple-element.118), channel_id=1, source_target_pairs={{0,16},{16,0},{1,17},{17,1},{2,18},{18,2},{3,19},{19,3},{4,20},{20... | collective-permute-start | bytes 4534280 | tf_op jit(solution)/shard_map/ppermute | solution.py:450
  96.8 9.8 %collective-permute-start.26 = (bf16[1,136,1024]{2,1,0:T(8,128)(2,1)S(1)}, bf16[1,136,1024]{2,1,0:T(8,128)(2,1)S(1)}, u32[]{:S(2)}, u32[]{:S(2)}) collective-permute-start(bf16[1,136,1024]{2,1,0:T(8,128)(2,1)S(1)} %get-tuple-element.113), channel_id=1, source_target_pairs={{0,1},{1,0},{2,3},{3,2},{4,5},{5,4},{6,7},{7,6},{8,9},{9,8},{10,11... | collective-permute-start | bytes 835592 | tf_op jit(solution)/shard_map/ppermute | solution.py:447
  97.4 10.5 %collective-permute-start.25 = (bf16[1,136,1024]{2,1,0:T(8,128)(2,1)S(1)}, bf16[1,136,1024]{2,1,0:T(8,128)(2,1)S(1)}, u32[]{:S(2)}, u32[]{:S(2)}) collective-permute-start(bf16[1,136,1024]{2,1,0:T(8,128)(2,1)S(1)} %get-tuple-element.112), channel_id=1, source_target_pairs={{0,4},{2,6},{4,8},{6,10},{8,12},{10,14},{12,0},{14,2},{1,5},{3,7},... | collective-permute-start | bytes 835592 | tf_op jit(solution)/shard_map/ppermute | solution.py:456
  97.5 10.4 %collective-permute-start.27 = (bf16[1,136,1024]{2,1,0:T(8,128)(2,1)S(1)}, bf16[1,136,1024]{2,1,0:T(8,128)(2,1)S(1)}, u32[]{:S(2)}, u32[]{:S(2)}) collective-permute-start(bf16[1,136,1024]{2,1,0:T(8,128)(2,1)S(1)} %add_convert_fusion.5), channel_id=1, source_target_pairs={{0,2},{2,0},{4,6},{6,4},{8,10},{10,8},{12,14},{14,12},{1,3},{3,1},... | collective-permute-start | bytes 835592 | tf_op jit(solution)/shard_map/ppermute | solution.py:453
  100.1 12.2 %collective-permute-start.21 = (bf16[1,136,1024]{2,1,0:T(8,128)(2,1)S(1)}, bf16[1,136,1024]{2,1,0:T(8,128)(2,1)S(1)}, u32[]{:S(2)}, u32[]{:S(2)}) collective-permute-start(bf16[1,136,1024]{2,1,0:T(8,128)(2,1)S(1)} %get-tuple-element.100), channel_id=1, source_target_pairs={{0,1},{1,0},{2,3},{3,2},{4,5},{5,4},{6,7},{7,6},{8,9},{9,8},{10,11... | collective-permute-start | bytes 835592 | tf_op jit(solution)/shard_map/ppermute | solution.py:447
  100.6 20.8 %collective-permute-start.34 = (bf16[1,136,1024]{2,1,0:T(8,128)(2,1)S(1)}, bf16[1,136,1024]{2,1,0:T(8,128)(2,1)S(1)}, u32[]{:S(2)}, u32[]{:S(2)}) collective-permute-start(bf16[1,136,1024]{2,1,0:T(8,128)(2,1)S(1)} %get-tuple-element.126), channel_id=1, source_target_pairs={{0,1},{1,0},{2,3},{3,2},{4,5},{5,4},{6,7},{7,6},{8,9},{9,8},{10,11... | collective-permute-start | bytes 835592 | tf_op jit(solution)/shard_map/ppermute | solution.py:447
  106.6 14.8 %collective-permute-start.35 = (bf16[1,136,1024]{2,1,0:T(8,128)(2,1)S(1)}, bf16[1,136,1024]{2,1,0:T(8,128)(2,1)S(1)}, u32[]{:S(2)}, u32[]{:S(2)}) collective-permute-start(bf16[1,136,1024]{2,1,0:T(8,128)(2,1)S(1)} %get-tuple-element.127), channel_id=1, source_target_pairs={{0,2},{2,0},{4,6},{6,4},{8,10},{10,8},{12,14},{14,12},{1,3},{3,1},... | collective-permute-start | bytes 835592 | tf_op jit(solution)/shard_map/ppermute | solution.py:453
  108.0 12.7 %collective-permute-start.32 = (bf16[1,136,1024]{2,1,0:T(8,128)(2,1)S(1)}, bf16[1,136,1024]{2,1,0:T(8,128)(2,1)S(1)}, u32[]{:S(2)}, u32[]{:S(2)}) collective-permute-start(bf16[1,136,1024]{2,1,0:T(8,128)(2,1)S(1)} %add_convert_fusion.4), channel_id=1, source_target_pairs={{0,2},{2,0},{4,6},{6,4},{8,10},{10,8},{12,14},{14,12},{1,3},{3,1},... | collective-permute-start | bytes 835592 | tf_op jit(solution)/shard_map/ppermute | solution.py:453
  109.2 12.2 %collective-permute-start.36 = (bf16[1,136,1024]{2,1,0:T(8,128)(2,1)S(1)}, bf16[1,136,1024]{2,1,0:T(8,128)(2,1)S(1)}, u32[]{:S(2)}, u32[]{:S(2)}) collective-permute-start(bf16[1,136,1024]{2,1,0:T(8,128)(2,1)S(1)} %add_convert_fusion.3), channel_id=1, source_target_pairs={{0,4},{2,6},{4,8},{6,10},{8,12},{10,14},{12,0},{14,2},{1,5},{3,7},... | collective-permute-start | bytes 835592 | tf_op jit(solution)/shard_map/ppermute | solution.py:456
  112.4 16.7 %collective-permute-start.31 = (bf16[1,136,1024]{2,1,0:T(8,128)(2,1)S(1)}, bf16[1,136,1024]{2,1,0:T(8,128)(2,1)S(1)}, u32[]{:S(2)}, u32[]{:S(2)}) collective-permute-start(bf16[1,136,1024]{2,1,0:T(8,128)(2,1)S(1)} %add_convert_fusion.2), channel_id=1, source_target_pairs={{0,12},{2,14},{4,0},{6,2},{8,4},{10,6},{12,8},{14,10},{1,13},{3,15... | collective-permute-start | bytes 835592 | tf_op jit(solution)/shard_map/ppermute | solution.py:456
  120.8 8.3 %collective-permute-start.33 = (bf16[1,136,1024]{2,1,0:T(8,128)(2,1)S(1)}, bf16[1,136,1024]{2,1,0:T(8,128)(2,1)S(1)}, u32[]{:S(2)}, u32[]{:S(2)}) collective-permute-start(bf16[1,136,1024]{2,1,0:T(8,128)(2,1)S(1)} %add_convert_fusion.1), channel_id=1, source_target_pairs={{0,1},{1,0},{2,3},{3,2},{4,5},{5,4},{6,7},{7,6},{8,9},{9,8},{10,11... | collective-permute-start | bytes 835592 | tf_op jit(solution)/shard_map/ppermute | solution.py:447
  121.6 9.1 %collective-permute-start.37 = (bf16[1,136,1024]{2,1,0:T(8,128)(2,1)S(1)}, bf16[1,136,1024]{2,1,0:T(8,128)(2,1)S(1)}, u32[]{:S(2)}, u32[]{:S(2)}) collective-permute-start(bf16[1,136,1024]{2,1,0:T(8,128)(2,1)S(1)} %add_convert_fusion), channel_id=1, source_target_pairs={{0,4},{2,6},{4,8},{6,10},{8,12},{10,14},{12,0},{14,2},{1,5},{3,7},... | collective-permute-start | bytes 835592 | tf_op jit(solution)/shard_map/ppermute | solution.py:456
  121.7 9.0 %collective-permute-start.38 = (bf16[1,136,1024]{2,1,0:T(8,128)(2,1)S(1)}, bf16[1,136,1024]{2,1,0:T(8,128)(2,1)S(1)}, u32[]{:S(2)}, u32[]{:S(2)}) collective-permute-start(bf16[1,136,1024]{2,1,0:T(8,128)(2,1)S(1)} %get-tuple-element.132), channel_id=1, source_target_pairs={{0,2},{2,0},{4,6},{6,4},{8,10},{10,8},{12,14},{14,12},{1,3},{3,1},... | collective-permute-start | bytes 835592 | tf_op jit(solution)/shard_map/ppermute | solution.py:453

commit v18 on v17

--- a/solution.py
+++ b/solution.py
@@ -534,13 +534,13 @@
         [mine_3, other_3, x_3, y_3, z_3, keep_2y], [from_x2, from_y1, from_z1]
     )
     from_z3, from_y2, from_x1 = over_z(z_3, 1), over_y(total(keep_2y, from_x2)), over_x(x_1)
-    from_x3, from_y3 = over_x(x_3), over_y(y_3)
+    from_y3 = over_y(y_3)
     packed = [mine_0, over_role(other_0), mine_1, over_role(other_1), mine_3, over_role(other_3)]
     (d_down,) = grads_call(which_ref, packed, width, part, True)
     from_z3, from_x20, from_y2 = tied([from_z3, from_x20, from_y2], [d_down])
     far, step_2 = total(far, from_z1, from_z3), total(keep_2, from_x20, from_y2)
-    (from_x1,) = tied([from_x1], [far, step_2])
-    from_far, from_z2 = over_y(far), over_z(step_2, 1)
+    from_x1, x_3 = tied([from_x1, x_3], [far, step_2])
+    from_far, from_z2, from_x3 = over_y(far), over_z(step_2, 1), over_x(x_3)
     home_1 = over_z(total(keep_1, from_x1, from_y1), -1)
     from_x0 = over_x(total(side_0, from_far))
     from_x3, from_y3, from_z2 = tied([from_x3, from_y3, from_z2], [from_far])

time: 132 us -> 132 us (level)
  starting transfers between devices: 38 us -> 39.6 us
  waiting for transfers between devices: 43.3 us -> 41.7 us
    ppermute x11, waiting for transfers between devices: 8.33 us -> 4.17 us  [over_y(): lax.ppermute(array, 'ep', [(i, i + 1 - 2 * (i % n_y)) for i in range(ep)])]
    ppermute x13, waiting for transfers between devices: 29.8 us -> 32.5 us  [over_z(): lax.ppermute(array, 'ep', [(i, (i + shift * n_y) % ep) for i in range(ep)])]
    ppermute x13, starting transfers between devices: 13.4 us -> 15.2 us  [over_z(): lax.ppermute(array, 'ep', [(i, (i + shift * n_y) % ep) for i in range(ep)])]
  transfers between devices with their start and end apart: 39 -> 39, of which waited for: 12 -> 15; matrix products, arithmetic and copies ran while one was open for 1% -> 1% of each run, Pallas kernels for 35% -> 35%
where the time goes in v18:
time: 132 us
  Pallas kernels  47.6 us (36%)
  waiting for transfers between devices  41.7 us (32%)
  starting transfers between devices  39.6 us (30%)
  other arithmetic  2.4 us (2%)
    ppermute x13, waiting for transfers between devices, over_z(): lax.ppermute(array, 'ep', [(i, (i + shift * n_y) % ep) for i in range(ep)])  32.5 us
    pallas_call x3, Pallas kernels, rows_call(): pl.pallas_call(functools.partial(rows_kernel, count, ways, capacity, slot...  31.6 us
    ppermute x13, starting transfers between devices, over_z(): lax.ppermute(array, 'ep', [(i, (i + shift * n_y) % ep) for i in range(ep)])  15.2 us
    ppermute x10, starting transfers between devices, over_x(): return lax.ppermute(array, 'tp', [(0, 1), (1, 0)])  12.4 us
    ppermute x11, starting transfers between devices, over_y(): lax.ppermute(array, 'ep', [(i, i + 1 - 2 * (i % n_y)) for i in range(ep)])  10.9 us
    pallas_call x2, Pallas kernels, grads_call(): pl.pallas_call(functools.partial(grads_kernel, count, *starts, 2 * per),...  10.8 us
    ppermute x11, waiting for transfers between devices, over_y(): lax.ppermute(array, 'ep', [(i, i + 1 - 2 * (i % n_y)) for i in range(ep)])  4.17 us
    ppermute x10, waiting for transfers between devices, over_x(): return lax.ppermute(array, 'tp', [(0, 1), (1, 0)])  3.56 us
  transfers between devices with their start and end apart: 39, of which 15 were waited for; matrix products, arithmetic and copies ran while one was open for 1% of the time, Pallas kernels for 35%

profile of v18, /device:TPU:0, one launch (start us, length us, event | category | flops | bytes accessed | tf_op | source)
XLA Modules:
  0.0 132.3 jit_solution(11910376473048127566)
XLA Ops:
  0.6 1.8 %join.1.refs_4_ = bf16[256,1024]{1,0:T(8,128)(2,1)} custom-call(bf16[128,1024]{1,0:T(8,128)(2,1)} %top_ref.1, bf16[128,1024]{1,0:T(8,128)(2,1)} %bottom_ref.1), custom_call_target="tpu_custom_call" | custom-call | bytes 1048576 | tf_op jit(solution)/shard_map/join/pallas_call | solution.py:180
  2.5 3.1 %collective-permute-start = (bf16[256,1024]{1,0:T(8,128)(2,1)}, bf16[256,1024]{1,0:T(8,128)(2,1)}, u32[]{:S(2)}, u32[]{:S(2)}) collective-permute-start(bf16[256,1024]{1,0:T(8,128)(2,1)} %join.1.refs_4_), channel_id=1, source_target_pairs={{0,4},{2,6},{4,8},{6,10},{8,12},{10,14},{12,0},{14,2},{1,5},{3,7},... | collective-permute-start | bytes 1572872 | tf_op jit(solution)/shard_map/ppermute | solution.py:456
  5.6 1.5 %collective-permute-start.1 = (bf16[256,1024]{1,0:T(8,128)(2,1)}, bf16[256,1024]{1,0:T(8,128)(2,1)}, u32[]{:S(2)}, u32[]{:S(2)}) collective-permute-start(bf16[256,1024]{1,0:T(8,128)(2,1)} %join.1.refs_4_), channel_id=1, source_target_pairs={{0,2},{2,0},{4,6},{6,4},{8,10},{10,8},{12,14},{14,12},{1,3},{3,1},... | collective-permute-start | bytes 1572872 | tf_op jit(solution)/shard_map/ppermute | solution.py:453
  7.1 1.5 %collective-permute-start.2 = (bf16[256,1024]{1,0:T(8,128)(2,1)}, bf16[256,1024]{1,0:T(8,128)(2,1)}, u32[]{:S(2)}, u32[]{:S(2)}) collective-permute-start(bf16[256,1024]{1,0:T(8,128)(2,1)} %join.1.refs_4_), channel_id=1, source_target_pairs={{0,1},{1,0},{2,3},{3,2},{4,5},{5,4},{6,7},{7,6},{8,9},{9,8},{10,11... | collective-permute-start | bytes 1572872 | tf_op jit(solution)/shard_map/ppermute | solution.py:447
  8.6 3.4 %weights.1 = (bf16[2048,768]{1,0:T(8,128)(2,1)S(1)}, bf16[384,2048]{1,0:T(8,128)(2,1)}) custom-call(s32[1]{0:T(128)} %bitcast.2.tp_ref, bf16[1,2048,384]{2,1,0:T(8,128)(2,1)} %wg_ref.1, bf16[1,2048,384]{2,1,0:T(8,128)(2,1)} %wu_ref.1, bf16[1,384,2048]{2,1,0:T(8,128)(2,1)} %wd_ref.1), custom_call_target="tpu_custom_call" | custom-call | bytes 9437184 | tf_op jit(solution)/shard_map/weights/pallas_call | solution.py:141
  12.0 7.8 %collective-permute-done.refs_4_ = bf16[256,1024]{1,0:T(8,128)(2,1)} collective-permute-done((bf16[256,1024]{1,0:T(8,128)(2,1)}, bf16[256,1024]{1,0:T(8,128)(2,1)}, u32[]{:S(2)}, u32[]{:S(2)}) %collective-permute-start) | collective-permute-done | bytes 524320 | tf_op jit(solution)/shard_map/ppermute | solution.py:456
  19.8 0.7 collective-permute-done.2.refs_5_
  20.5 0.5 collective-permute-start.4
  21.0 1.6 %collective-permute-start.7 = (bf16[256,1024]{1,0:T(8,128)(2,1)}, bf16[256,1024]{1,0:T(8,128)(2,1)}, u32[]{:S(2)}, u32[]{:S(2)}) collective-permute-start(bf16[256,1024]{1,0:T(8,128)(2,1)} %collective-permute-done.refs_4_), channel_id=1, source_target_pairs={{0,4},{2,6},{4,8},{6,10},{8,12},{10,14},{12,0},{14,2},{1,5},{3,7},... | collective-permute-start | bytes 1572872 | tf_op jit(solution)/shard_map/ppermute | solution.py:456
  22.6 1.5 %collective-permute-start.5 = (bf16[256,1024]{1,0:T(8,128)(2,1)}, bf16[256,1024]{1,0:T(8,128)(2,1)}, u32[]{:S(2)}, u32[]{:S(2)}) collective-permute-start(bf16[256,1024]{1,0:T(8,128)(2,1)} %collective-permute-done.1.refs_6_), channel_id=1, source_target_pairs={{0,1},{1,0},{2,3},{3,2},{4,5},{5,4},{6,7},{7,6},{8,9},{9,8},{10,11... | collective-permute-start | bytes 1572872 | tf_op jit(solution)/shard_map/ppermute | solution.py:447
  24.6 12.3 %collective-permute-done.7.refs_8_ = bf16[256,1024]{1,0:T(8,128)(2,1)} collective-permute-done((bf16[256,1024]{1,0:T(8,128)(2,1)}, bf16[256,1024]{1,0:T(8,128)(2,1)}, u32[]{:S(2)}, u32[]{:S(2)}) %collective-permute-start.7) | collective-permute-done | bytes 524320 | tf_op jit(solution)/shard_map/ppermute | solution.py:456
  37.0 0.9 collective-permute-start.6
  37.9 0.8 collective-permute-start.11
  38.7 1.5 %collective-permute-start.9 = (bf16[256,1024]{1,0:T(8,128)(2,1)}, bf16[256,1024]{1,0:T(8,128)(2,1)S(1)}, u32[]{:S(2)}, u32[]{:S(2)}) collective-permute-start(bf16[256,1024]{1,0:T(8,128)(2,1)} %collective-permute-done.7.refs_8_), channel_id=1, source_target_pairs={{0,1},{1,0},{2,3},{3,2},{4,5},{5,4},{6,7},{7,6},{8,9},{9,8},{10,11... | collective-permute-start | bytes 1572872 | tf_op jit(solution)/shard_map/ppermute | solution.py:447
  40.6 0.9 collective-permute-start.13
  41.6 9.5 %rows.3 = (bf16[144,5248]{1,0:T(8,128)(2,1)S(1)}, bf16[144,5248]{1,0:T(8,128)(2,1)S(1)}, bf16[1,136,1024]{2,1,0:T(8,128)(2,1)S(1)}, bf16[1,136,1024]{2,1,0:T(8,1...) custom-call(s32[3]{0:T(128)S(1)} %pad_add_fusion.where_ref, ...), custom_call_target="tpu_custom_call" | custom-call | flops 3170893824 | bytes 13631488 | tf_op jit(solution)/shard_map/rows/pallas_call | solution.py:321
  51.1 1.1 collective-permute-start.12
  52.6 1.0 collective-permute-start.14
  53.6 1.5 %collective-permute-start.10 = (bf16[256,1024]{1,0:T(8,128)(2,1)}, bf16[256,1024]{1,0:T(8,128)(2,1)S(1)}, u32[]{:S(2)}, u32[]{:S(2)}) collective-permute-start(bf16[256,1024]{1,0:T(8,128)(2,1)} %collective-permute-done.refs_4_), channel_id=1, source_target_pairs={{0,1},{1,0},{2,3},{3,2},{4,5},{5,4},{6,7},{7,6},{8,9},{9,8},{10,11... | collective-permute-start | bytes 1572872 | tf_op jit(solution)/shard_map/ppermute | solution.py:447
  55.4 2.7 %collective-permute-start.16 = (bf16[2,16,128]{2,1,0:T(8,128)(2,1)S(1)}, bf16[2,16,128]{2,1,0:T(8,128)(2,1)S(1)}, u32[]{:S(2)}, u32[]{:S(2)}) collective-permute-start(bf16[2,16,128]{2,1,0:T(8,128)(2,1)S(1)} %pad_maximum_fusion.refs_8_), channel_id=1, source_target_pairs={{0,8},{2,10},{4,12},{6,14},{8,0},{10,2},{12,4},{14,6},{1,9},{3,11}... | collective-permute-start | bytes 24584 | tf_op jit(solution)/shard_map/ppermute | solution.py:456
  58.1 7.4 %collective-permute-done.12.refs_7_ = bf16[256,1024]{1,0:T(8,128)(2,1)S(1)} collective-permute-done((bf16[256,1024]{1,0:T(8,128)(2,1)}, bf16[256,1024]{1,0:T(8,128)(2,1)S(1)}, u32[]{:S(2)}, u32[]{:S(2)}) %collective-permute-start.12) | collective-permute-done | bytes 524320 | tf_op jit(solution)/shard_map/ppermute | solution.py:456
  65.7 0.7 collective-permute-start.18
  66.4 0.9 collective-permute-start.19
  67.3 1.5 %collective-permute-start.20 = (bf16[256,1024]{1,0:T(8,128)(2,1)}, bf16[256,1024]{1,0:T(8,128)(2,1)S(1)}, u32[]{:S(2)}, u32[]{:S(2)}) collective-permute-start(bf16[256,1024]{1,0:T(8,128)(2,1)} %collective-permute-done.11.refs_4_), channel_id=1, source_target_pairs={{0,1},{1,0},{2,3},{3,2},{4,5},{5,4},{6,7},{7,6},{8,9},{9,8},{10,11... | collective-permute-start | bytes 1572872 | tf_op jit(solution)/shard_map/ppermute | solution.py:447
  69.3 12.9 %rows.4 = (bf16[288,5248]{1,0:T(8,128)(2,1)S(1)}, bf16[288,5248]{1,0:T(8,128)(2,1)S(1)}, bf16[1,136,1024]{2,1,0:T(8,128)(2,1)S(1)}, bf16[1,136,1024]{2,1,0:T(8,1...) custom-call(s32[3]{0:T(128)S(1)} %pad_add_fusion.where_ref, ...), custom_call_target="tpu_custom_call" | custom-call | flops 6341787648 | bytes 17825792 | tf_op jit(solution)/shard_map/rows/pallas_call | solution.py:321
  82.8 0.8 collective-permute-start.23
  83.6 1.7 %collective-permute-start.22 = (bf16[1,136,1024]{2,1,0:T(8,128)(2,1)S(1)}, bf16[1,136,1024]{2,1,0:T(8,128)(2,1)S(1)}, u32[]{:S(2)}, u32[]{:S(2)}) collective-permute-start(bf16[1,136,1024]{2,1,0:T(8,128)(2,1)S(1)} %get-tuple-element.109), channel_id=1, source_target_pairs={{0,1},{1,0},{2,3},{3,2},{4,5},{5,4},{6,7},{7,6},{8,9},{9,8},{10,11... | collective-permute-start | bytes 835592 | tf_op jit(solution)/shard_map/ppermute | solution.py:447
  85.3 2.1 %collective-permute-start.24 = (bf16[1,136,1024]{2,1,0:T(8,128)(2,1)S(1)}, bf16[1,136,1024]{2,1,0:T(8,128)(2,1)S(1)}, u32[]{:S(2)}, u32[]{:S(2)}) collective-permute-start(bf16[1,136,1024]{2,1,0:T(8,128)(2,1)S(1)} %get-tuple-element.111), channel_id=1, source_target_pairs={{0,12},{2,14},{4,0},{6,2},{8,4},{10,6},{12,8},{14,10},{1,13},{3,15... | collective-permute-start | bytes 835592 | tf_op jit(solution)/shard_map/ppermute | solution.py:456
  87.4 9.3 %rows.5 = (bf16[144,5248]{1,0:T(8,128)(2,1)S(1)}, bf16[144,5248]{1,0:T(8,128)(2,1)S(1)}, bf16[1,136,1024]{2,1,0:T(8,128)(2,1)S(1)}, bf16[1,136,1024]{2,1,0:T(8,1...) custom-call(s32[3]{0:T(128)S(1)} %pad_add_fusion.where_ref, ...), custom_call_target="tpu_custom_call" | custom-call | flops 3170893824 | bytes 13631488 | tf_op jit(solution)/shard_map/rows/pallas_call | solution.py:321
  96.8 0.6 collective-permute-start.26
  97.5 1.1 collective-permute-start.27
  98.6 1.5 %collective-permute-done.30.refs_5_ = bf16[144,5248]{1,0:T(8,128)(2,1)S(1)} collective-permute-done((bf16[144,5248]{1,0:T(8,128)(2,1)S(1)}, bf16[144,5248]{1,0:T(8,128)(2,1)S(1)}, u32[]{:S(2)}, u32[]{:S(2)}) %collective-permute-start.30) | collective-permute-done | bytes 1511456 | tf_op jit(solution)/shard_map/ppermute | solution.py:450
  100.1 0.5 collective-permute-start.21
  100.6 1.0 collective-permute-start.35
  101.6 4.4 %grads.2 = bf16[1,384,2048]{2,1,0:T(8,128)(2,1)} custom-call(s32[1]{0:T(128)} %bitcast.2.tp_ref, bf16[144,5248]{1,0:T(8,128)(2,1)S(1)} %get-tuple-element.85.refs_0_, bf16[144,5248]{1,0:T(8,128)(2,1)S(1)} %collective-permute-done.28.refs_1_, bf16[288,5248]{1,0:T(8,128)(2,1)S(1)} %get-tuple-element.102.refs_9_.refs_2_, ...), custom_call_target="tpu_custom_call" | custom-call | flops 1811939328 | bytes 5603328 | tf_op jit(solution)/shard_map/grads/pallas_call | solution.py:413
  106.3 1.6 %collective-permute-done.25 = bf16[1,136,1024]{2,1,0:T(8,128)(2,1)S(1)} collective-permute-done((bf16[1,136,1024]{2,1,0:T(8,128)(2,1)S(1)}, bf16[1,136,1024]{2,1,0:T(8,128)(2,1)S(1)}, u32[]{:S(2)}, u32[]{:S(2)}) %collective-permute-start.25) | collective-permute-done | bytes 278560 | tf_op jit(solution)/shard_map/ppermute | solution.py:456
  108.0 1.0 collective-permute-start.32
  109.5 2.4 %collective-permute-done.21 = bf16[1,136,1024]{2,1,0:T(8,128)(2,1)S(1)} collective-permute-done((bf16[1,136,1024]{2,1,0:T(8,128)(2,1)S(1)}, bf16[1,136,1024]{2,1,0:T(8,128)(2,1)S(1)}, u32[]{:S(2)}, u32[]{:S(2)}) %collective-permute-start.21) | collective-permute-done | bytes 278560 | tf_op jit(solution)/shard_map/ppermute | solution.py:447
  111.8 0.5 collective-permute-start.34
  112.5 2.4 %collective-permute-start.31 = (bf16[1,136,1024]{2,1,0:T(8,128)(2,1)S(1)}, bf16[1,136,1024]{2,1,0:T(8,128)(2,1)S(1)}, u32[]{:S(2)}, u32[]{:S(2)}) collective-permute-start(bf16[1,136,1024]{2,1,0:T(8,128)(2,1)S(1)} %add_convert_fusion.2), channel_id=1, source_target_pairs={{0,12},{2,14},{4,0},{6,2},{8,4},{10,6},{12,8},{14,10},{1,13},{3,15... | collective-permute-start | bytes 835592 | tf_op jit(solution)/shard_map/ppermute | solution.py:456
  114.9 3.3 %collective-permute-done.32 = bf16[1,136,1024]{2,1,0:T(8,128)(2,1)S(1)} collective-permute-done((bf16[1,136,1024]{2,1,0:T(8,128)(2,1)S(1)}, bf16[1,136,1024]{2,1,0:T(8,128)(2,1)S(1)}, u32[]{:S(2)}, u32[]{:S(2)}) %collective-permute-start.32) | collective-permute-done | bytes 278560 | tf_op jit(solution)/shard_map/ppermute | solution.py:453
  118.3 1.6 %collective-permute-start.33 = (bf16[1,136,1024]{2,1,0:T(8,128)(2,1)S(1)}, bf16[1,136,1024]{2,1,0:T(8,128)(2,1)S(1)}, u32[]{:S(2)}, u32[]{:S(2)}) collective-permute-start(bf16[1,136,1024]{2,1,0:T(8,128)(2,1)S(1)} %add_convert_fusion.1), channel_id=1, source_target_pairs={{0,1},{1,0},{2,3},{3,2},{4,5},{5,4},{6,7},{7,6},{8,9},{9,8},{10,11... | collective-permute-start | bytes 835592 | tf_op jit(solution)/shard_map/ppermute | solution.py:447
  120.0 0.6 collective-permute-done.36
  120.9 1.1 collective-permute-start.38
  122.1 6.3 %grads.3 = (bf16[1,2048,384]{2,1,0:T(8,128)(2,1)}, bf16[1,2048,384]{2,1,0:T(8,128)(2,1)}) custom-call(s32[1]{0:T(128)} %bitcast.2.tp_ref, bf16[144,5248]{1,0:T(8,128)(2,1)S(1)} %get-tuple-element.85.refs_0_, bf16[144,5248]{1,0:T(8,128)(2,1)S(1)} %collective-permute-done.28.refs_1_, bf16[288,5248]{1,0:T(8,128)(2,1)S(1)} %get-tuple-element.102.refs_9_.refs_2_, ...), custom_call_target="tpu_custom_call" | custom-call | flops 3623878656 | bytes 6488064 | tf_op jit(solution)/shard_map/grads/pallas_call | solution.py:413
  128.4 2.2 %collective-permute-done.37 = bf16[1,136,1024]{2,1,0:T(8,128)(2,1)S(1)} collective-permute-done((bf16[1,136,1024]{2,1,0:T(8,128)(2,1)S(1)}, bf16[1,136,1024]{2,1,0:T(8,128)(2,1)S(1)}, u32[]{:S(2)}, u32[]{:S(2)}) %collective-permute-start.37) | collective-permute-done | bytes 278560 | tf_op jit(solution)/shard_map/ppermute | solution.py:456
  130.7 0.9 fusion
  131.7 0.6 select_reduce_fusion
  (57 shorter events, 4.7 us)
Async XLA Ops:
  2.5 17.3 %collective-permute-start = (bf16[256,1024]{1,0:T(8,128)(2,1)}, bf16[256,1024]{1,0:T(8,128)(2,1)}, u32[]{:S(2)}, u32[]{:S(2)}) collective-permute-start(bf16[256,1024]{1,0:T(8,128)(2,1)} %join.1.refs_4_), channel_id=1, source_target_pairs={{0,4},{2,6},{4,8},{6,10},{8,12},{10,14},{12,0},{14,2},{1,5},{3,7},... | collective-permute-start | bytes 1572872 | tf_op jit(solution)/shard_map/ppermute | solution.py:456
  5.6 14.3 %collective-permute-start.1 = (bf16[256,1024]{1,0:T(8,128)(2,1)}, bf16[256,1024]{1,0:T(8,128)(2,1)}, u32[]{:S(2)}, u32[]{:S(2)}) collective-permute-start(bf16[256,1024]{1,0:T(8,128)(2,1)} %join.1.refs_4_), channel_id=1, source_target_pairs={{0,2},{2,0},{4,6},{6,4},{8,10},{10,8},{12,14},{14,12},{1,3},{3,1},... | collective-permute-start | bytes 1572872 | tf_op jit(solution)/shard_map/ppermute | solution.py:453
  7.1 13.4 %collective-permute-start.2 = (bf16[256,1024]{1,0:T(8,128)(2,1)}, bf16[256,1024]{1,0:T(8,128)(2,1)}, u32[]{:S(2)}, u32[]{:S(2)}) collective-permute-start(bf16[256,1024]{1,0:T(8,128)(2,1)} %join.1.refs_4_), channel_id=1, source_target_pairs={{0,1},{1,0},{2,3},{3,2},{4,5},{5,4},{6,7},{7,6},{8,9},{9,8},{10,11... | collective-permute-start | bytes 1572872 | tf_op jit(solution)/shard_map/ppermute | solution.py:447
  8.6 16.0 %copy-start.1 = (bf16[128,8]{0,1:T(8,128)(2,1)S(1)}, bf16[128,8]{0,1:T(8,128)(2,1)}, u32[]{:S(2)}) copy-start(bf16[128,8]{0,1:T(8,128)(2,1)} %param.10) | copy-start | bytes 6148
  8.6 16.0 %copy-start = (s32[128,8]{0,1:T(8,128)S(1)}, s32[128,8]{0,1:T(8,128)}, u32[]{:S(2)}) copy-start(s32[128,8]{0,1:T(8,128)} %param.9) | copy-start | bytes 12292
  20.5 21.1 %collective-permute-start.3 = (bf16[2048,768]{1,0:T(8,128)(2,1)S(1)}, bf16[2048,768]{1,0:T(8,128)(2,1)}, u32[]{:S(2)}, u32[]{:S(2)}) collective-permute-start(bf16[2048,768]{1,0:T(8,128)(2,1)S(1)} %get-tuple-element.75.refs_0_), channel_id=1, source_target_pairs={{0,16},{16,0},{1,17},{17,1},{2,18},{18,2},{3,19},{19,3},{4,20},{20... | collective-permute-start | bytes 9437192 | tf_op jit(solution)/shard_map/ppermute | solution.py:450
  20.5 21.1 %collective-permute-start.4 = (bf16[384,2048]{1,0:T(8,128)(2,1)}, bf16[384,2048]{1,0:T(8,128)(2,1)}, u32[]{:S(2)}, u32[]{:S(2)}) collective-permute-start(bf16[384,2048]{1,0:T(8,128)(2,1)} %get-tuple-element.76.refs_2_), channel_id=1, source_target_pairs={{0,16},{16,0},{1,17},{17,1},{2,18},{18,2},{3,19},{19,3},{4,20},{20... | collective-permute-start | bytes 4718600 | tf_op jit(solution)/shard_map/ppermute | solution.py:450
  21.0 15.9 %collective-permute-start.7 = (bf16[256,1024]{1,0:T(8,128)(2,1)}, bf16[256,1024]{1,0:T(8,128)(2,1)}, u32[]{:S(2)}, u32[]{:S(2)}) collective-permute-start(bf16[256,1024]{1,0:T(8,128)(2,1)} %collective-permute-done.refs_4_), channel_id=1, source_target_pairs={{0,4},{2,6},{4,8},{6,10},{8,12},{10,14},{12,0},{14,2},{1,5},{3,7},... | collective-permute-start | bytes 1572872 | tf_op jit(solution)/shard_map/ppermute | solution.py:456
  22.6 15.3 %collective-permute-start.5 = (bf16[256,1024]{1,0:T(8,128)(2,1)}, bf16[256,1024]{1,0:T(8,128)(2,1)}, u32[]{:S(2)}, u32[]{:S(2)}) collective-permute-start(bf16[256,1024]{1,0:T(8,128)(2,1)} %collective-permute-done.1.refs_6_), channel_id=1, source_target_pairs={{0,1},{1,0},{2,3},{3,2},{4,5},{5,4},{6,7},{7,6},{8,9},{9,8},{10,11... | collective-permute-start | bytes 1572872 | tf_op jit(solution)/shard_map/ppermute | solution.py:447
  24.1 14.6 %collective-permute-start.8 = (bf16[256,1024]{1,0:T(8,128)(2,1)}, bf16[256,1024]{1,0:T(8,128)(2,1)}, u32[]{:S(2)}, u32[]{:S(2)}) collective-permute-start(bf16[256,1024]{1,0:T(8,128)(2,1)} %collective-permute-done.refs_4_), channel_id=1, source_target_pairs={{0,2},{2,0},{4,6},{6,4},{8,10},{10,8},{12,14},{14,12},{1,3},{3,1},... | collective-permute-start | bytes 1572872 | tf_op jit(solution)/shard_map/ppermute | solution.py:453
  37.0 3.6 %collective-permute-start.6 = (bf16[16,128]{1,0:T(8,128)(2,1)S(1)}, bf16[16,128]{1,0:T(8,128)(2,1)S(1)}, u32[]{:S(2)}, u32[]{:S(2)}) collective-permute-start(bf16[16,128]{1,0:T(8,128)(2,1)S(1)} %get-tuple-element.142), channel_id=1, source_target_pairs={{0,2},{2,0},{4,6},{6,4},{8,10},{10,8},{12,14},{14,12},{1,3},{3,1},... | collective-permute-start | bytes 12296 | tf_op jit(solution)/shard_map/ppermute | solution.py:453
  37.9 13.2 %collective-permute-start.11 = (bf16[256,1024]{1,0:T(8,128)(2,1)}, bf16[256,1024]{1,0:T(8,128)(2,1)}, u32[]{:S(2)}, u32[]{:S(2)}) collective-permute-start(bf16[256,1024]{1,0:T(8,128)(2,1)} %join.1.refs_4_), channel_id=1, source_target_pairs={{0,12},{2,14},{4,0},{6,2},{8,4},{10,6},{12,8},{14,10},{1,13},{3,15... | collective-permute-start | bytes 1572872 | tf_op jit(solution)/shard_map/ppermute | solution.py:456
  38.7 13.4 %collective-permute-start.9 = (bf16[256,1024]{1,0:T(8,128)(2,1)}, bf16[256,1024]{1,0:T(8,128)(2,1)S(1)}, u32[]{:S(2)}, u32[]{:S(2)}) collective-permute-start(bf16[256,1024]{1,0:T(8,128)(2,1)} %collective-permute-done.7.refs_8_), channel_id=1, source_target_pairs={{0,1},{1,0},{2,3},{3,2},{4,5},{5,4},{6,7},{7,6},{8,9},{9,8},{10,11... | collective-permute-start | bytes 1572872 | tf_op jit(solution)/shard_map/ppermute | solution.py:447
  40.6 12.1 %collective-permute-start.13 = (bf16[256,1024]{1,0:T(8,128)(2,1)}, bf16[256,1024]{1,0:T(8,128)(2,1)S(1)}, u32[]{:S(2)}, u32[]{:S(2)}) collective-permute-start(bf16[256,1024]{1,0:T(8,128)(2,1)} %collective-permute-done.7.refs_8_), channel_id=1, source_target_pairs={{0,2},{2,0},{4,6},{6,4},{8,10},{10,8},{12,14},{14,12},{1,3},{3,1},... | collective-permute-start | bytes 1572872 | tf_op jit(solution)/shard_map/ppermute | solution.py:453
  51.1 14.4 %collective-permute-start.12 = (bf16[256,1024]{1,0:T(8,128)(2,1)}, bf16[256,1024]{1,0:T(8,128)(2,1)S(1)}, u32[]{:S(2)}, u32[]{:S(2)}) collective-permute-start(bf16[256,1024]{1,0:T(8,128)(2,1)} %collective-permute-done.5.refs_7_), channel_id=1, source_target_pairs={{0,4},{2,6},{4,8},{6,10},{8,12},{10,14},{12,0},{14,2},{1,5},{3,7},... | collective-permute-start | bytes 1572872 | tf_op jit(solution)/shard_map/ppermute | solution.py:456
  52.6 13.1 %collective-permute-start.14 = (bf16[256,1024]{1,0:T(8,128)(2,1)S(1)}, bf16[256,1024]{1,0:T(8,128)(2,1)S(1)}, u32[]{:S(2)}, u32[]{:S(2)}) collective-permute-start(bf16[256,1024]{1,0:T(8,128)(2,1)S(1)} %collective-permute-done.9.refs_9_), channel_id=1, source_target_pairs={{0,2},{2,0},{4,6},{6,4},{8,10},{10,8},{12,14},{14,12},{1,3},{3,1},... | collective-permute-start | bytes 1572872 | tf_op jit(solution)/shard_map/ppermute | solution.py:453
  53.6 12.7 %collective-permute-start.10 = (bf16[256,1024]{1,0:T(8,128)(2,1)}, bf16[256,1024]{1,0:T(8,128)(2,1)S(1)}, u32[]{:S(2)}, u32[]{:S(2)}) collective-permute-start(bf16[256,1024]{1,0:T(8,128)(2,1)} %collective-permute-done.refs_4_), channel_id=1, source_target_pairs={{0,1},{1,0},{2,3},{3,2},{4,5},{5,4},{6,7},{7,6},{8,9},{9,8},{10,11... | collective-permute-start | bytes 1572872 | tf_op jit(solution)/shard_map/ppermute | solution.py:447
  55.2 12.2 %collective-permute-start.15 = (bf16[2,16,128]{2,1,0:T(8,128)(2,1)S(1)}, bf16[2,16,128]{2,1,0:T(8,128)(2,1)S(1)}, u32[]{:S(2)}, u32[]{:S(2)}) collective-permute-start(bf16[2,16,128]{2,1,0:T(8,128)(2,1)S(1)} %pad_maximum_fusion.refs_8_), channel_id=1, source_target_pairs={{0,4},{2,6},{4,8},{6,10},{8,12},{10,14},{12,0},{14,2},{1,5},{3,7},... | collective-permute-start | bytes 24584 | tf_op jit(solution)/shard_map/ppermute | solution.py:456
  55.4 13.4 %collective-permute-start.16 = (bf16[2,16,128]{2,1,0:T(8,128)(2,1)S(1)}, bf16[2,16,128]{2,1,0:T(8,128)(2,1)S(1)}, u32[]{:S(2)}, u32[]{:S(2)}) collective-permute-start(bf16[2,16,128]{2,1,0:T(8,128)(2,1)S(1)} %pad_maximum_fusion.refs_8_), channel_id=1, source_target_pairs={{0,8},{2,10},{4,12},{6,14},{8,0},{10,2},{12,4},{14,6},{1,9},{3,11}... | collective-permute-start | bytes 24584 | tf_op jit(solution)/shard_map/ppermute | solution.py:456
  65.5 3.8 %collective-permute-start.17 = (bf16[2,16,128]{2,1,0:T(8,128)(2,1)S(1)}, bf16[2,16,128]{2,1,0:T(8,128)(2,1)S(1)}, u32[]{:S(2)}, u32[]{:S(2)}) collective-permute-start(bf16[2,16,128]{2,1,0:T(8,128)(2,1)S(1)} %pad_maximum_fusion.refs_8_), channel_id=1, source_target_pairs={{0,12},{2,14},{4,0},{6,2},{8,4},{10,6},{12,8},{14,10},{1,13},{3,15... | collective-permute-start | bytes 24584 | tf_op jit(solution)/shard_map/ppermute | solution.py:456
  65.7 16.5 %collective-permute-start.18 = (bf16[256,1024]{1,0:T(8,128)(2,1)}, bf16[256,1024]{1,0:T(8,128)(2,1)S(1)}, u32[]{:S(2)}, u32[]{:S(2)}) collective-permute-start(bf16[256,1024]{1,0:T(8,128)(2,1)} %collective-permute-done.5.refs_7_), channel_id=1, source_target_pairs={{0,12},{2,14},{4,0},{6,2},{8,4},{10,6},{12,8},{14,10},{1,13},{3,15... | collective-permute-start | bytes 1572872 | tf_op jit(solution)/shard_map/ppermute | solution.py:456
  66.4 15.8 %collective-permute-start.19 = (bf16[256,1024]{1,0:T(8,128)(2,1)}, bf16[256,1024]{1,0:T(8,128)(2,1)S(1)}, u32[]{:S(2)}, u32[]{:S(2)}) collective-permute-start(bf16[256,1024]{1,0:T(8,128)(2,1)} %collective-permute-done.11.refs_4_), channel_id=1, source_target_pairs={{0,2},{2,0},{4,6},{6,4},{8,10},{10,8},{12,14},{14,12},{1,3},{3,1},... | collective-permute-start | bytes 1572872 | tf_op jit(solution)/shard_map/ppermute | solution.py:453
  67.3 14.9 %collective-permute-start.20 = (bf16[256,1024]{1,0:T(8,128)(2,1)}, bf16[256,1024]{1,0:T(8,128)(2,1)S(1)}, u32[]{:S(2)}, u32[]{:S(2)}) collective-permute-start(bf16[256,1024]{1,0:T(8,128)(2,1)} %collective-permute-done.11.refs_4_), channel_id=1, source_target_pairs={{0,1},{1,0},{2,3},{3,2},{4,5},{5,4},{6,7},{7,6},{8,9},{9,8},{10,11... | collective-permute-start | bytes 1572872 | tf_op jit(solution)/shard_map/ppermute | solution.py:447
  82.2 18.4 %collective-permute-start.29 = (bf16[288,5248]{1,0:T(8,128)(2,1)S(1)}, bf16[288,5248]{1,0:T(8,128)(2,1)S(1)}, u32[]{:S(2)}, u32[]{:S(2)}) collective-permute-start(bf16[288,5248]{1,0:T(8,128)(2,1)S(1)} %get-tuple-element.118), channel_id=1, source_target_pairs={{0,16},{16,0},{1,17},{17,1},{2,18},{18,2},{3,19},{19,3},{4,20},{20... | collective-permute-start | bytes 9068552 | tf_op jit(solution)/shard_map/ppermute | solution.py:450
  82.3 15.2 %collective-permute-start.28 = (bf16[144,5248]{1,0:T(8,128)(2,1)S(1)}, bf16[144,5248]{1,0:T(8,128)(2,1)S(1)}, u32[]{:S(2)}, u32[]{:S(2)}) collective-permute-start(bf16[144,5248]{1,0:T(8,128)(2,1)S(1)} %get-tuple-element.117), channel_id=1, source_target_pairs={{0,16},{16,0},{1,17},{17,1},{2,18},{18,2},{3,19},{19,3},{4,20},{20... | collective-permute-start | bytes 4534280 | tf_op jit(solution)/shard_map/ppermute | solution.py:450
  82.8 13.9 %collective-permute-start.23 = (bf16[1,136,1024]{2,1,0:T(8,128)(2,1)S(1)}, bf16[1,136,1024]{2,1,0:T(8,128)(2,1)S(1)}, u32[]{:S(2)}, u32[]{:S(2)}) collective-permute-start(bf16[1,136,1024]{2,1,0:T(8,128)(2,1)S(1)} %get-tuple-element.110), channel_id=1, source_target_pairs={{0,2},{2,0},{4,6},{6,4},{8,10},{10,8},{12,14},{14,12},{1,3},{3,1},... | collective-permute-start | bytes 835592 | tf_op jit(solution)/shard_map/ppermute | solution.py:453
  83.6 13.1 %collective-permute-start.22 = (bf16[1,136,1024]{2,1,0:T(8,128)(2,1)S(1)}, bf16[1,136,1024]{2,1,0:T(8,128)(2,1)S(1)}, u32[]{:S(2)}, u32[]{:S(2)}) collective-permute-start(bf16[1,136,1024]{2,1,0:T(8,128)(2,1)S(1)} %get-tuple-element.109), channel_id=1, source_target_pairs={{0,1},{1,0},{2,3},{3,2},{4,5},{5,4},{6,7},{7,6},{8,9},{9,8},{10,11... | collective-permute-start | bytes 835592 | tf_op jit(solution)/shard_map/ppermute | solution.py:447
  85.3 11.4 %collective-permute-start.24 = (bf16[1,136,1024]{2,1,0:T(8,128)(2,1)S(1)}, bf16[1,136,1024]{2,1,0:T(8,128)(2,1)S(1)}, u32[]{:S(2)}, u32[]{:S(2)}) collective-permute-start(bf16[1,136,1024]{2,1,0:T(8,128)(2,1)S(1)} %get-tuple-element.111), channel_id=1, source_target_pairs={{0,12},{2,14},{4,0},{6,2},{8,4},{10,6},{12,8},{14,10},{1,13},{3,15... | collective-permute-start | bytes 835592 | tf_op jit(solution)/shard_map/ppermute | solution.py:456
  96.7 3.4 %collective-permute-start.30 = (bf16[144,5248]{1,0:T(8,128)(2,1)S(1)}, bf16[144,5248]{1,0:T(8,128)(2,1)S(1)}, u32[]{:S(2)}, u32[]{:S(2)}) collective-permute-start(bf16[144,5248]{1,0:T(8,128)(2,1)S(1)} %get-tuple-element.120), channel_id=1, source_target_pairs={{0,16},{16,0},{1,17},{17,1},{2,18},{18,2},{3,19},{19,3},{4,20},{20... | collective-permute-start | bytes 4534280 | tf_op jit(solution)/shard_map/ppermute | solution.py:450
  96.8 9.5 %collective-permute-start.26 = (bf16[1,136,1024]{2,1,0:T(8,128)(2,1)S(1)}, bf16[1,136,1024]{2,1,0:T(8,128)(2,1)S(1)}, u32[]{:S(2)}, u32[]{:S(2)}) collective-permute-start(bf16[1,136,1024]{2,1,0:T(8,128)(2,1)S(1)} %get-tuple-element.115), channel_id=1, source_target_pairs={{0,1},{1,0},{2,3},{3,2},{4,5},{5,4},{6,7},{7,6},{8,9},{9,8},{10,11... | collective-permute-start | bytes 835592 | tf_op jit(solution)/shard_map/ppermute | solution.py:447
  97.4 10.5 %collective-permute-start.25 = (bf16[1,136,1024]{2,1,0:T(8,128)(2,1)S(1)}, bf16[1,136,1024]{2,1,0:T(8,128)(2,1)S(1)}, u32[]{:S(2)}, u32[]{:S(2)}) collective-permute-start(bf16[1,136,1024]{2,1,0:T(8,128)(2,1)S(1)} %get-tuple-element.114), channel_id=1, source_target_pairs={{0,4},{2,6},{4,8},{6,10},{8,12},{10,14},{12,0},{14,2},{1,5},{3,7},... | collective-permute-start | bytes 835592 | tf_op jit(solution)/shard_map/ppermute | solution.py:456
  97.5 10.4 %collective-permute-start.27 = (bf16[1,136,1024]{2,1,0:T(8,128)(2,1)S(1)}, bf16[1,136,1024]{2,1,0:T(8,128)(2,1)S(1)}, u32[]{:S(2)}, u32[]{:S(2)}) collective-permute-start(bf16[1,136,1024]{2,1,0:T(8,128)(2,1)S(1)} %add_convert_fusion.5), channel_id=1, source_target_pairs={{0,2},{2,0},{4,6},{6,4},{8,10},{10,8},{12,14},{14,12},{1,3},{3,1},... | collective-permute-start | bytes 835592 | tf_op jit(solution)/shard_map/ppermute | solution.py:453
  100.1 11.7 %collective-permute-start.21 = (bf16[1,136,1024]{2,1,0:T(8,128)(2,1)S(1)}, bf16[1,136,1024]{2,1,0:T(8,128)(2,1)S(1)}, u32[]{:S(2)}, u32[]{:S(2)}) collective-permute-start(bf16[1,136,1024]{2,1,0:T(8,128)(2,1)S(1)} %get-tuple-element.101), channel_id=1, source_target_pairs={{0,1},{1,0},{2,3},{3,2},{4,5},{5,4},{6,7},{7,6},{8,9},{9,8},{10,11... | collective-permute-start | bytes 835592 | tf_op jit(solution)/shard_map/ppermute | solution.py:447
  100.6 19.2 %collective-permute-start.35 = (bf16[1,136,1024]{2,1,0:T(8,128)(2,1)S(1)}, bf16[1,136,1024]{2,1,0:T(8,128)(2,1)S(1)}, u32[]{:S(2)}, u32[]{:S(2)}) collective-permute-start(bf16[1,136,1024]{2,1,0:T(8,128)(2,1)S(1)} %get-tuple-element.129), channel_id=1, source_target_pairs={{0,2},{2,0},{4,6},{6,4},{8,10},{10,8},{12,14},{14,12},{1,3},{3,1},... | collective-permute-start | bytes 835592 | tf_op jit(solution)/shard_map/ppermute | solution.py:453
  108.0 10.2 %collective-permute-start.32 = (bf16[1,136,1024]{2,1,0:T(8,128)(2,1)S(1)}, bf16[1,136,1024]{2,1,0:T(8,128)(2,1)S(1)}, u32[]{:S(2)}, u32[]{:S(2)}) collective-permute-start(bf16[1,136,1024]{2,1,0:T(8,128)(2,1)S(1)} %add_convert_fusion.4), channel_id=1, source_target_pairs={{0,2},{2,0},{4,6},{6,4},{8,10},{10,8},{12,14},{14,12},{1,3},{3,1},... | collective-permute-start | bytes 835592 | tf_op jit(solution)/shard_map/ppermute | solution.py:453
  109.2 11.5 %collective-permute-start.36 = (bf16[1,136,1024]{2,1,0:T(8,128)(2,1)S(1)}, bf16[1,136,1024]{2,1,0:T(8,128)(2,1)S(1)}, u32[]{:S(2)}, u32[]{:S(2)}) collective-permute-start(bf16[1,136,1024]{2,1,0:T(8,128)(2,1)S(1)} %add_convert_fusion.3), channel_id=1, source_target_pairs={{0,4},{2,6},{4,8},{6,10},{8,12},{10,14},{12,0},{14,2},{1,5},{3,7},... | collective-permute-start | bytes 835592 | tf_op jit(solution)/shard_map/ppermute | solution.py:456
  111.8 8.2 %collective-permute-start.34 = (bf16[1,136,1024]{2,1,0:T(8,128)(2,1)S(1)}, bf16[1,136,1024]{2,1,0:T(8,128)(2,1)S(1)}, u32[]{:S(2)}, u32[]{:S(2)}) collective-permute-start(bf16[1,136,1024]{2,1,0:T(8,128)(2,1)S(1)} %get-tuple-element.128), channel_id=1, source_target_pairs={{0,1},{1,0},{2,3},{3,2},{4,5},{5,4},{6,7},{7,6},{8,9},{9,8},{10,11... | collective-permute-start | bytes 835592 | tf_op jit(solution)/shard_map/ppermute | solution.py:447
  112.5 15.9 %collective-permute-start.31 = (bf16[1,136,1024]{2,1,0:T(8,128)(2,1)S(1)}, bf16[1,136,1024]{2,1,0:T(8,128)(2,1)S(1)}, u32[]{:S(2)}, u32[]{:S(2)}) collective-permute-start(bf16[1,136,1024]{2,1,0:T(8,128)(2,1)S(1)} %add_convert_fusion.2), channel_id=1, source_target_pairs={{0,12},{2,14},{4,0},{6,2},{8,4},{10,6},{12,8},{14,10},{1,13},{3,15... | collective-permute-start | bytes 835592 | tf_op jit(solution)/shard_map/ppermute | solution.py:456
  118.3 10.2 %collective-permute-start.33 = (bf16[1,136,1024]{2,1,0:T(8,128)(2,1)S(1)}, bf16[1,136,1024]{2,1,0:T(8,128)(2,1)S(1)}, u32[]{:S(2)}, u32[]{:S(2)}) collective-permute-start(bf16[1,136,1024]{2,1,0:T(8,128)(2,1)S(1)} %add_convert_fusion.1), channel_id=1, source_target_pairs={{0,1},{1,0},{2,3},{3,2},{4,5},{5,4},{6,7},{7,6},{8,9},{9,8},{10,11... | collective-permute-start | bytes 835592 | tf_op jit(solution)/shard_map/ppermute | solution.py:447
  120.9 9.8 %collective-permute-start.37 = (bf16[1,136,1024]{2,1,0:T(8,128)(2,1)S(1)}, bf16[1,136,1024]{2,1,0:T(8,128)(2,1)S(1)}, u32[]{:S(2)}, u32[]{:S(2)}) collective-permute-start(bf16[1,136,1024]{2,1,0:T(8,128)(2,1)S(1)} %add_convert_fusion), channel_id=1, source_target_pairs={{0,4},{2,6},{4,8},{6,10},{8,12},{10,14},{12,0},{14,2},{1,5},{3,7},... | collective-permute-start | bytes 835592 | tf_op jit(solution)/shard_map/ppermute | solution.py:456
  120.9 9.7 %collective-permute-start.38 = (bf16[1,136,1024]{2,1,0:T(8,128)(2,1)S(1)}, bf16[1,136,1024]{2,1,0:T(8,128)(2,1)S(1)}, u32[]{:S(2)}, u32[]{:S(2)}) collective-permute-start(bf16[1,136,1024]{2,1,0:T(8,128)(2,1)S(1)} %get-tuple-element.134), channel_id=1, source_target_pairs={{0,2},{2,0},{4,6},{6,4},{8,10},{10,8},{12,14},{14,12},{1,3},{3,1},... | collective-permute-start | bytes 835592 | tf_op jit(solution)/shard_map/ppermute | solution.py:453

commit v19 on v17

--- a/solution.py
+++ b/solution.py
@@ -291,24 +291,17 @@
             for side in range(2):
                 number, slot = ways[chunk, y, side]
                 packets[number][slot, tok:] = extra.astype(jnp.bfloat16)
-    early = count == 1
-    grads = [outs[expert][:, both_at] for expert in range(2)]
-    if early:
-        grads = [dot(low_picks[0, expert], grads[expert], ((0,), (0,))).astype(jnp.bfloat16) for expert in range(2)]
+    placed = []
+    for expert in range(2):
+        parts = [dot(low_picks[chunk, expert], outs[expert][spans[chunk], both_at], ((0,), (0,))) for chunk in range(count)]
+        placed.append(jnp.concatenate(parts, 0).astype(jnp.bfloat16))
     for side in (1, 0):
-        low = [dot(grads[expert], wgu[expert][sides[side], :], ((1,), (1,))) for expert in range(2)]
+        total = dot(placed[0], wgu[0][sides[side], :], ((1,), (1,))) + dot(placed[1], wgu[1][sides[side], :], ((1,), (1,)))
         for chunk in range(count):
-            if early:
-                total = low[0] + low[1]
-            else:
-                rows = slice(chunk * slots, (chunk + 1) * slots)
-                total = sum(
-                    dot(low_picks[chunk, expert], low[expert][rows].astype(jnp.bfloat16), ((0,), (0,)))
-                    for expert in range(2)
-                )
             for y in range(2):
                 number, slot = ways[chunk, y, side]
-                packets[number][slot, :tok] = total[y * tok : (y + 1) * tok].astype(jnp.bfloat16)
+                start = (2 * chunk + y) * tok
+                packets[number][slot, :tok] = total[start : start + tok].astype(jnp.bfloat16)
 
 
 def rows_call(items, owners, capacity, slots, where, weights, units, tables, after):

time: 132 us -> 133 us (level)
  no operation moved by 1% of the time
where the time goes in v19:
time: 133 us
  Pallas kernels  48.3 us (36%)
  waiting for transfers between devices  43.4 us (33%)
  starting transfers between devices  37.9 us (28%)
  other arithmetic  2.4 us (2%)
    pallas_call x3, Pallas kernels, rows_call(): pl.pallas_call(functools.partial(rows_kernel, count, ways, capacity, slot...  32.3 us
    ppermute x13, waiting for transfers between devices, over_z(): lax.ppermute(array, 'ep', [(i, (i + shift * n_y) % ep) for i in range(ep)])  29.8 us
    ppermute x13, starting transfers between devices, over_z(): lax.ppermute(array, 'ep', [(i, (i + shift * n_y) % ep) for i in range(ep)])  13.4 us
    ppermute x10, starting transfers between devices, over_x(): return lax.ppermute(array, 'tp', [(0, 1), (1, 0)])  12.4 us
    ppermute x11, starting transfers between devices, over_y(): lax.ppermute(array, 'ep', [(i, i + 1 - 2 * (i % n_y)) for i in range(ep)])  10.9 us
    pallas_call x2, Pallas kernels, grads_call(): pl.pallas_call(functools.partial(grads_kernel, count, *starts, 2 * per),...  10.7 us
    ppermute x11, waiting for transfers between devices, over_y(): lax.ppermute(array, 'ep', [(i, i + 1 - 2 * (i % n_y)) for i in range(ep)])  8.33 us
    ppermute x10, waiting for transfers between devices, over_x(): return lax.ppermute(array, 'tp', [(0, 1), (1, 0)])  3.71 us
  transfers between devices with their start and end apart: 39, of which 12 were waited for; matrix products, arithmetic and copies ran while one was open for 1% of the time, Pallas kernels for 35%

profile of v19, /device:TPU:0, one launch (start us, length us, event | category | flops | bytes accessed | tf_op | source)
XLA Modules:
  0.0 132.9 jit_solution(6654955728186097034)
XLA Ops:
  0.6 1.8 %join.1.refs_4_ = bf16[256,1024]{1,0:T(8,128)(2,1)} custom-call(bf16[128,1024]{1,0:T(8,128)(2,1)} %top_ref.1, bf16[128,1024]{1,0:T(8,128)(2,1)} %bottom_ref.1), custom_call_target="tpu_custom_call" | custom-call | bytes 1048576 | tf_op jit(solution)/shard_map/join/pallas_call | solution.py:180
  2.5 3.1 %collective-permute-start = (bf16[256,1024]{1,0:T(8,128)(2,1)}, bf16[256,1024]{1,0:T(8,128)(2,1)}, u32[]{:S(2)}, u32[]{:S(2)}) collective-permute-start(bf16[256,1024]{1,0:T(8,128)(2,1)} %join.1.refs_4_), channel_id=1, source_target_pairs={{0,4},{2,6},{4,8},{6,10},{8,12},{10,14},{12,0},{14,2},{1,5},{3,7},... | collective-permute-start | bytes 1572872 | tf_op jit(solution)/shard_map/ppermute | solution.py:449
  5.6 1.5 %collective-permute-start.1 = (bf16[256,1024]{1,0:T(8,128)(2,1)}, bf16[256,1024]{1,0:T(8,128)(2,1)}, u32[]{:S(2)}, u32[]{:S(2)}) collective-permute-start(bf16[256,1024]{1,0:T(8,128)(2,1)} %join.1.refs_4_), channel_id=1, source_target_pairs={{0,2},{2,0},{4,6},{6,4},{8,10},{10,8},{12,14},{14,12},{1,3},{3,1},... | collective-permute-start | bytes 1572872 | tf_op jit(solution)/shard_map/ppermute | solution.py:446
  7.1 1.5 %collective-permute-start.2 = (bf16[256,1024]{1,0:T(8,128)(2,1)}, bf16[256,1024]{1,0:T(8,128)(2,1)}, u32[]{:S(2)}, u32[]{:S(2)}) collective-permute-start(bf16[256,1024]{1,0:T(8,128)(2,1)} %join.1.refs_4_), channel_id=1, source_target_pairs={{0,1},{1,0},{2,3},{3,2},{4,5},{5,4},{6,7},{7,6},{8,9},{9,8},{10,11... | collective-permute-start | bytes 1572872 | tf_op jit(solution)/shard_map/ppermute | solution.py:440
  8.6 3.4 %weights.1 = (bf16[2048,768]{1,0:T(8,128)(2,1)S(1)}, bf16[384,2048]{1,0:T(8,128)(2,1)}) custom-call(s32[1]{0:T(128)} %bitcast.2.tp_ref, bf16[1,2048,384]{2,1,0:T(8,128)(2,1)} %wg_ref.1, bf16[1,2048,384]{2,1,0:T(8,128)(2,1)} %wu_ref.1, bf16[1,384,2048]{2,1,0:T(8,128)(2,1)} %wd_ref.1), custom_call_target="tpu_custom_call" | custom-call | bytes 9437184 | tf_op jit(solution)/shard_map/weights/pallas_call | solution.py:141
  12.0 7.8 %collective-permute-done.refs_4_ = bf16[256,1024]{1,0:T(8,128)(2,1)} collective-permute-done((bf16[256,1024]{1,0:T(8,128)(2,1)}, bf16[256,1024]{1,0:T(8,128)(2,1)}, u32[]{:S(2)}, u32[]{:S(2)}) %collective-permute-start) | collective-permute-done | bytes 524320 | tf_op jit(solution)/shard_map/ppermute | solution.py:449
  19.8 0.7 collective-permute-done.2.refs_5_
  20.5 0.5 collective-permute-start.4
  21.0 1.6 %collective-permute-start.7 = (bf16[256,1024]{1,0:T(8,128)(2,1)}, bf16[256,1024]{1,0:T(8,128)(2,1)}, u32[]{:S(2)}, u32[]{:S(2)}) collective-permute-start(bf16[256,1024]{1,0:T(8,128)(2,1)} %collective-permute-done.refs_4_), channel_id=1, source_target_pairs={{0,4},{2,6},{4,8},{6,10},{8,12},{10,14},{12,0},{14,2},{1,5},{3,7},... | collective-permute-start | bytes 1572872 | tf_op jit(solution)/shard_map/ppermute | solution.py:449
  22.6 1.5 %collective-permute-start.5 = (bf16[256,1024]{1,0:T(8,128)(2,1)}, bf16[256,1024]{1,0:T(8,128)(2,1)}, u32[]{:S(2)}, u32[]{:S(2)}) collective-permute-start(bf16[256,1024]{1,0:T(8,128)(2,1)} %collective-permute-done.1.refs_6_), channel_id=1, source_target_pairs={{0,1},{1,0},{2,3},{3,2},{4,5},{5,4},{6,7},{7,6},{8,9},{9,8},{10,11... | collective-permute-start | bytes 1572872 | tf_op jit(solution)/shard_map/ppermute | solution.py:440
  24.1 0.5 collective-permute-start.8
  24.6 12.3 %collective-permute-done.7.refs_8_ = bf16[256,1024]{1,0:T(8,128)(2,1)} collective-permute-done((bf16[256,1024]{1,0:T(8,128)(2,1)}, bf16[256,1024]{1,0:T(8,128)(2,1)}, u32[]{:S(2)}, u32[]{:S(2)}) %collective-permute-start.7) | collective-permute-done | bytes 524320 | tf_op jit(solution)/shard_map/ppermute | solution.py:449
  37.0 0.9 collective-permute-start.6
  37.9 0.8 collective-permute-start.11
  38.7 1.5 %collective-permute-start.9 = (bf16[256,1024]{1,0:T(8,128)(2,1)}, bf16[256,1024]{1,0:T(8,128)(2,1)S(1)}, u32[]{:S(2)}, u32[]{:S(2)}) collective-permute-start(bf16[256,1024]{1,0:T(8,128)(2,1)} %collective-permute-done.7.refs_8_), channel_id=1, source_target_pairs={{0,1},{1,0},{2,3},{3,2},{4,5},{5,4},{6,7},{7,6},{8,9},{9,8},{10,11... | collective-permute-start | bytes 1572872 | tf_op jit(solution)/shard_map/ppermute | solution.py:440
  40.6 0.9 collective-permute-start.13
  41.6 9.5 %rows.3 = (bf16[144,5248]{1,0:T(8,128)(2,1)S(1)}, bf16[144,5248]{1,0:T(8,128)(2,1)S(1)}, bf16[1,136,1024]{2,1,0:T(8,128)(2,1)S(1)}, bf16[1,136,1024]{2,1,0:T(8,1...) custom-call(s32[3]{0:T(128)S(1)} %pad_add_fusion.where_ref, ...), custom_call_target="tpu_custom_call" | custom-call | flops 3170893824 | bytes 13631488 | tf_op jit(solution)/shard_map/rows/pallas_call | solution.py:314
  51.1 1.1 collective-permute-start.12
  52.6 1.0 collective-permute-start.14
  53.6 1.5 %collective-permute-start.10 = (bf16[256,1024]{1,0:T(8,128)(2,1)}, bf16[256,1024]{1,0:T(8,128)(2,1)S(1)}, u32[]{:S(2)}, u32[]{:S(2)}) collective-permute-start(bf16[256,1024]{1,0:T(8,128)(2,1)} %collective-permute-done.refs_4_), channel_id=1, source_target_pairs={{0,1},{1,0},{2,3},{3,2},{4,5},{5,4},{6,7},{7,6},{8,9},{9,8},{10,11... | collective-permute-start | bytes 1572872 | tf_op jit(solution)/shard_map/ppermute | solution.py:440
  55.4 2.7 %collective-permute-start.16 = (bf16[2,16,128]{2,1,0:T(8,128)(2,1)S(1)}, bf16[2,16,128]{2,1,0:T(8,128)(2,1)S(1)}, u32[]{:S(2)}, u32[]{:S(2)}) collective-permute-start(bf16[2,16,128]{2,1,0:T(8,128)(2,1)S(1)} %pad_maximum_fusion.refs_8_), channel_id=1, source_target_pairs={{0,8},{2,10},{4,12},{6,14},{8,0},{10,2},{12,4},{14,6},{1,9},{3,11}... | collective-permute-start | bytes 24584 | tf_op jit(solution)/shard_map/ppermute | solution.py:449
  58.1 7.4 %collective-permute-done.12.refs_7_ = bf16[256,1024]{1,0:T(8,128)(2,1)S(1)} collective-permute-done((bf16[256,1024]{1,0:T(8,128)(2,1)}, bf16[256,1024]{1,0:T(8,128)(2,1)S(1)}, u32[]{:S(2)}, u32[]{:S(2)}) %collective-permute-start.12) | collective-permute-done | bytes 524320 | tf_op jit(solution)/shard_map/ppermute | solution.py:449
  65.7 0.7 collective-permute-start.18
  66.4 0.9 collective-permute-start.19
  67.3 1.5 %collective-permute-start.20 = (bf16[256,1024]{1,0:T(8,128)(2,1)}, bf16[256,1024]{1,0:T(8,128)(2,1)S(1)}, u32[]{:S(2)}, u32[]{:S(2)}) collective-permute-start(bf16[256,1024]{1,0:T(8,128)(2,1)} %collective-permute-done.11.refs_4_), channel_id=1, source_target_pairs={{0,1},{1,0},{2,3},{3,2},{4,5},{5,4},{6,7},{7,6},{8,9},{9,8},{10,11... | collective-permute-start | bytes 1572872 | tf_op jit(solution)/shard_map/ppermute | solution.py:440
  69.3 13.5 %rows.4 = (bf16[288,5248]{1,0:T(8,128)(2,1)S(1)}, bf16[288,5248]{1,0:T(8,128)(2,1)S(1)}, bf16[1,136,1024]{2,1,0:T(8,128)(2,1)S(1)}, bf16[1,136,1024]{2,1,0:T(8,1...) custom-call(s32[3]{0:T(128)S(1)} %pad_add_fusion.where_ref, ...), custom_call_target="tpu_custom_call" | custom-call | flops 6341787648 | bytes 17825792 | tf_op jit(solution)/shard_map/rows/pallas_call | solution.py:314
  83.0 0.5 collective-permute-start.28
  83.5 0.8 collective-permute-start.24
  84.3 1.7 %collective-permute-start.23 = (bf16[1,136,1024]{2,1,0:T(8,128)(2,1)S(1)}, bf16[1,136,1024]{2,1,0:T(8,128)(2,1)S(1)}, u32[]{:S(2)}, u32[]{:S(2)}) collective-permute-start(bf16[1,136,1024]{2,1,0:T(8,128)(2,1)S(1)} %get-tuple-element.110), channel_id=1, source_target_pairs={{0,1},{1,0},{2,3},{3,2},{4,5},{5,4},{6,7},{7,6},{8,9},{9,8},{10,11... | collective-permute-start | bytes 835592 | tf_op jit(solution)/shard_map/ppermute | solution.py:440
  86.0 2.1 %collective-permute-start.22 = (bf16[1,136,1024]{2,1,0:T(8,128)(2,1)S(1)}, bf16[1,136,1024]{2,1,0:T(8,128)(2,1)S(1)}, u32[]{:S(2)}, u32[]{:S(2)}) collective-permute-start(bf16[1,136,1024]{2,1,0:T(8,128)(2,1)S(1)} %get-tuple-element.102), channel_id=1, source_target_pairs={{0,12},{2,14},{4,0},{6,2},{8,4},{10,6},{12,8},{14,10},{1,13},{3,15... | collective-permute-start | bytes 835592 | tf_op jit(solution)/shard_map/ppermute | solution.py:449
  88.0 9.3 %rows.5 = (bf16[144,5248]{1,0:T(8,128)(2,1)S(1)}, bf16[144,5248]{1,0:T(8,128)(2,1)S(1)}, bf16[1,136,1024]{2,1,0:T(8,128)(2,1)S(1)}, bf16[1,136,1024]{2,1,0:T(8,1...) custom-call(s32[3]{0:T(128)S(1)} %pad_add_fusion.where_ref, ...), custom_call_target="tpu_custom_call" | custom-call | flops 3170893824 | bytes 13631488 | tf_op jit(solution)/shard_map/rows/pallas_call | solution.py:314
  97.5 0.6 collective-permute-start.26
  98.1 1.1 collective-permute-start.27
  99.3 1.5 %collective-permute-done.30.refs_5_ = bf16[144,5248]{1,0:T(8,128)(2,1)S(1)} collective-permute-done((bf16[144,5248]{1,0:T(8,128)(2,1)S(1)}, bf16[144,5248]{1,0:T(8,128)(2,1)S(1)}, u32[]{:S(2)}, u32[]{:S(2)}) %collective-permute-start.30) | collective-permute-done | bytes 1511456 | tf_op jit(solution)/shard_map/ppermute | solution.py:443
  100.8 0.5 collective-permute-start.21
  101.3 1.5 %collective-permute-start.34 = (bf16[1,136,1024]{2,1,0:T(8,128)(2,1)S(1)}, bf16[1,136,1024]{2,1,0:T(8,128)(2,1)S(1)}, u32[]{:S(2)}, u32[]{:S(2)}) collective-permute-start(bf16[1,136,1024]{2,1,0:T(8,128)(2,1)S(1)} %get-tuple-element.126), channel_id=1, source_target_pairs={{0,1},{1,0},{2,3},{3,2},{4,5},{5,4},{6,7},{7,6},{8,9},{9,8},{10,11... | collective-permute-start | bytes 835592 | tf_op jit(solution)/shard_map/ppermute | solution.py:440
  102.8 4.4 %grads.2 = bf16[1,384,2048]{2,1,0:T(8,128)(2,1)} custom-call(s32[1]{0:T(128)} %bitcast.2.tp_ref, bf16[144,5248]{1,0:T(8,128)(2,1)S(1)} %get-tuple-element.84.refs_0_, bf16[144,5248]{1,0:T(8,128)(2,1)S(1)} %collective-permute-done.28.refs_1_, bf16[288,5248]{1,0:T(8,128)(2,1)S(1)} %get-tuple-element.103.refs_9_.refs_2_, ...), custom_call_target="tpu_custom_call" | custom-call | flops 1811939328 | bytes 5603328 | tf_op jit(solution)/shard_map/grads/pallas_call | solution.py:406
  107.2 1.1 collective-permute-start.35
  108.7 1.0 collective-permute-start.32
  109.9 3.0 %collective-permute-done.21 = bf16[1,136,1024]{2,1,0:T(8,128)(2,1)S(1)} collective-permute-done((bf16[1,136,1024]{2,1,0:T(8,128)(2,1)S(1)}, bf16[1,136,1024]{2,1,0:T(8,128)(2,1)S(1)}, u32[]{:S(2)}, u32[]{:S(2)}) %collective-permute-start.21) | collective-permute-done | bytes 278560 | tf_op jit(solution)/shard_map/ppermute | solution.py:440
  113.1 0.9 collective-permute-start.31
  113.9 7.5 %collective-permute-done.32 = bf16[1,136,1024]{2,1,0:T(8,128)(2,1)S(1)} collective-permute-done((bf16[1,136,1024]{2,1,0:T(8,128)(2,1)S(1)}, bf16[1,136,1024]{2,1,0:T(8,128)(2,1)S(1)}, u32[]{:S(2)}, u32[]{:S(2)}) %collective-permute-start.32) | collective-permute-done | bytes 278560 | tf_op jit(solution)/shard_map/ppermute | solution.py:446
  121.5 0.6 collective-permute-start.33
  122.3 1.1 collective-permute-start.38
  123.4 6.3 %grads.3 = (bf16[1,2048,384]{2,1,0:T(8,128)(2,1)}, bf16[1,2048,384]{2,1,0:T(8,128)(2,1)}) custom-call(s32[1]{0:T(128)} %bitcast.2.tp_ref, bf16[144,5248]{1,0:T(8,128)(2,1)S(1)} %get-tuple-element.84.refs_0_, bf16[144,5248]{1,0:T(8,128)(2,1)S(1)} %collective-permute-done.28.refs_1_, bf16[288,5248]{1,0:T(8,128)(2,1)S(1)} %get-tuple-element.103.refs_9_.refs_2_, ...), custom_call_target="tpu_custom_call" | custom-call | flops 3623878656 | bytes 6488064 | tf_op jit(solution)/shard_map/grads/pallas_call | solution.py:406
  129.8 1.6 %collective-permute-done.37 = bf16[1,136,1024]{2,1,0:T(8,128)(2,1)S(1)} collective-permute-done((bf16[1,136,1024]{2,1,0:T(8,128)(2,1)S(1)}, bf16[1,136,1024]{2,1,0:T(8,128)(2,1)S(1)}, u32[]{:S(2)}, u32[]{:S(2)}) %collective-permute-start.37) | collective-permute-done | bytes 278560 | tf_op jit(solution)/shard_map/ppermute | solution.py:449
  131.3 0.9 fusion
  132.3 0.6 select_reduce_fusion
  (57 shorter events, 3.2 us)
Async XLA Ops:
  2.5 17.3 %collective-permute-start = (bf16[256,1024]{1,0:T(8,128)(2,1)}, bf16[256,1024]{1,0:T(8,128)(2,1)}, u32[]{:S(2)}, u32[]{:S(2)}) collective-permute-start(bf16[256,1024]{1,0:T(8,128)(2,1)} %join.1.refs_4_), channel_id=1, source_target_pairs={{0,4},{2,6},{4,8},{6,10},{8,12},{10,14},{12,0},{14,2},{1,5},{3,7},... | collective-permute-start | bytes 1572872 | tf_op jit(solution)/shard_map/ppermute | solution.py:449
  5.6 14.3 %collective-permute-start.1 = (bf16[256,1024]{1,0:T(8,128)(2,1)}, bf16[256,1024]{1,0:T(8,128)(2,1)}, u32[]{:S(2)}, u32[]{:S(2)}) collective-permute-start(bf16[256,1024]{1,0:T(8,128)(2,1)} %join.1.refs_4_), channel_id=1, source_target_pairs={{0,2},{2,0},{4,6},{6,4},{8,10},{10,8},{12,14},{14,12},{1,3},{3,1},... | collective-permute-start | bytes 1572872 | tf_op jit(solution)/shard_map/ppermute | solution.py:446
  7.1 13.4 %collective-permute-start.2 = (bf16[256,1024]{1,0:T(8,128)(2,1)}, bf16[256,1024]{1,0:T(8,128)(2,1)}, u32[]{:S(2)}, u32[]{:S(2)}) collective-permute-start(bf16[256,1024]{1,0:T(8,128)(2,1)} %join.1.refs_4_), channel_id=1, source_target_pairs={{0,1},{1,0},{2,3},{3,2},{4,5},{5,4},{6,7},{7,6},{8,9},{9,8},{10,11... | collective-permute-start | bytes 1572872 | tf_op jit(solution)/shard_map/ppermute | solution.py:440
  8.6 16.0 %copy-start.1 = (bf16[128,8]{0,1:T(8,128)(2,1)S(1)}, bf16[128,8]{0,1:T(8,128)(2,1)}, u32[]{:S(2)}) copy-start(bf16[128,8]{0,1:T(8,128)(2,1)} %param.10) | copy-start | bytes 6148
  8.6 16.0 %copy-start = (s32[128,8]{0,1:T(8,128)S(1)}, s32[128,8]{0,1:T(8,128)}, u32[]{:S(2)}) copy-start(s32[128,8]{0,1:T(8,128)} %param.9) | copy-start | bytes 12292
  20.5 21.1 %collective-permute-start.3 = (bf16[2048,768]{1,0:T(8,128)(2,1)S(1)}, bf16[2048,768]{1,0:T(8,128)(2,1)}, u32[]{:S(2)}, u32[]{:S(2)}) collective-permute-start(bf16[2048,768]{1,0:T(8,128)(2,1)S(1)} %get-tuple-element.74.refs_0_), channel_id=1, source_target_pairs={{0,16},{16,0},{1,17},{17,1},{2,18},{18,2},{3,19},{19,3},{4,20},{20... | collective-permute-start | bytes 9437192 | tf_op jit(solution)/shard_map/ppermute | solution.py:443
  20.5 21.1 %collective-permute-start.4 = (bf16[384,2048]{1,0:T(8,128)(2,1)}, bf16[384,2048]{1,0:T(8,128)(2,1)}, u32[]{:S(2)}, u32[]{:S(2)}) collective-permute-start(bf16[384,2048]{1,0:T(8,128)(2,1)} %get-tuple-element.75.refs_2_), channel_id=1, source_target_pairs={{0,16},{16,0},{1,17},{17,1},{2,18},{18,2},{3,19},{19,3},{4,20},{20... | collective-permute-start | bytes 4718600 | tf_op jit(solution)/shard_map/ppermute | solution.py:443
  21.0 15.9 %collective-permute-start.7 = (bf16[256,1024]{1,0:T(8,128)(2,1)}, bf16[256,1024]{1,0:T(8,128)(2,1)}, u32[]{:S(2)}, u32[]{:S(2)}) collective-permute-start(bf16[256,1024]{1,0:T(8,128)(2,1)} %collective-permute-done.refs_4_), channel_id=1, source_target_pairs={{0,4},{2,6},{4,8},{6,10},{8,12},{10,14},{12,0},{14,2},{1,5},{3,7},... | collective-permute-start | bytes 1572872 | tf_op jit(solution)/shard_map/ppermute | solution.py:449
  22.6 15.3 %collective-permute-start.5 = (bf16[256,1024]{1,0:T(8,128)(2,1)}, bf16[256,1024]{1,0:T(8,128)(2,1)}, u32[]{:S(2)}, u32[]{:S(2)}) collective-permute-start(bf16[256,1024]{1,0:T(8,128)(2,1)} %collective-permute-done.1.refs_6_), channel_id=1, source_target_pairs={{0,1},{1,0},{2,3},{3,2},{4,5},{5,4},{6,7},{7,6},{8,9},{9,8},{10,11... | collective-permute-start | bytes 1572872 | tf_op jit(solution)/shard_map/ppermute | solution.py:440
  24.1 14.6 %collective-permute-start.8 = (bf16[256,1024]{1,0:T(8,128)(2,1)}, bf16[256,1024]{1,0:T(8,128)(2,1)}, u32[]{:S(2)}, u32[]{:S(2)}) collective-permute-start(bf16[256,1024]{1,0:T(8,128)(2,1)} %collective-permute-done.refs_4_), channel_id=1, source_target_pairs={{0,2},{2,0},{4,6},{6,4},{8,10},{10,8},{12,14},{14,12},{1,3},{3,1},... | collective-permute-start | bytes 1572872 | tf_op jit(solution)/shard_map/ppermute | solution.py:446
  37.0 3.6 %collective-permute-start.6 = (bf16[16,128]{1,0:T(8,128)(2,1)S(1)}, bf16[16,128]{1,0:T(8,128)(2,1)S(1)}, u32[]{:S(2)}, u32[]{:S(2)}) collective-permute-start(bf16[16,128]{1,0:T(8,128)(2,1)S(1)} %get-tuple-element.140), channel_id=1, source_target_pairs={{0,2},{2,0},{4,6},{6,4},{8,10},{10,8},{12,14},{14,12},{1,3},{3,1},... | collective-permute-start | bytes 12296 | tf_op jit(solution)/shard_map/ppermute | solution.py:446
  37.9 13.2 %collective-permute-start.11 = (bf16[256,1024]{1,0:T(8,128)(2,1)}, bf16[256,1024]{1,0:T(8,128)(2,1)}, u32[]{:S(2)}, u32[]{:S(2)}) collective-permute-start(bf16[256,1024]{1,0:T(8,128)(2,1)} %join.1.refs_4_), channel_id=1, source_target_pairs={{0,12},{2,14},{4,0},{6,2},{8,4},{10,6},{12,8},{14,10},{1,13},{3,15... | collective-permute-start | bytes 1572872 | tf_op jit(solution)/shard_map/ppermute | solution.py:449
  38.7 13.4 %collective-permute-start.9 = (bf16[256,1024]{1,0:T(8,128)(2,1)}, bf16[256,1024]{1,0:T(8,128)(2,1)S(1)}, u32[]{:S(2)}, u32[]{:S(2)}) collective-permute-start(bf16[256,1024]{1,0:T(8,128)(2,1)} %collective-permute-done.7.refs_8_), channel_id=1, source_target_pairs={{0,1},{1,0},{2,3},{3,2},{4,5},{5,4},{6,7},{7,6},{8,9},{9,8},{10,11... | collective-permute-start | bytes 1572872 | tf_op jit(solution)/shard_map/ppermute | solution.py:440
  40.6 12.1 %collective-permute-start.13 = (bf16[256,1024]{1,0:T(8,128)(2,1)}, bf16[256,1024]{1,0:T(8,128)(2,1)S(1)}, u32[]{:S(2)}, u32[]{:S(2)}) collective-permute-start(bf16[256,1024]{1,0:T(8,128)(2,1)} %collective-permute-done.7.refs_8_), channel_id=1, source_target_pairs={{0,2},{2,0},{4,6},{6,4},{8,10},{10,8},{12,14},{14,12},{1,3},{3,1},... | collective-permute-start | bytes 1572872 | tf_op jit(solution)/shard_map/ppermute | solution.py:446
  51.1 14.4 %collective-permute-start.12 = (bf16[256,1024]{1,0:T(8,128)(2,1)}, bf16[256,1024]{1,0:T(8,128)(2,1)S(1)}, u32[]{:S(2)}, u32[]{:S(2)}) collective-permute-start(bf16[256,1024]{1,0:T(8,128)(2,1)} %collective-permute-done.5.refs_7_), channel_id=1, source_target_pairs={{0,4},{2,6},{4,8},{6,10},{8,12},{10,14},{12,0},{14,2},{1,5},{3,7},... | collective-permute-start | bytes 1572872 | tf_op jit(solution)/shard_map/ppermute | solution.py:449
  52.6 13.1 %collective-permute-start.14 = (bf16[256,1024]{1,0:T(8,128)(2,1)S(1)}, bf16[256,1024]{1,0:T(8,128)(2,1)S(1)}, u32[]{:S(2)}, u32[]{:S(2)}) collective-permute-start(bf16[256,1024]{1,0:T(8,128)(2,1)S(1)} %collective-permute-done.9.refs_9_), channel_id=1, source_target_pairs={{0,2},{2,0},{4,6},{6,4},{8,10},{10,8},{12,14},{14,12},{1,3},{3,1},... | collective-permute-start | bytes 1572872 | tf_op jit(solution)/shard_map/ppermute | solution.py:446
  53.6 12.7 %collective-permute-start.10 = (bf16[256,1024]{1,0:T(8,128)(2,1)}, bf16[256,1024]{1,0:T(8,128)(2,1)S(1)}, u32[]{:S(2)}, u32[]{:S(2)}) collective-permute-start(bf16[256,1024]{1,0:T(8,128)(2,1)} %collective-permute-done.refs_4_), channel_id=1, source_target_pairs={{0,1},{1,0},{2,3},{3,2},{4,5},{5,4},{6,7},{7,6},{8,9},{9,8},{10,11... | collective-permute-start | bytes 1572872 | tf_op jit(solution)/shard_map/ppermute | solution.py:440
  55.2 12.2 %collective-permute-start.15 = (bf16[2,16,128]{2,1,0:T(8,128)(2,1)S(1)}, bf16[2,16,128]{2,1,0:T(8,128)(2,1)S(1)}, u32[]{:S(2)}, u32[]{:S(2)}) collective-permute-start(bf16[2,16,128]{2,1,0:T(8,128)(2,1)S(1)} %pad_maximum_fusion.refs_8_), channel_id=1, source_target_pairs={{0,4},{2,6},{4,8},{6,10},{8,12},{10,14},{12,0},{14,2},{1,5},{3,7},... | collective-permute-start | bytes 24584 | tf_op jit(solution)/shard_map/ppermute | solution.py:449
  55.4 13.4 %collective-permute-start.16 = (bf16[2,16,128]{2,1,0:T(8,128)(2,1)S(1)}, bf16[2,16,128]{2,1,0:T(8,128)(2,1)S(1)}, u32[]{:S(2)}, u32[]{:S(2)}) collective-permute-start(bf16[2,16,128]{2,1,0:T(8,128)(2,1)S(1)} %pad_maximum_fusion.refs_8_), channel_id=1, source_target_pairs={{0,8},{2,10},{4,12},{6,14},{8,0},{10,2},{12,4},{14,6},{1,9},{3,11}... | collective-permute-start | bytes 24584 | tf_op jit(solution)/shard_map/ppermute | solution.py:449
  65.5 3.8 %collective-permute-start.17 = (bf16[2,16,128]{2,1,0:T(8,128)(2,1)S(1)}, bf16[2,16,128]{2,1,0:T(8,128)(2,1)S(1)}, u32[]{:S(2)}, u32[]{:S(2)}) collective-permute-start(bf16[2,16,128]{2,1,0:T(8,128)(2,1)S(1)} %pad_maximum_fusion.refs_8_), channel_id=1, source_target_pairs={{0,12},{2,14},{4,0},{6,2},{8,4},{10,6},{12,8},{14,10},{1,13},{3,15... | collective-permute-start | bytes 24584 | tf_op jit(solution)/shard_map/ppermute | solution.py:449
  65.7 17.2 %collective-permute-start.18 = (bf16[256,1024]{1,0:T(8,128)(2,1)}, bf16[256,1024]{1,0:T(8,128)(2,1)S(1)}, u32[]{:S(2)}, u32[]{:S(2)}) collective-permute-start(bf16[256,1024]{1,0:T(8,128)(2,1)} %collective-permute-done.5.refs_7_), channel_id=1, source_target_pairs={{0,12},{2,14},{4,0},{6,2},{8,4},{10,6},{12,8},{14,10},{1,13},{3,15... | collective-permute-start | bytes 1572872 | tf_op jit(solution)/shard_map/ppermute | solution.py:449
  66.4 16.5 %collective-permute-start.19 = (bf16[256,1024]{1,0:T(8,128)(2,1)}, bf16[256,1024]{1,0:T(8,128)(2,1)S(1)}, u32[]{:S(2)}, u32[]{:S(2)}) collective-permute-start(bf16[256,1024]{1,0:T(8,128)(2,1)} %collective-permute-done.11.refs_4_), channel_id=1, source_target_pairs={{0,2},{2,0},{4,6},{6,4},{8,10},{10,8},{12,14},{14,12},{1,3},{3,1},... | collective-permute-start | bytes 1572872 | tf_op jit(solution)/shard_map/ppermute | solution.py:446
  67.3 15.5 %collective-permute-start.20 = (bf16[256,1024]{1,0:T(8,128)(2,1)}, bf16[256,1024]{1,0:T(8,128)(2,1)S(1)}, u32[]{:S(2)}, u32[]{:S(2)}) collective-permute-start(bf16[256,1024]{1,0:T(8,128)(2,1)} %collective-permute-done.11.refs_4_), channel_id=1, source_target_pairs={{0,1},{1,0},{2,3},{3,2},{4,5},{5,4},{6,7},{7,6},{8,9},{9,8},{10,11... | collective-permute-start | bytes 1572872 | tf_op jit(solution)/shard_map/ppermute | solution.py:440
  82.9 18.4 %collective-permute-start.29 = (bf16[288,5248]{1,0:T(8,128)(2,1)S(1)}, bf16[288,5248]{1,0:T(8,128)(2,1)S(1)}, u32[]{:S(2)}, u32[]{:S(2)}) collective-permute-start(bf16[288,5248]{1,0:T(8,128)(2,1)S(1)} %get-tuple-element.116), channel_id=1, source_target_pairs={{0,16},{16,0},{1,17},{17,1},{2,18},{18,2},{3,19},{19,3},{4,20},{20... | collective-permute-start | bytes 9068552 | tf_op jit(solution)/shard_map/ppermute | solution.py:443
  83.0 15.2 %collective-permute-start.28 = (bf16[144,5248]{1,0:T(8,128)(2,1)S(1)}, bf16[144,5248]{1,0:T(8,128)(2,1)S(1)}, u32[]{:S(2)}, u32[]{:S(2)}) collective-permute-start(bf16[144,5248]{1,0:T(8,128)(2,1)S(1)} %get-tuple-element.115), channel_id=1, source_target_pairs={{0,16},{16,0},{1,17},{17,1},{2,18},{18,2},{3,19},{19,3},{4,20},{20... | collective-permute-start | bytes 4534280 | tf_op jit(solution)/shard_map/ppermute | solution.py:443
  83.5 13.9 %collective-permute-start.24 = (bf16[1,136,1024]{2,1,0:T(8,128)(2,1)S(1)}, bf16[1,136,1024]{2,1,0:T(8,128)(2,1)S(1)}, u32[]{:S(2)}, u32[]{:S(2)}) collective-permute-start(bf16[1,136,1024]{2,1,0:T(8,128)(2,1)S(1)} %get-tuple-element.111), channel_id=1, source_target_pairs={{0,2},{2,0},{4,6},{6,4},{8,10},{10,8},{12,14},{14,12},{1,3},{3,1},... | collective-permute-start | bytes 835592 | tf_op jit(solution)/shard_map/ppermute | solution.py:446
  84.3 13.1 %collective-permute-start.23 = (bf16[1,136,1024]{2,1,0:T(8,128)(2,1)S(1)}, bf16[1,136,1024]{2,1,0:T(8,128)(2,1)S(1)}, u32[]{:S(2)}, u32[]{:S(2)}) collective-permute-start(bf16[1,136,1024]{2,1,0:T(8,128)(2,1)S(1)} %get-tuple-element.110), channel_id=1, source_target_pairs={{0,1},{1,0},{2,3},{3,2},{4,5},{5,4},{6,7},{7,6},{8,9},{9,8},{10,11... | collective-permute-start | bytes 835592 | tf_op jit(solution)/shard_map/ppermute | solution.py:440
  86.0 11.4 %collective-permute-start.22 = (bf16[1,136,1024]{2,1,0:T(8,128)(2,1)S(1)}, bf16[1,136,1024]{2,1,0:T(8,128)(2,1)S(1)}, u32[]{:S(2)}, u32[]{:S(2)}) collective-permute-start(bf16[1,136,1024]{2,1,0:T(8,128)(2,1)S(1)} %get-tuple-element.102), channel_id=1, source_target_pairs={{0,12},{2,14},{4,0},{6,2},{8,4},{10,6},{12,8},{14,10},{1,13},{3,15... | collective-permute-start | bytes 835592 | tf_op jit(solution)/shard_map/ppermute | solution.py:449
  97.4 3.4 %collective-permute-start.30 = (bf16[144,5248]{1,0:T(8,128)(2,1)S(1)}, bf16[144,5248]{1,0:T(8,128)(2,1)S(1)}, u32[]{:S(2)}, u32[]{:S(2)}) collective-permute-start(bf16[144,5248]{1,0:T(8,128)(2,1)S(1)} %get-tuple-element.118), channel_id=1, source_target_pairs={{0,16},{16,0},{1,17},{17,1},{2,18},{18,2},{3,19},{19,3},{4,20},{20... | collective-permute-start | bytes 4534280 | tf_op jit(solution)/shard_map/ppermute | solution.py:443
  97.5 9.8 %collective-permute-start.26 = (bf16[1,136,1024]{2,1,0:T(8,128)(2,1)S(1)}, bf16[1,136,1024]{2,1,0:T(8,128)(2,1)S(1)}, u32[]{:S(2)}, u32[]{:S(2)}) collective-permute-start(bf16[1,136,1024]{2,1,0:T(8,128)(2,1)S(1)} %get-tuple-element.113), channel_id=1, source_target_pairs={{0,1},{1,0},{2,3},{3,2},{4,5},{5,4},{6,7},{7,6},{8,9},{9,8},{10,11... | collective-permute-start | bytes 835592 | tf_op jit(solution)/shard_map/ppermute | solution.py:440
  98.1 10.5 %collective-permute-start.25 = (bf16[1,136,1024]{2,1,0:T(8,128)(2,1)S(1)}, bf16[1,136,1024]{2,1,0:T(8,128)(2,1)S(1)}, u32[]{:S(2)}, u32[]{:S(2)}) collective-permute-start(bf16[1,136,1024]{2,1,0:T(8,128)(2,1)S(1)} %get-tuple-element.112), channel_id=1, source_target_pairs={{0,4},{2,6},{4,8},{6,10},{8,12},{10,14},{12,0},{14,2},{1,5},{3,7},... | collective-permute-start | bytes 835592 | tf_op jit(solution)/shard_map/ppermute | solution.py:449
  98.1 10.4 %collective-permute-start.27 = (bf16[1,136,1024]{2,1,0:T(8,128)(2,1)S(1)}, bf16[1,136,1024]{2,1,0:T(8,128)(2,1)S(1)}, u32[]{:S(2)}, u32[]{:S(2)}) collective-permute-start(bf16[1,136,1024]{2,1,0:T(8,128)(2,1)S(1)} %add_convert_fusion.5), channel_id=1, source_target_pairs={{0,2},{2,0},{4,6},{6,4},{8,10},{10,8},{12,14},{14,12},{1,3},{3,1},... | collective-permute-start | bytes 835592 | tf_op jit(solution)/shard_map/ppermute | solution.py:446
  100.8 12.2 %collective-permute-start.21 = (bf16[1,136,1024]{2,1,0:T(8,128)(2,1)S(1)}, bf16[1,136,1024]{2,1,0:T(8,128)(2,1)S(1)}, u32[]{:S(2)}, u32[]{:S(2)}) collective-permute-start(bf16[1,136,1024]{2,1,0:T(8,128)(2,1)S(1)} %get-tuple-element.100), channel_id=1, source_target_pairs={{0,1},{1,0},{2,3},{3,2},{4,5},{5,4},{6,7},{7,6},{8,9},{9,8},{10,11... | collective-permute-start | bytes 835592 | tf_op jit(solution)/shard_map/ppermute | solution.py:440
  101.3 20.8 %collective-permute-start.34 = (bf16[1,136,1024]{2,1,0:T(8,128)(2,1)S(1)}, bf16[1,136,1024]{2,1,0:T(8,128)(2,1)S(1)}, u32[]{:S(2)}, u32[]{:S(2)}) collective-permute-start(bf16[1,136,1024]{2,1,0:T(8,128)(2,1)S(1)} %get-tuple-element.126), channel_id=1, source_target_pairs={{0,1},{1,0},{2,3},{3,2},{4,5},{5,4},{6,7},{7,6},{8,9},{9,8},{10,11... | collective-permute-start | bytes 835592 | tf_op jit(solution)/shard_map/ppermute | solution.py:440
  107.2 14.8 %collective-permute-start.35 = (bf16[1,136,1024]{2,1,0:T(8,128)(2,1)S(1)}, bf16[1,136,1024]{2,1,0:T(8,128)(2,1)S(1)}, u32[]{:S(2)}, u32[]{:S(2)}) collective-permute-start(bf16[1,136,1024]{2,1,0:T(8,128)(2,1)S(1)} %get-tuple-element.127), channel_id=1, source_target_pairs={{0,2},{2,0},{4,6},{6,4},{8,10},{10,8},{12,14},{14,12},{1,3},{3,1},... | collective-permute-start | bytes 835592 | tf_op jit(solution)/shard_map/ppermute | solution.py:446
  108.7 12.7 %collective-permute-start.32 = (bf16[1,136,1024]{2,1,0:T(8,128)(2,1)S(1)}, bf16[1,136,1024]{2,1,0:T(8,128)(2,1)S(1)}, u32[]{:S(2)}, u32[]{:S(2)}) collective-permute-start(bf16[1,136,1024]{2,1,0:T(8,128)(2,1)S(1)} %add_convert_fusion.4), channel_id=1, source_target_pairs={{0,2},{2,0},{4,6},{6,4},{8,10},{10,8},{12,14},{14,12},{1,3},{3,1},... | collective-permute-start | bytes 835592 | tf_op jit(solution)/shard_map/ppermute | solution.py:446
  109.9 12.2 %collective-permute-start.36 = (bf16[1,136,1024]{2,1,0:T(8,128)(2,1)S(1)}, bf16[1,136,1024]{2,1,0:T(8,128)(2,1)S(1)}, u32[]{:S(2)}, u32[]{:S(2)}) collective-permute-start(bf16[1,136,1024]{2,1,0:T(8,128)(2,1)S(1)} %add_convert_fusion.3), channel_id=1, source_target_pairs={{0,4},{2,6},{4,8},{6,10},{8,12},{10,14},{12,0},{14,2},{1,5},{3,7},... | collective-permute-start | bytes 835592 | tf_op jit(solution)/shard_map/ppermute | solution.py:449
  113.1 16.7 %collective-permute-start.31 = (bf16[1,136,1024]{2,1,0:T(8,128)(2,1)S(1)}, bf16[1,136,1024]{2,1,0:T(8,128)(2,1)S(1)}, u32[]{:S(2)}, u32[]{:S(2)}) collective-permute-start(bf16[1,136,1024]{2,1,0:T(8,128)(2,1)S(1)} %add_convert_fusion.2), channel_id=1, source_target_pairs={{0,12},{2,14},{4,0},{6,2},{8,4},{10,6},{12,8},{14,10},{1,13},{3,15... | collective-permute-start | bytes 835592 | tf_op jit(solution)/shard_map/ppermute | solution.py:449
  121.5 8.3 %collective-permute-start.33 = (bf16[1,136,1024]{2,1,0:T(8,128)(2,1)S(1)}, bf16[1,136,1024]{2,1,0:T(8,128)(2,1)S(1)}, u32[]{:S(2)}, u32[]{:S(2)}) collective-permute-start(bf16[1,136,1024]{2,1,0:T(8,128)(2,1)S(1)} %add_convert_fusion.1), channel_id=1, source_target_pairs={{0,1},{1,0},{2,3},{3,2},{4,5},{5,4},{6,7},{7,6},{8,9},{9,8},{10,11... | collective-permute-start | bytes 835592 | tf_op jit(solution)/shard_map/ppermute | solution.py:440
  122.3 9.1 %collective-permute-start.37 = (bf16[1,136,1024]{2,1,0:T(8,128)(2,1)S(1)}, bf16[1,136,1024]{2,1,0:T(8,128)(2,1)S(1)}, u32[]{:S(2)}, u32[]{:S(2)}) collective-permute-start(bf16[1,136,1024]{2,1,0:T(8,128)(2,1)S(1)} %add_convert_fusion), channel_id=1, source_target_pairs={{0,4},{2,6},{4,8},{6,10},{8,12},{10,14},{12,0},{14,2},{1,5},{3,7},... | collective-permute-start | bytes 835592 | tf_op jit(solution)/shard_map/ppermute | solution.py:449
  122.3 9.0 %collective-permute-start.38 = (bf16[1,136,1024]{2,1,0:T(8,128)(2,1)S(1)}, bf16[1,136,1024]{2,1,0:T(8,128)(2,1)S(1)}, u32[]{:S(2)}, u32[]{:S(2)}) collective-permute-start(bf16[1,136,1024]{2,1,0:T(8,128)(2,1)S(1)} %get-tuple-element.132), channel_id=1, source_target_pairs={{0,2},{2,0},{4,6},{6,4},{8,10},{10,8},{12,14},{14,12},{1,3},{3,1},... | collective-permute-start | bytes 835592 | tf_op jit(solution)/shard_map/ppermute | solution.py:446
